TPU v7x, 32 devices: a whole 2x2x4 slice. The times are simulated.
32 devices in a mesh: hash: 4 (over z), head: 4 (over y, x), seq: 2 (over core).
Axes of the slice: x: 2, y: 2, z: 4, core: 2. Of those that a mesh axis runs over, the one named last changes fastest.
Arguments:
- inputs: bfloat16 [2, 2048, 2, 768], P('seq', 'hash'), may hold values from -18 to 18
- w_qkv: bfloat16 [3, 768, 768], P(None, None, 'head'), may hold values from -0.21875 to 0.21875
- w_out: bfloat16 [768, 768], P('head'), may hold values from -2.5 to 2.5
- feedforward_up_weight: bfloat16 [768, 3072], P(None, 'head'), may hold values from -0.21875 to 0.21875
- feedforward_down_weight: bfloat16 [3072, 768], P('head'), may hold values from -0.109375 to 0.109375
- norm_gain: float32 [2, 768], replicated, may hold values from 0.1 to 1.9
- norm_bias: float32 [2, 768], replicated, may hold values from -3 to 3
- planes: int32 [32, 8, 64], P('hash'), may hold values from 0 to 1
- mask_pos: int32 [2, 1024], replicated, may hold values from 0 to 4096, as said below
- cot_rows: bfloat16 [2, 1024, 768], replicated, may hold values from -6 to 6
Outputs:
- layer_out: bfloat16 [2, 2048, 2, 768], P('seq', 'hash')
- grad_inputs: float32 [2, 2048, 2, 768], P('seq', 'hash')
- grad_w_qkv: float32 [3, 768, 768], P(None, None, 'head')
- grad_w_out: float32 [768, 768], P('head')
- grad_w_up: float32 [768, 3072], P(None, 'head')
- grad_w_down: float32 [3072, 768], P('head')
- grad_norm_gain: float32 [2, 768], P(None, 'head')
- grad_norm_bias: float32 [2, 768], P(None, 'head')
- stream_rms: float32 [3], replicated
Inputs may be any that keep to these rules, and one draw needn't show every extreme that they name: `mask_pos`: each row lists between 204 and 1024 distinct positions in increasing order and fills its remaining slots with 4096; in every draw some sequence fills all 1024 slots.
All inputs are finite; a program needn't handle non-finite values.
Results may differ from a plain program's by a relative error of at most 0.012.
Values may be sent and summed in bfloat16 or wider, within the bound.
No kernel may reach another device: no remote copies, remote signals or barrier semaphores. Data moves between devices by JAX's collectives and lax.ppermute only.
A program may use at most 384 MiB of HBM per device.

v0:
```python
from functools import partial

import jax
import jax.numpy as jnp
from jax import lax
from jax.sharding import PartitionSpec as P

HEAD_DIM = 64
HASHES = 32


highest_precision = lax.Precision.HIGHEST
sharpness = 3.0


def code_values(rows_in, signed):
    unit_rows = rows_in * lax.rsqrt(jnp.sum(rows_in * rows_in, axis=-1, keepdims=True) + 1e-06)
    project = (
        jnp.einsum("lhe,tbe->lhtb", unit_rows, signed, precision=highest_precision) * sharpness
    )
    upper = jax.nn.sigmoid(project)
    lower = jax.nn.sigmoid(-project)
    codes = jnp.ones(project.shape[:-1] + (1,), jnp.float32)
    for bit_index in range(project.shape[-1]):
        codes = jnp.concatenate(
            [
                codes * lower[..., bit_index : bit_index + 1],
                codes * upper[..., bit_index : bit_index + 1],
            ],
            axis=-1,
        )
    return codes


def layer_norm(values_in, gain_row, bias_row):
    center = values_in - jnp.mean(values_in, axis=-1, keepdims=True)
    spread = jnp.mean(center * center, axis=-1, keepdims=True)
    return center * lax.rsqrt(spread + 1e-05) * gain_row + bias_row


def gelu_exact(values_in):
    return jax.nn.gelu(values_in, approximate=False)


def seq_slice(block, seq_id):
    return lax.dynamic_index_in_dim(block, seq_id, 1, keepdims=False)


def seq_entry(block, seq_id):
    return lax.dynamic_index_in_dim(block, seq_id, 0, keepdims=False)


def shards(
    inputs,
    w_qkv,
    w_out,
    feedforward_up_weight,
    feedforward_down_weight,
    norm_gain,
    norm_bias,
    planes,
    mask_pos,
    cot_rows,
):
    own_rows = inputs[0]
    piece, seq_count, model_width = own_rows.shape
    head_width = w_out.shape[0]
    head_count = head_width // HEAD_DIM
    hash_count = lax.axis_size("hash")
    half_len = piece * hash_count
    hash_index = lax.axis_index("hash")
    half_index = lax.axis_index("seq")
    head_index = lax.axis_index("head")
    signed = (2 * planes - 1).astype(jnp.float32)
    code_map = partial(code_values, signed=signed)
    seq_ids = jnp.arange(seq_count, dtype=jnp.int32)
    piece_ids = jnp.arange(piece, dtype=jnp.int32)

    def split_heads(block):
        return block.astype(jnp.float32).reshape(block.shape[0], head_count, HEAD_DIM)

    qkv_own = jnp.einsum(
        "lsd,cde->lsce", own_rows, w_qkv, preferred_element_type=jnp.float32
    ).astype(jnp.bfloat16)
    qkv_all = lax.all_gather(qkv_own, "hash", axis=0, tiled=True)

    def key_table(seq_id):
        packed = seq_slice(qkv_all, seq_id)
        key_codes = code_map(split_heads(packed[:, 1])).astype(jnp.bfloat16)
        value_rows = packed[:, 2].reshape(half_len, head_count, HEAD_DIM)
        return jnp.einsum(
            "lhtb,lhe->htbe", key_codes, value_rows, preferred_element_type=jnp.float32
        )

    partial_tables = lax.map(key_table, seq_ids)
    tables = lax.psum(partial_tables, "seq").astype(jnp.bfloat16)
    row_count = piece * lax.axis_size("hash")

    def estimate_one_seq(seq_id):
        query_codes = code_map(split_heads(seq_slice(qkv_all, seq_id)[:, 0])).astype(jnp.bfloat16)
        mixed_rows = jnp.einsum(
            "lhtb,htbe->lhe",
            query_codes,
            seq_entry(tables, seq_id),
            preferred_element_type=jnp.float32,
        )
        return mixed_rows.reshape(row_count, head_width) / HASHES

    estimate = lax.psum_scatter(
        jnp.moveaxis(lax.map(estimate_one_seq, seq_ids), 0, 1),
        "hash",
        scatter_dimension=0,
        tiled=True,
    )
    attn_b = estimate.astype(jnp.bfloat16)
    out_part = jnp.einsum("lse,ed->lsd", attn_b, w_out, preferred_element_type=jnp.float32)
    attention_result = lax.psum(out_part, "head")
    resid_in = own_rows.astype(jnp.float32)
    first_sum = resid_in + attention_result
    normalized_rows, first_pull = jax.vjp(layer_norm, first_sum, norm_gain[0], norm_bias[0])
    normalized_rows_backward = normalized_rows.astype(jnp.bfloat16)
    preactivation = jnp.einsum(
        "gbk,km->gbm",
        normalized_rows_backward,
        feedforward_up_weight,
        preferred_element_type=jnp.float32,
    )
    hidden_f, gelu_pull = jax.vjp(gelu_exact, preactivation)
    hidden_rows_backward = hidden_f.astype(jnp.bfloat16)
    feedforward_piece = jnp.einsum(
        "uxr,ro->uxo",
        hidden_rows_backward,
        feedforward_down_weight,
        preferred_element_type=jnp.float32,
    )
    feedforward_result = lax.psum(feedforward_piece, "head")
    second_sum = normalized_rows_backward.astype(jnp.float32) + feedforward_result
    result, second_pull = jax.vjp(layer_norm, second_sum, norm_gain[1], norm_bias[1])
    layer_out = result.astype(jnp.bfloat16)
    row_base = half_index * half_len + hash_index * piece
    pick_own = (mask_pos[:, :, None] == row_base + piece_ids[None, None, :]).astype(jnp.bfloat16)
    grad_out = jnp.einsum("sml,smd->lsd", pick_own, cot_rows, preferred_element_type=jnp.float32)
    grad_second, gain_second, bias_second = second_pull(grad_out)
    feedforward_gradient_rows = grad_second.astype(jnp.bfloat16)
    down_gradient = jnp.einsum(
        "jbt,jbq->tq",
        hidden_rows_backward,
        feedforward_gradient_rows,
        preferred_element_type=jnp.float32,
    )
    hidden_gradient = jnp.einsum(
        "rab,eb->rae",
        feedforward_gradient_rows,
        feedforward_down_weight,
        preferred_element_type=jnp.float32,
    )
    preactivation_gradient_rows = gelu_pull(hidden_gradient)[0].astype(jnp.bfloat16)
    up_gradient = jnp.einsum(
        "pnq,pnm->qm",
        normalized_rows_backward,
        preactivation_gradient_rows,
        preferred_element_type=jnp.float32,
    )
    backward_piece = jnp.einsum(
        "cxt,qt->cxq",
        preactivation_gradient_rows,
        feedforward_up_weight,
        preferred_element_type=jnp.float32,
    )
    grad_normed = grad_second + lax.psum(backward_piece, "head")
    grad_first, gain_first, bias_first = first_pull(grad_normed)
    grad_attn_b = grad_first.astype(jnp.bfloat16)
    grad_w_out = jnp.einsum("lse,lsd->ed", attn_b, grad_attn_b, preferred_element_type=jnp.float32)
    grad_estimate_b = jnp.einsum(
        "lsd,ed->lse", grad_attn_b, w_out, preferred_element_type=jnp.float32
    ).astype(jnp.bfloat16)

    def query_side(query_flat, seq_tables, grad_rows):
        row_total = query_flat.shape[0]
        query_f = query_flat.reshape(row_total, head_count, HEAD_DIM)
        query_codes, code_pull = jax.vjp(code_map, query_f)
        codes_b = query_codes.astype(jnp.bfloat16)
        grad_heads = grad_rows.reshape(row_total, head_count, HEAD_DIM)
        table_grad = (
            jnp.einsum("lhtb,lhe->htbe", codes_b, grad_heads, preferred_element_type=jnp.float32)
            / HASHES
        )
        code_grad = (
            jnp.einsum("lhe,htbe->lhtb", grad_heads, seq_tables, preferred_element_type=jnp.float32)
            / HASHES
        )
        query_grad = code_pull(code_grad)[0]
        return (table_grad, query_grad.reshape(row_total, head_width))

    def key_side(packed, seq_grad_tables):
        row_total = packed.shape[0]
        key_codes, key_pull = jax.vjp(code_map, split_heads(packed[:, 1]))
        codes_b = key_codes.astype(jnp.bfloat16)
        value_rows = packed[:, 2].reshape(row_total, head_count, HEAD_DIM)
        value_grad = jnp.einsum(
            "lhtb,htbe->lhe", codes_b, seq_grad_tables, preferred_element_type=jnp.float32
        )
        code_grad = jnp.einsum(
            "lhe,htbe->lhtb", value_rows, seq_grad_tables, preferred_element_type=jnp.float32
        )
        key_grad = key_pull(code_grad)[0]
        return (key_grad.reshape(row_total, head_width), value_grad.reshape(row_total, head_width))

    grad_all = lax.all_gather(grad_estimate_b, "hash", axis=0, tiled=True)

    def dense_query(seq_id):
        return query_side(
            seq_slice(qkv_all, seq_id)[:, 0].astype(jnp.float32),
            seq_entry(tables, seq_id),
            seq_slice(grad_all, seq_id),
        )

    table_parts, query_grad_all = lax.map(dense_query, seq_ids)
    grad_tables = lax.psum(table_parts, "seq").astype(jnp.bfloat16)

    def dense_one_seq(seq_id):
        key_grad, value_grad = key_side(seq_slice(qkv_all, seq_id), seq_entry(grad_tables, seq_id))
        return jnp.stack([seq_entry(query_grad_all, seq_id), key_grad, value_grad], axis=1)

    grad_qkv = lax.psum_scatter(
        jnp.moveaxis(lax.map(dense_one_seq, seq_ids), 0, 1), "hash", scatter_dimension=0, tiled=True
    )
    grad_qkv_b = grad_qkv.astype(jnp.bfloat16)
    grad_w_qkv = jnp.einsum(
        "lsd,lsce->cde", own_rows, grad_qkv_b, preferred_element_type=jnp.float32
    )
    input_part = jnp.einsum("lsce,cde->lsd", grad_qkv_b, w_qkv, preferred_element_type=jnp.float32)
    grad_inputs = grad_first + lax.psum(input_part, "head")
    squares = jnp.stack(
        [
            jnp.sum(resid_in * resid_in),
            jnp.sum(attention_result * attention_result),
            jnp.sum(first_sum * first_sum),
        ]
    )
    totals = lax.psum(
        (
            grad_w_qkv,
            grad_w_out,
            up_gradient,
            down_gradient,
            jnp.stack([gain_first, gain_second]),
            jnp.stack([bias_first, bias_second]),
            squares,
        ),
        ("hash", "seq"),
    )
    element_count = piece * seq_count * model_width * hash_count * lax.axis_size("seq")
    stream_rms = jnp.sqrt(totals[6] / element_count)
    quarter = model_width // lax.axis_size("head")
    grad_gain = lax.dynamic_slice_in_dim(totals[4], head_index * quarter, quarter, 1)
    grad_bias = lax.dynamic_slice_in_dim(totals[5], head_index * quarter, quarter, 1)
    return (
        layer_out[None],
        grad_inputs[None],
        totals[0],
        totals[1],
        totals[2],
        totals[3],
        grad_gain,
        grad_bias,
        stream_rms,
    )


def solution(mesh):
    placed = (
        P("seq", "hash", None, None),
        P(None, None, "head"),
        P("head", None),
        P(None, "head"),
        P("head", None),
        P(),
        P(),
        P("hash", None, None),
        P(),
        P(),
    )
    return jax.shard_map(
        shards,
        mesh=mesh,
        in_specs=placed,
        out_specs=(
            P("seq", "hash", None, None),
            P("seq", "hash", None, None),
            P(None, None, "head"),
            P("head", None),
            P(None, "head"),
            P("head", None),
            P(None, "head"),
            P(None, "head"),
            P(),
        ),
        check_vma=False,
    )
```

profile of v0, /device:TPU:1, one launch (start us, length us, event | category | flops | bytes accessed | tf_op | source)
XLA Modules:
  0.0 1840.3 jit_solution(2245616367222977012)
XLA Ops:
  11.3 91.7 %all-gather.3.cloned.1.call-done = bf16[2048,2,3,192]{0,3,2,1:T(8,128)(2,1)} async-done(((bf16[512,2,3,192]{0,3,2,1:T(8,128)(2,1)}), bf16[2048,2,3,192]{0,3,2,1:T(8,128)(2,1)}) %all-gather.3.cloned.1.call-update) | async-done | bytes 4718608 | tf_op jit(solution)/shard_map/all_gather | solution.py:85
  105.0 109.8 %while.42 = (s32[]{:T(128)}, f32[2,3,8,256,64]{3,4,2,1,0:T(8,128)}, s32[2]{0:T(128)S(1)}, bf16[2048,2,3,192]{0,3,2,1:T(8,128)(2,1)}, f32[8,8,64]{2,1,0:T(8,128)S(1)}, /*index=5*/s32[]{:T(128)}, s32[]{:T(128)}, s32[]{:T(128)}) while((s32[]{:T(128)}, f32[2,3,8,256,64]{3,4,2,1,0:T(8,128)}, s32[2]{0:T(128)S(1)}, ...), condition=%wide.region_2.3_spmd, body=%wide.region_0.2_spmd.sunk | while | flops 2017296384 | bytes 179421840 | solution.py:95
  122.2 9.0 fusion.295
  131.3 15.5 multiply_convert_fusion.11
  146.7 13.1 bitcast_dynamic-update-slice_fusion.4
  177.1 9.0 fusion.295
  186.2 15.5 multiply_convert_fusion.11
  201.6 13.1 bitcast_dynamic-update-slice_fusion.4
  214.8 13.4 all-reduce.51
  230.2 112.8 %while.43 = (s32[]{:T(128)}, f32[2,2048,192]{1,2,0:T(8,128)}, s32[2]{0:T(128)S(1)}, bf16[2,3,8,256,64]{3,4,2,1,0:T(8,128)(2,1)}, bf16[2048,2,3,192]{0,3,2,1:T(8,...) while((s32[]{:T(128)}, f32[2,2048,192]{1,2,0:T(8,128)}, s32[2]{0:T(128)S(1)}, ...), condition=%wide.region_6.7_spmd, body=%wide.region_4.6_spmd.sunk | while | flops 2017689600 | bytes 180994704 | solution.py:110
  247.4 9.0 fusion.304
  256.5 15.5 multiply_convert_fusion.12
  271.9 12.0 fusion.305
  303.8 9.0 fusion.304
  312.9 15.5 multiply_convert_fusion.12
  328.3 12.0 fusion.305
  343.3 57.9 %reduce-scatter.3.cloned.1.call-done = f32[512,2,192]{0,2,1:T(8,128)} async-done(((f32[2048,2,192]{0,2,1:T(8,128)}), f32[512,2,192]{0,2,1:T(8,128)}) %reduce-scatter.3.cloned.1.call-update) | async-done | bytes 786448 | tf_op jit(solution)/shard_map/reduce_scatter | solution.py:109
  404.8 87.5 %all-reduce.42.cloned.1.call-done = f32[512,2,768]{2,0,1:T(8,128)} async-done(((f32[512,2,768]{2,0,1:T(8,128)}), f32[512,2,768]{2,0,1:T(8,128)}) %all-reduce.42.cloned.1.call-update) | async-done | bytes 3145744 | tf_op jit(solution)/shard_map/psum | solution.py:117
  513.5 87.0 %all-reduce.44.cloned.1.call-done = f32[512,2,768]{2,0,1:T(8,128)} async-done(((f32[512,2,768]{2,0,1:T(8,128)}), f32[512,2,768]{2,0,1:T(8,128)}) %all-reduce.44.cloned.1.call-update) | async-done | bytes 3145744 | tf_op jit(solution)/shard_map/psum | solution.py:136
  620.4 87.3 %all-reduce.46.cloned.1.call-done = f32[512,2,768]{2,0,1:T(8,128)} async-done(((f32[512,2,768]{2,0,1:T(8,128)}), f32[512,2,768]{2,0,1:T(8,128)}) %all-reduce.46.cloned.1.call-update) | async-done | bytes 3145744 | tf_op jit(solution)/shard_map/psum | solution.py:170
  716.9 37.0 %all-gather.5.cloned.1.call-done = bf16[2048,2,192]{0,2,1:T(8,128)(2,1)} async-done(((bf16[512,2,192]{0,2,1:T(8,128)(2,1)}), bf16[2048,2,192]{0,2,1:T(8,128)(2,1)}) %all-gather.5.cloned.1.call-update) | async-done | bytes 1572880 | tf_op jit(solution)/shard_map/all_gather | solution.py:209
  758.0 337.8 %while.44 = (s32[]{:T(128)}, f32[2,3,8,256,64]{3,4,2,1,0:T(8,128)}, f32[2,2048,192]{1,2,0:T(8,128)}, s32[2]{0:T(128)S(1)}, bf16[2048,2,3,192]{0,3,2,1:T(8,128)(2...) while((s32[]{:T(128)}, f32[2,3,8,256,64]{3,4,2,1,0:T(8,128)}, ...), condition=%wide.region_36.37_spmd, body=%wide.region_19.36_spmd.sunk | while | flops 4049946624 | bytes 631915840 | solution.py:218
  795.9 9.4 broadcast_multiply_fusion.51
  810.4 20.6 %multiply_bitcast_fusion.2 = f32[2048,3,8,256]{0,3,2,1:T(8,128)} fusion(bf16[2048,3,64,1]{0,2,3,1:T(8,128)(2,1)} %bitcast.658, bf16[2,3,8,256,64]{3,4,2,1,0:T(8,128)(2,1)} %get-tuple-element.1075, s32[]{:T(128)S(6)} %select_n.32), kind=kOutput, calls=%fused_computation.109.clone.1 | convolution fusion | flops 1623195648 | bytes 51904516 | tf_op jit(solution)/shard_map/while/body/eval_jaxpr/lhe,htbe->lhtb/dot_general | solution.py:189
  831.0 43.0 %multiply_reduce_fusion.49 = (f32[2048,3,8]{0,2,1:T(8,128)}, f32[2048,3,8]{0,2,1:T(8,128)}, f32[2048,3,8,128]{0,3,2,1:T(8,128)}, bf16[2048,3,8,128]{0,3,2,1:T(8,128)(2,1)}, bf16[2048,3,8,128]{0,3,2,1:T(8,128)(2,1)}) fusion(f32[2048,3,8,256]{0,3,2,1:T(8,128)} %multiply_bitcast_fusion.2, f32[2048,3,8,64]{0,3,2,1:T(8,128)} %get-tuple-element.896, ...), kind=kLoop, calls=%fused_computation.117.clone.1 | loop fusion | flops 75399168 | bytes 126615552 | tf_op jit(solution)/shard_map/while/body/eval_jaxpr/transpose(jvp())/reduce_sum | solution.py:27
  874.0 14.8 multiply_reduce_fusion.50
  916.0 11.0 bitcast_dynamic-update-slice_fusion.5
  944.4 9.4 broadcast_multiply_fusion.51
  958.9 20.6 %multiply_bitcast_fusion.2 = f32[2048,3,8,256]{0,3,2,1:T(8,128)} fusion(bf16[2048,3,64,1]{0,2,3,1:T(8,128)(2,1)} %bitcast.658, bf16[2,3,8,256,64]{3,4,2,1,0:T(8,128)(2,1)} %get-tuple-element.1075, s32[]{:T(128)S(6)} %select_n.32), kind=kOutput, calls=%fused_computation.109.clone.1 | convolution fusion | flops 1623195648 | bytes 51904516 | tf_op jit(solution)/shard_map/while/body/eval_jaxpr/lhe,htbe->lhtb/dot_general | solution.py:189
  979.5 43.0 %multiply_reduce_fusion.49 = (f32[2048,3,8]{0,2,1:T(8,128)}, f32[2048,3,8]{0,2,1:T(8,128)}, f32[2048,3,8,128]{0,3,2,1:T(8,128)}, bf16[2048,3,8,128]{0,3,2,1:T(8,128)(2,1)}, bf16[2048,3,8,128]{0,3,2,1:T(8,128)(2,1)}) fusion(f32[2048,3,8,256]{0,3,2,1:T(8,128)} %multiply_bitcast_fusion.2, f32[2048,3,8,64]{0,3,2,1:T(8,128)} %get-tuple-element.896, ...), kind=kLoop, calls=%fused_computation.117.clone.1 | loop fusion | flops 75399168 | bytes 126615552 | tf_op jit(solution)/shard_map/while/body/eval_jaxpr/transpose(jvp())/reduce_sum | solution.py:27
  1022.5 14.8 multiply_reduce_fusion.50
  1064.5 11.0 bitcast_dynamic-update-slice_fusion.5
  1095.8 13.2 all-reduce.52
  1109.0 309.1 %while.45 = (s32[]{:T(128)}, f32[2,2048,3,192]{1,3,2,0:T(8,128)}, s32[2]{0:T(128)S(1)}, f32[2,2048,192]{1,2,0:T(8,128)}, bf16[2048,2,3,192]{0,3,2,1:T(8,128)(2,1...) while((s32[]{:T(128)}, f32[2,2048,3,192]{1,3,2,0:T(8,128)}, ...), condition=%wide.region_55.56_spmd, body=%wide.region_38.55_spmd.sunk | while | flops 4039329792 | bytes 575293248 | solution.py:226
  1127.5 10.0 broadcast_multiply_fusion.57
  1141.0 20.6 %convolution_bitcast_fusion.8 = f32[2048,3,8,256]{0,3,2,1:T(8,128)} fusion(bf16[2048,3,64,1]{0,2,3,1:T(8,128)(2,1)} %bitcast.660, bf16[2,3,8,256,64]{3,4,2,1,0:T(8,128)(2,1)} %get-tuple-element.1105, s32[]{:T(128)S(6)} %select_n.33), kind=kOutput, calls=%fused_computation.248.clone.1 | convolution fusion | flops 1610612736 | bytes 51904516 | tf_op jit(solution)/shard_map/while/body/eval_jaxpr/lhe,htbe->lhtb/dot_general | solution.py:203
  1161.6 42.8 %multiply_reduce_fusion.56 = (f32[2048,3,8]{0,2,1:T(8,128)}, f32[2048,3,8]{0,2,1:T(8,128)}, f32[2048,3,8,128]{0,3,2,1:T(8,128)}, bf16[2048,3,8,128]{0,3,2,1:T(8,128)(2,1)}, bf16[2048,3,8,128]{0,3,2,1:T(8,128)(2,1)}) fusion(f32[2048,3,8,256]{0,3,2,1:T(8,128)} %convolution_bitcast_fusion.8, f32[2048,3,8,64]{0,3,2,1:T(8,128)} %get-tuple-element.963, ...), kind=kLoop, calls=%fused_computation.247.clone.1 | loop fusion | flops 75399168 | bytes 126615552 | tf_op jit(solution)/shard_map/while/body/eval_jaxpr/transpose(jvp())/reduce_sum | solution.py:27
  1204.3 14.8 multiply_reduce_fusion.57
  1242.8 12.0 fusion.321
  1277.9 10.0 broadcast_multiply_fusion.57
  1291.4 20.6 %convolution_bitcast_fusion.8 = f32[2048,3,8,256]{0,3,2,1:T(8,128)} fusion(bf16[2048,3,64,1]{0,2,3,1:T(8,128)(2,1)} %bitcast.660, bf16[2,3,8,256,64]{3,4,2,1,0:T(8,128)(2,1)} %get-tuple-element.1105, s32[]{:T(128)S(6)} %select_n.33), kind=kOutput, calls=%fused_computation.248.clone.1 | convolution fusion | flops 1610612736 | bytes 51904516 | tf_op jit(solution)/shard_map/while/body/eval_jaxpr/lhe,htbe->lhtb/dot_general | solution.py:203
  1312.0 42.8 %multiply_reduce_fusion.56 = (f32[2048,3,8]{0,2,1:T(8,128)}, f32[2048,3,8]{0,2,1:T(8,128)}, f32[2048,3,8,128]{0,3,2,1:T(8,128)}, bf16[2048,3,8,128]{0,3,2,1:T(8,128)(2,1)}, bf16[2048,3,8,128]{0,3,2,1:T(8,128)(2,1)}) fusion(f32[2048,3,8,256]{0,3,2,1:T(8,128)} %convolution_bitcast_fusion.8, f32[2048,3,8,64]{0,3,2,1:T(8,128)} %get-tuple-element.963, ...), kind=kLoop, calls=%fused_computation.247.clone.1 | loop fusion | flops 75399168 | bytes 126615552 | tf_op jit(solution)/shard_map/while/body/eval_jaxpr/transpose(jvp())/reduce_sum | solution.py:27
  1354.8 14.8 multiply_reduce_fusion.57
  1393.2 12.0 fusion.321
  1418.2 159.3 %reduce-scatter.5.cloned.1.call-done = f32[512,2,3,192]{0,3,2,1:T(8,128)} async-done(((f32[2048,2,3,192]{0,3,2,1:T(8,128)}), f32[512,2,3,192]{0,3,2,1:T(8,128)}) %reduce-scatter.5.cloned.1.call-update) | async-done | bytes 2359312 | tf_op jit(solution)/shard_map/reduce_scatter | solution.py:225
  1605.5 25.3 %all-reduce.32 = (f32[2,768]{1,0:T(2,128)S(1)}, f32[2,768]{1,0:T(2,128)S(1)}, f32[3]{0:T(128)S(1)}) all-reduce(f32[2,768]{1,0:T(2,128)S(1)} %pad_maximum_fusion.28, f32[2,768]{1,0:T(2,128)S(1)} %pad_maximum_fusion.29, f32[3]{0:T(128)S(1)} %pad_maximum_fusion.30), channel_id=1, replica_groups=mesh['hash'=4,'head'=4,'seq'=2] {'hash','seq'}, use_global_device_ids=true, to_apply=%region_64.65 | all-reduce | flops 3075 | bytes 24600 | tf_op jit(solution)/shard_map/psum | solution.py:241
  1632.6 38.3 %all-reduce.48.cloned.1.call-done = f32[512,2,768]{2,0,1:T(8,128)} async-done(((f32[512,2,768]{2,0,1:T(8,128)}), f32[512,2,768]{2,0,1:T(8,128)}) %all-reduce.48.cloned.1.call-update) | async-done | bytes 3145744 | tf_op jit(solution)/shard_map/psum | solution.py:233
  1677.3 148.7 %all-reduce.50.cloned.1.call-done = (f32[3,768,192]{1,2,0:T(8,128)}, f32[192,768]{1,0:T(8,128)}, f32[768,768]{1,0:T(8,128)}, f32[768,768]{1,0:T(8,128)}) async-done(((f32[3,768,192]{1,2,0:T(8,128)}, f32[192,768]{1,0:T(8,128)}, f32[768,768]{1,0:T(8,128)}, f32[768,768]{1,0:T(8,128)}), (f32[3,768,192]{1,2,0:T(8,128)}, f32[192,768]{1,0:T(8,128)}, f32[768,768]{1,0:T(8,128)}, ...) | async-done | bytes 7077904 | tf_op jit(solution)/shard_map/psum | solution.py:241
  (899 shorter events, 364.6 us)
Async XLA Ops:
  7.2 597.5 %copy-start = (bf16[2,1024,768]{2,1,0:T(8,128)(2,1)S(1)}, bf16[2,1024,768]{2,1,0:T(8,128)(2,1)}, u32[]{:S(2)}) copy-start(bf16[2,1024,768]{2,1,0:T(8,128)(2,1)} %param.27) | copy-start | bytes 9437188
  7.2 95.7 %all-gather.3.cloned.1.call-start = ((), (), s32[]{:S(2)}) async-start(), calls=%async_computation.2 | async-start | bytes 5898240 | tf_op jit(solution)/shard_map/all_gather | solution.py:85
  11.2 390.0 %reduce-scatter.3.cloned.1.call-start = ((), (), s32[]{:S(2)}) async-start(), calls=%async_computation.3 | async-start | bytes 3932160 | tf_op jit(solution)/shard_map/reduce_scatter | solution.py:109
  343.0 58.2 %copy-start.113 = (bf16[192,768]{1,0:T(8,128)(2,1)S(1)}, bf16[192,768]{1,0:T(8,128)(2,1)}, u32[]{:S(2)}) copy-start(bf16[192,768]{1,0:T(8,128)(2,1)} %param.20) | copy-start | bytes 884740
  343.0 61.7 %copy-start.134 = (f32[2,768]{1,0:T(2,128)S(1)}, f32[2,768]{1,0:T(2,128)}, u32[]{:S(2)}) copy-start(f32[2,768]{1,0:T(2,128)} %param.24) | copy-start | bytes 18436
  343.0 61.7 %copy-start.135 = (f32[2,768]{1,0:T(2,128)S(1)}, f32[2,768]{1,0:T(2,128)}, u32[]{:S(2)}) copy-start(f32[2,768]{1,0:T(2,128)} %param.23) | copy-start | bytes 18436
  343.0 149.2 %all-reduce.42.cloned.1.call-start = ((), (), s32[]{:S(2)}) async-start(), calls=%async_computation.4 | async-start | bytes 6291456 | tf_op jit(solution)/shard_map/psum | solution.py:117
  404.6 195.8 %all-reduce.44.cloned.1.call-start = ((), (), s32[]{:S(2)}) async-start(), calls=%async_computation.5 | async-start | bytes 6291456 | tf_op jit(solution)/shard_map/psum | solution.py:136
  404.7 195.7 %copy-start.128 = (f32[768]{0:T(1024)}, f32[768]{0:T(1024)S(1)}, u32[]{:S(2)}) copy-start(f32[768]{0:T(1024)S(1)} %get-tuple-element.201) | copy-start | bytes 9220
  404.8 307.5 %copy-start.117 = (f32[768]{0:T(1024)}, f32[768]{0:T(1024)S(1)}, u32[]{:S(2)}) copy-start(f32[768]{0:T(1024)S(1)} %get-tuple-element.465) | copy-start | bytes 9220
  496.5 215.8 %copy-start.115 = (f32[512,2]{0,1:T(2,128)}, f32[512,2]{0,1:T(2,128)S(1)}, u32[]{:S(2)}) copy-start(f32[512,2]{0,1:T(2,128)S(1)} %broadcast_multiply_fusion.29) | copy-start | bytes 12292
  497.0 215.3 %copy-start.119 = (f32[512,2]{0,1:T(2,128)}, f32[512,2]{0,1:T(2,128)S(1)}, u32[]{:S(2)}) copy-start(f32[512,2]{0,1:T(2,128)S(1)} %fusion.217) | copy-start | bytes 12292
  500.9 8.0 copy-start.106
  500.9 9.2 copy-start.138
  513.1 194.6 %all-reduce.46.cloned.1.call-start = ((), (), s32[]{:S(2)}) async-start(), calls=%async_computation.6 | async-start | bytes 6291456 | tf_op jit(solution)/shard_map/psum | solution.py:170
  610.3 97.4 %copy-start.132 = (f32[512,2]{0,1:T(2,128)}, f32[512,2]{0,1:T(2,128)S(1)}, u32[]{:S(2)}) copy-start(f32[512,2]{0,1:T(2,128)S(1)} %negate_multiply_fusion.2) | copy-start | bytes 12292
  620.4 87.4 %copy-start.29 = (f32[512,2,768]{2,0,1:T(8,128)S(1)}, f32[512,2,768]{2,0,1:T(8,128)}, u32[]{:S(2)}) copy-start(f32[512,2,768]{2,0,1:T(8,128)} %copy-done.28) | copy-start | bytes 9437188
  620.4 133.5 %all-gather.5.cloned.1.call-start = ((), (), s32[]{:S(2)}) async-start(), calls=%async_computation.7 | async-start | bytes 1966080 | tf_op jit(solution)/shard_map/all_gather | solution.py:209
  713.6 42.4 %copy-start.121 = (f32[512,2]{0,1:T(2,128)}, f32[512,2]{0,1:T(2,128)S(1)}, u32[]{:S(2)}) copy-start(f32[512,2]{0,1:T(2,128)S(1)} %negate_multiply_fusion.1) | copy-start | bytes 12292
  716.8 860.7 %reduce-scatter.5.cloned.1.call-start = ((), (), s32[]{:S(2)}) async-start(), calls=%async_computation.8 | async-start | bytes 11796480 | tf_op jit(solution)/shard_map/reduce_scatter | solution.py:225
  795.7 10.3 copy-start.2
  795.7 12.2 copy-start.3
  795.8 12.1 copy-start.39
  795.9 12.1 copy-start.41
  795.9 13.6 copy-start.96
  905.4 10.6 slice-start
  906.0 9.9 slice-start.1
  906.1 9.9 slice-start.2
  944.2 10.3 copy-start.2
  944.2 12.2 copy-start.3
  944.3 12.1 copy-start.39
  944.4 12.1 copy-start.41
  944.4 13.6 copy-start.96
  1053.9 10.6 slice-start
  1054.6 9.9 slice-start.1
  1054.6 9.9 slice-start.2
  1127.3 10.2 copy-start.4
  1127.3 12.1 copy-start.5
  1127.4 12.1 copy-start.40
  1127.5 12.0 copy-start.42
  1277.7 10.2 copy-start.4
  1277.7 12.1 copy-start.5
  1277.8 12.1 copy-start.40
  1277.9 12.0 copy-start.42
  1418.1 159.4 %copy-start.142 = (bf16[3,768,192]{1,2,0:T(8,128)(2,1)S(1)}, bf16[3,768,192]{1,2,0:T(8,128)(2,1)}, u32[]{:S(2)}) copy-start(bf16[3,768,192]{1,2,0:T(8,128)(2,1)} %param.19) | copy-start | bytes 2654212
  1418.1 252.8 %all-reduce.48.cloned.1.call-start = ((), (), s32[]{:S(2)}) async-start(), calls=%async_computation.9 | async-start | bytes 6291456 | tf_op jit(solution)/shard_map/psum | solution.py:233
  1582.4 243.6 %all-reduce.50.cloned.1.call-start = ((), (), s32[]{:S(2)}) async-start(), calls=%async_computation.10 | async-start | bytes 14155776 | tf_op jit(solution)/shard_map/psum | solution.py:241
  1596.9 74.0 %copy-start.34 = (f32[512,2,768]{2,0,1:T(8,128)S(1)}, f32[512,2,768]{2,0,1:T(8,128)}, u32[]{:S(2)}) copy-start(f32[512,2,768]{2,0,1:T(8,128)} %copy-done.32) | copy-start | bytes 9437188
  (216 other events, 560.8 us)
Sparse Core Ops, SparseCore 0:
  11.3 91.5 all-gather.2
  343.1 58.0 reduce-scatter.2
  404.9 87.3 all-reduce.41
  513.2 87.1 all-reduce.43
  620.5 87.2 all-reduce.45
  716.9 36.9 all-gather.4
  1418.2 159.2 reduce-scatter.4
  1582.4 88.4 all-reduce.47
  1674.1 151.7 all-reduce.49
where the time goes:
time: 1850 us; the launch traced here: 1840 us
  waiting for transfers between devices  795 us (43%)
  other arithmetic  507 us (27%)
  matrix products  265 us (14%)
  local copies, waits for them, and re-layouts  137 us (7%)
  loops' own time  69 us (4%)
  blocking collectives  51.9 us (3%)
    reduce_sum x28, other arithmetic, code_values(): codes * lower[..., bit_index:bit_index + 1]  289 us
    reduce_scatter x1, waiting for transfers between devices, shards(): lax.psum_scatter(jnp.moveaxis(lax.map(dense_one_seq, seq_ids), 0, 1), 'ha...  159 us
    psum x1, waiting for transfers between devices, shards(): lax.psum((grad_w_qkv, grad_w_out, up_gradient, down_gradient, jnp.stack([...  149 us
    mul x48, other arithmetic, code_values(): codes * lower[..., bit_index:bit_index + 1]  115 us
    all_gather x1, waiting for transfers between devices, shards(): qkv_all = lax.all_gather(qkv_own, 'hash', axis=0, tiled=True)  91.7 us
    psum x1, waiting for transfers between devices, shards(): attention_result = lax.psum(out_part, 'head')  87.5 us
    psum x1, waiting for transfers between devices, shards(): grad_normed = grad_second + lax.psum(backward_piece, 'head')  87.3 us
    psum x1, waiting for transfers between devices, shards(): feedforward_result = lax.psum(feedforward_piece, 'head')  87 us
  transfers between devices with their start and end apart: 9, of which 9 were waited for; matrix products, arithmetic and copies ran while one was open for 2% of the time, Pallas kernels for 0%

commit v1 on v0

v1 whole, which is shorter than its diff:
```python
from functools import partial

import jax
import jax.numpy as jnp
import numpy as np
from jax import lax
from jax.experimental import pallas as pl
from jax.experimental.pallas import tpu as pltpu
from jax.sharding import PartitionSpec as P

HEAD_DIM = 64
HASHES = 32
BITS = 8
SETS = 8
BUCKETS = 1 << BITS
ROWS = BUCKETS * SETS

bf16 = jnp.bfloat16
f32 = jnp.float32
NN = (((1,), (0,)), ((), ()))
NT = (((1,), (1,)), ((), ()))
TN = (((0,), (0,)), ((), ()))


def dot(a, b, dims):
    return lax.dot_general(a, b, dims, preferred_element_type=f32)


def sides(rows, planes):
    x = rows.astype(f32)
    inv = lax.rsqrt(jnp.sum(x * x, axis=0, keepdims=True) + 1e-6)
    proj = dot(planes, rows, NN) * (3.0 * inv)
    small = jnp.exp(-proj)
    upper = 1.0 / (1.0 + small)
    return inv, upper, small * upper


def products(upper, lower, first, count):
    out = None
    for i in range(first, first + count):
        lo, up = lower[SETS * i : SETS * (i + 1)], upper[SETS * i : SETS * (i + 1)]
        out = [lo, up] if out is None else [c * lo for c in out] + [c * up for c in out]
    return out


def half_codes(upper, lower):
    low = jnp.concatenate(products(upper, lower, 0, 4), axis=0).astype(bf16)
    high = [jnp.concatenate([a, a], axis=0).astype(bf16) for a in products(upper, lower, 4, 4)]
    return low, high


def code_chunk(low, high, first, count):
    return jnp.concatenate(
        [high[a] * low[16 * j : 16 * (j + 1)] for a in range(first, first + count) for j in range(8)],
        axis=0,
    )


def pull_back(rows, planes_t, inv, upper, sums):
    total = sums[BITS * SETS :][:SETS]
    grad_proj = sums[: BITS * SETS] - upper * jnp.concatenate([total] * BITS, axis=0)
    head = grad_proj.astype(bf16)
    tail = (grad_proj - head.astype(f32)).astype(bf16)
    grad_unit = dot(planes_t, jnp.concatenate([head, tail], axis=0), NN) * (3.0 * inv)
    x = rows.astype(f32)
    return grad_unit - x * (inv * inv * jnp.sum(x * grad_unit, axis=0, keepdims=True))


def both(a, b):
    return jnp.concatenate([a[...], b[...]], axis=1)


def key_kernel(planes, ka, va, kb, vb, *refs, chunk):
    start, out = (None, *refs) if len(refs) == 1 else refs
    _, upper, lower = sides(both(ka, kb), planes[...])
    low, high = half_codes(upper, lower)
    values = both(va, vb)
    for c in range(0, 16, chunk):
        at = slice(128 * c, 128 * (c + chunk))
        part = dot(code_chunk(low, high, c, chunk), values, NT)
        if start is not None:
            part = part + start[0, at, :]
        out[0, at, :] = part.astype(out.dtype)


def query_kernel(planes, qa, qb, tables, ea, eb, *, chunk):
    _, upper, lower = sides(both(qa, qb), planes[...])
    low, high = half_codes(upper, lower)
    width = qa.shape[1]
    acc = jnp.zeros((HEAD_DIM, 2 * width), f32)
    for c in range(0, 16, chunk):
        acc += dot(tables[0, 128 * c : 128 * (c + chunk), :], code_chunk(low, high, c, chunk), TN)
    acc = acc * (1.0 / HASHES)
    ea[...] = acc[:, :width].astype(ea.dtype)
    eb[...] = acc[:, width:].astype(eb.dtype)


def query_back_kernel(planes, planes_t, bits, qa, ga, qb, gb, tables, *refs, chunk):
    start, out, da, db = (None, *refs) if len(refs) == 3 else refs
    rows = both(qa, qb)
    inv, upper, lower = sides(rows, planes[...])
    low, high = half_codes(upper, lower)
    grad = both(ga, gb)
    width = qa.shape[1]
    sums = jnp.zeros((bits.shape[0], 2 * width), f32)
    for c in range(0, 16, chunk):
        at = slice(128 * c, 128 * (c + chunk))
        codes = code_chunk(low, high, c, chunk)
        part = dot(codes, grad, NT)
        if start is not None:
            part = (part + start[0, at, :]) * (1.0 / HASHES)
        out[0, at, :] = part.astype(out.dtype)
        weighted = dot(tables[0, at, :], grad, NN).astype(bf16) * codes
        sums += dot(bits[:, at], weighted, NN)
    back = pull_back(rows, planes_t[...], inv, upper, sums * (1.0 / HASHES))
    da[...] = back[:, :width].astype(da.dtype)
    db[...] = back[:, width:].astype(db.dtype)


def key_back_kernel(planes, planes_t, bits, ka, va, kb, vb, grad_tables, da, db, *, chunk):
    rows = both(ka, kb)
    inv, upper, lower = sides(rows, planes[...])
    low, high = half_codes(upper, lower)
    values = both(va, vb)
    width = ka.shape[1]
    sums = jnp.zeros((bits.shape[0], 2 * width), f32)
    grad_values = jnp.zeros((HEAD_DIM, 2 * width), f32)
    for c in range(0, 16, chunk):
        at = slice(128 * c, 128 * (c + chunk))
        codes = code_chunk(low, high, c, chunk)
        grad_values += dot(grad_tables[0, at, :], codes, TN)
        weighted = dot(grad_tables[0, at, :], values, NN).astype(bf16) * codes
        sums += dot(bits[:, at], weighted, NN)
    back = pull_back(rows, planes_t[...], inv, upper, sums)
    da[0] = back[:, :width].astype(da.dtype)
    db[0] = back[:, width:].astype(db.dtype)
    da[1] = grad_values[:, :width].astype(da.dtype)
    db[1] = grad_values[:, width:].astype(db.dtype)


def bit_rows():
    out = np.zeros((80, BUCKETS, SETS), np.float32)
    for t in range(SETS):
        for i in range(BITS):
            out[i * SETS + t, :, t] = (np.arange(BUCKETS) >> i) & 1
        out[BITS * SETS + t, :, t] = 1
    return jnp.asarray(out.reshape(80, ROWS), bf16)


def whole(*shape):
    return pl.BlockSpec(shape, lambda h: (0,) * len(shape))


def per_head(width, offset=0):
    return pl.BlockSpec((HEAD_DIM, width), lambda h: (h + offset, 0))


def table_spec():
    return pl.BlockSpec((1, ROWS, HEAD_DIM), lambda h: (h, 0, 0))


def call(kernel, heads, micros, name, in_specs, out_specs, out_shape):
    return pl.pallas_call(
        kernel,
        grid=(heads,),
        in_specs=in_specs,
        out_specs=out_specs,
        out_shape=out_shape,
        compiler_params=pltpu.CompilerParams(vmem_limit_bytes=48 << 20),
        cost_estimate=pl.CostEstimate(
            flops=int(micros * 1.1e9), bytes_accessed=4 << 20, transcendentals=0
        ),
        name=name,
    )


def key_tables(planes, kv_a, kv_b, start=None):
    heads, width = kv_a.shape[0] // (2 * HEAD_DIM), kv_a.shape[1]
    specs = [whole(64, 64)] + [per_head(width), per_head(width, heads)] * 2
    args = [planes, kv_a, kv_a, kv_b, kv_b]
    if start is not None:
        specs.append(table_spec())
        args.append(start)
    return call(
        partial(key_kernel, chunk=2),
        heads,
        10,
        "key_tables",
        specs,
        table_spec(),
        jax.ShapeDtypeStruct((heads, ROWS, HEAD_DIM), f32 if start is None else bf16),
    )(*args)


def query_estimates(planes, q_a, q_b, tables, kind_a, kind_b):
    heads, width = q_a.shape[0] // HEAD_DIM, q_a.shape[1]
    return call(
        partial(query_kernel, chunk=2),
        heads,
        7,
        "query_estimates",
        [whole(64, 64), per_head(width), per_head(width), table_spec()],
        [per_head(width), per_head(width)],
        [jax.ShapeDtypeStruct(q_a.shape, kind) for kind in (kind_a, kind_b)],
    )(planes, q_a, q_b, tables)


def query_backward(planes, planes_t, bits, q_a, g_a, q_b, g_b, tables, start, kind_a, kind_b):
    heads, width = q_a.shape[0] // HEAD_DIM, q_a.shape[1]
    specs = [whole(64, 64), whole(64, 128), whole(80, ROWS)] + [per_head(width)] * 4 + [table_spec()]
    args = [planes, planes_t, bits, q_a, g_a, q_b, g_b, tables]
    if start is not None:
        specs.append(table_spec())
        args.append(start)
    return call(
        partial(query_back_kernel, chunk=4),
        heads,
        20,
        "query_backward",
        specs,
        [table_spec(), per_head(width), per_head(width)],
        [jax.ShapeDtypeStruct((heads, ROWS, HEAD_DIM), f32 if start is None else bf16)]
        + [jax.ShapeDtypeStruct(q_a.shape, kind) for kind in (kind_a, kind_b)],
    )(*args)


def key_backward(planes, planes_t, bits, kv_a, kv_b, grad_tables, kind_a, kind_b):
    heads, width = kv_a.shape[0] // (2 * HEAD_DIM), kv_a.shape[1]
    pair = pl.BlockSpec((2, HEAD_DIM, width), lambda h: (0, h, 0))
    return call(
        partial(key_back_kernel, chunk=4),
        heads,
        18,
        "key_backward",
        [whole(64, 64), whole(64, 128), whole(80, ROWS)]
        + [per_head(width), per_head(width, heads)] * 2
        + [table_spec()],
        [pair, pair],
        [jax.ShapeDtypeStruct((2, heads * HEAD_DIM, width), kind) for kind in (kind_a, kind_b)],
    )(planes, planes_t, bits, kv_a, kv_a, kv_b, kv_b, grad_tables)


def layer_norm(values_in, gain_row, bias_row):
    center = values_in - jnp.mean(values_in, axis=-1, keepdims=True)
    spread = jnp.mean(center * center, axis=-1, keepdims=True)
    return center * lax.rsqrt(spread + 1e-05) * gain_row + bias_row


def gelu_exact(values_in):
    return jax.nn.gelu(values_in, approximate=False)


def shards(
    inputs,
    w_qkv,
    w_out,
    up_weight,
    down_weight,
    norm_gain,
    norm_bias,
    planes,
    mask_pos,
    cot_rows,
):
    own = inputs[0]
    piece, seqs, width = own.shape
    hash_count, head_count = lax.axis_size("hash"), lax.axis_size("head")
    groups, places = seqs, hash_count // seqs
    assert places == 2 and lax.axis_size("seq") == 2 and head_count == 4
    assert planes.shape[0] * hash_count == 4 * SETS
    quarter = piece // head_count
    rows = groups * quarter
    half_len = piece * hash_count
    hash_id, d, s = lax.axis_index("hash"), lax.axis_index("head"), lax.axis_index("seq")
    g, r = hash_id // places, hash_id % places

    def over_seq(x):
        return lax.ppermute(x, "seq", [(0, 1), (1, 0)])

    def over_place(x):
        return lax.ppermute(x, "hash", [(h, h ^ 1) for h in range(hash_count)])

    def over_group(x, k):
        moves = [(h, ((h // places + k) % groups) * places + h % places) for h in range(hash_count)]
        return lax.ppermute(x, "hash", moves)

    def over_head(x, j):
        return lax.ppermute(x, "head", [(h, h ^ j) for h in range(head_count)])

    def seq_rows(block, index):
        return lax.dynamic_index_in_dim(block, index % seqs, 1, keepdims=False)

    my_quarter = lax.dynamic_slice_in_dim(own, d * quarter, quarter, 0)
    arrived = [over_group(seq_rows(my_quarter, g + k), k) for k in range(1, groups)]
    dense_in = jnp.stack([seq_rows(my_quarter, g)] + arrived)
    blocks = [dense_in]
    for j in range(1, head_count):
        here = seq_rows(lax.dynamic_slice_in_dim(own, (d ^ j) * quarter, quarter, 0), g)
        blocks.append(jnp.concatenate([here[None], over_head(dense_in[1:], j)]))
    tokens = jnp.stack(blocks).reshape(head_count * rows, width)
    dense_in = dense_in.reshape(rows, width)

    signed = (2 * planes - 1).astype(bf16)
    signed = lax.all_gather(signed, "hash", axis=0, tiled=True)
    signed = lax.dynamic_slice_in_dim(signed, (r * 2 + s) * SETS, SETS, 0)
    signed = signed.transpose(1, 0, 2).reshape(BITS * SETS, HEAD_DIM)
    signed_t = jnp.concatenate([signed.T, signed.T], axis=1)
    bits = bit_rows()

    head_width = w_out.shape[0]
    n_tokens = head_count * rows

    def project(w):
        return jnp.einsum("cde,ld->cel", w, tokens, preferred_element_type=f32).astype(bf16)

    kv = project(w_qkv[1:]).reshape(2 * head_width, n_tokens)
    q = project(w_qkv[:1]).reshape(head_width, n_tokens)
    kv_o, q_o = over_seq(kv), over_seq(q)
    kv_z = over_place(kv)
    q_z = over_place(q)
    kv_zo, q_zo = over_seq(kv_z), over_seq(q_z)

    tables = key_tables(signed, kv, kv_o)
    tables = key_tables(signed, kv_z, kv_zo, tables)

    def to_owner(own_part, own_other, far_part, far_other):
        far = (far_part.astype(f32) + over_seq(far_other).astype(f32)).astype(bf16)
        far = over_place(far)
        return own_part + over_seq(own_other).astype(f32) + far.astype(f32)

    e_z, e_zo = query_estimates(signed, q_z, q_zo, tables, bf16, bf16)
    e, e_o = query_estimates(signed, q, q_o, tables, f32, bf16)
    attn = to_owner(e, e_o, e_z, e_zo).astype(bf16)

    def to_dense(block):
        parts = [block[:, j * rows : (j + 1) * rows] for j in range(head_count)]
        return jnp.concatenate([parts[0]] + [over_head(parts[j], j) for j in range(1, head_count)], 0)

    attn_t = to_dense(attn)

    packed = jnp.concatenate([up_weight.T, down_weight, w_out], axis=0)
    pack_half = packed.shape[0] // 2

    def halves(mine, other):
        first = jnp.where(s == 0, mine, other)
        second = jnp.where(s == 0, other, mine)
        return jnp.concatenate([first, second], axis=-2)

    my_half = lax.dynamic_slice_in_dim(packed, s * pack_half, pack_half, 0)
    fetched = jnp.stack([over_head(my_half, j) for j in range(1, head_count)])
    fetched = halves(fetched, over_seq(fetched))
    hidden_own = down_weight.shape[0]
    all_weights = jnp.concatenate([packed[None], fetched], axis=0)
    up_t = all_weights[:, :hidden_own].reshape(head_count * hidden_own, width)
    down = all_weights[:, hidden_own : 2 * hidden_own].reshape(head_count * hidden_own, width)
    out_w = all_weights[:, 2 * hidden_own :].reshape(head_count * head_width, width)
    qkv_w = [w_qkv] + [over_head(w_qkv, j) for j in range(1, head_count)]

    slot = jnp.arange(groups, dtype=jnp.int32)[:, None]
    place_of = ((g - slot) % groups) * places + r
    position = s * half_len + place_of * piece + d * quarter + jnp.arange(quarter, dtype=jnp.int32)[None]
    mask_row = lax.dynamic_index_in_dim(mask_pos, g, 0, keepdims=False)
    cot = lax.dynamic_index_in_dim(cot_rows, g, 0, keepdims=False)
    pick = (position.reshape(rows)[:, None] == mask_row[None]).astype(bf16)
    grad_out = jnp.dot(pick, cot, preferred_element_type=f32)

    attn_out = dot(attn_t, out_w, TN)
    resid = dense_in.astype(f32)
    first_sum = resid + attn_out
    normed_f, first_pull = jax.vjp(layer_norm, first_sum, norm_gain[0], norm_bias[0])
    normed = normed_f.astype(bf16)
    pre = dot(normed, up_t, NT)
    hidden_f, gelu_pull = jax.vjp(gelu_exact, pre)
    hidden = hidden_f.astype(bf16)
    second_sum = normed.astype(f32) + dot(hidden, down, NN)
    result, second_pull = jax.vjp(layer_norm, second_sum, norm_gain[1], norm_bias[1])

    grad_second, gain_second, bias_second = second_pull(grad_out)
    grad_ffn = grad_second.astype(bf16)
    grad_pre = gelu_pull(dot(grad_ffn, down, NT))[0].astype(bf16)
    grad_normed = grad_second + dot(grad_pre, up_t, NN)
    grad_first, gain_first, bias_first = first_pull(grad_normed)
    grad_attn = grad_first.astype(bf16)
    grad_est = dot(out_w, grad_attn, NT).astype(bf16)
    est_parts = [grad_est[j * head_width : (j + 1) * head_width] for j in range(head_count)]
    grad = jnp.concatenate(
        [est_parts[0]] + [over_head(est_parts[j], j) for j in range(1, head_count)], axis=1
    )

    grad_o = over_seq(grad)
    grad_z = over_place(grad)
    grad_zo = over_seq(grad_z)
    part, dq, dq_o = query_backward(
        signed, signed_t, bits, q, grad, q_o, grad_o, tables, None, f32, bf16
    )
    grad_tables, dq_z, dq_zo = query_backward(
        signed, signed_t, bits, q_z, grad_z, q_zo, grad_zo, tables, part, bf16, bf16
    )
    dkv_z, dkv_zo = key_backward(signed, signed_t, bits, kv_z, kv_zo, grad_tables, bf16, bf16)
    dkv, dkv_o = key_backward(signed, signed_t, bits, kv, kv_o, grad_tables, f32, bf16)
    grad_q = to_owner(dq, dq_o, dq_z, dq_zo).astype(bf16)
    grad_kv = to_owner(dkv, dkv_o, dkv_z, dkv_zo).astype(bf16)
    grad_qkv = jnp.concatenate([grad_q[None], grad_kv])

    grad_in = grad_first
    for j in range(head_count):
        block = grad_qkv[:, :, j * rows : (j + 1) * rows]
        if j:
            block = over_head(block, j)
        grad_in = grad_in + jnp.einsum("cel,cde->ld", block, qkv_w[j], preferred_element_type=f32)

    def home(dense):
        dense = dense.reshape(groups, quarter, width)
        parts = [dense[0]] + [over_group(dense[k], groups - k) for k in range(1, groups)]
        table = [jnp.stack(parts)]
        for j in range(1, head_count):
            table.append(jnp.stack([over_head(part, j) for part in parts]))
        table = jnp.stack(table)
        columns = []
        for q_at in range(head_count):
            block = lax.dynamic_index_in_dim(table, q_at ^ d, 0, keepdims=False)
            columns.append(
                jnp.stack(
                    [
                        lax.dynamic_index_in_dim(block, (at - g) % groups, 0, keepdims=False)
                        for at in range(seqs)
                    ],
                    axis=1,
                )
            )
        return jnp.concatenate(columns, axis=0)

    layer_out = home(result.astype(bf16))
    grad_inputs = home(grad_in.astype(bf16)).astype(f32)

    def over_hash_sum(x):
        half = x.shape[0] // 2
        mine = lax.dynamic_slice_in_dim(x, r * half, half, 0)
        other = over_place(lax.dynamic_slice_in_dim(x, (1 - r) * half, half, 0))
        total = mine.astype(f32) + other.astype(f32)
        total = sum(
            [total] + [over_group(total.astype(bf16), k).astype(f32) for k in range(1, groups)]
        ).astype(bf16)
        far = over_place(total)
        first, second = jnp.where(r == 0, total, far), jnp.where(r == 0, far, total)
        return jnp.concatenate([first, second], axis=0)

    def reduce_weights(parts):
        half = parts.shape[1] // 2
        parts = parts.astype(bf16)
        mine = lax.dynamic_slice_in_dim(parts, s * half, half, 1)
        other = over_seq(lax.dynamic_slice_in_dim(parts, (1 - s) * half, half, 1))
        chip = (mine.astype(f32) + other.astype(f32)).astype(bf16)
        total = sum([chip[0].astype(f32)] + [over_head(chip[j], j).astype(f32) for j in range(1, 4)])
        total = over_hash_sum(total.astype(bf16))
        return halves(total, over_seq(total)).astype(f32)

    grad_down = dot(hidden, grad_ffn, TN).reshape(head_count, hidden_own, width)
    grad_up = dot(grad_pre, normed, TN).reshape(head_count, hidden_own, width)
    grad_out_w = dot(attn_t, grad_attn, NN).reshape(head_count, head_width, width)
    down_total = reduce_weights(grad_down)
    up_total = reduce_weights(grad_up)
    out_total = reduce_weights(grad_out_w)

    grad_w_qkv = jnp.einsum("ld,cel->cde", tokens, grad_qkv, preferred_element_type=f32)
    grad_w_qkv = grad_w_qkv.reshape(3 * width, head_width).astype(bf16)
    half = grad_w_qkv.shape[0] // 2
    mine = lax.dynamic_slice_in_dim(grad_w_qkv, s * half, half, 0)
    other = over_seq(lax.dynamic_slice_in_dim(grad_w_qkv, (1 - s) * half, half, 0))
    total = over_hash_sum((mine.astype(f32) + other.astype(f32)).astype(bf16))
    grad_w_qkv = halves(total, over_seq(total)).reshape(3, width, head_width).astype(f32)

    squares = jnp.stack([jnp.sum(resid * resid), jnp.sum(attn_out * attn_out), jnp.sum(first_sum * first_sum)])
    small = jnp.concatenate(
        [gain_first, gain_second, bias_first, bias_second, jnp.pad(squares, (0, width - 3))]
    ).reshape(5, width)
    small = small + over_seq(small)
    small = small + over_head(small, 1)
    small = small + over_head(small, 2)
    small = small + over_place(small)
    small = sum([small] + [over_group(small, k) for k in range(1, groups)])
    count = piece * seqs * width * hash_count * 2
    stream_rms = jnp.sqrt(small[4, :3] / count)
    share = width // head_count
    mine = lax.dynamic_slice_in_dim(small, d * share, share, 1)
    return (
        layer_out[None],
        grad_inputs[None],
        grad_w_qkv,
        out_total,
        up_total.T,
        down_total,
        mine[0:2],
        mine[2:4],
        stream_rms,
    )


def solution(mesh):
    placed = (
        P("seq", "hash", None, None),
        P(None, None, "head"),
        P("head", None),
        P(None, "head"),
        P("head", None),
        P(),
        P(),
        P("hash", None, None),
        P(),
        P(),
    )
    return jax.shard_map(
        shards,
        mesh=mesh,
        in_specs=placed,
        out_specs=(
            P("seq", "hash", None, None),
            P("seq", "hash", None, None),
            P(None, None, "head"),
            P("head", None),
            P(None, "head"),
            P("head", None),
            P(None, "head"),
            P(None, "head"),
            P(),
        ),
        check_vma=False,
    )
```

time: 1850 us -> 567 us (0.31)
  waiting for transfers between devices: 795 us -> 218 us
  other arithmetic: 507 us -> 49.5 us
  matrix products: 265 us -> 30.7 us
  Pallas kernels: 0 us -> 110 us
  starting transfers between devices: 0.87 us -> 105 us
  local copies, waits for them, and re-layouts: 137 us -> 33.6 us
  loops' own time: 69 us -> 0 us
  blocking collectives: 51.9 us -> 13.5 us
    psum x5 -> x0, waiting for transfers between devices: 449 us -> none  [the longest x1 149 us: shards(): lax.psum((grad_w_qkv, grad_w_out, up_gradient, down_gradient, jnp.stack([...]
    reduce_sum x38 -> x1, other arithmetic: 297 us -> 1.73 us  [shards(): jnp.sum(resid * resid)]
    dot_general x37 -> x16, matrix products: 265 us -> 29.9 us  [the longest x9 24.5 us: dot(): return lax.dot_general(a, b, dims, preferred_element_type=f32)]
    ppermute x0 -> x86, waiting for transfers between devices: none -> 218 us  [the longest x41 145 us: over_head(): return lax.ppermute(x, 'head', [(h, h ^ j) for h in range(head_count)])]
    reduce_scatter x2 -> x0, waiting for transfers between devices: 217 us -> none  [the longest x1 159 us: shards(): lax.psum_scatter(jnp.moveaxis(lax.map(dense_one_seq, seq_ids), 0, 1), 'ha...]
    all_gather x2 -> x0, waiting for transfers between devices: 129 us -> none  [the longest x1 91.7 us: shards(): qkv_all = lax.all_gather(qkv_own, 'hash', axis=0, tiled=True)]
    mul x52 -> x0, other arithmetic: 116 us -> none  [the longest x48 115 us: code_values(): codes * lower[..., bit_index:bit_index + 1]]
    pallas_call x0 -> x8, Pallas kernels: none -> 110 us  [the longest x2 41.1 us: query_backward(): call(partial(query_back_kernel, chunk=4), heads, 20, 'query_backward', sp...]
  transfers between devices with their start and end apart: 9 -> 86, of which waited for: 9 -> 30; matrix products, arithmetic and copies ran while one was open for 2% -> 13% of each run, Pallas kernels for 0% -> 19%
where the time goes in v1:
time: 567 us; the launch traced here: 562 us
  waiting for transfers between devices  218 us (38%)
  Pallas kernels  110 us (19%)
  starting transfers between devices  105 us (19%)
  other arithmetic  49.5 us (9%)
  local copies, waits for them, and re-layouts  33.6 us (6%)
  matrix products  30.7 us (5%)
  blocking collectives  13.5 us (2%)
    ppermute x41, waiting for transfers between devices, over_head(): return lax.ppermute(x, 'head', [(h, h ^ j) for h in range(head_count)])  145 us
    pallas_call x2, Pallas kernels, query_backward(): call(partial(query_back_kernel, chunk=4), heads, 20, 'query_backward', sp...  41.1 us
    ppermute x15, waiting for transfers between devices, over_place(): return lax.ppermute(x, 'hash', [(h, h ^ 1) for h in range(hash_count)])  40.8 us
    ppermute x41, starting transfers between devices, over_head(): return lax.ppermute(x, 'head', [(h, h ^ j) for h in range(head_count)])  40.5 us
    ppermute x22, starting transfers between devices, over_seq(): return lax.ppermute(x, 'seq', [(0, 1), (1, 0)])  37.6 us
    pallas_call x2, Pallas kernels, key_backward(): call(partial(key_back_kernel, chunk=4), heads, 18, 'key_backward', [whole...  36.8 us
    ppermute x8, waiting for transfers between devices, over_group(): return lax.ppermute(x, 'hash', moves)  29.4 us
    dot_general x9, matrix products, dot(): return lax.dot_general(a, b, dims, preferred_element_type=f32)  24.5 us
  transfers between devices with their start and end apart: 86, of which 30 were waited for; matrix products, arithmetic and copies ran while one was open for 13% of the time, Pallas kernels for 19%

profile of v1, /device:TPU:1, one launch (start us, length us, event | category | flops | bytes accessed | tf_op | source)
XLA Modules:
  0.0 562.2 jit_solution(2740440198831385776)
XLA Ops:
  0.8 4.5 constant_dynamic-slice_fusion.15
  6.0 3.1 collective-permute-start
  11.5 4.0 pad_maximum_fusion.4
  26.3 59.4 %collective-permute-done.2 = bf16[1,128,768]{2,1,0:T(8,128)(2,1)S(1)} collective-permute-done((bf16[1,128,768]{2,1,0:T(8,128)(2,1)}, bf16[1,128,768]{2,1,0:T(8,128)(2,1)S(1)}, u32[]{:S(2)}, u32[]{:S(2)}) %collective-permute-start.2) | collective-permute-done | bytes 196640 | tf_op jit(solution)/shard_map/ppermute | solution.py:288
  86.0 4.4 collective-permute-done.1
  95.4 4.2 collective-permute-done.9.qa
  99.6 8.1 %collective-permute-start.7 = (bf16[384,1024]{1,0:T(8,128)(2,1)}, bf16[384,1024]{1,0:T(8,128)(2,1)}, u32[]{:S(2)}, u32[]{:S(2)}) collective-permute-start(bf16[384,1024]{1,0:T(8,128)(2,1)} %bitcast.21.ka.va), channel_id=1, source_target_pairs={{0,1},{1,0},{2,3},{3,2},{4,5},{5,4},{6,7},{7,6},{8,9},{9,8},{10,11... | collective-permute-start | bytes 2359304 | tf_op jit(solution)/shard_map/ppermute | solution.py:278
  108.4 13.5 %all_gather.3 = bf16[32,8,64]{2,0,1:T(8,128)(2,1)S(1)} all-gather(bf16[8,8,64]{2,0,1:T(8,128)(2,1)S(1)} %fusion.44), channel_id=1, replica_groups=mesh['hash'=4,'head'=4,'seq'=2] {'hash'}, dimensions={0}, use_global_device_ids=true | all-gather | bytes 40960 | tf_op jit(solution)/shard_map/all_gather | solution.py:304
  122.2 5.3 collective-permute-start.4
  128.1 3.7 pad_maximum_fusion.3
  131.8 8.9 %key_tables.2.refs_0_ = f32[3,2048,64]{2,1,0:T(8,128)S(1)} custom-call(bf16[64,64]{1,0:T(8,128)(2,1)S(1)} %dynamic-slice_bitcast_fusion.16.planes, bf16[384,1024]{1,0:T(8,128)(2,1)} %bitcast.21.ka.va, bf16[384,1024]{1,0:T(8,128)(2,1)} %bitcast.21.ka.va, bf16[384,1024]{1,0:T(8,128)(2,1)} %collective-permute-done.7.kb.vb, ...), custom_call_target="tpu_custom_call" | custom-call | flops 11000000512 | bytes 4194304 | tf_op jit(solution)/shard_map/key_tables/pallas_call | solution.py:184
  142.4 9.5 %key_tables.3.tables = bf16[3,2048,64]{2,1,0:T(8,128)(2,1)S(1)} custom-call(bf16[64,64]{1,0:T(8,128)(2,1)S(1)} %dynamic-slice_bitcast_fusion.16.planes, bf16[384,1024]{1,0:T(8,128)(2,1)} %collective-permute-done.5.ka.va, bf16[384,1024]{1,0:T(8,128)(2,1)} %collective-permute-done.5.ka.va, bf16[384,1024]{1,0:T(8,128)(2,1)S(1)} %collective-permute-done.6.kb.vb, ...), custom_call_target="tpu_custom_call" | custom-call | flops 11000000512 | bytes 4194304 | tf_op jit(solution)/shard_map/key_tables/pallas_call | solution.py:184
  152.0 5.8 %query_estimates.3 = (bf16[192,1024]{1,0:T(8,128)(2,1)S(1)}, bf16[192,1024]{1,0:T(8,128)(2,1)S(1)}) custom-call(bf16[64,64]{1,0:T(8,128)(2,1)S(1)} %dynamic-slice_bitcast_fusion.16.planes, bf16[192,1024]{1,0:T(8,128)(2,1)S(1)} %copy-done.6, bf16[192,1024]{1,0:T(8,128)(2,1)S(1)} %collective-permute-done.10.qb, bf16[3,2048,64]{2,1,0:T(8,128)(2,1)S(1)} %key_tables.3.tables), custom_call_target="tpu_custom_call" | custom-call | flops 7699999744 | bytes 4194304 | tf_op jit(solution)/shard_map/query_estimates/pallas_call | solution.py:197
  158.3 7.5 %query_estimates.2 = (f32[192,1024]{1,0:T(8,128)S(1)}, bf16[192,1024]{1,0:T(8,128)(2,1)}) custom-call(bf16[64,64]{1,0:T(8,128)(2,1)S(1)} %dynamic-slice_bitcast_fusion.16.planes, bf16[192,1024]{1,0:T(8,128)(2,1)} %fusion.15.qa, bf16[192,1024]{1,0:T(8,128)(2,1)S(1)} %collective-permute-done.4.qb, bf16[3,2048,64]{2,1,0:T(8,128)(2,1)S(1)} %key_tables.3.tables), custom_call_target="tpu_custom_call" | custom-call | flops 7699999744 | bytes 4194304 | tf_op jit(solution)/shard_map/query_estimates/pallas_call | solution.py:197
  170.7 7.5 %collective-permute-done.12 = bf16[192,1024]{1,0:T(8,128)(2,1)} collective-permute-done((bf16[192,1024]{1,0:T(8,128)(2,1)}, bf16[192,1024]{1,0:T(8,128)(2,1)}, u32[]{:S(2)}, u32[]{:S(2)}) %collective-permute-start.12) | collective-permute-done | bytes 393248 | tf_op jit(solution)/shard_map/ppermute | solution.py:281
  182.5 3.6 broadcast_select_fusion.1
  186.1 7.4 %pad_maximum_fusion = (bf16[4,768,768]{2,1,0:T(8,128)(2,1)S(1)}, bf16[4,768,768]{2,1,0:T(8,128)(2,1)S(1)}) fusion(bf16[1,1728,768]{2,1,0:T(8,128)(2,1)S(1)} %copy-done.17, bf16[3,864,768]{2,1,0:T(8,128)(2,1)S(1)} %get-tuple-element.77, bf16[3,864,768]{2,1,0:T(8,128)(2,1)S(1)} %get-tuple-element.76), kind=kLoop, calls=%fused_computation.3 | loop fusion | flops 28311552 | bytes 20054016 | tf_op jit(solution)/shard_map/concatenate | solution.py:353
  196.4 7.7 %multiply_convert_fusion = (bf16[256,3072]{1,0:T(8,128)(2,1)S(1)}, f32[256,3072]{1,0:T(8,128)S(1)}, f32[256,3072]{1,0:T(8,128)S(1)}) fusion(bf16[3072,768]{1,0:T(8,128)(2,1)S(1)} %bitcast.241, f32[256,768]{1,0:T(8,128)S(1)} %get-tuple-element.73, f32[768]{0:T(1024)S(1)} %get-tuple-element.65, f32[768]{0:T(1024)S(1)} %get-tuple-element.156, ...), kind=kOutput, calls=%fused_computation.13 | convolution fusion | flops 1260060672 | bytes 13377536 | tf_op jit(solution)/shard_map/dot_general | solution.py:26
  207.2 4.0 convolution_convert_fusion
  213.3 3.1 multiply_reduce_fusion.4
  216.4 3.8 convolution_convert_fusion.1
  226.7 3.4 constant_dynamic-slice_fusion.2
  240.7 3.0 collective-permute-start.85
  243.7 4.3 collective-permute-done.85
  250.4 4.9 collective-permute-start.57
  258.5 3.8 collective-permute-done.22
  264.8 7.0 %collective-permute-done.24 = bf16[128,768]{1,0:T(8,128)(2,1)S(1)} collective-permute-done((bf16[128,768]{1,0:T(8,128)(2,1)S(1)}, bf16[128,768]{1,0:T(8,128)(2,1)S(1)}, u32[]{:S(2)}, u32[]{:S(2)}) %collective-permute-start.24) | collective-permute-done | bytes 196640 | tf_op jit(solution)/shard_map/ppermute | solution.py:288
  287.4 5.1 collective-permute-start.33
  292.7 21.0 %query_backward.2 = (f32[3,2048,64]{2,1,0:T(8,128)}, f32[192,1024]{1,0:T(8,128)S(1)}, bf16[192,1024]{1,0:T(8,128)(2,1)S(1)}) custom-call(bf16[64,64]{1,0:T(8,128)(2,1)S(1)} %dynamic-slice_bitcast_fusion.16.planes, bf16[64,128]{1,0:T(8,128)(2,1)S(1)} %pad_maximum_fusion.20.planes_t, bf16[80,2048]{1,0:T(8,128)(2,1)S(1)} %copy-done.12, ...), custom_call_target="tpu_custom_call" | custom-call | flops 22000001024 | bytes 4194304 | tf_op jit(solution)/shard_map/query_backward/pallas_call | solution.py:215
  316.1 20.1 %query_backward.3 = (bf16[3,2048,64]{2,1,0:T(8,128)(2,1)S(1)}, bf16[192,1024]{1,0:T(8,128)(2,1)S(1)}, bf16[192,1024]{1,0:T(8,128)(2,1)S(1)}) custom-call(bf16[64,64]{1,0:T(8,128)(2,1)S(1)} %dynamic-slice_bitcast_fusion.16.planes, bf16[64,128]{1,0:T(8,128)(2,1)S(1)} %pad_maximum_fusion.20.planes_t, bf16[80,2048]{1,0:T(8,128)(2,1)S(1)} %copy-done.12, ...), custom_call_target="tpu_custom_call" | custom-call | flops 22000001024 | bytes 4194304 | tf_op jit(solution)/shard_map/query_backward/pallas_call | solution.py:215
  336.5 18.2 %key_backward.3 = (bf16[2,192,1024]{2,1,0:T(8,128)(2,1)S(1)}, bf16[2,192,1024]{2,1,0:T(8,128)(2,1)S(1)}) custom-call(bf16[64,64]{1,0:T(8,128)(2,1)S(1)} %dynamic-slice_bitcast_fusion.16.planes, bf16[64,128]{1,0:T(8,128)(2,1)S(1)} %pad_maximum_fusion.20.planes_t, bf16[80,2048]{1,0:T(8,128)(2,1)S(1)} %copy-done.12, ...), custom_call_target="tpu_custom_call" | custom-call | flops 19800000512 | bytes 4194304 | tf_op jit(solution)/shard_map/key_backward/pallas_call | solution.py:230
  357.3 18.6 %key_backward.2 = (f32[2,192,1024]{2,1,0:T(8,128)S(1)}, bf16[2,192,1024]{2,1,0:T(8,128)(2,1)S(1)}) custom-call(bf16[64,64]{1,0:T(8,128)(2,1)S(1)} %dynamic-slice_bitcast_fusion.16.planes, bf16[64,128]{1,0:T(8,128)(2,1)S(1)} %pad_maximum_fusion.20.planes_t, bf16[80,2048]{1,0:T(8,128)(2,1)S(1)} %copy-done.12, bf16[384,1024]{1,0:T(8,128)(2,1)} %bitcast.21.ka.va, ...), custom_call_target="tpu_custom_call" | custom-call | flops 19800000512 | bytes 4194304 | tf_op jit(solution)/shard_map/key_backward/pallas_call | solution.py:230
  376.8 4.4 collective-permute-start.44
  390.7 12.4 %collective-permute-done.38 = bf16[2,192,1024]{2,1,0:T(8,128)(2,1)S(1)} collective-permute-done((bf16[2,192,1024]{2,1,0:T(8,128)(2,1)S(1)}, bf16[2,192,1024]{2,1,0:T(8,128)(2,1)S(1)}, u32[]{:S(2)}, u32[]{:S(2)}) %collective-permute-start.38) | collective-permute-done | bytes 786464 | tf_op jit(solution)/shard_map/ppermute | solution.py:281
  407.9 18.3 %collective-permute-done.43 = bf16[3,192,256]{2,1,0:T(8,128)(2,1)S(1)} collective-permute-done((bf16[3,192,256]{2,1,0:T(8,128)(2,1)S(1)}, bf16[3,192,256]{2,1,0:T(8,128)(2,1)S(1)}, u32[]{:S(2)}, u32[]{:S(2)}) %collective-permute-start.43) | collective-permute-done | bytes 294944 | tf_op jit(solution)/shard_map/ppermute | solution.py:288
  429.1 3.9 collective-permute-done.41
  436.0 9.5 %collective-permute-done.39 = bf16[3,192,256]{2,1,0:T(8,128)(2,1)S(1)} collective-permute-done((bf16[3,192,256]{2,1,0:T(8,128)(2,1)S(1)}, bf16[3,192,256]{2,1,0:T(8,128)(2,1)S(1)}, u32[]{:S(2)}, u32[]{:S(2)}) %collective-permute-start.39) | collective-permute-done | bytes 294944 | tf_op jit(solution)/shard_map/ppermute | solution.py:288
  453.6 4.2 collective-permute-done.76
  458.7 12.0 %collective-permute-done.66 = bf16[384,768]{1,0:T(8,128)(2,1)S(1)} collective-permute-done((bf16[384,768]{1,0:T(8,128)(2,1)S(1)}, bf16[384,768]{1,0:T(8,128)(2,1)S(1)}, u32[]{:S(2)}, u32[]{:S(2)}) %collective-permute-start.66) | collective-permute-done | bytes 589856 | tf_op jit(solution)/shard_map/ppermute | solution.py:288
  474.3 8.9 %collective-permute-done.68 = bf16[384,768]{1,0:T(8,128)(2,1)S(1)} collective-permute-done((bf16[384,768]{1,0:T(8,128)(2,1)S(1)}, bf16[384,768]{1,0:T(8,128)(2,1)S(1)}, u32[]{:S(2)}, u32[]{:S(2)}) %collective-permute-start.68) | collective-permute-done | bytes 589856 | tf_op jit(solution)/shard_map/ppermute | solution.py:288
  485.6 3.3 collective-permute-done.53
  491.6 4.4 collective-permute-done.47
  502.8 4.1 copy.41
  513.6 19.0 %collective-permute-done.78 = bf16[192,768]{1,0:T(8,128)(2,1)S(1)} collective-permute-done((bf16[192,768]{1,0:T(8,128)(2,1)S(1)}, bf16[192,768]{1,0:T(8,128)(2,1)S(1)}, u32[]{:S(2)}, u32[]{:S(2)}) %collective-permute-start.78) | collective-permute-done | bytes 294944 | tf_op jit(solution)/shard_map/ppermute | solution.py:285
  532.8 6.2 %collective-permute-done.70 = bf16[192,768]{1,0:T(8,128)(2,1)S(1)} collective-permute-done((bf16[192,768]{1,0:T(8,128)(2,1)S(1)}, bf16[192,768]{1,0:T(8,128)(2,1)S(1)}, u32[]{:S(2)}, u32[]{:S(2)}) %collective-permute-start.70) | collective-permute-done | bytes 294944 | tf_op jit(solution)/shard_map/ppermute | solution.py:285
  540.0 5.2 collective-permute-done.79
  546.8 4.8 collective-permute-done.71
  555.8 3.2 copy.43
  (366 shorter events, 147.6 us)
Async XLA Ops:
  6.0 14.7 %collective-permute-start = (bf16[128,768]{1,0:T(8,128)(2,1)}, bf16[128,768]{1,0:T(8,128)(2,1)}, u32[]{:S(2)}, u32[]{:S(2)}) collective-permute-start(bf16[128,768]{1,0:T(8,128)(2,1)} %bitcast.228), channel_id=1, source_target_pairs={{0,16},{8,24},{16,0},{24,8},{1,17},{9,25},{17,1},{25,9},{2,18},{10... | collective-permute-start | bytes 589832 | tf_op jit(solution)/shard_map/ppermute | solution.py:285
  18.0 109.5 %collective-permute-start.16 = (bf16[864,768]{1,0:T(8,128)(2,1)}, bf16[864,768]{1,0:T(8,128)(2,1)}, u32[]{:S(2)}, u32[]{:S(2)}) collective-permute-start(bf16[864,768]{1,0:T(8,128)(2,1)} %constant_dynamic-slice_fusion.10), channel_id=1, source_target_pairs={{0,2},{2,0},{4,6},{6,4},{1,3},{3,1},{5,7},{7,5},{8,10},{10,8},{12,... | collective-permute-start | bytes 3981320 | tf_op jit(solution)/shard_map/ppermute | solution.py:288
  19.2 108.4 %collective-permute-start.17 = (bf16[864,768]{1,0:T(8,128)(2,1)}, bf16[864,768]{1,0:T(8,128)(2,1)}, u32[]{:S(2)}, u32[]{:S(2)}) collective-permute-start(bf16[864,768]{1,0:T(8,128)(2,1)} %constant_dynamic-slice_fusion.10), channel_id=1, source_target_pairs={{0,4},{2,6},{4,0},{6,2},{1,5},{3,7},{5,1},{7,3},{8,12},{10,14},{12... | collective-permute-start | bytes 3981320 | tf_op jit(solution)/shard_map/ppermute | solution.py:288
  20.4 107.6 %collective-permute-start.18 = (bf16[864,768]{1,0:T(8,128)(2,1)}, bf16[864,768]{1,0:T(8,128)(2,1)}, u32[]{:S(2)}, u32[]{:S(2)}) collective-permute-start(bf16[864,768]{1,0:T(8,128)(2,1)} %constant_dynamic-slice_fusion.10), channel_id=1, source_target_pairs={{0,6},{2,4},{4,2},{6,0},{1,7},{3,5},{5,3},{7,1},{8,14},{10,12},{12... | collective-permute-start | bytes 3981320 | tf_op jit(solution)/shard_map/ppermute | solution.py:288
  20.6 65.0 %collective-permute-start.2 = (bf16[1,128,768]{2,1,0:T(8,128)(2,1)}, bf16[1,128,768]{2,1,0:T(8,128)(2,1)S(1)}, u32[]{:S(2)}, u32[]{:S(2)}) collective-permute-start(bf16[1,128,768]{2,1,0:T(8,128)(2,1)} %bitcast.2), channel_id=1, source_target_pairs={{0,4},{2,6},{4,0},{6,2},{1,5},{3,7},{5,1},{7,3},{8,12},{10,14},{12... | collective-permute-start | bytes 589832 | tf_op jit(solution)/shard_map/ppermute | solution.py:288
  23.1 62.8 %collective-permute-start.3 = (bf16[1,128,768]{2,1,0:T(8,128)(2,1)}, bf16[1,128,768]{2,1,0:T(8,128)(2,1)S(1)}, u32[]{:S(2)}, u32[]{:S(2)}) collective-permute-start(bf16[1,128,768]{2,1,0:T(8,128)(2,1)} %bitcast.2), channel_id=1, source_target_pairs={{0,6},{2,4},{4,2},{6,0},{1,7},{3,5},{5,3},{7,1},{8,14},{10,12},{12... | collective-permute-start | bytes 589832 | tf_op jit(solution)/shard_map/ppermute | solution.py:288
  95.2 27.0 %collective-permute-start.5 = (bf16[384,1024]{1,0:T(8,128)(2,1)}, bf16[384,1024]{1,0:T(8,128)(2,1)}, u32[]{:S(2)}, u32[]{:S(2)}) collective-permute-start(bf16[384,1024]{1,0:T(8,128)(2,1)} %bitcast.21.ka.va), channel_id=1, source_target_pairs={{0,8},{8,0},{16,24},{24,16},{1,9},{9,1},{17,25},{25,17},{2,10},{10... | collective-permute-start | bytes 2359304 | tf_op jit(solution)/shard_map/ppermute | solution.py:281
  99.6 32.2 %collective-permute-start.7 = (bf16[384,1024]{1,0:T(8,128)(2,1)}, bf16[384,1024]{1,0:T(8,128)(2,1)}, u32[]{:S(2)}, u32[]{:S(2)}) collective-permute-start(bf16[384,1024]{1,0:T(8,128)(2,1)} %bitcast.21.ka.va), channel_id=1, source_target_pairs={{0,1},{1,0},{2,3},{3,2},{4,5},{5,4},{6,7},{7,6},{8,9},{9,8},{10,11... | collective-permute-start | bytes 2359304 | tf_op jit(solution)/shard_map/ppermute | solution.py:278
  122.2 36.1 %collective-permute-start.4 = (bf16[192,1024]{1,0:T(8,128)(2,1)}, bf16[192,1024]{1,0:T(8,128)(2,1)S(1)}, u32[]{:S(2)}, u32[]{:S(2)}) collective-permute-start(bf16[192,1024]{1,0:T(8,128)(2,1)} %fusion.15.qa), channel_id=1, source_target_pairs={{0,1},{1,0},{2,3},{3,2},{4,5},{5,4},{6,7},{7,6},{8,9},{9,8},{10,11... | collective-permute-start | bytes 1179656 | tf_op jit(solution)/shard_map/ppermute | solution.py:278
  127.5 24.5 %collective-permute-start.10 = (bf16[192,1024]{1,0:T(8,128)(2,1)}, bf16[192,1024]{1,0:T(8,128)(2,1)S(1)}, u32[]{:S(2)}, u32[]{:S(2)}) collective-permute-start(bf16[192,1024]{1,0:T(8,128)(2,1)} %copy-done.5), channel_id=1, source_target_pairs={{0,1},{1,0},{2,3},{3,2},{4,5},{5,4},{6,7},{7,6},{8,9},{9,8},{10,11... | collective-permute-start | bytes 1179656 | tf_op jit(solution)/shard_map/ppermute | solution.py:278
  127.6 14.8 %collective-permute-start.6 = (bf16[384,1024]{1,0:T(8,128)(2,1)}, bf16[384,1024]{1,0:T(8,128)(2,1)S(1)}, u32[]{:S(2)}, u32[]{:S(2)}) collective-permute-start(bf16[384,1024]{1,0:T(8,128)(2,1)} %collective-permute-done.5.ka.va), channel_id=1, source_target_pairs={{0,1},{1,0},{2,3},{3,2},{4,5},{5,4},{6,7},{7,6},{8,9},{9,8},{10,11... | collective-permute-start | bytes 2359304 | tf_op jit(solution)/shard_map/ppermute | solution.py:278
  131.7 50.8 %collective-permute-start.19 = (bf16[3,864,768]{2,1,0:T(8,128)(2,1)}, bf16[3,864,768]{2,1,0:T(8,128)(2,1)}, u32[]{:S(2)}, u32[]{:S(2)}) collective-permute-start(bf16[3,864,768]{2,1,0:T(8,128)(2,1)} %pad_maximum_fusion.3), channel_id=1, source_target_pairs={{0,1},{1,0},{2,3},{3,2},{4,5},{5,4},{6,7},{7,6},{8,9},{9,8},{10,11... | collective-permute-start | bytes 11943944 | tf_op jit(solution)/shard_map/ppermute | solution.py:278
  232.0 18.4 %collective-permute-start.27 = (bf16[192,256]{1,0:T(8,128)(2,1)S(1)}, bf16[192,256]{1,0:T(8,128)(2,1)S(1)}, u32[]{:S(2)}, u32[]{:S(2)}) collective-permute-start(bf16[192,256]{1,0:T(8,128)(2,1)S(1)} %get-tuple-element.133), channel_id=1, source_target_pairs={{0,2},{2,0},{4,6},{6,4},{1,3},{3,1},{5,7},{7,5},{8,10},{10,8},{12,... | collective-permute-start | bytes 294920 | tf_op jit(solution)/shard_map/ppermute | solution.py:288
  233.2 17.1 %collective-permute-start.28 = (bf16[192,256]{1,0:T(8,128)(2,1)S(1)}, bf16[192,256]{1,0:T(8,128)(2,1)S(1)}, u32[]{:S(2)}, u32[]{:S(2)}) collective-permute-start(bf16[192,256]{1,0:T(8,128)(2,1)S(1)} %get-tuple-element.132), channel_id=1, source_target_pairs={{0,4},{2,6},{4,0},{6,2},{1,5},{3,7},{5,1},{7,3},{8,12},{10,14},{12... | collective-permute-start | bytes 294920 | tf_op jit(solution)/shard_map/ppermute | solution.py:288
  234.5 22.6 %collective-permute-start.29 = (bf16[192,256]{1,0:T(8,128)(2,1)S(1)}, bf16[192,256]{1,0:T(8,128)(2,1)S(1)}, u32[]{:S(2)}, u32[]{:S(2)}) collective-permute-start(bf16[192,256]{1,0:T(8,128)(2,1)S(1)} %get-tuple-element.131), channel_id=1, source_target_pairs={{0,6},{2,4},{4,2},{6,0},{1,7},{3,5},{5,3},{7,1},{8,14},{10,12},{12... | collective-permute-start | bytes 294920 | tf_op jit(solution)/shard_map/ppermute | solution.py:288
  236.0 19.3 %collective-permute-start.20 = (bf16[128,768]{1,0:T(8,128)(2,1)S(1)}, bf16[128,768]{1,0:T(8,128)(2,1)S(1)}, u32[]{:S(2)}, u32[]{:S(2)}) collective-permute-start(bf16[128,768]{1,0:T(8,128)(2,1)S(1)} %get-tuple-element.135), channel_id=1, source_target_pairs={{0,16},{8,24},{16,0},{24,8},{1,17},{9,25},{17,1},{25,9},{2,18},{10... | collective-permute-start | bytes 589832 | tf_op jit(solution)/shard_map/ppermute | solution.py:285
  250.4 22.9 %collective-permute-start.57 = (bf16[4,96,768]{2,1,0:T(8,128)(2,1)S(1)}, bf16[4,96,768]{2,1,0:T(8,128)(2,1)S(1)}, u32[]{:S(2)}, u32[]{:S(2)}) collective-permute-start(bf16[4,96,768]{2,1,0:T(8,128)(2,1)S(1)} %constant_dynamic-slice_fusion.6), channel_id=1, source_target_pairs={{0,1},{1,0},{2,3},{3,2},{4,5},{5,4},{6,7},{7,6},{8,9},{9,8},{10,11... | collective-permute-start | bytes 1769480 | tf_op jit(solution)/shard_map/ppermute | solution.py:278
  257.3 15.7 %collective-permute-start.25 = (bf16[128,768]{1,0:T(8,128)(2,1)S(1)}, bf16[128,768]{1,0:T(8,128)(2,1)S(1)}, u32[]{:S(2)}, u32[]{:S(2)}) collective-permute-start(bf16[128,768]{1,0:T(8,128)(2,1)S(1)} %get-tuple-element.136), channel_id=1, source_target_pairs={{0,6},{2,4},{4,2},{6,0},{1,7},{3,5},{5,3},{7,1},{8,14},{10,12},{12... | collective-permute-start | bytes 589832 | tf_op jit(solution)/shard_map/ppermute | solution.py:288
  263.1 120.7 %collective-permute-start.73 = (bf16[4,384,768]{2,1,0:T(8,128)(2,1)}, bf16[4,384,768]{2,1,0:T(8,128)(2,1)}, u32[]{:S(2)}, u32[]{:S(2)}) collective-permute-start(bf16[4,384,768]{2,1,0:T(8,128)(2,1)} %constant_dynamic-slice_fusion.2), channel_id=1, source_target_pairs={{0,1},{1,0},{2,3},{3,2},{4,5},{5,4},{6,7},{7,6},{8,9},{9,8},{10,11... | collective-permute-start | bytes 7077896 | tf_op jit(solution)/shard_map/ppermute | solution.py:278
  271.7 115.9 %collective-permute-start.65 = (bf16[4,384,768]{2,1,0:T(8,128)(2,1)}, bf16[4,384,768]{2,1,0:T(8,128)(2,1)}, u32[]{:S(2)}, u32[]{:S(2)}) collective-permute-start(bf16[4,384,768]{2,1,0:T(8,128)(2,1)} %constant_dynamic-slice_fusion.4), channel_id=1, source_target_pairs={{0,1},{1,0},{2,3},{3,2},{4,5},{5,4},{6,7},{7,6},{8,9},{9,8},{10,11... | collective-permute-start | bytes 7077896 | tf_op jit(solution)/shard_map/ppermute | solution.py:278
  287.4 28.7 %collective-permute-start.33 = (bf16[192,1024]{1,0:T(8,128)(2,1)S(1)}, bf16[192,1024]{1,0:T(8,128)(2,1)S(1)}, u32[]{:S(2)}, u32[]{:S(2)}) collective-permute-start(bf16[192,1024]{1,0:T(8,128)(2,1)S(1)} %collective-permute-done.32.ga), channel_id=1, source_target_pairs={{0,1},{1,0},{2,3},{3,2},{4,5},{5,4},{6,7},{7,6},{8,9},{9,8},{10,11... | collective-permute-start | bytes 1179656 | tf_op jit(solution)/shard_map/ppermute | solution.py:278
  292.5 21.9 %collective-permute-start.62 = (bf16[48,768]{1,0:T(8,128)(2,1)S(1)}, bf16[48,768]{1,0:T(8,128)(2,1)S(1)}, u32[]{:S(2)}, u32[]{:S(2)}) collective-permute-start(bf16[48,768]{1,0:T(8,128)(2,1)S(1)} %fusion.41), channel_id=1, source_target_pairs={{0,16},{8,24},{16,0},{24,8},{1,17},{9,25},{17,1},{25,9},{2,18},{10... | collective-permute-start | bytes 221192 | tf_op jit(solution)/shard_map/ppermute | solution.py:285
  313.6 63.2 %collective-permute-start.31 = (bf16[192,1024]{1,0:T(8,128)(2,1)S(1)}, bf16[192,1024]{1,0:T(8,128)(2,1)}, u32[]{:S(2)}, u32[]{:S(2)}) collective-permute-start(bf16[192,1024]{1,0:T(8,128)(2,1)S(1)} %get-tuple-element.28), channel_id=1, source_target_pairs={{0,1},{1,0},{2,3},{3,2},{4,5},{5,4},{6,7},{7,6},{8,9},{9,8},{10,11... | collective-permute-start | bytes 1179656 | tf_op jit(solution)/shard_map/ppermute | solution.py:278
  314.5 40.2 %collective-permute-start.63 = (bf16[48,768]{1,0:T(8,128)(2,1)S(1)}, bf16[48,768]{1,0:T(8,128)(2,1)S(1)}, u32[]{:S(2)}, u32[]{:S(2)}) collective-permute-start(bf16[48,768]{1,0:T(8,128)(2,1)S(1)} %add_convert_fusion.18), channel_id=1, source_target_pairs={{0,8},{8,0},{16,24},{24,16},{1,9},{9,1},{17,25},{25,17},{2,10},{10... | collective-permute-start | bytes 221192 | tf_op jit(solution)/shard_map/ppermute | solution.py:281
  336.2 18.9 %collective-permute-start.34 = (bf16[192,1024]{1,0:T(8,128)(2,1)S(1)}, bf16[192,1024]{1,0:T(8,128)(2,1)S(1)}, u32[]{:S(2)}, u32[]{:S(2)}) collective-permute-start(bf16[192,1024]{1,0:T(8,128)(2,1)S(1)} %get-tuple-element.31), channel_id=1, source_target_pairs={{0,1},{1,0},{2,3},{3,2},{4,5},{5,4},{6,7},{7,6},{8,9},{9,8},{10,11... | collective-permute-start | bytes 1179656 | tf_op jit(solution)/shard_map/ppermute | solution.py:278
  354.7 27.9 %collective-permute-start.37 = (bf16[2,192,1024]{2,1,0:T(8,128)(2,1)S(1)}, bf16[2,192,1024]{2,1,0:T(8,128)(2,1)S(1)}, u32[]{:S(2)}, u32[]{:S(2)}) collective-permute-start(bf16[2,192,1024]{2,1,0:T(8,128)(2,1)S(1)} %get-tuple-element.36), channel_id=1, source_target_pairs={{0,1},{1,0},{2,3},{3,2},{4,5},{5,4},{6,7},{7,6},{8,9},{9,8},{10,11... | collective-permute-start | bytes 2359304 | tf_op jit(solution)/shard_map/ppermute | solution.py:278
  357.3 24.0 %collective-permute-start.35 = (bf16[192,1024]{1,0:T(8,128)(2,1)S(1)}, bf16[192,1024]{1,0:T(8,128)(2,1)S(1)}, u32[]{:S(2)}, u32[]{:S(2)}) collective-permute-start(bf16[192,1024]{1,0:T(8,128)(2,1)S(1)} %add_convert_fusion.8), channel_id=1, source_target_pairs={{0,8},{8,0},{16,24},{24,16},{1,9},{9,1},{17,25},{25,17},{2,10},{10... | collective-permute-start | bytes 1179656 | tf_op jit(solution)/shard_map/ppermute | solution.py:281
  376.8 30.0 %collective-permute-start.44 = (bf16[3,768,192]{1,2,0:T(8,128)(2,1)S(1)}, bf16[3,768,192]{1,2,0:T(8,128)(2,1)S(1)}, u32[]{:S(2)}, u32[]{:S(2)}) collective-permute-start(bf16[3,768,192]{1,2,0:T(8,128)(2,1)S(1)} %copy-done.26), channel_id=1, source_target_pairs={{0,6},{2,4},{4,2},{6,0},{1,7},{3,5},{5,3},{7,1},{8,14},{10,12},{12... | collective-permute-start | bytes 2654216 | tf_op jit(solution)/shard_map/ppermute | solution.py:288
  381.3 46.0 %collective-permute-start.42 = (bf16[3,768,192]{1,2,0:T(8,128)(2,1)S(1)}, bf16[3,768,192]{1,2,0:T(8,128)(2,1)S(1)}, u32[]{:S(2)}, u32[]{:S(2)}) collective-permute-start(bf16[3,768,192]{1,2,0:T(8,128)(2,1)S(1)} %copy-done.26), channel_id=1, source_target_pairs={{0,4},{2,6},{4,0},{6,2},{1,5},{3,7},{5,1},{7,3},{8,12},{10,14},{12... | collective-permute-start | bytes 2654216 | tf_op jit(solution)/shard_map/ppermute | solution.py:288
  383.8 19.2 %collective-permute-start.38 = (bf16[2,192,1024]{2,1,0:T(8,128)(2,1)S(1)}, bf16[2,192,1024]{2,1,0:T(8,128)(2,1)S(1)}, u32[]{:S(2)}, u32[]{:S(2)}) collective-permute-start(bf16[2,192,1024]{2,1,0:T(8,128)(2,1)S(1)} %add_convert_fusion.4), channel_id=1, source_target_pairs={{0,8},{8,0},{16,24},{24,16},{1,9},{9,1},{17,25},{25,17},{2,10},{10... | collective-permute-start | bytes 2359304 | tf_op jit(solution)/shard_map/ppermute | solution.py:281
  387.7 47.0 %collective-permute-start.40 = (bf16[3,768,192]{1,2,0:T(8,128)(2,1)S(1)}, bf16[3,768,192]{1,2,0:T(8,128)(2,1)S(1)}, u32[]{:S(2)}, u32[]{:S(2)}) collective-permute-start(bf16[3,768,192]{1,2,0:T(8,128)(2,1)S(1)} %copy-done.26), channel_id=1, source_target_pairs={{0,2},{2,0},{4,6},{6,4},{1,3},{3,1},{5,7},{7,5},{8,10},{10,8},{12,... | collective-permute-start | bytes 2654216 | tf_op jit(solution)/shard_map/ppermute | solution.py:288
  403.5 22.7 %collective-permute-start.43 = (bf16[3,192,256]{2,1,0:T(8,128)(2,1)S(1)}, bf16[3,192,256]{2,1,0:T(8,128)(2,1)S(1)}, u32[]{:S(2)}, u32[]{:S(2)}) collective-permute-start(bf16[3,192,256]{2,1,0:T(8,128)(2,1)S(1)} %get-tuple-element.113), channel_id=1, source_target_pairs={{0,6},{2,4},{4,2},{6,0},{1,7},{3,5},{5,3},{7,1},{8,14},{10,12},{12... | collective-permute-start | bytes 884744 | tf_op jit(solution)/shard_map/ppermute | solution.py:288
  406.7 26.2 %collective-permute-start.41 = (bf16[3,192,256]{2,1,0:T(8,128)(2,1)S(1)}, bf16[3,192,256]{2,1,0:T(8,128)(2,1)S(1)}, u32[]{:S(2)}, u32[]{:S(2)}) collective-permute-start(bf16[3,192,256]{2,1,0:T(8,128)(2,1)S(1)} %get-tuple-element.112), channel_id=1, source_target_pairs={{0,4},{2,6},{4,0},{6,2},{1,5},{3,7},{5,1},{7,3},{8,12},{10,14},{12... | collective-permute-start | bytes 884744 | tf_op jit(solution)/shard_map/ppermute | solution.py:288
  406.9 42.3 %collective-permute-start.74 = (bf16[384,768]{1,0:T(8,128)(2,1)S(1)}, bf16[384,768]{1,0:T(8,128)(2,1)S(1)}, u32[]{:S(2)}, u32[]{:S(2)}) collective-permute-start(bf16[384,768]{1,0:T(8,128)(2,1)S(1)} %get-tuple-element.80), channel_id=1, source_target_pairs={{0,2},{2,0},{4,6},{6,4},{1,3},{3,1},{5,7},{7,5},{8,10},{10,8},{12,... | collective-permute-start | bytes 1769480 | tf_op jit(solution)/shard_map/ppermute | solution.py:288
  426.2 19.2 %collective-permute-start.39 = (bf16[3,192,256]{2,1,0:T(8,128)(2,1)S(1)}, bf16[3,192,256]{2,1,0:T(8,128)(2,1)S(1)}, u32[]{:S(2)}, u32[]{:S(2)}) collective-permute-start(bf16[3,192,256]{2,1,0:T(8,128)(2,1)S(1)} %get-tuple-element.111), channel_id=1, source_target_pairs={{0,2},{2,0},{4,6},{6,4},{1,3},{3,1},{5,7},{7,5},{8,10},{10,8},{12,... | collective-permute-start | bytes 884744 | tf_op jit(solution)/shard_map/ppermute | solution.py:288
  427.3 24.3 %collective-permute-start.75 = (bf16[384,768]{1,0:T(8,128)(2,1)S(1)}, bf16[384,768]{1,0:T(8,128)(2,1)S(1)}, u32[]{:S(2)}, u32[]{:S(2)}) collective-permute-start(bf16[384,768]{1,0:T(8,128)(2,1)S(1)} %get-tuple-element.82), channel_id=1, source_target_pairs={{0,4},{2,6},{4,0},{6,2},{1,5},{3,7},{5,1},{7,3},{8,12},{10,14},{12... | collective-permute-start | bytes 1769480 | tf_op jit(solution)/shard_map/ppermute | solution.py:288
  433.0 24.8 %collective-permute-start.76 = (bf16[384,768]{1,0:T(8,128)(2,1)S(1)}, bf16[384,768]{1,0:T(8,128)(2,1)S(1)}, u32[]{:S(2)}, u32[]{:S(2)}) collective-permute-start(bf16[384,768]{1,0:T(8,128)(2,1)S(1)} %get-tuple-element.81), channel_id=1, source_target_pairs={{0,6},{2,4},{4,2},{6,0},{1,7},{3,5},{5,3},{7,1},{8,14},{10,12},{12... | collective-permute-start | bytes 1769480 | tf_op jit(solution)/shard_map/ppermute | solution.py:288
  434.6 36.1 %collective-permute-start.66 = (bf16[384,768]{1,0:T(8,128)(2,1)S(1)}, bf16[384,768]{1,0:T(8,128)(2,1)S(1)}, u32[]{:S(2)}, u32[]{:S(2)}) collective-permute-start(bf16[384,768]{1,0:T(8,128)(2,1)S(1)} %get-tuple-element.83), channel_id=1, source_target_pairs={{0,2},{2,0},{4,6},{6,4},{1,3},{3,1},{5,7},{7,5},{8,10},{10,8},{12,... | collective-permute-start | bytes 1769480 | tf_op jit(solution)/shard_map/ppermute | solution.py:288
  449.1 22.4 %collective-permute-start.67 = (bf16[384,768]{1,0:T(8,128)(2,1)S(1)}, bf16[384,768]{1,0:T(8,128)(2,1)S(1)}, u32[]{:S(2)}, u32[]{:S(2)}) collective-permute-start(bf16[384,768]{1,0:T(8,128)(2,1)S(1)} %get-tuple-element.85), channel_id=1, source_target_pairs={{0,4},{2,6},{4,0},{6,2},{1,5},{3,7},{5,1},{7,3},{8,12},{10,14},{12... | collective-permute-start | bytes 1769480 | tf_op jit(solution)/shard_map/ppermute | solution.py:288
  449.1 34.0 %collective-permute-start.68 = (bf16[384,768]{1,0:T(8,128)(2,1)S(1)}, bf16[384,768]{1,0:T(8,128)(2,1)S(1)}, u32[]{:S(2)}, u32[]{:S(2)}) collective-permute-start(bf16[384,768]{1,0:T(8,128)(2,1)S(1)} %get-tuple-element.84), channel_id=1, source_target_pairs={{0,6},{2,4},{4,2},{6,0},{1,7},{3,5},{5,3},{7,1},{8,14},{10,12},{12... | collective-permute-start | bytes 1769480 | tf_op jit(solution)/shard_map/ppermute | solution.py:288
  451.5 33.1 %collective-permute-start.45 = (bf16[128,768]{1,0:T(8,128)(2,1)S(1)}, bf16[128,768]{1,0:T(8,128)(2,1)S(1)}, u32[]{:S(2)}, u32[]{:S(2)}) collective-permute-start(bf16[128,768]{1,0:T(8,128)(2,1)S(1)} %get-tuple-element.128), channel_id=1, source_target_pairs={{0,16},{8,24},{16,0},{24,8},{1,17},{9,25},{17,1},{25,9},{2,18},{10... | collective-permute-start | bytes 589832 | tf_op jit(solution)/shard_map/ppermute | solution.py:285
  457.8 32.3 %collective-permute-start.46 = (bf16[128,768]{1,0:T(8,128)(2,1)S(1)}, bf16[128,768]{1,0:T(8,128)(2,1)S(1)}, u32[]{:S(2)}, u32[]{:S(2)}) collective-permute-start(bf16[128,768]{1,0:T(8,128)(2,1)S(1)} %get-tuple-element.129), channel_id=1, source_target_pairs={{0,2},{2,0},{4,6},{6,4},{1,3},{3,1},{5,7},{7,5},{8,10},{10,8},{12,... | collective-permute-start | bytes 589832 | tf_op jit(solution)/shard_map/ppermute | solution.py:288
  470.7 25.7 %collective-permute-start.48 = (bf16[128,768]{1,0:T(8,128)(2,1)S(1)}, bf16[128,768]{1,0:T(8,128)(2,1)S(1)}, u32[]{:S(2)}, u32[]{:S(2)}) collective-permute-start(bf16[128,768]{1,0:T(8,128)(2,1)S(1)} %get-tuple-element.129), channel_id=1, source_target_pairs={{0,4},{2,6},{4,0},{6,2},{1,5},{3,7},{5,1},{7,3},{8,12},{10,14},{12... | collective-permute-start | bytes 589832 | tf_op jit(solution)/shard_map/ppermute | solution.py:288
  471.5 27.6 %collective-permute-start.50 = (bf16[128,768]{1,0:T(8,128)(2,1)S(1)}, bf16[128,768]{1,0:T(8,128)(2,1)S(1)}, u32[]{:S(2)}, u32[]{:S(2)}) collective-permute-start(bf16[128,768]{1,0:T(8,128)(2,1)S(1)} %get-tuple-element.129), channel_id=1, source_target_pairs={{0,6},{2,4},{4,2},{6,0},{1,7},{3,5},{5,3},{7,1},{8,14},{10,12},{12... | collective-permute-start | bytes 589832 | tf_op jit(solution)/shard_map/ppermute | solution.py:288
  490.1 16.8 %collective-permute-start.77 = (bf16[192,768]{1,0:T(8,128)(2,1)S(1)}, bf16[192,768]{1,0:T(8,128)(2,1)S(1)}, u32[]{:S(2)}, u32[]{:S(2)}) collective-permute-start(bf16[192,768]{1,0:T(8,128)(2,1)S(1)} %constant_dynamic-slice_fusion.1), channel_id=1, source_target_pairs={{0,8},{8,0},{16,24},{24,16},{1,9},{9,1},{17,25},{25,17},{2,10},{10... | collective-permute-start | bytes 884744 | tf_op jit(solution)/shard_map/ppermute | solution.py:281
  507.0 25.6 %collective-permute-start.78 = (bf16[192,768]{1,0:T(8,128)(2,1)S(1)}, bf16[192,768]{1,0:T(8,128)(2,1)S(1)}, u32[]{:S(2)}, u32[]{:S(2)}) collective-permute-start(bf16[192,768]{1,0:T(8,128)(2,1)S(1)} %fusion.24), channel_id=1, source_target_pairs={{0,16},{8,24},{16,0},{24,8},{1,17},{9,25},{17,1},{25,9},{2,18},{10... | collective-permute-start | bytes 884744 | tf_op jit(solution)/shard_map/ppermute | solution.py:285
  510.7 28.3 %collective-permute-start.70 = (bf16[192,768]{1,0:T(8,128)(2,1)S(1)}, bf16[192,768]{1,0:T(8,128)(2,1)S(1)}, u32[]{:S(2)}, u32[]{:S(2)}) collective-permute-start(bf16[192,768]{1,0:T(8,128)(2,1)S(1)} %fusion.23), channel_id=1, source_target_pairs={{0,16},{8,24},{16,0},{24,8},{1,17},{9,25},{17,1},{25,9},{2,18},{10... | collective-permute-start | bytes 884744 | tf_op jit(solution)/shard_map/ppermute | solution.py:285
  511.3 27.9 %collective-permute-start.55 = (bf16[576,192]{0,1:T(8,128)(2,1)S(1)}, bf16[576,192]{0,1:T(8,128)(2,1)S(1)}, u32[]{:S(2)}, u32[]{:S(2)}) collective-permute-start(bf16[576,192]{0,1:T(8,128)(2,1)S(1)} %add_convert_fusion.17), channel_id=1, source_target_pairs={{0,8},{8,0},{16,24},{24,16},{1,9},{9,1},{17,25},{25,17},{2,10},{10... | collective-permute-start | bytes 663560 | tf_op jit(solution)/shard_map/ppermute | solution.py:281
  (80 other events, 1128.0 us)

commit v2 on v1

--- a/solution.py
+++ b/solution.py
@@ -240,14 +240,145 @@
     )(planes, planes_t, bits, kv_a, kv_a, kv_b, kv_b, grad_tables)
 
 
-def layer_norm(values_in, gain_row, bias_row):
-    center = values_in - jnp.mean(values_in, axis=-1, keepdims=True)
-    spread = jnp.mean(center * center, axis=-1, keepdims=True)
-    return center * lax.rsqrt(spread + 1e-05) * gain_row + bias_row
-
-
-def gelu_exact(values_in):
-    return jax.nn.gelu(values_in, approximate=False)
+def norm(x):
+    center = x - jnp.mean(x, axis=-1, keepdims=True)
+    inv = lax.rsqrt(jnp.mean(center * center, axis=-1, keepdims=True) + 1e-5)
+    return center * inv, inv
+
+
+def norm_back(grad, unit, inv):
+    return inv * (
+        grad
+        - jnp.mean(grad, axis=-1, keepdims=True)
+        - unit * jnp.mean(grad * unit, axis=-1, keepdims=True)
+    )
+
+
+def column_sum(x):
+    return jnp.sum(x, axis=0, keepdims=True)
+
+
+def core_rows(core, ref, which):
+    half = ref.shape[0] // 2
+    at = core[0] if which == 0 else 1 - core[0]
+    return ref[pl.ds(pl.multiple_of(at * half, 16), half), :]
+
+
+def dense_kernel(core, x_in, grad_out, gain, bias, *refs):
+    attn, weights = refs[0:4], refs[4:12]
+    layer_out, grad_first_out, normed_out, hidden, grad_pre, grad_ffn_out, grad_attn_out = refs[12:19]
+    estimates, small, slope = refs[19:23], refs[23], refs[24]
+    part = hidden.shape[2]
+    blocks = range(8)
+    heads = jnp.concatenate([core_rows(core, attn[b // 2], b % 2) for b in blocks], axis=0)
+    out_w = jnp.concatenate([weights[b][2 * part :, :] for b in blocks], axis=0)
+    attn_out = dot(heads, out_w, TN)
+    resid = x_in[...].astype(f32)
+    first = resid + attn_out
+    small[4:5, :] = column_sum(resid * resid)
+    small[5:6, :] = column_sum(attn_out * attn_out)
+    small[6:7, :] = column_sum(first * first)
+    small[7:8, :] = jnp.zeros_like(small[7:8, :])
+    unit_1, inv_1 = norm(first)
+    normed = (unit_1 * gain[0:1, :] + bias[0:1, :]).astype(bf16)
+    normed_out[...] = normed
+    second = normed.astype(f32)
+    for b in blocks:
+        pre = dot(normed, weights[b][0:part, :], NT)
+        below = 0.5 * (1.0 + lax.erf(pre * 0.7071067811865476))
+        rows = (pre * below).astype(bf16)
+        hidden[b] = rows
+        slope[b] = below + pre * (0.3989422804014327 * jnp.exp(-0.5 * pre * pre))
+        second = second + dot(rows, weights[b][part : 2 * part, :], NN)
+    unit_2, inv_2 = norm(second)
+    layer_out[...] = (unit_2 * gain[1:2, :] + bias[1:2, :]).astype(layer_out.dtype)
+    grad = grad_out[...]
+    small[1:2, :] = column_sum(grad * unit_2)
+    small[3:4, :] = column_sum(grad)
+    grad_second = norm_back(grad * gain[1:2, :], unit_2, inv_2)
+    grad_ffn = grad_second.astype(bf16)
+    grad_ffn_out[...] = grad_ffn
+    grad_normed = grad_second
+    for b in blocks:
+        rows = (dot(grad_ffn, weights[b][part : 2 * part, :], NT) * slope[b]).astype(bf16)
+        grad_pre[b] = rows
+        grad_normed = grad_normed + dot(rows, weights[b][0:part, :], NN)
+    small[0:1, :] = column_sum(grad_normed * unit_1)
+    small[2:3, :] = column_sum(grad_normed)
+    grad_first = norm_back(grad_normed * gain[0:1, :], unit_1, inv_1)
+    grad_first_out[...] = grad_first
+    grad_attn = grad_first.astype(bf16)
+    grad_attn_out[...] = grad_attn
+    for b in blocks:
+        half = estimates[0].shape[0] // 2
+        at = core[0] if b % 2 == 0 else 1 - core[0]
+        estimates[b // 2][pl.ds(pl.multiple_of(at * half, 16), half), :] = dot(
+            weights[b][2 * part :, :], grad_attn, NT
+        ).astype(bf16)
+
+
+def weight_grad_kernel(core, normed, hidden, grad_pre, grad_ffn, grad_attn, *refs):
+    attn, outs = refs[0:4], refs[4:8]
+    part = hidden.shape[2]
+    for b in range(8):
+        down_out, up = outs[b % 2], outs[2 + b % 2]
+        down_out[b // 2, 0:part, :] = dot(hidden[b], grad_ffn[...], TN).astype(bf16)
+        down_out[b // 2, part:, :] = dot(core_rows(core, attn[b // 2], b % 2), grad_attn[...], NN).astype(bf16)
+        up[b // 2] = dot(grad_pre[b], normed[...], TN).astype(bf16)
+
+
+def vmem(count):
+    return [pl.BlockSpec(memory_space=pltpu.VMEM)] * count
+
+
+def dense(core, x_in, grad_out, gain, bias, attn, weights):
+    rows, width = x_in.shape
+    part = (weights[0].shape[0] - attn[0].shape[0] // 2) // 2
+    shape = jax.ShapeDtypeStruct
+    out_shape = [
+        shape((rows, width), bf16),
+        shape((rows, width), f32),
+        shape((rows, width), bf16),
+        shape((8, rows, part), bf16),
+        shape((8, rows, part), bf16),
+        shape((rows, width), bf16),
+        shape((rows, width), bf16),
+        *[shape(attn[0].shape, bf16)] * 4,
+        shape((8, width), f32),
+    ]
+    return pl.pallas_call(
+        dense_kernel,
+        in_specs=[pl.BlockSpec(memory_space=pltpu.SMEM)] + vmem(16),
+        out_specs=vmem(12),
+        out_shape=out_shape,
+        scratch_shapes=[pltpu.VMEM((8, rows, part), f32)],
+        compiler_params=pltpu.CompilerParams(vmem_limit_bytes=56 << 20),
+        cost_estimate=pl.CostEstimate(flops=18 * 10**9, bytes_accessed=4 << 20, transcendentals=0),
+        name="dense",
+    )(core, x_in, grad_out, gain, bias, *attn, *weights)
+
+
+def weight_grads(core, normed, hidden, grad_pre, grad_ffn, grad_attn, attn):
+    width, part = normed.shape[1], hidden.shape[2]
+    shapes = [jax.ShapeDtypeStruct((4, part + attn[0].shape[0] // 2, width), bf16)] * 2
+    shapes += [jax.ShapeDtypeStruct((4, part, width), bf16)] * 2
+    return pl.pallas_call(
+        weight_grad_kernel,
+        in_specs=[pl.BlockSpec(memory_space=pltpu.SMEM)] + vmem(9),
+        out_specs=vmem(4),
+        out_shape=shapes,
+        compiler_params=pltpu.CompilerParams(vmem_limit_bytes=56 << 20),
+        cost_estimate=pl.CostEstimate(flops=7 * 10**9, bytes_accessed=4 << 20, transcendentals=0),
+        name="weight_grads",
+    )(core, normed, hidden, grad_pre, grad_ffn, grad_attn, *attn)
+
+
+def after(x, *others):
+    return lax.optimization_barrier((x, *others))[0]
+
+
+def add(a, *others):
+    return sum([b.astype(f32) for b in others], a.astype(f32))
 
 
 def shards(
@@ -271,6 +402,9 @@
     quarter = piece // head_count
     rows = groups * quarter
     half_len = piece * hash_count
+    head_width = w_out.shape[0]
+    hidden_own = down_weight.shape[0]
+    n_tokens = head_count * rows
     hash_id, d, s = lax.axis_index("hash"), lax.axis_index("head"), lax.axis_index("seq")
     g, r = hash_id // places, hash_id % places
 
@@ -292,69 +426,65 @@
 
     my_quarter = lax.dynamic_slice_in_dim(own, d * quarter, quarter, 0)
     arrived = [over_group(seq_rows(my_quarter, g + k), k) for k in range(1, groups)]
+
+    signed = (2 * planes - 1).astype(bf16)
+    if planes.shape[0] == SETS and groups == 2:
+        moves = [
+            ((2 * rr + ss) * 2 + gg, (gg * places + rr) * 2 + ss)
+            for gg in range(2)
+            for rr in range(2)
+            for ss in range(2)
+        ]
+        signed = lax.ppermute(signed, ("hash", "seq"), moves)
+    else:
+        signed = lax.all_gather(signed, "hash", axis=0, tiled=True)
+        signed = lax.dynamic_slice_in_dim(signed, (r * 2 + s) * SETS, SETS, 0)
+    signed = signed.transpose(1, 0, 2).reshape(BITS * SETS, HEAD_DIM)
+    signed_t = jnp.concatenate([signed.T, signed.T], axis=1)
+    bits = bit_rows()
+
     dense_in = jnp.stack([seq_rows(my_quarter, g)] + arrived)
     blocks = [dense_in]
     for j in range(1, head_count):
         here = seq_rows(lax.dynamic_slice_in_dim(own, (d ^ j) * quarter, quarter, 0), g)
         blocks.append(jnp.concatenate([here[None], over_head(dense_in[1:], j)]))
-    tokens = jnp.stack(blocks).reshape(head_count * rows, width)
+    tokens = jnp.stack(blocks).reshape(n_tokens, width)
     dense_in = dense_in.reshape(rows, width)
-
-    signed = (2 * planes - 1).astype(bf16)
-    signed = lax.all_gather(signed, "hash", axis=0, tiled=True)
-    signed = lax.dynamic_slice_in_dim(signed, (r * 2 + s) * SETS, SETS, 0)
-    signed = signed.transpose(1, 0, 2).reshape(BITS * SETS, HEAD_DIM)
-    signed_t = jnp.concatenate([signed.T, signed.T], axis=1)
-    bits = bit_rows()
-
-    head_width = w_out.shape[0]
-    n_tokens = head_count * rows
 
     def project(w):
         return jnp.einsum("cde,ld->cel", w, tokens, preferred_element_type=f32).astype(bf16)
 
     kv = project(w_qkv[1:]).reshape(2 * head_width, n_tokens)
     q = project(w_qkv[:1]).reshape(head_width, n_tokens)
-    kv_o, q_o = over_seq(kv), over_seq(q)
     kv_z = over_place(kv)
-    q_z = over_place(q)
-    kv_zo, q_zo = over_seq(kv_z), over_seq(q_z)
-
-    tables = key_tables(signed, kv, kv_o)
-    tables = key_tables(signed, kv_z, kv_zo, tables)
-
-    def to_owner(own_part, own_other, far_part, far_other):
-        far = (far_part.astype(f32) + over_seq(far_other).astype(f32)).astype(bf16)
-        far = over_place(far)
-        return own_part + over_seq(own_other).astype(f32) + far.astype(f32)
-
-    e_z, e_zo = query_estimates(signed, q_z, q_zo, tables, bf16, bf16)
-    e, e_o = query_estimates(signed, q, q_o, tables, f32, bf16)
-    attn = to_owner(e, e_o, e_z, e_zo).astype(bf16)
-
-    def to_dense(block):
-        parts = [block[:, j * rows : (j + 1) * rows] for j in range(head_count)]
-        return jnp.concatenate([parts[0]] + [over_head(parts[j], j) for j in range(1, head_count)], 0)
-
-    attn_t = to_dense(attn)
-
-    packed = jnp.concatenate([up_weight.T, down_weight, w_out], axis=0)
-    pack_half = packed.shape[0] // 2
-
-    def halves(mine, other):
-        first = jnp.where(s == 0, mine, other)
-        second = jnp.where(s == 0, other, mine)
-        return jnp.concatenate([first, second], axis=-2)
-
-    my_half = lax.dynamic_slice_in_dim(packed, s * pack_half, pack_half, 0)
-    fetched = jnp.stack([over_head(my_half, j) for j in range(1, head_count)])
-    fetched = halves(fetched, over_seq(fetched))
-    hidden_own = down_weight.shape[0]
-    all_weights = jnp.concatenate([packed[None], fetched], axis=0)
-    up_t = all_weights[:, :hidden_own].reshape(head_count * hidden_own, width)
-    down = all_weights[:, hidden_own : 2 * hidden_own].reshape(head_count * hidden_own, width)
-    out_w = all_weights[:, 2 * hidden_own :].reshape(head_count * head_width, width)
-    qkv_w = [w_qkv] + [over_head(w_qkv, j) for j in range(1, head_count)]
+    kv_o = over_seq(kv)
+    q_o = over_seq(q)
+    q_z = over_place(after(q, kv_o))
+
+    def core_half(at):
+        cut = hidden_own // 2
+        out_cut = head_width // 2
+        return jnp.concatenate(
+            [
+                lax.dynamic_slice_in_dim(up_weight, at * cut, cut, 1).T,
+                lax.dynamic_slice_in_dim(down_weight, at * cut, cut, 0),
+                lax.dynamic_slice_in_dim(w_out, at * out_cut, out_cut, 0),
+            ],
+            axis=0,
+        )
+
+    weights = [core_half(s), core_half(1 - s)]
+    my_half = after(weights[0], tokens)
+    fetched = [over_head(my_half, j) for j in range(1, head_count)]
+    for block in fetched:
+        weights += [block, over_seq(block)]
+    qkv_cut = width // 2
+    qkv_half = lax.dynamic_slice_in_dim(w_qkv, s * qkv_cut, qkv_cut, 1)
+    qkv_half = after(qkv_half, *weights)
+    qkv_blocks = [over_head(qkv_half, j) for j in range(1, head_count)]
+    qkv_far = [over_seq(block) for block in qkv_blocks]
+    qkv_near = [lax.dynamic_slice_in_dim(w_qkv, s * qkv_cut, qkv_cut, 1)] + qkv_blocks
+    qkv_far = [lax.dynamic_slice_in_dim(w_qkv, (1 - s) * qkv_cut, qkv_cut, 1)] + qkv_far
 
     slot = jnp.arange(groups, dtype=jnp.int32)[:, None]
     place_of = ((g - slot) % groups) * places + r
@@ -364,58 +494,84 @@
     pick = (position.reshape(rows)[:, None] == mask_row[None]).astype(bf16)
     grad_out = jnp.dot(pick, cot, preferred_element_type=f32)
 
-    attn_out = dot(attn_t, out_w, TN)
-    resid = dense_in.astype(f32)
-    first_sum = resid + attn_out
-    normed_f, first_pull = jax.vjp(layer_norm, first_sum, norm_gain[0], norm_bias[0])
-    normed = normed_f.astype(bf16)
-    pre = dot(normed, up_t, NT)
-    hidden_f, gelu_pull = jax.vjp(gelu_exact, pre)
-    hidden = hidden_f.astype(bf16)
-    second_sum = normed.astype(f32) + dot(hidden, down, NN)
-    result, second_pull = jax.vjp(layer_norm, second_sum, norm_gain[1], norm_bias[1])
-
-    grad_second, gain_second, bias_second = second_pull(grad_out)
-    grad_ffn = grad_second.astype(bf16)
-    grad_pre = gelu_pull(dot(grad_ffn, down, NT))[0].astype(bf16)
-    grad_normed = grad_second + dot(grad_pre, up_t, NN)
-    grad_first, gain_first, bias_first = first_pull(grad_normed)
-    grad_attn = grad_first.astype(bf16)
-    grad_est = dot(out_w, grad_attn, NT).astype(bf16)
-    est_parts = [grad_est[j * head_width : (j + 1) * head_width] for j in range(head_count)]
+    kv_zo = over_seq(kv_z)
+    q_zo = over_seq(q_z)
+    tables = key_tables(signed, kv, kv_o)
+    tables = key_tables(signed, after(kv_z, grad_out), kv_zo, tables)
+
+    e_z, e_zo = query_estimates(signed, q_z, q_zo, tables, bf16, bf16)
+    e_far = add(e_z, over_seq(e_zo)).astype(bf16)
+    e_far = over_place(e_far)
+    e, e_o = query_estimates(signed, q, q_o, tables, f32, bf16)
+    attn = add(e, over_seq(e_o), e_far).astype(bf16)
+
+    def to_dense(block):
+        parts = [block[..., j * rows : (j + 1) * rows] for j in range(head_count)]
+        return [parts[0]] + [over_head(parts[j], j) for j in range(1, head_count)]
+
+    attn_parts = to_dense(attn)
+
+    core = s.astype(jnp.int32).reshape(1)
+    (layer_rows, grad_first, normed, hidden, grad_pre, grad_ffn, grad_attn, *rest) = dense(
+        core, dense_in, grad_out, norm_gain, norm_bias, attn_parts, weights
+    )
+    est_parts, small = rest[:4], rest[4]
     grad = jnp.concatenate(
         [est_parts[0]] + [over_head(est_parts[j], j) for j in range(1, head_count)], axis=1
     )
-
+    mine_a, other_a, mine_b, other_b = weight_grads(
+        core, normed, hidden, grad_pre, grad_ffn, grad_attn, attn_parts
+    )
+
+    grad_z = over_place(grad)
     grad_o = over_seq(grad)
-    grad_z = over_place(grad)
     grad_zo = over_seq(grad_z)
+    swap_a = over_seq(after(other_a, grad_o))
+    swap_b = over_seq(after(other_b, grad_o))
     part, dq, dq_o = query_backward(
         signed, signed_t, bits, q, grad, q_o, grad_o, tables, None, f32, bf16
     )
+    chip_a = add(mine_a, swap_a).astype(bf16)
+    chip_b = add(mine_b, swap_b).astype(bf16)
+
+    a_far = over_head(jnp.stack([chip_a[1], chip_a[3]]), 1)
+    b_far = over_head(jnp.stack([chip_b[2], chip_b[3]]), 2)
     grad_tables, dq_z, dq_zo = query_backward(
-        signed, signed_t, bits, q_z, grad_z, q_zo, grad_zo, tables, part, bf16, bf16
-    )
-    dkv_z, dkv_zo = key_backward(signed, signed_t, bits, kv_z, kv_zo, grad_tables, bf16, bf16)
-    dkv, dkv_o = key_backward(signed, signed_t, bits, kv, kv_o, grad_tables, f32, bf16)
-    grad_q = to_owner(dq, dq_o, dq_z, dq_zo).astype(bf16)
-    grad_kv = to_owner(dkv, dkv_o, dkv_z, dkv_zo).astype(bf16)
-    grad_qkv = jnp.concatenate([grad_q[None], grad_kv])
-
-    grad_in = grad_first
+        signed, signed_t, bits, after(q_z, chip_a, chip_b), grad_z, q_zo, grad_zo, tables, part, bf16, bf16
+    )
+    a_two = [add(chip_a[0], a_far[0]), add(chip_a[2], a_far[1]).astype(bf16)]
+    b_two = [add(chip_b[0], b_far[0]), add(chip_b[1], b_far[1]).astype(bf16)]
+    a_last = over_head(a_two[1], 2)
+    b_last = over_head(b_two[1], 1)
+    dkv_z, dkv_zo = key_backward(
+        signed, signed_t, bits, after(kv_z, a_two[1], b_two[1]), kv_zo, grad_tables, bf16, bf16
+    )
+    dkv_far = add(dkv_z, over_seq(dkv_zo)).astype(bf16)
+    dkv_far = over_place(dkv_far)
+    a_sum = add(a_two[0], a_last).astype(bf16)
+    b_sum = add(b_two[0], b_last).astype(bf16)
+    dq_far = over_place(add(dq_z, over_seq(dq_zo)).astype(bf16))
+    grad_q = add(dq, over_seq(dq_o), dq_far).astype(bf16)
+    dkv, dkv_o = key_backward(
+        signed, signed_t, bits, after(kv, a_sum, b_sum), kv_o, grad_tables, f32, bf16
+    )
+    grad_kv = add(dkv, over_seq(dkv_o), dkv_far).astype(bf16)
+    q_parts, kv_parts = to_dense(grad_q), to_dense(grad_kv)
+
+    near, far = 0.0, 0.0
     for j in range(head_count):
-        block = grad_qkv[:, :, j * rows : (j + 1) * rows]
-        if j:
-            block = over_head(block, j)
-        grad_in = grad_in + jnp.einsum("cel,cde->ld", block, qkv_w[j], preferred_element_type=f32)
-
-    def home(dense):
-        dense = dense.reshape(groups, quarter, width)
-        parts = [dense[0]] + [over_group(dense[k], groups - k) for k in range(1, groups)]
-        table = [jnp.stack(parts)]
-        for j in range(1, head_count):
-            table.append(jnp.stack([over_head(part, j) for part in parts]))
-        table = jnp.stack(table)
+        block = jnp.concatenate([q_parts[j][None], kv_parts[j]])
+        near = near + jnp.einsum("cel,cde->ld", block, qkv_near[j], preferred_element_type=f32)
+        far = far + jnp.einsum("cel,cde->ld", block, qkv_far[j], preferred_element_type=f32)
+    grad_in = grad_first + jnp.concatenate(
+        [jnp.where(s == 0, near, far), jnp.where(s == 0, far, near)], axis=1
+    )
+
+    def home(dense_rows):
+        dense_rows = dense_rows.reshape(groups, quarter, width)
+        parts = [dense_rows[0]] + [over_group(dense_rows[k], groups - k) for k in range(1, groups)]
+        parts = jnp.stack(parts)
+        table = jnp.stack([parts] + [over_head(parts, j) for j in range(1, head_count)])
         columns = []
         for q_at in range(head_count):
             block = lax.dynamic_index_in_dim(table, q_at ^ d, 0, keepdims=False)
@@ -430,68 +586,58 @@
             )
         return jnp.concatenate(columns, axis=0)
 
-    layer_out = home(result.astype(bf16))
+    layer_out = home(after(layer_rows, grad_tables))
     grad_inputs = home(grad_in.astype(bf16)).astype(f32)
+
+    def in_halves(index, mine, other):
+        first = jnp.where(index == 0, mine, other)
+        second = jnp.where(index == 0, other, mine)
+        return jnp.concatenate([first, second], axis=0)
 
     def over_hash_sum(x):
         half = x.shape[0] // 2
         mine = lax.dynamic_slice_in_dim(x, r * half, half, 0)
-        other = over_place(lax.dynamic_slice_in_dim(x, (1 - r) * half, half, 0))
-        total = mine.astype(f32) + other.astype(f32)
-        total = sum(
-            [total] + [over_group(total.astype(bf16), k).astype(f32) for k in range(1, groups)]
-        ).astype(bf16)
-        far = over_place(total)
-        first, second = jnp.where(r == 0, total, far), jnp.where(r == 0, far, total)
-        return jnp.concatenate([first, second], axis=0)
-
-    def reduce_weights(parts):
-        half = parts.shape[1] // 2
-        parts = parts.astype(bf16)
-        mine = lax.dynamic_slice_in_dim(parts, s * half, half, 1)
-        other = over_seq(lax.dynamic_slice_in_dim(parts, (1 - s) * half, half, 1))
-        chip = (mine.astype(f32) + other.astype(f32)).astype(bf16)
-        total = sum([chip[0].astype(f32)] + [over_head(chip[j], j).astype(f32) for j in range(1, 4)])
-        total = over_hash_sum(total.astype(bf16))
-        return halves(total, over_seq(total)).astype(f32)
-
-    grad_down = dot(hidden, grad_ffn, TN).reshape(head_count, hidden_own, width)
-    grad_up = dot(grad_pre, normed, TN).reshape(head_count, hidden_own, width)
-    grad_out_w = dot(attn_t, grad_attn, NN).reshape(head_count, head_width, width)
-    down_total = reduce_weights(grad_down)
-    up_total = reduce_weights(grad_up)
-    out_total = reduce_weights(grad_out_w)
-
+        total = add(mine, over_place(lax.dynamic_slice_in_dim(x, (1 - r) * half, half, 0)))
+        sent = total.astype(bf16)
+        total = add(total, *[over_group(sent, k) for k in range(1, groups)]).astype(bf16)
+        return in_halves(r, total, over_place(total))
+
+    a_sum, b_sum = over_hash_sum(a_sum), over_hash_sum(b_sum)
+    a_other, b_other = over_seq(a_sum), over_seq(b_sum)
+    cut = hidden_own // 2
+    grad_w_down = in_halves(s, a_sum[:cut], a_other[:cut]).astype(f32)
+    grad_w_out = in_halves(s, a_sum[cut:], a_other[cut:]).astype(f32)
+    grad_w_up = in_halves(s, b_sum, b_other).T.astype(f32)
+
+    grad_qkv = jnp.concatenate([grad_q[None], grad_kv])
     grad_w_qkv = jnp.einsum("ld,cel->cde", tokens, grad_qkv, preferred_element_type=f32)
     grad_w_qkv = grad_w_qkv.reshape(3 * width, head_width).astype(bf16)
     half = grad_w_qkv.shape[0] // 2
     mine = lax.dynamic_slice_in_dim(grad_w_qkv, s * half, half, 0)
     other = over_seq(lax.dynamic_slice_in_dim(grad_w_qkv, (1 - s) * half, half, 0))
-    total = over_hash_sum((mine.astype(f32) + other.astype(f32)).astype(bf16))
-    grad_w_qkv = halves(total, over_seq(total)).reshape(3, width, head_width).astype(f32)
-
-    squares = jnp.stack([jnp.sum(resid * resid), jnp.sum(attn_out * attn_out), jnp.sum(first_sum * first_sum)])
-    small = jnp.concatenate(
-        [gain_first, gain_second, bias_first, bias_second, jnp.pad(squares, (0, width - 3))]
-    ).reshape(5, width)
+    total = over_hash_sum(add(mine, other).astype(bf16))
+    grad_w_qkv = in_halves(s, total, over_seq(total)).reshape(3, width, head_width).astype(f32)
+
+    small = after(small, part)
     small = small + over_seq(small)
     small = small + over_head(small, 1)
-    small = small + over_head(small, 2)
+    small = small + over_head(after(small, grad_tables), 2)
     small = small + over_place(small)
+    small = after(small, dkv_z)
     small = sum([small] + [over_group(small, k) for k in range(1, groups)])
     count = piece * seqs * width * hash_count * 2
-    stream_rms = jnp.sqrt(small[4, :3] / count)
+    stream_rms = jnp.sqrt(jnp.sum(small[4:7], axis=1) / count)
     share = width // head_count
-    mine = lax.dynamic_slice_in_dim(small, d * share, share, 1)
+    norm_grads = lax.dynamic_slice_in_dim(small, d * share, share, 1)
     return (
         layer_out[None],
         grad_inputs[None],
         grad_w_qkv,
-        out_total,
-        up_total.T,
-        down_total,
-        mine[0:2],
-        mine[2:4],
+        grad_w_out,
+        grad_w_up,
+        grad_w_down,
+        norm_grads[0:2],
+        norm_grads[2:4],
         stream_rms,
     )
 

time: 567 us -> 489 us (0.86)
  waiting for transfers between devices: 218 us -> 173 us
  other arithmetic: 49.5 us -> 25.8 us
  Pallas kernels: 110 us -> 129 us
  matrix products: 30.7 us -> 13.3 us
  blocking collectives: 13.5 us -> 0 us
  local copies, waits for them, and re-layouts: 33.6 us -> 42.3 us
  starting transfers between devices: 105 us -> 97.4 us
    ppermute x41 -> x33, waiting for transfers between devices: 145 us -> 104 us  [over_head(): return lax.ppermute(x, 'head', [(h, h ^ j) for h in range(head_count)])]
    pallas_call x0 -> x2, Pallas kernels: none -> 25.7 us  [the longest x1 16.8 us: dense(): pl.pallas_call(dense_kernel, in_specs=[pl.BlockSpec(memory_space=pltpu.SM...]
    dot_general x13 -> x8, matrix products: 26.6 us -> 9.27 us  [the longest x4 4.67 us: shards(): jnp.einsum('cel,cde->ld', block, qkv_far[j], preferred_element_type=f32)]
    ppermute x41 -> x33, starting transfers between devices: 40.5 us -> 26.6 us  [over_head(): return lax.ppermute(x, 'head', [(h, h ^ j) for h in range(head_count)])]
    all_gather x1 -> x0, blocking collectives: 13.5 us -> none  [shards(): signed = lax.all_gather(signed, 'hash', axis=0, tiled=True)]
    concatenate x9 -> x5, other arithmetic: 14.6 us -> 3.81 us  [the longest x2 3.58 us: core_half(): jnp.concatenate([lax.dynamic_slice_in_dim(up_weight, at * cut, cut, 1).T,...]
    ppermute x0 -> x1, waiting for transfers between devices: none -> 9.24 us  [shards(): signed = lax.ppermute(signed, ('hash', 'seq'), moves)]
    unnamed x93 -> x109, local copies, waits for them, and re-layouts: 17.2 us -> 25.9 us
  transfers between devices with their start and end apart: 86 -> 79, of which waited for: 30 -> 33; matrix products, arithmetic and copies ran while one was open for 13% -> 13% of each run, Pallas kernels for 19% -> 23%
where the time goes in v2:
time: 489 us; the launch traced here: 484 us
  waiting for transfers between devices  173 us (35%)
  Pallas kernels  129 us (26%)
  starting transfers between devices  97.4 us (20%)
  local copies, waits for them, and re-layouts  42.3 us (9%)
  other arithmetic  25.8 us (5%)
  matrix products  13.3 us (3%)
    ppermute x33, waiting for transfers between devices, over_head(): return lax.ppermute(x, 'head', [(h, h ^ j) for h in range(head_count)])  104 us
    ppermute x25, starting transfers between devices, over_seq(): return lax.ppermute(x, 'seq', [(0, 1), (1, 0)])  42.7 us
    pallas_call x2, Pallas kernels, query_backward(): call(partial(query_back_kernel, chunk=4), heads, 20, 'query_backward', sp...  40 us
    ppermute x13, waiting for transfers between devices, over_place(): return lax.ppermute(x, 'hash', [(h, h ^ 1) for h in range(hash_count)])  37.1 us
    pallas_call x2, Pallas kernels, key_backward(): call(partial(key_back_kernel, chunk=4), heads, 18, 'key_backward', [whole...  34.7 us
    ppermute x33, starting transfers between devices, over_head(): return lax.ppermute(x, 'head', [(h, h ^ j) for h in range(head_count)])  26.6 us
    unnamed x109, local copies, waits for them, and re-layouts  25.9 us
    ppermute x7, waiting for transfers between devices, over_group(): return lax.ppermute(x, 'hash', moves)  21.3 us
  transfers between devices with their start and end apart: 79, of which 33 were waited for; matrix products, arithmetic and copies ran while one was open for 13% of the time, Pallas kernels for 23%

profile of v2, /device:TPU:1, one launch (start us, length us, event | category | flops | bytes accessed | tf_op | source)
XLA Modules:
  0.0 483.7 jit_solution(16220095412011727332)
XLA Ops:
  0.8 4.5 constant_dynamic-slice_fusion.14
  6.0 3.1 collective-permute-start
  25.8 5.2 %collective-permute-done.4 = bf16[1,128,768]{2,1,0:T(8,128)(2,1)S(1)} collective-permute-done((bf16[1,128,768]{2,1,0:T(8,128)(2,1)}, bf16[1,128,768]{2,1,0:T(8,128)(2,1)S(1)}, u32[]{:S(2)}, u32[]{:S(2)}) %collective-permute-start.4) | collective-permute-done | bytes 196640 | tf_op jit(solution)/shard_map/ppermute | solution.py:422
  33.1 3.4 collective-permute-start.8
  42.0 4.4 collective-permute-start.1
  47.1 9.2 %collective-permute-done.1 = bf16[8,8,64]{2,0,1:T(8,128)(2,1)S(1)} collective-permute-done((bf16[8,8,64]{2,0,1:T(8,128)(2,1)S(1)}, bf16[8,8,64]{2,0,1:T(8,128)(2,1)S(1)}, u32[]{:S(2)}, u32[]{:S(2)}) %collective-permute-start.1) | collective-permute-done | bytes 8224 | tf_op jit(solution)/shard_map/ppermute | solution.py:438
  57.4 7.8 %key_tables.2.refs_0_ = f32[3,2048,64]{2,1,0:T(8,128)S(1)} custom-call(bf16[64,64]{1,0:T(8,128)(2,1)S(1)} %bitcast.182, bf16[384,1024]{1,0:T(8,128)(2,1)S(1)} %bitcast.178, bf16[384,1024]{1,0:T(8,128)(2,1)S(1)} %bitcast.179, bf16[384,1024]{1,0:T(8,128)(2,1)S(1)} %collective-permute-done.8.kb.vb, bf16[384,1024]{1,0:T(8,128)(2,1)S(1)} %collective-permute-done.8.kb.vb), custom_call_target="tpu_custom_call" | custom-call | flops 11000000512 | bytes 4194304 | tf_op jit(solution)/shard_map/key_tables/pallas_call | solution.py:184
  67.4 3.4 collective-permute-done.21.refs_10_
  72.6 27.2 %collective-permute-done.19.refs_8_ = bf16[864,768]{1,0:T(8,128)(2,1)} collective-permute-done((bf16[864,768]{1,0:T(8,128)(2,1)S(1)}, bf16[864,768]{1,0:T(8,128)(2,1)}, u32[]{:S(2)}, u32[]{:S(2)}) %collective-permute-start.19) | collective-permute-done | bytes 1327136 | tf_op jit(solution)/shard_map/ppermute | solution.py:422
  100.8 9.1 %key_tables.3.tables = bf16[3,2048,64]{2,1,0:T(8,128)(2,1)S(1)} custom-call(bf16[64,64]{1,0:T(8,128)(2,1)S(1)} %bitcast.183, bf16[384,1024]{1,0:T(8,128)(2,1)S(1)} %collective-permute-done.6.ka.va, bf16[384,1024]{1,0:T(8,128)(2,1)S(1)} %collective-permute-done.6.ka.va, bf16[384,1024]{1,0:T(8,128)(2,1)S(1)} %collective-permute-done.7.kb.vb, ...), custom_call_target="tpu_custom_call" | custom-call | flops 11000000512 | bytes 4194304 | tf_op jit(solution)/shard_map/key_tables/pallas_call | solution.py:184
  109.9 5.8 %query_estimates.3 = (bf16[192,1024]{1,0:T(8,128)(2,1)S(1)}, bf16[192,1024]{1,0:T(8,128)(2,1)S(1)}) custom-call(bf16[64,64]{1,0:T(8,128)(2,1)S(1)} %bitcast.184, bf16[192,1024]{1,0:T(8,128)(2,1)S(1)} %collective-permute-done.10.qa, bf16[192,1024]{1,0:T(8,128)(2,1)S(1)} %collective-permute-done.11.qb, bf16[3,2048,64]{2,1,0:T(8,128)(2,1)S(1)} %key_tables.3.tables), custom_call_target="tpu_custom_call" | custom-call | flops 7699999744 | bytes 4194304 | tf_op jit(solution)/shard_map/query_estimates/pallas_call | solution.py:197
  115.9 6.0 %query_estimates.2 = (f32[192,1024]{1,0:T(8,128)S(1)}, bf16[192,1024]{1,0:T(8,128)(2,1)S(1)}) custom-call(bf16[64,64]{1,0:T(8,128)(2,1)S(1)} %bitcast.185, bf16[192,1024]{1,0:T(8,128)(2,1)S(1)} %fusion.5.qa, bf16[192,1024]{1,0:T(8,128)(2,1)S(1)} %collective-permute-done.5.qb, bf16[3,2048,64]{2,1,0:T(8,128)(2,1)S(1)} %key_tables.3.tables), custom_call_target="tpu_custom_call" | custom-call | flops 7699999744 | bytes 4194304 | tf_op jit(solution)/shard_map/query_estimates/pallas_call | solution.py:197
  123.8 9.5 %collective-permute-done.13 = bf16[192,1024]{1,0:T(8,128)(2,1)S(1)} collective-permute-done((bf16[192,1024]{1,0:T(8,128)(2,1)S(1)}, bf16[192,1024]{1,0:T(8,128)(2,1)S(1)}, u32[]{:S(2)}, u32[]{:S(2)}) %collective-permute-start.13) | collective-permute-done | bytes 393248 | tf_op jit(solution)/shard_map/ppermute | solution.py:415
  142.7 16.8 %dense.1 = (bf16[256,768]{1,0:T(8,128)(2,1)}, f32[256,768]{1,0:T(8,128)}, bf16[256,768]{1,0:T(8,128)(2,1)}, bf16[8,256,384]{2,1,0:T(8,128)(2,1)}, bf16[8,256,384...) custom-call(s32[1]{0:T(128)} %bitcast.core, ...), custom_call_target="tpu_custom_call" | custom-call | flops 17999998976 | bytes 4194304 | tf_op jit(solution)/shard_map/dense/pallas_call | solution.py:349
  165.6 5.0 %collective-permute-start.26 = (bf16[192,1024]{1,0:T(8,128)(2,1)S(1)}, bf16[192,1024]{1,0:T(8,128)(2,1)S(1)}, u32[]{:S(2)}, u32[]{:S(2)}) collective-permute-start(bf16[192,1024]{1,0:T(8,128)(2,1)S(1)} %constant_dynamic-update-slice_fusion.ga), channel_id=1, source_target_pairs={{0,1},{1,0},{2,3},{3,2},{4,5},{5,4},{6,7},{7,6},{8,9},{9,8},{10,11... | collective-permute-start | bytes 1179656 | tf_op jit(solution)/shard_map/ppermute | solution.py:412
  170.5 9.0 %weight_grads.1 = (bf16[4,480,768]{2,1,0:T(8,128)(2,1)}, bf16[4,480,768]{2,1,0:T(8,128)(2,1)}, bf16[4,384,768]{2,1,0:T(8,128)(2,1)}, bf16[4,384,768]{2,1,0:T(8,128)(2,1)}) custom-call(s32[1]{0:T(128)} %bitcast.core, bf16[256,768]{1,0:T(8,128)(2,1)} %get-tuple-element.60.normed, bf16[8,256,384]{2,1,0:T(8,128)(2,1)} %get-tuple-element.61.hidden, ...), custom_call_target="tpu_custom_call" | custom-call | flops 7000000000 | bytes 4194304 | tf_op jit(solution)/shard_map/weight_grads/pallas_call | solution.py:365
  185.5 19.6 %query_backward.2 = (f32[3,2048,64]{2,1,0:T(8,128)}, f32[192,1024]{1,0:T(8,128)S(1)}, bf16[192,1024]{1,0:T(8,128)(2,1)S(1)}) custom-call(bf16[64,64]{1,0:T(8,128)(2,1)S(1)} %bitcast.187, bf16[64,128]{1,0:T(8,128)(2,1)S(1)} %pad_maximum_fusion.24.planes_t, bf16[80,2048]{1,0:T(8,128)(2,1)S(1)} %copy-done.14, bf16[192,1024]{1,0:T(8,128)(2,1)S(1)} %copy-done.9, ...), custom_call_target="tpu_custom_call" | custom-call | flops 22000001024 | bytes 4194304 | tf_op jit(solution)/shard_map/query_backward/pallas_call | solution.py:215
  209.9 3.1 add_convert_fusion.1
  213.6 2.8 add_convert_fusion
  216.4 20.3 %query_backward.3 = (bf16[3,2048,64]{2,1,0:T(8,128)(2,1)S(1)}, bf16[192,1024]{1,0:T(8,128)(2,1)S(1)}, bf16[192,1024]{1,0:T(8,128)(2,1)S(1)}) custom-call(bf16[64,64]{1,0:T(8,128)(2,1)S(1)} %bitcast.188, bf16[64,128]{1,0:T(8,128)(2,1)S(1)} %pad_maximum_fusion.24.planes_t, bf16[80,2048]{1,0:T(8,128)(2,1)S(1)} %copy-done.14, ...), custom_call_target="tpu_custom_call" | custom-call | flops 22000001024 | bytes 4194304 | tf_op jit(solution)/shard_map/query_backward/pallas_call | solution.py:215
  242.9 5.8 %collective-permute-done.31 = bf16[128,768]{1,0:T(8,128)(2,1)S(1)} collective-permute-done((bf16[128,768]{1,0:T(8,128)(2,1)S(1)}, bf16[128,768]{1,0:T(8,128)(2,1)S(1)}, u32[]{:S(2)}, u32[]{:S(2)}) %collective-permute-start.31) | collective-permute-done | bytes 196640 | tf_op jit(solution)/shard_map/ppermute | solution.py:419
  254.0 3.9 collective-permute-done.33
  257.9 3.7 collective-permute-start.35
  261.8 5.4 %collective-permute-done.34 = bf16[2,128,768]{2,1,0:T(8,128)(2,1)S(1)} collective-permute-done((bf16[2,128,768]{2,1,0:T(8,128)(2,1)S(1)}, bf16[2,128,768]{2,1,0:T(8,128)(2,1)S(1)}, u32[]{:S(2)}, u32[]{:S(2)}) %collective-permute-start.34) | collective-permute-done | bytes 393248 | tf_op jit(solution)/shard_map/ppermute | solution.py:422
  268.4 10.8 %collective-permute-done.41 = bf16[384,768]{1,0:T(8,128)(2,1)S(1)} collective-permute-done((bf16[384,768]{1,0:T(8,128)(2,1)S(1)}, bf16[384,768]{1,0:T(8,128)(2,1)S(1)}, u32[]{:S(2)}, u32[]{:S(2)}) %collective-permute-start.41) | collective-permute-done | bytes 589856 | tf_op jit(solution)/shard_map/ppermute | solution.py:422
  280.6 2.8 copy.42
  285.6 2.6 collective-permute-start.71
  288.1 32.2 %collective-permute-done.38 = bf16[2,480,768]{2,1,0:T(8,128)(2,1)S(1)} collective-permute-done((bf16[2,480,768]{2,1,0:T(8,128)(2,1)S(1)}, bf16[2,480,768]{2,1,0:T(8,128)(2,1)S(1)}, u32[]{:S(2)}, u32[]{:S(2)}) %collective-permute-start.38) | collective-permute-done | bytes 1474592 | tf_op jit(solution)/shard_map/ppermute | solution.py:422
  320.5 17.4 %key_backward.3 = (bf16[2,192,1024]{2,1,0:T(8,128)(2,1)S(1)}, bf16[2,192,1024]{2,1,0:T(8,128)(2,1)S(1)}) custom-call(bf16[64,64]{1,0:T(8,128)(2,1)S(1)} %bitcast.189, bf16[64,128]{1,0:T(8,128)(2,1)S(1)} %pad_maximum_fusion.24.planes_t, bf16[80,2048]{1,0:T(8,128)(2,1)S(1)} %copy-done.14, bf16[384,1024]{1,0:T(8,128)(2,1)S(1)} %copy-done.7, ...), custom_call_target="tpu_custom_call" | custom-call | flops 19800000512 | bytes 4194304 | tf_op jit(solution)/shard_map/key_backward/pallas_call | solution.py:230
  338.7 2.8 collective-permute-done.78
  344.9 3.7 collective-permute-done.72
  348.7 7.5 %collective-permute-start.43 = (bf16[2,192,1024]{2,1,0:T(8,128)(2,1)S(1)}, bf16[2,192,1024]{2,1,0:T(8,128)(2,1)S(1)}, u32[]{:S(2)}, u32[]{:S(2)}) collective-permute-start(bf16[2,192,1024]{2,1,0:T(8,128)(2,1)S(1)} %get-tuple-element.89), channel_id=1, source_target_pairs={{0,1},{1,0},{2,3},{3,2},{4,5},{5,4},{6,7},{7,6},{8,9},{9,8},{10,11... | collective-permute-start | bytes 2359304 | tf_op jit(solution)/shard_map/ppermute | solution.py:412
  357.8 17.2 %key_backward.2 = (f32[2,192,1024]{2,1,0:T(8,128)S(1)}, bf16[2,192,1024]{2,1,0:T(8,128)(2,1)S(1)}) custom-call(bf16[64,64]{1,0:T(8,128)(2,1)S(1)} %bitcast.190, bf16[64,128]{1,0:T(8,128)(2,1)S(1)} %pad_maximum_fusion.24.planes_t, bf16[80,2048]{1,0:T(8,128)(2,1)S(1)} %copy-done.14, bf16[384,1024]{1,0:T(8,128)(2,1)S(1)} %bitcast.180, ...), custom_call_target="tpu_custom_call" | custom-call | flops 19800000512 | bytes 4194304 | tf_op jit(solution)/shard_map/key_backward/pallas_call | solution.py:230
  375.1 4.9 %collective-permute-start.73 = (bf16[384,768]{1,0:T(8,128)(2,1)S(1)}, bf16[384,768]{1,0:T(8,128)(2,1)S(1)}, u32[]{:S(2)}, u32[]{:S(2)}) collective-permute-start(bf16[384,768]{1,0:T(8,128)(2,1)S(1)} %pad_maximum_fusion.7), channel_id=1, source_target_pairs={{0,1},{1,0},{2,3},{3,2},{4,5},{5,4},{6,7},{7,6},{8,9},{9,8},{10,11... | collective-permute-start | bytes 1769480 | tf_op jit(solution)/shard_map/ppermute | solution.py:412
  385.7 3.3 copy.45
  390.0 10.3 %collective-permute-done.44 = bf16[2,192,1024]{2,1,0:T(8,128)(2,1)} collective-permute-done((bf16[2,192,1024]{2,1,0:T(8,128)(2,1)}, bf16[2,192,1024]{2,1,0:T(8,128)(2,1)}, u32[]{:S(2)}, u32[]{:S(2)}) %collective-permute-start.44) | collective-permute-done | bytes 786464 | tf_op jit(solution)/shard_map/ppermute | solution.py:415
  406.2 3.4 collective-permute-done.52
  419.8 4.9 %collective-permute-start.61 = (bf16[1152,192]{0,1:T(8,128)(2,1)S(1)}, bf16[1152,192]{0,1:T(8,128)(2,1)S(1)}, u32[]{:S(2)}, u32[]{:S(2)}) collective-permute-start(bf16[1152,192]{0,1:T(8,128)(2,1)S(1)} %constant_dynamic-slice_fusion.4), channel_id=1, source_target_pairs={{0,1},{1,0},{2,3},{3,2},{4,5},{5,4},{6,7},{7,6},{8,9},{9,8},{10,11... | collective-permute-start | bytes 1327112 | tf_op jit(solution)/shard_map/ppermute | solution.py:412
  429.7 6.1 %collective-permute-done.67 = bf16[240,768]{1,0:T(8,128)(2,1)S(1)} collective-permute-done((bf16[240,768]{1,0:T(8,128)(2,1)S(1)}, bf16[240,768]{1,0:T(8,128)(2,1)S(1)}, u32[]{:S(2)}, u32[]{:S(2)}) %collective-permute-start.67) | collective-permute-done | bytes 368672 | tf_op jit(solution)/shard_map/ppermute | solution.py:419
  436.0 2.8 collective-permute-start.68
  438.8 3.4 collective-permute-done.57
  445.9 4.5 collective-permute-done.68
  452.5 3.2 collective-permute-done.62
  457.5 3.2 collective-permute-done.60
  461.5 4.1 copy.43
  465.6 3.2 collective-permute-done.63
  469.9 4.8 collective-permute-done.64
  474.9 2.7 collective-permute-start.65
  (332 shorter events, 125.7 us)
Async XLA Ops:
  6.0 14.0 %collective-permute-start = (bf16[128,768]{1,0:T(8,128)(2,1)}, bf16[128,768]{1,0:T(8,128)(2,1)}, u32[]{:S(2)}, u32[]{:S(2)}) collective-permute-start(bf16[128,768]{1,0:T(8,128)(2,1)} %bitcast.174), channel_id=1, source_target_pairs={{0,16},{8,24},{16,0},{24,8},{1,17},{9,25},{17,1},{25,9},{2,18},{10... | collective-permute-start | bytes 589832 | tf_op jit(solution)/shard_map/ppermute | solution.py:419
  36.5 20.9 %collective-permute-start.6 = (bf16[384,1024]{1,0:T(8,128)(2,1)S(1)}, bf16[384,1024]{1,0:T(8,128)(2,1)S(1)}, u32[]{:S(2)}, u32[]{:S(2)}) collective-permute-start(bf16[384,1024]{1,0:T(8,128)(2,1)S(1)} %bitcast.177), channel_id=1, source_target_pairs={{0,8},{8,0},{16,24},{24,16},{1,9},{9,1},{17,25},{25,17},{2,10},{10... | collective-permute-start | bytes 2359304 | tf_op jit(solution)/shard_map/ppermute | solution.py:415
  39.3 31.5 %collective-permute-start.21 = (bf16[864,768]{1,0:T(8,128)(2,1)S(1)}, bf16[864,768]{1,0:T(8,128)(2,1)}, u32[]{:S(2)}, u32[]{:S(2)}) collective-permute-start(bf16[864,768]{1,0:T(8,128)(2,1)S(1)} %pad_maximum_fusion.4.refs_4_), channel_id=1, source_target_pairs={{0,6},{2,4},{4,2},{6,0},{1,7},{3,5},{5,3},{7,1},{8,14},{10,12},{12... | collective-permute-start | bytes 3981320 | tf_op jit(solution)/shard_map/ppermute | solution.py:422
  40.5 59.3 %collective-permute-start.19 = (bf16[864,768]{1,0:T(8,128)(2,1)S(1)}, bf16[864,768]{1,0:T(8,128)(2,1)}, u32[]{:S(2)}, u32[]{:S(2)}) collective-permute-start(bf16[864,768]{1,0:T(8,128)(2,1)S(1)} %pad_maximum_fusion.4.refs_4_), channel_id=1, source_target_pairs={{0,4},{2,6},{4,0},{6,2},{1,5},{3,7},{5,1},{7,3},{8,12},{10,14},{12... | collective-permute-start | bytes 3981320 | tf_op jit(solution)/shard_map/ppermute | solution.py:422
  41.7 58.6 %collective-permute-start.17 = (bf16[864,768]{1,0:T(8,128)(2,1)S(1)}, bf16[864,768]{1,0:T(8,128)(2,1)}, u32[]{:S(2)}, u32[]{:S(2)}) collective-permute-start(bf16[864,768]{1,0:T(8,128)(2,1)S(1)} %pad_maximum_fusion.4.refs_4_), channel_id=1, source_target_pairs={{0,2},{2,0},{4,6},{6,4},{1,3},{3,1},{5,7},{7,5},{8,10},{10,8},{12,... | collective-permute-start | bytes 3981320 | tf_op jit(solution)/shard_map/ppermute | solution.py:422
  42.0 14.3 %collective-permute-start.1 = (bf16[8,8,64]{2,0,1:T(8,128)(2,1)S(1)}, bf16[8,8,64]{2,0,1:T(8,128)(2,1)S(1)}, u32[]{:S(2)}, u32[]{:S(2)}) collective-permute-start(bf16[8,8,64]{2,0,1:T(8,128)(2,1)S(1)} %fusion.30), channel_id=1, source_target_pairs={{0,0},{8,1},{16,8},{24,9},{1,16},{9,17},{17,24},{25,25},{2,2},{10,... | collective-permute-start | bytes 24584 | tf_op jit(solution)/shard_map/ppermute | solution.py:438
  57.4 42.9 %collective-permute-start.7 = (bf16[384,1024]{1,0:T(8,128)(2,1)S(1)}, bf16[384,1024]{1,0:T(8,128)(2,1)S(1)}, u32[]{:S(2)}, u32[]{:S(2)}) collective-permute-start(bf16[384,1024]{1,0:T(8,128)(2,1)S(1)} %collective-permute-done.6.ka.va), channel_id=1, source_target_pairs={{0,1},{1,0},{2,3},{3,2},{4,5},{5,4},{6,7},{7,6},{8,9},{9,8},{10,11... | collective-permute-start | bytes 2359304 | tf_op jit(solution)/shard_map/ppermute | solution.py:412
  66.9 48.9 %collective-permute-start.5 = (bf16[192,1024]{1,0:T(8,128)(2,1)S(1)}, bf16[192,1024]{1,0:T(8,128)(2,1)S(1)}, u32[]{:S(2)}, u32[]{:S(2)}) collective-permute-start(bf16[192,1024]{1,0:T(8,128)(2,1)S(1)} %fusion.5.qa), channel_id=1, source_target_pairs={{0,1},{1,0},{2,3},{3,2},{4,5},{5,4},{6,7},{7,6},{8,9},{9,8},{10,11... | collective-permute-start | bytes 1179656 | tf_op jit(solution)/shard_map/ppermute | solution.py:412
  70.8 39.1 %collective-permute-start.11 = (bf16[192,1024]{1,0:T(8,128)(2,1)S(1)}, bf16[192,1024]{1,0:T(8,128)(2,1)S(1)}, u32[]{:S(2)}, u32[]{:S(2)}) collective-permute-start(bf16[192,1024]{1,0:T(8,128)(2,1)S(1)} %collective-permute-done.10.qa), channel_id=1, source_target_pairs={{0,1},{1,0},{2,3},{3,2},{4,5},{5,4},{6,7},{7,6},{8,9},{9,8},{10,11... | collective-permute-start | bytes 1179656 | tf_op jit(solution)/shard_map/ppermute | solution.py:412
  99.8 42.2 %collective-permute-start.22 = (bf16[864,768]{1,0:T(8,128)(2,1)}, bf16[864,768]{1,0:T(8,128)(2,1)}, u32[]{:S(2)}, u32[]{:S(2)}) collective-permute-start(bf16[864,768]{1,0:T(8,128)(2,1)} %collective-permute-done.21.refs_10_), channel_id=1, source_target_pairs={{0,1},{1,0},{2,3},{3,2},{4,5},{5,4},{6,7},{7,6},{8,9},{9,8},{10,11... | collective-permute-start | bytes 3981320 | tf_op jit(solution)/shard_map/ppermute | solution.py:412
  100.3 41.7 %collective-permute-start.20 = (bf16[864,768]{1,0:T(8,128)(2,1)}, bf16[864,768]{1,0:T(8,128)(2,1)}, u32[]{:S(2)}, u32[]{:S(2)}) collective-permute-start(bf16[864,768]{1,0:T(8,128)(2,1)} %collective-permute-done.19.refs_8_), channel_id=1, source_target_pairs={{0,1},{1,0},{2,3},{3,2},{4,5},{5,4},{6,7},{7,6},{8,9},{9,8},{10,11... | collective-permute-start | bytes 3981320 | tf_op jit(solution)/shard_map/ppermute | solution.py:412
  100.3 41.7 %collective-permute-start.18 = (bf16[864,768]{1,0:T(8,128)(2,1)}, bf16[864,768]{1,0:T(8,128)(2,1)}, u32[]{:S(2)}, u32[]{:S(2)}) collective-permute-start(bf16[864,768]{1,0:T(8,128)(2,1)} %collective-permute-done.17.refs_6_), channel_id=1, source_target_pairs={{0,1},{1,0},{2,3},{3,2},{4,5},{5,4},{6,7},{7,6},{8,9},{9,8},{10,11... | collective-permute-start | bytes 3981320 | tf_op jit(solution)/shard_map/ppermute | solution.py:412
  122.6 10.7 %collective-permute-start.13 = (bf16[192,1024]{1,0:T(8,128)(2,1)S(1)}, bf16[192,1024]{1,0:T(8,128)(2,1)S(1)}, u32[]{:S(2)}, u32[]{:S(2)}) collective-permute-start(bf16[192,1024]{1,0:T(8,128)(2,1)S(1)} %add_convert_fusion.10), channel_id=1, source_target_pairs={{0,8},{8,0},{16,24},{24,16},{1,9},{9,1},{17,25},{25,17},{2,10},{10... | collective-permute-start | bytes 1179656 | tf_op jit(solution)/shard_map/ppermute | solution.py:415
  165.6 13.9 %collective-permute-start.26 = (bf16[192,1024]{1,0:T(8,128)(2,1)S(1)}, bf16[192,1024]{1,0:T(8,128)(2,1)S(1)}, u32[]{:S(2)}, u32[]{:S(2)}) collective-permute-start(bf16[192,1024]{1,0:T(8,128)(2,1)S(1)} %constant_dynamic-update-slice_fusion.ga), channel_id=1, source_target_pairs={{0,1},{1,0},{2,3},{3,2},{4,5},{5,4},{6,7},{7,6},{8,9},{9,8},{10,11... | collective-permute-start | bytes 1179656 | tf_op jit(solution)/shard_map/ppermute | solution.py:412
  180.2 33.4 %collective-permute-start.27 = (bf16[4,480,768]{2,1,0:T(8,128)(2,1)}, bf16[4,480,768]{2,1,0:T(8,128)(2,1)}, u32[]{:S(2)}, u32[]{:S(2)}) collective-permute-start(bf16[4,480,768]{2,1,0:T(8,128)(2,1)} %get-tuple-element.71), channel_id=1, source_target_pairs={{0,1},{1,0},{2,3},{3,2},{4,5},{5,4},{6,7},{7,6},{8,9},{9,8},{10,11... | collective-permute-start | bytes 8847368 | tf_op jit(solution)/shard_map/ppermute | solution.py:412
  180.2 29.6 %collective-permute-start.28 = (bf16[4,384,768]{2,1,0:T(8,128)(2,1)}, bf16[4,384,768]{2,1,0:T(8,128)(2,1)}, u32[]{:S(2)}, u32[]{:S(2)}) collective-permute-start(bf16[4,384,768]{2,1,0:T(8,128)(2,1)} %get-tuple-element.74), channel_id=1, source_target_pairs={{0,1},{1,0},{2,3},{3,2},{4,5},{5,4},{6,7},{7,6},{8,9},{9,8},{10,11... | collective-permute-start | bytes 7077896 | tf_op jit(solution)/shard_map/ppermute | solution.py:412
  180.9 26.5 %collective-permute-start.29 = (bf16[192,1024]{1,0:T(8,128)(2,1)S(1)}, bf16[192,1024]{1,0:T(8,128)(2,1)}, u32[]{:S(2)}, u32[]{:S(2)}) collective-permute-start(bf16[192,1024]{1,0:T(8,128)(2,1)S(1)} %constant_dynamic-update-slice_fusion.ga), channel_id=1, source_target_pairs={{0,8},{8,0},{16,24},{24,16},{1,9},{9,1},{17,25},{25,17},{2,10},{10... | collective-permute-start | bytes 1179656 | tf_op jit(solution)/shard_map/ppermute | solution.py:415
  213.0 37.3 %collective-permute-start.40 = (bf16[2,384,768]{2,1,0:T(8,128)(2,1)S(1)}, bf16[2,384,768]{2,1,0:T(8,128)(2,1)S(1)}, u32[]{:S(2)}, u32[]{:S(2)}) collective-permute-start(bf16[2,384,768]{2,1,0:T(8,128)(2,1)S(1)} %stack.192), channel_id=1, source_target_pairs={{0,4},{2,6},{4,0},{6,2},{1,5},{3,7},{5,1},{7,3},{8,12},{10,14},{12... | collective-permute-start | bytes 3538952 | tf_op jit(solution)/shard_map/ppermute | solution.py:422
  237.8 10.9 %collective-permute-start.31 = (bf16[128,768]{1,0:T(8,128)(2,1)S(1)}, bf16[128,768]{1,0:T(8,128)(2,1)S(1)}, u32[]{:S(2)}, u32[]{:S(2)}) collective-permute-start(bf16[128,768]{1,0:T(8,128)(2,1)S(1)} %get-tuple-element.171), channel_id=1, source_target_pairs={{0,16},{8,24},{16,0},{24,8},{1,17},{9,25},{17,1},{25,9},{2,18},{10... | collective-permute-start | bytes 589832 | tf_op jit(solution)/shard_map/ppermute | solution.py:419
  239.0 13.1 %collective-permute-start.36 = (bf16[192,1024]{1,0:T(8,128)(2,1)S(1)}, bf16[192,1024]{1,0:T(8,128)(2,1)S(1)}, u32[]{:S(2)}, u32[]{:S(2)}) collective-permute-start(bf16[192,1024]{1,0:T(8,128)(2,1)S(1)} %get-tuple-element.83), channel_id=1, source_target_pairs={{0,1},{1,0},{2,3},{3,2},{4,5},{5,4},{6,7},{7,6},{8,9},{9,8},{10,11... | collective-permute-start | bytes 1179656 | tf_op jit(solution)/shard_map/ppermute | solution.py:412
  249.3 12.2 %collective-permute-start.32 = (bf16[2,128,768]{2,1,0:T(8,128)(2,1)S(1)}, bf16[2,128,768]{2,1,0:T(8,128)(2,1)S(1)}, u32[]{:S(2)}, u32[]{:S(2)}) collective-permute-start(bf16[2,128,768]{2,1,0:T(8,128)(2,1)S(1)} %get-tuple-element.169), channel_id=1, source_target_pairs={{0,2},{2,0},{4,6},{6,4},{1,3},{3,1},{5,7},{7,5},{8,10},{10,8},{12,... | collective-permute-start | bytes 1179656 | tf_op jit(solution)/shard_map/ppermute | solution.py:422
  250.3 16.9 %collective-permute-start.34 = (bf16[2,128,768]{2,1,0:T(8,128)(2,1)S(1)}, bf16[2,128,768]{2,1,0:T(8,128)(2,1)S(1)}, u32[]{:S(2)}, u32[]{:S(2)}) collective-permute-start(bf16[2,128,768]{2,1,0:T(8,128)(2,1)S(1)} %get-tuple-element.169), channel_id=1, source_target_pairs={{0,6},{2,4},{4,2},{6,0},{1,7},{3,5},{5,3},{7,1},{8,14},{10,12},{12... | collective-permute-start | bytes 1179656 | tf_op jit(solution)/shard_map/ppermute | solution.py:422
  251.6 27.5 %collective-permute-start.41 = (bf16[384,768]{1,0:T(8,128)(2,1)S(1)}, bf16[384,768]{1,0:T(8,128)(2,1)S(1)}, u32[]{:S(2)}, u32[]{:S(2)}) collective-permute-start(bf16[384,768]{1,0:T(8,128)(2,1)S(1)} %fusion.21), channel_id=1, source_target_pairs={{0,2},{2,0},{4,6},{6,4},{1,3},{3,1},{5,7},{7,5},{8,10},{10,8},{12,... | collective-permute-start | bytes 1769480 | tf_op jit(solution)/shard_map/ppermute | solution.py:422
  252.6 128.6 %collective-permute-start.53 = (bf16[3,384,192]{1,2,0:T(8,128)(2,1)S(1)}, bf16[3,384,192]{1,2,0:T(8,128)(2,1)}, u32[]{:S(2)}, u32[]{:S(2)}) collective-permute-start(bf16[3,384,192]{1,2,0:T(8,128)(2,1)S(1)} %copy-done.23), channel_id=1, source_target_pairs={{0,6},{2,4},{4,2},{6,0},{1,7},{3,5},{5,3},{7,1},{8,14},{10,12},{12... | collective-permute-start | bytes 1327112 | tf_op jit(solution)/shard_map/ppermute | solution.py:422
  257.9 25.5 %collective-permute-start.35 = (bf16[192,1024]{1,0:T(8,128)(2,1)S(1)}, bf16[192,1024]{1,0:T(8,128)(2,1)S(1)}, u32[]{:S(2)}, u32[]{:S(2)}) collective-permute-start(bf16[192,1024]{1,0:T(8,128)(2,1)S(1)} %get-tuple-element.81), channel_id=1, source_target_pairs={{0,1},{1,0},{2,3},{3,2},{4,5},{5,4},{6,7},{7,6},{8,9},{9,8},{10,11... | collective-permute-start | bytes 1179656 | tf_op jit(solution)/shard_map/ppermute | solution.py:412
  261.6 58.7 %collective-permute-start.38 = (bf16[2,480,768]{2,1,0:T(8,128)(2,1)S(1)}, bf16[2,480,768]{2,1,0:T(8,128)(2,1)S(1)}, u32[]{:S(2)}, u32[]{:S(2)}) collective-permute-start(bf16[2,480,768]{2,1,0:T(8,128)(2,1)S(1)} %pad_maximum_fusion.3), channel_id=1, source_target_pairs={{0,2},{2,0},{4,6},{6,4},{1,3},{3,1},{5,7},{7,5},{8,10},{10,8},{12,... | collective-permute-start | bytes 4423688 | tf_op jit(solution)/shard_map/ppermute | solution.py:422
  267.2 17.1 %collective-permute-start.37 = (bf16[192,1024]{1,0:T(8,128)(2,1)S(1)}, bf16[192,1024]{1,0:T(8,128)(2,1)S(1)}, u32[]{:S(2)}, u32[]{:S(2)}) collective-permute-start(bf16[192,1024]{1,0:T(8,128)(2,1)S(1)} %add_convert_fusion.8), channel_id=1, source_target_pairs={{0,8},{8,0},{16,24},{24,16},{1,9},{9,1},{17,25},{25,17},{2,10},{10... | collective-permute-start | bytes 1179656 | tf_op jit(solution)/shard_map/ppermute | solution.py:415
  283.4 99.5 %collective-permute-start.50 = (bf16[3,384,192]{1,2,0:T(8,128)(2,1)S(1)}, bf16[3,384,192]{1,2,0:T(8,128)(2,1)}, u32[]{:S(2)}, u32[]{:S(2)}) collective-permute-start(bf16[3,384,192]{1,2,0:T(8,128)(2,1)S(1)} %copy-done.23), channel_id=1, source_target_pairs={{0,4},{2,6},{4,0},{6,2},{1,5},{3,7},{5,1},{7,3},{8,12},{10,14},{12... | collective-permute-start | bytes 1327112 | tf_op jit(solution)/shard_map/ppermute | solution.py:422
  284.3 99.1 %collective-permute-start.47 = (bf16[3,384,192]{1,2,0:T(8,128)(2,1)S(1)}, bf16[3,384,192]{1,2,0:T(8,128)(2,1)}, u32[]{:S(2)}, u32[]{:S(2)}) collective-permute-start(bf16[3,384,192]{1,2,0:T(8,128)(2,1)S(1)} %copy-done.23), channel_id=1, source_target_pairs={{0,2},{2,0},{4,6},{6,4},{1,3},{3,1},{5,7},{7,5},{8,10},{10,8},{12,... | collective-permute-start | bytes 1327112 | tf_op jit(solution)/shard_map/ppermute | solution.py:422
  285.6 56.9 %collective-permute-start.71 = (bf16[192,768]{1,0:T(8,128)(2,1)S(1)}, bf16[192,768]{1,0:T(8,128)(2,1)S(1)}, u32[]{:S(2)}, u32[]{:S(2)}) collective-permute-start(bf16[192,768]{1,0:T(8,128)(2,1)S(1)} %fusion.22), channel_id=1, source_target_pairs={{0,16},{8,24},{16,0},{24,8},{1,17},{9,25},{17,1},{25,9},{2,18},{10... | collective-permute-start | bytes 884744 | tf_op jit(solution)/shard_map/ppermute | solution.py:419
  341.5 14.7 %collective-permute-start.39 = (bf16[480,768]{1,0:T(8,128)(2,1)S(1)}, bf16[480,768]{1,0:T(8,128)(2,1)S(1)}, u32[]{:S(2)}, u32[]{:S(2)}) collective-permute-start(bf16[480,768]{1,0:T(8,128)(2,1)S(1)} %fusion.18), channel_id=1, source_target_pairs={{0,4},{2,6},{4,0},{6,2},{1,5},{3,7},{5,1},{7,3},{8,12},{10,14},{12... | collective-permute-start | bytes 2211848 | tf_op jit(solution)/shard_map/ppermute | solution.py:422
  348.7 26.4 %collective-permute-start.43 = (bf16[2,192,1024]{2,1,0:T(8,128)(2,1)S(1)}, bf16[2,192,1024]{2,1,0:T(8,128)(2,1)S(1)}, u32[]{:S(2)}, u32[]{:S(2)}) collective-permute-start(bf16[2,192,1024]{2,1,0:T(8,128)(2,1)S(1)} %get-tuple-element.89), channel_id=1, source_target_pairs={{0,1},{1,0},{2,3},{3,2},{4,5},{5,4},{6,7},{7,6},{8,9},{9,8},{10,11... | collective-permute-start | bytes 2359304 | tf_op jit(solution)/shard_map/ppermute | solution.py:412
  356.6 24.7 %collective-permute-start.66 = (bf16[240,768]{1,0:T(8,128)(2,1)S(1)}, bf16[240,768]{1,0:T(8,128)(2,1)S(1)}, u32[]{:S(2)}, u32[]{:S(2)}) collective-permute-start(bf16[240,768]{1,0:T(8,128)(2,1)S(1)} %constant_dynamic-slice_fusion.2), channel_id=1, source_target_pairs={{0,8},{8,0},{16,24},{24,16},{1,9},{9,1},{17,25},{25,17},{2,10},{10... | collective-permute-start | bytes 1105928 | tf_op jit(solution)/shard_map/ppermute | solution.py:415
  381.3 19.1 %collective-permute-start.44 = (bf16[2,192,1024]{2,1,0:T(8,128)(2,1)}, bf16[2,192,1024]{2,1,0:T(8,128)(2,1)}, u32[]{:S(2)}, u32[]{:S(2)}) collective-permute-start(bf16[2,192,1024]{2,1,0:T(8,128)(2,1)} %add_convert_fusion.3), channel_id=1, source_target_pairs={{0,8},{8,0},{16,24},{24,16},{1,9},{9,1},{17,25},{25,17},{2,10},{10... | collective-permute-start | bytes 2359304 | tf_op jit(solution)/shard_map/ppermute | solution.py:415
  382.8 29.0 %collective-permute-start.56 = (bf16[3,384,192]{1,2,0:T(8,128)(2,1)}, bf16[3,384,192]{1,2,0:T(8,128)(2,1)}, u32[]{:S(2)}, u32[]{:S(2)}) collective-permute-start(bf16[3,384,192]{1,2,0:T(8,128)(2,1)} %collective-permute-done.53), channel_id=1, source_target_pairs={{0,1},{1,0},{2,3},{3,2},{4,5},{5,4},{6,7},{7,6},{8,9},{9,8},{10,11... | collective-permute-start | bytes 1327112 | tf_op jit(solution)/shard_map/ppermute | solution.py:412
  383.4 36.4 %collective-permute-start.55 = (bf16[3,384,192]{1,2,0:T(8,128)(2,1)}, bf16[3,384,192]{1,2,0:T(8,128)(2,1)}, u32[]{:S(2)}, u32[]{:S(2)}) collective-permute-start(bf16[3,384,192]{1,2,0:T(8,128)(2,1)} %collective-permute-done.50), channel_id=1, source_target_pairs={{0,1},{1,0},{2,3},{3,2},{4,5},{5,4},{6,7},{7,6},{8,9},{9,8},{10,11... | collective-permute-start | bytes 1327112 | tf_op jit(solution)/shard_map/ppermute | solution.py:412
  383.5 44.5 %collective-permute-start.54 = (bf16[3,384,192]{1,2,0:T(8,128)(2,1)}, bf16[3,384,192]{1,2,0:T(8,128)(2,1)}, u32[]{:S(2)}, u32[]{:S(2)}) collective-permute-start(bf16[3,384,192]{1,2,0:T(8,128)(2,1)} %collective-permute-done.47), channel_id=1, source_target_pairs={{0,1},{1,0},{2,3},{3,2},{4,5},{5,4},{6,7},{7,6},{8,9},{9,8},{10,11... | collective-permute-start | bytes 1327112 | tf_op jit(solution)/shard_map/ppermute | solution.py:412
  389.0 15.9 %collective-permute-start.51 = (bf16[192,256]{1,0:T(8,128)(2,1)}, bf16[192,256]{1,0:T(8,128)(2,1)S(1)}, u32[]{:S(2)}, u32[]{:S(2)}) collective-permute-start(bf16[192,256]{1,0:T(8,128)(2,1)} %get-tuple-element.165), channel_id=1, source_target_pairs={{0,6},{2,4},{4,2},{6,0},{1,7},{3,5},{5,3},{7,1},{8,14},{10,12},{12... | collective-permute-start | bytes 294920 | tf_op jit(solution)/shard_map/ppermute | solution.py:422
  404.9 21.2 %collective-permute-start.45 = (bf16[192,256]{1,0:T(8,128)(2,1)S(1)}, bf16[192,256]{1,0:T(8,128)(2,1)S(1)}, u32[]{:S(2)}, u32[]{:S(2)}) collective-permute-start(bf16[192,256]{1,0:T(8,128)(2,1)S(1)} %copy-done.41), channel_id=1, source_target_pairs={{0,2},{2,0},{4,6},{6,4},{1,3},{3,1},{5,7},{7,5},{8,10},{10,8},{12,... | collective-permute-start | bytes 294920 | tf_op jit(solution)/shard_map/ppermute | solution.py:422
  415.4 20.4 %collective-permute-start.67 = (bf16[240,768]{1,0:T(8,128)(2,1)S(1)}, bf16[240,768]{1,0:T(8,128)(2,1)S(1)}, u32[]{:S(2)}, u32[]{:S(2)}) collective-permute-start(bf16[240,768]{1,0:T(8,128)(2,1)S(1)} %copy-done.40), channel_id=1, source_target_pairs={{0,16},{8,24},{16,0},{24,8},{1,17},{9,25},{17,1},{25,9},{2,18},{10... | collective-permute-start | bytes 1105928 | tf_op jit(solution)/shard_map/ppermute | solution.py:419
  419.8 25.2 %collective-permute-start.61 = (bf16[1152,192]{0,1:T(8,128)(2,1)S(1)}, bf16[1152,192]{0,1:T(8,128)(2,1)S(1)}, u32[]{:S(2)}, u32[]{:S(2)}) collective-permute-start(bf16[1152,192]{0,1:T(8,128)(2,1)S(1)} %constant_dynamic-slice_fusion.4), channel_id=1, source_target_pairs={{0,1},{1,0},{2,3},{3,2},{4,5},{5,4},{6,7},{7,6},{8,9},{9,8},{10,11... | collective-permute-start | bytes 1327112 | tf_op jit(solution)/shard_map/ppermute | solution.py:412
  429.6 12.6 %collective-permute-start.57 = (bf16[128,768]{1,0:T(8,128)(2,1)S(1)}, bf16[128,768]{1,0:T(8,128)(2,1)S(1)}, u32[]{:S(2)}, u32[]{:S(2)}) collective-permute-start(bf16[128,768]{1,0:T(8,128)(2,1)S(1)} %get-tuple-element.163), channel_id=1, source_target_pairs={{0,16},{8,24},{16,0},{24,8},{1,17},{9,25},{17,1},{25,9},{2,18},{10... | collective-permute-start | bytes 589832 | tf_op jit(solution)/shard_map/ppermute | solution.py:419
  436.0 14.4 %collective-permute-start.68 = (bf16[240,768]{1,0:T(8,128)(2,1)S(1)}, bf16[240,768]{1,0:T(8,128)(2,1)S(1)}, u32[]{:S(2)}, u32[]{:S(2)}) collective-permute-start(bf16[240,768]{1,0:T(8,128)(2,1)S(1)} %add_convert_fusion.11), channel_id=1, source_target_pairs={{0,8},{8,0},{16,24},{24,16},{1,9},{9,1},{17,25},{25,17},{2,10},{10... | collective-permute-start | bytes 1105928 | tf_op jit(solution)/shard_map/ppermute | solution.py:415
  442.3 15.2 %collective-permute-start.59 = (bf16[2,128,768]{2,1,0:T(8,128)(2,1)S(1)}, bf16[2,128,768]{2,1,0:T(8,128)(2,1)S(1)}, u32[]{:S(2)}, u32[]{:S(2)}) collective-permute-start(bf16[2,128,768]{2,1,0:T(8,128)(2,1)S(1)} %get-tuple-element.161), channel_id=1, source_target_pairs={{0,4},{2,6},{4,0},{6,2},{1,5},{3,7},{5,1},{7,3},{8,12},{10,14},{12... | collective-permute-start | bytes 1179656 | tf_op jit(solution)/shard_map/ppermute | solution.py:422
  443.1 14.4 %collective-permute-start.58 = (bf16[2,128,768]{2,1,0:T(8,128)(2,1)S(1)}, bf16[2,128,768]{2,1,0:T(8,128)(2,1)S(1)}, u32[]{:S(2)}, u32[]{:S(2)}) collective-permute-start(bf16[2,128,768]{2,1,0:T(8,128)(2,1)S(1)} %get-tuple-element.161), channel_id=1, source_target_pairs={{0,2},{2,0},{4,6},{6,4},{1,3},{3,1},{5,7},{7,5},{8,10},{10,8},{12,... | collective-permute-start | bytes 1179656 | tf_op jit(solution)/shard_map/ppermute | solution.py:422
  444.3 16.4 %collective-permute-start.60 = (bf16[2,128,768]{2,1,0:T(8,128)(2,1)S(1)}, bf16[2,128,768]{2,1,0:T(8,128)(2,1)S(1)}, u32[]{:S(2)}, u32[]{:S(2)}) collective-permute-start(bf16[2,128,768]{2,1,0:T(8,128)(2,1)S(1)} %get-tuple-element.161), channel_id=1, source_target_pairs={{0,6},{2,4},{4,2},{6,0},{1,7},{3,5},{5,3},{7,1},{8,14},{10,12},{12... | collective-permute-start | bytes 1179656 | tf_op jit(solution)/shard_map/ppermute | solution.py:422
  450.6 19.3 %collective-permute-start.69 = (bf16[480,768]{1,0:T(8,128)(2,1)S(1)}, bf16[480,768]{1,0:T(8,128)(2,1)S(1)}, u32[]{:S(2)}, u32[]{:S(2)}) collective-permute-start(bf16[480,768]{1,0:T(8,128)(2,1)S(1)} %pad_maximum_fusion.6), channel_id=1, source_target_pairs={{0,1},{1,0},{2,3},{3,2},{4,5},{5,4},{6,7},{7,6},{8,9},{9,8},{10,11... | collective-permute-start | bytes 2211848 | tf_op jit(solution)/shard_map/ppermute | solution.py:412
  455.9 12.9 %collective-permute-start.63 = (bf16[576,192]{0,1:T(8,128)(2,1)S(1)}, bf16[576,192]{0,1:T(8,128)(2,1)S(1)}, u32[]{:S(2)}, u32[]{:S(2)}) collective-permute-start(bf16[576,192]{0,1:T(8,128)(2,1)S(1)} %fusion.25), channel_id=1, source_target_pairs={{0,16},{8,24},{16,0},{24,8},{1,17},{9,25},{17,1},{25,9},{2,18},{10... | collective-permute-start | bytes 663560 | tf_op jit(solution)/shard_map/ppermute | solution.py:419
  (81 other events, 705.1 us)

commit v3 on v2

--- a/solution.py
+++ b/solution.py
@@ -83,16 +83,13 @@
         out[0, at, :] = part.astype(out.dtype)
 
 
-def query_kernel(planes, qa, qb, tables, ea, eb, *, chunk):
-    _, upper, lower = sides(both(qa, qb), planes[...])
+def query_kernel(planes, q, tables, out, *, chunk):
+    _, upper, lower = sides(q[...], planes[...])
     low, high = half_codes(upper, lower)
-    width = qa.shape[1]
-    acc = jnp.zeros((HEAD_DIM, 2 * width), f32)
+    acc = jnp.zeros((HEAD_DIM, q.shape[1]), f32)
     for c in range(0, 16, chunk):
         acc += dot(tables[0, 128 * c : 128 * (c + chunk), :], code_chunk(low, high, c, chunk), TN)
-    acc = acc * (1.0 / HASHES)
-    ea[...] = acc[:, :width].astype(ea.dtype)
-    eb[...] = acc[:, width:].astype(eb.dtype)
+    out[...] = (acc * (1.0 / HASHES)).astype(out.dtype)
 
 
 def query_back_kernel(planes, planes_t, bits, qa, ga, qb, gb, tables, *refs, chunk):
@@ -117,25 +114,22 @@
     db[...] = back[:, width:].astype(db.dtype)
 
 
-def key_back_kernel(planes, planes_t, bits, ka, va, kb, vb, grad_tables, da, db, *, chunk):
-    rows = both(ka, kb)
+def key_back_kernel(planes, planes_t, bits, keys, vals, grad_tables, out, *, chunk):
+    rows = keys[...]
     inv, upper, lower = sides(rows, planes[...])
     low, high = half_codes(upper, lower)
-    values = both(va, vb)
-    width = ka.shape[1]
-    sums = jnp.zeros((bits.shape[0], 2 * width), f32)
-    grad_values = jnp.zeros((HEAD_DIM, 2 * width), f32)
+    values = vals[...]
+    width = keys.shape[1]
+    sums = jnp.zeros((bits.shape[0], width), f32)
+    grad_values = jnp.zeros((HEAD_DIM, width), f32)
     for c in range(0, 16, chunk):
         at = slice(128 * c, 128 * (c + chunk))
         codes = code_chunk(low, high, c, chunk)
         grad_values += dot(grad_tables[0, at, :], codes, TN)
         weighted = dot(grad_tables[0, at, :], values, NN).astype(bf16) * codes
         sums += dot(bits[:, at], weighted, NN)
-    back = pull_back(rows, planes_t[...], inv, upper, sums)
-    da[0] = back[:, :width].astype(da.dtype)
-    db[0] = back[:, width:].astype(db.dtype)
-    da[1] = grad_values[:, :width].astype(da.dtype)
-    db[1] = grad_values[:, width:].astype(db.dtype)
+    out[0] = pull_back(rows, planes_t[...], inv, upper, sums).astype(out.dtype)
+    out[1] = grad_values.astype(out.dtype)
 
 
 def bit_rows():
@@ -168,7 +162,7 @@
         out_shape=out_shape,
         compiler_params=pltpu.CompilerParams(vmem_limit_bytes=48 << 20),
         cost_estimate=pl.CostEstimate(
-            flops=int(micros * 1.1e9), bytes_accessed=4 << 20, transcendentals=0
+            flops=int(micros * 1.1e9), bytes_accessed=1 << 20, transcendentals=0
         ),
         name=name,
     )
@@ -192,17 +186,17 @@
     )(*args)
 
 
-def query_estimates(planes, q_a, q_b, tables, kind_a, kind_b):
-    heads, width = q_a.shape[0] // HEAD_DIM, q_a.shape[1]
+def query_estimates(planes, q, tables, kind):
+    heads, width = q.shape[0] // HEAD_DIM, q.shape[1]
     return call(
         partial(query_kernel, chunk=2),
         heads,
-        7,
+        4,
         "query_estimates",
-        [whole(64, 64), per_head(width), per_head(width), table_spec()],
-        [per_head(width), per_head(width)],
-        [jax.ShapeDtypeStruct(q_a.shape, kind) for kind in (kind_a, kind_b)],
-    )(planes, q_a, q_b, tables)
+        [whole(64, 64), per_head(width), table_spec()],
+        per_head(width),
+        jax.ShapeDtypeStruct(q.shape, kind),
+    )(planes, q, tables)
 
 
 def query_backward(planes, planes_t, bits, q_a, g_a, q_b, g_b, tables, start, kind_a, kind_b):
@@ -224,20 +218,18 @@
     )(*args)
 
 
-def key_backward(planes, planes_t, bits, kv_a, kv_b, grad_tables, kind_a, kind_b):
-    heads, width = kv_a.shape[0] // (2 * HEAD_DIM), kv_a.shape[1]
-    pair = pl.BlockSpec((2, HEAD_DIM, width), lambda h: (0, h, 0))
+def key_backward(planes, planes_t, bits, kv, grad_tables, kind):
+    heads, width = kv.shape[0] // (2 * HEAD_DIM), kv.shape[1]
     return call(
         partial(key_back_kernel, chunk=4),
         heads,
-        18,
+        9,
         "key_backward",
         [whole(64, 64), whole(64, 128), whole(80, ROWS)]
-        + [per_head(width), per_head(width, heads)] * 2
-        + [table_spec()],
-        [pair, pair],
-        [jax.ShapeDtypeStruct((2, heads * HEAD_DIM, width), kind) for kind in (kind_a, kind_b)],
-    )(planes, planes_t, bits, kv_a, kv_a, kv_b, kv_b, grad_tables)
+        + [per_head(width), per_head(width, heads), table_spec()],
+        pl.BlockSpec((2, HEAD_DIM, width), lambda h: (0, h, 0)),
+        jax.ShapeDtypeStruct((2, heads * HEAD_DIM, width), kind),
+    )(planes, planes_t, bits, kv, kv, grad_tables)
 
 
 def norm(x):
@@ -317,13 +309,18 @@
         ).astype(bf16)
 
 
-def weight_grad_kernel(core, normed, hidden, grad_pre, grad_ffn, grad_attn, *refs):
+def weight_grad_kernel(core, normed, hidden, grad_pre, grad_ffn, grad_attn, small, *refs):
     attn, outs = refs[0:4], refs[4:8]
     part = hidden.shape[2]
+    sums = jnp.concatenate([small[...], jnp.zeros_like(small[...])], axis=0).astype(bf16)
     for b in range(8):
         down_out, up = outs[b % 2], outs[2 + b % 2]
         down_out[b // 2, 0:part, :] = dot(hidden[b], grad_ffn[...], TN).astype(bf16)
-        down_out[b // 2, part:, :] = dot(core_rows(core, attn[b // 2], b % 2), grad_attn[...], NN).astype(bf16)
+        heads = core_rows(core, attn[b // 2], b % 2)
+        at = part + heads.shape[0]
+        down_out[b // 2, part:at, :] = dot(heads, grad_attn[...], NN).astype(bf16)
+        down_out[b // 2, at : at + 16, :] = sums
+        down_out[b // 2, at + 16 :, :] = jnp.zeros_like(sums)
         up[b // 2] = dot(grad_pre[b], normed[...], TN).astype(bf16)
 
 
@@ -353,24 +350,24 @@
         out_shape=out_shape,
         scratch_shapes=[pltpu.VMEM((8, rows, part), f32)],
         compiler_params=pltpu.CompilerParams(vmem_limit_bytes=56 << 20),
-        cost_estimate=pl.CostEstimate(flops=18 * 10**9, bytes_accessed=4 << 20, transcendentals=0),
+        cost_estimate=pl.CostEstimate(flops=18 * 10**9, bytes_accessed=1 << 20, transcendentals=0),
         name="dense",
     )(core, x_in, grad_out, gain, bias, *attn, *weights)
 
 
-def weight_grads(core, normed, hidden, grad_pre, grad_ffn, grad_attn, attn):
+def weight_grads(core, normed, hidden, grad_pre, grad_ffn, grad_attn, small, attn):
     width, part = normed.shape[1], hidden.shape[2]
-    shapes = [jax.ShapeDtypeStruct((4, part + attn[0].shape[0] // 2, width), bf16)] * 2
+    shapes = [jax.ShapeDtypeStruct((4, part + attn[0].shape[0] // 2 + 32, width), bf16)] * 2
     shapes += [jax.ShapeDtypeStruct((4, part, width), bf16)] * 2
     return pl.pallas_call(
         weight_grad_kernel,
-        in_specs=[pl.BlockSpec(memory_space=pltpu.SMEM)] + vmem(9),
+        in_specs=[pl.BlockSpec(memory_space=pltpu.SMEM)] + vmem(10),
         out_specs=vmem(4),
         out_shape=shapes,
         compiler_params=pltpu.CompilerParams(vmem_limit_bytes=56 << 20),
-        cost_estimate=pl.CostEstimate(flops=7 * 10**9, bytes_accessed=4 << 20, transcendentals=0),
+        cost_estimate=pl.CostEstimate(flops=9 * 10**9, bytes_accessed=1 << 20, transcendentals=0),
         name="weight_grads",
-    )(core, normed, hidden, grad_pre, grad_ffn, grad_attn, *attn)
+    )(core, normed, hidden, grad_pre, grad_ffn, grad_attn, small, *attn)
 
 
 def after(x, *others):
@@ -476,15 +473,6 @@
     weights = [core_half(s), core_half(1 - s)]
     my_half = after(weights[0], tokens)
     fetched = [over_head(my_half, j) for j in range(1, head_count)]
-    for block in fetched:
-        weights += [block, over_seq(block)]
-    qkv_cut = width // 2
-    qkv_half = lax.dynamic_slice_in_dim(w_qkv, s * qkv_cut, qkv_cut, 1)
-    qkv_half = after(qkv_half, *weights)
-    qkv_blocks = [over_head(qkv_half, j) for j in range(1, head_count)]
-    qkv_far = [over_seq(block) for block in qkv_blocks]
-    qkv_near = [lax.dynamic_slice_in_dim(w_qkv, s * qkv_cut, qkv_cut, 1)] + qkv_blocks
-    qkv_far = [lax.dynamic_slice_in_dim(w_qkv, (1 - s) * qkv_cut, qkv_cut, 1)] + qkv_far
 
     slot = jnp.arange(groups, dtype=jnp.int32)[:, None]
     place_of = ((g - slot) % groups) * places + r
@@ -496,14 +484,22 @@
 
     kv_zo = over_seq(kv_z)
     q_zo = over_seq(q_z)
+    signed = after(signed, grad_out, weights[1])
     tables = key_tables(signed, kv, kv_o)
-    tables = key_tables(signed, after(kv_z, grad_out), kv_zo, tables)
-
-    e_z, e_zo = query_estimates(signed, q_z, q_zo, tables, bf16, bf16)
-    e_far = add(e_z, over_seq(e_zo)).astype(bf16)
+    tables = key_tables(signed, kv_z, kv_zo, tables)
+
+    e_zo = query_estimates(signed, q_zo, tables, bf16)
+    e_zo_moved = over_seq(e_zo)
+    e_z = query_estimates(signed, after(q_z, e_zo), tables, bf16)
+    e_far = add(e_z, after(e_zo_moved, e_z)).astype(bf16)
+    e_o = query_estimates(signed, after(q_o, e_far), tables, bf16)
     e_far = over_place(e_far)
-    e, e_o = query_estimates(signed, q, q_o, tables, f32, bf16)
-    attn = add(e, over_seq(e_o), e_far).astype(bf16)
+    e_o_moved = over_seq(e_o)
+    fetched = [after(block, e_o) for block in fetched]
+    e = query_estimates(signed, after(q, e_o, *fetched), tables, f32)
+    for block in fetched:
+        weights += [block, over_seq(block)]
+    attn = add(e, after(e_o_moved, e), after(e_far, e)).astype(bf16)
 
     def to_dense(block):
         parts = [block[..., j * rows : (j + 1) * rows] for j in range(head_count)]
@@ -511,6 +507,12 @@
 
     attn_parts = to_dense(attn)
 
+    def away(dense_rows):
+        dense_rows = dense_rows.reshape(groups, quarter, width)
+        return jnp.stack(
+            [dense_rows[0]] + [over_group(dense_rows[k], groups - k) for k in range(1, groups)]
+        )
+
     core = s.astype(jnp.int32).reshape(1)
     (layer_rows, grad_first, normed, hidden, grad_pre, grad_ffn, grad_attn, *rest) = dense(
         core, dense_in, grad_out, norm_gain, norm_bias, attn_parts, weights
@@ -520,58 +522,85 @@
         [est_parts[0]] + [over_head(est_parts[j], j) for j in range(1, head_count)], axis=1
     )
     mine_a, other_a, mine_b, other_b = weight_grads(
-        core, normed, hidden, grad_pre, grad_ffn, grad_attn, attn_parts
+        core, normed, hidden, grad_pre, grad_ffn, grad_attn, small, attn_parts
     )
 
     grad_z = over_place(grad)
     grad_o = over_seq(grad)
-    grad_zo = over_seq(grad_z)
     swap_a = over_seq(after(other_a, grad_o))
     swap_b = over_seq(after(other_b, grad_o))
+    layer_moved = away(layer_rows)
+    qkv_cut = width // 2
+    qkv_near = [lax.dynamic_slice_in_dim(w_qkv, s * qkv_cut, qkv_cut, 1)]
+    qkv_far = [lax.dynamic_slice_in_dim(w_qkv, (1 - s) * qkv_cut, qkv_cut, 1)]
+    qkv_half = after(qkv_near[0], grad_o)
+    qkv_near += [over_head(qkv_half, j) for j in range(1, head_count)]
     part, dq, dq_o = query_backward(
-        signed, signed_t, bits, q, grad, q_o, grad_o, tables, None, f32, bf16
-    )
-    chip_a = add(mine_a, swap_a).astype(bf16)
-    chip_b = add(mine_b, swap_b).astype(bf16)
-
-    a_far = over_head(jnp.stack([chip_a[1], chip_a[3]]), 1)
-    b_far = over_head(jnp.stack([chip_b[2], chip_b[3]]), 2)
+        signed, signed_t, bits, q, grad, q_o, after(grad_o, mine_a), tables, None, f32, bf16
+    )
+
+    grad_zo = over_seq(after(grad_z, part))
+    chip_a = add(mine_a, after(swap_a, part)).astype(bf16)
+    chip_b = add(mine_b, after(swap_b, part)).astype(bf16)
+    qkv_near[1:] = [after(block, part) for block in qkv_near[1:]]
+    layer_moved = after(layer_moved, part)
+    a_out, b_out = jnp.stack([chip_a[1], chip_a[3]]), jnp.stack([chip_b[2], chip_b[3]])
+    a_far, b_far = over_head(a_out, 1), over_head(b_out, 2)
+    dq_o = over_seq(dq_o)
+    q_gated = after(q_z, a_out, b_out, layer_moved, *qkv_near[1:])
     grad_tables, dq_z, dq_zo = query_backward(
-        signed, signed_t, bits, after(q_z, chip_a, chip_b), grad_z, q_zo, grad_zo, tables, part, bf16, bf16
-    )
+        signed, signed_t, bits, q_gated, grad_z, q_zo, grad_zo, tables, part, bf16, bf16
+    )
+
+    dq_zo = over_seq(dq_zo)
+    dq_own = add(dq, after(dq_o, dq_z))
+    qkv_swaps = [over_seq(block) for block in qkv_near[1:]]
+    dkv_zo = key_backward(signed, signed_t, bits, after(kv_zo, dq_own), grad_tables, bf16)
+
+    dkv_zo_moved = over_seq(dkv_zo)
+    qkv_far += [after(block, dkv_zo) for block in qkv_swaps]
+    dq_far = add(dq_z, after(dq_zo, dkv_zo)).astype(bf16)
+    a_far, b_far = after(a_far, dkv_zo), after(b_far, dkv_zo)
     a_two = [add(chip_a[0], a_far[0]), add(chip_a[2], a_far[1]).astype(bf16)]
     b_two = [add(chip_b[0], b_far[0]), add(chip_b[1], b_far[1]).astype(bf16)]
-    a_last = over_head(a_two[1], 2)
-    b_last = over_head(b_two[1], 1)
-    dkv_z, dkv_zo = key_backward(
-        signed, signed_t, bits, after(kv_z, a_two[1], b_two[1]), kv_zo, grad_tables, bf16, bf16
-    )
-    dkv_far = add(dkv_z, over_seq(dkv_zo)).astype(bf16)
-    dkv_far = over_place(dkv_far)
-    a_sum = add(a_two[0], a_last).astype(bf16)
-    b_sum = add(b_two[0], b_last).astype(bf16)
-    dq_far = over_place(add(dq_z, over_seq(dq_zo)).astype(bf16))
-    grad_q = add(dq, over_seq(dq_o), dq_far).astype(bf16)
-    dkv, dkv_o = key_backward(
-        signed, signed_t, bits, after(kv, a_sum, b_sum), kv_o, grad_tables, f32, bf16
-    )
-    grad_kv = add(dkv, over_seq(dkv_o), dkv_far).astype(bf16)
-    q_parts, kv_parts = to_dense(grad_q), to_dense(grad_kv)
+    kv_gated = after(kv_z, a_two[1], b_two[1], dq_far, *qkv_far)
+    dkv_z = key_backward(signed, signed_t, bits, kv_gated, grad_tables, bf16)
+    dq_far = over_place(dq_far)
+    a_last, b_last = over_head(a_two[1], 2), over_head(b_two[1], 1)
+
+    dkv_far = add(dkv_z, after(dkv_zo_moved, dkv_z)).astype(bf16)
+    grad_q = add(dq_own, after(dq_far, dkv_z)).astype(bf16)
+    dkv_o = key_backward(signed, signed_t, bits, after(kv_o, dkv_far, grad_q), grad_tables, bf16)
+    dk_far, dv_far = over_place(dkv_far[0]), over_place(dkv_far[1])
+
+    dkv_o_moved = over_seq(dkv_o)
+    a_sum = add(a_two[0], after(a_last, dkv_o)).astype(bf16)
+    b_sum = add(b_two[0], after(b_last, dkv_o)).astype(bf16)
+    dk_far = after(dk_far, dkv_o)
+    layer_moved = after(layer_moved, dkv_o)
+    layer_moved = [layer_moved] + [over_head(layer_moved, j) for j in range(1, head_count)]
+    dkv = key_backward(signed, signed_t, bits, after(kv, a_sum, b_sum, dk_far), grad_tables, f32)
+
+    dkv_o_moved = after(dkv_o_moved, dkv)
+    grad_k = add(dkv[0], dkv_o_moved[0], dk_far)
+    grad_v = add(dkv[1], dkv_o_moved[1], after(dv_far, dkv))
+    grad_qkv = jnp.stack([grad_q, grad_k.astype(bf16), grad_v.astype(bf16)])
+    qkv_parts = to_dense(grad_qkv)
 
     near, far = 0.0, 0.0
     for j in range(head_count):
-        block = jnp.concatenate([q_parts[j][None], kv_parts[j]])
+        block = qkv_parts[j]
         near = near + jnp.einsum("cel,cde->ld", block, qkv_near[j], preferred_element_type=f32)
         far = far + jnp.einsum("cel,cde->ld", block, qkv_far[j], preferred_element_type=f32)
     grad_in = grad_first + jnp.concatenate(
         [jnp.where(s == 0, near, far), jnp.where(s == 0, far, near)], axis=1
     )
 
-    def home(dense_rows):
-        dense_rows = dense_rows.reshape(groups, quarter, width)
-        parts = [dense_rows[0]] + [over_group(dense_rows[k], groups - k) for k in range(1, groups)]
-        parts = jnp.stack(parts)
-        table = jnp.stack([parts] + [over_head(parts, j) for j in range(1, head_count)])
+    grad_moved = away(grad_in.astype(bf16))
+    grad_moved = [grad_moved] + [over_head(grad_moved, j) for j in range(1, head_count)]
+
+    def home(blocks):
+        table = jnp.stack(blocks)
         columns = []
         for q_at in range(head_count):
             block = lax.dynamic_index_in_dim(table, q_at ^ d, 0, keepdims=False)
@@ -586,8 +615,8 @@
             )
         return jnp.concatenate(columns, axis=0)
 
-    layer_out = home(after(layer_rows, grad_tables))
-    grad_inputs = home(grad_in.astype(bf16)).astype(f32)
+    layer_out = home([after(x, dkv) for x in layer_moved])
+    grad_inputs = home(grad_moved).astype(f32)
 
     def in_halves(index, mine, other):
         first = jnp.where(index == 0, mine, other)
@@ -606,10 +635,11 @@
     a_other, b_other = over_seq(a_sum), over_seq(b_sum)
     cut = hidden_own // 2
     grad_w_down = in_halves(s, a_sum[:cut], a_other[:cut]).astype(f32)
-    grad_w_out = in_halves(s, a_sum[cut:], a_other[cut:]).astype(f32)
+    out_cut = cut + head_width // 2
+    grad_w_out = in_halves(s, a_sum[cut:out_cut], a_other[cut:out_cut]).astype(f32)
+    small = a_sum[out_cut : out_cut + 8].astype(f32)
     grad_w_up = in_halves(s, b_sum, b_other).T.astype(f32)
 
-    grad_qkv = jnp.concatenate([grad_q[None], grad_kv])
     grad_w_qkv = jnp.einsum("ld,cel->cde", tokens, grad_qkv, preferred_element_type=f32)
     grad_w_qkv = grad_w_qkv.reshape(3 * width, head_width).astype(bf16)
     half = grad_w_qkv.shape[0] // 2
@@ -618,13 +648,6 @@
     total = over_hash_sum(add(mine, other).astype(bf16))
     grad_w_qkv = in_halves(s, total, over_seq(total)).reshape(3, width, head_width).astype(f32)
 
-    small = after(small, part)
-    small = small + over_seq(small)
-    small = small + over_head(small, 1)
-    small = small + over_head(after(small, grad_tables), 2)
-    small = small + over_place(small)
-    small = after(small, dkv_z)
-    small = sum([small] + [over_group(small, k) for k in range(1, groups)])
     count = piece * seqs * width * hash_count * 2
     stream_rms = jnp.sqrt(jnp.sum(small[4:7], axis=1) / count)
     share = width // head_count

time: 489 us -> 431 us (0.88)
  waiting for transfers between devices: 173 us -> 113 us
  starting transfers between devices: 97.4 us -> 81.5 us
  other arithmetic: 25.8 us -> 34.4 us
  Pallas kernels: 129 us -> 136 us
    ppermute x33 -> x28, waiting for transfers between devices: 104 us -> 46.2 us  [over_head(): return lax.ppermute(x, 'head', [(h, h ^ j) for h in range(head_count)])]
    ppermute x25 -> x24, starting transfers between devices: 42.7 us -> 28.5 us  [over_seq(): return lax.ppermute(x, 'seq', [(0, 1), (1, 0)])]
    ppermute x7 -> x6, waiting for transfers between devices: 21.3 us -> 33.4 us  [over_group(): return lax.ppermute(x, 'hash', moves)]
    ppermute x1, waiting for transfers between devices: 9.24 us -> 0.01 us  [shards(): signed = lax.ppermute(signed, ('hash', 'seq'), moves)]
    pallas_call x4 -> x8, Pallas kernels: 46.5 us -> 52.1 us  [the longest x4 38.7 us: key_backward(): call(partial(key_back_kernel, chunk=4), heads, 9, 'key_backward', [whole(...]
    ppermute x33 -> x28, starting transfers between devices: 26.6 us -> 30.8 us  [over_head(): return lax.ppermute(x, 'head', [(h, h ^ j) for h in range(head_count)])]
    ppermute x7 -> x6, starting transfers between devices: 11 us -> 7.99 us  [over_group(): return lax.ppermute(x, 'hash', moves)]
    unnamed x109 -> x113, local copies, waits for them, and re-layouts: 25.9 us -> 26.6 us
  transfers between devices with their start and end apart: 79 -> 72, of which waited for: 33 -> 19; matrix products, arithmetic and copies ran while one was open for 13% -> 17% of each run, Pallas kernels for 23% -> 28%
where the time goes in v3:
time: 431 us; the launch traced here: 427 us
  Pallas kernels  136 us (32%)
  waiting for transfers between devices  113 us (26%)
  starting transfers between devices  81.5 us (19%)
  local copies, waits for them, and re-layouts  45.9 us (11%)
  other arithmetic  34.4 us (8%)
  matrix products  13.3 us (3%)
    ppermute x28, waiting for transfers between devices, over_head(): return lax.ppermute(x, 'head', [(h, h ^ j) for h in range(head_count)])  46.2 us
    pallas_call x2, Pallas kernels, query_backward(): call(partial(query_back_kernel, chunk=4), heads, 20, 'query_backward', sp...  39.8 us
    pallas_call x4, Pallas kernels, key_backward(): call(partial(key_back_kernel, chunk=4), heads, 9, 'key_backward', [whole(...  38.7 us
    ppermute x6, waiting for transfers between devices, over_group(): return lax.ppermute(x, 'hash', moves)  33.4 us
    ppermute x13, waiting for transfers between devices, over_place(): return lax.ppermute(x, 'hash', [(h, h ^ 1) for h in range(hash_count)])  33.2 us
    ppermute x28, starting transfers between devices, over_head(): return lax.ppermute(x, 'head', [(h, h ^ j) for h in range(head_count)])  30.8 us
    ppermute x24, starting transfers between devices, over_seq(): return lax.ppermute(x, 'seq', [(0, 1), (1, 0)])  28.5 us
    unnamed x113, local copies, waits for them, and re-layouts  26.6 us
  transfers between devices with their start and end apart: 72, of which 19 were waited for; matrix products, arithmetic and copies ran while one was open for 17% of the time, Pallas kernels for 28%

profile of v3, /device:TPU:1, one launch (start us, length us, event | category | flops | bytes accessed | tf_op | source)
XLA Modules:
  0.0 426.6 jit_solution(1986621301236854654)
XLA Ops:
  0.8 4.5 %constant_dynamic-slice_fusion.12 = (bf16[1,128,1,768]{3,2,1,0:T(2,128)(2,1)S(1)}, bf16[1,128,1,768]{3,2,1,0:T(2,128)(2,1)}, bf16[1,128,1,768]{3,2,1,0:T(2,128)(...) fusion(bf16[1,512,2,768]{3,2,1,0:T(2,128)(2,1)} %param.11, s32[]{:T(128)S(6)} %select_n.312, ...), kind=kLoop, calls=%fused_computation.159 | loop fusion | bytes 1966104 | tf_op jit(solution)/shard_map/jit(dynamic_index_in_dim)/dynamic_slice | solution.py:422
  6.0 3.1 collective-permute-start
  9.8 2.6 collective-permute-start.1
  14.1 2.4 constant_dynamic-slice_fusion.8
  17.7 2.1 copy.52
  21.8 2.5 collective-permute-start.4
  27.5 2.4 collective-permute-done.4
  30.0 4.3 collective-permute-done.3
  48.4 8.7 %collective-permute-done.9.ka.va.keys.vals = bf16[384,1024]{1,0:T(8,128)(2,1)} collective-permute-done((bf16[384,1024]{1,0:T(8,128)(2,1)}, bf16[384,1024]{1,0:T(8,128)(2,1)}, u32[]{:S(2)}, u32[]{:S(2)}) %collective-permute-start.9) | collective-permute-done | bytes 786464 | tf_op jit(solution)/shard_map/ppermute | solution.py:412
  58.5 8.9 %key_tables.2.refs_0_ = f32[3,2048,64]{2,1,0:T(8,128)S(1)} custom-call(bf16[64,64]{1,0:T(8,128)(2,1)S(1)} %bitcast.201, bf16[384,1024]{1,0:T(8,128)(2,1)} %bitcast.25.ka.va.keys.vals, bf16[384,1024]{1,0:T(8,128)(2,1)} %bitcast.25.ka.va.keys.vals, bf16[384,1024]{1,0:T(8,128)(2,1)} %collective-permute-done.6.kb.vb.keys.vals, ...), custom_call_target="tpu_custom_call" | custom-call | flops 11000000512 | bytes 1048576 | tf_op jit(solution)/shard_map/key_tables/pallas_call | solution.py:178
  69.2 2.2 collective-permute-start.14
  71.6 9.2 %key_tables.3.tables = bf16[3,2048,64]{2,1,0:T(8,128)(2,1)S(1)} custom-call(bf16[64,64]{1,0:T(8,128)(2,1)S(1)} %bitcast.202, bf16[384,1024]{1,0:T(8,128)(2,1)} %collective-permute-done.9.ka.va.keys.vals, bf16[384,1024]{1,0:T(8,128)(2,1)} %collective-permute-done.9.ka.va.keys.vals, bf16[384,1024]{1,0:T(8,128)(2,1)S(1)} %collective-permute-done.10.kb.vb.keys.vals, ...), custom_call_target="tpu_custom_call" | custom-call | flops 11000000512 | bytes 1048576 | tf_op jit(solution)/shard_map/key_tables/pallas_call | solution.py:178
  80.9 3.3 query_estimates.4
  84.5 3.3 query_estimates.5
  87.9 3.3 query_estimates.6
  91.3 11.9 %collective-permute-done.14.refs_10_ = bf16[864,768]{1,0:T(8,128)(2,1)S(1)} collective-permute-done((bf16[864,768]{1,0:T(8,128)(2,1)S(1)}, bf16[864,768]{1,0:T(8,128)(2,1)S(1)}, u32[]{:S(2)}, u32[]{:S(2)}) %collective-permute-start.14) | collective-permute-done | bytes 1327136 | tf_op jit(solution)/shard_map/ppermute | solution.py:419
  106.4 3.5 query_estimates.7
  109.9 5.8 %collective-permute-done.16 = bf16[192,1024]{1,0:T(8,128)(2,1)S(1)} collective-permute-done((bf16[192,1024]{1,0:T(8,128)(2,1)S(1)}, bf16[192,1024]{1,0:T(8,128)(2,1)S(1)}, u32[]{:S(2)}, u32[]{:S(2)}) %collective-permute-start.16) | collective-permute-done | bytes 393248 | tf_op jit(solution)/shard_map/ppermute | solution.py:412
  121.3 3.2 collective-permute-done.19.refs_3_
  126.8 16.8 %dense.1 = (bf16[256,768]{1,0:T(8,128)(2,1)}, f32[256,768]{1,0:T(8,128)}, bf16[256,768]{1,0:T(8,128)(2,1)}, bf16[8,256,384]{2,1,0:T(8,128)(2,1)}, bf16[8,256,384...) custom-call(s32[1]{0:T(128)} %bitcast.core, ...), custom_call_target="tpu_custom_call" | custom-call | flops 17999998976 | bytes 1048576 | tf_op jit(solution)/shard_map/dense/pallas_call | solution.py:346
  149.7 4.9 %collective-permute-start.27 = (bf16[192,1024]{1,0:T(8,128)(2,1)S(1)}, bf16[192,1024]{1,0:T(8,128)(2,1)S(1)}, u32[]{:S(2)}, u32[]{:S(2)}) collective-permute-start(bf16[192,1024]{1,0:T(8,128)(2,1)S(1)} %constant_dynamic-update-slice_fusion.ga), channel_id=1, source_target_pairs={{0,1},{1,0},{2,3},{3,2},{4,5},{5,4},{6,7},{7,6},{8,9},{9,8},{10,11... | collective-permute-start | bytes 1179656 | tf_op jit(solution)/shard_map/ppermute | solution.py:409
  154.6 9.5 %weight_grads.1 = (bf16[4,512,768]{2,1,0:T(8,128)(2,1)}, bf16[4,512,768]{2,1,0:T(8,128)(2,1)}, bf16[4,384,768]{2,1,0:T(8,128)(2,1)}, bf16[4,384,768]{2,1,0:T(8,128)(2,1)}) custom-call(s32[1]{0:T(128)} %bitcast.core, bf16[256,768]{1,0:T(8,128)(2,1)} %get-tuple-element.95.normed, bf16[8,256,384]{2,1,0:T(8,128)(2,1)} %get-tuple-element.96.hidden, ...), custom_call_target="tpu_custom_call" | custom-call | flops 8999999488 | bytes 1048576 | tf_op jit(solution)/shard_map/weight_grads/pallas_call | solution.py:362
  170.7 7.9 %collective-permute-done.23 = bf16[128,768]{1,0:T(8,128)(2,1)} collective-permute-done((bf16[128,768]{1,0:T(8,128)(2,1)}, bf16[128,768]{1,0:T(8,128)(2,1)}, u32[]{:S(2)}, u32[]{:S(2)}) %collective-permute-start.23) | collective-permute-done | bytes 196640 | tf_op jit(solution)/shard_map/ppermute | solution.py:416
  185.5 19.6 %query_backward.2 = (f32[3,2048,64]{2,1,0:T(8,128)}, f32[192,1024]{1,0:T(8,128)S(1)}, bf16[192,1024]{1,0:T(8,128)(2,1)S(1)}) custom-call(bf16[64,64]{1,0:T(8,128)(2,1)S(1)} %bitcast.208, bf16[64,128]{1,0:T(8,128)(2,1)S(1)} %pad_maximum_fusion.13.planes_t, bf16[80,2048]{1,0:T(8,128)(2,1)S(1)} %copy-done.4, bf16[192,1024]{1,0:T(8,128)(2,1)S(1)} %fusion.5.q.qa, ...), custom_call_target="tpu_custom_call" | custom-call | flops 22000001024 | bytes 1048576 | tf_op jit(solution)/shard_map/query_backward/pallas_call | solution.py:209
  205.1 2.2 collective-permute-start.30
  207.9 2.4 add_convert_fusion.1
  211.8 2.7 add_convert_fusion
  215.8 20.2 %query_backward.3 = (bf16[3,2048,64]{2,1,0:T(8,128)(2,1)S(1)}, bf16[192,1024]{1,0:T(8,128)(2,1)S(1)}, bf16[192,1024]{1,0:T(8,128)(2,1)S(1)}) custom-call(bf16[64,64]{1,0:T(8,128)(2,1)S(1)} %bitcast.209, bf16[64,128]{1,0:T(8,128)(2,1)S(1)} %pad_maximum_fusion.13.planes_t, bf16[80,2048]{1,0:T(8,128)(2,1)S(1)} %copy-done.4, ...), custom_call_target="tpu_custom_call" | custom-call | flops 22000001024 | bytes 1048576 | tf_op jit(solution)/shard_map/query_backward/pallas_call | solution.py:209
  238.5 8.8 %key_backward.4 = bf16[2,192,1024]{2,1,0:T(8,128)(2,1)S(1)} custom-call(bf16[64,64]{1,0:T(8,128)(2,1)S(1)} %bitcast.210, bf16[64,128]{1,0:T(8,128)(2,1)S(1)} %pad_maximum_fusion.13.planes_t, bf16[80,2048]{1,0:T(8,128)(2,1)S(1)} %copy-done.4, bf16[384,1024]{1,0:T(8,128)(2,1)S(1)} %collective-permute-done.10.kb.vb.keys.vals, ...), custom_call_target="tpu_custom_call" | custom-call | flops 9900000256 | bytes 1048576 | tf_op jit(solution)/shard_map/key_backward/pallas_call | solution.py:223
  249.6 2.2 collective-permute-start.43
  251.8 19.9 %collective-permute-done.29 = bf16[2,512,768]{2,1,0:T(8,128)(2,1)S(1)} collective-permute-done((bf16[2,512,768]{2,1,0:T(8,128)(2,1)S(1)}, bf16[2,512,768]{2,1,0:T(8,128)(2,1)S(1)}, u32[]{:S(2)}, u32[]{:S(2)}) %collective-permute-start.29) | collective-permute-done | bytes 1572896 | tf_op jit(solution)/shard_map/ppermute | solution.py:419
  272.9 10.0 %key_backward.5 = bf16[2,192,1024]{2,1,0:T(8,128)(2,1)S(1)} custom-call(bf16[64,64]{1,0:T(8,128)(2,1)S(1)} %bitcast.211, bf16[64,128]{1,0:T(8,128)(2,1)S(1)} %pad_maximum_fusion.13.planes_t, bf16[80,2048]{1,0:T(8,128)(2,1)S(1)} %copy-done.4, bf16[384,1024]{1,0:T(8,128)(2,1)} %collective-permute-done.9.ka.va.keys.vals, ...), custom_call_target="tpu_custom_call" | custom-call | flops 9900000256 | bytes 1048576 | tf_op jit(solution)/shard_map/key_backward/pallas_call | solution.py:223
  283.3 9.8 %key_backward.6 = bf16[2,192,1024]{2,1,0:T(8,128)(2,1)S(1)} custom-call(bf16[64,64]{1,0:T(8,128)(2,1)S(1)} %bitcast.212, bf16[64,128]{1,0:T(8,128)(2,1)S(1)} %pad_maximum_fusion.13.planes_t, bf16[80,2048]{1,0:T(8,128)(2,1)S(1)} %copy-done.4, bf16[384,1024]{1,0:T(8,128)(2,1)} %collective-permute-done.6.kb.vb.keys.vals, ...), custom_call_target="tpu_custom_call" | custom-call | flops 9900000256 | bytes 1048576 | tf_op jit(solution)/shard_map/key_backward/pallas_call | solution.py:223
  298.9 4.1 collective-permute-done.68
  304.0 2.2 collective-permute-start.69
  309.4 6.8 %collective-permute-done.46 = bf16[192,1024]{1,0:T(8,128)(2,1)S(1)} collective-permute-done((bf16[192,1024]{1,0:T(8,128)(2,1)}, bf16[192,1024]{1,0:T(8,128)(2,1)S(1)}, u32[]{:S(2)}, u32[]{:S(2)}) %collective-permute-start.46) | collective-permute-done | bytes 393248 | tf_op jit(solution)/shard_map/ppermute | solution.py:412
  316.2 3.5 collective-permute-start.47
  319.7 3.2 collective-permute-start.50
  326.1 10.1 %key_backward.7 = f32[2,192,1024]{2,1,0:T(8,128)S(1)} custom-call(bf16[64,64]{1,0:T(8,128)(2,1)S(1)} %bitcast.213, bf16[64,128]{1,0:T(8,128)(2,1)S(1)} %pad_maximum_fusion.13.planes_t, bf16[80,2048]{1,0:T(8,128)(2,1)S(1)} %copy-done.4, bf16[384,1024]{1,0:T(8,128)(2,1)} %bitcast.25.ka.va.keys.vals, bf16[384,1024]{1,0:T(8,128)(2,1)} %bitcast.25.ka.va.keys.vals, ...), custom_call_target="tpu_custom_call" | custom-call | flops 9900000256 | bytes 1048576 | tf_op jit(solution)/shard_map/key_backward/pallas_call | solution.py:223
  340.4 2.8 copy.46
  347.0 6.2 %collective-permute-start.59 = (bf16[1152,192]{0,1:T(8,128)(2,1)S(1)}, bf16[1152,192]{0,1:T(8,128)(2,1)S(1)}, u32[]{:S(2)}, u32[]{:S(2)}) collective-permute-start(bf16[1152,192]{0,1:T(8,128)(2,1)S(1)} %constant_dynamic-slice_fusion.4), channel_id=1, source_target_pairs={{0,1},{1,0},{2,3},{3,2},{4,5},{5,4},{6,7},{7,6},{8,9},{9,8},{10,11... | collective-permute-start | bytes 1327112 | tf_op jit(solution)/shard_map/ppermute | solution.py:409
  353.8 3.0 collective-permute-start.71
  369.3 8.1 %collective-permute-done.55 = bf16[128,768]{1,0:T(8,128)(2,1)S(1)} collective-permute-done((bf16[128,768]{1,0:T(8,128)(2,1)S(1)}, bf16[128,768]{1,0:T(8,128)(2,1)S(1)}, u32[]{:S(2)}, u32[]{:S(2)}) %collective-permute-start.55) | collective-permute-done | bytes 196640 | tf_op jit(solution)/shard_map/ppermute | solution.py:416
  382.2 2.2 copy.49
  384.4 15.2 %collective-permute-done.65 = bf16[256,768]{1,0:T(8,128)(2,1)} collective-permute-done((bf16[256,768]{1,0:T(8,128)(2,1)}, bf16[256,768]{1,0:T(8,128)(2,1)}, u32[]{:S(2)}, u32[]{:S(2)}) %collective-permute-start.65) | collective-permute-done | bytes 393248 | tf_op jit(solution)/shard_map/ppermute | solution.py:416
  402.7 2.1 collective-permute-done.61
  406.5 4.1 copy.47
  410.6 7.8 %collective-permute-done.62 = bf16[576,192]{0,1:T(8,128)(2,1)S(1)} collective-permute-done((bf16[576,192]{0,1:T(8,128)(2,1)S(1)}, bf16[576,192]{0,1:T(8,128)(2,1)S(1)}, u32[]{:S(2)}, u32[]{:S(2)}) %collective-permute-start.62) | collective-permute-done | bytes 221216 | tf_op jit(solution)/shard_map/ppermute | solution.py:412
  (324 shorter events, 118.8 us)
Async XLA Ops:
  6.0 15.8 %collective-permute-start = (bf16[128,768]{1,0:T(8,128)(2,1)}, bf16[128,768]{1,0:T(8,128)(2,1)}, u32[]{:S(2)}, u32[]{:S(2)}) collective-permute-start(bf16[128,768]{1,0:T(8,128)(2,1)} %bitcast.199), channel_id=1, source_target_pairs={{0,16},{8,24},{16,0},{24,8},{1,17},{9,25},{17,1},{25,9},{2,18},{10... | collective-permute-start | bytes 589832 | tf_op jit(solution)/shard_map/ppermute | solution.py:416
  9.8 33.5 %collective-permute-start.1 = (bf16[8,8,64]{2,0,1:T(8,128)(2,1)}, bf16[8,8,64]{2,0,1:T(8,128)(2,1)S(1)}, u32[]{:S(2)}, u32[]{:S(2)}) collective-permute-start(bf16[8,8,64]{2,0,1:T(8,128)(2,1)} %fusion.36), channel_id=1, source_target_pairs={{0,0},{8,1},{16,8},{24,9},{1,16},{9,17},{17,24},{25,25},{2,2},{10,... | collective-permute-start | bytes 24584 | tf_op jit(solution)/shard_map/ppermute | solution.py:435
  37.7 19.3 %collective-permute-start.9 = (bf16[384,1024]{1,0:T(8,128)(2,1)}, bf16[384,1024]{1,0:T(8,128)(2,1)}, u32[]{:S(2)}, u32[]{:S(2)}) collective-permute-start(bf16[384,1024]{1,0:T(8,128)(2,1)} %bitcast.25.ka.va.keys.vals), channel_id=1, source_target_pairs={{0,8},{8,0},{16,24},{24,16},{1,9},{9,1},{17,25},{25,17},{2,10},{10... | collective-permute-start | bytes 2359304 | tf_op jit(solution)/shard_map/ppermute | solution.py:412
  43.2 48.0 %collective-permute-start.12 = (bf16[864,768]{1,0:T(8,128)(2,1)S(1)}, bf16[864,768]{1,0:T(8,128)(2,1)S(1)}, u32[]{:S(2)}, u32[]{:S(2)}) collective-permute-start(bf16[864,768]{1,0:T(8,128)(2,1)S(1)} %pad_maximum_fusion.5.refs_4_), channel_id=1, source_target_pairs={{0,2},{2,0},{4,6},{6,4},{1,3},{3,1},{5,7},{7,5},{8,10},{10,8},{12,... | collective-permute-start | bytes 3981320 | tf_op jit(solution)/shard_map/ppermute | solution.py:419
  44.5 46.7 %collective-permute-start.13 = (bf16[864,768]{1,0:T(8,128)(2,1)S(1)}, bf16[864,768]{1,0:T(8,128)(2,1)S(1)}, u32[]{:S(2)}, u32[]{:S(2)}) collective-permute-start(bf16[864,768]{1,0:T(8,128)(2,1)S(1)} %pad_maximum_fusion.5.refs_4_), channel_id=1, source_target_pairs={{0,4},{2,6},{4,0},{6,2},{1,5},{3,7},{5,1},{7,3},{8,12},{10,14},{12... | collective-permute-start | bytes 3981320 | tf_op jit(solution)/shard_map/ppermute | solution.py:419
  46.4 41.5 %collective-permute-start.5 = (bf16[192,1024]{1,0:T(8,128)(2,1)S(1)}, bf16[192,1024]{1,0:T(8,128)(2,1)S(1)}, u32[]{:S(2)}, u32[]{:S(2)}) collective-permute-start(bf16[192,1024]{1,0:T(8,128)(2,1)S(1)} %fusion.5.q.qa), channel_id=1, source_target_pairs={{0,1},{1,0},{2,3},{3,2},{4,5},{5,4},{6,7},{7,6},{8,9},{9,8},{10,11... | collective-permute-start | bytes 1179656 | tf_op jit(solution)/shard_map/ppermute | solution.py:409
  47.3 21.8 %collective-permute-start.7 = (bf16[192,1024]{1,0:T(8,128)(2,1)S(1)}, bf16[192,1024]{1,0:T(8,128)(2,1)S(1)}, u32[]{:S(2)}, u32[]{:S(2)}) collective-permute-start(bf16[192,1024]{1,0:T(8,128)(2,1)S(1)} %fusion.5.q.qa), channel_id=1, source_target_pairs={{0,8},{8,0},{16,24},{24,16},{1,9},{9,1},{17,25},{25,17},{2,10},{10... | collective-permute-start | bytes 1179656 | tf_op jit(solution)/shard_map/ppermute | solution.py:412
  57.0 14.3 %collective-permute-start.10 = (bf16[384,1024]{1,0:T(8,128)(2,1)}, bf16[384,1024]{1,0:T(8,128)(2,1)S(1)}, u32[]{:S(2)}, u32[]{:S(2)}) collective-permute-start(bf16[384,1024]{1,0:T(8,128)(2,1)} %collective-permute-done.9.ka.va.keys.vals), channel_id=1, source_target_pairs={{0,1},{1,0},{2,3},{3,2},{4,5},{5,4},{6,7},{7,6},{8,9},{9,8},{10,11... | collective-permute-start | bytes 2359304 | tf_op jit(solution)/shard_map/ppermute | solution.py:409
  69.2 34.0 %collective-permute-start.14 = (bf16[864,768]{1,0:T(8,128)(2,1)S(1)}, bf16[864,768]{1,0:T(8,128)(2,1)S(1)}, u32[]{:S(2)}, u32[]{:S(2)}) collective-permute-start(bf16[864,768]{1,0:T(8,128)(2,1)S(1)} %pad_maximum_fusion.5.refs_4_), channel_id=1, source_target_pairs={{0,6},{2,4},{4,2},{6,0},{1,7},{3,5},{5,3},{7,1},{8,14},{10,12},{12... | collective-permute-start | bytes 3981320 | tf_op jit(solution)/shard_map/ppermute | solution.py:419
  103.2 21.3 %collective-permute-start.20 = (bf16[864,768]{1,0:T(8,128)(2,1)S(1)}, bf16[864,768]{1,0:T(8,128)(2,1)S(1)}, u32[]{:S(2)}, u32[]{:S(2)}) collective-permute-start(bf16[864,768]{1,0:T(8,128)(2,1)S(1)} %collective-permute-done.12.refs_6_), channel_id=1, source_target_pairs={{0,1},{1,0},{2,3},{3,2},{4,5},{5,4},{6,7},{7,6},{8,9},{9,8},{10,11... | collective-permute-start | bytes 3981320 | tf_op jit(solution)/shard_map/ppermute | solution.py:409
  104.6 19.9 %collective-permute-start.21 = (bf16[864,768]{1,0:T(8,128)(2,1)S(1)}, bf16[864,768]{1,0:T(8,128)(2,1)S(1)}, u32[]{:S(2)}, u32[]{:S(2)}) collective-permute-start(bf16[864,768]{1,0:T(8,128)(2,1)S(1)} %collective-permute-done.13.refs_8_), channel_id=1, source_target_pairs={{0,1},{1,0},{2,3},{3,2},{4,5},{5,4},{6,7},{7,6},{8,9},{9,8},{10,11... | collective-permute-start | bytes 3981320 | tf_op jit(solution)/shard_map/ppermute | solution.py:409
  104.7 19.8 %collective-permute-start.22 = (bf16[864,768]{1,0:T(8,128)(2,1)S(1)}, bf16[864,768]{1,0:T(8,128)(2,1)S(1)}, u32[]{:S(2)}, u32[]{:S(2)}) collective-permute-start(bf16[864,768]{1,0:T(8,128)(2,1)S(1)} %collective-permute-done.14.refs_10_), channel_id=1, source_target_pairs={{0,1},{1,0},{2,3},{3,2},{4,5},{5,4},{6,7},{7,6},{8,9},{9,8},{10,11... | collective-permute-start | bytes 3981320 | tf_op jit(solution)/shard_map/ppermute | solution.py:409
  149.7 14.5 %collective-permute-start.27 = (bf16[192,1024]{1,0:T(8,128)(2,1)S(1)}, bf16[192,1024]{1,0:T(8,128)(2,1)S(1)}, u32[]{:S(2)}, u32[]{:S(2)}) collective-permute-start(bf16[192,1024]{1,0:T(8,128)(2,1)S(1)} %constant_dynamic-update-slice_fusion.ga), channel_id=1, source_target_pairs={{0,1},{1,0},{2,3},{3,2},{4,5},{5,4},{6,7},{7,6},{8,9},{9,8},{10,11... | collective-permute-start | bytes 1179656 | tf_op jit(solution)/shard_map/ppermute | solution.py:409
  164.9 46.5 %collective-permute-start.28 = (bf16[4,512,768]{2,1,0:T(8,128)(2,1)}, bf16[4,512,768]{2,1,0:T(8,128)(2,1)}, u32[]{:S(2)}, u32[]{:S(2)}) collective-permute-start(bf16[4,512,768]{2,1,0:T(8,128)(2,1)} %get-tuple-element.106), channel_id=1, source_target_pairs={{0,1},{1,0},{2,3},{3,2},{4,5},{5,4},{6,7},{7,6},{8,9},{9,8},{10,11... | collective-permute-start | bytes 9437192 | tf_op jit(solution)/shard_map/ppermute | solution.py:409
  164.9 16.9 %collective-permute-start.35 = (bf16[192,1024]{1,0:T(8,128)(2,1)S(1)}, bf16[192,1024]{1,0:T(8,128)(2,1)S(1)}, u32[]{:S(2)}, u32[]{:S(2)}) collective-permute-start(bf16[192,1024]{1,0:T(8,128)(2,1)S(1)} %constant_dynamic-update-slice_fusion.ga), channel_id=1, source_target_pairs={{0,8},{8,0},{16,24},{24,16},{1,9},{9,1},{17,25},{25,17},{2,10},{10... | collective-permute-start | bytes 1179656 | tf_op jit(solution)/shard_map/ppermute | solution.py:412
  168.4 39.4 %collective-permute-start.31 = (bf16[4,384,768]{2,1,0:T(8,128)(2,1)}, bf16[4,384,768]{2,1,0:T(8,128)(2,1)}, u32[]{:S(2)}, u32[]{:S(2)}) collective-permute-start(bf16[4,384,768]{2,1,0:T(8,128)(2,1)} %get-tuple-element.112), channel_id=1, source_target_pairs={{0,1},{1,0},{2,3},{3,2},{4,5},{5,4},{6,7},{7,6},{8,9},{9,8},{10,11... | collective-permute-start | bytes 7077896 | tf_op jit(solution)/shard_map/ppermute | solution.py:409
  180.4 24.7 %collective-permute-start.32 = (bf16[3,384,192]{1,2,0:T(8,128)(2,1)}, bf16[3,384,192]{1,2,0:T(8,128)(2,1)}, u32[]{:S(2)}, u32[]{:S(2)}) collective-permute-start(bf16[3,384,192]{1,2,0:T(8,128)(2,1)} %get-tuple-element.114), channel_id=1, source_target_pairs={{0,2},{2,0},{4,6},{6,4},{1,3},{3,1},{5,7},{7,5},{8,10},{10,8},{12,... | collective-permute-start | bytes 1327112 | tf_op jit(solution)/shard_map/ppermute | solution.py:419
  181.6 25.7 %collective-permute-start.33 = (bf16[3,384,192]{1,2,0:T(8,128)(2,1)}, bf16[3,384,192]{1,2,0:T(8,128)(2,1)}, u32[]{:S(2)}, u32[]{:S(2)}) collective-permute-start(bf16[3,384,192]{1,2,0:T(8,128)(2,1)} %get-tuple-element.114), channel_id=1, source_target_pairs={{0,4},{2,6},{4,0},{6,2},{1,5},{3,7},{5,1},{7,3},{8,12},{10,14},{12... | collective-permute-start | bytes 1327112 | tf_op jit(solution)/shard_map/ppermute | solution.py:419
  181.9 25.5 %collective-permute-start.34 = (bf16[3,384,192]{1,2,0:T(8,128)(2,1)}, bf16[3,384,192]{1,2,0:T(8,128)(2,1)}, u32[]{:S(2)}, u32[]{:S(2)}) collective-permute-start(bf16[3,384,192]{1,2,0:T(8,128)(2,1)} %get-tuple-element.114), channel_id=1, source_target_pairs={{0,6},{2,4},{4,2},{6,0},{1,7},{3,5},{5,3},{7,1},{8,14},{10,12},{12... | collective-permute-start | bytes 1327112 | tf_op jit(solution)/shard_map/ppermute | solution.py:419
  205.1 30.8 %collective-permute-start.30 = (bf16[192,1024]{1,0:T(8,128)(2,1)S(1)}, bf16[192,1024]{1,0:T(8,128)(2,1)}, u32[]{:S(2)}, u32[]{:S(2)}) collective-permute-start(bf16[192,1024]{1,0:T(8,128)(2,1)S(1)} %get-tuple-element.109), channel_id=1, source_target_pairs={{0,1},{1,0},{2,3},{3,2},{4,5},{5,4},{6,7},{7,6},{8,9},{9,8},{10,11... | collective-permute-start | bytes 1179656 | tf_op jit(solution)/shard_map/ppermute | solution.py:409
  207.4 30.7 %collective-permute-start.39 = (bf16[3,384,192]{1,2,0:T(8,128)(2,1)}, bf16[3,384,192]{1,2,0:T(8,128)(2,1)}, u32[]{:S(2)}, u32[]{:S(2)}) collective-permute-start(bf16[3,384,192]{1,2,0:T(8,128)(2,1)} %collective-permute-done.32), channel_id=1, source_target_pairs={{0,1},{1,0},{2,3},{3,2},{4,5},{5,4},{6,7},{7,6},{8,9},{9,8},{10,11... | collective-permute-start | bytes 1327112 | tf_op jit(solution)/shard_map/ppermute | solution.py:409
  207.8 39.4 %collective-permute-start.40 = (bf16[3,384,192]{1,2,0:T(8,128)(2,1)}, bf16[3,384,192]{1,2,0:T(8,128)(2,1)}, u32[]{:S(2)}, u32[]{:S(2)}) collective-permute-start(bf16[3,384,192]{1,2,0:T(8,128)(2,1)} %collective-permute-done.33), channel_id=1, source_target_pairs={{0,1},{1,0},{2,3},{3,2},{4,5},{5,4},{6,7},{7,6},{8,9},{9,8},{10,11... | collective-permute-start | bytes 1327112 | tf_op jit(solution)/shard_map/ppermute | solution.py:409
  211.4 36.2 %collective-permute-start.41 = (bf16[3,384,192]{1,2,0:T(8,128)(2,1)}, bf16[3,384,192]{1,2,0:T(8,128)(2,1)}, u32[]{:S(2)}, u32[]{:S(2)}) collective-permute-start(bf16[3,384,192]{1,2,0:T(8,128)(2,1)} %collective-permute-done.34), channel_id=1, source_target_pairs={{0,1},{1,0},{2,3},{3,2},{4,5},{5,4},{6,7},{7,6},{8,9},{9,8},{10,11... | collective-permute-start | bytes 1327112 | tf_op jit(solution)/shard_map/ppermute | solution.py:409
  214.8 32.7 %collective-permute-start.37 = (bf16[2,384,768]{2,1,0:T(8,128)(2,1)}, bf16[2,384,768]{2,1,0:T(8,128)(2,1)}, u32[]{:S(2)}, u32[]{:S(2)}) collective-permute-start(bf16[2,384,768]{2,1,0:T(8,128)(2,1)} %stack.208), channel_id=1, source_target_pairs={{0,4},{2,6},{4,0},{6,2},{1,5},{3,7},{5,1},{7,3},{8,12},{10,14},{12... | collective-permute-start | bytes 3538952 | tf_op jit(solution)/shard_map/ppermute | solution.py:419
  236.0 35.7 %collective-permute-start.29 = (bf16[2,512,768]{2,1,0:T(8,128)(2,1)S(1)}, bf16[2,512,768]{2,1,0:T(8,128)(2,1)S(1)}, u32[]{:S(2)}, u32[]{:S(2)}) collective-permute-start(bf16[2,512,768]{2,1,0:T(8,128)(2,1)S(1)} %pad_maximum_fusion.1), channel_id=1, source_target_pairs={{0,2},{2,0},{4,6},{6,4},{1,3},{3,1},{5,7},{7,5},{8,10},{10,8},{12,... | collective-permute-start | bytes 4718600 | tf_op jit(solution)/shard_map/ppermute | solution.py:419
  247.3 35.6 %collective-permute-start.42 = (bf16[2,192,1024]{2,1,0:T(8,128)(2,1)S(1)}, bf16[2,192,1024]{2,1,0:T(8,128)(2,1)S(1)}, u32[]{:S(2)}, u32[]{:S(2)}) collective-permute-start(bf16[2,192,1024]{2,1,0:T(8,128)(2,1)S(1)} %key_backward.4), channel_id=1, source_target_pairs={{0,1},{1,0},{2,3},{3,2},{4,5},{5,4},{6,7},{7,6},{8,9},{9,8},{10,11... | collective-permute-start | bytes 2359304 | tf_op jit(solution)/shard_map/ppermute | solution.py:409
  248.7 44.4 %collective-permute-start.45 = (bf16[384,768]{1,0:T(8,128)(2,1)S(1)}, bf16[384,768]{1,0:T(8,128)(2,1)S(1)}, u32[]{:S(2)}, u32[]{:S(2)}) collective-permute-start(bf16[384,768]{1,0:T(8,128)(2,1)S(1)} %fusion.24), channel_id=1, source_target_pairs={{0,2},{2,0},{4,6},{6,4},{1,3},{3,1},{5,7},{7,5},{8,10},{10,8},{12,... | collective-permute-start | bytes 1769480 | tf_op jit(solution)/shard_map/ppermute | solution.py:419
  249.6 33.6 %collective-permute-start.43 = (bf16[192,1024]{1,0:T(8,128)(2,1)S(1)}, bf16[192,1024]{1,0:T(8,128)(2,1)S(1)}, u32[]{:S(2)}, u32[]{:S(2)}) collective-permute-start(bf16[192,1024]{1,0:T(8,128)(2,1)S(1)} %add_convert_fusion.8), channel_id=1, source_target_pairs={{0,8},{8,0},{16,24},{24,16},{1,9},{9,1},{17,25},{25,17},{2,10},{10... | collective-permute-start | bytes 1179656 | tf_op jit(solution)/shard_map/ppermute | solution.py:412
  297.3 26.7 %collective-permute-start.44 = (bf16[512,768]{1,0:T(8,128)(2,1)}, bf16[512,768]{1,0:T(8,128)(2,1)}, u32[]{:S(2)}, u32[]{:S(2)}) collective-permute-start(bf16[512,768]{1,0:T(8,128)(2,1)} %fusion.14), channel_id=1, source_target_pairs={{0,4},{2,6},{4,0},{6,2},{1,5},{3,7},{5,1},{7,3},{8,12},{10,14},{12... | collective-permute-start | bytes 2359304 | tf_op jit(solution)/shard_map/ppermute | solution.py:419
  298.9 17.3 %collective-permute-start.46 = (bf16[192,1024]{1,0:T(8,128)(2,1)}, bf16[192,1024]{1,0:T(8,128)(2,1)S(1)}, u32[]{:S(2)}, u32[]{:S(2)}) collective-permute-start(bf16[192,1024]{1,0:T(8,128)(2,1)} %get-tuple-element.212), channel_id=1, source_target_pairs={{0,8},{8,0},{16,24},{24,16},{1,9},{9,1},{17,25},{25,17},{2,10},{10... | collective-permute-start | bytes 1179656 | tf_op jit(solution)/shard_map/ppermute | solution.py:412
  304.0 15.6 %collective-permute-start.69 = (bf16[192,768]{1,0:T(8,128)(2,1)S(1)}, bf16[192,768]{1,0:T(8,128)(2,1)S(1)}, u32[]{:S(2)}, u32[]{:S(2)}) collective-permute-start(bf16[192,768]{1,0:T(8,128)(2,1)S(1)} %fusion.25), channel_id=1, source_target_pairs={{0,16},{8,24},{16,0},{24,8},{1,17},{9,25},{17,1},{25,9},{2,18},{10... | collective-permute-start | bytes 884744 | tf_op jit(solution)/shard_map/ppermute | solution.py:416
  306.3 30.0 %collective-permute-start.49 = (bf16[2,128,768]{2,1,0:T(8,128)(2,1)S(1)}, bf16[2,128,768]{2,1,0:T(8,128)(2,1)S(1)}, u32[]{:S(2)}, u32[]{:S(2)}) collective-permute-start(bf16[2,128,768]{2,1,0:T(8,128)(2,1)S(1)} %copy-done.25), channel_id=1, source_target_pairs={{0,6},{2,4},{4,2},{6,0},{1,7},{3,5},{5,3},{7,1},{8,14},{10,12},{12... | collective-permute-start | bytes 1179656 | tf_op jit(solution)/shard_map/ppermute | solution.py:419
  307.8 29.8 %collective-permute-start.48 = (bf16[2,128,768]{2,1,0:T(8,128)(2,1)S(1)}, bf16[2,128,768]{2,1,0:T(8,128)(2,1)S(1)}, u32[]{:S(2)}, u32[]{:S(2)}) collective-permute-start(bf16[2,128,768]{2,1,0:T(8,128)(2,1)S(1)} %copy-done.25), channel_id=1, source_target_pairs={{0,4},{2,6},{4,0},{6,2},{1,5},{3,7},{5,1},{7,3},{8,12},{10,14},{12... | collective-permute-start | bytes 1179656 | tf_op jit(solution)/shard_map/ppermute | solution.py:419
  316.2 23.3 %collective-permute-start.47 = (bf16[2,128,768]{2,1,0:T(8,128)(2,1)S(1)}, bf16[2,128,768]{2,1,0:T(8,128)(2,1)S(1)}, u32[]{:S(2)}, u32[]{:S(2)}) collective-permute-start(bf16[2,128,768]{2,1,0:T(8,128)(2,1)S(1)} %copy-done.25), channel_id=1, source_target_pairs={{0,2},{2,0},{4,6},{6,4},{1,3},{3,1},{5,7},{7,5},{8,10},{10,8},{12,... | collective-permute-start | bytes 1179656 | tf_op jit(solution)/shard_map/ppermute | solution.py:419
  319.7 18.0 %collective-permute-start.50 = (bf16[2,192,1024]{2,1,0:T(8,128)(2,1)S(1)}, bf16[2,192,1024]{2,1,0:T(8,128)(2,1)S(1)}, u32[]{:S(2)}, u32[]{:S(2)}) collective-permute-start(bf16[2,192,1024]{2,1,0:T(8,128)(2,1)S(1)} %key_backward.6), channel_id=1, source_target_pairs={{0,1},{1,0},{2,3},{3,2},{4,5},{5,4},{6,7},{7,6},{8,9},{9,8},{10,11... | collective-permute-start | bytes 2359304 | tf_op jit(solution)/shard_map/ppermute | solution.py:409
  324.0 13.7 %collective-permute-start.51 = (bf16[192,1024]{1,0:T(8,128)(2,1)}, bf16[192,1024]{1,0:T(8,128)(2,1)S(1)}, u32[]{:S(2)}, u32[]{:S(2)}) collective-permute-start(bf16[192,1024]{1,0:T(8,128)(2,1)} %get-tuple-element.211), channel_id=1, source_target_pairs={{0,8},{8,0},{16,24},{24,16},{1,9},{9,1},{17,25},{25,17},{2,10},{10... | collective-permute-start | bytes 1179656 | tf_op jit(solution)/shard_map/ppermute | solution.py:412
  336.2 17.4 %collective-permute-start.70 = (bf16[192,768]{1,0:T(8,128)(2,1)S(1)}, bf16[192,768]{1,0:T(8,128)(2,1)S(1)}, u32[]{:S(2)}, u32[]{:S(2)}) collective-permute-start(bf16[192,768]{1,0:T(8,128)(2,1)S(1)} %add_convert_fusion.11), channel_id=1, source_target_pairs={{0,8},{8,0},{16,24},{24,16},{1,9},{9,1},{17,25},{25,17},{2,10},{10... | collective-permute-start | bytes 884744 | tf_op jit(solution)/shard_map/ppermute | solution.py:412
  344.7 14.9 %collective-permute-start.53 = (bf16[3,192,256]{2,1,0:T(8,128)(2,1)S(1)}, bf16[3,192,256]{2,1,0:T(8,128)(2,1)S(1)}, u32[]{:S(2)}, u32[]{:S(2)}) collective-permute-start(bf16[3,192,256]{2,1,0:T(8,128)(2,1)S(1)} %get-tuple-element.198), channel_id=1, source_target_pairs={{0,4},{2,6},{4,0},{6,2},{1,5},{3,7},{5,1},{7,3},{8,12},{10,14},{12... | collective-permute-start | bytes 884744 | tf_op jit(solution)/shard_map/ppermute | solution.py:419
  345.0 17.4 %collective-permute-start.52 = (bf16[3,192,256]{2,1,0:T(8,128)(2,1)S(1)}, bf16[3,192,256]{2,1,0:T(8,128)(2,1)S(1)}, u32[]{:S(2)}, u32[]{:S(2)}) collective-permute-start(bf16[3,192,256]{2,1,0:T(8,128)(2,1)S(1)} %get-tuple-element.196), channel_id=1, source_target_pairs={{0,2},{2,0},{4,6},{6,4},{1,3},{3,1},{5,7},{7,5},{8,10},{10,8},{12,... | collective-permute-start | bytes 884744 | tf_op jit(solution)/shard_map/ppermute | solution.py:419
  347.0 19.1 %collective-permute-start.59 = (bf16[1152,192]{0,1:T(8,128)(2,1)S(1)}, bf16[1152,192]{0,1:T(8,128)(2,1)S(1)}, u32[]{:S(2)}, u32[]{:S(2)}) collective-permute-start(bf16[1152,192]{0,1:T(8,128)(2,1)S(1)} %constant_dynamic-slice_fusion.4), channel_id=1, source_target_pairs={{0,1},{1,0},{2,3},{3,2},{4,5},{5,4},{6,7},{7,6},{8,9},{9,8},{10,11... | collective-permute-start | bytes 1327112 | tf_op jit(solution)/shard_map/ppermute | solution.py:409
  353.6 14.3 %collective-permute-start.64 = (bf16[256,768]{1,0:T(8,128)(2,1)S(1)}, bf16[256,768]{1,0:T(8,128)(2,1)S(1)}, u32[]{:S(2)}, u32[]{:S(2)}) collective-permute-start(bf16[256,768]{1,0:T(8,128)(2,1)S(1)} %constant_dynamic-slice_fusion.2), channel_id=1, source_target_pairs={{0,8},{8,0},{16,24},{24,16},{1,9},{9,1},{17,25},{25,17},{2,10},{10... | collective-permute-start | bytes 1179656 | tf_op jit(solution)/shard_map/ppermute | solution.py:412
  353.8 27.9 %collective-permute-start.71 = (bf16[384,768]{1,0:T(8,128)(2,1)S(1)}, bf16[384,768]{1,0:T(8,128)(2,1)S(1)}, u32[]{:S(2)}, u32[]{:S(2)}) collective-permute-start(bf16[384,768]{1,0:T(8,128)(2,1)S(1)} %pad_maximum_fusion.8), channel_id=1, source_target_pairs={{0,1},{1,0},{2,3},{3,2},{4,5},{5,4},{6,7},{7,6},{8,9},{9,8},{10,11... | collective-permute-start | bytes 1769480 | tf_op jit(solution)/shard_map/ppermute | solution.py:409
  368.7 30.9 %collective-permute-start.65 = (bf16[256,768]{1,0:T(8,128)(2,1)}, bf16[256,768]{1,0:T(8,128)(2,1)}, u32[]{:S(2)}, u32[]{:S(2)}) collective-permute-start(bf16[256,768]{1,0:T(8,128)(2,1)} %fusion.22), channel_id=1, source_target_pairs={{0,16},{8,24},{16,0},{24,8},{1,17},{9,25},{17,1},{25,9},{2,18},{10... | collective-permute-start | bytes 1179656 | tf_op jit(solution)/shard_map/ppermute | solution.py:416
  378.2 22.8 %collective-permute-start.58 = (bf16[2,128,768]{2,1,0:T(8,128)(2,1)}, bf16[2,128,768]{2,1,0:T(8,128)(2,1)}, u32[]{:S(2)}, u32[]{:S(2)}) collective-permute-start(bf16[2,128,768]{2,1,0:T(8,128)(2,1)} %get-tuple-element.218), channel_id=1, source_target_pairs={{0,6},{2,4},{4,2},{6,0},{1,7},{3,5},{5,3},{7,1},{8,14},{10,12},{12... | collective-permute-start | bytes 1179656 | tf_op jit(solution)/shard_map/ppermute | solution.py:419
  379.8 21.2 %collective-permute-start.57 = (bf16[2,128,768]{2,1,0:T(8,128)(2,1)}, bf16[2,128,768]{2,1,0:T(8,128)(2,1)}, u32[]{:S(2)}, u32[]{:S(2)}) collective-permute-start(bf16[2,128,768]{2,1,0:T(8,128)(2,1)} %get-tuple-element.218), channel_id=1, source_target_pairs={{0,4},{2,6},{4,0},{6,2},{1,5},{3,7},{5,1},{7,3},{8,12},{10,14},{12... | collective-permute-start | bytes 1179656 | tf_op jit(solution)/shard_map/ppermute | solution.py:419
  380.0 21.0 %collective-permute-start.56 = (bf16[2,128,768]{2,1,0:T(8,128)(2,1)}, bf16[2,128,768]{2,1,0:T(8,128)(2,1)}, u32[]{:S(2)}, u32[]{:S(2)}) collective-permute-start(bf16[2,128,768]{2,1,0:T(8,128)(2,1)} %get-tuple-element.218), channel_id=1, source_target_pairs={{0,2},{2,0},{4,6},{6,4},{1,3},{3,1},{5,7},{7,5},{8,10},{10,8},{12,... | collective-permute-start | bytes 1179656 | tf_op jit(solution)/shard_map/ppermute | solution.py:419
  381.7 23.2 %collective-permute-start.61 = (bf16[576,192]{0,1:T(8,128)(2,1)}, bf16[576,192]{0,1:T(8,128)(2,1)}, u32[]{:S(2)}, u32[]{:S(2)}) collective-permute-start(bf16[576,192]{0,1:T(8,128)(2,1)} %fusion.28), channel_id=1, source_target_pairs={{0,16},{8,24},{16,0},{24,8},{1,17},{9,25},{17,1},{25,9},{2,18},{10... | collective-permute-start | bytes 663560 | tf_op jit(solution)/shard_map/ppermute | solution.py:416
  400.9 18.3 %collective-permute-start.66 = (bf16[256,768]{1,0:T(8,128)(2,1)S(1)}, bf16[256,768]{1,0:T(8,128)(2,1)S(1)}, u32[]{:S(2)}, u32[]{:S(2)}) collective-permute-start(bf16[256,768]{1,0:T(8,128)(2,1)S(1)} %add_convert_fusion.6), channel_id=1, source_target_pairs={{0,8},{8,0},{16,24},{24,16},{1,9},{9,1},{17,25},{25,17},{2,10},{10... | collective-permute-start | bytes 1179656 | tf_op jit(solution)/shard_map/ppermute | solution.py:412
  (76 other events, 708.0 us)

commit v4 on v3

--- a/solution.py
+++ b/solution.py
@@ -66,15 +66,16 @@
     return grad_unit - x * (inv * inv * jnp.sum(x * grad_unit, axis=0, keepdims=True))
 
 
-def both(a, b):
-    return jnp.concatenate([a[...], b[...]], axis=1)
-
-
-def key_kernel(planes, ka, va, kb, vb, *refs, chunk):
-    start, out = (None, *refs) if len(refs) == 1 else refs
-    _, upper, lower = sides(both(ka, kb), planes[...])
+def both(*refs):
+    return jnp.concatenate([ref[...] for ref in refs], axis=1)
+
+
+def key_kernel(planes, *refs, chunk, blocks):
+    keys, vals, out = refs[:blocks], refs[blocks : 2 * blocks], refs[-1]
+    start = refs[2 * blocks] if len(refs) > 2 * blocks + 1 else None
+    _, upper, lower = sides(both(*keys), planes[...])
     low, high = half_codes(upper, lower)
-    values = both(va, vb)
+    values = both(*vals)
     for c in range(0, 16, chunk):
         at = slice(128 * c, 128 * (c + chunk))
         part = dot(code_chunk(low, high, c, chunk), values, NT)
@@ -168,21 +169,21 @@
     )
 
 
-def key_tables(planes, kv_a, kv_b, start=None):
-    heads, width = kv_a.shape[0] // (2 * HEAD_DIM), kv_a.shape[1]
-    specs = [whole(64, 64)] + [per_head(width), per_head(width, heads)] * 2
-    args = [planes, kv_a, kv_a, kv_b, kv_b]
+def key_tables(planes, blocks, start, kind):
+    heads, width = blocks[0].shape[0] // (2 * HEAD_DIM), blocks[0].shape[1]
+    specs = [whole(64, 64)] + [per_head(width)] * len(blocks) + [per_head(width, heads)] * len(blocks)
+    args = [planes, *blocks, *blocks]
     if start is not None:
         specs.append(table_spec())
         args.append(start)
     return call(
-        partial(key_kernel, chunk=2),
+        partial(key_kernel, chunk=2, blocks=len(blocks)),
         heads,
-        10,
+        5 * len(blocks),
         "key_tables",
         specs,
         table_spec(),
-        jax.ShapeDtypeStruct((heads, ROWS, HEAD_DIM), f32 if start is None else bf16),
+        jax.ShapeDtypeStruct((heads, ROWS, HEAD_DIM), kind),
     )(*args)
 
 
@@ -257,13 +258,13 @@
 
 
 def dense_kernel(core, x_in, grad_out, gain, bias, *refs):
-    attn, weights = refs[0:4], refs[4:12]
-    layer_out, grad_first_out, normed_out, hidden, grad_pre, grad_ffn_out, grad_attn_out = refs[12:19]
-    estimates, small, slope = refs[19:23], refs[23], refs[24]
+    attn, ups, downs = refs[0:4], refs[4:12], refs[12:20]
+    layer_out, grad_first_out, normed_out, hidden, grad_pre, grad_ffn_out, grad_attn_out = refs[20:27]
+    estimates, small, slope = refs[27:31], refs[31], refs[32]
     part = hidden.shape[2]
     blocks = range(8)
     heads = jnp.concatenate([core_rows(core, attn[b // 2], b % 2) for b in blocks], axis=0)
-    out_w = jnp.concatenate([weights[b][2 * part :, :] for b in blocks], axis=0)
+    out_w = jnp.concatenate([downs[b][part:, :] for b in blocks], axis=0)
     attn_out = dot(heads, out_w, TN)
     resid = x_in[...].astype(f32)
     first = resid + attn_out
@@ -276,12 +277,12 @@
     normed_out[...] = normed
     second = normed.astype(f32)
     for b in blocks:
-        pre = dot(normed, weights[b][0:part, :], NT)
+        pre = dot(normed, ups[b][...], NT)
         below = 0.5 * (1.0 + lax.erf(pre * 0.7071067811865476))
         rows = (pre * below).astype(bf16)
         hidden[b] = rows
         slope[b] = below + pre * (0.3989422804014327 * jnp.exp(-0.5 * pre * pre))
-        second = second + dot(rows, weights[b][part : 2 * part, :], NN)
+        second = second + dot(rows, downs[b][0:part, :], NN)
     unit_2, inv_2 = norm(second)
     layer_out[...] = (unit_2 * gain[1:2, :] + bias[1:2, :]).astype(layer_out.dtype)
     grad = grad_out[...]
@@ -292,9 +293,9 @@
     grad_ffn_out[...] = grad_ffn
     grad_normed = grad_second
     for b in blocks:
-        rows = (dot(grad_ffn, weights[b][part : 2 * part, :], NT) * slope[b]).astype(bf16)
+        rows = (dot(grad_ffn, downs[b][0:part, :], NT) * slope[b]).astype(bf16)
         grad_pre[b] = rows
-        grad_normed = grad_normed + dot(rows, weights[b][0:part, :], NN)
+        grad_normed = grad_normed + dot(rows, ups[b][...], NN)
     small[0:1, :] = column_sum(grad_normed * unit_1)
     small[2:3, :] = column_sum(grad_normed)
     grad_first = norm_back(grad_normed * gain[0:1, :], unit_1, inv_1)
@@ -305,32 +306,32 @@
         half = estimates[0].shape[0] // 2
         at = core[0] if b % 2 == 0 else 1 - core[0]
         estimates[b // 2][pl.ds(pl.multiple_of(at * half, 16), half), :] = dot(
-            weights[b][2 * part :, :], grad_attn, NT
+            downs[b][part:, :], grad_attn, NT
         ).astype(bf16)
 
 
 def weight_grad_kernel(core, normed, hidden, grad_pre, grad_ffn, grad_attn, small, *refs):
-    attn, outs = refs[0:4], refs[4:8]
+    attn, down_out, ups = refs[0:4], refs[4], refs[5:7]
     part = hidden.shape[2]
     sums = jnp.concatenate([small[...], jnp.zeros_like(small[...])], axis=0).astype(bf16)
     for b in range(8):
-        down_out, up = outs[b % 2], outs[2 + b % 2]
-        down_out[b // 2, 0:part, :] = dot(hidden[b], grad_ffn[...], TN).astype(bf16)
+        owner = (core[1] ^ (b // 2)) * 2 + (core[0] if b % 2 == 0 else 1 - core[0])
         heads = core_rows(core, attn[b // 2], b % 2)
         at = part + heads.shape[0]
-        down_out[b // 2, part:at, :] = dot(heads, grad_attn[...], NN).astype(bf16)
-        down_out[b // 2, at : at + 16, :] = sums
-        down_out[b // 2, at + 16 :, :] = jnp.zeros_like(sums)
-        up[b // 2] = dot(grad_pre[b], normed[...], TN).astype(bf16)
+        down_out[owner, 0:part, :] = dot(hidden[b], grad_ffn[...], TN).astype(bf16)
+        down_out[owner, part:at, :] = dot(heads, grad_attn[...], NN).astype(bf16)
+        down_out[owner, at : at + 16, :] = sums
+        down_out[owner, at + 16 :, :] = jnp.zeros_like(sums)
+        ups[b % 2][b // 2] = dot(grad_pre[b], normed[...], TN).astype(bf16)
 
 
 def vmem(count):
     return [pl.BlockSpec(memory_space=pltpu.VMEM)] * count
 
 
-def dense(core, x_in, grad_out, gain, bias, attn, weights):
+def dense(core, x_in, grad_out, gain, bias, attn, ups, downs):
     rows, width = x_in.shape
-    part = (weights[0].shape[0] - attn[0].shape[0] // 2) // 2
+    part = ups[0].shape[0]
     shape = jax.ShapeDtypeStruct
     out_shape = [
         shape((rows, width), bf16),
@@ -345,24 +346,24 @@
     ]
     return pl.pallas_call(
         dense_kernel,
-        in_specs=[pl.BlockSpec(memory_space=pltpu.SMEM)] + vmem(16),
+        in_specs=[pl.BlockSpec(memory_space=pltpu.SMEM)] + vmem(24),
         out_specs=vmem(12),
         out_shape=out_shape,
         scratch_shapes=[pltpu.VMEM((8, rows, part), f32)],
         compiler_params=pltpu.CompilerParams(vmem_limit_bytes=56 << 20),
         cost_estimate=pl.CostEstimate(flops=18 * 10**9, bytes_accessed=1 << 20, transcendentals=0),
         name="dense",
-    )(core, x_in, grad_out, gain, bias, *attn, *weights)
+    )(core, x_in, grad_out, gain, bias, *attn, *ups, *downs)
 
 
 def weight_grads(core, normed, hidden, grad_pre, grad_ffn, grad_attn, small, attn):
     width, part = normed.shape[1], hidden.shape[2]
-    shapes = [jax.ShapeDtypeStruct((4, part + attn[0].shape[0] // 2 + 32, width), bf16)] * 2
+    shapes = [jax.ShapeDtypeStruct((8, part + attn[0].shape[0] // 2 + 32, width), bf16)]
     shapes += [jax.ShapeDtypeStruct((4, part, width), bf16)] * 2
     return pl.pallas_call(
         weight_grad_kernel,
         in_specs=[pl.BlockSpec(memory_space=pltpu.SMEM)] + vmem(10),
-        out_specs=vmem(4),
+        out_specs=vmem(3),
         out_shape=shapes,
         compiler_params=pltpu.CompilerParams(vmem_limit_bytes=56 << 20),
         cost_estimate=pl.CostEstimate(flops=9 * 10**9, bytes_accessed=1 << 20, transcendentals=0),
@@ -441,38 +442,16 @@
     bits = bit_rows()
 
     dense_in = jnp.stack([seq_rows(my_quarter, g)] + arrived)
-    blocks = [dense_in]
-    for j in range(1, head_count):
-        here = seq_rows(lax.dynamic_slice_in_dim(own, (d ^ j) * quarter, quarter, 0), g)
-        blocks.append(jnp.concatenate([here[None], over_head(dense_in[1:], j)]))
-    tokens = jnp.stack(blocks).reshape(n_tokens, width)
-    dense_in = dense_in.reshape(rows, width)
-
-    def project(w):
-        return jnp.einsum("cde,ld->cel", w, tokens, preferred_element_type=f32).astype(bf16)
-
-    kv = project(w_qkv[1:]).reshape(2 * head_width, n_tokens)
-    q = project(w_qkv[:1]).reshape(head_width, n_tokens)
-    kv_z = over_place(kv)
-    kv_o = over_seq(kv)
-    q_o = over_seq(q)
-    q_z = over_place(after(q, kv_o))
 
     def core_half(at):
         cut = hidden_own // 2
         out_cut = head_width // 2
-        return jnp.concatenate(
-            [
-                lax.dynamic_slice_in_dim(up_weight, at * cut, cut, 1).T,
-                lax.dynamic_slice_in_dim(down_weight, at * cut, cut, 0),
-                lax.dynamic_slice_in_dim(w_out, at * out_cut, out_cut, 0),
-            ],
-            axis=0,
-        )
-
-    weights = [core_half(s), core_half(1 - s)]
-    my_half = after(weights[0], tokens)
-    fetched = [over_head(my_half, j) for j in range(1, head_count)]
+        down = lax.dynamic_slice_in_dim(down_weight, at * cut, cut, 0)
+        out = lax.dynamic_slice_in_dim(w_out, at * out_cut, out_cut, 0)
+        return lax.dynamic_slice_in_dim(up_weight, at * cut, cut, 1).T, jnp.concatenate([down, out])
+
+    up, down = core_half(s)
+    ups, downs = [[x] for x in core_half(1 - s)]
 
     slot = jnp.arange(groups, dtype=jnp.int32)[:, None]
     place_of = ((g - slot) % groups) * places + r
@@ -482,12 +461,47 @@
     pick = (position.reshape(rows)[:, None] == mask_row[None]).astype(bf16)
     grad_out = jnp.dot(pick, cot, preferred_element_type=f32)
 
+    blocks = [dense_in]
+    for j in range(1, head_count):
+        here = seq_rows(lax.dynamic_slice_in_dim(own, (d ^ j) * quarter, quarter, 0), g)
+        there = after(over_head(dense_in[1:], j), up, down, *ups, *downs, grad_out, signed_t)
+        blocks.append(jnp.concatenate([here[None], there]))
+    tokens = jnp.stack(blocks).reshape(n_tokens, width)
+    dense_in = dense_in.reshape(rows, width)
+
+    def project(w):
+        return jnp.einsum("cde,ld->cel", w, tokens, preferred_element_type=f32).astype(bf16)
+
+    kv = project(w_qkv[1:]).reshape(2 * head_width, n_tokens)
+    q = project(w_qkv[:1]).reshape(head_width, n_tokens)
+    kv_z = over_place(kv)
+    kv_o = over_seq(kv)
+    q_o = over_seq(q)
+    q_z = over_place(after(q, kv_o))
+
+    up = after(up, tokens)
+    ups, downs = [up] + ups, [down] + downs
+    up_x, up_y = over_head(up, 1), over_head(up, 2)
+    tables = key_tables(after(signed, up, q), [kv, kv_o], None, f32)
+
+    kv_z = after(kv_z, tables)
     kv_zo = over_seq(kv_z)
+    up_x, up_y = after(up_x, tables), after(up_y, tables)
+    down = after(down, up_x, up_y)
+    down_x, down_y = over_head(down, 1), over_head(down, 2)
+    tables = key_tables(after(signed, down), [kv_z], tables, f32)
+
+    up_xo, up_yo = over_seq(after(up_x, tables)), over_seq(after(up_y, tables))
+    q_z = after(q_z, tables)
     q_zo = over_seq(q_z)
-    signed = after(signed, grad_out, weights[1])
-    tables = key_tables(signed, kv, kv_o)
-    tables = key_tables(signed, kv_z, kv_zo, tables)
-
+    kv_zo = after(kv_zo, tables)
+    tables = key_tables(after(signed, q_z), [kv_zo], tables, bf16)
+
+    q_zo = after(q_zo, tables)
+    down_x, down_y = after(down_x, tables), after(down_y, tables)
+    up_d, down_d = over_head(after(up_x, tables), 2), over_head(down_y, 1)
+    down_xo, down_yo = over_seq(down_x), over_seq(down_y)
+    q_zo = after(q_zo, down_x, down_y)
     e_zo = query_estimates(signed, q_zo, tables, bf16)
     e_zo_moved = over_seq(e_zo)
     e_z = query_estimates(signed, after(q_z, e_zo), tables, bf16)
@@ -495,92 +509,113 @@
     e_o = query_estimates(signed, after(q_o, e_far), tables, bf16)
     e_far = over_place(e_far)
     e_o_moved = over_seq(e_o)
-    fetched = [after(block, e_o) for block in fetched]
-    e = query_estimates(signed, after(q, e_o, *fetched), tables, f32)
-    for block in fetched:
-        weights += [block, over_seq(block)]
-    attn = add(e, after(e_o_moved, e), after(e_far, e)).astype(bf16)
+    e = query_estimates(signed, after(q, e_o), tables, f32)
+    e_far = after(e_far, e)
+    up_d, down_d = after(up_d, e), after(down_d, e)
+    up_xo, up_yo = after(up_xo, e_zo), after(up_yo, e_zo)
+    down_xo, down_yo = after(down_xo, e_zo), after(down_yo, e_zo)
+    ups += [up_x, up_xo, up_y, up_yo, up_d, over_seq(up_d)]
+    downs += [down_x, down_xo, down_y, down_yo, down_d, over_seq(down_d)]
+    attn = add(e, after(e_o_moved, e), e_far).astype(bf16)
 
     def to_dense(block):
         parts = [block[..., j * rows : (j + 1) * rows] for j in range(head_count)]
-        return [parts[0]] + [over_head(parts[j], j) for j in range(1, head_count)]
+        moved = [over_head(parts[j], j) for j in range(1, head_count)]
+        return [parts[0], *lax.optimization_barrier(moved)]
 
     attn_parts = to_dense(attn)
 
     def away(dense_rows):
         dense_rows = dense_rows.reshape(groups, quarter, width)
-        return jnp.stack(
-            [dense_rows[0]] + [over_group(dense_rows[k], groups - k) for k in range(1, groups)]
-        )
-
-    core = s.astype(jnp.int32).reshape(1)
+        return [dense_rows[0]] + [over_group(dense_rows[k], groups - k) for k in range(1, groups)]
+
+    core = jnp.stack([s, d]).astype(jnp.int32)
     (layer_rows, grad_first, normed, hidden, grad_pre, grad_ffn, grad_attn, *rest) = dense(
-        core, dense_in, grad_out, norm_gain, norm_bias, attn_parts, weights
+        core, dense_in, grad_out, norm_gain, norm_bias, attn_parts, ups, downs
     )
     est_parts, small = rest[:4], rest[4]
     grad = jnp.concatenate(
         [est_parts[0]] + [over_head(est_parts[j], j) for j in range(1, head_count)], axis=1
     )
-    mine_a, other_a, mine_b, other_b = weight_grads(
+    a_grads, mine_b, other_b = weight_grads(
         core, normed, hidden, grad_pre, grad_ffn, grad_attn, small, attn_parts
     )
 
+    a_sum = lax.psum_scatter(a_grads, ("head", "seq"), scatter_dimension=0, tiled=True)[0]
     grad_z = over_place(grad)
     grad_o = over_seq(grad)
-    swap_a = over_seq(after(other_a, grad_o))
     swap_b = over_seq(after(other_b, grad_o))
     layer_moved = away(layer_rows)
+    part, dq, dq_o = query_backward(
+        signed, signed_t, bits, q, grad, q_o, after(grad_o, mine_b), tables, None, f32, bf16
+    )
+
+    grad_zo = over_seq(after(grad_z, part))
+    layer_moved = jnp.stack([after(x, part) for x in layer_moved])
+    cut = mine_b.shape[1] // 2
+    chip_b = add(mine_b, after(swap_b, part)).astype(bf16)
+    x_out = jnp.stack([chip_b[1, :cut], chip_b[3, :cut]])
+    y_out = jnp.stack([chip_b[2, cut:], chip_b[3, cut:]])
+    x_far, y_far = over_head(x_out, 1), over_head(y_out, 2)
+    dq_o = over_seq(dq_o)
+    q_gated = after(q_z, x_out, y_out, layer_moved)
+    grad_tables, dq_z, dq_zo = query_backward(
+        signed, signed_t, bits, q_gated, grad_z, q_zo, grad_zo, tables, part, bf16, bf16
+    )
+
+    x_far, y_far = after(x_far, dq_z), after(y_far, dq_z)
+    x_own = add(chip_b[0, :cut], x_far[0])
+    y_own = add(chip_b[0, cut:], y_far[0])
+    x_out = add(chip_b[2, :cut], x_far[1]).astype(bf16)
+    y_out = add(chip_b[1, cut:], y_far[1]).astype(bf16)
+    x_last, y_last = over_head(x_out, 2), over_head(y_out, 1)
+    dq_zo = over_seq(dq_zo)
+    dq_own = add(dq, after(dq_o, dq_z))
+    dkv_zo = key_backward(
+        signed, signed_t, bits, after(kv_zo, dq_own, x_out, y_out), grad_tables, bf16
+    )
+
+    dkv_zo_moved = over_seq(dkv_zo)
+    dq_far = add(dq_z, after(dq_zo, dkv_zo)).astype(bf16)
+    b_halves = jnp.stack(
+        [add(x_own, after(x_last, dkv_zo)), add(y_own, after(y_last, dkv_zo))]
+    ).astype(bf16)
+    b_keep = lax.dynamic_index_in_dim(b_halves, r, 0, keepdims=False)
+    b_send = lax.dynamic_index_in_dim(b_halves, 1 - r, 0, keepdims=False)
+    dkv_z = key_backward(
+        signed, signed_t, bits, after(kv_z, dq_far, b_keep, b_send), grad_tables, bf16
+    )
+    dq_far, b_far = over_place(dq_far), over_place(b_send)
+
+    dkv_far = add(dkv_z, after(dkv_zo_moved, dkv_z)).astype(bf16)
+    grad_q = add(dq_own, after(dq_far, dkv_z)).astype(bf16)
+    b_keep = add(b_keep, after(b_far, dkv_z))
+    b_send = b_keep.astype(bf16)
+    dkv_o = key_backward(
+        signed, signed_t, bits, after(kv_o, dkv_far, grad_q, b_send), grad_tables, bf16
+    )
+    dk_far, dv_far = over_place(dkv_far[0]), over_place(after(dkv_far[1], dkv_o))
+    b_far = [over_group(b_send, k) for k in range(1, groups)]
+
+    dkv_o_moved = over_seq(dkv_o)
+    a_sum = after(a_sum, dkv_o)
+    dk_far = after(dk_far, dkv_o)
+    b_send = add(b_keep, *[after(x, dkv_o) for x in b_far]).astype(bf16)
+    layer_moved = after(layer_moved, dkv_o)
+    layer_moved = [layer_moved] + [over_head(layer_moved, j) for j in range(1, head_count)]
     qkv_cut = width // 2
     qkv_near = [lax.dynamic_slice_in_dim(w_qkv, s * qkv_cut, qkv_cut, 1)]
     qkv_far = [lax.dynamic_slice_in_dim(w_qkv, (1 - s) * qkv_cut, qkv_cut, 1)]
-    qkv_half = after(qkv_near[0], grad_o)
-    qkv_near += [over_head(qkv_half, j) for j in range(1, head_count)]
-    part, dq, dq_o = query_backward(
-        signed, signed_t, bits, q, grad, q_o, after(grad_o, mine_a), tables, None, f32, bf16
-    )
-
-    grad_zo = over_seq(after(grad_z, part))
-    chip_a = add(mine_a, after(swap_a, part)).astype(bf16)
-    chip_b = add(mine_b, after(swap_b, part)).astype(bf16)
-    qkv_near[1:] = [after(block, part) for block in qkv_near[1:]]
-    layer_moved = after(layer_moved, part)
-    a_out, b_out = jnp.stack([chip_a[1], chip_a[3]]), jnp.stack([chip_b[2], chip_b[3]])
-    a_far, b_far = over_head(a_out, 1), over_head(b_out, 2)
-    dq_o = over_seq(dq_o)
-    q_gated = after(q_z, a_out, b_out, layer_moved, *qkv_near[1:])
-    grad_tables, dq_z, dq_zo = query_backward(
-        signed, signed_t, bits, q_gated, grad_z, q_zo, grad_zo, tables, part, bf16, bf16
-    )
-
-    dq_zo = over_seq(dq_zo)
-    dq_own = add(dq, after(dq_o, dq_z))
-    qkv_swaps = [over_seq(block) for block in qkv_near[1:]]
-    dkv_zo = key_backward(signed, signed_t, bits, after(kv_zo, dq_own), grad_tables, bf16)
-
-    dkv_zo_moved = over_seq(dkv_zo)
-    qkv_far += [after(block, dkv_zo) for block in qkv_swaps]
-    dq_far = add(dq_z, after(dq_zo, dkv_zo)).astype(bf16)
-    a_far, b_far = after(a_far, dkv_zo), after(b_far, dkv_zo)
-    a_two = [add(chip_a[0], a_far[0]), add(chip_a[2], a_far[1]).astype(bf16)]
-    b_two = [add(chip_b[0], b_far[0]), add(chip_b[1], b_far[1]).astype(bf16)]
-    kv_gated = after(kv_z, a_two[1], b_two[1], dq_far, *qkv_far)
-    dkv_z = key_backward(signed, signed_t, bits, kv_gated, grad_tables, bf16)
-    dq_far = over_place(dq_far)
-    a_last, b_last = over_head(a_two[1], 2), over_head(b_two[1], 1)
-
-    dkv_far = add(dkv_z, after(dkv_zo_moved, dkv_z)).astype(bf16)
-    grad_q = add(dq_own, after(dq_far, dkv_z)).astype(bf16)
-    dkv_o = key_backward(signed, signed_t, bits, after(kv_o, dkv_far, grad_q), grad_tables, bf16)
-    dk_far, dv_far = over_place(dkv_far[0]), over_place(dkv_far[1])
-
-    dkv_o_moved = over_seq(dkv_o)
-    a_sum = add(a_two[0], after(a_last, dkv_o)).astype(bf16)
-    b_sum = add(b_two[0], after(b_last, dkv_o)).astype(bf16)
-    dk_far = after(dk_far, dkv_o)
-    layer_moved = after(layer_moved, dkv_o)
-    layer_moved = [layer_moved] + [over_head(layer_moved, j) for j in range(1, head_count)]
-    dkv = key_backward(signed, signed_t, bits, after(kv, a_sum, b_sum, dk_far), grad_tables, f32)
-
+    qkv_half = after(qkv_near[0], dkv_z)
+    qkv_near += [after(over_head(qkv_half, j), dkv_o) for j in range(1, head_count)]
+    dkv = key_backward(
+        signed, signed_t, bits, after(kv, dk_far, b_send, a_sum), grad_tables, f32
+    )
+    a_sum = lax.psum(a_sum, "hash")
+    b_far = over_place(b_send)
+
+    qkv_near[1:] = [after(x, dkv) for x in qkv_near[1:]]
+    qkv_far += [over_seq(x) for x in qkv_near[1:]]
     dkv_o_moved = after(dkv_o_moved, dkv)
     grad_k = add(dkv[0], dkv_o_moved[0], dk_far)
     grad_v = add(dkv[1], dkv_o_moved[1], after(dv_far, dkv))
@@ -596,7 +631,7 @@
         [jnp.where(s == 0, near, far), jnp.where(s == 0, far, near)], axis=1
     )
 
-    grad_moved = away(grad_in.astype(bf16))
+    grad_moved = jnp.stack(away(grad_in.astype(bf16)))
     grad_moved = [grad_moved] + [over_head(grad_moved, j) for j in range(1, head_count)]
 
     def home(blocks):
@@ -615,7 +650,7 @@
             )
         return jnp.concatenate(columns, axis=0)
 
-    layer_out = home([after(x, dkv) for x in layer_moved])
+    layer_out = home([after(x, grad_moved[0]) for x in layer_moved])
     grad_inputs = home(grad_moved).astype(f32)
 
     def in_halves(index, mine, other):
@@ -631,13 +666,8 @@
         total = add(total, *[over_group(sent, k) for k in range(1, groups)]).astype(bf16)
         return in_halves(r, total, over_place(total))
 
-    a_sum, b_sum = over_hash_sum(a_sum), over_hash_sum(b_sum)
-    a_other, b_other = over_seq(a_sum), over_seq(b_sum)
-    cut = hidden_own // 2
-    grad_w_down = in_halves(s, a_sum[:cut], a_other[:cut]).astype(f32)
-    out_cut = cut + head_width // 2
-    grad_w_out = in_halves(s, a_sum[cut:out_cut], a_other[cut:out_cut]).astype(f32)
-    small = a_sum[out_cut : out_cut + 8].astype(f32)
+    b_sum = in_halves(r, b_send, after(b_far, dkv))
+    b_other = over_seq(b_sum)
     grad_w_up = in_halves(s, b_sum, b_other).T.astype(f32)
 
     grad_w_qkv = jnp.einsum("ld,cel->cde", tokens, grad_qkv, preferred_element_type=f32)
@@ -646,7 +676,14 @@
     mine = lax.dynamic_slice_in_dim(grad_w_qkv, s * half, half, 0)
     other = over_seq(lax.dynamic_slice_in_dim(grad_w_qkv, (1 - s) * half, half, 0))
     total = over_hash_sum(add(mine, other).astype(bf16))
+    a_sum = after(a_sum, total)
     grad_w_qkv = in_halves(s, total, over_seq(total)).reshape(3, width, head_width).astype(f32)
+
+    a_other = over_seq(a_sum)
+    cut, out_cut = hidden_own // 2, (hidden_own + head_width) // 2
+    grad_w_down = in_halves(s, a_sum[:cut], a_other[:cut]).astype(f32)
+    grad_w_out = in_halves(s, a_sum[cut:out_cut], a_other[cut:out_cut]).astype(f32)
+    small = a_sum[out_cut : out_cut + 8].astype(f32)
 
     count = piece * seqs * width * hash_count * 2
     stream_rms = jnp.sqrt(jnp.sum(small[4:7], axis=1) / count)

time: 431 us -> 378 us (0.88)
  waiting for transfers between devices: 113 us -> 77.5 us
  between operations: 2.25 us -> 15.6 us
  other arithmetic: 34.4 us -> 23.2 us
  starting transfers between devices: 81.5 us -> 71.8 us
  matrix products: 13.3 us -> 7.96 us
    ppermute x28 -> x31, waiting for transfers between devices: 46.2 us -> 29.9 us  [over_head(): return lax.ppermute(x, 'head', [(h, h ^ j) for h in range(head_count)])]
    ppermute x6 -> x5, waiting for transfers between devices: 33.4 us -> 23.7 us  [over_group(): return lax.ppermute(x, 'hash', moves)]
    ppermute x13 -> x11, waiting for transfers between devices: 33.2 us -> 23.8 us  [over_place(): return lax.ppermute(x, 'hash', [(h, h ^ 1) for h in range(hash_count)])]
    convert_element_type x7 -> x5, other arithmetic: 8.65 us -> 1.26 us  [the longest x1 0.82 us: shards(): b_send = add(b_keep, *[after(x, dkv_o) for x in b_far]).astype(bf16)]
    ppermute x28 -> x31, starting transfers between devices: 30.8 us -> 26.7 us  [over_head(): return lax.ppermute(x, 'head', [(h, h ^ j) for h in range(head_count)])]
    ppermute x13 -> x11, starting transfers between devices: 11.6 us -> 8.08 us  [over_place(): return lax.ppermute(x, 'hash', [(h, h ^ 1) for h in range(hash_count)])]
    ppermute x24 -> x26, starting transfers between devices: 28.5 us -> 25.5 us  [over_seq(): return lax.ppermute(x, 'seq', [(0, 1), (1, 0)])]
    ppermute x6 -> x5, starting transfers between devices: 7.99 us -> 8.81 us  [over_group(): return lax.ppermute(x, 'hash', moves)]
  transfers between devices with their start and end apart: 72 -> 76, of which waited for: 19 -> 22; matrix products, arithmetic and copies ran while one was open for 17% -> 14% of each run, Pallas kernels for 28% -> 31%
where the time goes in v4:
time: 378 us; the launch traced here: 375 us
  Pallas kernels  135 us (36%)
  waiting for transfers between devices  77.5 us (21%)
  starting transfers between devices  71.8 us (19%)
  local copies, waits for them, and re-layouts  43.7 us (12%)
  other arithmetic  23.2 us (6%)
  between operations  15.6 us (4%)
  matrix products  7.96 us (2%)
    pallas_call x2, Pallas kernels, query_backward(): call(partial(query_back_kernel, chunk=4), heads, 20, 'query_backward', sp...  39.9 us
    pallas_call x4, Pallas kernels, key_backward(): call(partial(key_back_kernel, chunk=4), heads, 9, 'key_backward', [whole(...  36.3 us
    ppermute x31, waiting for transfers between devices, over_head(): return lax.ppermute(x, 'head', [(h, h ^ j) for h in range(head_count)])  29.9 us
    ppermute x31, starting transfers between devices, over_head(): return lax.ppermute(x, 'head', [(h, h ^ j) for h in range(head_count)])  26.7 us
    unnamed x121, local copies, waits for them, and re-layouts  25.8 us
    ppermute x26, starting transfers between devices, over_seq(): return lax.ppermute(x, 'seq', [(0, 1), (1, 0)])  25.5 us
    ppermute x11, waiting for transfers between devices, over_place(): return lax.ppermute(x, 'hash', [(h, h ^ 1) for h in range(hash_count)])  23.8 us
    ppermute x5, waiting for transfers between devices, over_group(): return lax.ppermute(x, 'hash', moves)  23.7 us
  transfers between devices with their start and end apart: 76, of which 22 were waited for; matrix products, arithmetic and copies ran while one was open for 14% of the time, Pallas kernels for 31%

profile of v4, /device:TPU:1, one launch (start us, length us, event | category | flops | bytes accessed | tf_op | source)
XLA Modules:
  0.0 374.6 jit_solution(18334379570171883705)
XLA Ops:
  7.3 4.5 %constant_dynamic-slice_fusion.12 = (bf16[1,128,1,768]{3,2,1,0:T(2,128)(2,1)}, bf16[1,128,1,768]{3,2,1,0:T(2,128)(2,1)S(1)}, bf16[1,128,1,768]{3,2,1,0:T(2,128)(...) fusion(bf16[1,512,2,768]{3,2,1,0:T(2,128)(2,1)} %param.11, s32[]{:T(128)S(6)} %select_n.293, ...), kind=kLoop, calls=%fused_computation.160 | loop fusion | bytes 1966104 | tf_op jit(solution)/shard_map/jit(dynamic_index_in_dim)/dynamic_slice | solution.py:423
  12.6 3.1 collective-permute-start
  16.3 2.6 collective-permute-start.1
  19.6 1.9 copy_bitcast_fusion.3
  22.9 1.8 copy_bitcast_fusion.1
  24.6 2.3 fusion.grad_out
  31.3 2.6 collective-permute-start.4
  36.0 3.3 collective-permute-done.4
  39.4 4.4 %collective-permute-done.3 = bf16[1,128,768]{2,1,0:T(8,128)(2,1)S(1)} collective-permute-done((bf16[1,128,768]{2,1,0:T(8,128)(2,1)}, bf16[1,128,768]{2,1,0:T(8,128)(2,1)S(1)}, u32[]{:S(2)}, u32[]{:S(2)}) %collective-permute-start.3) | collective-permute-done | bytes 196640 | tf_op jit(solution)/shard_map/ppermute | solution.py:420
  49.4 7.8 %key_tables.3.refs_2_ = f32[3,2048,64]{2,1,0:T(8,128)S(1)} custom-call(bf16[64,64]{1,0:T(8,128)(2,1)S(1)} %bitcast.218, bf16[384,1024]{1,0:T(8,128)(2,1)S(1)} %bitcast.213, bf16[384,1024]{1,0:T(8,128)(2,1)S(1)} %collective-permute-done.6.refs_1_.refs_3_.keys.vals, bf16[384,1024]{1,0:T(8,128)(2,1)S(1)} %bitcast.214, ...), custom_call_target="tpu_custom_call" | custom-call | flops 11000000512 | bytes 1048576 | tf_op jit(solution)/shard_map/key_tables/pallas_call | solution.py:179
  58.9 7.8 %collective-permute-done.10.refs_0_.refs_1_.keys.vals = bf16[384,1024]{1,0:T(8,128)(2,1)S(1)} collective-permute-done((bf16[384,1024]{1,0:T(8,128)(2,1)S(1)}, bf16[384,1024]{1,0:T(8,128)(2,1)S(1)}, u32[]{:S(2)}, u32[]{:S(2)}) %collective-permute-start.10) | collective-permute-done | bytes 786464 | tf_op jit(solution)/shard_map/ppermute | solution.py:413
  70.1 5.5 %key_tables.4.refs_2_ = f32[3,2048,64]{2,1,0:T(8,128)S(1)} custom-call(bf16[64,64]{1,0:T(8,128)(2,1)S(1)} %bitcast.219, bf16[384,1024]{1,0:T(8,128)(2,1)S(1)} %collective-permute-done.10.refs_0_.refs_1_.keys.vals, bf16[384,1024]{1,0:T(8,128)(2,1)S(1)} %collective-permute-done.10.refs_0_.refs_1_.keys.vals, f32[3,2048,64]{2,1,0:T(8,128)} %copy-done.11), custom_call_target="tpu_custom_call" | custom-call | flops 5500000256 | bytes 1048576 | tf_op jit(solution)/shard_map/key_tables/pallas_call | solution.py:179
  75.6 3.7 collective-permute-done.7.q.qa
  79.3 1.9 collective-permute-start.21
  81.3 5.3 %key_tables.5.tables = bf16[3,2048,64]{2,1,0:T(8,128)(2,1)S(1)} custom-call(bf16[64,64]{1,0:T(8,128)(2,1)S(1)} %bitcast.220, bf16[384,1024]{1,0:T(8,128)(2,1)} %collective-permute-done.12.refs_0_.refs_1_.keys.vals, bf16[384,1024]{1,0:T(8,128)(2,1)} %collective-permute-done.12.refs_0_.refs_1_.keys.vals, f32[3,2048,64]{2,1,0:T(8,128)S(1)} %key_tables.4.refs_2_), custom_call_target="tpu_custom_call" | custom-call | flops 5500000256 | bytes 1048576 | tf_op jit(solution)/shard_map/key_tables/pallas_call | solution.py:179
  86.8 3.3 query_estimates.4
  92.3 3.3 query_estimates.5
  98.0 3.3 query_estimates.6
  101.4 8.7 %collective-permute-done.23.refs_10_ = bf16[384,768]{1,0:T(8,128)(2,1)S(1)} collective-permute-done((bf16[384,768]{1,0:T(8,128)(2,1)}, bf16[384,768]{1,0:T(8,128)(2,1)S(1)}, u32[]{:S(2)}, u32[]{:S(2)}) %collective-permute-start.23) | collective-permute-done | bytes 589856 | tf_op jit(solution)/shard_map/ppermute | solution.py:420
  110.6 1.9 collective-permute-start.16
  112.4 3.5 query_estimates.7
  116.0 3.1 collective-permute-done.17
  119.1 2.5 collective-permute-start.22
  128.9 2.2 collective-permute-done.20.refs_3_
  132.3 17.4 %dense.1 = (bf16[256,768]{1,0:T(8,128)(2,1)}, f32[256,768]{1,0:T(8,128)}, bf16[256,768]{1,0:T(8,128)(2,1)}, bf16[8,256,384]{2,1,0:T(8,128)(2,1)}, bf16[8,256,384...) custom-call(s32[2]{0:T(128)} %pad_add_fusion.core, ...), custom_call_target="tpu_custom_call" | custom-call | flops 17999998976 | bytes 1048576 | tf_op jit(solution)/shard_map/dense/pallas_call | solution.py:347
  153.5 2.6 collective-permute-done.31
  156.1 2.6 collective-permute-start.32
  158.7 9.4 %weight_grads.1 = (bf16[8,512,768]{2,1,0:T(8,128)(2,1)}, bf16[4,384,768]{2,1,0:T(8,128)(2,1)}, bf16[4,384,768]{2,1,0:T(8,128)(2,1)}) custom-call(s32[2]{0:T(128)} %pad_add_fusion.core, bf16[256,768]{1,0:T(8,128)(2,1)} %get-tuple-element.150.normed, bf16[8,256,384]{2,1,0:T(8,128)(2,1)} %get-tuple-element.151.hidden, ...), custom_call_target="tpu_custom_call" | custom-call | flops 8999999488 | bytes 1048576 | tf_op jit(solution)/shard_map/weight_grads/pallas_call | solution.py:363
  175.5 19.6 %query_backward.2 = (f32[3,2048,64]{2,1,0:T(8,128)}, f32[192,1024]{1,0:T(8,128)S(1)}, bf16[192,1024]{1,0:T(8,128)(2,1)S(1)}) custom-call(bf16[64,64]{1,0:T(8,128)(2,1)S(1)} %bitcast.225, bf16[64,128]{1,0:T(8,128)(2,1)S(1)} %pad_maximum_fusion.12.planes_t, bf16[80,2048]{1,0:T(8,128)(2,1)S(1)} %copy-done.10, bf16[192,1024]{1,0:T(8,128)(2,1)S(1)} %fusion.4.q.qa, ...), custom_call_target="tpu_custom_call" | custom-call | flops 22000001024 | bytes 1048576 | tf_op jit(solution)/shard_map/query_backward/pallas_call | solution.py:210
  197.1 2.2 add_convert_fusion
  200.8 20.2 %query_backward.3 = (bf16[3,2048,64]{2,1,0:T(8,128)(2,1)S(1)}, bf16[192,1024]{1,0:T(8,128)(2,1)S(1)}, bf16[192,1024]{1,0:T(8,128)(2,1)S(1)}) custom-call(bf16[64,64]{1,0:T(8,128)(2,1)S(1)} %bitcast.226, bf16[64,128]{1,0:T(8,128)(2,1)S(1)} %pad_maximum_fusion.12.planes_t, bf16[80,2048]{1,0:T(8,128)(2,1)S(1)} %copy-done.10, bf16[192,1024]{1,0:T(8,128)(2,1)S(1)} %copy-done.3, ...), custom_call_target="tpu_custom_call" | custom-call | flops 22000001024 | bytes 1048576 | tf_op jit(solution)/shard_map/query_backward/pallas_call | solution.py:210
  222.2 2.5 collective-permute-done.40
  226.3 9.8 %key_backward.4 = bf16[2,192,1024]{2,1,0:T(8,128)(2,1)S(1)} custom-call(bf16[64,64]{1,0:T(8,128)(2,1)S(1)} %bitcast.227, bf16[64,128]{1,0:T(8,128)(2,1)S(1)} %pad_maximum_fusion.12.planes_t, bf16[80,2048]{1,0:T(8,128)(2,1)S(1)} %copy-done.10, bf16[384,1024]{1,0:T(8,128)(2,1)} %collective-permute-done.12.refs_0_.refs_1_.keys.vals, ...), custom_call_target="tpu_custom_call" | custom-call | flops 9900000256 | bytes 1048576 | tf_op jit(solution)/shard_map/key_backward/pallas_call | solution.py:224
  239.6 9.0 %key_backward.5 = bf16[2,192,1024]{2,1,0:T(8,128)(2,1)S(1)} custom-call(bf16[64,64]{1,0:T(8,128)(2,1)S(1)} %bitcast.228, bf16[64,128]{1,0:T(8,128)(2,1)S(1)} %pad_maximum_fusion.12.planes_t, bf16[80,2048]{1,0:T(8,128)(2,1)S(1)} %copy-done.10, bf16[384,1024]{1,0:T(8,128)(2,1)S(1)} %collective-permute-done.10.refs_0_.refs_1_.keys.vals, ...), custom_call_target="tpu_custom_call" | custom-call | flops 9900000256 | bytes 1048576 | tf_op jit(solution)/shard_map/key_backward/pallas_call | solution.py:224
  252.2 2.5 collective-permute-done.45
  254.8 2.2 collective-permute-start.47
  259.3 8.7 %key_backward.6 = bf16[2,192,1024]{2,1,0:T(8,128)(2,1)S(1)} custom-call(bf16[64,64]{1,0:T(8,128)(2,1)S(1)} %bitcast.229, bf16[64,128]{1,0:T(8,128)(2,1)S(1)} %pad_maximum_fusion.12.planes_t, bf16[80,2048]{1,0:T(8,128)(2,1)S(1)} %copy-done.10, bf16[384,1024]{1,0:T(8,128)(2,1)S(1)} %collective-permute-done.6.refs_1_.refs_3_.keys.vals, ...), custom_call_target="tpu_custom_call" | custom-call | flops 9900000256 | bytes 1048576 | tf_op jit(solution)/shard_map/key_backward/pallas_call | solution.py:224
  276.2 8.8 %key_backward.7 = f32[2,192,1024]{2,1,0:T(8,128)S(1)} custom-call(bf16[64,64]{1,0:T(8,128)(2,1)S(1)} %bitcast.230, bf16[64,128]{1,0:T(8,128)(2,1)S(1)} %pad_maximum_fusion.12.planes_t, bf16[80,2048]{1,0:T(8,128)(2,1)S(1)} %copy-done.10, bf16[384,1024]{1,0:T(8,128)(2,1)S(1)} %bitcast.215, bf16[384,1024]{1,0:T(8,128)(2,1)S(1)} %bitcast.216, ...), custom_call_target="tpu_custom_call" | custom-call | flops 9900000256 | bytes 1048576 | tf_op jit(solution)/shard_map/key_backward/pallas_call | solution.py:224
  292.2 6.3 %collective-permute-done.72 = bf16[192,768]{1,0:T(8,128)(2,1)} collective-permute-done((bf16[192,768]{1,0:T(8,128)(2,1)}, bf16[192,768]{1,0:T(8,128)(2,1)}, u32[]{:S(2)}, u32[]{:S(2)}) %collective-permute-start.72) | collective-permute-done | bytes 294944 | tf_op jit(solution)/shard_map/ppermute | solution.py:413
  298.6 3.7 collective-permute-start.58
  310.8 2.1 collective-permute-start.59
  313.9 2.2 collective-permute-start.67
  316.5 2.2 copy.50
  318.7 12.9 %collective-permute-done.59 = bf16[128,768]{1,0:T(8,128)(2,1)} collective-permute-done((bf16[128,768]{1,0:T(8,128)(2,1)}, bf16[128,768]{1,0:T(8,128)(2,1)}, u32[]{:S(2)}, u32[]{:S(2)}) %collective-permute-start.59) | collective-permute-done | bytes 196640 | tf_op jit(solution)/shard_map/ppermute | solution.py:417
  337.4 2.8 copy.47
  340.2 10.8 %collective-permute-done.68 = bf16[576,192]{0,1:T(8,128)(2,1)S(1)} collective-permute-done((bf16[576,192]{0,1:T(8,128)(2,1)S(1)}, bf16[576,192]{0,1:T(8,128)(2,1)S(1)}, u32[]{:S(2)}, u32[]{:S(2)}) %collective-permute-start.68) | collective-permute-done | bytes 221216 | tf_op jit(solution)/shard_map/ppermute | solution.py:417
  351.3 1.8 collective-permute-done.64
  353.8 4.1 %copy.48 = f32[1,512,2,768]{3,2,1,0:T(2,128)} copy(f32[1,512,2,768]{3,1,2,0:T(8,128)S(1)} %maximum_convert_fusion) | data formatting | bytes 6291456
  (336 shorter events, 102.3 us)
Async XLA Ops:
  7.2 267.6 %reduce-scatter.2.cloned.1.call-start = ((), (), s32[]{:S(2)}) async-start(), calls=%async_computation.1 | async-start | bytes 7077888 | tf_op jit(solution)/shard_map/reduce_scatter | solution.py:544
  12.6 18.7 %collective-permute-start = (bf16[128,768]{1,0:T(8,128)(2,1)}, bf16[128,768]{1,0:T(8,128)(2,1)}, u32[]{:S(2)}, u32[]{:S(2)}) collective-permute-start(bf16[128,768]{1,0:T(8,128)(2,1)} %bitcast.210), channel_id=1, source_target_pairs={{0,16},{8,24},{16,0},{24,8},{1,17},{9,25},{17,1},{25,9},{2,18},{10... | collective-permute-start | bytes 589832 | tf_op jit(solution)/shard_map/ppermute | solution.py:417
  16.3 14.9 %collective-permute-start.1 = (bf16[8,8,64]{2,0,1:T(8,128)(2,1)}, bf16[8,8,64]{2,0,1:T(8,128)(2,1)S(1)}, u32[]{:S(2)}, u32[]{:S(2)}) collective-permute-start(bf16[8,8,64]{2,0,1:T(8,128)(2,1)} %fusion.41), channel_id=1, source_target_pairs={{0,0},{8,1},{16,8},{24,9},{1,16},{9,17},{17,24},{25,25},{2,2},{10,... | collective-permute-start | bytes 24584 | tf_op jit(solution)/shard_map/ppermute | solution.py:436
  46.7 21.5 %collective-permute-start.8 = (bf16[384,768]{1,0:T(8,128)(2,1)}, bf16[384,768]{1,0:T(8,128)(2,1)}, u32[]{:S(2)}, u32[]{:S(2)}) collective-permute-start(bf16[384,768]{1,0:T(8,128)(2,1)} %bitcast.13.refs_4_), channel_id=1, source_target_pairs={{0,2},{2,0},{4,6},{6,4},{1,3},{3,1},{5,7},{7,5},{8,10},{10,8},{12,... | collective-permute-start | bytes 1769480 | tf_op jit(solution)/shard_map/ppermute | solution.py:420
  47.9 20.3 %collective-permute-start.9 = (bf16[384,768]{1,0:T(8,128)(2,1)}, bf16[384,768]{1,0:T(8,128)(2,1)}, u32[]{:S(2)}, u32[]{:S(2)}) collective-permute-start(bf16[384,768]{1,0:T(8,128)(2,1)} %bitcast.13.refs_4_), channel_id=1, source_target_pairs={{0,4},{2,6},{4,0},{6,2},{1,5},{3,7},{5,1},{7,3},{8,12},{10,14},{12... | collective-permute-start | bytes 1769480 | tf_op jit(solution)/shard_map/ppermute | solution.py:420
  48.2 18.5 %collective-permute-start.10 = (bf16[384,1024]{1,0:T(8,128)(2,1)S(1)}, bf16[384,1024]{1,0:T(8,128)(2,1)S(1)}, u32[]{:S(2)}, u32[]{:S(2)}) collective-permute-start(bf16[384,1024]{1,0:T(8,128)(2,1)S(1)} %bitcast.212), channel_id=1, source_target_pairs={{0,8},{8,0},{16,24},{24,16},{1,9},{9,1},{17,25},{25,17},{2,10},{10... | collective-permute-start | bytes 2359304 | tf_op jit(solution)/shard_map/ppermute | solution.py:413
  66.7 14.5 %collective-permute-start.12 = (bf16[384,1024]{1,0:T(8,128)(2,1)S(1)}, bf16[384,1024]{1,0:T(8,128)(2,1)}, u32[]{:S(2)}, u32[]{:S(2)}) collective-permute-start(bf16[384,1024]{1,0:T(8,128)(2,1)S(1)} %collective-permute-done.10.refs_0_.refs_1_.keys.vals), channel_id=1, source_target_pairs={{0,1},{1,0},{2,3},{3,2},{4,5},{5,4},{6,7},{7,6},{8,9},{9,8},{10,11... | collective-permute-start | bytes 2359304 | tf_op jit(solution)/shard_map/ppermute | solution.py:410
  68.2 28.8 %collective-permute-start.5 = (bf16[192,1024]{1,0:T(8,128)(2,1)S(1)}, bf16[192,1024]{1,0:T(8,128)(2,1)S(1)}, u32[]{:S(2)}, u32[]{:S(2)}) collective-permute-start(bf16[192,1024]{1,0:T(8,128)(2,1)S(1)} %fusion.4.q.qa), channel_id=1, source_target_pairs={{0,1},{1,0},{2,3},{3,2},{4,5},{5,4},{6,7},{7,6},{8,9},{9,8},{10,11... | collective-permute-start | bytes 1179656 | tf_op jit(solution)/shard_map/ppermute | solution.py:410
  68.2 18.4 %collective-permute-start.13 = (bf16[480,768]{1,0:T(8,128)(2,1)}, bf16[480,768]{1,0:T(8,128)(2,1)S(1)}, u32[]{:S(2)}, u32[]{:S(2)}) collective-permute-start(bf16[480,768]{1,0:T(8,128)(2,1)} %get-tuple-element.117.refs_12_), channel_id=1, source_target_pairs={{0,2},{2,0},{4,6},{6,4},{1,3},{3,1},{5,7},{7,5},{8,10},{10,8},{12,... | collective-permute-start | bytes 2211848 | tf_op jit(solution)/shard_map/ppermute | solution.py:420
  69.3 17.5 %collective-permute-start.14 = (bf16[480,768]{1,0:T(8,128)(2,1)}, bf16[480,768]{1,0:T(8,128)(2,1)S(1)}, u32[]{:S(2)}, u32[]{:S(2)}) collective-permute-start(bf16[480,768]{1,0:T(8,128)(2,1)} %get-tuple-element.117.refs_12_), channel_id=1, source_target_pairs={{0,4},{2,6},{4,0},{6,2},{1,5},{3,7},{5,1},{7,3},{8,12},{10,14},{12... | collective-permute-start | bytes 2211848 | tf_op jit(solution)/shard_map/ppermute | solution.py:420
  79.3 43.2 %collective-permute-start.21 = (bf16[384,768]{1,0:T(8,128)(2,1)}, bf16[384,768]{1,0:T(8,128)(2,1)S(1)}, u32[]{:S(2)}, u32[]{:S(2)}) collective-permute-start(bf16[384,768]{1,0:T(8,128)(2,1)} %collective-permute-done.8.refs_6_), channel_id=1, source_target_pairs={{0,1},{1,0},{2,3},{3,2},{4,5},{5,4},{6,7},{7,6},{8,9},{9,8},{10,11... | collective-permute-start | bytes 1769480 | tf_op jit(solution)/shard_map/ppermute | solution.py:410
  91.8 33.1 %collective-permute-start.25 = (bf16[480,768]{1,0:T(8,128)(2,1)S(1)}, bf16[480,768]{1,0:T(8,128)(2,1)S(1)}, u32[]{:S(2)}, u32[]{:S(2)}) collective-permute-start(bf16[480,768]{1,0:T(8,128)(2,1)S(1)} %collective-permute-done.13.refs_14_), channel_id=1, source_target_pairs={{0,1},{1,0},{2,3},{3,2},{4,5},{5,4},{6,7},{7,6},{8,9},{9,8},{10,11... | collective-permute-start | bytes 2211848 | tf_op jit(solution)/shard_map/ppermute | solution.py:410
  91.9 18.7 %collective-permute-start.27 = (bf16[480,768]{1,0:T(8,128)(2,1)S(1)}, bf16[480,768]{1,0:T(8,128)(2,1)S(1)}, u32[]{:S(2)}, u32[]{:S(2)}) collective-permute-start(bf16[480,768]{1,0:T(8,128)(2,1)S(1)} %collective-permute-done.14.refs_16_), channel_id=1, source_target_pairs={{0,2},{2,0},{4,6},{6,4},{1,3},{3,1},{5,7},{7,5},{8,10},{10,8},{12,... | collective-permute-start | bytes 2211848 | tf_op jit(solution)/shard_map/ppermute | solution.py:420
  95.6 14.4 %collective-permute-start.23 = (bf16[384,768]{1,0:T(8,128)(2,1)}, bf16[384,768]{1,0:T(8,128)(2,1)S(1)}, u32[]{:S(2)}, u32[]{:S(2)}) collective-permute-start(bf16[384,768]{1,0:T(8,128)(2,1)} %collective-permute-done.8.refs_6_), channel_id=1, source_target_pairs={{0,4},{2,6},{4,0},{6,2},{1,5},{3,7},{5,1},{7,3},{8,12},{10,14},{12... | collective-permute-start | bytes 1769480 | tf_op jit(solution)/shard_map/ppermute | solution.py:420
  97.0 28.3 %collective-permute-start.26 = (bf16[480,768]{1,0:T(8,128)(2,1)S(1)}, bf16[480,768]{1,0:T(8,128)(2,1)S(1)}, u32[]{:S(2)}, u32[]{:S(2)}) collective-permute-start(bf16[480,768]{1,0:T(8,128)(2,1)S(1)} %collective-permute-done.14.refs_16_), channel_id=1, source_target_pairs={{0,1},{1,0},{2,3},{3,2},{4,5},{5,4},{6,7},{7,6},{8,9},{9,8},{10,11... | collective-permute-start | bytes 2211848 | tf_op jit(solution)/shard_map/ppermute | solution.py:410
  168.9 28.2 %collective-permute-start.34 = (bf16[4,384,768]{2,1,0:T(8,128)(2,1)}, bf16[4,384,768]{2,1,0:T(8,128)(2,1)}, u32[]{:S(2)}, u32[]{:S(2)}) collective-permute-start(bf16[4,384,768]{2,1,0:T(8,128)(2,1)} %get-tuple-element.162), channel_id=1, source_target_pairs={{0,1},{1,0},{2,3},{3,2},{4,5},{5,4},{6,7},{7,6},{8,9},{9,8},{10,11... | collective-permute-start | bytes 7077896 | tf_op jit(solution)/shard_map/ppermute | solution.py:410
  169.7 25.5 %collective-permute-start.33 = (bf16[128,768]{1,0:T(8,128)(2,1)}, bf16[128,768]{1,0:T(8,128)(2,1)}, u32[]{:S(2)}, u32[]{:S(2)}) collective-permute-start(bf16[128,768]{1,0:T(8,128)(2,1)} %get-tuple-element.286), channel_id=1, source_target_pairs={{0,16},{8,24},{16,0},{24,8},{1,17},{9,25},{17,1},{25,9},{2,18},{10... | collective-permute-start | bytes 589832 | tf_op jit(solution)/shard_map/ppermute | solution.py:417
  171.0 188.9 %all-reduce.2.cloned.1.call-start = ((), (), s32[]{:S(2)}) async-start(), calls=%async_computation.2 | async-start | bytes 1572864 | tf_op jit(solution)/shard_map/psum | solution.py:614
  171.0 25.0 %collective-permute-start.35 = (bf16[192,1024]{1,0:T(8,128)(2,1)S(1)}, bf16[192,1024]{1,0:T(8,128)(2,1)S(1)}, u32[]{:S(2)}, u32[]{:S(2)}) collective-permute-start(bf16[192,1024]{1,0:T(8,128)(2,1)S(1)} %constant_dynamic-update-slice_fusion.ga), channel_id=1, source_target_pairs={{0,8},{8,0},{16,24},{24,16},{1,9},{9,1},{17,25},{25,17},{2,10},{10... | collective-permute-start | bytes 1179656 | tf_op jit(solution)/shard_map/ppermute | solution.py:413
  195.2 25.9 %collective-permute-start.38 = (bf16[192,1024]{1,0:T(8,128)(2,1)S(1)}, bf16[192,1024]{1,0:T(8,128)(2,1)S(1)}, u32[]{:S(2)}, u32[]{:S(2)}) collective-permute-start(bf16[192,1024]{1,0:T(8,128)(2,1)S(1)} %get-tuple-element.169), channel_id=1, source_target_pairs={{0,1},{1,0},{2,3},{3,2},{4,5},{5,4},{6,7},{7,6},{8,9},{9,8},{10,11... | collective-permute-start | bytes 1179656 | tf_op jit(solution)/shard_map/ppermute | solution.py:410
  199.4 25.3 %collective-permute-start.40 = (bf16[2,192,768]{2,1,0:T(8,128)(2,1)S(1)}, bf16[2,192,768]{2,1,0:T(8,128)(2,1)S(1)}, u32[]{:S(2)}, u32[]{:S(2)}) collective-permute-start(bf16[2,192,768]{2,1,0:T(8,128)(2,1)S(1)} %stack.239), channel_id=1, source_target_pairs={{0,4},{2,6},{4,0},{6,2},{1,5},{3,7},{5,1},{7,3},{8,12},{10,14},{12... | collective-permute-start | bytes 1769480 | tf_op jit(solution)/shard_map/ppermute | solution.py:420
  199.7 24.9 %collective-permute-start.39 = (bf16[2,192,768]{2,1,0:T(8,128)(2,1)S(1)}, bf16[2,192,768]{2,1,0:T(8,128)(2,1)S(1)}, u32[]{:S(2)}, u32[]{:S(2)}) collective-permute-start(bf16[2,192,768]{2,1,0:T(8,128)(2,1)S(1)} %pad_maximum_fusion.6), channel_id=1, source_target_pairs={{0,2},{2,0},{4,6},{6,4},{1,3},{3,1},{5,7},{7,5},{8,10},{10,8},{12,... | collective-permute-start | bytes 1769480 | tf_op jit(solution)/shard_map/ppermute | solution.py:420
  221.0 16.4 %collective-permute-start.37 = (bf16[192,1024]{1,0:T(8,128)(2,1)S(1)}, bf16[192,1024]{1,0:T(8,128)(2,1)S(1)}, u32[]{:S(2)}, u32[]{:S(2)}) collective-permute-start(bf16[192,1024]{1,0:T(8,128)(2,1)S(1)} %get-tuple-element.167), channel_id=1, source_target_pairs={{0,1},{1,0},{2,3},{3,2},{4,5},{5,4},{6,7},{7,6},{8,9},{9,8},{10,11... | collective-permute-start | bytes 1179656 | tf_op jit(solution)/shard_map/ppermute | solution.py:410
  224.8 14.1 %collective-permute-start.42 = (bf16[192,768]{1,0:T(8,128)(2,1)S(1)}, bf16[192,768]{1,0:T(8,128)(2,1)S(1)}, u32[]{:S(2)}, u32[]{:S(2)}) collective-permute-start(bf16[192,768]{1,0:T(8,128)(2,1)S(1)} %get-tuple-element.231), channel_id=1, source_target_pairs={{0,2},{2,0},{4,6},{6,4},{1,3},{3,1},{5,7},{7,5},{8,10},{10,8},{12,... | collective-permute-start | bytes 884744 | tf_op jit(solution)/shard_map/ppermute | solution.py:420
  226.0 12.8 %collective-permute-start.41 = (bf16[192,768]{1,0:T(8,128)(2,1)S(1)}, bf16[192,768]{1,0:T(8,128)(2,1)S(1)}, u32[]{:S(2)}, u32[]{:S(2)}) collective-permute-start(bf16[192,768]{1,0:T(8,128)(2,1)S(1)} %get-tuple-element.232), channel_id=1, source_target_pairs={{0,4},{2,6},{4,0},{6,2},{1,5},{3,7},{5,1},{7,3},{8,12},{10,14},{12... | collective-permute-start | bytes 884744 | tf_op jit(solution)/shard_map/ppermute | solution.py:420
  236.1 20.8 %collective-permute-start.43 = (bf16[2,192,1024]{2,1,0:T(8,128)(2,1)S(1)}, bf16[2,192,1024]{2,1,0:T(8,128)(2,1)S(1)}, u32[]{:S(2)}, u32[]{:S(2)}) collective-permute-start(bf16[2,192,1024]{2,1,0:T(8,128)(2,1)S(1)} %key_backward.4), channel_id=1, source_target_pairs={{0,1},{1,0},{2,3},{3,2},{4,5},{5,4},{6,7},{7,6},{8,9},{9,8},{10,11... | collective-permute-start | bytes 2359304 | tf_op jit(solution)/shard_map/ppermute | solution.py:410
  237.6 13.5 %collective-permute-start.44 = (bf16[192,1024]{1,0:T(8,128)(2,1)S(1)}, bf16[192,1024]{1,0:T(8,128)(2,1)S(1)}, u32[]{:S(2)}, u32[]{:S(2)}) collective-permute-start(bf16[192,1024]{1,0:T(8,128)(2,1)S(1)} %add_convert_fusion.4), channel_id=1, source_target_pairs={{0,8},{8,0},{16,24},{24,16},{1,9},{9,1},{17,25},{25,17},{2,10},{10... | collective-permute-start | bytes 1179656 | tf_op jit(solution)/shard_map/ppermute | solution.py:413
  239.3 15.4 %collective-permute-start.45 = (bf16[192,768]{1,0:T(8,128)(2,1)S(1)}, bf16[192,768]{1,0:T(8,128)(2,1)S(1)}, u32[]{:S(2)}, u32[]{:S(2)}) collective-permute-start(bf16[192,768]{1,0:T(8,128)(2,1)S(1)} %get-tuple-element.277), channel_id=1, source_target_pairs={{0,8},{8,0},{16,24},{24,16},{1,9},{9,1},{17,25},{25,17},{2,10},{10... | collective-permute-start | bytes 884744 | tf_op jit(solution)/shard_map/ppermute | solution.py:413
  248.6 19.4 %collective-permute-start.55 = (bf16[3,384,192]{1,2,0:T(8,128)(2,1)S(1)}, bf16[3,384,192]{1,2,0:T(8,128)(2,1)S(1)}, u32[]{:S(2)}, u32[]{:S(2)}) collective-permute-start(bf16[3,384,192]{1,2,0:T(8,128)(2,1)S(1)} %copy-done.32), channel_id=1, source_target_pairs={{0,6},{2,4},{4,2},{6,0},{1,7},{3,5},{5,3},{7,1},{8,14},{10,12},{12... | collective-permute-start | bytes 1327112 | tf_op jit(solution)/shard_map/ppermute | solution.py:420
  249.9 21.4 %collective-permute-start.54 = (bf16[3,384,192]{1,2,0:T(8,128)(2,1)S(1)}, bf16[3,384,192]{1,2,0:T(8,128)(2,1)S(1)}, u32[]{:S(2)}, u32[]{:S(2)}) collective-permute-start(bf16[3,384,192]{1,2,0:T(8,128)(2,1)S(1)} %copy-done.32), channel_id=1, source_target_pairs={{0,4},{2,6},{4,0},{6,2},{1,5},{3,7},{5,1},{7,3},{8,12},{10,14},{12... | collective-permute-start | bytes 1327112 | tf_op jit(solution)/shard_map/ppermute | solution.py:420
  251.0 21.4 %collective-permute-start.53 = (bf16[3,384,192]{1,2,0:T(8,128)(2,1)S(1)}, bf16[3,384,192]{1,2,0:T(8,128)(2,1)S(1)}, u32[]{:S(2)}, u32[]{:S(2)}) collective-permute-start(bf16[3,384,192]{1,2,0:T(8,128)(2,1)S(1)} %copy-done.32), channel_id=1, source_target_pairs={{0,2},{2,0},{4,6},{6,4},{1,3},{3,1},{5,7},{7,5},{8,10},{10,8},{12,... | collective-permute-start | bytes 1327112 | tf_op jit(solution)/shard_map/ppermute | solution.py:420
  254.8 18.9 %collective-permute-start.47 = (bf16[192,768]{1,0:T(8,128)(2,1)S(1)}, bf16[192,768]{1,0:T(8,128)(2,1)S(1)}, u32[]{:S(2)}, u32[]{:S(2)}) collective-permute-start(bf16[192,768]{1,0:T(8,128)(2,1)S(1)} %fusion.21), channel_id=1, source_target_pairs={{0,16},{8,24},{16,0},{24,8},{1,17},{9,25},{17,1},{25,9},{2,18},{10... | collective-permute-start | bytes 884744 | tf_op jit(solution)/shard_map/ppermute | solution.py:417
  258.1 16.7 %collective-permute-start.46 = (bf16[192,1024]{1,0:T(8,128)(2,1)S(1)}, bf16[192,1024]{1,0:T(8,128)(2,1)}, u32[]{:S(2)}, u32[]{:S(2)}) collective-permute-start(bf16[192,1024]{1,0:T(8,128)(2,1)S(1)} %get-tuple-element.273), channel_id=1, source_target_pairs={{0,8},{8,0},{16,24},{24,16},{1,9},{9,1},{17,25},{25,17},{2,10},{10... | collective-permute-start | bytes 1179656 | tf_op jit(solution)/shard_map/ppermute | solution.py:413
  268.0 17.0 %collective-permute-start.48 = (bf16[2,192,1024]{2,1,0:T(8,128)(2,1)S(1)}, bf16[2,192,1024]{2,1,0:T(8,128)(2,1)S(1)}, u32[]{:S(2)}, u32[]{:S(2)}) collective-permute-start(bf16[2,192,1024]{2,1,0:T(8,128)(2,1)S(1)} %key_backward.6), channel_id=1, source_target_pairs={{0,1},{1,0},{2,3},{3,2},{4,5},{5,4},{6,7},{7,6},{8,9},{9,8},{10,11... | collective-permute-start | bytes 2359304 | tf_op jit(solution)/shard_map/ppermute | solution.py:410
  271.3 62.8 %collective-permute-start.62 = (bf16[2,128,768]{2,1,0:T(8,128)(2,1)S(1)}, bf16[2,128,768]{2,1,0:T(8,128)(2,1)}, u32[]{:S(2)}, u32[]{:S(2)}) collective-permute-start(bf16[2,128,768]{2,1,0:T(8,128)(2,1)S(1)} %pad_maximum_fusion.10), channel_id=1, source_target_pairs={{0,6},{2,4},{4,2},{6,0},{1,7},{3,5},{5,3},{7,1},{8,14},{10,12},{12... | collective-permute-start | bytes 1179656 | tf_op jit(solution)/shard_map/ppermute | solution.py:420
  272.4 12.6 %collective-permute-start.49 = (bf16[192,1024]{1,0:T(8,128)(2,1)}, bf16[192,1024]{1,0:T(8,128)(2,1)}, u32[]{:S(2)}, u32[]{:S(2)}) collective-permute-start(bf16[192,1024]{1,0:T(8,128)(2,1)} %get-tuple-element.191), channel_id=1, source_target_pairs={{0,8},{8,0},{16,24},{24,16},{1,9},{9,1},{17,25},{25,17},{2,10},{10... | collective-permute-start | bytes 1179656 | tf_op jit(solution)/shard_map/ppermute | solution.py:413
  274.5 24.1 %collective-permute-start.72 = (bf16[192,768]{1,0:T(8,128)(2,1)}, bf16[192,768]{1,0:T(8,128)(2,1)}, u32[]{:S(2)}, u32[]{:S(2)}) collective-permute-start(bf16[192,768]{1,0:T(8,128)(2,1)} %add_convert_fusion.7), channel_id=1, source_target_pairs={{0,8},{8,0},{16,24},{24,16},{1,9},{9,1},{17,25},{25,17},{2,10},{10... | collective-permute-start | bytes 884744 | tf_op jit(solution)/shard_map/ppermute | solution.py:413
  286.8 17.1 %collective-permute-start.50 = (bf16[3,192,256]{2,1,0:T(8,128)(2,1)S(1)}, bf16[3,192,256]{2,1,0:T(8,128)(2,1)S(1)}, u32[]{:S(2)}, u32[]{:S(2)}) collective-permute-start(bf16[3,192,256]{2,1,0:T(8,128)(2,1)S(1)} %get-tuple-element.264), channel_id=1, source_target_pairs={{0,2},{2,0},{4,6},{6,4},{1,3},{3,1},{5,7},{7,5},{8,10},{10,8},{12,... | collective-permute-start | bytes 884744 | tf_op jit(solution)/shard_map/ppermute | solution.py:420
  288.1 17.0 %collective-permute-start.51 = (bf16[3,192,256]{2,1,0:T(8,128)(2,1)S(1)}, bf16[3,192,256]{2,1,0:T(8,128)(2,1)S(1)}, u32[]{:S(2)}, u32[]{:S(2)}) collective-permute-start(bf16[3,192,256]{2,1,0:T(8,128)(2,1)S(1)} %get-tuple-element.263), channel_id=1, source_target_pairs={{0,4},{2,6},{4,0},{6,2},{1,5},{3,7},{5,1},{7,3},{8,12},{10,14},{12... | collective-permute-start | bytes 884744 | tf_op jit(solution)/shard_map/ppermute | solution.py:420
  288.4 17.1 %collective-permute-start.52 = (bf16[3,192,256]{2,1,0:T(8,128)(2,1)S(1)}, bf16[3,192,256]{2,1,0:T(8,128)(2,1)S(1)}, u32[]{:S(2)}, u32[]{:S(2)}) collective-permute-start(bf16[3,192,256]{2,1,0:T(8,128)(2,1)S(1)} %get-tuple-element.262), channel_id=1, source_target_pairs={{0,6},{2,4},{4,2},{6,0},{1,7},{3,5},{5,3},{7,1},{8,14},{10,12},{12... | collective-permute-start | bytes 884744 | tf_op jit(solution)/shard_map/ppermute | solution.py:420
  303.9 31.1 %collective-permute-start.61 = (bf16[2,128,768]{2,1,0:T(8,128)(2,1)S(1)}, bf16[2,128,768]{2,1,0:T(8,128)(2,1)}, u32[]{:S(2)}, u32[]{:S(2)}) collective-permute-start(bf16[2,128,768]{2,1,0:T(8,128)(2,1)S(1)} %pad_maximum_fusion.10), channel_id=1, source_target_pairs={{0,4},{2,6},{4,0},{6,2},{1,5},{3,7},{5,1},{7,3},{8,12},{10,14},{12... | collective-permute-start | bytes 1179656 | tf_op jit(solution)/shard_map/ppermute | solution.py:420
  306.4 28.9 %collective-permute-start.60 = (bf16[2,128,768]{2,1,0:T(8,128)(2,1)S(1)}, bf16[2,128,768]{2,1,0:T(8,128)(2,1)}, u32[]{:S(2)}, u32[]{:S(2)}) collective-permute-start(bf16[2,128,768]{2,1,0:T(8,128)(2,1)S(1)} %pad_maximum_fusion.10), channel_id=1, source_target_pairs={{0,2},{2,0},{4,6},{6,4},{1,3},{3,1},{5,7},{7,5},{8,10},{10,8},{12,... | collective-permute-start | bytes 1179656 | tf_op jit(solution)/shard_map/ppermute | solution.py:420
  310.8 20.7 %collective-permute-start.59 = (bf16[128,768]{1,0:T(8,128)(2,1)}, bf16[128,768]{1,0:T(8,128)(2,1)}, u32[]{:S(2)}, u32[]{:S(2)}) collective-permute-start(bf16[128,768]{1,0:T(8,128)(2,1)} %get-tuple-element.284), channel_id=1, source_target_pairs={{0,16},{8,24},{16,0},{24,8},{1,17},{9,25},{17,1},{25,9},{2,18},{10... | collective-permute-start | bytes 589832 | tf_op jit(solution)/shard_map/ppermute | solution.py:417
  313.9 23.0 %collective-permute-start.67 = (bf16[576,192]{0,1:T(8,128)(2,1)}, bf16[576,192]{0,1:T(8,128)(2,1)S(1)}, u32[]{:S(2)}, u32[]{:S(2)}) collective-permute-start(bf16[576,192]{0,1:T(8,128)(2,1)} %constant_dynamic-slice_fusion), channel_id=1, source_target_pairs={{0,8},{8,0},{16,24},{24,16},{1,9},{9,1},{17,25},{25,17},{2,10},{10... | collective-permute-start | bytes 663560 | tf_op jit(solution)/shard_map/ppermute | solution.py:413
  332.6 18.6 %collective-permute-start.65 = (bf16[2,128,768]{2,1,0:T(8,128)(2,1)S(1)}, bf16[2,128,768]{2,1,0:T(8,128)(2,1)S(1)}, u32[]{:S(2)}, u32[]{:S(2)}) collective-permute-start(bf16[2,128,768]{2,1,0:T(8,128)(2,1)S(1)} %get-tuple-element.282), channel_id=1, source_target_pairs={{0,6},{2,4},{4,2},{6,0},{1,7},{3,5},{5,3},{7,1},{8,14},{10,12},{12... | collective-permute-start | bytes 1179656 | tf_op jit(solution)/shard_map/ppermute | solution.py:420
  334.1 19.0 %collective-permute-start.64 = (bf16[2,128,768]{2,1,0:T(8,128)(2,1)S(1)}, bf16[2,128,768]{2,1,0:T(8,128)(2,1)S(1)}, u32[]{:S(2)}, u32[]{:S(2)}) collective-permute-start(bf16[2,128,768]{2,1,0:T(8,128)(2,1)S(1)} %get-tuple-element.282), channel_id=1, source_target_pairs={{0,4},{2,6},{4,0},{6,2},{1,5},{3,7},{5,1},{7,3},{8,12},{10,14},{12... | collective-permute-start | bytes 1179656 | tf_op jit(solution)/shard_map/ppermute | solution.py:420
  335.0 18.0 %collective-permute-start.63 = (bf16[2,128,768]{2,1,0:T(8,128)(2,1)S(1)}, bf16[2,128,768]{2,1,0:T(8,128)(2,1)S(1)}, u32[]{:S(2)}, u32[]{:S(2)}) collective-permute-start(bf16[2,128,768]{2,1,0:T(8,128)(2,1)S(1)} %get-tuple-element.282), channel_id=1, source_target_pairs={{0,2},{2,0},{4,6},{6,4},{1,3},{3,1},{5,7},{7,5},{8,10},{10,8},{12,... | collective-permute-start | bytes 1179656 | tf_op jit(solution)/shard_map/ppermute | solution.py:420
  337.1 13.9 %collective-permute-start.68 = (bf16[576,192]{0,1:T(8,128)(2,1)S(1)}, bf16[576,192]{0,1:T(8,128)(2,1)S(1)}, u32[]{:S(2)}, u32[]{:S(2)}) collective-permute-start(bf16[576,192]{0,1:T(8,128)(2,1)S(1)} %fusion.24), channel_id=1, source_target_pairs={{0,16},{8,24},{16,0},{24,8},{1,17},{9,25},{17,1},{25,9},{2,18},{10... | collective-permute-start | bytes 663560 | tf_op jit(solution)/shard_map/ppermute | solution.py:417
  (85 other events, 564.2 us)
Sparse Core Ops, SparseCore 0:
  171.1 73.6 reduce-scatter.1
  274.9 59.3 all-reduce.1

commit v5 on v4

--- a/solution.py
+++ b/solution.py
@@ -259,8 +259,8 @@
 
 def dense_kernel(core, x_in, grad_out, gain, bias, *refs):
     attn, ups, downs = refs[0:4], refs[4:12], refs[12:20]
-    layer_out, grad_first_out, normed_out, hidden, grad_pre, grad_ffn_out, grad_attn_out = refs[20:27]
-    estimates, small, slope = refs[27:31], refs[31], refs[32]
+    layer_out, first_out, normed_out, grad_second_out, slope, grad_down, small = refs[20:27]
+    hidden = refs[27]
     part = hidden.shape[2]
     blocks = range(8)
     heads = jnp.concatenate([core_rows(core, attn[b // 2], b % 2) for b in blocks], axis=0)
@@ -268,11 +268,11 @@
     attn_out = dot(heads, out_w, TN)
     resid = x_in[...].astype(f32)
     first = resid + attn_out
-    small[4:5, :] = column_sum(resid * resid)
-    small[5:6, :] = column_sum(attn_out * attn_out)
-    small[6:7, :] = column_sum(first * first)
-    small[7:8, :] = jnp.zeros_like(small[7:8, :])
-    unit_1, inv_1 = norm(first)
+    first_out[...] = first
+    small[0:1, :] = column_sum(resid * resid)
+    small[1:2, :] = column_sum(attn_out * attn_out)
+    small[2:3, :] = column_sum(first * first)
+    unit_1, _ = norm(first)
     normed = (unit_1 * gain[0:1, :] + bias[0:1, :]).astype(bf16)
     normed_out[...] = normed
     second = normed.astype(f32)
@@ -286,19 +286,34 @@
     unit_2, inv_2 = norm(second)
     layer_out[...] = (unit_2 * gain[1:2, :] + bias[1:2, :]).astype(layer_out.dtype)
     grad = grad_out[...]
-    small[1:2, :] = column_sum(grad * unit_2)
-    small[3:4, :] = column_sum(grad)
+    small[3:4, :] = column_sum(grad * unit_2)
+    small[4:5, :] = column_sum(grad)
+    small[5:8, :] = jnp.zeros_like(small[5:8, :])
     grad_second = norm_back(grad * gain[1:2, :], unit_2, inv_2)
+    grad_second_out[...] = grad_second
     grad_ffn = grad_second.astype(bf16)
-    grad_ffn_out[...] = grad_ffn
-    grad_normed = grad_second
+    for b in blocks:
+        owner = (core[1] ^ (b // 2)) * 2 + (core[0] if b % 2 == 0 else 1 - core[0])
+        grad_down[owner] = dot(hidden[b], grad_ffn, TN).astype(bf16)
+
+
+def dense_back_kernel(core, first, grad_second, slope, gain, *refs):
+    ups, downs = refs[0:8], refs[8:16]
+    grad_first_out, grad_attn_out, grad_pre = refs[16:19]
+    estimates, small = refs[19:23], refs[23]
+    part = grad_pre.shape[2]
+    blocks = range(8)
+    grad_normed = grad_second[...]
+    grad_ffn = grad_normed.astype(bf16)
     for b in blocks:
         rows = (dot(grad_ffn, downs[b][0:part, :], NT) * slope[b]).astype(bf16)
         grad_pre[b] = rows
         grad_normed = grad_normed + dot(rows, ups[b][...], NN)
-    small[0:1, :] = column_sum(grad_normed * unit_1)
-    small[2:3, :] = column_sum(grad_normed)
-    grad_first = norm_back(grad_normed * gain[0:1, :], unit_1, inv_1)
+    unit, inv = norm(first[...])
+    small[0:1, :] = column_sum(grad_normed * unit)
+    small[1:2, :] = column_sum(grad_normed)
+    small[2:8, :] = jnp.zeros_like(small[2:8, :])
+    grad_first = norm_back(grad_normed * gain[0:1, :], unit, inv)
     grad_first_out[...] = grad_first
     grad_attn = grad_first.astype(bf16)
     grad_attn_out[...] = grad_attn
@@ -310,65 +325,97 @@
         ).astype(bf16)
 
 
-def weight_grad_kernel(core, normed, hidden, grad_pre, grad_ffn, grad_attn, small, *refs):
-    attn, down_out, ups = refs[0:4], refs[4], refs[5:7]
-    part = hidden.shape[2]
-    sums = jnp.concatenate([small[...], jnp.zeros_like(small[...])], axis=0).astype(bf16)
+def weight_grad_kernel(core, normed, grad_pre, grad_attn, small_a, small_b, *refs):
+    attn, outs = refs[0:4], refs[4:6]
+    part = grad_pre.shape[2]
+    sums = jnp.concatenate([small_a[...], small_b[...]], axis=0).astype(bf16)
     for b in range(8):
-        owner = (core[1] ^ (b // 2)) * 2 + (core[0] if b % 2 == 0 else 1 - core[0])
+        out = outs[b % 2]
         heads = core_rows(core, attn[b // 2], b % 2)
         at = part + heads.shape[0]
-        down_out[owner, 0:part, :] = dot(hidden[b], grad_ffn[...], TN).astype(bf16)
-        down_out[owner, part:at, :] = dot(heads, grad_attn[...], NN).astype(bf16)
-        down_out[owner, at : at + 16, :] = sums
-        down_out[owner, at + 16 :, :] = jnp.zeros_like(sums)
-        ups[b % 2][b // 2] = dot(grad_pre[b], normed[...], TN).astype(bf16)
+        out[b // 2, 0:part, :] = dot(grad_pre[b], normed[...], TN).astype(bf16)
+        out[b // 2, part:at, :] = dot(heads, grad_attn[...], NN).astype(bf16)
+        out[b // 2, at : at + 16, :] = sums
+        out[b // 2, at + 16 :, :] = jnp.zeros_like(sums)
+
+
+def input_grad_kernel(core, grad_first, *refs):
+    blocks, near, far, out = refs[0:4], refs[4:8], refs[8:12], refs[12]
+    half = near[0].shape[1]
+    total = grad_first[...]
+    for which, halves in enumerate((near, far)):
+        at = core[0] if which == 0 else 1 - core[0]
+        at = pl.ds(pl.multiple_of(at * half, 16), half)
+        for j in range(4):
+            rows = jnp.concatenate([blocks[j][c, at, :] for c in range(3)], axis=0)
+            weights = jnp.concatenate([halves[j][c] for c in range(3)], axis=0)
+            total = total + dot(rows, weights, TN)
+    out[...] = total.astype(out.dtype)
 
 
 def vmem(count):
     return [pl.BlockSpec(memory_space=pltpu.VMEM)] * count
+
+
+def single(kernel, core, args, out_shape, micros, name, scratch=()):
+    return pl.pallas_call(
+        kernel,
+        in_specs=[pl.BlockSpec(memory_space=pltpu.SMEM)] + vmem(len(args)),
+        out_specs=vmem(len(out_shape)),
+        out_shape=out_shape,
+        scratch_shapes=scratch,
+        compiler_params=pltpu.CompilerParams(vmem_limit_bytes=56 << 20),
+        cost_estimate=pl.CostEstimate(
+            flops=int(micros * 1.1e9), bytes_accessed=1 << 20, transcendentals=0
+        ),
+        name=name,
+    )(core, *args)
+
+
+shape = jax.ShapeDtypeStruct
 
 
 def dense(core, x_in, grad_out, gain, bias, attn, ups, downs):
     rows, width = x_in.shape
     part = ups[0].shape[0]
-    shape = jax.ShapeDtypeStruct
     out_shape = [
         shape((rows, width), bf16),
         shape((rows, width), f32),
         shape((rows, width), bf16),
-        shape((8, rows, part), bf16),
-        shape((8, rows, part), bf16),
+        shape((rows, width), f32),
+        shape((8, rows, part), f32),
+        shape((8, part, width), bf16),
+        shape((8, width), f32),
+    ]
+    args = [x_in, grad_out, gain, bias, *attn, *ups, *downs]
+    scratch = [pltpu.VMEM((8, rows, part), bf16)]
+    return single(dense_kernel, core, args, out_shape, 14, "dense", scratch)
+
+
+def dense_back(core, first, grad_second, slope, gain, attn, ups, downs):
+    rows, width = first.shape
+    out_shape = [
+        shape((rows, width), f32),
         shape((rows, width), bf16),
-        shape((rows, width), bf16),
+        shape((8, rows, ups[0].shape[0]), bf16),
         *[shape(attn[0].shape, bf16)] * 4,
         shape((8, width), f32),
     ]
-    return pl.pallas_call(
-        dense_kernel,
-        in_specs=[pl.BlockSpec(memory_space=pltpu.SMEM)] + vmem(24),
-        out_specs=vmem(12),
-        out_shape=out_shape,
-        scratch_shapes=[pltpu.VMEM((8, rows, part), f32)],
-        compiler_params=pltpu.CompilerParams(vmem_limit_bytes=56 << 20),
-        cost_estimate=pl.CostEstimate(flops=18 * 10**9, bytes_accessed=1 << 20, transcendentals=0),
-        name="dense",
-    )(core, x_in, grad_out, gain, bias, *attn, *ups, *downs)
-
-
-def weight_grads(core, normed, hidden, grad_pre, grad_ffn, grad_attn, small, attn):
-    width, part = normed.shape[1], hidden.shape[2]
-    shapes = [jax.ShapeDtypeStruct((8, part + attn[0].shape[0] // 2 + 32, width), bf16)]
-    shapes += [jax.ShapeDtypeStruct((4, part, width), bf16)] * 2
-    return pl.pallas_call(
-        weight_grad_kernel,
-        in_specs=[pl.BlockSpec(memory_space=pltpu.SMEM)] + vmem(10),
-        out_specs=vmem(3),
-        out_shape=shapes,
-        compiler_params=pltpu.CompilerParams(vmem_limit_bytes=56 << 20),
-        cost_estimate=pl.CostEstimate(flops=9 * 10**9, bytes_accessed=1 << 20, transcendentals=0),
-        name="weight_grads",
-    )(core, normed, hidden, grad_pre, grad_ffn, grad_attn, small, *attn)
+    args = [first, grad_second, slope, gain, *ups, *downs]
+    return single(dense_back_kernel, core, args, out_shape, 8, "dense_back")
+
+
+def weight_grads(core, normed, grad_pre, grad_attn, small_a, small_b, attn):
+    width, part = normed.shape[1], grad_pre.shape[2]
+    out_shape = [shape((4, part + attn[0].shape[0] // 2 + 32, width), bf16)] * 2
+    args = [normed, grad_pre, grad_attn, small_a, small_b, *attn]
+    return single(weight_grad_kernel, core, args, out_shape, 6, "weight_grads")
+
+
+def input_grad(core, grad_first, blocks, near, far):
+    out_shape = [shape(grad_first.shape, bf16)]
+    args = [grad_first, *blocks, *near, *far]
+    return single(input_grad_kernel, core, args, out_shape, 3, "input_grad")[0]
 
 
 def after(x, *others):
@@ -479,7 +526,7 @@
     q_o = over_seq(q)
     q_z = over_place(after(q, kv_o))
 
-    up = after(up, tokens)
+    up = after(up, q)
     ups, downs = [up] + ups, [down] + downs
     up_x, up_y = over_head(up, 1), over_head(up, 2)
     tables = key_tables(after(signed, up, q), [kv, kv_o], None, f32)
@@ -489,7 +536,11 @@
     up_x, up_y = after(up_x, tables), after(up_y, tables)
     down = after(down, up_x, up_y)
     down_x, down_y = over_head(down, 1), over_head(down, 2)
-    tables = key_tables(after(signed, down), [kv_z], tables, f32)
+    qkv_cut = head_width // 2
+    w_qkv_t = w_qkv.transpose(0, 2, 1)
+    qkv_near = [lax.dynamic_slice_in_dim(w_qkv_t, s * qkv_cut, qkv_cut, 1)]
+    qkv_far = [lax.dynamic_slice_in_dim(w_qkv_t, (1 - s) * qkv_cut, qkv_cut, 1)]
+    tables = key_tables(after(signed, down, qkv_near[0], qkv_far[0]), [kv_z], tables, f32)
 
     up_xo, up_yo = over_seq(after(up_x, tables)), over_seq(after(up_y, tables))
     q_z = after(q_z, tables)
@@ -511,7 +562,7 @@
     e_o_moved = over_seq(e_o)
     e = query_estimates(signed, after(q, e_o), tables, f32)
     e_far = after(e_far, e)
-    up_d, down_d = after(up_d, e), after(down_d, e)
+    up_d, down_d = after(up_d, e_far), after(down_d, e_far)
     up_xo, up_yo = after(up_xo, e_zo), after(up_yo, e_zo)
     down_xo, down_yo = after(down_xo, e_zo), after(down_yo, e_zo)
     ups += [up_x, up_xo, up_y, up_yo, up_d, over_seq(up_d)]
@@ -530,18 +581,18 @@
         return [dense_rows[0]] + [over_group(dense_rows[k], groups - k) for k in range(1, groups)]
 
     core = jnp.stack([s, d]).astype(jnp.int32)
-    (layer_rows, grad_first, normed, hidden, grad_pre, grad_ffn, grad_attn, *rest) = dense(
+    layer_rows, first, normed, grad_second, slope, a_grads, small_a = dense(
         core, dense_in, grad_out, norm_gain, norm_bias, attn_parts, ups, downs
     )
-    est_parts, small = rest[:4], rest[4]
+    a_sum = lax.psum_scatter(a_grads, ("head", "seq"), scatter_dimension=0, tiled=True)[0]
+    (grad_first, grad_attn, grad_pre, *est_parts, small_b) = dense_back(
+        core, first, grad_second, slope, norm_gain, attn_parts, ups, downs
+    )
     grad = jnp.concatenate(
         [est_parts[0]] + [over_head(est_parts[j], j) for j in range(1, head_count)], axis=1
     )
-    a_grads, mine_b, other_b = weight_grads(
-        core, normed, hidden, grad_pre, grad_ffn, grad_attn, small, attn_parts
-    )
-
-    a_sum = lax.psum_scatter(a_grads, ("head", "seq"), scatter_dimension=0, tiled=True)[0]
+    mine_b, other_b = weight_grads(core, normed, grad_pre, grad_attn, small_a, small_b, attn_parts)
+
     grad_z = over_place(grad)
     grad_o = over_seq(grad)
     swap_b = over_seq(after(other_b, grad_o))
@@ -563,6 +614,7 @@
         signed, signed_t, bits, q_gated, grad_z, q_zo, grad_zo, tables, part, bf16, bf16
     )
 
+    a_sum = after(a_sum, dq_z)
     x_far, y_far = after(x_far, dq_z), after(y_far, dq_z)
     x_own = add(chip_b[0, :cut], x_far[0])
     y_own = add(chip_b[0, cut:], y_far[0])
@@ -572,8 +624,9 @@
     dq_zo = over_seq(dq_zo)
     dq_own = add(dq, after(dq_o, dq_z))
     dkv_zo = key_backward(
-        signed, signed_t, bits, after(kv_zo, dq_own, x_out, y_out), grad_tables, bf16
-    )
+        signed, signed_t, bits, after(kv_zo, dq_own, x_out, y_out, a_sum), grad_tables, bf16
+    )
+    a_sum = lax.psum(a_sum, "hash")
 
     dkv_zo_moved = over_seq(dkv_zo)
     dq_far = add(dq_z, after(dq_zo, dkv_zo)).astype(bf16)
@@ -603,15 +656,11 @@
     b_send = add(b_keep, *[after(x, dkv_o) for x in b_far]).astype(bf16)
     layer_moved = after(layer_moved, dkv_o)
     layer_moved = [layer_moved] + [over_head(layer_moved, j) for j in range(1, head_count)]
-    qkv_cut = width // 2
-    qkv_near = [lax.dynamic_slice_in_dim(w_qkv, s * qkv_cut, qkv_cut, 1)]
-    qkv_far = [lax.dynamic_slice_in_dim(w_qkv, (1 - s) * qkv_cut, qkv_cut, 1)]
     qkv_half = after(qkv_near[0], dkv_z)
     qkv_near += [after(over_head(qkv_half, j), dkv_o) for j in range(1, head_count)]
     dkv = key_backward(
         signed, signed_t, bits, after(kv, dk_far, b_send, a_sum), grad_tables, f32
     )
-    a_sum = lax.psum(a_sum, "hash")
     b_far = over_place(b_send)
 
     qkv_near[1:] = [after(x, dkv) for x in qkv_near[1:]]
@@ -622,16 +671,25 @@
     grad_qkv = jnp.stack([grad_q, grad_k.astype(bf16), grad_v.astype(bf16)])
     qkv_parts = to_dense(grad_qkv)
 
-    near, far = 0.0, 0.0
-    for j in range(head_count):
-        block = qkv_parts[j]
-        near = near + jnp.einsum("cel,cde->ld", block, qkv_near[j], preferred_element_type=f32)
-        far = far + jnp.einsum("cel,cde->ld", block, qkv_far[j], preferred_element_type=f32)
-    grad_in = grad_first + jnp.concatenate(
-        [jnp.where(s == 0, near, far), jnp.where(s == 0, far, near)], axis=1
-    )
-
-    grad_moved = jnp.stack(away(grad_in.astype(bf16)))
+    grad_in = input_grad(core, grad_first, qkv_parts, qkv_near, qkv_far)
+
+    def in_halves(index, mine, other):
+        first = jnp.where(index == 0, mine, other)
+        second = jnp.where(index == 0, other, mine)
+        return jnp.concatenate([first, second], axis=0)
+
+    def split(x, index):
+        half = x.shape[0] // 2
+        return [lax.dynamic_slice_in_dim(x, at * half, half, 0) for at in (index, 1 - index)]
+
+    w_grad = dot(grad_qkv.reshape(3 * head_width, n_tokens), tokens, NN).astype(bf16)
+    w_keep, w_send = split(w_grad, s)
+    w_keep, w_send = split(add(w_keep, over_seq(w_send)).astype(bf16), r)
+    grad_moved = away(grad_in)
+    w_keep = add(w_keep, over_place(w_send))
+    w_send = w_keep.astype(bf16)
+    grad_moved = after(jnp.stack(grad_moved), w_send)
+    w_keep = add(w_keep, *[over_group(w_send, k) for k in range(1, groups)]).astype(bf16)
     grad_moved = [grad_moved] + [over_head(grad_moved, j) for j in range(1, head_count)]
 
     def home(blocks):
@@ -653,40 +711,19 @@
     layer_out = home([after(x, grad_moved[0]) for x in layer_moved])
     grad_inputs = home(grad_moved).astype(f32)
 
-    def in_halves(index, mine, other):
-        first = jnp.where(index == 0, mine, other)
-        second = jnp.where(index == 0, other, mine)
-        return jnp.concatenate([first, second], axis=0)
-
-    def over_hash_sum(x):
-        half = x.shape[0] // 2
-        mine = lax.dynamic_slice_in_dim(x, r * half, half, 0)
-        total = add(mine, over_place(lax.dynamic_slice_in_dim(x, (1 - r) * half, half, 0)))
-        sent = total.astype(bf16)
-        total = add(total, *[over_group(sent, k) for k in range(1, groups)]).astype(bf16)
-        return in_halves(r, total, over_place(total))
-
-    b_sum = in_halves(r, b_send, after(b_far, dkv))
+    w_grad = in_halves(r, w_keep, over_place(w_keep))
+    w_grad = in_halves(s, w_grad, over_seq(w_grad)).reshape(3, head_width, width)
+    grad_w_qkv = w_grad.transpose(0, 2, 1).astype(f32)
+    grad_w_down = in_halves(s, a_sum, over_seq(a_sum)).astype(f32)
+    b_sum = in_halves(r, b_send, after(b_far, grad_moved[0]))
     b_other = over_seq(b_sum)
-    grad_w_up = in_halves(s, b_sum, b_other).T.astype(f32)
-
-    grad_w_qkv = jnp.einsum("ld,cel->cde", tokens, grad_qkv, preferred_element_type=f32)
-    grad_w_qkv = grad_w_qkv.reshape(3 * width, head_width).astype(bf16)
-    half = grad_w_qkv.shape[0] // 2
-    mine = lax.dynamic_slice_in_dim(grad_w_qkv, s * half, half, 0)
-    other = over_seq(lax.dynamic_slice_in_dim(grad_w_qkv, (1 - s) * half, half, 0))
-    total = over_hash_sum(add(mine, other).astype(bf16))
-    a_sum = after(a_sum, total)
-    grad_w_qkv = in_halves(s, total, over_seq(total)).reshape(3, width, head_width).astype(f32)
-
-    a_other = over_seq(a_sum)
     cut, out_cut = hidden_own // 2, (hidden_own + head_width) // 2
-    grad_w_down = in_halves(s, a_sum[:cut], a_other[:cut]).astype(f32)
-    grad_w_out = in_halves(s, a_sum[cut:out_cut], a_other[cut:out_cut]).astype(f32)
-    small = a_sum[out_cut : out_cut + 8].astype(f32)
+    grad_w_up = in_halves(s, b_sum[:cut], b_other[:cut]).T.astype(f32)
+    grad_w_out = in_halves(s, b_sum[cut:out_cut], b_other[cut:out_cut]).astype(f32)
+    small = b_sum[out_cut : out_cut + 16].astype(f32)
 
     count = piece * seqs * width * hash_count * 2
-    stream_rms = jnp.sqrt(jnp.sum(small[4:7], axis=1) / count)
+    stream_rms = jnp.sqrt(jnp.sum(small[0:3], axis=1) / count)
     share = width // head_count
     norm_grads = lax.dynamic_slice_in_dim(small, d * share, share, 1)
     return (
@@ -696,8 +733,8 @@
         grad_w_out,
         grad_w_up,
         grad_w_down,
-        norm_grads[0:2],
-        norm_grads[2:4],
+        jnp.stack([norm_grads[8], norm_grads[3]]),
+        jnp.stack([norm_grads[9], norm_grads[4]]),
         stream_rms,
     )
 

time: 378 us -> 405 us (1.071)
  waiting for transfers between devices: 77.5 us -> 91.5 us
  Pallas kernels: 135 us -> 146 us
  other arithmetic: 23.2 us -> 30.8 us
    ppermute x31, waiting for transfers between devices: 29.9 us -> 49 us  [over_head(): return lax.ppermute(x, 'head', [(h, h ^ j) for h in range(head_count)])]
    pallas_call x2 -> x4, Pallas kernels: 26.8 us -> 39.3 us  [single(): pl.pallas_call(kernel, in_specs=[pl.BlockSpec(memory_space=pltpu.SMEM)] +...]
    ppermute x5, waiting for transfers between devices: 23.7 us -> 15.5 us  [over_group(): return lax.ppermute(x, 'hash', moves)]
    unnamed x121 -> x137, local copies, waits for them, and re-layouts: 25.8 us -> 28 us
  transfers between devices with their start and end apart: 76 -> 76, of which waited for: 22 -> 25; matrix products, arithmetic and copies ran while one was open for 14% -> 14% of each run, Pallas kernels for 31% -> 29%
where the time goes in v5:
time: 405 us; the launch traced here: 402 us
  Pallas kernels  146 us (36%)
  waiting for transfers between devices  91.5 us (23%)
  starting transfers between devices  69.6 us (17%)
  local copies, waits for them, and re-layouts  44.8 us (11%)
  other arithmetic  30.8 us (8%)
  between operations  15.5 us (4%)
  matrix products  4.05 us (1%)
    ppermute x31, waiting for transfers between devices, over_head(): return lax.ppermute(x, 'head', [(h, h ^ j) for h in range(head_count)])  49 us
    pallas_call x2, Pallas kernels, query_backward(): call(partial(query_back_kernel, chunk=4), heads, 20, 'query_backward', sp...  39.8 us
    pallas_call x4, Pallas kernels, single(): pl.pallas_call(kernel, in_specs=[pl.BlockSpec(memory_space=pltpu.SMEM)] +...  39.3 us
    pallas_call x4, Pallas kernels, key_backward(): call(partial(key_back_kernel, chunk=4), heads, 9, 'key_backward', [whole(...  35.5 us
    ppermute x31, starting transfers between devices, over_head(): return lax.ppermute(x, 'head', [(h, h ^ j) for h in range(head_count)])  29.1 us
    unnamed x137, local copies, waits for them, and re-layouts  28 us
    ppermute x11, waiting for transfers between devices, over_place(): return lax.ppermute(x, 'hash', [(h, h ^ 1) for h in range(hash_count)])  25.6 us
    ppermute x26, starting transfers between devices, over_seq(): return lax.ppermute(x, 'seq', [(0, 1), (1, 0)])  24.6 us
  transfers between devices with their start and end apart: 76, of which 25 were waited for; matrix products, arithmetic and copies ran while one was open for 14% of the time, Pallas kernels for 29%

profile of v5, /device:TPU:1, one launch (start us, length us, event | category | flops | bytes accessed | tf_op | source)
XLA Modules:
  0.0 401.8 jit_solution(378204786004912839)
XLA Ops:
  7.3 4.5 %constant_dynamic-slice_fusion.10 = (bf16[1,128,1,768]{3,2,1,0:T(2,128)(2,1)}, bf16[1,128,1,768]{3,2,1,0:T(2,128)(2,1)S(1)}, bf16[1,128,1,768]{3,2,1,0:T(2,128)(...) fusion(bf16[1,512,2,768]{3,2,1,0:T(2,128)(2,1)} %param.11, s32[]{:T(128)S(6)} %select_n.281, ...), kind=kLoop, calls=%fused_computation.140 | loop fusion | bytes 1966104 | tf_op jit(solution)/shard_map/jit(dynamic_index_in_dim)/dynamic_slice | solution.py:470
  12.6 3.1 collective-permute-start
  16.3 2.6 collective-permute-start.1
  20.9 1.9 copy_bitcast_fusion.2
  36.0 2.3 collective-permute-done.2
  38.4 4.8 %collective-permute-done.3 = bf16[1,128,768]{2,1,0:T(8,128)(2,1)S(1)} collective-permute-done((bf16[1,128,768]{2,1,0:T(8,128)(2,1)}, bf16[1,128,768]{2,1,0:T(8,128)(2,1)S(1)}, u32[]{:S(2)}, u32[]{:S(2)}) %collective-permute-start.3) | collective-permute-done | bytes 196640 | tf_op jit(solution)/shard_map/ppermute | solution.py:467
  49.7 7.8 %key_tables.3.refs_2_ = f32[3,2048,64]{2,1,0:T(8,128)S(1)} custom-call(bf16[64,64]{1,0:T(8,128)(2,1)S(1)} %bitcast.176, bf16[384,1024]{1,0:T(8,128)(2,1)S(1)} %bitcast.171, bf16[384,1024]{1,0:T(8,128)(2,1)S(1)} %collective-permute-done.6.refs_1_.refs_3_.keys.vals, bf16[384,1024]{1,0:T(8,128)(2,1)S(1)} %bitcast.172, ...), custom_call_target="tpu_custom_call" | custom-call | flops 11000000512 | bytes 1048576 | tf_op jit(solution)/shard_map/key_tables/pallas_call | solution.py:179
  59.2 6.8 %collective-permute-done.10.refs_0_.refs_1_.keys.vals = bf16[384,1024]{1,0:T(8,128)(2,1)S(1)} collective-permute-done((bf16[384,1024]{1,0:T(8,128)(2,1)S(1)}, bf16[384,1024]{1,0:T(8,128)(2,1)S(1)}, u32[]{:S(2)}, u32[]{:S(2)}) %collective-permute-start.10) | collective-permute-done | bytes 786464 | tf_op jit(solution)/shard_map/ppermute | solution.py:460
  69.9 5.5 %key_tables.4.refs_2_ = f32[3,2048,64]{2,1,0:T(8,128)S(1)} custom-call(bf16[64,64]{1,0:T(8,128)(2,1)S(1)} %bitcast.177, bf16[384,1024]{1,0:T(8,128)(2,1)S(1)} %collective-permute-done.10.refs_0_.refs_1_.keys.vals, bf16[384,1024]{1,0:T(8,128)(2,1)S(1)} %collective-permute-done.10.refs_0_.refs_1_.keys.vals, f32[3,2048,64]{2,1,0:T(8,128)} %copy-done.11), custom_call_target="tpu_custom_call" | custom-call | flops 5500000256 | bytes 1048576 | tf_op jit(solution)/shard_map/key_tables/pallas_call | solution.py:179
  75.4 3.6 collective-permute-done.7.q.qa
  79.1 2.0 collective-permute-start.22
  81.1 4.2 %key_tables.5.tables = bf16[3,2048,64]{2,1,0:T(8,128)(2,1)S(1)} custom-call(bf16[64,64]{1,0:T(8,128)(2,1)S(1)} %bitcast.178, bf16[384,1024]{1,0:T(8,128)(2,1)S(1)} %collective-permute-done.12.refs_0_.refs_1_.keys.vals, bf16[384,1024]{1,0:T(8,128)(2,1)S(1)} %collective-permute-done.12.refs_0_.refs_1_.keys.vals, f32[3,2048,64]{2,1,0:T(8,128)S(1)} %key_tables.4.refs_2_), custom_call_target="tpu_custom_call" | custom-call | flops 5500000256 | bytes 1048576 | tf_op jit(solution)/shard_map/key_tables/pallas_call | solution.py:179
  86.5 3.3 query_estimates.4
  92.1 3.3 query_estimates.5
  97.1 3.3 query_estimates.6
  100.4 9.2 %collective-permute-done.27.refs_18_.refs_14_ = bf16[480,768]{1,0:T(8,128)(2,1)S(1)} collective-permute-done((bf16[480,768]{1,0:T(8,128)(2,1)S(1)}, bf16[480,768]{1,0:T(8,128)(2,1)S(1)}, u32[]{:S(2)}, u32[]{:S(2)}) %collective-permute-start.27) | collective-permute-done | bytes 737312 | tf_op jit(solution)/shard_map/ppermute | solution.py:467
  110.5 3.5 query_estimates.7
  124.0 15.2 %dense.1 = (bf16[256,768]{1,0:T(8,128)(2,1)}, f32[256,768]{1,0:T(8,128)}, bf16[256,768]{1,0:T(8,128)(2,1)}, f32[256,768]{1,0:T(8,128)}, f32[8,256,384]{2,1,0:T(8...) custom-call(s32[2]{0:T(128)} %pad_add_fusion.core, bf16[256,768]{1,0:T(8,128)(2,1)} %bitcast.213, ...), custom_call_target="tpu_custom_call" | custom-call | flops 15399999488 | bytes 1048576 | tf_op jit(solution)/shard_map/dense/pallas_call | solution.py:361
  139.2 12.2 %dense_back.1 = (f32[256,768]{1,0:T(8,128)}, bf16[256,768]{1,0:T(8,128)(2,1)}, bf16[8,256,384]{2,1,0:T(8,128)(2,1)}, bf16[192,256]{1,0:T(8,128)(2,1)}, bf16[192,...) custom-call(s32[2]{0:T(128)} %pad_add_fusion.core, ...), custom_call_target="tpu_custom_call" | custom-call | flops 8800000000 | bytes 1048576 | tf_op jit(solution)/shard_map/dense_back/pallas_call | solution.py:361
  156.3 2.1 collective-permute-done.31
  158.4 3.1 collective-permute-start.32
  161.5 6.8 %weight_grads.1 = (bf16[4,512,768]{2,1,0:T(8,128)(2,1)}, bf16[4,512,768]{2,1,0:T(8,128)(2,1)}) custom-call(s32[2]{0:T(128)} %pad_add_fusion.core, bf16[256,768]{1,0:T(8,128)(2,1)} %get-tuple-element.156.normed, bf16[8,256,384]{2,1,0:T(8,128)(2,1)} %get-tuple-element.157.grad_pre, bf16[256,768]{1,0:T(8,128)(2,1)} %get-tuple-element.158.grad_attn, ...), custom_call_target="tpu_custom_call" | custom-call | flops 6600000000 | bytes 1048576 | tf_op jit(solution)/shard_map/weight_grads/pallas_call | solution.py:361
  175.0 19.6 %query_backward.2 = (f32[3,2048,64]{2,1,0:T(8,128)}, f32[192,1024]{1,0:T(8,128)S(1)}, bf16[192,1024]{1,0:T(8,128)(2,1)S(1)}) custom-call(bf16[64,64]{1,0:T(8,128)(2,1)S(1)} %bitcast.183, bf16[64,128]{1,0:T(8,128)(2,1)S(1)} %pad_maximum_fusion.13.planes_t, bf16[80,2048]{1,0:T(8,128)(2,1)S(1)} %copy-done.10, bf16[192,1024]{1,0:T(8,128)(2,1)S(1)} %fusion.3.q.qa, ...), custom_call_target="tpu_custom_call" | custom-call | flops 22000001024 | bytes 1048576 | tf_op jit(solution)/shard_map/query_backward/pallas_call | solution.py:210
  196.5 2.7 add_convert_fusion
  200.4 20.2 %query_backward.3 = (bf16[3,2048,64]{2,1,0:T(8,128)(2,1)S(1)}, bf16[192,1024]{1,0:T(8,128)(2,1)S(1)}, bf16[192,1024]{1,0:T(8,128)(2,1)S(1)}) custom-call(bf16[64,64]{1,0:T(8,128)(2,1)S(1)} %bitcast.184, bf16[64,128]{1,0:T(8,128)(2,1)S(1)} %pad_maximum_fusion.13.planes_t, bf16[80,2048]{1,0:T(8,128)(2,1)S(1)} %copy-done.10, ...), custom_call_target="tpu_custom_call" | custom-call | flops 22000001024 | bytes 1048576 | tf_op jit(solution)/shard_map/query_backward/pallas_call | solution.py:210
  222.7 1.9 collective-permute-done.39
  230.0 8.8 %key_backward.4 = bf16[2,192,1024]{2,1,0:T(8,128)(2,1)S(1)} custom-call(bf16[64,64]{1,0:T(8,128)(2,1)S(1)} %bitcast.185, bf16[64,128]{1,0:T(8,128)(2,1)S(1)} %pad_maximum_fusion.13.planes_t, bf16[80,2048]{1,0:T(8,128)(2,1)S(1)} %copy-done.10, bf16[384,1024]{1,0:T(8,128)(2,1)S(1)} %copy-done.5, bf16[384,1024]{1,0:T(8,128)(2,1)S(1)} %copy-done.5, ...), custom_call_target="tpu_custom_call" | custom-call | flops 9900000256 | bytes 1048576 | tf_op jit(solution)/shard_map/key_backward/pallas_call | solution.py:224
  238.8 2.2 collective-permute-start.43
  245.7 9.0 %key_backward.5 = bf16[2,192,1024]{2,1,0:T(8,128)(2,1)S(1)} custom-call(bf16[64,64]{1,0:T(8,128)(2,1)S(1)} %bitcast.186, bf16[64,128]{1,0:T(8,128)(2,1)S(1)} %pad_maximum_fusion.13.planes_t, bf16[80,2048]{1,0:T(8,128)(2,1)S(1)} %copy-done.10, bf16[384,1024]{1,0:T(8,128)(2,1)S(1)} %collective-permute-done.10.refs_0_.refs_1_.keys.vals, ...), custom_call_target="tpu_custom_call" | custom-call | flops 9900000256 | bytes 1048576 | tf_op jit(solution)/shard_map/key_backward/pallas_call | solution.py:224
  257.4 14.8 %collective-permute-done.44 = bf16[192,1024]{1,0:T(8,128)(2,1)S(1)} collective-permute-done((bf16[192,1024]{1,0:T(8,128)(2,1)S(1)}, bf16[192,1024]{1,0:T(8,128)(2,1)S(1)}, u32[]{:S(2)}, u32[]{:S(2)}) %collective-permute-start.44) | collective-permute-done | bytes 393248 | tf_op jit(solution)/shard_map/ppermute | solution.py:460
  274.6 2.7 collective-permute-start.46
  277.3 8.7 %key_backward.6 = bf16[2,192,1024]{2,1,0:T(8,128)(2,1)S(1)} custom-call(bf16[64,64]{1,0:T(8,128)(2,1)S(1)} %bitcast.187, bf16[64,128]{1,0:T(8,128)(2,1)S(1)} %pad_maximum_fusion.13.planes_t, bf16[80,2048]{1,0:T(8,128)(2,1)S(1)} %copy-done.10, bf16[384,1024]{1,0:T(8,128)(2,1)S(1)} %collective-permute-done.6.refs_1_.refs_3_.keys.vals, ...), custom_call_target="tpu_custom_call" | custom-call | flops 9900000256 | bytes 1048576 | tf_op jit(solution)/shard_map/key_backward/pallas_call | solution.py:224
  286.1 6.9 %collective-permute-done.47 = bf16[256,768]{1,0:T(8,128)(2,1)} collective-permute-done((bf16[256,768]{1,0:T(8,128)(2,1)}, bf16[256,768]{1,0:T(8,128)(2,1)}, u32[]{:S(2)}, u32[]{:S(2)}) %collective-permute-start.47) | collective-permute-done | bytes 393248 | tf_op jit(solution)/shard_map/ppermute | solution.py:464
  294.3 2.0 add_convert_fusion.3
  297.8 9.1 %key_backward.7 = f32[2,192,1024]{2,1,0:T(8,128)S(1)} custom-call(bf16[64,64]{1,0:T(8,128)(2,1)S(1)} %bitcast.188, bf16[64,128]{1,0:T(8,128)(2,1)S(1)} %pad_maximum_fusion.13.planes_t, bf16[80,2048]{1,0:T(8,128)(2,1)S(1)} %copy-done.10, bf16[384,1024]{1,0:T(8,128)(2,1)S(1)} %bitcast.173, bf16[384,1024]{1,0:T(8,128)(2,1)S(1)} %bitcast.174, ...), custom_call_target="tpu_custom_call" | custom-call | flops 9900000256 | bytes 1048576 | tf_op jit(solution)/shard_map/key_backward/pallas_call | solution.py:224
  314.7 4.6 %collective-permute-done.50.refs_1_ = bf16[3,192,256]{2,1,0:T(8,128)(2,1)} collective-permute-done((bf16[3,192,256]{2,1,0:T(8,128)(2,1)}, bf16[3,192,256]{2,1,0:T(8,128)(2,1)}, u32[]{:S(2)}, u32[]{:S(2)}) %collective-permute-start.50) | collective-permute-done | bytes 294944 | tf_op jit(solution)/shard_map/ppermute | solution.py:467
  319.2 1.8 collective-permute-start.52
  323.0 5.1 %collective-permute-done.52.refs_3_ = bf16[3,192,256]{2,1,0:T(8,128)(2,1)} collective-permute-done((bf16[3,192,256]{2,1,0:T(8,128)(2,1)S(1)}, bf16[3,192,256]{2,1,0:T(8,128)(2,1)}, u32[]{:S(2)}, u32[]{:S(2)}) %collective-permute-start.52) | collective-permute-done | bytes 294944 | tf_op jit(solution)/shard_map/ppermute | solution.py:467
  328.4 2.3 collective-permute-start.63
  333.2 5.1 %input_grad.1 = bf16[256,768]{1,0:T(8,128)(2,1)} custom-call(s32[2]{0:T(128)} %pad_add_fusion.core, f32[256,768]{1,0:T(8,128)} %get-tuple-element.191.grad_first, bf16[3,192,256]{2,1,0:T(8,128)(2,1)} %get-tuple-element.271.refs_0_, bf16[3,192,256]{2,1,0:T(8,128)(2,1)} %collective-permute-done.50.refs_1_, bf16[3,192,256]{2,1,0:T(8,128)(2,1)} %copy-done.59, ...), custom_call_target="tpu_custom_call" | custom-call | flops 3300000000 | bytes 1048576 | tf_op jit(solution)/shard_map/input_grad/pallas_call | solution.py:361
  342.6 8.6 %collective-permute-done.59 = bf16[128,768]{1,0:T(8,128)(2,1)S(1)} collective-permute-done((bf16[128,768]{1,0:T(8,128)(2,1)S(1)}, bf16[128,768]{1,0:T(8,128)(2,1)S(1)}, u32[]{:S(2)}, u32[]{:S(2)}) %collective-permute-start.59) | collective-permute-done | bytes 196640 | tf_op jit(solution)/shard_map/ppermute | solution.py:464
  356.6 5.3 %collective-permute-done.64 = bf16[2,128,768]{2,1,0:T(8,128)(2,1)S(1)} collective-permute-done((bf16[2,128,768]{2,1,0:T(8,128)(2,1)S(1)}, bf16[2,128,768]{2,1,0:T(8,128)(2,1)S(1)}, u32[]{:S(2)}, u32[]{:S(2)}) %collective-permute-start.64) | collective-permute-done | bytes 393248 | tf_op jit(solution)/shard_map/ppermute | solution.py:467
  361.9 3.1 collective-permute-start.72
  366.2 2.8 copy.46
  370.4 2.3 collective-permute-done.66
  372.7 6.0 %collective-permute-done.67 = bf16[2,128,768]{2,1,0:T(8,128)(2,1)S(1)} collective-permute-done((bf16[2,128,768]{2,1,0:T(8,128)(2,1)S(1)}, bf16[2,128,768]{2,1,0:T(8,128)(2,1)S(1)}, u32[]{:S(2)}, u32[]{:S(2)}) %collective-permute-start.67) | collective-permute-done | bytes 393248 | tf_op jit(solution)/shard_map/ppermute | solution.py:467
  379.5 4.1 %copy.47 = f32[1,512,2,768]{3,2,1,0:T(2,128)} copy(f32[1,512,2,768]{3,1,2,0:T(8,128)S(1)} %maximum_convert_fusion) | data formatting | bytes 6291456
  387.3 2.0 copy.48
  (346 shorter events, 113.4 us)
Async XLA Ops:
  7.2 220.3 %reduce-scatter.2.cloned.1.call-start = ((), (), s32[]{:S(2)}) async-start(), calls=%async_computation.1 | async-start | bytes 5308416 | tf_op jit(solution)/shard_map/reduce_scatter | solution.py:587
  12.6 18.8 %collective-permute-start = (bf16[128,768]{1,0:T(8,128)(2,1)}, bf16[128,768]{1,0:T(8,128)(2,1)}, u32[]{:S(2)}, u32[]{:S(2)}) collective-permute-start(bf16[128,768]{1,0:T(8,128)(2,1)} %bitcast.168), channel_id=1, source_target_pairs={{0,16},{8,24},{16,0},{24,8},{1,17},{9,25},{17,1},{25,9},{2,18},{10... | collective-permute-start | bytes 589832 | tf_op jit(solution)/shard_map/ppermute | solution.py:464
  16.3 14.9 %collective-permute-start.1 = (bf16[8,8,64]{2,0,1:T(8,128)(2,1)}, bf16[8,8,64]{2,0,1:T(8,128)(2,1)S(1)}, u32[]{:S(2)}, u32[]{:S(2)}) collective-permute-start(bf16[8,8,64]{2,0,1:T(8,128)(2,1)} %fusion.31), channel_id=1, source_target_pairs={{0,0},{8,1},{16,8},{24,9},{1,16},{9,17},{17,24},{25,25},{2,2},{10,... | collective-permute-start | bytes 24584 | tf_op jit(solution)/shard_map/ppermute | solution.py:483
  46.9 19.1 %collective-permute-start.10 = (bf16[384,1024]{1,0:T(8,128)(2,1)S(1)}, bf16[384,1024]{1,0:T(8,128)(2,1)S(1)}, u32[]{:S(2)}, u32[]{:S(2)}) collective-permute-start(bf16[384,1024]{1,0:T(8,128)(2,1)S(1)} %bitcast.170), channel_id=1, source_target_pairs={{0,8},{8,0},{16,24},{24,16},{1,9},{9,1},{17,25},{25,17},{2,10},{10... | collective-permute-start | bytes 2359304 | tf_op jit(solution)/shard_map/ppermute | solution.py:460
  48.2 19.7 %collective-permute-start.9 = (bf16[384,768]{1,0:T(8,128)(2,1)S(1)}, bf16[384,768]{1,0:T(8,128)(2,1)S(1)}, u32[]{:S(2)}, u32[]{:S(2)}) collective-permute-start(bf16[384,768]{1,0:T(8,128)(2,1)S(1)} %bitcast.204), channel_id=1, source_target_pairs={{0,4},{2,6},{4,0},{6,2},{1,5},{3,7},{5,1},{7,3},{8,12},{10,14},{12... | collective-permute-start | bytes 1769480 | tf_op jit(solution)/shard_map/ppermute | solution.py:467
  49.5 18.4 %collective-permute-start.8 = (bf16[384,768]{1,0:T(8,128)(2,1)S(1)}, bf16[384,768]{1,0:T(8,128)(2,1)S(1)}, u32[]{:S(2)}, u32[]{:S(2)}) collective-permute-start(bf16[384,768]{1,0:T(8,128)(2,1)S(1)} %bitcast.205), channel_id=1, source_target_pairs={{0,2},{2,0},{4,6},{6,4},{1,3},{3,1},{5,7},{7,5},{8,10},{10,8},{12,... | collective-permute-start | bytes 1769480 | tf_op jit(solution)/shard_map/ppermute | solution.py:467
  66.1 15.0 %collective-permute-start.12 = (bf16[384,1024]{1,0:T(8,128)(2,1)S(1)}, bf16[384,1024]{1,0:T(8,128)(2,1)S(1)}, u32[]{:S(2)}, u32[]{:S(2)}) collective-permute-start(bf16[384,1024]{1,0:T(8,128)(2,1)S(1)} %collective-permute-done.10.refs_0_.refs_1_.keys.vals), channel_id=1, source_target_pairs={{0,1},{1,0},{2,3},{3,2},{4,5},{5,4},{6,7},{7,6},{8,9},{9,8},{10,11... | collective-permute-start | bytes 2359304 | tf_op jit(solution)/shard_map/ppermute | solution.py:457
  67.9 28.7 %collective-permute-start.5 = (bf16[192,1024]{1,0:T(8,128)(2,1)S(1)}, bf16[192,1024]{1,0:T(8,128)(2,1)S(1)}, u32[]{:S(2)}, u32[]{:S(2)}) collective-permute-start(bf16[192,1024]{1,0:T(8,128)(2,1)S(1)} %fusion.3.q.qa), channel_id=1, source_target_pairs={{0,1},{1,0},{2,3},{3,2},{4,5},{5,4},{6,7},{7,6},{8,9},{9,8},{10,11... | collective-permute-start | bytes 1179656 | tf_op jit(solution)/shard_map/ppermute | solution.py:457
  67.9 17.6 %collective-permute-start.14 = (bf16[480,768]{1,0:T(8,128)(2,1)S(1)}, bf16[480,768]{1,0:T(8,128)(2,1)S(1)}, u32[]{:S(2)}, u32[]{:S(2)}) collective-permute-start(bf16[480,768]{1,0:T(8,128)(2,1)S(1)} %copy-done.36), channel_id=1, source_target_pairs={{0,4},{2,6},{4,0},{6,2},{1,5},{3,7},{5,1},{7,3},{8,12},{10,14},{12... | collective-permute-start | bytes 2211848 | tf_op jit(solution)/shard_map/ppermute | solution.py:467
  69.2 17.2 %collective-permute-start.13 = (bf16[480,768]{1,0:T(8,128)(2,1)S(1)}, bf16[480,768]{1,0:T(8,128)(2,1)S(1)}, u32[]{:S(2)}, u32[]{:S(2)}) collective-permute-start(bf16[480,768]{1,0:T(8,128)(2,1)S(1)} %copy-done.36), channel_id=1, source_target_pairs={{0,2},{2,0},{4,6},{6,4},{1,3},{3,1},{5,7},{7,5},{8,10},{10,8},{12,... | collective-permute-start | bytes 2211848 | tf_op jit(solution)/shard_map/ppermute | solution.py:467
  79.1 35.6 %collective-permute-start.22 = (bf16[384,768]{1,0:T(8,128)(2,1)S(1)}, bf16[384,768]{1,0:T(8,128)(2,1)S(1)}, u32[]{:S(2)}, u32[]{:S(2)}) collective-permute-start(bf16[384,768]{1,0:T(8,128)(2,1)S(1)} %collective-permute-done.9.refs_8_.refs_4_), channel_id=1, source_target_pairs={{0,1},{1,0},{2,3},{3,2},{4,5},{5,4},{6,7},{7,6},{8,9},{9,8},{10,11... | collective-permute-start | bytes 1769480 | tf_op jit(solution)/shard_map/ppermute | solution.py:457
  91.5 18.1 %collective-permute-start.27 = (bf16[480,768]{1,0:T(8,128)(2,1)S(1)}, bf16[480,768]{1,0:T(8,128)(2,1)S(1)}, u32[]{:S(2)}, u32[]{:S(2)}) collective-permute-start(bf16[480,768]{1,0:T(8,128)(2,1)S(1)} %collective-permute-done.14.refs_16_.refs_12_), channel_id=1, source_target_pairs={{0,2},{2,0},{4,6},{6,4},{1,3},{3,1},{5,7},{7,5},{8,10},{10,8},{12,... | collective-permute-start | bytes 2211848 | tf_op jit(solution)/shard_map/ppermute | solution.py:467
  91.8 25.7 %collective-permute-start.26 = (bf16[480,768]{1,0:T(8,128)(2,1)S(1)}, bf16[480,768]{1,0:T(8,128)(2,1)S(1)}, u32[]{:S(2)}, u32[]{:S(2)}) collective-permute-start(bf16[480,768]{1,0:T(8,128)(2,1)S(1)} %collective-permute-done.14.refs_16_.refs_12_), channel_id=1, source_target_pairs={{0,1},{1,0},{2,3},{3,2},{4,5},{5,4},{6,7},{7,6},{8,9},{9,8},{10,11... | collective-permute-start | bytes 2211848 | tf_op jit(solution)/shard_map/ppermute | solution.py:457
  95.4 18.6 %collective-permute-start.23 = (bf16[384,768]{1,0:T(8,128)(2,1)S(1)}, bf16[384,768]{1,0:T(8,128)(2,1)S(1)}, u32[]{:S(2)}, u32[]{:S(2)}) collective-permute-start(bf16[384,768]{1,0:T(8,128)(2,1)S(1)} %collective-permute-done.8.refs_6_.refs_2_), channel_id=1, source_target_pairs={{0,4},{2,6},{4,0},{6,2},{1,5},{3,7},{5,1},{7,3},{8,12},{10,14},{12... | collective-permute-start | bytes 1769480 | tf_op jit(solution)/shard_map/ppermute | solution.py:467
  96.6 13.8 %collective-permute-start.17 = (bf16[192,1024]{1,0:T(8,128)(2,1)S(1)}, bf16[192,1024]{1,0:T(8,128)(2,1)S(1)}, u32[]{:S(2)}, u32[]{:S(2)}) collective-permute-start(bf16[192,1024]{1,0:T(8,128)(2,1)S(1)} %add_convert_fusion.9), channel_id=1, source_target_pairs={{0,8},{8,0},{16,24},{24,16},{1,9},{9,1},{17,25},{25,17},{2,10},{10... | collective-permute-start | bytes 1179656 | tf_op jit(solution)/shard_map/ppermute | solution.py:460
  154.3 131.8 %all-reduce.2.cloned.1.call-start = ((), (), s32[]{:S(2)}) async-start(), calls=%async_computation.2 | async-start | bytes 1179648 | tf_op jit(solution)/shard_map/psum | solution.py:629
  169.0 27.5 %collective-permute-start.34 = (bf16[4,512,768]{2,1,0:T(8,128)(2,1)}, bf16[4,512,768]{2,1,0:T(8,128)(2,1)}, u32[]{:S(2)}, u32[]{:S(2)}) collective-permute-start(bf16[4,512,768]{2,1,0:T(8,128)(2,1)} %get-tuple-element.167), channel_id=1, source_target_pairs={{0,1},{1,0},{2,3},{3,2},{4,5},{5,4},{6,7},{7,6},{8,9},{9,8},{10,11... | collective-permute-start | bytes 9437192 | tf_op jit(solution)/shard_map/ppermute | solution.py:457
  170.1 25.5 %collective-permute-start.33 = (bf16[128,768]{1,0:T(8,128)(2,1)S(1)}, bf16[128,768]{1,0:T(8,128)(2,1)S(1)}, u32[]{:S(2)}, u32[]{:S(2)}) collective-permute-start(bf16[128,768]{1,0:T(8,128)(2,1)S(1)} %get-tuple-element.291), channel_id=1, source_target_pairs={{0,16},{8,24},{16,0},{24,8},{1,17},{9,25},{17,1},{25,9},{2,18},{10... | collective-permute-start | bytes 589832 | tf_op jit(solution)/shard_map/ppermute | solution.py:464
  171.4 23.2 %collective-permute-start.35 = (bf16[192,1024]{1,0:T(8,128)(2,1)S(1)}, bf16[192,1024]{1,0:T(8,128)(2,1)S(1)}, u32[]{:S(2)}, u32[]{:S(2)}) collective-permute-start(bf16[192,1024]{1,0:T(8,128)(2,1)S(1)} %constant_dynamic-update-slice_fusion.ga), channel_id=1, source_target_pairs={{0,8},{8,0},{16,24},{24,16},{1,9},{9,1},{17,25},{25,17},{2,10},{10... | collective-permute-start | bytes 1179656 | tf_op jit(solution)/shard_map/ppermute | solution.py:460
  195.7 25.0 %collective-permute-start.38 = (bf16[192,1024]{1,0:T(8,128)(2,1)S(1)}, bf16[192,1024]{1,0:T(8,128)(2,1)S(1)}, u32[]{:S(2)}, u32[]{:S(2)}) collective-permute-start(bf16[192,1024]{1,0:T(8,128)(2,1)S(1)} %get-tuple-element.174), channel_id=1, source_target_pairs={{0,1},{1,0},{2,3},{3,2},{4,5},{5,4},{6,7},{7,6},{8,9},{9,8},{10,11... | collective-permute-start | bytes 1179656 | tf_op jit(solution)/shard_map/ppermute | solution.py:457
  199.4 25.1 %collective-permute-start.39 = (bf16[2,256,768]{2,1,0:T(8,128)(2,1)S(1)}, bf16[2,256,768]{2,1,0:T(8,128)(2,1)S(1)}, u32[]{:S(2)}, u32[]{:S(2)}) collective-permute-start(bf16[2,256,768]{2,1,0:T(8,128)(2,1)S(1)} %pad_maximum_fusion.6), channel_id=1, source_target_pairs={{0,2},{2,0},{4,6},{6,4},{1,3},{3,1},{5,7},{7,5},{8,10},{10,8},{12,... | collective-permute-start | bytes 2359304 | tf_op jit(solution)/shard_map/ppermute | solution.py:467
  199.9 24.7 %collective-permute-start.40 = (bf16[2,256,768]{2,1,0:T(8,128)(2,1)S(1)}, bf16[2,256,768]{2,1,0:T(8,128)(2,1)S(1)}, u32[]{:S(2)}, u32[]{:S(2)}) collective-permute-start(bf16[2,256,768]{2,1,0:T(8,128)(2,1)S(1)} %stack.247), channel_id=1, source_target_pairs={{0,4},{2,6},{4,0},{6,2},{1,5},{3,7},{5,1},{7,3},{8,12},{10,14},{12... | collective-permute-start | bytes 2359304 | tf_op jit(solution)/shard_map/ppermute | solution.py:467
  220.6 20.4 %collective-permute-start.37 = (bf16[192,1024]{1,0:T(8,128)(2,1)S(1)}, bf16[192,1024]{1,0:T(8,128)(2,1)}, u32[]{:S(2)}, u32[]{:S(2)}) collective-permute-start(bf16[192,1024]{1,0:T(8,128)(2,1)S(1)} %get-tuple-element.172), channel_id=1, source_target_pairs={{0,1},{1,0},{2,3},{3,2},{4,5},{5,4},{6,7},{7,6},{8,9},{9,8},{10,11... | collective-permute-start | bytes 1179656 | tf_op jit(solution)/shard_map/ppermute | solution.py:457
  225.9 15.1 %collective-permute-start.41 = (bf16[256,768]{1,0:T(8,128)(2,1)}, bf16[256,768]{1,0:T(8,128)(2,1)S(1)}, u32[]{:S(2)}, u32[]{:S(2)}) collective-permute-start(bf16[256,768]{1,0:T(8,128)(2,1)} %get-tuple-element.236), channel_id=1, source_target_pairs={{0,4},{2,6},{4,0},{6,2},{1,5},{3,7},{5,1},{7,3},{8,12},{10,14},{12... | collective-permute-start | bytes 1179656 | tf_op jit(solution)/shard_map/ppermute | solution.py:467
  226.5 14.5 %collective-permute-start.42 = (bf16[256,768]{1,0:T(8,128)(2,1)}, bf16[256,768]{1,0:T(8,128)(2,1)S(1)}, u32[]{:S(2)}, u32[]{:S(2)}) collective-permute-start(bf16[256,768]{1,0:T(8,128)(2,1)} %get-tuple-element.235), channel_id=1, source_target_pairs={{0,2},{2,0},{4,6},{6,4},{1,3},{3,1},{5,7},{7,5},{8,10},{10,8},{12,... | collective-permute-start | bytes 1179656 | tf_op jit(solution)/shard_map/ppermute | solution.py:467
  238.8 34.5 %collective-permute-start.43 = (bf16[2,192,1024]{2,1,0:T(8,128)(2,1)S(1)}, bf16[2,192,1024]{2,1,0:T(8,128)(2,1)S(1)}, u32[]{:S(2)}, u32[]{:S(2)}) collective-permute-start(bf16[2,192,1024]{2,1,0:T(8,128)(2,1)S(1)} %key_backward.4), channel_id=1, source_target_pairs={{0,1},{1,0},{2,3},{3,2},{4,5},{5,4},{6,7},{7,6},{8,9},{9,8},{10,11... | collective-permute-start | bytes 2359304 | tf_op jit(solution)/shard_map/ppermute | solution.py:457
  243.9 12.5 %collective-permute-start.45 = (bf16[256,768]{1,0:T(8,128)(2,1)S(1)}, bf16[256,768]{1,0:T(8,128)(2,1)S(1)}, u32[]{:S(2)}, u32[]{:S(2)}) collective-permute-start(bf16[256,768]{1,0:T(8,128)(2,1)S(1)} %get-tuple-element.284), channel_id=1, source_target_pairs={{0,8},{8,0},{16,24},{24,16},{1,9},{9,1},{17,25},{25,17},{2,10},{10... | collective-permute-start | bytes 1179656 | tf_op jit(solution)/shard_map/ppermute | solution.py:460
  245.6 26.6 %collective-permute-start.44 = (bf16[192,1024]{1,0:T(8,128)(2,1)S(1)}, bf16[192,1024]{1,0:T(8,128)(2,1)S(1)}, u32[]{:S(2)}, u32[]{:S(2)}) collective-permute-start(bf16[192,1024]{1,0:T(8,128)(2,1)S(1)} %add_convert_fusion.5), channel_id=1, source_target_pairs={{0,8},{8,0},{16,24},{24,16},{1,9},{9,1},{17,25},{25,17},{2,10},{10... | collective-permute-start | bytes 1179656 | tf_op jit(solution)/shard_map/ppermute | solution.py:460
  254.6 56.1 %collective-permute-start.55 = (bf16[3,96,768]{2,1,0:T(8,128)(2,1)}, bf16[3,96,768]{2,1,0:T(8,128)(2,1)}, u32[]{:S(2)}, u32[]{:S(2)}) collective-permute-start(bf16[3,96,768]{2,1,0:T(8,128)(2,1)} %get-tuple-element.202.refs_4_), channel_id=1, source_target_pairs={{0,6},{2,4},{4,2},{6,0},{1,7},{3,5},{5,3},{7,1},{8,14},{10,12},{12... | collective-permute-start | bytes 1327112 | tf_op jit(solution)/shard_map/ppermute | solution.py:467
  255.9 54.9 %collective-permute-start.54 = (bf16[3,96,768]{2,1,0:T(8,128)(2,1)}, bf16[3,96,768]{2,1,0:T(8,128)(2,1)}, u32[]{:S(2)}, u32[]{:S(2)}) collective-permute-start(bf16[3,96,768]{2,1,0:T(8,128)(2,1)} %get-tuple-element.202.refs_4_), channel_id=1, source_target_pairs={{0,4},{2,6},{4,0},{6,2},{1,5},{3,7},{5,1},{7,3},{8,12},{10,14},{12... | collective-permute-start | bytes 1327112 | tf_op jit(solution)/shard_map/ppermute | solution.py:467
  256.4 54.4 %collective-permute-start.53 = (bf16[3,96,768]{2,1,0:T(8,128)(2,1)}, bf16[3,96,768]{2,1,0:T(8,128)(2,1)}, u32[]{:S(2)}, u32[]{:S(2)}) collective-permute-start(bf16[3,96,768]{2,1,0:T(8,128)(2,1)} %get-tuple-element.202.refs_4_), channel_id=1, source_target_pairs={{0,2},{2,0},{4,6},{6,4},{1,3},{3,1},{5,7},{7,5},{8,10},{10,8},{12,... | collective-permute-start | bytes 1327112 | tf_op jit(solution)/shard_map/ppermute | solution.py:467
  273.0 20.0 %collective-permute-start.47 = (bf16[256,768]{1,0:T(8,128)(2,1)}, bf16[256,768]{1,0:T(8,128)(2,1)}, u32[]{:S(2)}, u32[]{:S(2)}) collective-permute-start(bf16[256,768]{1,0:T(8,128)(2,1)} %fusion.13), channel_id=1, source_target_pairs={{0,16},{8,24},{16,0},{24,8},{1,17},{9,25},{17,1},{25,9},{2,18},{10... | collective-permute-start | bytes 1179656 | tf_op jit(solution)/shard_map/ppermute | solution.py:464
  274.6 21.8 %collective-permute-start.46 = (bf16[192,1024]{1,0:T(8,128)(2,1)}, bf16[192,1024]{1,0:T(8,128)(2,1)}, u32[]{:S(2)}, u32[]{:S(2)}) collective-permute-start(bf16[192,1024]{1,0:T(8,128)(2,1)} %get-tuple-element.282), channel_id=1, source_target_pairs={{0,8},{8,0},{16,24},{24,16},{1,9},{9,1},{17,25},{25,17},{2,10},{10... | collective-permute-start | bytes 1179656 | tf_op jit(solution)/shard_map/ppermute | solution.py:460
  293.0 14.9 %collective-permute-start.48 = (bf16[2,192,1024]{2,1,0:T(8,128)(2,1)S(1)}, bf16[2,192,1024]{2,1,0:T(8,128)(2,1)S(1)}, u32[]{:S(2)}, u32[]{:S(2)}) collective-permute-start(bf16[2,192,1024]{2,1,0:T(8,128)(2,1)S(1)} %key_backward.6), channel_id=1, source_target_pairs={{0,1},{1,0},{2,3},{3,2},{4,5},{5,4},{6,7},{7,6},{8,9},{9,8},{10,11... | collective-permute-start | bytes 2359304 | tf_op jit(solution)/shard_map/ppermute | solution.py:457
  310.7 17.7 %collective-permute-start.58 = (bf16[3,96,768]{2,1,0:T(8,128)(2,1)}, bf16[3,96,768]{2,1,0:T(8,128)(2,1)S(1)}, u32[]{:S(2)}, u32[]{:S(2)}) collective-permute-start(bf16[3,96,768]{2,1,0:T(8,128)(2,1)} %collective-permute-done.55.refs_7_), channel_id=1, source_target_pairs={{0,1},{1,0},{2,3},{3,2},{4,5},{5,4},{6,7},{7,6},{8,9},{9,8},{10,11... | collective-permute-start | bytes 1327112 | tf_op jit(solution)/shard_map/ppermute | solution.py:457
  311.1 19.6 %collective-permute-start.57 = (bf16[3,96,768]{2,1,0:T(8,128)(2,1)}, bf16[3,96,768]{2,1,0:T(8,128)(2,1)S(1)}, u32[]{:S(2)}, u32[]{:S(2)}) collective-permute-start(bf16[3,96,768]{2,1,0:T(8,128)(2,1)} %collective-permute-done.54.refs_6_), channel_id=1, source_target_pairs={{0,1},{1,0},{2,3},{3,2},{4,5},{5,4},{6,7},{7,6},{8,9},{9,8},{10,11... | collective-permute-start | bytes 1327112 | tf_op jit(solution)/shard_map/ppermute | solution.py:457
  311.3 21.1 %collective-permute-start.56 = (bf16[3,96,768]{2,1,0:T(8,128)(2,1)}, bf16[3,96,768]{2,1,0:T(8,128)(2,1)S(1)}, u32[]{:S(2)}, u32[]{:S(2)}) collective-permute-start(bf16[3,96,768]{2,1,0:T(8,128)(2,1)} %collective-permute-done.53.refs_5_), channel_id=1, source_target_pairs={{0,1},{1,0},{2,3},{3,2},{4,5},{5,4},{6,7},{7,6},{8,9},{9,8},{10,11... | collective-permute-start | bytes 1327112 | tf_op jit(solution)/shard_map/ppermute | solution.py:457
  322.3 30.7 %collective-permute-start.71 = (bf16[256,768]{1,0:T(8,128)(2,1)S(1)}, bf16[256,768]{1,0:T(8,128)(2,1)S(1)}, u32[]{:S(2)}, u32[]{:S(2)}) collective-permute-start(bf16[256,768]{1,0:T(8,128)(2,1)S(1)} %copy-done.24), channel_id=1, source_target_pairs={{0,8},{8,0},{16,24},{24,16},{1,9},{9,1},{17,25},{25,17},{2,10},{10... | collective-permute-start | bytes 1179656 | tf_op jit(solution)/shard_map/ppermute | solution.py:460
  328.0 25.7 %collective-permute-start.62 = (bf16[2,128,768]{2,1,0:T(8,128)(2,1)S(1)}, bf16[2,128,768]{2,1,0:T(8,128)(2,1)S(1)}, u32[]{:S(2)}, u32[]{:S(2)}) collective-permute-start(bf16[2,128,768]{2,1,0:T(8,128)(2,1)S(1)} %copy-done.23), channel_id=1, source_target_pairs={{0,2},{2,0},{4,6},{6,4},{1,3},{3,1},{5,7},{7,5},{8,10},{10,8},{12,... | collective-permute-start | bytes 1179656 | tf_op jit(solution)/shard_map/ppermute | solution.py:467
  328.4 26.0 %collective-permute-start.63 = (bf16[2,128,768]{2,1,0:T(8,128)(2,1)S(1)}, bf16[2,128,768]{2,1,0:T(8,128)(2,1)S(1)}, u32[]{:S(2)}, u32[]{:S(2)}) collective-permute-start(bf16[2,128,768]{2,1,0:T(8,128)(2,1)S(1)} %copy-done.23), channel_id=1, source_target_pairs={{0,4},{2,6},{4,0},{6,2},{1,5},{3,7},{5,1},{7,3},{8,12},{10,14},{12... | collective-permute-start | bytes 1179656 | tf_op jit(solution)/shard_map/ppermute | solution.py:467
  339.4 11.8 %collective-permute-start.59 = (bf16[128,768]{1,0:T(8,128)(2,1)S(1)}, bf16[128,768]{1,0:T(8,128)(2,1)S(1)}, u32[]{:S(2)}, u32[]{:S(2)}) collective-permute-start(bf16[128,768]{1,0:T(8,128)(2,1)S(1)} %get-tuple-element.289), channel_id=1, source_target_pairs={{0,16},{8,24},{16,0},{24,8},{1,17},{9,25},{17,1},{25,9},{2,18},{10... | collective-permute-start | bytes 589832 | tf_op jit(solution)/shard_map/ppermute | solution.py:464
  340.0 12.8 %collective-permute-start.61 = (bf16[144,768]{1,0:T(8,128)(2,1)S(1)}, bf16[144,768]{1,0:T(8,128)(2,1)S(1)}, u32[]{:S(2)}, u32[]{:S(2)}) collective-permute-start(bf16[144,768]{1,0:T(8,128)(2,1)S(1)} %constant_dynamic-slice_fusion), channel_id=1, source_target_pairs={{0,8},{8,0},{16,24},{24,16},{1,9},{9,1},{17,25},{25,17},{2,10},{10... | collective-permute-start | bytes 663560 | tf_op jit(solution)/shard_map/ppermute | solution.py:460
  352.9 16.6 %collective-permute-start.68 = (bf16[144,768]{1,0:T(8,128)(2,1)S(1)}, bf16[144,768]{1,0:T(8,128)(2,1)S(1)}, u32[]{:S(2)}, u32[]{:S(2)}) collective-permute-start(bf16[144,768]{1,0:T(8,128)(2,1)S(1)} %fusion.17), channel_id=1, source_target_pairs={{0,16},{8,24},{16,0},{24,8},{1,17},{9,25},{17,1},{25,9},{2,18},{10... | collective-permute-start | bytes 663560 | tf_op jit(solution)/shard_map/ppermute | solution.py:464
  353.0 17.4 %collective-permute-start.65 = (bf16[2,128,768]{2,1,0:T(8,128)(2,1)S(1)}, bf16[2,128,768]{2,1,0:T(8,128)(2,1)S(1)}, u32[]{:S(2)}, u32[]{:S(2)}) collective-permute-start(bf16[2,128,768]{2,1,0:T(8,128)(2,1)S(1)} %pad_maximum_fusion.12), channel_id=1, source_target_pairs={{0,2},{2,0},{4,6},{6,4},{1,3},{3,1},{5,7},{7,5},{8,10},{10,8},{12,... | collective-permute-start | bytes 1179656 | tf_op jit(solution)/shard_map/ppermute | solution.py:467
  353.7 19.0 %collective-permute-start.66 = (bf16[2,128,768]{2,1,0:T(8,128)(2,1)S(1)}, bf16[2,128,768]{2,1,0:T(8,128)(2,1)S(1)}, u32[]{:S(2)}, u32[]{:S(2)}) collective-permute-start(bf16[2,128,768]{2,1,0:T(8,128)(2,1)S(1)} %pad_maximum_fusion.12), channel_id=1, source_target_pairs={{0,4},{2,6},{4,0},{6,2},{1,5},{3,7},{5,1},{7,3},{8,12},{10,14},{12... | collective-permute-start | bytes 1179656 | tf_op jit(solution)/shard_map/ppermute | solution.py:467
  354.4 24.3 %collective-permute-start.67 = (bf16[2,128,768]{2,1,0:T(8,128)(2,1)S(1)}, bf16[2,128,768]{2,1,0:T(8,128)(2,1)S(1)}, u32[]{:S(2)}, u32[]{:S(2)}) collective-permute-start(bf16[2,128,768]{2,1,0:T(8,128)(2,1)S(1)} %pad_maximum_fusion.12), channel_id=1, source_target_pairs={{0,6},{2,4},{4,2},{6,0},{1,7},{3,5},{5,3},{7,1},{8,14},{10,12},{12... | collective-permute-start | bytes 1179656 | tf_op jit(solution)/shard_map/ppermute | solution.py:467
  361.9 24.3 %collective-permute-start.72 = (bf16[512,768]{1,0:T(8,128)(2,1)S(1)}, bf16[512,768]{1,0:T(8,128)(2,1)S(1)}, u32[]{:S(2)}, u32[]{:S(2)}) collective-permute-start(bf16[512,768]{1,0:T(8,128)(2,1)S(1)} %pad_maximum_fusion.4), channel_id=1, source_target_pairs={{0,1},{1,0},{2,3},{3,2},{4,5},{5,4},{6,7},{7,6},{8,9},{9,8},{10,11... | collective-permute-start | bytes 2359304 | tf_op jit(solution)/shard_map/ppermute | solution.py:457
  369.7 14.0 %collective-permute-start.69 = (bf16[144,768]{1,0:T(8,128)(2,1)S(1)}, bf16[144,768]{1,0:T(8,128)(2,1)S(1)}, u32[]{:S(2)}, u32[]{:S(2)}) collective-permute-start(bf16[144,768]{1,0:T(8,128)(2,1)S(1)} %add_convert_fusion.10), channel_id=1, source_target_pairs={{0,8},{8,0},{16,24},{24,16},{1,9},{9,1},{17,25},{25,17},{2,10},{10... | collective-permute-start | bytes 663560 | tf_op jit(solution)/shard_map/ppermute | solution.py:460
  (93 other events, 661.9 us)
Sparse Core Ops, SparseCore 0:
  154.4 64.9 reduce-scatter.1
  227.6 46.0 all-reduce.1

commit v6 on v5

--- a/solution.py
+++ b/solution.py
@@ -20,6 +20,9 @@
 NN = (((1,), (0,)), ((), ()))
 NT = (((1,), (1,)), ((), ()))
 TN = (((0,), (0,)), ((), ()))
+
+
+shape = jax.ShapeDtypeStruct
 
 
 def dot(a, b, dims):
@@ -93,26 +96,30 @@
     out[...] = (acc * (1.0 / HASHES)).astype(out.dtype)
 
 
-def query_back_kernel(planes, planes_t, bits, qa, ga, qb, gb, tables, *refs, chunk):
-    start, out, da, db = (None, *refs) if len(refs) == 3 else refs
-    rows = both(qa, qb)
+def query_back_kernel(planes, planes_t, bits, tables, *refs, chunk, blocks, last):
+    queries, grads = refs[:blocks], refs[blocks : 2 * blocks]
+    start = refs[2 * blocks] if len(refs) > 3 * blocks + 1 else None
+    out, back_out = refs[-1 - blocks], refs[-blocks:]
+    rows = both(*queries)
     inv, upper, lower = sides(rows, planes[...])
     low, high = half_codes(upper, lower)
-    grad = both(ga, gb)
-    width = qa.shape[1]
-    sums = jnp.zeros((bits.shape[0], 2 * width), f32)
+    grad = both(*grads)
+    sums = jnp.zeros((bits.shape[0], rows.shape[1]), f32)
     for c in range(0, 16, chunk):
         at = slice(128 * c, 128 * (c + chunk))
         codes = code_chunk(low, high, c, chunk)
         part = dot(codes, grad, NT)
         if start is not None:
-            part = (part + start[0, at, :]) * (1.0 / HASHES)
+            part = part + start[0, at, :]
+        if last:
+            part = part * (1.0 / HASHES)
         out[0, at, :] = part.astype(out.dtype)
         weighted = dot(tables[0, at, :], grad, NN).astype(bf16) * codes
         sums += dot(bits[:, at], weighted, NN)
     back = pull_back(rows, planes_t[...], inv, upper, sums * (1.0 / HASHES))
-    da[...] = back[:, :width].astype(da.dtype)
-    db[...] = back[:, width:].astype(db.dtype)
+    width = back_out[0].shape[1]
+    for i in range(blocks):
+        back_out[i][...] = back[:, i * width : (i + 1) * width].astype(back_out[i].dtype)
 
 
 def key_back_kernel(planes, planes_t, bits, keys, vals, grad_tables, out, *, chunk):
@@ -179,7 +186,7 @@
     return call(
         partial(key_kernel, chunk=2, blocks=len(blocks)),
         heads,
-        5 * len(blocks),
+        15 * len(blocks),
         "key_tables",
         specs,
         table_spec(),
@@ -192,7 +199,7 @@
     return call(
         partial(query_kernel, chunk=2),
         heads,
-        4,
+        10,
         "query_estimates",
         [whole(64, 64), per_head(width), table_spec()],
         per_head(width),
@@ -200,22 +207,23 @@
     )(planes, q, tables)
 
 
-def query_backward(planes, planes_t, bits, q_a, g_a, q_b, g_b, tables, start, kind_a, kind_b):
-    heads, width = q_a.shape[0] // HEAD_DIM, q_a.shape[1]
-    specs = [whole(64, 64), whole(64, 128), whole(80, ROWS)] + [per_head(width)] * 4 + [table_spec()]
-    args = [planes, planes_t, bits, q_a, g_a, q_b, g_b, tables]
+def query_backward(planes, planes_t, bits, tables, queries, grads, start, last, kinds):
+    heads, width = queries[0].shape[0] // HEAD_DIM, queries[0].shape[1]
+    blocks = len(queries)
+    specs = [whole(64, 64), whole(64, 128), whole(80, ROWS), table_spec()] + [per_head(width)] * (2 * blocks)
+    args = [planes, planes_t, bits, tables, *queries, *grads]
     if start is not None:
         specs.append(table_spec())
         args.append(start)
     return call(
-        partial(query_back_kernel, chunk=4),
+        partial(query_back_kernel, chunk=4, blocks=blocks, last=last),
         heads,
-        20,
+        25 * blocks,
         "query_backward",
         specs,
-        [table_spec(), per_head(width), per_head(width)],
-        [jax.ShapeDtypeStruct((heads, ROWS, HEAD_DIM), f32 if start is None else bf16)]
-        + [jax.ShapeDtypeStruct(q_a.shape, kind) for kind in (kind_a, kind_b)],
+        [table_spec()] + [per_head(width)] * blocks,
+        [shape((heads, ROWS, HEAD_DIM), bf16 if last else f32)]
+        + [shape(queries[0].shape, kind) for kind in kinds],
     )(*args)
 
 
@@ -224,7 +232,7 @@
     return call(
         partial(key_back_kernel, chunk=4),
         heads,
-        9,
+        25,
         "key_backward",
         [whole(64, 64), whole(64, 128), whole(80, ROWS)]
         + [per_head(width), per_head(width, heads), table_spec()],
@@ -257,11 +265,19 @@
     return ref[pl.ds(pl.multiple_of(at * half, 16), half), :]
 
 
+def share_rows(keep, give, at, rows):
+    part = keep.shape[2]
+    for out in (keep, give):
+        out[at] = rows[:, :part]
+        out[at + 1] = rows[:, part:]
+
+
 def dense_kernel(core, x_in, grad_out, gain, bias, *refs):
     attn, ups, downs = refs[0:4], refs[4:12], refs[12:20]
-    layer_out, first_out, normed_out, grad_second_out, slope, grad_down, small = refs[20:27]
-    hidden = refs[27]
-    part = hidden.shape[2]
+    layer_out, first_out, grad_second_out, slope, keep, give, heads_give, small = refs[20:28]
+    for j in range(4):
+        heads_give[j] = core_rows(core, attn[j], 1)
+    part = slope.shape[2]
     blocks = range(8)
     heads = jnp.concatenate([core_rows(core, attn[b // 2], b % 2) for b in blocks], axis=0)
     out_w = jnp.concatenate([downs[b][part:, :] for b in blocks], axis=0)
@@ -274,13 +290,13 @@
     small[2:3, :] = column_sum(first * first)
     unit_1, _ = norm(first)
     normed = (unit_1 * gain[0:1, :] + bias[0:1, :]).astype(bf16)
-    normed_out[...] = normed
+    share_rows(keep, give, 4, normed)
     second = normed.astype(f32)
     for b in blocks:
         pre = dot(normed, ups[b][...], NT)
         below = 0.5 * (1.0 + lax.erf(pre * 0.7071067811865476))
         rows = (pre * below).astype(bf16)
-        hidden[b] = rows
+        (keep, give)[b % 2][b // 2] = rows
         slope[b] = below + pre * (0.3989422804014327 * jnp.exp(-0.5 * pre * pre))
         second = second + dot(rows, downs[b][0:part, :], NN)
     unit_2, inv_2 = norm(second)
@@ -291,23 +307,20 @@
     small[5:8, :] = jnp.zeros_like(small[5:8, :])
     grad_second = norm_back(grad * gain[1:2, :], unit_2, inv_2)
     grad_second_out[...] = grad_second
-    grad_ffn = grad_second.astype(bf16)
-    for b in blocks:
-        owner = (core[1] ^ (b // 2)) * 2 + (core[0] if b % 2 == 0 else 1 - core[0])
-        grad_down[owner] = dot(hidden[b], grad_ffn, TN).astype(bf16)
+    share_rows(keep, give, 6, grad_second.astype(bf16))
 
 
 def dense_back_kernel(core, first, grad_second, slope, gain, *refs):
     ups, downs = refs[0:8], refs[8:16]
-    grad_first_out, grad_attn_out, grad_pre = refs[16:19]
+    grad_first_out, keep, give = refs[16:19]
     estimates, small = refs[19:23], refs[23]
-    part = grad_pre.shape[2]
+    part = slope.shape[2]
     blocks = range(8)
     grad_normed = grad_second[...]
     grad_ffn = grad_normed.astype(bf16)
     for b in blocks:
         rows = (dot(grad_ffn, downs[b][0:part, :], NT) * slope[b]).astype(bf16)
-        grad_pre[b] = rows
+        (keep, give)[b % 2][b // 2] = rows
         grad_normed = grad_normed + dot(rows, ups[b][...], NN)
     unit, inv = norm(first[...])
     small[0:1, :] = column_sum(grad_normed * unit)
@@ -316,7 +329,7 @@
     grad_first = norm_back(grad_normed * gain[0:1, :], unit, inv)
     grad_first_out[...] = grad_first
     grad_attn = grad_first.astype(bf16)
-    grad_attn_out[...] = grad_attn
+    share_rows(keep, give, 4, grad_attn)
     for b in blocks:
         half = estimates[0].shape[0] // 2
         at = core[0] if b % 2 == 0 else 1 - core[0]
@@ -325,18 +338,31 @@
         ).astype(bf16)
 
 
-def weight_grad_kernel(core, normed, grad_pre, grad_attn, small_a, small_b, *refs):
-    attn, outs = refs[0:4], refs[4:6]
-    part = grad_pre.shape[2]
+def weight_grad_kernel(core, small_a, small_b, *refs):
+    near, far, near_back, far_back = refs[0:4]
+    attn, attn_far, out = refs[4:8], refs[8], refs[9]
+    part = near.shape[2]
     sums = jnp.concatenate([small_a[...], small_b[...]], axis=0).astype(bf16)
-    for b in range(8):
-        out = outs[b % 2]
-        heads = core_rows(core, attn[b // 2], b % 2)
-        at = part + heads.shape[0]
-        out[b // 2, 0:part, :] = dot(grad_pre[b], normed[...], TN).astype(bf16)
-        out[b // 2, part:at, :] = dot(heads, grad_attn[...], NN).astype(bf16)
-        out[b // 2, at : at + 16, :] = sums
-        out[b // 2, at + 16 :, :] = jnp.zeros_like(sums)
+
+    def wide(ref, at):
+        return jnp.concatenate([ref[at], ref[at + 1]], axis=1)
+
+    def rows(ref, other, at):
+        return jnp.concatenate([wide(ref, at), wide(other, at)], axis=0)
+
+    normed, grad_ffn = rows(near, far, 4), rows(near, far, 6)
+    grad_attn = rows(near_back, far_back, 4)
+    for j in range(4):
+        owner = core[1] ^ j
+        hidden = jnp.concatenate([near[j], far[j]], axis=0)
+        grad_pre = jnp.concatenate([near_back[j], far_back[j]], axis=0)
+        out[owner, 0:part, :] = dot(grad_pre, normed, TN).astype(bf16)
+        out[owner, part : 2 * part, :] = dot(hidden, grad_ffn, TN).astype(bf16)
+        heads = jnp.concatenate([core_rows(core, attn[j], 0), attn_far[j]], axis=1)
+        at = 2 * part + heads.shape[0]
+        out[owner, 2 * part : at, :] = dot(heads, grad_attn, NN).astype(bf16)
+        out[owner, at : at + 16, :] = sums
+        out[owner, at + 16 :, :] = jnp.zeros_like(sums)
 
 
 def input_grad_kernel(core, grad_first, *refs):
@@ -372,32 +398,30 @@
     )(core, *args)
 
 
-shape = jax.ShapeDtypeStruct
-
-
 def dense(core, x_in, grad_out, gain, bias, attn, ups, downs):
     rows, width = x_in.shape
     part = ups[0].shape[0]
     out_shape = [
         shape((rows, width), bf16),
         shape((rows, width), f32),
-        shape((rows, width), bf16),
         shape((rows, width), f32),
         shape((8, rows, part), f32),
-        shape((8, part, width), bf16),
+        shape((8, rows, part), bf16),
+        shape((8, rows, part), bf16),
+        shape((4, attn[0].shape[0] // 2, rows), bf16),
         shape((8, width), f32),
     ]
     args = [x_in, grad_out, gain, bias, *attn, *ups, *downs]
-    scratch = [pltpu.VMEM((8, rows, part), bf16)]
-    return single(dense_kernel, core, args, out_shape, 14, "dense", scratch)
+    return single(dense_kernel, core, args, out_shape, 14, "dense")
 
 
 def dense_back(core, first, grad_second, slope, gain, attn, ups, downs):
     rows, width = first.shape
+    part = ups[0].shape[0]
     out_shape = [
         shape((rows, width), f32),
-        shape((rows, width), bf16),
-        shape((8, rows, ups[0].shape[0]), bf16),
+        shape((6, rows, part), bf16),
+        shape((6, rows, part), bf16),
         *[shape(attn[0].shape, bf16)] * 4,
         shape((8, width), f32),
     ]
@@ -405,11 +429,11 @@
     return single(dense_back_kernel, core, args, out_shape, 8, "dense_back")
 
 
-def weight_grads(core, normed, grad_pre, grad_attn, small_a, small_b, attn):
-    width, part = normed.shape[1], grad_pre.shape[2]
-    out_shape = [shape((4, part + attn[0].shape[0] // 2 + 32, width), bf16)] * 2
-    args = [normed, grad_pre, grad_attn, small_a, small_b, *attn]
-    return single(weight_grad_kernel, core, args, out_shape, 6, "weight_grads")
+def weight_grads(core, small_a, small_b, shared, attn, attn_far):
+    part, width = shared[0].shape[2], small_a.shape[1]
+    out_shape = [shape((4, 2 * part + attn[0].shape[0] // 2 + 32, width), bf16)]
+    args = [small_a, small_b, *shared, *attn, attn_far]
+    return single(weight_grad_kernel, core, args, out_shape, 7, "weight_grads")[0]
 
 
 def input_grad(core, grad_first, blocks, near, far):
@@ -550,12 +574,14 @@
 
     q_zo = after(q_zo, tables)
     down_x, down_y = after(down_x, tables), after(down_y, tables)
+    up_xo, up_yo = after(up_xo, tables), after(up_yo, tables)
     up_d, down_d = over_head(after(up_x, tables), 2), over_head(down_y, 1)
     down_xo, down_yo = over_seq(down_x), over_seq(down_y)
-    q_zo = after(q_zo, down_x, down_y)
+    q_zo = after(q_zo, down_x, down_y, up_xo, up_yo)
     e_zo = query_estimates(signed, q_zo, tables, bf16)
     e_zo_moved = over_seq(e_zo)
-    e_z = query_estimates(signed, after(q_z, e_zo), tables, bf16)
+    down_xo, down_yo = after(down_xo, e_zo), after(down_yo, e_zo)
+    e_z = query_estimates(signed, after(q_z, e_zo, down_xo, down_yo), tables, bf16)
     e_far = add(e_z, after(e_zo_moved, e_z)).astype(bf16)
     e_o = query_estimates(signed, after(q_o, e_far), tables, bf16)
     e_far = over_place(e_far)
@@ -563,8 +589,6 @@
     e = query_estimates(signed, after(q, e_o), tables, f32)
     e_far = after(e_far, e)
     up_d, down_d = after(up_d, e_far), after(down_d, e_far)
-    up_xo, up_yo = after(up_xo, e_zo), after(up_yo, e_zo)
-    down_xo, down_yo = after(down_xo, e_zo), after(down_yo, e_zo)
     ups += [up_x, up_xo, up_y, up_yo, up_d, over_seq(up_d)]
     downs += [down_x, down_xo, down_y, down_yo, down_d, over_seq(down_d)]
     attn = add(e, after(e_o_moved, e), e_far).astype(bf16)
@@ -581,91 +605,73 @@
         return [dense_rows[0]] + [over_group(dense_rows[k], groups - k) for k in range(1, groups)]
 
     core = jnp.stack([s, d]).astype(jnp.int32)
-    layer_rows, first, normed, grad_second, slope, a_grads, small_a = dense(
+    layer_rows, first, grad_second, slope, near, give, heads_give, small_a = dense(
         core, dense_in, grad_out, norm_gain, norm_bias, attn_parts, ups, downs
     )
-    a_sum = lax.psum_scatter(a_grads, ("head", "seq"), scatter_dimension=0, tiled=True)[0]
-    (grad_first, grad_attn, grad_pre, *est_parts, small_b) = dense_back(
+    far, heads_far = over_seq(give), over_seq(heads_give)
+    grad_first, near_back, give_back, *est_parts, small_b = dense_back(
         core, first, grad_second, slope, norm_gain, attn_parts, ups, downs
     )
-    grad = jnp.concatenate(
-        [est_parts[0]] + [over_head(est_parts[j], j) for j in range(1, head_count)], axis=1
-    )
-    mine_b, other_b = weight_grads(core, normed, grad_pre, grad_attn, small_a, small_b, attn_parts)
-
+    far_back = over_seq(give_back)
+    est_moved = [over_head(est_parts[j], j) for j in range(1, head_count)]
+    grad = jnp.concatenate([est_parts[0], *lax.optimization_barrier(est_moved)], axis=1)
+    layer_moved = away(layer_rows)
+    weight_parts = weight_grads(
+        core, after(small_a, grad), small_b, [near, far, near_back, far_back], attn_parts, heads_far
+    )
+
+    weight_sum = lax.psum_scatter(weight_parts, "head", scatter_dimension=0, tiled=True)[0]
     grad_z = over_place(grad)
-    grad_o = over_seq(grad)
-    swap_b = over_seq(after(other_b, grad_o))
-    layer_moved = away(layer_rows)
+    grad_o = after(over_seq(grad), weight_parts)
+    layer_moved = jnp.stack([after(x, weight_parts) for x in layer_moved])
     part, dq, dq_o = query_backward(
-        signed, signed_t, bits, q, grad, q_o, after(grad_o, mine_b), tables, None, f32, bf16
-    )
-
-    grad_zo = over_seq(after(grad_z, part))
-    layer_moved = jnp.stack([after(x, part) for x in layer_moved])
-    cut = mine_b.shape[1] // 2
-    chip_b = add(mine_b, after(swap_b, part)).astype(bf16)
-    x_out = jnp.stack([chip_b[1, :cut], chip_b[3, :cut]])
-    y_out = jnp.stack([chip_b[2, cut:], chip_b[3, cut:]])
-    x_far, y_far = over_head(x_out, 1), over_head(y_out, 2)
+        signed, signed_t, bits, tables, [after(q, layer_moved), q_o], [grad, grad_o], None, False, [f32, bf16]
+    )
+
+    grad_z = after(grad_z, part)
+    grad_zo = over_seq(grad_z)
     dq_o = over_seq(dq_o)
-    q_gated = after(q_z, x_out, y_out, layer_moved)
-    grad_tables, dq_z, dq_zo = query_backward(
-        signed, signed_t, bits, q_gated, grad_z, q_zo, grad_zo, tables, part, bf16, bf16
-    )
-
-    a_sum = after(a_sum, dq_z)
-    x_far, y_far = after(x_far, dq_z), after(y_far, dq_z)
-    x_own = add(chip_b[0, :cut], x_far[0])
-    y_own = add(chip_b[0, cut:], y_far[0])
-    x_out = add(chip_b[2, :cut], x_far[1]).astype(bf16)
-    y_out = add(chip_b[1, cut:], y_far[1]).astype(bf16)
-    x_last, y_last = over_head(x_out, 2), over_head(y_out, 1)
+    part, dq_z = query_backward(
+        signed, signed_t, bits, tables, [q_z], [grad_z], part, False, [f32]
+    )
+
+    dq_own = add(dq, after(dq_o, dq_z))
+    grad_zo = after(grad_zo, dq_z)
+    grad_tables, dq_zo = query_backward(
+        signed, signed_t, bits, tables, [after(q_zo, dq_own)], [grad_zo], part, True, [bf16]
+    )
+
     dq_zo = over_seq(dq_zo)
-    dq_own = add(dq, after(dq_o, dq_z))
-    dkv_zo = key_backward(
-        signed, signed_t, bits, after(kv_zo, dq_own, x_out, y_out, a_sum), grad_tables, bf16
-    )
-    a_sum = lax.psum(a_sum, "hash")
+    dkv_zo = key_backward(signed, signed_t, bits, kv_zo, grad_tables, bf16)
 
     dkv_zo_moved = over_seq(dkv_zo)
     dq_far = add(dq_z, after(dq_zo, dkv_zo)).astype(bf16)
-    b_halves = jnp.stack(
-        [add(x_own, after(x_last, dkv_zo)), add(y_own, after(y_last, dkv_zo))]
-    ).astype(bf16)
-    b_keep = lax.dynamic_index_in_dim(b_halves, r, 0, keepdims=False)
-    b_send = lax.dynamic_index_in_dim(b_halves, 1 - r, 0, keepdims=False)
-    dkv_z = key_backward(
-        signed, signed_t, bits, after(kv_z, dq_far, b_keep, b_send), grad_tables, bf16
-    )
-    dq_far, b_far = over_place(dq_far), over_place(b_send)
+    layer_moved = [layer_moved] + [over_head(layer_moved, j) for j in range(1, head_count)]
+    dkv_z = key_backward(signed, signed_t, bits, after(kv_z, dq_far), grad_tables, bf16)
+    dq_far = over_place(dq_far)
 
     dkv_far = add(dkv_z, after(dkv_zo_moved, dkv_z)).astype(bf16)
     grad_q = add(dq_own, after(dq_far, dkv_z)).astype(bf16)
-    b_keep = add(b_keep, after(b_far, dkv_z))
-    b_send = b_keep.astype(bf16)
+    weight_sum = after(weight_sum, dkv_z)
+    layer_moved = [after(x, dkv_z) for x in layer_moved]
     dkv_o = key_backward(
-        signed, signed_t, bits, after(kv_o, dkv_far, grad_q, b_send), grad_tables, bf16
-    )
+        signed, signed_t, bits, after(kv_o, dkv_far, grad_q, weight_sum, *layer_moved), grad_tables, bf16
+    )
+    weight_sum = lax.psum(weight_sum, "hash")
     dk_far, dv_far = over_place(dkv_far[0]), over_place(after(dkv_far[1], dkv_o))
-    b_far = [over_group(b_send, k) for k in range(1, groups)]
+    qkv_half = after(qkv_near[0], dkv_z)
+    qkv_moved = [over_head(qkv_half, j) for j in range(1, head_count)]
 
     dkv_o_moved = over_seq(dkv_o)
-    a_sum = after(a_sum, dkv_o)
     dk_far = after(dk_far, dkv_o)
-    b_send = add(b_keep, *[after(x, dkv_o) for x in b_far]).astype(bf16)
-    layer_moved = after(layer_moved, dkv_o)
-    layer_moved = [layer_moved] + [over_head(layer_moved, j) for j in range(1, head_count)]
-    qkv_half = after(qkv_near[0], dkv_z)
-    qkv_near += [after(over_head(qkv_half, j), dkv_o) for j in range(1, head_count)]
+    qkv_near += [after(x, dkv_o) for x in qkv_moved]
     dkv = key_backward(
-        signed, signed_t, bits, after(kv, dk_far, b_send, a_sum), grad_tables, f32
-    )
-    b_far = over_place(b_send)
-
-    qkv_near[1:] = [after(x, dkv) for x in qkv_near[1:]]
+        signed, signed_t, bits, after(kv, dk_far, *qkv_near[1:]), grad_tables, f32
+    )
     qkv_far += [over_seq(x) for x in qkv_near[1:]]
+
     dkv_o_moved = after(dkv_o_moved, dkv)
+    qkv_far[1:] = [after(x, dkv) for x in qkv_far[1:]]
     grad_k = add(dkv[0], dkv_o_moved[0], dk_far)
     grad_v = add(dkv[1], dkv_o_moved[1], after(dv_far, dkv))
     grad_qkv = jnp.stack([grad_q, grad_k.astype(bf16), grad_v.astype(bf16)])
@@ -714,13 +720,17 @@
     w_grad = in_halves(r, w_keep, over_place(w_keep))
     w_grad = in_halves(s, w_grad, over_seq(w_grad)).reshape(3, head_width, width)
     grad_w_qkv = w_grad.transpose(0, 2, 1).astype(f32)
-    grad_w_down = in_halves(s, a_sum, over_seq(a_sum)).astype(f32)
-    b_sum = in_halves(r, b_send, after(b_far, grad_moved[0]))
-    b_other = over_seq(b_sum)
-    cut, out_cut = hidden_own // 2, (hidden_own + head_width) // 2
-    grad_w_up = in_halves(s, b_sum[:cut], b_other[:cut]).T.astype(f32)
-    grad_w_out = in_halves(s, b_sum[cut:out_cut], b_other[cut:out_cut]).astype(f32)
-    small = b_sum[out_cut : out_cut + 16].astype(f32)
+    weight_sum = after(weight_sum, w_keep)
+    weight_far = over_seq(weight_sum)
+    cut = hidden_own // 2
+    ends = [0, cut, 2 * cut, 2 * cut + head_width // 2]
+    grad_w_up, grad_w_down, grad_w_out = [
+        in_halves(s, weight_sum[a:b], weight_far[a:b]) for a, b in zip(ends, ends[1:])
+    ]
+    grad_w_up = grad_w_up.T.astype(f32)
+    grad_w_down, grad_w_out = grad_w_down.astype(f32), grad_w_out.astype(f32)
+    at = slice(ends[3], ends[3] + 16)
+    small = add(weight_sum[at], weight_far[at])
 
     count = piece * seqs * width * hash_count * 2
     stream_rms = jnp.sqrt(jnp.sum(small[0:3], axis=1) / count)

time: 405 us -> 375 us (0.926)
  waiting for transfers between devices: 91.5 us -> 71.9 us
  other arithmetic: 30.8 us -> 21.6 us
  local copies, waits for them, and re-layouts: 44.8 us -> 38.3 us
    ppermute x31 -> x27, waiting for transfers between devices: 49 us -> 32.3 us  [over_head(): return lax.ppermute(x, 'head', [(h, h ^ j) for h in range(head_count)])]
    ppermute x11 -> x9, waiting for transfers between devices: 25.6 us -> 16.9 us  [over_place(): return lax.ppermute(x, 'hash', [(h, h ^ 1) for h in range(hash_count)])]
    ppermute x26 -> x27, starting transfers between devices: 24.6 us -> 31.9 us  [over_seq(): return lax.ppermute(x, 'seq', [(0, 1), (1, 0)])]
    ppermute x5 -> x4, waiting for transfers between devices: 15.5 us -> 22.5 us  [over_group(): return lax.ppermute(x, 'hash', moves)]
    unnamed x137 -> x129, local copies, waits for them, and re-layouts: 28 us -> 21.9 us
    convert_element_type x8 -> x3, other arithmetic: 9.43 us -> 3.99 us  [the longest x2 3.82 us: shards(): grad_w_down, grad_w_out = (grad_w_down.astype(f32), grad_w_out.astype(f32))]
    ppermute x31 -> x27, starting transfers between devices: 29.1 us -> 24.9 us  [over_head(): return lax.ppermute(x, 'head', [(h, h ^ j) for h in range(head_count)])]
    pallas_call x13 -> x14, Pallas kernels: 106 us -> 110 us  [the longest x3 43.5 us: query_backward(): call(partial(query_back_kernel, chunk=4, blocks=blocks, last=last), heads...]
  transfers between devices with their start and end apart: 76 -> 70, of which waited for: 25 -> 19; matrix products, arithmetic and copies ran while one was open for 14% -> 10% of each run, Pallas kernels for 29% -> 36%
where the time goes in v6:
time: 375 us; the launch traced here: 372 us
  Pallas kernels  148 us (39%)
  starting transfers between devices  72 us (19%)
  waiting for transfers between devices  71.9 us (19%)
  local copies, waits for them, and re-layouts  38.3 us (10%)
  other arithmetic  21.6 us (6%)
  between operations  15.7 us (4%)
  matrix products  4.09 us (1%)
    pallas_call x3, Pallas kernels, query_backward(): call(partial(query_back_kernel, chunk=4, blocks=blocks, last=last), heads...  43.5 us
    pallas_call x4, Pallas kernels, single(): pl.pallas_call(kernel, in_specs=[pl.BlockSpec(memory_space=pltpu.SMEM)] +...  38.2 us
    pallas_call x4, Pallas kernels, key_backward(): call(partial(key_back_kernel, chunk=4), heads, 25, 'key_backward', [whole...  35.3 us
    ppermute x27, waiting for transfers between devices, over_head(): return lax.ppermute(x, 'head', [(h, h ^ j) for h in range(head_count)])  32.3 us
    ppermute x27, starting transfers between devices, over_seq(): return lax.ppermute(x, 'seq', [(0, 1), (1, 0)])  31.9 us
    ppermute x27, starting transfers between devices, over_head(): return lax.ppermute(x, 'head', [(h, h ^ j) for h in range(head_count)])  24.9 us
    ppermute x4, waiting for transfers between devices, over_group(): return lax.ppermute(x, 'hash', moves)  22.5 us
    unnamed x129, local copies, waits for them, and re-layouts  21.9 us
  transfers between devices with their start and end apart: 70, of which 19 were waited for; matrix products, arithmetic and copies ran while one was open for 10% of the time, Pallas kernels for 36%

profile of v6, /device:TPU:1, one launch (start us, length us, event | category | flops | bytes accessed | tf_op | source)
XLA Modules:
  0.0 371.7 jit_solution(11466450242220322499)
XLA Ops:
  7.3 4.5 %constant_dynamic-slice_fusion.10 = (bf16[1,128,1,768]{3,2,1,0:T(2,128)(2,1)}, bf16[1,128,1,768]{3,2,1,0:T(2,128)(2,1)S(1)}, bf16[1,128,1,768]{3,2,1,0:T(2,128)(...) fusion(bf16[1,512,2,768]{3,2,1,0:T(2,128)(2,1)} %param.11, s32[]{:T(128)S(6)} %select_n.262, ...), kind=kLoop, calls=%fused_computation.111 | loop fusion | bytes 1966104 | tf_op jit(solution)/shard_map/jit(dynamic_index_in_dim)/dynamic_slice | solution.py:494
  12.6 3.1 collective-permute-start
  16.3 2.7 collective-permute-start.1
  21.0 1.9 copy_bitcast_fusion.2
  22.9 1.8 copy_bitcast_fusion
  34.4 1.7 fusion.27
  36.1 2.3 collective-permute-done.2
  38.5 4.8 %collective-permute-done.3 = bf16[1,128,768]{2,1,0:T(8,128)(2,1)S(1)} collective-permute-done((bf16[1,128,768]{2,1,0:T(8,128)(2,1)}, bf16[1,128,768]{2,1,0:T(8,128)(2,1)S(1)}, u32[]{:S(2)}, u32[]{:S(2)}) %collective-permute-start.3) | collective-permute-done | bytes 196640 | tf_op jit(solution)/shard_map/ppermute | solution.py:491
  51.2 7.8 %key_tables.3.refs_2_ = f32[3,2048,64]{2,1,0:T(8,128)S(1)} custom-call(bf16[64,64]{1,0:T(8,128)(2,1)S(1)} %bitcast.153, bf16[384,1024]{1,0:T(8,128)(2,1)S(1)} %bitcast.148, bf16[384,1024]{1,0:T(8,128)(2,1)S(1)} %collective-permute-done.6.refs_1_.refs_3_.keys.vals, bf16[384,1024]{1,0:T(8,128)(2,1)S(1)} %bitcast.149, ...), custom_call_target="tpu_custom_call" | custom-call | flops 32999999488 | bytes 1048576 | tf_op jit(solution)/shard_map/key_tables/pallas_call | solution.py:186
  60.7 6.5 %collective-permute-done.10.refs_0_.refs_1_.keys.vals = bf16[384,1024]{1,0:T(8,128)(2,1)S(1)} collective-permute-done((bf16[384,1024]{1,0:T(8,128)(2,1)S(1)}, bf16[384,1024]{1,0:T(8,128)(2,1)S(1)}, u32[]{:S(2)}, u32[]{:S(2)}) %collective-permute-start.10) | collective-permute-done | bytes 786464 | tf_op jit(solution)/shard_map/ppermute | solution.py:484
  68.7 5.5 %key_tables.4.refs_2_ = f32[3,2048,64]{2,1,0:T(8,128)S(1)} custom-call(bf16[64,64]{1,0:T(8,128)(2,1)S(1)} %bitcast.154, bf16[384,1024]{1,0:T(8,128)(2,1)S(1)} %collective-permute-done.10.refs_0_.refs_1_.keys.vals, bf16[384,1024]{1,0:T(8,128)(2,1)S(1)} %collective-permute-done.10.refs_0_.refs_1_.keys.vals, f32[3,2048,64]{2,1,0:T(8,128)} %copy-done.9), custom_call_target="tpu_custom_call" | custom-call | flops 16499999744 | bytes 1048576 | tf_op jit(solution)/shard_map/key_tables/pallas_call | solution.py:186
  76.8 2.6 collective-permute-done.7.q.refs_0_
  80.3 4.2 %key_tables.5.tables = bf16[3,2048,64]{2,1,0:T(8,128)(2,1)S(1)} custom-call(bf16[64,64]{1,0:T(8,128)(2,1)S(1)} %bitcast.155, bf16[384,1024]{1,0:T(8,128)(2,1)S(1)} %collective-permute-done.12.refs_0_.refs_1_.keys.vals, bf16[384,1024]{1,0:T(8,128)(2,1)S(1)} %collective-permute-done.12.refs_0_.refs_1_.keys.vals, f32[3,2048,64]{2,1,0:T(8,128)S(1)} %key_tables.4.refs_2_), custom_call_target="tpu_custom_call" | custom-call | flops 16499999744 | bytes 1048576 | tf_op jit(solution)/shard_map/key_tables/pallas_call | solution.py:186
  85.1 6.6 %collective-permute-done.14.refs_16_.refs_12_ = bf16[480,768]{1,0:T(8,128)(2,1)S(1)} collective-permute-done((bf16[480,768]{1,0:T(8,128)(2,1)S(1)}, bf16[480,768]{1,0:T(8,128)(2,1)S(1)}, u32[]{:S(2)}, u32[]{:S(2)}) %collective-permute-start.14) | collective-permute-done | bytes 737312 | tf_op jit(solution)/shard_map/ppermute | solution.py:491
  94.8 3.3 query_estimates.4
  98.7 3.3 query_estimates.5
  103.7 3.3 query_estimates.6
  108.0 3.7 query_estimates.7
  119.7 2.0 collective-permute-done.24.refs_3_.refs_7_
  122.8 12.7 %dense.1 = (bf16[256,768]{1,0:T(8,128)(2,1)}, f32[256,768]{1,0:T(8,128)}, f32[256,768]{1,0:T(8,128)}, f32[8,256,384]{2,1,0:T(8,128)}, bf16[8,256,384]{2,1,0:T(8,...) custom-call(s32[2]{0:T(128)} %pad_add_fusion.core, ...), custom_call_target="tpu_custom_call" | custom-call | flops 15399999488 | bytes 1048576 | tf_op jit(solution)/shard_map/dense/pallas_call | solution.py:387
  135.4 1.8 collective-permute-start.32
  137.2 12.0 %dense_back.1 = (f32[256,768]{1,0:T(8,128)}, bf16[6,256,384]{2,1,0:T(8,128)(2,1)}, bf16[6,256,384]{2,1,0:T(8,128)(2,1)}, bf16[192,256]{1,0:T(8,128)(2,1)}, bf16[...) custom-call(s32[2]{0:T(128)} %pad_add_fusion.core, ...), custom_call_target="tpu_custom_call" | custom-call | flops 8800000000 | bytes 1048576 | tf_op jit(solution)/shard_map/dense_back/pallas_call | solution.py:387
  159.1 8.4 %weight_grads.1 = bf16[4,896,768]{2,1,0:T(8,128)(2,1)} custom-call(s32[2]{0:T(128)} %pad_add_fusion.core, f32[8,768]{1,0:T(8,128)} %get-tuple-element.159.small_a, f32[8,768]{1,0:T(8,128)} %get-tuple-element.160.small_b, bf16[8,256,384]{2,1,0:T(8,128)(2,1)} %get-tuple-element.161.refs_0_, bf16[8,256,384]{2,1,0:T(8,128)(2,1)} %collective-permute-done.32.refs_1_, ...), custom_call_target="tpu_custom_call" | custom-call | flops 7699999744 | bytes 1048576 | tf_op jit(solution)/shard_map/weight_grads/pallas_call | solution.py:387
  171.1 20.7 %query_backward.3 = (f32[3,2048,64]{2,1,0:T(8,128)}, f32[192,1024]{1,0:T(8,128)S(1)}, bf16[192,1024]{1,0:T(8,128)(2,1)S(1)}) custom-call(bf16[64,64]{1,0:T(8,128)(2,1)S(1)} %bitcast.160, bf16[64,128]{1,0:T(8,128)(2,1)S(1)} %pad_maximum_fusion.11.planes_t, bf16[80,2048]{1,0:T(8,128)(2,1)S(1)} %copy-done.8, bf16[3,2048,64]{2,1,0:T(8,128)(2,1)S(1)} %copy-done.11, ...), custom_call_target="tpu_custom_call" | custom-call | flops 54999998464 | bytes 1048576 | tf_op jit(solution)/shard_map/query_backward/pallas_call | solution.py:218
  192.3 11.7 %query_backward.4 = (f32[3,2048,64]{2,1,0:T(8,128)}, f32[192,1024]{1,0:T(8,128)S(1)}) custom-call(bf16[64,64]{1,0:T(8,128)(2,1)S(1)} %bitcast.161, bf16[64,128]{1,0:T(8,128)(2,1)S(1)} %pad_maximum_fusion.11.planes_t, bf16[80,2048]{1,0:T(8,128)(2,1)S(1)} %copy-done.8, bf16[3,2048,64]{2,1,0:T(8,128)(2,1)S(1)} %copy-done.11, ...), custom_call_target="tpu_custom_call" | custom-call | flops 27499999232 | bytes 1048576 | tf_op jit(solution)/shard_map/query_backward/pallas_call | solution.py:218
  207.3 11.1 %query_backward.5 = (bf16[3,2048,64]{2,1,0:T(8,128)(2,1)S(1)}, bf16[192,1024]{1,0:T(8,128)(2,1)S(1)}) custom-call(bf16[64,64]{1,0:T(8,128)(2,1)S(1)} %bitcast.162, bf16[64,128]{1,0:T(8,128)(2,1)S(1)} %pad_maximum_fusion.11.planes_t, bf16[80,2048]{1,0:T(8,128)(2,1)S(1)} %copy-done.8, bf16[3,2048,64]{2,1,0:T(8,128)(2,1)S(1)} %copy-done.11, ...), custom_call_target="tpu_custom_call" | custom-call | flops 27499999232 | bytes 1048576 | tf_op jit(solution)/shard_map/query_backward/pallas_call | solution.py:218
  219.4 8.7 %key_backward.4 = bf16[2,192,1024]{2,1,0:T(8,128)(2,1)S(1)} custom-call(bf16[64,64]{1,0:T(8,128)(2,1)S(1)} %bitcast.163, bf16[64,128]{1,0:T(8,128)(2,1)S(1)} %pad_maximum_fusion.11.planes_t, bf16[80,2048]{1,0:T(8,128)(2,1)S(1)} %copy-done.8, bf16[384,1024]{1,0:T(8,128)(2,1)S(1)} %collective-permute-done.12.refs_0_.refs_1_.keys.vals, ...), custom_call_target="tpu_custom_call" | custom-call | flops 27499999232 | bytes 1048576 | tf_op jit(solution)/shard_map/key_backward/pallas_call | solution.py:232
  228.9 8.8 %key_backward.5 = bf16[2,192,1024]{2,1,0:T(8,128)(2,1)S(1)} custom-call(bf16[64,64]{1,0:T(8,128)(2,1)S(1)} %bitcast.164, bf16[64,128]{1,0:T(8,128)(2,1)S(1)} %pad_maximum_fusion.11.planes_t, bf16[80,2048]{1,0:T(8,128)(2,1)S(1)} %copy-done.8, bf16[384,1024]{1,0:T(8,128)(2,1)S(1)} %collective-permute-done.10.refs_0_.refs_1_.keys.vals, ...), custom_call_target="tpu_custom_call" | custom-call | flops 27499999232 | bytes 1048576 | tf_op jit(solution)/shard_map/key_backward/pallas_call | solution.py:232
  238.9 1.7 collective-permute-start.48
  243.6 8.8 %key_backward.6 = bf16[2,192,1024]{2,1,0:T(8,128)(2,1)S(1)} custom-call(bf16[64,64]{1,0:T(8,128)(2,1)S(1)} %bitcast.165, bf16[64,128]{1,0:T(8,128)(2,1)S(1)} %pad_maximum_fusion.11.planes_t, bf16[80,2048]{1,0:T(8,128)(2,1)S(1)} %copy-done.8, bf16[384,1024]{1,0:T(8,128)(2,1)S(1)} %copy-done.5, bf16[384,1024]{1,0:T(8,128)(2,1)S(1)} %copy-done.5, ...), custom_call_target="tpu_custom_call" | custom-call | flops 27499999232 | bytes 1048576 | tf_op jit(solution)/shard_map/key_backward/pallas_call | solution.py:232
  254.8 5.7 %collective-permute-done.48.refs_6_ = bf16[3,96,768]{2,1,0:T(8,128)(2,1)} collective-permute-done((bf16[3,96,768]{2,1,0:T(8,128)(2,1)}, bf16[3,96,768]{2,1,0:T(8,128)(2,1)}, u32[]{:S(2)}, u32[]{:S(2)}) %collective-permute-start.48) | collective-permute-done | bytes 442400 | tf_op jit(solution)/shard_map/ppermute | solution.py:491
  260.5 3.8 %collective-permute-start.57 = (bf16[3,96,768]{2,1,0:T(8,128)(2,1)}, bf16[3,96,768]{2,1,0:T(8,128)(2,1)S(1)}, u32[]{:S(2)}, u32[]{:S(2)}) collective-permute-start(bf16[3,96,768]{2,1,0:T(8,128)(2,1)} %collective-permute-done.49.refs_7_), channel_id=1, source_target_pairs={{0,1},{1,0},{2,3},{3,2},{4,5},{5,4},{6,7},{7,6},{8,9},{9,8},{10,11... | collective-permute-start | bytes 1327112 | tf_op jit(solution)/shard_map/ppermute | solution.py:481
  264.8 9.1 %key_backward.7 = f32[2,192,1024]{2,1,0:T(8,128)S(1)} custom-call(bf16[64,64]{1,0:T(8,128)(2,1)S(1)} %bitcast.166, bf16[64,128]{1,0:T(8,128)(2,1)S(1)} %pad_maximum_fusion.11.planes_t, bf16[80,2048]{1,0:T(8,128)(2,1)S(1)} %copy-done.8, bf16[384,1024]{1,0:T(8,128)(2,1)S(1)} %bitcast.150, bf16[384,1024]{1,0:T(8,128)(2,1)S(1)} %bitcast.151, ...), custom_call_target="tpu_custom_call" | custom-call | flops 27499999232 | bytes 1048576 | tf_op jit(solution)/shard_map/key_backward/pallas_call | solution.py:232
  273.9 6.9 %collective-permute-done.51 = bf16[192,1024]{1,0:T(8,128)(2,1)S(1)} collective-permute-done((bf16[192,1024]{1,0:T(8,128)(2,1)S(1)}, bf16[192,1024]{1,0:T(8,128)(2,1)S(1)}, u32[]{:S(2)}, u32[]{:S(2)}) %collective-permute-start.51) | collective-permute-done | bytes 393248 | tf_op jit(solution)/shard_map/ppermute | solution.py:484
  287.5 4.2 %collective-permute-start.59 = (bf16[288,768]{1,0:T(8,128)(2,1)S(1)}, bf16[288,768]{1,0:T(8,128)(2,1)S(1)}, u32[]{:S(2)}, u32[]{:S(2)}) collective-permute-start(bf16[288,768]{1,0:T(8,128)(2,1)S(1)} %constant_dynamic-slice_fusion.1), channel_id=1, source_target_pairs={{0,1},{1,0},{2,3},{3,2},{4,5},{5,4},{6,7},{7,6},{8,9},{9,8},{10,11... | collective-permute-start | bytes 1327112 | tf_op jit(solution)/shard_map/ppermute | solution.py:481
  291.7 2.7 collective-permute-done.53.refs_2_
  294.4 1.7 collective-permute-done.54.refs_3_
  296.9 5.2 %input_grad.1 = bf16[256,768]{1,0:T(8,128)(2,1)} custom-call(s32[2]{0:T(128)} %pad_add_fusion.core, f32[256,768]{1,0:T(8,128)} %get-tuple-element.184.grad_first, bf16[3,192,256]{2,1,0:T(8,128)(2,1)} %get-tuple-element.272.refs_0_, bf16[3,192,256]{2,1,0:T(8,128)(2,1)} %copy-done.52, bf16[3,192,256]{2,1,0:T(8,128)(2,1)} %copy-done.53, ...), custom_call_target="tpu_custom_call" | custom-call | flops 3300000000 | bytes 1048576 | tf_op jit(solution)/shard_map/input_grad/pallas_call | solution.py:387
  303.4 2.3 collective-permute-start.60
  305.7 17.8 %collective-permute-done.58 = bf16[128,768]{1,0:T(8,128)(2,1)S(1)} collective-permute-done((bf16[128,768]{1,0:T(8,128)(2,1)S(1)}, bf16[128,768]{1,0:T(8,128)(2,1)S(1)}, u32[]{:S(2)}, u32[]{:S(2)}) %collective-permute-start.58) | collective-permute-done | bytes 196640 | tf_op jit(solution)/shard_map/ppermute | solution.py:488
  323.6 2.1 collective-permute-start.61
  327.8 2.8 copy.59
  330.6 4.7 %collective-permute-done.64 = bf16[144,768]{1,0:T(8,128)(2,1)S(1)} collective-permute-done((bf16[144,768]{1,0:T(8,128)(2,1)S(1)}, bf16[144,768]{1,0:T(8,128)(2,1)S(1)}, u32[]{:S(2)}, u32[]{:S(2)}) %collective-permute-start.64) | collective-permute-done | bytes 221216 | tf_op jit(solution)/shard_map/ppermute | solution.py:488
  337.6 2.5 collective-permute-done.63
  342.1 5.4 %collective-permute-start.66 = (bf16[288,768]{1,0:T(8,128)(2,1)S(1)}, bf16[288,768]{1,0:T(8,128)(2,1)S(1)}, u32[]{:S(2)}, u32[]{:S(2)}) collective-permute-start(bf16[288,768]{1,0:T(8,128)(2,1)S(1)} %pad_maximum_fusion.7), channel_id=1, source_target_pairs={{0,1},{1,0},{2,3},{3,2},{4,5},{5,4},{6,7},{7,6},{8,9},{9,8},{10,11... | collective-permute-start | bytes 1327112 | tf_op jit(solution)/shard_map/ppermute | solution.py:481
  347.9 4.1 %copy.60 = f32[1,512,2,768]{3,2,1,0:T(2,128)} copy(f32[1,512,2,768]{3,1,2,0:T(8,128)S(1)} %maximum_convert_fusion) | data formatting | bytes 6291456
  356.3 2.0 copy.61
  359.5 3.0 maximum_convert_fusion.1
  (315 shorter events, 92.1 us)
Async XLA Ops:
  7.2 236.0 %reduce-scatter.4.cloned.1.call-start = ((), (), s32[]{:S(2)}) async-start(), calls=%async_computation.2 | async-start | bytes 6881280
  12.6 18.9 %collective-permute-start = (bf16[128,768]{1,0:T(8,128)(2,1)}, bf16[128,768]{1,0:T(8,128)(2,1)}, u32[]{:S(2)}, u32[]{:S(2)}) collective-permute-start(bf16[128,768]{1,0:T(8,128)(2,1)} %bitcast.145), channel_id=1, source_target_pairs={{0,16},{8,24},{16,0},{24,8},{1,17},{9,25},{17,1},{25,9},{2,18},{10... | collective-permute-start | bytes 589832 | tf_op jit(solution)/shard_map/ppermute | solution.py:488
  16.3 15.0 %collective-permute-start.1 = (bf16[8,8,64]{2,0,1:T(8,128)(2,1)}, bf16[8,8,64]{2,0,1:T(8,128)(2,1)S(1)}, u32[]{:S(2)}, u32[]{:S(2)}) collective-permute-start(bf16[8,8,64]{2,0,1:T(8,128)(2,1)} %fusion.19), channel_id=1, source_target_pairs={{0,0},{8,1},{16,8},{24,9},{1,16},{9,17},{17,24},{25,25},{2,2},{10,... | collective-permute-start | bytes 24584 | tf_op jit(solution)/shard_map/ppermute | solution.py:507
  33.1 10.2 %collective-permute-start.3 = (bf16[1,128,768]{2,1,0:T(8,128)(2,1)}, bf16[1,128,768]{2,1,0:T(8,128)(2,1)S(1)}, u32[]{:S(2)}, u32[]{:S(2)}) collective-permute-start(bf16[1,128,768]{2,1,0:T(8,128)(2,1)} %bitcast.4), channel_id=1, source_target_pairs={{0,4},{2,6},{4,0},{6,2},{1,5},{3,7},{5,1},{7,3},{8,12},{10,14},{12... | collective-permute-start | bytes 589832 | tf_op jit(solution)/shard_map/ppermute | solution.py:491
  34.3 9.9 %collective-permute-start.4 = (bf16[1,128,768]{2,1,0:T(8,128)(2,1)}, bf16[1,128,768]{2,1,0:T(8,128)(2,1)S(1)}, u32[]{:S(2)}, u32[]{:S(2)}) collective-permute-start(bf16[1,128,768]{2,1,0:T(8,128)(2,1)} %bitcast.4), channel_id=1, source_target_pairs={{0,6},{2,4},{4,2},{6,0},{1,7},{3,5},{5,3},{7,1},{8,14},{10,12},{12... | collective-permute-start | bytes 589832 | tf_op jit(solution)/shard_map/ppermute | solution.py:491
  48.7 18.5 %collective-permute-start.10 = (bf16[384,1024]{1,0:T(8,128)(2,1)S(1)}, bf16[384,1024]{1,0:T(8,128)(2,1)S(1)}, u32[]{:S(2)}, u32[]{:S(2)}) collective-permute-start(bf16[384,1024]{1,0:T(8,128)(2,1)S(1)} %bitcast.147), channel_id=1, source_target_pairs={{0,8},{8,0},{16,24},{24,16},{1,9},{9,1},{17,25},{25,17},{2,10},{10... | collective-permute-start | bytes 2359304 | tf_op jit(solution)/shard_map/ppermute | solution.py:484
  49.7 17.4 %collective-permute-start.9 = (bf16[384,768]{1,0:T(8,128)(2,1)S(1)}, bf16[384,768]{1,0:T(8,128)(2,1)S(1)}, u32[]{:S(2)}, u32[]{:S(2)}) collective-permute-start(bf16[384,768]{1,0:T(8,128)(2,1)S(1)} %bitcast.183), channel_id=1, source_target_pairs={{0,4},{2,6},{4,0},{6,2},{1,5},{3,7},{5,1},{7,3},{8,12},{10,14},{12... | collective-permute-start | bytes 1769480 | tf_op jit(solution)/shard_map/ppermute | solution.py:491
  50.9 16.2 %collective-permute-start.8 = (bf16[384,768]{1,0:T(8,128)(2,1)S(1)}, bf16[384,768]{1,0:T(8,128)(2,1)S(1)}, u32[]{:S(2)}, u32[]{:S(2)}) collective-permute-start(bf16[384,768]{1,0:T(8,128)(2,1)S(1)} %bitcast.184), channel_id=1, source_target_pairs={{0,2},{2,0},{4,6},{6,4},{1,3},{3,1},{5,7},{7,5},{8,10},{10,8},{12,... | collective-permute-start | bytes 1769480 | tf_op jit(solution)/shard_map/ppermute | solution.py:491
  67.1 13.1 %collective-permute-start.12 = (bf16[384,1024]{1,0:T(8,128)(2,1)S(1)}, bf16[384,1024]{1,0:T(8,128)(2,1)S(1)}, u32[]{:S(2)}, u32[]{:S(2)}) collective-permute-start(bf16[384,1024]{1,0:T(8,128)(2,1)S(1)} %collective-permute-done.10.refs_0_.refs_1_.keys.vals), channel_id=1, source_target_pairs={{0,1},{1,0},{2,3},{3,2},{4,5},{5,4},{6,7},{7,6},{8,9},{9,8},{10,11... | collective-permute-start | bytes 2359304 | tf_op jit(solution)/shard_map/ppermute | solution.py:481
  68.7 10.7 %collective-permute-start.7 = (bf16[192,1024]{1,0:T(8,128)(2,1)S(1)}, bf16[192,1024]{1,0:T(8,128)(2,1)S(1)}, u32[]{:S(2)}, u32[]{:S(2)}) collective-permute-start(bf16[192,1024]{1,0:T(8,128)(2,1)S(1)} %fusion.3.q.refs_0_), channel_id=1, source_target_pairs={{0,8},{8,0},{16,24},{24,16},{1,9},{9,1},{17,25},{25,17},{2,10},{10... | collective-permute-start | bytes 1179656 | tf_op jit(solution)/shard_map/ppermute | solution.py:484
  74.2 17.6 %collective-permute-start.14 = (bf16[480,768]{1,0:T(8,128)(2,1)S(1)}, bf16[480,768]{1,0:T(8,128)(2,1)S(1)}, u32[]{:S(2)}, u32[]{:S(2)}) collective-permute-start(bf16[480,768]{1,0:T(8,128)(2,1)S(1)} %copy-done.27), channel_id=1, source_target_pairs={{0,4},{2,6},{4,0},{6,2},{1,5},{3,7},{5,1},{7,3},{8,12},{10,14},{12... | collective-permute-start | bytes 2211848 | tf_op jit(solution)/shard_map/ppermute | solution.py:491
  75.5 18.9 %collective-permute-start.13 = (bf16[480,768]{1,0:T(8,128)(2,1)S(1)}, bf16[480,768]{1,0:T(8,128)(2,1)S(1)}, u32[]{:S(2)}, u32[]{:S(2)}) collective-permute-start(bf16[480,768]{1,0:T(8,128)(2,1)S(1)} %copy-done.27), channel_id=1, source_target_pairs={{0,2},{2,0},{4,6},{6,4},{1,3},{3,1},{5,7},{7,5},{8,10},{10,8},{12,... | collective-permute-start | bytes 2211848 | tf_op jit(solution)/shard_map/ppermute | solution.py:491
  79.4 13.8 %collective-permute-start.15 = (bf16[384,768]{1,0:T(8,128)(2,1)S(1)}, bf16[384,768]{1,0:T(8,128)(2,1)}, u32[]{:S(2)}, u32[]{:S(2)}) collective-permute-start(bf16[384,768]{1,0:T(8,128)(2,1)S(1)} %collective-permute-done.8.refs_6_.refs_2_), channel_id=1, source_target_pairs={{0,1},{1,0},{2,3},{3,2},{4,5},{5,4},{6,7},{7,6},{8,9},{9,8},{10,11... | collective-permute-start | bytes 1769480 | tf_op jit(solution)/shard_map/ppermute | solution.py:481
  80.3 14.1 %collective-permute-start.11 = (bf16[192,1024]{1,0:T(8,128)(2,1)S(1)}, bf16[192,1024]{1,0:T(8,128)(2,1)S(1)}, u32[]{:S(2)}, u32[]{:S(2)}) collective-permute-start(bf16[192,1024]{1,0:T(8,128)(2,1)S(1)} %collective-permute-done.7.q.refs_0_), channel_id=1, source_target_pairs={{0,1},{1,0},{2,3},{3,2},{4,5},{5,4},{6,7},{7,6},{8,9},{9,8},{10,11... | collective-permute-start | bytes 1179656 | tf_op jit(solution)/shard_map/ppermute | solution.py:481
  84.5 19.1 %collective-permute-start.5 = (bf16[192,1024]{1,0:T(8,128)(2,1)S(1)}, bf16[192,1024]{1,0:T(8,128)(2,1)S(1)}, u32[]{:S(2)}, u32[]{:S(2)}) collective-permute-start(bf16[192,1024]{1,0:T(8,128)(2,1)S(1)} %fusion.3.q.refs_0_), channel_id=1, source_target_pairs={{0,1},{1,0},{2,3},{3,2},{4,5},{5,4},{6,7},{7,6},{8,9},{9,8},{10,11... | collective-permute-start | bytes 1179656 | tf_op jit(solution)/shard_map/ppermute | solution.py:481
  93.2 19.1 %collective-permute-start.27 = (bf16[480,768]{1,0:T(8,128)(2,1)S(1)}, bf16[480,768]{1,0:T(8,128)(2,1)S(1)}, u32[]{:S(2)}, u32[]{:S(2)}) collective-permute-start(bf16[480,768]{1,0:T(8,128)(2,1)S(1)} %collective-permute-done.14.refs_16_.refs_12_), channel_id=1, source_target_pairs={{0,2},{2,0},{4,6},{6,4},{1,3},{3,1},{5,7},{7,5},{8,10},{10,8},{12,... | collective-permute-start | bytes 2211848 | tf_op jit(solution)/shard_map/ppermute | solution.py:491
  98.3 15.4 %collective-permute-start.25 = (bf16[384,768]{1,0:T(8,128)(2,1)S(1)}, bf16[384,768]{1,0:T(8,128)(2,1)S(1)}, u32[]{:S(2)}, u32[]{:S(2)}) collective-permute-start(bf16[384,768]{1,0:T(8,128)(2,1)S(1)} %collective-permute-done.8.refs_6_.refs_2_), channel_id=1, source_target_pairs={{0,4},{2,6},{4,0},{6,2},{1,5},{3,7},{5,1},{7,3},{8,12},{10,14},{12... | collective-permute-start | bytes 1769480 | tf_op jit(solution)/shard_map/ppermute | solution.py:491
  102.2 10.1 %collective-permute-start.21 = (bf16[192,1024]{1,0:T(8,128)(2,1)S(1)}, bf16[192,1024]{1,0:T(8,128)(2,1)S(1)}, u32[]{:S(2)}, u32[]{:S(2)}) collective-permute-start(bf16[192,1024]{1,0:T(8,128)(2,1)S(1)} %add_convert_fusion.5), channel_id=1, source_target_pairs={{0,8},{8,0},{16,24},{24,16},{1,9},{9,1},{17,25},{25,17},{2,10},{10... | collective-permute-start | bytes 1179656 | tf_op jit(solution)/shard_map/ppermute | solution.py:484
  135.4 23.7 %collective-permute-start.32 = (bf16[8,256,384]{2,1,0:T(8,128)(2,1)}, bf16[8,256,384]{2,1,0:T(8,128)(2,1)}, u32[]{:S(2)}, u32[]{:S(2)}) collective-permute-start(bf16[8,256,384]{2,1,0:T(8,128)(2,1)} %get-tuple-element.162), channel_id=1, source_target_pairs={{0,1},{1,0},{2,3},{3,2},{4,5},{5,4},{6,7},{7,6},{8,9},{9,8},{10,11... | collective-permute-start | bytes 4718600 | tf_op jit(solution)/shard_map/ppermute | solution.py:481
  149.2 9.9 %collective-permute-start.33 = (bf16[6,256,384]{2,1,0:T(8,128)(2,1)}, bf16[6,256,384]{2,1,0:T(8,128)(2,1)}, u32[]{:S(2)}, u32[]{:S(2)}) collective-permute-start(bf16[6,256,384]{2,1,0:T(8,128)(2,1)} %get-tuple-element.164), channel_id=1, source_target_pairs={{0,1},{1,0},{2,3},{3,2},{4,5},{5,4},{6,7},{7,6},{8,9},{9,8},{10,11... | collective-permute-start | bytes 3538952 | tf_op jit(solution)/shard_map/ppermute | solution.py:481
  155.3 12.4 %collective-permute-start.35 = (bf16[128,768]{1,0:T(8,128)(2,1)}, bf16[128,768]{1,0:T(8,128)(2,1)}, u32[]{:S(2)}, u32[]{:S(2)}) collective-permute-start(bf16[128,768]{1,0:T(8,128)(2,1)} %get-tuple-element.288), channel_id=1, source_target_pairs={{0,16},{8,24},{16,0},{24,8},{1,17},{9,25},{17,1},{25,9},{2,18},{10... | collective-permute-start | bytes 589832 | tf_op jit(solution)/shard_map/ppermute | solution.py:488
  156.4 11.3 %collective-permute-start.37 = (bf16[192,1024]{1,0:T(8,128)(2,1)S(1)}, bf16[192,1024]{1,0:T(8,128)(2,1)}, u32[]{:S(2)}, u32[]{:S(2)}) collective-permute-start(bf16[192,1024]{1,0:T(8,128)(2,1)S(1)} %constant_dynamic-update-slice_fusion.refs_2_), channel_id=1, source_target_pairs={{0,1},{1,0},{2,3},{3,2},{4,5},{5,4},{6,7},{7,6},{8,9},{9,8},{10,11... | collective-permute-start | bytes 1179656 | tf_op jit(solution)/shard_map/ppermute | solution.py:481
  157.7 34.2 %collective-permute-start.36 = (bf16[192,1024]{1,0:T(8,128)(2,1)S(1)}, bf16[192,1024]{1,0:T(8,128)(2,1)}, u32[]{:S(2)}, u32[]{:S(2)}) collective-permute-start(bf16[192,1024]{1,0:T(8,128)(2,1)S(1)} %constant_dynamic-update-slice_fusion.refs_2_), channel_id=1, source_target_pairs={{0,8},{8,0},{16,24},{24,16},{1,9},{9,1},{17,25},{25,17},{2,10},{10... | collective-permute-start | bytes 1179656 | tf_op jit(solution)/shard_map/ppermute | solution.py:484
  167.6 167.9 %all-reduce.3.cloned.1.call-start = ((), (), s32[]{:S(2)}) async-start(), calls=%async_computation.1 | async-start | bytes 2752512 | tf_op jit(solution)/shard_map/psum | solution.py:660
  191.8 15.3 %collective-permute-start.39 = (bf16[192,1024]{1,0:T(8,128)(2,1)}, bf16[192,1024]{1,0:T(8,128)(2,1)S(1)}, u32[]{:S(2)}, u32[]{:S(2)}) collective-permute-start(bf16[192,1024]{1,0:T(8,128)(2,1)} %collective-permute-done.36.refs_1_), channel_id=1, source_target_pairs={{0,1},{1,0},{2,3},{3,2},{4,5},{5,4},{6,7},{7,6},{8,9},{9,8},{10,11... | collective-permute-start | bytes 1179656 | tf_op jit(solution)/shard_map/ppermute | solution.py:481
  192.3 14.9 %collective-permute-start.38 = (bf16[192,1024]{1,0:T(8,128)(2,1)S(1)}, bf16[192,1024]{1,0:T(8,128)(2,1)S(1)}, u32[]{:S(2)}, u32[]{:S(2)}) collective-permute-start(bf16[192,1024]{1,0:T(8,128)(2,1)S(1)} %get-tuple-element.174), channel_id=1, source_target_pairs={{0,1},{1,0},{2,3},{3,2},{4,5},{5,4},{6,7},{7,6},{8,9},{9,8},{10,11... | collective-permute-start | bytes 1179656 | tf_op jit(solution)/shard_map/ppermute | solution.py:481
  204.0 33.6 %collective-permute-start.45 = (bf16[2,128,768]{2,1,0:T(8,128)(2,1)S(1)}, bf16[2,128,768]{2,1,0:T(8,128)(2,1)S(1)}, u32[]{:S(2)}, u32[]{:S(2)}) collective-permute-start(bf16[2,128,768]{2,1,0:T(8,128)(2,1)S(1)} %pad_maximum_fusion.9), channel_id=1, source_target_pairs={{0,4},{2,6},{4,0},{6,2},{1,5},{3,7},{5,1},{7,3},{8,12},{10,14},{12... | collective-permute-start | bytes 1179656 | tf_op jit(solution)/shard_map/ppermute | solution.py:491
  205.7 33.2 %collective-permute-start.44 = (bf16[2,128,768]{2,1,0:T(8,128)(2,1)S(1)}, bf16[2,128,768]{2,1,0:T(8,128)(2,1)S(1)}, u32[]{:S(2)}, u32[]{:S(2)}) collective-permute-start(bf16[2,128,768]{2,1,0:T(8,128)(2,1)S(1)} %pad_maximum_fusion.9), channel_id=1, source_target_pairs={{0,2},{2,0},{4,6},{6,4},{1,3},{3,1},{5,7},{7,5},{8,10},{10,8},{12,... | collective-permute-start | bytes 1179656 | tf_op jit(solution)/shard_map/ppermute | solution.py:491
  206.0 34.7 %collective-permute-start.46 = (bf16[2,128,768]{2,1,0:T(8,128)(2,1)S(1)}, bf16[2,128,768]{2,1,0:T(8,128)(2,1)S(1)}, u32[]{:S(2)}, u32[]{:S(2)}) collective-permute-start(bf16[2,128,768]{2,1,0:T(8,128)(2,1)S(1)} %pad_maximum_fusion.9), channel_id=1, source_target_pairs={{0,6},{2,4},{4,2},{6,0},{1,7},{3,5},{5,3},{7,1},{8,14},{10,12},{12... | collective-permute-start | bytes 1179656 | tf_op jit(solution)/shard_map/ppermute | solution.py:491
  228.2 12.5 %collective-permute-start.42 = (bf16[2,192,1024]{2,1,0:T(8,128)(2,1)S(1)}, bf16[2,192,1024]{2,1,0:T(8,128)(2,1)S(1)}, u32[]{:S(2)}, u32[]{:S(2)}) collective-permute-start(bf16[2,192,1024]{2,1,0:T(8,128)(2,1)S(1)} %key_backward.4), channel_id=1, source_target_pairs={{0,1},{1,0},{2,3},{3,2},{4,5},{5,4},{6,7},{7,6},{8,9},{9,8},{10,11... | collective-permute-start | bytes 2359304 | tf_op jit(solution)/shard_map/ppermute | solution.py:481
  228.4 12.2 %collective-permute-start.41 = (bf16[192,1024]{1,0:T(8,128)(2,1)S(1)}, bf16[192,1024]{1,0:T(8,128)(2,1)S(1)}, u32[]{:S(2)}, u32[]{:S(2)}) collective-permute-start(bf16[192,1024]{1,0:T(8,128)(2,1)S(1)} %add_convert_fusion.3), channel_id=1, source_target_pairs={{0,8},{8,0},{16,24},{24,16},{1,9},{9,1},{17,25},{25,17},{2,10},{10... | collective-permute-start | bytes 1179656 | tf_op jit(solution)/shard_map/ppermute | solution.py:484
  237.6 16.1 %collective-permute-start.49 = (bf16[3,96,768]{2,1,0:T(8,128)(2,1)}, bf16[3,96,768]{2,1,0:T(8,128)(2,1)}, u32[]{:S(2)}, u32[]{:S(2)}) collective-permute-start(bf16[3,96,768]{2,1,0:T(8,128)(2,1)} %get-tuple-element.193.refs_4_), channel_id=1, source_target_pairs={{0,6},{2,4},{4,2},{6,0},{1,7},{3,5},{5,3},{7,1},{8,14},{10,12},{12... | collective-permute-start | bytes 1327112 | tf_op jit(solution)/shard_map/ppermute | solution.py:491
  238.9 21.6 %collective-permute-start.48 = (bf16[3,96,768]{2,1,0:T(8,128)(2,1)}, bf16[3,96,768]{2,1,0:T(8,128)(2,1)}, u32[]{:S(2)}, u32[]{:S(2)}) collective-permute-start(bf16[3,96,768]{2,1,0:T(8,128)(2,1)} %get-tuple-element.193.refs_4_), channel_id=1, source_target_pairs={{0,4},{2,6},{4,0},{6,2},{1,5},{3,7},{5,1},{7,3},{8,12},{10,14},{12... | collective-permute-start | bytes 1327112 | tf_op jit(solution)/shard_map/ppermute | solution.py:491
  240.6 19.9 %collective-permute-start.47 = (bf16[3,96,768]{2,1,0:T(8,128)(2,1)}, bf16[3,96,768]{2,1,0:T(8,128)(2,1)}, u32[]{:S(2)}, u32[]{:S(2)}) collective-permute-start(bf16[3,96,768]{2,1,0:T(8,128)(2,1)} %get-tuple-element.193.refs_4_), channel_id=1, source_target_pairs={{0,2},{2,0},{4,6},{6,4},{1,3},{3,1},{5,7},{7,5},{8,10},{10,8},{12,... | collective-permute-start | bytes 1327112 | tf_op jit(solution)/shard_map/ppermute | solution.py:491
  241.9 18.6 %collective-permute-start.43 = (bf16[192,1024]{1,0:T(8,128)(2,1)}, bf16[192,1024]{1,0:T(8,128)(2,1)}, u32[]{:S(2)}, u32[]{:S(2)}) collective-permute-start(bf16[192,1024]{1,0:T(8,128)(2,1)} %get-tuple-element.281), channel_id=1, source_target_pairs={{0,8},{8,0},{16,24},{24,16},{1,9},{9,1},{17,25},{25,17},{2,10},{10... | collective-permute-start | bytes 1179656 | tf_op jit(solution)/shard_map/ppermute | solution.py:484
  252.3 28.5 %collective-permute-start.50 = (bf16[2,192,1024]{2,1,0:T(8,128)(2,1)S(1)}, bf16[2,192,1024]{2,1,0:T(8,128)(2,1)S(1)}, u32[]{:S(2)}, u32[]{:S(2)}) collective-permute-start(bf16[2,192,1024]{2,1,0:T(8,128)(2,1)S(1)} %key_backward.6), channel_id=1, source_target_pairs={{0,1},{1,0},{2,3},{3,2},{4,5},{5,4},{6,7},{7,6},{8,9},{9,8},{10,11... | collective-permute-start | bytes 2359304 | tf_op jit(solution)/shard_map/ppermute | solution.py:481
  253.7 27.1 %collective-permute-start.51 = (bf16[192,1024]{1,0:T(8,128)(2,1)S(1)}, bf16[192,1024]{1,0:T(8,128)(2,1)S(1)}, u32[]{:S(2)}, u32[]{:S(2)}) collective-permute-start(bf16[192,1024]{1,0:T(8,128)(2,1)S(1)} %copy-done.34), channel_id=1, source_target_pairs={{0,8},{8,0},{16,24},{24,16},{1,9},{9,1},{17,25},{25,17},{2,10},{10... | collective-permute-start | bytes 1179656 | tf_op jit(solution)/shard_map/ppermute | solution.py:484
  260.5 20.3 %collective-permute-start.57 = (bf16[3,96,768]{2,1,0:T(8,128)(2,1)}, bf16[3,96,768]{2,1,0:T(8,128)(2,1)S(1)}, u32[]{:S(2)}, u32[]{:S(2)}) collective-permute-start(bf16[3,96,768]{2,1,0:T(8,128)(2,1)} %collective-permute-done.49.refs_7_), channel_id=1, source_target_pairs={{0,1},{1,0},{2,3},{3,2},{4,5},{5,4},{6,7},{7,6},{8,9},{9,8},{10,11... | collective-permute-start | bytes 1327112 | tf_op jit(solution)/shard_map/ppermute | solution.py:481
  264.3 16.5 %collective-permute-start.56 = (bf16[3,96,768]{2,1,0:T(8,128)(2,1)}, bf16[3,96,768]{2,1,0:T(8,128)(2,1)S(1)}, u32[]{:S(2)}, u32[]{:S(2)}) collective-permute-start(bf16[3,96,768]{2,1,0:T(8,128)(2,1)} %collective-permute-done.48.refs_6_), channel_id=1, source_target_pairs={{0,1},{1,0},{2,3},{3,2},{4,5},{5,4},{6,7},{7,6},{8,9},{9,8},{10,11... | collective-permute-start | bytes 1327112 | tf_op jit(solution)/shard_map/ppermute | solution.py:481
  264.3 16.5 %collective-permute-start.55 = (bf16[3,96,768]{2,1,0:T(8,128)(2,1)}, bf16[3,96,768]{2,1,0:T(8,128)(2,1)S(1)}, u32[]{:S(2)}, u32[]{:S(2)}) collective-permute-start(bf16[3,96,768]{2,1,0:T(8,128)(2,1)} %collective-permute-done.47.refs_5_), channel_id=1, source_target_pairs={{0,1},{1,0},{2,3},{3,2},{4,5},{5,4},{6,7},{7,6},{8,9},{9,8},{10,11... | collective-permute-start | bytes 1327112 | tf_op jit(solution)/shard_map/ppermute | solution.py:481
  287.5 15.7 %collective-permute-start.59 = (bf16[288,768]{1,0:T(8,128)(2,1)S(1)}, bf16[288,768]{1,0:T(8,128)(2,1)S(1)}, u32[]{:S(2)}, u32[]{:S(2)}) collective-permute-start(bf16[288,768]{1,0:T(8,128)(2,1)S(1)} %constant_dynamic-slice_fusion.1), channel_id=1, source_target_pairs={{0,1},{1,0},{2,3},{3,2},{4,5},{5,4},{6,7},{7,6},{8,9},{9,8},{10,11... | collective-permute-start | bytes 1327112 | tf_op jit(solution)/shard_map/ppermute | solution.py:481
  303.1 20.3 %collective-permute-start.58 = (bf16[128,768]{1,0:T(8,128)(2,1)S(1)}, bf16[128,768]{1,0:T(8,128)(2,1)S(1)}, u32[]{:S(2)}, u32[]{:S(2)}) collective-permute-start(bf16[128,768]{1,0:T(8,128)(2,1)S(1)} %get-tuple-element.286), channel_id=1, source_target_pairs={{0,16},{8,24},{16,0},{24,8},{1,17},{9,25},{17,1},{25,9},{2,18},{10... | collective-permute-start | bytes 589832 | tf_op jit(solution)/shard_map/ppermute | solution.py:488
  303.4 20.1 %collective-permute-start.60 = (bf16[144,768]{1,0:T(8,128)(2,1)S(1)}, bf16[144,768]{1,0:T(8,128)(2,1)S(1)}, u32[]{:S(2)}, u32[]{:S(2)}) collective-permute-start(bf16[144,768]{1,0:T(8,128)(2,1)S(1)} %constant_dynamic-slice_fusion), channel_id=1, source_target_pairs={{0,8},{8,0},{16,24},{24,16},{1,9},{9,1},{17,25},{25,17},{2,10},{10... | collective-permute-start | bytes 663560 | tf_op jit(solution)/shard_map/ppermute | solution.py:484
  323.6 11.7 %collective-permute-start.64 = (bf16[144,768]{1,0:T(8,128)(2,1)S(1)}, bf16[144,768]{1,0:T(8,128)(2,1)S(1)}, u32[]{:S(2)}, u32[]{:S(2)}) collective-permute-start(bf16[144,768]{1,0:T(8,128)(2,1)S(1)} %fusion.13), channel_id=1, source_target_pairs={{0,16},{8,24},{16,0},{24,8},{1,17},{9,25},{17,1},{25,9},{2,18},{10... | collective-permute-start | bytes 663560 | tf_op jit(solution)/shard_map/ppermute | solution.py:488
  323.6 12.4 %collective-permute-start.61 = (bf16[2,128,768]{2,1,0:T(8,128)(2,1)S(1)}, bf16[2,128,768]{2,1,0:T(8,128)(2,1)S(1)}, u32[]{:S(2)}, u32[]{:S(2)}) collective-permute-start(bf16[2,128,768]{2,1,0:T(8,128)(2,1)S(1)} %pad_maximum_fusion.10), channel_id=1, source_target_pairs={{0,2},{2,0},{4,6},{6,4},{1,3},{3,1},{5,7},{7,5},{8,10},{10,8},{12,... | collective-permute-start | bytes 1179656 | tf_op jit(solution)/shard_map/ppermute | solution.py:491
  325.8 11.8 %collective-permute-start.62 = (bf16[2,128,768]{2,1,0:T(8,128)(2,1)S(1)}, bf16[2,128,768]{2,1,0:T(8,128)(2,1)}, u32[]{:S(2)}, u32[]{:S(2)}) collective-permute-start(bf16[2,128,768]{2,1,0:T(8,128)(2,1)S(1)} %pad_maximum_fusion.10), channel_id=1, source_target_pairs={{0,4},{2,6},{4,0},{6,2},{1,5},{3,7},{5,1},{7,3},{8,12},{10,14},{12... | collective-permute-start | bytes 1179656 | tf_op jit(solution)/shard_map/ppermute | solution.py:491
  325.8 14.4 %collective-permute-start.63 = (bf16[2,128,768]{2,1,0:T(8,128)(2,1)S(1)}, bf16[2,128,768]{2,1,0:T(8,128)(2,1)}, u32[]{:S(2)}, u32[]{:S(2)}) collective-permute-start(bf16[2,128,768]{2,1,0:T(8,128)(2,1)S(1)} %pad_maximum_fusion.10), channel_id=1, source_target_pairs={{0,6},{2,4},{4,2},{6,0},{1,7},{3,5},{5,3},{7,1},{8,14},{10,12},{12... | collective-permute-start | bytes 1179656 | tf_op jit(solution)/shard_map/ppermute | solution.py:491
  335.5 18.1 %collective-permute-start.67 = (bf16[896,768]{1,0:T(8,128)(2,1)}, bf16[896,768]{1,0:T(8,128)(2,1)S(1)}, u32[]{:S(2)}, u32[]{:S(2)}) collective-permute-start(bf16[896,768]{1,0:T(8,128)(2,1)} %all-reduce.3.cloned.1.call-done), channel_id=1, source_target_pairs={{0,1},{1,0},{2,3},{3,2},{4,5},{5,4},{6,7},{7,6},{8,9},{9,8},{10,11... | collective-permute-start | bytes 4128776 | tf_op jit(solution)/shard_map/ppermute | solution.py:481
  (83 other events, 579.2 us)
Sparse Core Ops, SparseCore 0:
  167.7 73.8 reduce-scatter.3
  243.9 79.9 all-reduce.2

commit v7 on v6

--- a/solution.py
+++ b/solution.py
@@ -535,7 +535,7 @@
     blocks = [dense_in]
     for j in range(1, head_count):
         here = seq_rows(lax.dynamic_slice_in_dim(own, (d ^ j) * quarter, quarter, 0), g)
-        there = after(over_head(dense_in[1:], j), up, down, *ups, *downs, grad_out, signed_t)
+        there = after(over_head(dense_in[1:], j), up, down, *ups, *downs, signed_t)
         blocks.append(jnp.concatenate([here[None], there]))
     tokens = jnp.stack(blocks).reshape(n_tokens, width)
     dense_in = dense_in.reshape(rows, width)
@@ -564,7 +564,7 @@
     w_qkv_t = w_qkv.transpose(0, 2, 1)
     qkv_near = [lax.dynamic_slice_in_dim(w_qkv_t, s * qkv_cut, qkv_cut, 1)]
     qkv_far = [lax.dynamic_slice_in_dim(w_qkv_t, (1 - s) * qkv_cut, qkv_cut, 1)]
-    tables = key_tables(after(signed, down, qkv_near[0], qkv_far[0]), [kv_z], tables, f32)
+    tables = key_tables(after(signed, down, qkv_near[0], qkv_far[0], grad_out), [kv_z], tables, f32)
 
     up_xo, up_yo = over_seq(after(up_x, tables)), over_seq(after(up_y, tables))
     q_z = after(q_z, tables)
@@ -614,19 +614,20 @@
     )
     far_back = over_seq(give_back)
     est_moved = [over_head(est_parts[j], j) for j in range(1, head_count)]
-    grad = jnp.concatenate([est_parts[0], *lax.optimization_barrier(est_moved)], axis=1)
     layer_moved = away(layer_rows)
     weight_parts = weight_grads(
-        core, after(small_a, grad), small_b, [near, far, near_back, far_back], attn_parts, heads_far
+        core, small_a, small_b, [near, far, near_back, far_back], attn_parts, heads_far
     )
 
     weight_sum = lax.psum_scatter(weight_parts, "head", scatter_dimension=0, tiled=True)[0]
-    grad_z = over_place(grad)
-    grad_o = after(over_seq(grad), weight_parts)
-    layer_moved = jnp.stack([after(x, weight_parts) for x in layer_moved])
+    est_moved = lax.optimization_barrier((*est_moved, weight_parts))[:-1]
+    grad = jnp.concatenate([est_parts[0], *est_moved], axis=1)
+    grad_z, grad_o = over_place(grad), over_seq(grad)
+    layer_moved = [after(x, weight_parts) for x in layer_moved]
     part, dq, dq_o = query_backward(
-        signed, signed_t, bits, tables, [after(q, layer_moved), q_o], [grad, grad_o], None, False, [f32, bf16]
-    )
+        signed, signed_t, bits, tables, [after(q, *layer_moved), q_o], [grad, grad_o], None, False, [f32, bf16]
+    )
+    layer_moved = jnp.stack([after(x, part) for x in layer_moved])
 
     grad_z = after(grad_z, part)
     grad_zo = over_seq(grad_z)
@@ -647,17 +648,19 @@
     dkv_zo_moved = over_seq(dkv_zo)
     dq_far = add(dq_z, after(dq_zo, dkv_zo)).astype(bf16)
     layer_moved = [layer_moved] + [over_head(layer_moved, j) for j in range(1, head_count)]
-    dkv_z = key_backward(signed, signed_t, bits, after(kv_z, dq_far), grad_tables, bf16)
+    weight_sum = after(weight_sum, dkv_zo)
+    dkv_z = key_backward(
+        signed, signed_t, bits, after(kv_z, dq_far, weight_sum), grad_tables, bf16
+    )
+    weight_sum = lax.psum(weight_sum, "hash")
     dq_far = over_place(dq_far)
 
     dkv_far = add(dkv_z, after(dkv_zo_moved, dkv_z)).astype(bf16)
     grad_q = add(dq_own, after(dq_far, dkv_z)).astype(bf16)
-    weight_sum = after(weight_sum, dkv_z)
     layer_moved = [after(x, dkv_z) for x in layer_moved]
     dkv_o = key_backward(
-        signed, signed_t, bits, after(kv_o, dkv_far, grad_q, weight_sum, *layer_moved), grad_tables, bf16
-    )
-    weight_sum = lax.psum(weight_sum, "hash")
+        signed, signed_t, bits, after(kv_o, dkv_far, grad_q, *layer_moved), grad_tables, bf16
+    )
     dk_far, dv_far = over_place(dkv_far[0]), over_place(after(dkv_far[1], dkv_o))
     qkv_half = after(qkv_near[0], dkv_z)
     qkv_moved = [over_head(qkv_half, j) for j in range(1, head_count)]

time: 375 us -> 382 us (1.019)
  starting transfers between devices: 72 us -> 83.2 us
  waiting for transfers between devices: 71.9 us -> 63 us
    ppermute x27, waiting for transfers between devices: 32.3 us -> 18.6 us  [over_head(): return lax.ppermute(x, 'head', [(h, h ^ j) for h in range(head_count)])]
    ppermute x4, waiting for transfers between devices: 22.5 us -> 11.8 us  [over_group(): return lax.ppermute(x, 'hash', moves)]
    ppermute x9, waiting for transfers between devices: 16.9 us -> 25.5 us  [over_place(): return lax.ppermute(x, 'hash', [(h, h ^ 1) for h in range(hash_count)])]
    ppermute x27, starting transfers between devices: 31.9 us -> 39.2 us  [over_seq(): return lax.ppermute(x, 'seq', [(0, 1), (1, 0)])]
    unnamed x3, waiting for transfers between devices: 0.05 us -> 6.74 us
    ppermute x4, starting transfers between devices: 4.32 us -> 10.8 us  [over_group(): return lax.ppermute(x, 'hash', moves)]
    ppermute x9, starting transfers between devices: 8.1 us -> 3.99 us  [over_place(): return lax.ppermute(x, 'hash', [(h, h ^ 1) for h in range(hash_count)])]
    unnamed x129 -> x143, local copies, waits for them, and re-layouts: 21.9 us -> 23.8 us
  transfers between devices with their start and end apart: 70 -> 70, of which waited for: 19 -> 16; matrix products, arithmetic and copies ran while one was open for 10% -> 11% of each run, Pallas kernels for 36% -> 36%
where the time goes in v7:
time: 382 us; the launch traced here: 378 us
  Pallas kernels  147 us (38%)
  starting transfers between devices  83.2 us (22%)
  waiting for transfers between devices  63 us (16%)
  local copies, waits for them, and re-layouts  40.6 us (11%)
  other arithmetic  24.5 us (6%)
  between operations  15.8 us (4%)
  matrix products  4.05 us (1%)
    pallas_call x3, Pallas kernels, query_backward(): call(partial(query_back_kernel, chunk=4, blocks=blocks, last=last), heads...  42.4 us
    ppermute x27, starting transfers between devices, over_seq(): return lax.ppermute(x, 'seq', [(0, 1), (1, 0)])  39.2 us
    pallas_call x4, Pallas kernels, single(): pl.pallas_call(kernel, in_specs=[pl.BlockSpec(memory_space=pltpu.SMEM)] +...  38.3 us
    pallas_call x4, Pallas kernels, key_backward(): call(partial(key_back_kernel, chunk=4), heads, 25, 'key_backward', [whole...  35.3 us
    ppermute x27, starting transfers between devices, over_head(): return lax.ppermute(x, 'head', [(h, h ^ j) for h in range(head_count)])  26.4 us
    ppermute x9, waiting for transfers between devices, over_place(): return lax.ppermute(x, 'hash', [(h, h ^ 1) for h in range(hash_count)])  25.5 us
    unnamed x143, local copies, waits for them, and re-layouts  23.8 us
    ppermute x27, waiting for transfers between devices, over_head(): return lax.ppermute(x, 'head', [(h, h ^ j) for h in range(head_count)])  18.6 us
  transfers between devices with their start and end apart: 70, of which 16 were waited for; matrix products, arithmetic and copies ran while one was open for 11% of the time, Pallas kernels for 36%

profile of v7, /device:TPU:1, one launch (start us, length us, event | category | flops | bytes accessed | tf_op | source)
XLA Modules:
  0.0 378.3 jit_solution(8804371777403843082)
XLA Ops:
  7.3 4.5 %constant_dynamic-slice_fusion.10 = (bf16[1,128,1,768]{3,2,1,0:T(2,128)(2,1)}, bf16[1,128,1,768]{3,2,1,0:T(2,128)(2,1)S(1)}, bf16[1,128,1,768]{3,2,1,0:T(2,128)(...) fusion(bf16[1,512,2,768]{3,2,1,0:T(2,128)(2,1)} %param.11, s32[]{:T(128)S(6)} %select_n.262, ...), kind=kLoop, calls=%fused_computation.111 | loop fusion | bytes 1966104 | tf_op jit(solution)/shard_map/jit(dynamic_index_in_dim)/dynamic_slice | solution.py:494
  12.6 3.1 collective-permute-start
  16.3 2.7 collective-permute-start.1
  19.0 2.4 constant_dynamic-slice_fusion.5
  22.6 2.0 copy_bitcast_fusion.2
  24.6 1.8 copy_bitcast_fusion
  28.9 2.2 copy.66
  31.1 2.1 copy.65
  38.0 2.3 collective-permute-done.2
  40.3 4.8 %collective-permute-done.3 = bf16[1,128,768]{2,1,0:T(8,128)(2,1)S(1)} collective-permute-done((bf16[1,128,768]{2,1,0:T(8,128)(2,1)}, bf16[1,128,768]{2,1,0:T(8,128)(2,1)S(1)}, u32[]{:S(2)}, u32[]{:S(2)}) %collective-permute-start.3) | collective-permute-done | bytes 196640 | tf_op jit(solution)/shard_map/ppermute | solution.py:491
  55.9 7.8 %key_tables.3.refs_2_ = f32[3,2048,64]{2,1,0:T(8,128)S(1)} custom-call(bf16[64,64]{1,0:T(8,128)(2,1)S(1)} %bitcast.153, bf16[384,1024]{1,0:T(8,128)(2,1)S(1)} %bitcast.148, bf16[384,1024]{1,0:T(8,128)(2,1)S(1)} %collective-permute-done.6.refs_1_.refs_3_.keys.vals, bf16[384,1024]{1,0:T(8,128)(2,1)S(1)} %bitcast.149, ...), custom_call_target="tpu_custom_call" | custom-call | flops 32999999488 | bytes 1048576 | tf_op jit(solution)/shard_map/key_tables/pallas_call | solution.py:186
  65.4 7.0 %collective-permute-done.10.refs_0_.refs_1_.keys.vals = bf16[384,1024]{1,0:T(8,128)(2,1)S(1)} collective-permute-done((bf16[384,1024]{1,0:T(8,128)(2,1)S(1)}, bf16[384,1024]{1,0:T(8,128)(2,1)S(1)}, u32[]{:S(2)}, u32[]{:S(2)}) %collective-permute-start.10) | collective-permute-done | bytes 786464 | tf_op jit(solution)/shard_map/ppermute | solution.py:484
  73.7 5.5 %key_tables.4.refs_2_ = f32[3,2048,64]{2,1,0:T(8,128)S(1)} custom-call(bf16[64,64]{1,0:T(8,128)(2,1)S(1)} %bitcast.154, bf16[384,1024]{1,0:T(8,128)(2,1)S(1)} %collective-permute-done.10.refs_0_.refs_1_.keys.vals, bf16[384,1024]{1,0:T(8,128)(2,1)S(1)} %collective-permute-done.10.refs_0_.refs_1_.keys.vals, f32[3,2048,64]{2,1,0:T(8,128)} %copy-done.13), custom_call_target="tpu_custom_call" | custom-call | flops 16499999744 | bytes 1048576 | tf_op jit(solution)/shard_map/key_tables/pallas_call | solution.py:186
  81.8 2.2 collective-permute-done.7.q.refs_0_
  84.9 4.2 %key_tables.5.tables = bf16[3,2048,64]{2,1,0:T(8,128)(2,1)S(1)} custom-call(bf16[64,64]{1,0:T(8,128)(2,1)S(1)} %bitcast.155, bf16[384,1024]{1,0:T(8,128)(2,1)S(1)} %collective-permute-done.12.refs_0_.refs_1_.keys.vals, bf16[384,1024]{1,0:T(8,128)(2,1)S(1)} %collective-permute-done.12.refs_0_.refs_1_.keys.vals, f32[3,2048,64]{2,1,0:T(8,128)S(1)} %key_tables.4.refs_2_), custom_call_target="tpu_custom_call" | custom-call | flops 16499999744 | bytes 1048576 | tf_op jit(solution)/shard_map/key_tables/pallas_call | solution.py:186
  89.7 7.2 %collective-permute-done.14.refs_16_.refs_12_ = bf16[480,768]{1,0:T(8,128)(2,1)S(1)} collective-permute-done((bf16[480,768]{1,0:T(8,128)(2,1)S(1)}, bf16[480,768]{1,0:T(8,128)(2,1)S(1)}, u32[]{:S(2)}, u32[]{:S(2)}) %collective-permute-start.14) | collective-permute-done | bytes 737312 | tf_op jit(solution)/shard_map/ppermute | solution.py:491
  99.6 3.3 query_estimates.4
  103.8 3.3 query_estimates.5
  108.4 3.3 query_estimates.6
  112.6 3.7 query_estimates.7
  127.4 12.7 %dense.1 = (bf16[256,768]{1,0:T(8,128)(2,1)}, f32[256,768]{1,0:T(8,128)}, f32[256,768]{1,0:T(8,128)}, f32[8,256,384]{2,1,0:T(8,128)}, bf16[8,256,384]{2,1,0:T(8,...) custom-call(s32[2]{0:T(128)} %pad_add_fusion.core, ...), custom_call_target="tpu_custom_call" | custom-call | flops 15399999488 | bytes 1048576 | tf_op jit(solution)/shard_map/dense/pallas_call | solution.py:387
  140.1 2.1 collective-permute-start.29
  142.3 12.0 %dense_back.1 = (f32[256,768]{1,0:T(8,128)}, bf16[6,256,384]{2,1,0:T(8,128)(2,1)}, bf16[6,256,384]{2,1,0:T(8,128)(2,1)}, bf16[192,256]{1,0:T(8,128)(2,1)}, bf16[...) custom-call(s32[2]{0:T(128)} %pad_add_fusion.core, ...), custom_call_target="tpu_custom_call" | custom-call | flops 8800000000 | bytes 1048576 | tf_op jit(solution)/shard_map/dense_back/pallas_call | solution.py:387
  160.0 8.5 %weight_grads.1 = bf16[4,896,768]{2,1,0:T(8,128)(2,1)} custom-call(s32[2]{0:T(128)} %pad_add_fusion.core, f32[8,768]{1,0:T(8,128)} %get-tuple-element.148.small_a, f32[8,768]{1,0:T(8,128)} %get-tuple-element.152.small_b, bf16[8,256,384]{2,1,0:T(8,128)(2,1)} %get-tuple-element.153.refs_0_, bf16[8,256,384]{2,1,0:T(8,128)(2,1)} %copy-done.40, ...), custom_call_target="tpu_custom_call" | custom-call | flops 7699999744 | bytes 1048576 | tf_op jit(solution)/shard_map/weight_grads/pallas_call | solution.py:387
  172.1 9.2 %collective-permute-done.32 = bf16[128,768]{1,0:T(8,128)(2,1)S(1)} collective-permute-done((bf16[128,768]{1,0:T(8,128)(2,1)S(1)}, bf16[128,768]{1,0:T(8,128)(2,1)S(1)}, u32[]{:S(2)}, u32[]{:S(2)}) %collective-permute-start.32) | collective-permute-done | bytes 196640 | tf_op jit(solution)/shard_map/ppermute | solution.py:488
  182.8 19.6 %query_backward.3 = (f32[3,2048,64]{2,1,0:T(8,128)}, f32[192,1024]{1,0:T(8,128)S(1)}, bf16[192,1024]{1,0:T(8,128)(2,1)S(1)}) custom-call(bf16[64,64]{1,0:T(8,128)(2,1)S(1)} %bitcast.160, bf16[64,128]{1,0:T(8,128)(2,1)S(1)} %pad_maximum_fusion.11.planes_t, bf16[80,2048]{1,0:T(8,128)(2,1)S(1)} %copy-done.12, bf16[3,2048,64]{2,1,0:T(8,128)(2,1)S(1)} %copy-done.15, ...), custom_call_target="tpu_custom_call" | custom-call | flops 54999998464 | bytes 1048576 | tf_op jit(solution)/shard_map/query_backward/pallas_call | solution.py:218
  203.4 11.6 %query_backward.4 = (f32[3,2048,64]{2,1,0:T(8,128)}, f32[192,1024]{1,0:T(8,128)S(1)}) custom-call(bf16[64,64]{1,0:T(8,128)(2,1)S(1)} %bitcast.161, bf16[64,128]{1,0:T(8,128)(2,1)S(1)} %pad_maximum_fusion.11.planes_t, bf16[80,2048]{1,0:T(8,128)(2,1)S(1)} %copy-done.12, bf16[3,2048,64]{2,1,0:T(8,128)(2,1)S(1)} %copy-done.15, ...), custom_call_target="tpu_custom_call" | custom-call | flops 27499999232 | bytes 1048576 | tf_op jit(solution)/shard_map/query_backward/pallas_call | solution.py:218
  217.9 11.2 %query_backward.5 = (bf16[3,2048,64]{2,1,0:T(8,128)(2,1)S(1)}, bf16[192,1024]{1,0:T(8,128)(2,1)S(1)}) custom-call(bf16[64,64]{1,0:T(8,128)(2,1)S(1)} %bitcast.162, bf16[64,128]{1,0:T(8,128)(2,1)S(1)} %pad_maximum_fusion.11.planes_t, bf16[80,2048]{1,0:T(8,128)(2,1)S(1)} %copy-done.12, bf16[3,2048,64]{2,1,0:T(8,128)(2,1)S(1)} %copy-done.15, ...), custom_call_target="tpu_custom_call" | custom-call | flops 27499999232 | bytes 1048576 | tf_op jit(solution)/shard_map/query_backward/pallas_call | solution.py:218
  230.4 8.8 %key_backward.4 = bf16[2,192,1024]{2,1,0:T(8,128)(2,1)S(1)} custom-call(bf16[64,64]{1,0:T(8,128)(2,1)S(1)} %bitcast.163, bf16[64,128]{1,0:T(8,128)(2,1)S(1)} %pad_maximum_fusion.11.planes_t, bf16[80,2048]{1,0:T(8,128)(2,1)S(1)} %copy-done.12, bf16[384,1024]{1,0:T(8,128)(2,1)S(1)} %copy-done.9, bf16[384,1024]{1,0:T(8,128)(2,1)S(1)} %copy-done.9, ...), custom_call_target="tpu_custom_call" | custom-call | flops 27499999232 | bytes 1048576 | tf_op jit(solution)/shard_map/key_backward/pallas_call | solution.py:232
  240.1 6.7 %reduce-scatter.4.cloned.1.call-done = bf16[1,896,768]{2,1,0:T(8,128)(2,1)} async-done(((bf16[4,896,768]{2,1,0:T(8,128)(2,1)}), bf16[1,896,768]{2,1,0:T(8,128)(2,1)}) %reduce-scatter.4.cloned.1.call-update) | async-done | bytes 1376272
  248.3 8.8 %key_backward.5 = bf16[2,192,1024]{2,1,0:T(8,128)(2,1)S(1)} custom-call(bf16[64,64]{1,0:T(8,128)(2,1)S(1)} %bitcast.164, bf16[64,128]{1,0:T(8,128)(2,1)S(1)} %pad_maximum_fusion.11.planes_t, bf16[80,2048]{1,0:T(8,128)(2,1)S(1)} %copy-done.12, bf16[384,1024]{1,0:T(8,128)(2,1)S(1)} %copy-done.7, bf16[384,1024]{1,0:T(8,128)(2,1)S(1)} %copy-done.7, ...), custom_call_target="tpu_custom_call" | custom-call | flops 27499999232 | bytes 1048576 | tf_op jit(solution)/shard_map/key_backward/pallas_call | solution.py:232
  258.2 4.9 %collective-permute-start.49 = (bf16[3,96,768]{2,1,0:T(8,128)(2,1)S(1)}, bf16[3,96,768]{2,1,0:T(8,128)(2,1)S(1)}, u32[]{:S(2)}, u32[]{:S(2)}) collective-permute-start(bf16[3,96,768]{2,1,0:T(8,128)(2,1)S(1)} %copy-done.33), channel_id=1, source_target_pairs={{0,6},{2,4},{4,2},{6,0},{1,7},{3,5},{5,3},{7,1},{8,14},{10,12},{12... | collective-permute-start | bytes 1327112 | tf_op jit(solution)/shard_map/ppermute | solution.py:491
  265.2 8.7 %key_backward.6 = bf16[2,192,1024]{2,1,0:T(8,128)(2,1)S(1)} custom-call(bf16[64,64]{1,0:T(8,128)(2,1)S(1)} %bitcast.165, bf16[64,128]{1,0:T(8,128)(2,1)S(1)} %pad_maximum_fusion.11.planes_t, bf16[80,2048]{1,0:T(8,128)(2,1)S(1)} %copy-done.12, bf16[384,1024]{1,0:T(8,128)(2,1)S(1)} %copy-done.5, bf16[384,1024]{1,0:T(8,128)(2,1)S(1)} %copy-done.5, ...), custom_call_target="tpu_custom_call" | custom-call | flops 27499999232 | bytes 1048576 | tf_op jit(solution)/shard_map/key_backward/pallas_call | solution.py:232
  275.6 13.0 %collective-permute-done.43 = bf16[192,1024]{1,0:T(8,128)(2,1)S(1)} collective-permute-done((bf16[192,1024]{1,0:T(8,128)(2,1)S(1)}, bf16[192,1024]{1,0:T(8,128)(2,1)S(1)}, u32[]{:S(2)}, u32[]{:S(2)}) %collective-permute-start.43) | collective-permute-done | bytes 393248 | tf_op jit(solution)/shard_map/ppermute | solution.py:484
  289.8 9.1 %key_backward.7 = f32[2,192,1024]{2,1,0:T(8,128)S(1)} custom-call(bf16[64,64]{1,0:T(8,128)(2,1)S(1)} %bitcast.166, bf16[64,128]{1,0:T(8,128)(2,1)S(1)} %pad_maximum_fusion.11.planes_t, bf16[80,2048]{1,0:T(8,128)(2,1)S(1)} %copy-done.12, bf16[384,1024]{1,0:T(8,128)(2,1)S(1)} %bitcast.150, bf16[384,1024]{1,0:T(8,128)(2,1)S(1)} %bitcast.151, ...), custom_call_target="tpu_custom_call" | custom-call | flops 27499999232 | bytes 1048576 | tf_op jit(solution)/shard_map/key_backward/pallas_call | solution.py:232
  304.1 7.0 %collective-permute-start.59 = (bf16[288,768]{1,0:T(8,128)(2,1)S(1)}, bf16[288,768]{1,0:T(8,128)(2,1)S(1)}, u32[]{:S(2)}, u32[]{:S(2)}) collective-permute-start(bf16[288,768]{1,0:T(8,128)(2,1)S(1)} %constant_dynamic-slice_fusion.1), channel_id=1, source_target_pairs={{0,1},{1,0},{2,3},{3,2},{4,5},{5,4},{6,7},{7,6},{8,9},{9,8},{10,11... | collective-permute-start | bytes 1327112 | tf_op jit(solution)/shard_map/ppermute | solution.py:481
  312.2 5.1 %input_grad.1 = bf16[256,768]{1,0:T(8,128)(2,1)} custom-call(s32[2]{0:T(128)} %pad_add_fusion.core, f32[256,768]{1,0:T(8,128)} %get-tuple-element.185.grad_first, bf16[3,192,256]{2,1,0:T(8,128)(2,1)} %get-tuple-element.272.refs_0_, bf16[3,192,256]{2,1,0:T(8,128)(2,1)} %copy-done.59, bf16[3,192,256]{2,1,0:T(8,128)(2,1)} %copy-done.60, ...), custom_call_target="tpu_custom_call" | custom-call | flops 3300000000 | bytes 1048576 | tf_op jit(solution)/shard_map/input_grad/pallas_call | solution.py:387
  318.4 3.7 collective-permute-start.58
  322.6 2.6 collective-permute-done.58
  325.3 2.3 collective-permute-done.60
  327.6 3.0 collective-permute-start.64
  330.6 1.8 collective-permute-start.61
  335.7 2.8 copy.59
  338.6 11.4 %collective-permute-start.67 = (bf16[896,768]{1,0:T(8,128)(2,1)}, bf16[896,768]{1,0:T(8,128)(2,1)S(1)}, u32[]{:S(2)}, u32[]{:S(2)}) collective-permute-start(bf16[896,768]{1,0:T(8,128)(2,1)} %all-reduce.3.cloned.1.call-done), channel_id=1, source_target_pairs={{0,1},{1,0},{2,3},{3,2},{4,5},{5,4},{6,7},{7,6},{8,9},{9,8},{10,11... | collective-permute-start | bytes 4128776 | tf_op jit(solution)/shard_map/ppermute | solution.py:481
  350.6 3.5 collective-permute-start.66
  354.5 4.1 %copy.60 = f32[1,512,2,768]{3,2,1,0:T(2,128)} copy(f32[1,512,2,768]{3,1,2,0:T(8,128)S(1)} %maximum_convert_fusion) | data formatting | bytes 6291456
  362.9 2.0 copy.61
  366.1 3.0 maximum_convert_fusion.1
  (329 shorter events, 87.8 us)
Async XLA Ops:
  7.2 239.6 %reduce-scatter.4.cloned.1.call-start = ((), (), s32[]{:S(2)}) async-start(), calls=%async_computation.2 | async-start | bytes 6881280
  12.6 20.7 %collective-permute-start = (bf16[128,768]{1,0:T(8,128)(2,1)}, bf16[128,768]{1,0:T(8,128)(2,1)}, u32[]{:S(2)}, u32[]{:S(2)}) collective-permute-start(bf16[128,768]{1,0:T(8,128)(2,1)} %bitcast.145), channel_id=1, source_target_pairs={{0,16},{8,24},{16,0},{24,8},{1,17},{9,25},{17,1},{25,9},{2,18},{10... | collective-permute-start | bytes 589832 | tf_op jit(solution)/shard_map/ppermute | solution.py:488
  16.3 16.9 %collective-permute-start.1 = (bf16[8,8,64]{2,0,1:T(8,128)(2,1)}, bf16[8,8,64]{2,0,1:T(8,128)(2,1)S(1)}, u32[]{:S(2)}, u32[]{:S(2)}) collective-permute-start(bf16[8,8,64]{2,0,1:T(8,128)(2,1)} %fusion.19), channel_id=1, source_target_pairs={{0,0},{8,1},{16,8},{24,9},{1,16},{9,17},{17,24},{25,25},{2,2},{10,... | collective-permute-start | bytes 24584 | tf_op jit(solution)/shard_map/ppermute | solution.py:507
  53.2 19.2 %collective-permute-start.10 = (bf16[384,1024]{1,0:T(8,128)(2,1)S(1)}, bf16[384,1024]{1,0:T(8,128)(2,1)S(1)}, u32[]{:S(2)}, u32[]{:S(2)}) collective-permute-start(bf16[384,1024]{1,0:T(8,128)(2,1)S(1)} %bitcast.147), channel_id=1, source_target_pairs={{0,8},{8,0},{16,24},{24,16},{1,9},{9,1},{17,25},{25,17},{2,10},{10... | collective-permute-start | bytes 2359304 | tf_op jit(solution)/shard_map/ppermute | solution.py:484
  54.3 18.1 %collective-permute-start.9 = (bf16[384,768]{1,0:T(8,128)(2,1)S(1)}, bf16[384,768]{1,0:T(8,128)(2,1)S(1)}, u32[]{:S(2)}, u32[]{:S(2)}) collective-permute-start(bf16[384,768]{1,0:T(8,128)(2,1)S(1)} %bitcast.183), channel_id=1, source_target_pairs={{0,4},{2,6},{4,0},{6,2},{1,5},{3,7},{5,1},{7,3},{8,12},{10,14},{12... | collective-permute-start | bytes 1769480 | tf_op jit(solution)/shard_map/ppermute | solution.py:491
  55.6 16.8 %collective-permute-start.8 = (bf16[384,768]{1,0:T(8,128)(2,1)S(1)}, bf16[384,768]{1,0:T(8,128)(2,1)S(1)}, u32[]{:S(2)}, u32[]{:S(2)}) collective-permute-start(bf16[384,768]{1,0:T(8,128)(2,1)S(1)} %bitcast.184), channel_id=1, source_target_pairs={{0,2},{2,0},{4,6},{6,4},{1,3},{3,1},{5,7},{7,5},{8,10},{10,8},{12,... | collective-permute-start | bytes 1769480 | tf_op jit(solution)/shard_map/ppermute | solution.py:491
  72.4 12.4 %collective-permute-start.12 = (bf16[384,1024]{1,0:T(8,128)(2,1)S(1)}, bf16[384,1024]{1,0:T(8,128)(2,1)S(1)}, u32[]{:S(2)}, u32[]{:S(2)}) collective-permute-start(bf16[384,1024]{1,0:T(8,128)(2,1)S(1)} %collective-permute-done.10.refs_0_.refs_1_.keys.vals), channel_id=1, source_target_pairs={{0,1},{1,0},{2,3},{3,2},{4,5},{5,4},{6,7},{7,6},{8,9},{9,8},{10,11... | collective-permute-start | bytes 2359304 | tf_op jit(solution)/shard_map/ppermute | solution.py:481
  73.3 10.7 %collective-permute-start.7 = (bf16[192,1024]{1,0:T(8,128)(2,1)S(1)}, bf16[192,1024]{1,0:T(8,128)(2,1)S(1)}, u32[]{:S(2)}, u32[]{:S(2)}) collective-permute-start(bf16[192,1024]{1,0:T(8,128)(2,1)S(1)} %fusion.3.q.refs_0_), channel_id=1, source_target_pairs={{0,8},{8,0},{16,24},{24,16},{1,9},{9,1},{17,25},{25,17},{2,10},{10... | collective-permute-start | bytes 1179656 | tf_op jit(solution)/shard_map/ppermute | solution.py:484
  79.2 17.7 %collective-permute-start.14 = (bf16[480,768]{1,0:T(8,128)(2,1)S(1)}, bf16[480,768]{1,0:T(8,128)(2,1)S(1)}, u32[]{:S(2)}, u32[]{:S(2)}) collective-permute-start(bf16[480,768]{1,0:T(8,128)(2,1)S(1)} %copy-done.31), channel_id=1, source_target_pairs={{0,4},{2,6},{4,0},{6,2},{1,5},{3,7},{5,1},{7,3},{8,12},{10,14},{12... | collective-permute-start | bytes 2211848 | tf_op jit(solution)/shard_map/ppermute | solution.py:491
  80.5 18.6 %collective-permute-start.13 = (bf16[480,768]{1,0:T(8,128)(2,1)S(1)}, bf16[480,768]{1,0:T(8,128)(2,1)S(1)}, u32[]{:S(2)}, u32[]{:S(2)}) collective-permute-start(bf16[480,768]{1,0:T(8,128)(2,1)S(1)} %copy-done.31), channel_id=1, source_target_pairs={{0,2},{2,0},{4,6},{6,4},{1,3},{3,1},{5,7},{7,5},{8,10},{10,8},{12,... | collective-permute-start | bytes 2211848 | tf_op jit(solution)/shard_map/ppermute | solution.py:491
  84.0 14.2 %collective-permute-start.15 = (bf16[384,768]{1,0:T(8,128)(2,1)S(1)}, bf16[384,768]{1,0:T(8,128)(2,1)}, u32[]{:S(2)}, u32[]{:S(2)}) collective-permute-start(bf16[384,768]{1,0:T(8,128)(2,1)S(1)} %collective-permute-done.8.refs_6_.refs_2_), channel_id=1, source_target_pairs={{0,1},{1,0},{2,3},{3,2},{4,5},{5,4},{6,7},{7,6},{8,9},{9,8},{10,11... | collective-permute-start | bytes 1769480 | tf_op jit(solution)/shard_map/ppermute | solution.py:481
  84.8 14.3 %collective-permute-start.11 = (bf16[192,1024]{1,0:T(8,128)(2,1)S(1)}, bf16[192,1024]{1,0:T(8,128)(2,1)S(1)}, u32[]{:S(2)}, u32[]{:S(2)}) collective-permute-start(bf16[192,1024]{1,0:T(8,128)(2,1)S(1)} %collective-permute-done.7.q.refs_0_), channel_id=1, source_target_pairs={{0,1},{1,0},{2,3},{3,2},{4,5},{5,4},{6,7},{7,6},{8,9},{9,8},{10,11... | collective-permute-start | bytes 1179656 | tf_op jit(solution)/shard_map/ppermute | solution.py:481
  89.2 19.1 %collective-permute-start.5 = (bf16[192,1024]{1,0:T(8,128)(2,1)S(1)}, bf16[192,1024]{1,0:T(8,128)(2,1)S(1)}, u32[]{:S(2)}, u32[]{:S(2)}) collective-permute-start(bf16[192,1024]{1,0:T(8,128)(2,1)S(1)} %fusion.3.q.refs_0_), channel_id=1, source_target_pairs={{0,1},{1,0},{2,3},{3,2},{4,5},{5,4},{6,7},{7,6},{8,9},{9,8},{10,11... | collective-permute-start | bytes 1179656 | tf_op jit(solution)/shard_map/ppermute | solution.py:481
  98.2 19.1 %collective-permute-start.27 = (bf16[480,768]{1,0:T(8,128)(2,1)S(1)}, bf16[480,768]{1,0:T(8,128)(2,1)S(1)}, u32[]{:S(2)}, u32[]{:S(2)}) collective-permute-start(bf16[480,768]{1,0:T(8,128)(2,1)S(1)} %collective-permute-done.14.refs_16_.refs_12_), channel_id=1, source_target_pairs={{0,2},{2,0},{4,6},{6,4},{1,3},{3,1},{5,7},{7,5},{8,10},{10,8},{12,... | collective-permute-start | bytes 2211848 | tf_op jit(solution)/shard_map/ppermute | solution.py:491
  103.2 15.7 %collective-permute-start.25 = (bf16[384,768]{1,0:T(8,128)(2,1)S(1)}, bf16[384,768]{1,0:T(8,128)(2,1)S(1)}, u32[]{:S(2)}, u32[]{:S(2)}) collective-permute-start(bf16[384,768]{1,0:T(8,128)(2,1)S(1)} %collective-permute-done.8.refs_6_.refs_2_), channel_id=1, source_target_pairs={{0,4},{2,6},{4,0},{6,2},{1,5},{3,7},{5,1},{7,3},{8,12},{10,14},{12... | collective-permute-start | bytes 1769480 | tf_op jit(solution)/shard_map/ppermute | solution.py:491
  140.1 18.4 %collective-permute-start.29 = (bf16[8,256,384]{2,1,0:T(8,128)(2,1)}, bf16[8,256,384]{2,1,0:T(8,128)(2,1)S(1)}, u32[]{:S(2)}, u32[]{:S(2)}) collective-permute-start(bf16[8,256,384]{2,1,0:T(8,128)(2,1)} %get-tuple-element.154), channel_id=1, source_target_pairs={{0,1},{1,0},{2,3},{3,2},{4,5},{5,4},{6,7},{7,6},{8,9},{9,8},{10,11... | collective-permute-start | bytes 4718600 | tf_op jit(solution)/shard_map/ppermute | solution.py:481
  154.9 13.7 %collective-permute-start.33 = (bf16[192,256]{1,0:T(8,128)(2,1)}, bf16[192,256]{1,0:T(8,128)(2,1)S(1)}, u32[]{:S(2)}, u32[]{:S(2)}) collective-permute-start(bf16[192,256]{1,0:T(8,128)(2,1)} %get-tuple-element.162), channel_id=1, source_target_pairs={{0,2},{2,0},{4,6},{6,4},{1,3},{3,1},{5,7},{7,5},{8,10},{10,8},{12,... | collective-permute-start | bytes 294920 | tf_op jit(solution)/shard_map/ppermute | solution.py:491
  155.1 13.4 %collective-permute-start.34 = (bf16[192,256]{1,0:T(8,128)(2,1)}, bf16[192,256]{1,0:T(8,128)(2,1)S(1)}, u32[]{:S(2)}, u32[]{:S(2)}) collective-permute-start(bf16[192,256]{1,0:T(8,128)(2,1)} %get-tuple-element.163), channel_id=1, source_target_pairs={{0,4},{2,6},{4,0},{6,2},{1,5},{3,7},{5,1},{7,3},{8,12},{10,14},{12... | collective-permute-start | bytes 294920 | tf_op jit(solution)/shard_map/ppermute | solution.py:491
  157.1 11.4 %collective-permute-start.35 = (bf16[192,256]{1,0:T(8,128)(2,1)}, bf16[192,256]{1,0:T(8,128)(2,1)S(1)}, u32[]{:S(2)}, u32[]{:S(2)}) collective-permute-start(bf16[192,256]{1,0:T(8,128)(2,1)} %get-tuple-element.164), channel_id=1, source_target_pairs={{0,6},{2,4},{4,2},{6,0},{1,7},{3,5},{5,3},{7,1},{8,14},{10,12},{12... | collective-permute-start | bytes 294920 | tf_op jit(solution)/shard_map/ppermute | solution.py:491
  168.6 12.7 %collective-permute-start.36 = (bf16[192,1024]{1,0:T(8,128)(2,1)S(1)}, bf16[192,1024]{1,0:T(8,128)(2,1)S(1)}, u32[]{:S(2)}, u32[]{:S(2)}) collective-permute-start(bf16[192,1024]{1,0:T(8,128)(2,1)S(1)} %constant_dynamic-update-slice_fusion.refs_2_), channel_id=1, source_target_pairs={{0,1},{1,0},{2,3},{3,2},{4,5},{5,4},{6,7},{7,6},{8,9},{9,8},{10,11... | collective-permute-start | bytes 1179656 | tf_op jit(solution)/shard_map/ppermute | solution.py:481
  169.6 11.7 %collective-permute-start.32 = (bf16[128,768]{1,0:T(8,128)(2,1)S(1)}, bf16[128,768]{1,0:T(8,128)(2,1)S(1)}, u32[]{:S(2)}, u32[]{:S(2)}) collective-permute-start(bf16[128,768]{1,0:T(8,128)(2,1)S(1)} %get-tuple-element.288), channel_id=1, source_target_pairs={{0,16},{8,24},{16,0},{24,8},{1,17},{9,25},{17,1},{25,9},{2,18},{10... | collective-permute-start | bytes 589832 | tf_op jit(solution)/shard_map/ppermute | solution.py:488
  170.6 31.9 %collective-permute-start.37 = (bf16[192,1024]{1,0:T(8,128)(2,1)S(1)}, bf16[192,1024]{1,0:T(8,128)(2,1)S(1)}, u32[]{:S(2)}, u32[]{:S(2)}) collective-permute-start(bf16[192,1024]{1,0:T(8,128)(2,1)S(1)} %constant_dynamic-update-slice_fusion.refs_2_), channel_id=1, source_target_pairs={{0,8},{8,0},{16,24},{24,16},{1,9},{9,1},{17,25},{25,17},{2,10},{10... | collective-permute-start | bytes 1179656 | tf_op jit(solution)/shard_map/ppermute | solution.py:484
  172.0 166.6 %all-reduce.3.cloned.1.call-start = ((), (), s32[]{:S(2)}) async-start(), calls=%async_computation.1 | async-start | bytes 2752512 | tf_op jit(solution)/shard_map/psum | solution.py:655
  202.4 15.3 %collective-permute-start.39 = (bf16[192,1024]{1,0:T(8,128)(2,1)S(1)}, bf16[192,1024]{1,0:T(8,128)(2,1)S(1)}, u32[]{:S(2)}, u32[]{:S(2)}) collective-permute-start(bf16[192,1024]{1,0:T(8,128)(2,1)S(1)} %collective-permute-done.37.refs_1_), channel_id=1, source_target_pairs={{0,1},{1,0},{2,3},{3,2},{4,5},{5,4},{6,7},{7,6},{8,9},{9,8},{10,11... | collective-permute-start | bytes 1179656 | tf_op jit(solution)/shard_map/ppermute | solution.py:481
  203.3 14.4 %collective-permute-start.38 = (bf16[192,1024]{1,0:T(8,128)(2,1)S(1)}, bf16[192,1024]{1,0:T(8,128)(2,1)S(1)}, u32[]{:S(2)}, u32[]{:S(2)}) collective-permute-start(bf16[192,1024]{1,0:T(8,128)(2,1)S(1)} %get-tuple-element.174), channel_id=1, source_target_pairs={{0,1},{1,0},{2,3},{3,2},{4,5},{5,4},{6,7},{7,6},{8,9},{9,8},{10,11... | collective-permute-start | bytes 1179656 | tf_op jit(solution)/shard_map/ppermute | solution.py:481
  215.0 48.1 %collective-permute-start.45 = (bf16[2,128,768]{2,1,0:T(8,128)(2,1)S(1)}, bf16[2,128,768]{2,1,0:T(8,128)(2,1)}, u32[]{:S(2)}, u32[]{:S(2)}) collective-permute-start(bf16[2,128,768]{2,1,0:T(8,128)(2,1)S(1)} %pad_maximum_fusion.9), channel_id=1, source_target_pairs={{0,4},{2,6},{4,0},{6,2},{1,5},{3,7},{5,1},{7,3},{8,12},{10,14},{12... | collective-permute-start | bytes 1179656 | tf_op jit(solution)/shard_map/ppermute | solution.py:491
  215.6 47.5 %collective-permute-start.44 = (bf16[2,128,768]{2,1,0:T(8,128)(2,1)S(1)}, bf16[2,128,768]{2,1,0:T(8,128)(2,1)}, u32[]{:S(2)}, u32[]{:S(2)}) collective-permute-start(bf16[2,128,768]{2,1,0:T(8,128)(2,1)S(1)} %pad_maximum_fusion.9), channel_id=1, source_target_pairs={{0,2},{2,0},{4,6},{6,4},{1,3},{3,1},{5,7},{7,5},{8,10},{10,8},{12,... | collective-permute-start | bytes 1179656 | tf_op jit(solution)/shard_map/ppermute | solution.py:491
  216.3 48.7 %collective-permute-start.46 = (bf16[2,128,768]{2,1,0:T(8,128)(2,1)S(1)}, bf16[2,128,768]{2,1,0:T(8,128)(2,1)}, u32[]{:S(2)}, u32[]{:S(2)}) collective-permute-start(bf16[2,128,768]{2,1,0:T(8,128)(2,1)S(1)} %pad_maximum_fusion.9), channel_id=1, source_target_pairs={{0,6},{2,4},{4,2},{6,0},{1,7},{3,5},{5,3},{7,1},{8,14},{10,12},{12... | collective-permute-start | bytes 1179656 | tf_op jit(solution)/shard_map/ppermute | solution.py:491
  229.1 10.2 %collective-permute-start.40 = (bf16[192,1024]{1,0:T(8,128)(2,1)S(1)}, bf16[192,1024]{1,0:T(8,128)(2,1)S(1)}, u32[]{:S(2)}, u32[]{:S(2)}) collective-permute-start(bf16[192,1024]{1,0:T(8,128)(2,1)S(1)} %get-tuple-element.179), channel_id=1, source_target_pairs={{0,1},{1,0},{2,3},{3,2},{4,5},{5,4},{6,7},{7,6},{8,9},{9,8},{10,11... | collective-permute-start | bytes 1179656 | tf_op jit(solution)/shard_map/ppermute | solution.py:481
  239.2 24.4 %collective-permute-start.42 = (bf16[2,192,1024]{2,1,0:T(8,128)(2,1)S(1)}, bf16[2,192,1024]{2,1,0:T(8,128)(2,1)}, u32[]{:S(2)}, u32[]{:S(2)}) collective-permute-start(bf16[2,192,1024]{2,1,0:T(8,128)(2,1)S(1)} %key_backward.4), channel_id=1, source_target_pairs={{0,1},{1,0},{2,3},{3,2},{4,5},{5,4},{6,7},{7,6},{8,9},{9,8},{10,11... | collective-permute-start | bytes 2359304 | tf_op jit(solution)/shard_map/ppermute | solution.py:481
  240.1 16.9 %collective-permute-start.41 = (bf16[192,1024]{1,0:T(8,128)(2,1)}, bf16[192,1024]{1,0:T(8,128)(2,1)}, u32[]{:S(2)}, u32[]{:S(2)}) collective-permute-start(bf16[192,1024]{1,0:T(8,128)(2,1)} %add_convert_fusion.3), channel_id=1, source_target_pairs={{0,8},{8,0},{16,24},{24,16},{1,9},{9,1},{17,25},{25,17},{2,10},{10... | collective-permute-start | bytes 1179656 | tf_op jit(solution)/shard_map/ppermute | solution.py:484
  258.2 30.4 %collective-permute-start.49 = (bf16[3,96,768]{2,1,0:T(8,128)(2,1)S(1)}, bf16[3,96,768]{2,1,0:T(8,128)(2,1)S(1)}, u32[]{:S(2)}, u32[]{:S(2)}) collective-permute-start(bf16[3,96,768]{2,1,0:T(8,128)(2,1)S(1)} %copy-done.33), channel_id=1, source_target_pairs={{0,6},{2,4},{4,2},{6,0},{1,7},{3,5},{5,3},{7,1},{8,14},{10,12},{12... | collective-permute-start | bytes 1327112 | tf_op jit(solution)/shard_map/ppermute | solution.py:491
  263.1 25.5 %collective-permute-start.48 = (bf16[3,96,768]{2,1,0:T(8,128)(2,1)S(1)}, bf16[3,96,768]{2,1,0:T(8,128)(2,1)S(1)}, u32[]{:S(2)}, u32[]{:S(2)}) collective-permute-start(bf16[3,96,768]{2,1,0:T(8,128)(2,1)S(1)} %copy-done.33), channel_id=1, source_target_pairs={{0,4},{2,6},{4,0},{6,2},{1,5},{3,7},{5,1},{7,3},{8,12},{10,14},{12... | collective-permute-start | bytes 1327112 | tf_op jit(solution)/shard_map/ppermute | solution.py:491
  263.2 25.5 %collective-permute-start.47 = (bf16[3,96,768]{2,1,0:T(8,128)(2,1)S(1)}, bf16[3,96,768]{2,1,0:T(8,128)(2,1)S(1)}, u32[]{:S(2)}, u32[]{:S(2)}) collective-permute-start(bf16[3,96,768]{2,1,0:T(8,128)(2,1)S(1)} %copy-done.33), channel_id=1, source_target_pairs={{0,2},{2,0},{4,6},{6,4},{1,3},{3,1},{5,7},{7,5},{8,10},{10,8},{12,... | collective-permute-start | bytes 1327112 | tf_op jit(solution)/shard_map/ppermute | solution.py:491
  265.1 23.6 %collective-permute-start.43 = (bf16[192,1024]{1,0:T(8,128)(2,1)S(1)}, bf16[192,1024]{1,0:T(8,128)(2,1)S(1)}, u32[]{:S(2)}, u32[]{:S(2)}) collective-permute-start(bf16[192,1024]{1,0:T(8,128)(2,1)S(1)} %get-tuple-element.281), channel_id=1, source_target_pairs={{0,8},{8,0},{16,24},{24,16},{1,9},{9,1},{17,25},{25,17},{2,10},{10... | collective-permute-start | bytes 1179656 | tf_op jit(solution)/shard_map/ppermute | solution.py:484
  274.0 25.0 %collective-permute-start.50 = (bf16[2,192,1024]{2,1,0:T(8,128)(2,1)S(1)}, bf16[2,192,1024]{2,1,0:T(8,128)(2,1)S(1)}, u32[]{:S(2)}, u32[]{:S(2)}) collective-permute-start(bf16[2,192,1024]{2,1,0:T(8,128)(2,1)S(1)} %key_backward.6), channel_id=1, source_target_pairs={{0,1},{1,0},{2,3},{3,2},{4,5},{5,4},{6,7},{7,6},{8,9},{9,8},{10,11... | collective-permute-start | bytes 2359304 | tf_op jit(solution)/shard_map/ppermute | solution.py:481
  288.6 10.3 %collective-permute-start.51 = (bf16[192,1024]{1,0:T(8,128)(2,1)S(1)}, bf16[192,1024]{1,0:T(8,128)(2,1)S(1)}, u32[]{:S(2)}, u32[]{:S(2)}) collective-permute-start(bf16[192,1024]{1,0:T(8,128)(2,1)S(1)} %get-tuple-element.199), channel_id=1, source_target_pairs={{0,8},{8,0},{16,24},{24,16},{1,9},{9,1},{17,25},{25,17},{2,10},{10... | collective-permute-start | bytes 1179656 | tf_op jit(solution)/shard_map/ppermute | solution.py:484
  288.7 14.0 %collective-permute-start.57 = (bf16[3,96,768]{2,1,0:T(8,128)(2,1)S(1)}, bf16[3,96,768]{2,1,0:T(8,128)(2,1)S(1)}, u32[]{:S(2)}, u32[]{:S(2)}) collective-permute-start(bf16[3,96,768]{2,1,0:T(8,128)(2,1)S(1)} %collective-permute-done.49.refs_7_), channel_id=1, source_target_pairs={{0,1},{1,0},{2,3},{3,2},{4,5},{5,4},{6,7},{7,6},{8,9},{9,8},{10,11... | collective-permute-start | bytes 1327112 | tf_op jit(solution)/shard_map/ppermute | solution.py:481
  289.3 14.8 %collective-permute-start.56 = (bf16[3,96,768]{2,1,0:T(8,128)(2,1)S(1)}, bf16[3,96,768]{2,1,0:T(8,128)(2,1)S(1)}, u32[]{:S(2)}, u32[]{:S(2)}) collective-permute-start(bf16[3,96,768]{2,1,0:T(8,128)(2,1)S(1)} %collective-permute-done.48.refs_6_), channel_id=1, source_target_pairs={{0,1},{1,0},{2,3},{3,2},{4,5},{5,4},{6,7},{7,6},{8,9},{9,8},{10,11... | collective-permute-start | bytes 1327112 | tf_op jit(solution)/shard_map/ppermute | solution.py:481
  289.4 21.7 %collective-permute-start.55 = (bf16[3,96,768]{2,1,0:T(8,128)(2,1)S(1)}, bf16[3,96,768]{2,1,0:T(8,128)(2,1)S(1)}, u32[]{:S(2)}, u32[]{:S(2)}) collective-permute-start(bf16[3,96,768]{2,1,0:T(8,128)(2,1)S(1)} %collective-permute-done.47.refs_5_), channel_id=1, source_target_pairs={{0,1},{1,0},{2,3},{3,2},{4,5},{5,4},{6,7},{7,6},{8,9},{9,8},{10,11... | collective-permute-start | bytes 1327112 | tf_op jit(solution)/shard_map/ppermute | solution.py:481
  300.3 10.8 %collective-permute-start.52 = (bf16[3,192,256]{2,1,0:T(8,128)(2,1)S(1)}, bf16[3,192,256]{2,1,0:T(8,128)(2,1)S(1)}, u32[]{:S(2)}, u32[]{:S(2)}) collective-permute-start(bf16[3,192,256]{2,1,0:T(8,128)(2,1)S(1)} %get-tuple-element.271), channel_id=1, source_target_pairs={{0,2},{2,0},{4,6},{6,4},{1,3},{3,1},{5,7},{7,5},{8,10},{10,8},{12,... | collective-permute-start | bytes 884744 | tf_op jit(solution)/shard_map/ppermute | solution.py:491
  304.1 18.0 %collective-permute-start.59 = (bf16[288,768]{1,0:T(8,128)(2,1)S(1)}, bf16[288,768]{1,0:T(8,128)(2,1)S(1)}, u32[]{:S(2)}, u32[]{:S(2)}) collective-permute-start(bf16[288,768]{1,0:T(8,128)(2,1)S(1)} %constant_dynamic-slice_fusion.1), channel_id=1, source_target_pairs={{0,1},{1,0},{2,3},{3,2},{4,5},{5,4},{6,7},{7,6},{8,9},{9,8},{10,11... | collective-permute-start | bytes 1327112 | tf_op jit(solution)/shard_map/ppermute | solution.py:481
  327.6 10.8 %collective-permute-start.64 = (bf16[144,768]{1,0:T(8,128)(2,1)S(1)}, bf16[144,768]{1,0:T(8,128)(2,1)S(1)}, u32[]{:S(2)}, u32[]{:S(2)}) collective-permute-start(bf16[144,768]{1,0:T(8,128)(2,1)S(1)} %fusion.13), channel_id=1, source_target_pairs={{0,16},{8,24},{16,0},{24,8},{1,17},{9,25},{17,1},{25,9},{2,18},{10... | collective-permute-start | bytes 663560 | tf_op jit(solution)/shard_map/ppermute | solution.py:488
  330.6 19.5 %collective-permute-start.61 = (bf16[2,128,768]{2,1,0:T(8,128)(2,1)S(1)}, bf16[2,128,768]{2,1,0:T(8,128)(2,1)S(1)}, u32[]{:S(2)}, u32[]{:S(2)}) collective-permute-start(bf16[2,128,768]{2,1,0:T(8,128)(2,1)S(1)} %pad_maximum_fusion.10), channel_id=1, source_target_pairs={{0,2},{2,0},{4,6},{6,4},{1,3},{3,1},{5,7},{7,5},{8,10},{10,8},{12,... | collective-permute-start | bytes 1179656 | tf_op jit(solution)/shard_map/ppermute | solution.py:491
  332.4 17.7 %collective-permute-start.62 = (bf16[2,128,768]{2,1,0:T(8,128)(2,1)S(1)}, bf16[2,128,768]{2,1,0:T(8,128)(2,1)S(1)}, u32[]{:S(2)}, u32[]{:S(2)}) collective-permute-start(bf16[2,128,768]{2,1,0:T(8,128)(2,1)S(1)} %pad_maximum_fusion.10), channel_id=1, source_target_pairs={{0,4},{2,6},{4,0},{6,2},{1,5},{3,7},{5,1},{7,3},{8,12},{10,14},{12... | collective-permute-start | bytes 1179656 | tf_op jit(solution)/shard_map/ppermute | solution.py:491
  332.4 17.7 %collective-permute-start.63 = (bf16[2,128,768]{2,1,0:T(8,128)(2,1)S(1)}, bf16[2,128,768]{2,1,0:T(8,128)(2,1)S(1)}, u32[]{:S(2)}, u32[]{:S(2)}) collective-permute-start(bf16[2,128,768]{2,1,0:T(8,128)(2,1)S(1)} %pad_maximum_fusion.10), channel_id=1, source_target_pairs={{0,6},{2,4},{4,2},{6,0},{1,7},{3,5},{5,3},{7,1},{8,14},{10,12},{12... | collective-permute-start | bytes 1179656 | tf_op jit(solution)/shard_map/ppermute | solution.py:491
  338.5 12.0 %collective-permute-start.65 = (bf16[144,768]{1,0:T(8,128)(2,1)S(1)}, bf16[144,768]{1,0:T(8,128)(2,1)S(1)}, u32[]{:S(2)}, u32[]{:S(2)}) collective-permute-start(bf16[144,768]{1,0:T(8,128)(2,1)S(1)} %add_convert_fusion.6), channel_id=1, source_target_pairs={{0,8},{8,0},{16,24},{24,16},{1,9},{9,1},{17,25},{25,17},{2,10},{10... | collective-permute-start | bytes 663560 | tf_op jit(solution)/shard_map/ppermute | solution.py:484
  338.6 21.5 %collective-permute-start.67 = (bf16[896,768]{1,0:T(8,128)(2,1)}, bf16[896,768]{1,0:T(8,128)(2,1)S(1)}, u32[]{:S(2)}, u32[]{:S(2)}) collective-permute-start(bf16[896,768]{1,0:T(8,128)(2,1)} %all-reduce.3.cloned.1.call-done), channel_id=1, source_target_pairs={{0,1},{1,0},{2,3},{3,2},{4,5},{5,4},{6,7},{7,6},{8,9},{9,8},{10,11... | collective-permute-start | bytes 4128776 | tf_op jit(solution)/shard_map/ppermute | solution.py:481
  (90 other events, 615.5 us)
Sparse Core Ops, SparseCore 0:
  172.1 74.6 reduce-scatter.3
  249.2 72.9 all-reduce.2

commit v8 on v6

--- a/solution.py
+++ b/solution.py
@@ -87,18 +87,19 @@
         out[0, at, :] = part.astype(out.dtype)
 
 
-def query_kernel(planes, q, tables, out, *, chunk):
-    _, upper, lower = sides(q[...], planes[...])
+def query_kernel(planes, tables, *refs, chunk):
+    rows, out = both(*refs[:-1]), refs[-1]
+    _, upper, lower = sides(rows, planes[...])
     low, high = half_codes(upper, lower)
-    acc = jnp.zeros((HEAD_DIM, q.shape[1]), f32)
+    acc = jnp.zeros((HEAD_DIM, rows.shape[1]), f32)
     for c in range(0, 16, chunk):
         acc += dot(tables[0, 128 * c : 128 * (c + chunk), :], code_chunk(low, high, c, chunk), TN)
     out[...] = (acc * (1.0 / HASHES)).astype(out.dtype)
 
 
 def query_back_kernel(planes, planes_t, bits, tables, *refs, chunk, blocks, last):
-    queries, grads = refs[:blocks], refs[blocks : 2 * blocks]
-    start = refs[2 * blocks] if len(refs) > 3 * blocks + 1 else None
+    queries, grads = refs[: 2 * blocks], refs[2 * blocks : 3 * blocks]
+    start = refs[3 * blocks] if len(refs) > 4 * blocks + 1 else None
     out, back_out = refs[-1 - blocks], refs[-blocks:]
     rows = both(*queries)
     inv, upper, lower = sides(rows, planes[...])
@@ -122,12 +123,12 @@
         back_out[i][...] = back[:, i * width : (i + 1) * width].astype(back_out[i].dtype)
 
 
-def key_back_kernel(planes, planes_t, bits, keys, vals, grad_tables, out, *, chunk):
-    rows = keys[...]
+def key_back_kernel(planes, planes_t, bits, ka, kb, va, vb, grad_tables, out, *, chunk):
+    rows = both(ka, kb)
     inv, upper, lower = sides(rows, planes[...])
     low, high = half_codes(upper, lower)
-    values = vals[...]
-    width = keys.shape[1]
+    values = both(va, vb)
+    width = rows.shape[1]
     sums = jnp.zeros((bits.shape[0], width), f32)
     grad_values = jnp.zeros((HEAD_DIM, width), f32)
     for c in range(0, 16, chunk):
@@ -153,8 +154,14 @@
     return pl.BlockSpec(shape, lambda h: (0,) * len(shape))
 
 
-def per_head(width, offset=0):
+def head_rows(array, heads, which):
+    width = array.shape[1]
+    offset = (which - 3) * heads + array.shape[0] // HEAD_DIM
     return pl.BlockSpec((HEAD_DIM, width), lambda h: (h + offset, 0))
+
+
+def per_head(width):
+    return pl.BlockSpec((HEAD_DIM, width), lambda h: (h, 0))
 
 
 def table_spec():
@@ -176,42 +183,46 @@
     )
 
 
-def key_tables(planes, blocks, start, kind):
-    heads, width = blocks[0].shape[0] // (2 * HEAD_DIM), blocks[0].shape[1]
-    specs = [whole(64, 64)] + [per_head(width)] * len(blocks) + [per_head(width, heads)] * len(blocks)
+def key_tables(planes, heads, blocks, start, kind):
     args = [planes, *blocks, *blocks]
+    specs = [whole(64, 64)] + [head_rows(x, heads, w) for w in (1, 2) for x in blocks]
     if start is not None:
         specs.append(table_spec())
         args.append(start)
     return call(
         partial(key_kernel, chunk=2, blocks=len(blocks)),
         heads,
-        15 * len(blocks),
+        30 if len(blocks) > 1 else 1,
         "key_tables",
         specs,
         table_spec(),
-        jax.ShapeDtypeStruct((heads, ROWS, HEAD_DIM), kind),
+        shape((heads, ROWS, HEAD_DIM), kind),
     )(*args)
 
 
-def query_estimates(planes, q, tables, kind):
-    heads, width = q.shape[0] // HEAD_DIM, q.shape[1]
+def query_estimates(planes, heads, near, far, tables, kind):
+    width = near.shape[1] + far.shape[1]
     return call(
         partial(query_kernel, chunk=2),
         heads,
-        10,
+        1,
         "query_estimates",
-        [whole(64, 64), per_head(width), table_spec()],
+        [whole(64, 64), table_spec(), head_rows(near, heads, 0), per_head(far.shape[1])],
         per_head(width),
-        jax.ShapeDtypeStruct(q.shape, kind),
-    )(planes, q, tables)
-
-
-def query_backward(planes, planes_t, bits, tables, queries, grads, start, last, kinds):
-    heads, width = queries[0].shape[0] // HEAD_DIM, queries[0].shape[1]
-    blocks = len(queries)
-    specs = [whole(64, 64), whole(64, 128), whole(80, ROWS), table_spec()] + [per_head(width)] * (2 * blocks)
-    args = [planes, planes_t, bits, tables, *queries, *grads]
+        shape((heads * HEAD_DIM, width), kind),
+    )(planes, tables, near, far)
+
+
+def query_backward(planes, planes_t, bits, heads, tables, queries, grads, start, last, kinds):
+    width = grads[0].shape[1]
+    blocks = len(grads)
+    specs = [whole(64, 64), whole(64, 128), whole(80, ROWS), table_spec()]
+    args = [planes, planes_t, bits, tables]
+    for near, far in queries:
+        specs += [head_rows(near, heads, 0), per_head(far.shape[1])]
+        args += [near, far]
+    specs += [per_head(width)] * blocks
+    args += grads
     if start is not None:
         specs.append(table_spec())
         args.append(start)
@@ -223,22 +234,23 @@
         specs,
         [table_spec()] + [per_head(width)] * blocks,
         [shape((heads, ROWS, HEAD_DIM), bf16 if last else f32)]
-        + [shape(queries[0].shape, kind) for kind in kinds],
+        + [shape(grads[0].shape, kind) for kind in kinds],
     )(*args)
 
 
-def key_backward(planes, planes_t, bits, kv, grad_tables, kind):
-    heads, width = kv.shape[0] // (2 * HEAD_DIM), kv.shape[1]
+def key_backward(planes, planes_t, bits, heads, near, far, grad_tables, kind):
+    width = near.shape[1] + far.shape[1]
     return call(
         partial(key_back_kernel, chunk=4),
         heads,
         25,
         "key_backward",
         [whole(64, 64), whole(64, 128), whole(80, ROWS)]
-        + [per_head(width), per_head(width, heads), table_spec()],
+        + [head_rows(x, heads, w) for w in (1, 2) for x in (near, far)]
+        + [table_spec()],
         pl.BlockSpec((2, HEAD_DIM, width), lambda h: (0, h, 0)),
-        jax.ShapeDtypeStruct((2, heads * HEAD_DIM, width), kind),
-    )(planes, planes_t, bits, kv, kv, grad_tables)
+        shape((2, heads * HEAD_DIM, width), kind),
+    )(planes, planes_t, bits, near, far, near, far, grad_tables)
 
 
 def norm(x):
@@ -293,7 +305,7 @@
     share_rows(keep, give, 4, normed)
     second = normed.astype(f32)
     for b in blocks:
-        pre = dot(normed, ups[b][...], NT)
+        pre = dot(normed, ups[b][...], NN)
         below = 0.5 * (1.0 + lax.erf(pre * 0.7071067811865476))
         rows = (pre * below).astype(bf16)
         (keep, give)[b % 2][b // 2] = rows
@@ -321,7 +333,7 @@
     for b in blocks:
         rows = (dot(grad_ffn, downs[b][0:part, :], NT) * slope[b]).astype(bf16)
         (keep, give)[b % 2][b // 2] = rows
-        grad_normed = grad_normed + dot(rows, ups[b][...], NN)
+        grad_normed = grad_normed + dot(rows, ups[b][...], NT)
     unit, inv = norm(first[...])
     small[0:1, :] = column_sum(grad_normed * unit)
     small[1:2, :] = column_sum(grad_normed)
@@ -400,7 +412,7 @@
 
 def dense(core, x_in, grad_out, gain, bias, attn, ups, downs):
     rows, width = x_in.shape
-    part = ups[0].shape[0]
+    part = ups[0].shape[1]
     out_shape = [
         shape((rows, width), bf16),
         shape((rows, width), f32),
@@ -417,7 +429,7 @@
 
 def dense_back(core, first, grad_second, slope, gain, attn, ups, downs):
     rows, width = first.shape
-    part = ups[0].shape[0]
+    part = ups[0].shape[1]
     out_shape = [
         shape((rows, width), f32),
         shape((6, rows, part), bf16),
@@ -493,6 +505,11 @@
     def seq_rows(block, index):
         return lax.dynamic_index_in_dim(block, index % seqs, 1, keepdims=False)
 
+    here = [
+        seq_rows(lax.dynamic_slice_in_dim(own, (d ^ j) * quarter, quarter, 0), g)
+        for j in range(head_count)
+    ]
+    near_tokens = jnp.concatenate(here)
     my_quarter = lax.dynamic_slice_in_dim(own, d * quarter, quarter, 0)
     arrived = [over_group(seq_rows(my_quarter, g + k), k) for k in range(1, groups)]
 
@@ -512,18 +529,36 @@
     signed_t = jnp.concatenate([signed.T, signed.T], axis=1)
     bits = bit_rows()
 
-    dense_in = jnp.stack([seq_rows(my_quarter, g)] + arrived)
-
-    def core_half(at):
-        cut = hidden_own // 2
-        out_cut = head_width // 2
-        down = lax.dynamic_slice_in_dim(down_weight, at * cut, cut, 0)
-        out = lax.dynamic_slice_in_dim(w_out, at * out_cut, out_cut, 0)
-        return lax.dynamic_slice_in_dim(up_weight, at * cut, cut, 1).T, jnp.concatenate([down, out])
-
-    up, down = core_half(s)
-    ups, downs = [[x] for x in core_half(1 - s)]
-
+    def down_half(at):
+        cut, out_cut = hidden_own // 2, head_width // 2
+        rows_down = lax.dynamic_slice_in_dim(down_weight, at * cut, cut, 0)
+        return jnp.concatenate([rows_down, lax.dynamic_slice_in_dim(w_out, at * out_cut, out_cut, 0)])
+
+    down, downs = down_half(s), [down_half(1 - s)]
+
+    head_n = head_width // HEAD_DIM
+
+    def project(w, rows_in):
+        out = jnp.einsum("cde,ld->cel", w, rows_in, preferred_element_type=f32)
+        return out.astype(bf16).reshape(-1, rows_in.shape[0])
+
+    near_tokens = after(near_tokens, *arrived)
+    near = project(w_qkv, near_tokens)
+    near_z, near_o = over_place(near), over_seq(near)
+    far_quarter = jnp.stack(arrived)
+    moved = [over_head(far_quarter, j) for j in range(1, head_count)]
+    ready = after(signed, near_z)
+    tables = key_tables(ready, head_n, [near, near_o], None, f32)
+    moved = [after(x, tables) for x in moved]
+
+    near_z = after(near_z, tables)
+    near_zo = over_seq(near_z)
+
+    up_weight, mask_pos = after(up_weight, tables), after(mask_pos, tables)
+    up, up_other = [
+        lax.dynamic_slice_in_dim(up_weight, at * (hidden_own // 2), hidden_own // 2, 1) for at in (s, 1 - s)
+    ]
+    ups = [up_other]
     slot = jnp.arange(groups, dtype=jnp.int32)[:, None]
     place_of = ((g - slot) % groups) * places + r
     position = s * half_len + place_of * piece + d * quarter + jnp.arange(quarter, dtype=jnp.int32)[None]
@@ -531,62 +566,57 @@
     cot = lax.dynamic_index_in_dim(cot_rows, g, 0, keepdims=False)
     pick = (position.reshape(rows)[:, None] == mask_row[None]).astype(bf16)
     grad_out = jnp.dot(pick, cot, preferred_element_type=f32)
-
-    blocks = [dense_in]
-    for j in range(1, head_count):
-        here = seq_rows(lax.dynamic_slice_in_dim(own, (d ^ j) * quarter, quarter, 0), g)
-        there = after(over_head(dense_in[1:], j), up, down, *ups, *downs, grad_out, signed_t)
-        blocks.append(jnp.concatenate([here[None], there]))
-    tokens = jnp.stack(blocks).reshape(n_tokens, width)
-    dense_in = dense_in.reshape(rows, width)
-
-    def project(w):
-        return jnp.einsum("cde,ld->cel", w, tokens, preferred_element_type=f32).astype(bf16)
-
-    kv = project(w_qkv[1:]).reshape(2 * head_width, n_tokens)
-    q = project(w_qkv[:1]).reshape(head_width, n_tokens)
-    kv_z = over_place(kv)
-    kv_o = over_seq(kv)
-    q_o = over_seq(q)
-    q_z = over_place(after(q, kv_o))
-
-    up = after(up, q)
+    ready = after(signed, grad_out, up, down, *ups, *downs)
+    tables = key_tables(ready, head_n, [near_z, near_zo], tables, f32)
+
+    far_tokens = jnp.stack([far_quarter, *moved]).reshape(-1, width)
+    kv = project(w_qkv[1:], far_tokens)
+    q = project(after(w_qkv[:1], kv), far_tokens)
+    tokens = jnp.concatenate([near_tokens, far_tokens])
+    dense_in = jnp.concatenate([here[0], *arrived])
+    kv_z, kv_o = over_place(kv), over_seq(kv)
+    q_o, q_z = over_seq(q), over_place(q)
+    n_near = near.shape[1]
+
     ups, downs = [up] + ups, [down] + downs
+    up = after(up, kv)
     up_x, up_y = over_head(up, 1), over_head(up, 2)
-    tables = key_tables(after(signed, up, q), [kv, kv_o], None, f32)
+    qkv_cut = head_width // 2
+    w_qkv_t = w_qkv.transpose(0, 2, 1)
+    qkv_near = [lax.dynamic_slice_in_dim(w_qkv_t, s * qkv_cut, qkv_cut, 1)]
+    qkv_far = [lax.dynamic_slice_in_dim(w_qkv_t, (1 - s) * qkv_cut, qkv_cut, 1)]
+    tables = key_tables(after(signed, q), head_n, [kv, kv_o], tables, f32)
 
     kv_z = after(kv_z, tables)
     kv_zo = over_seq(kv_z)
     up_x, up_y = after(up_x, tables), after(up_y, tables)
     down = after(down, up_x, up_y)
-    down_x, down_y = over_head(down, 1), over_head(down, 2)
-    qkv_cut = head_width // 2
-    w_qkv_t = w_qkv.transpose(0, 2, 1)
-    qkv_near = [lax.dynamic_slice_in_dim(w_qkv_t, s * qkv_cut, qkv_cut, 1)]
-    qkv_far = [lax.dynamic_slice_in_dim(w_qkv_t, (1 - s) * qkv_cut, qkv_cut, 1)]
-    tables = key_tables(after(signed, down, qkv_near[0], qkv_far[0]), [kv_z], tables, f32)
-
-    up_xo, up_yo = over_seq(after(up_x, tables)), over_seq(after(up_y, tables))
+    down_x, down_y, up_d = over_head(down, 1), over_head(down, 2), over_head(up_x, 2)
+    up_xo, up_yo = over_seq(up_x), over_seq(up_y)
+    ready = after(signed, down, tokens, dense_in, qkv_near[0], qkv_far[0])
+    tables = key_tables(ready, head_n, [kv_z], tables, f32)
+
     q_z = after(q_z, tables)
     q_zo = over_seq(q_z)
     kv_zo = after(kv_zo, tables)
-    tables = key_tables(after(signed, q_z), [kv_zo], tables, bf16)
+    tables = key_tables(after(signed, q_z), head_n, [kv_zo], tables, bf16)
 
     q_zo = after(q_zo, tables)
-    down_x, down_y = after(down_x, tables), after(down_y, tables)
     up_xo, up_yo = after(up_xo, tables), after(up_yo, tables)
-    up_d, down_d = over_head(after(up_x, tables), 2), over_head(down_y, 1)
+    q_zo = after(q_zo, up_xo, up_yo)
+    e_zo = query_estimates(signed, head_n, near_zo, q_zo, tables, bf16)
+    down_x, down_y = after(down_x, e_zo), after(down_y, e_zo)
+    down_d = over_head(down_y, 1)
     down_xo, down_yo = over_seq(down_x), over_seq(down_y)
-    q_zo = after(q_zo, down_x, down_y, up_xo, up_yo)
-    e_zo = query_estimates(signed, q_zo, tables, bf16)
     e_zo_moved = over_seq(e_zo)
-    down_xo, down_yo = after(down_xo, e_zo), after(down_yo, e_zo)
-    e_z = query_estimates(signed, after(q_z, e_zo, down_xo, down_yo), tables, bf16)
+    e_z = query_estimates(signed, head_n, near_z, after(q_z, e_zo, down_x, down_y), tables, bf16)
     e_far = add(e_z, after(e_zo_moved, e_z)).astype(bf16)
-    e_o = query_estimates(signed, after(q_o, e_far), tables, bf16)
+    down_xo, down_yo = after(down_xo, e_z), after(down_yo, e_z)
+    ready = after(q_o, e_far, down_xo, down_yo)
+    e_o = query_estimates(signed, head_n, near_o, ready, tables, bf16)
     e_far = over_place(e_far)
     e_o_moved = over_seq(e_o)
-    e = query_estimates(signed, after(q, e_o), tables, f32)
+    e = query_estimates(signed, head_n, near, after(q, e_o), tables, f32)
     e_far = after(e_far, e)
     up_d, down_d = after(up_d, e_far), after(down_d, e_far)
     ups += [up_x, up_xo, up_y, up_yo, up_d, over_seq(up_d)]
@@ -594,7 +624,11 @@
     attn = add(e, after(e_o_moved, e), e_far).astype(bf16)
 
     def to_dense(block):
-        parts = [block[..., j * rows : (j + 1) * rows] for j in range(head_count)]
+        parts = []
+        for j in range(head_count):
+            a, b = j * quarter, n_near + j * (rows - quarter)
+            cut = [block[..., a : a + quarter], block[..., b : b + rows - quarter]]
+            parts.append(jnp.concatenate(cut, axis=-1))
         moved = [over_head(parts[j], j) for j in range(1, head_count)]
         return [parts[0], *lax.optimization_barrier(moved)]
 
@@ -605,19 +639,22 @@
         return [dense_rows[0]] + [over_group(dense_rows[k], groups - k) for k in range(1, groups)]
 
     core = jnp.stack([s, d]).astype(jnp.int32)
-    layer_rows, first, grad_second, slope, near, give, heads_give, small_a = dense(
+    layer_rows, first, grad_second, slope, keep, give, heads_give, small_a = dense(
         core, dense_in, grad_out, norm_gain, norm_bias, attn_parts, ups, downs
     )
-    far, heads_far = over_seq(give), over_seq(heads_give)
-    grad_first, near_back, give_back, *est_parts, small_b = dense_back(
+    taken, heads_far = over_seq(give), over_seq(heads_give)
+    grad_first, keep_back, give_back, *est_parts, small_b = dense_back(
         core, first, grad_second, slope, norm_gain, attn_parts, ups, downs
     )
-    far_back = over_seq(give_back)
+    taken_back = over_seq(give_back)
     est_moved = [over_head(est_parts[j], j) for j in range(1, head_count)]
-    grad = jnp.concatenate([est_parts[0], *lax.optimization_barrier(est_moved)], axis=1)
+    est_parts = [est_parts[0], *lax.optimization_barrier(est_moved)]
+    grad = jnp.concatenate(
+        [x[:, :quarter] for x in est_parts] + [x[:, quarter:] for x in est_parts], axis=1
+    )
     layer_moved = away(layer_rows)
     weight_parts = weight_grads(
-        core, after(small_a, grad), small_b, [near, far, near_back, far_back], attn_parts, heads_far
+        core, after(small_a, grad), small_b, [keep, taken, keep_back, taken_back], attn_parts, heads_far
     )
 
     weight_sum = lax.psum_scatter(weight_parts, "head", scatter_dimension=0, tiled=True)[0]
@@ -625,29 +662,30 @@
     grad_o = after(over_seq(grad), weight_parts)
     layer_moved = jnp.stack([after(x, weight_parts) for x in layer_moved])
     part, dq, dq_o = query_backward(
-        signed, signed_t, bits, tables, [after(q, layer_moved), q_o], [grad, grad_o], None, False, [f32, bf16]
+        signed, signed_t, bits, head_n, tables, [(near, after(q, layer_moved)), (near_o, q_o)], [grad, grad_o],
+        None, False, [f32, bf16],
     )
 
     grad_z = after(grad_z, part)
     grad_zo = over_seq(grad_z)
     dq_o = over_seq(dq_o)
     part, dq_z = query_backward(
-        signed, signed_t, bits, tables, [q_z], [grad_z], part, False, [f32]
+        signed, signed_t, bits, head_n, tables, [(near_z, q_z)], [grad_z], part, False, [f32]
     )
 
     dq_own = add(dq, after(dq_o, dq_z))
     grad_zo = after(grad_zo, dq_z)
     grad_tables, dq_zo = query_backward(
-        signed, signed_t, bits, tables, [after(q_zo, dq_own)], [grad_zo], part, True, [bf16]
+        signed, signed_t, bits, head_n, tables, [(near_zo, after(q_zo, dq_own))], [grad_zo], part, True, [bf16]
     )
 
     dq_zo = over_seq(dq_zo)
-    dkv_zo = key_backward(signed, signed_t, bits, kv_zo, grad_tables, bf16)
+    dkv_zo = key_backward(signed, signed_t, bits, head_n, near_zo, kv_zo, grad_tables, bf16)
 
     dkv_zo_moved = over_seq(dkv_zo)
     dq_far = add(dq_z, after(dq_zo, dkv_zo)).astype(bf16)
     layer_moved = [layer_moved] + [over_head(layer_moved, j) for j in range(1, head_count)]
-    dkv_z = key_backward(signed, signed_t, bits, after(kv_z, dq_far), grad_tables, bf16)
+    dkv_z = key_backward(signed, signed_t, bits, head_n, near_z, after(kv_z, dq_far), grad_tables, bf16)
     dq_far = over_place(dq_far)
 
     dkv_far = add(dkv_z, after(dkv_zo_moved, dkv_z)).astype(bf16)
@@ -655,7 +693,8 @@
     weight_sum = after(weight_sum, dkv_z)
     layer_moved = [after(x, dkv_z) for x in layer_moved]
     dkv_o = key_backward(
-        signed, signed_t, bits, after(kv_o, dkv_far, grad_q, weight_sum, *layer_moved), grad_tables, bf16
+        signed, signed_t, bits, head_n, near_o, after(kv_o, dkv_far, grad_q, weight_sum, *layer_moved),
+        grad_tables, bf16,
     )
     weight_sum = lax.psum(weight_sum, "hash")
     dk_far, dv_far = over_place(dkv_far[0]), over_place(after(dkv_far[1], dkv_o))
@@ -666,7 +705,7 @@
     dk_far = after(dk_far, dkv_o)
     qkv_near += [after(x, dkv_o) for x in qkv_moved]
     dkv = key_backward(
-        signed, signed_t, bits, after(kv, dk_far, *qkv_near[1:]), grad_tables, f32
+        signed, signed_t, bits, head_n, near, after(kv, dk_far, *qkv_near[1:]), grad_tables, f32
     )
     qkv_far += [over_seq(x) for x in qkv_near[1:]]
 
@@ -720,7 +759,7 @@
     w_grad = in_halves(r, w_keep, over_place(w_keep))
     w_grad = in_halves(s, w_grad, over_seq(w_grad)).reshape(3, head_width, width)
     grad_w_qkv = w_grad.transpose(0, 2, 1).astype(f32)
-    weight_sum = after(weight_sum, w_keep)
+    weight_sum = after(weight_sum, grad_in)
     weight_far = over_seq(weight_sum)
     cut = hidden_own // 2
     ends = [0, cut, 2 * cut, 2 * cut + head_width // 2]

time: 375 us -> 382 us (1.019)
  waiting for transfers between devices: 71.9 us -> 58.7 us
  Pallas kernels: 148 us -> 159 us
  other arithmetic: 21.6 us -> 26.5 us
    pallas_call x7 -> x9, Pallas kernels: 31.1 us -> 39.6 us  [the longest x5 23.2 us: key_tables(): call(partial(key_kernel, chunk=2, blocks=len(blocks)), heads, 30 if len(b...]
    ppermute x4, waiting for transfers between devices: 22.5 us -> 14.9 us  [over_group(): return lax.ppermute(x, 'hash', moves)]
    ppermute x9 -> x10, waiting for transfers between devices: 16.9 us -> 9.5 us  [over_place(): return lax.ppermute(x, 'hash', [(h, h ^ 1) for h in range(hash_count)])]
    concatenate x1 -> x11, other arithmetic: 1.31 us -> 5.55 us  [the longest x1 1.7 us: shards(): dense_in = jnp.concatenate([here[0], *arrived])]
    unnamed x129 -> x149, local copies, waits for them, and re-layouts: 21.9 us -> 25.3 us
    ppermute x27 -> x29, starting transfers between devices: 31.9 us -> 30.1 us  [over_seq(): return lax.ppermute(x, 'seq', [(0, 1), (1, 0)])]
    ppermute x9 -> x10, starting transfers between devices: 8.1 us -> 7.57 us  [over_place(): return lax.ppermute(x, 'hash', [(h, h ^ 1) for h in range(hash_count)])]
  transfers between devices with their start and end apart: 70 -> 73, of which waited for: 19 -> 13; matrix products, arithmetic and copies ran while one was open for 10% -> 11% of each run, Pallas kernels for 36% -> 36%
where the time goes in v8:
time: 382 us; the launch traced here: 378 us
  Pallas kernels  159 us (42%)
  starting transfers between devices  71.9 us (19%)
  waiting for transfers between devices  58.7 us (15%)
  local copies, waits for them, and re-layouts  42 us (11%)
  other arithmetic  26.5 us (7%)
  between operations  15.6 us (4%)
  matrix products  4.14 us (1%)
    pallas_call x3, Pallas kernels, query_backward(): call(partial(query_back_kernel, chunk=4, blocks=blocks, last=last), heads...  43.2 us
    pallas_call x4, Pallas kernels, key_backward(): call(partial(key_back_kernel, chunk=4), heads, 25, 'key_backward', [whole...  38.3 us
    pallas_call x4, Pallas kernels, single(): pl.pallas_call(kernel, in_specs=[pl.BlockSpec(memory_space=pltpu.SMEM)] +...  38.1 us
    ppermute x27, waiting for transfers between devices, over_head(): return lax.ppermute(x, 'head', [(h, h ^ j) for h in range(head_count)])  34.2 us
    ppermute x29, starting transfers between devices, over_seq(): return lax.ppermute(x, 'seq', [(0, 1), (1, 0)])  30.1 us
    unnamed x149, local copies, waits for them, and re-layouts  25.3 us
    ppermute x27, starting transfers between devices, over_head(): return lax.ppermute(x, 'head', [(h, h ^ j) for h in range(head_count)])  24.1 us
    pallas_call x5, Pallas kernels, key_tables(): call(partial(key_kernel, chunk=2, blocks=len(blocks)), heads, 30 if len(b...  23.2 us
  transfers between devices with their start and end apart: 73, of which 13 were waited for; matrix products, arithmetic and copies ran while one was open for 11% of the time, Pallas kernels for 36%

profile of v8, /device:TPU:1, one launch (start us, length us, event | category | flops | bytes accessed | tf_op | source)
XLA Modules:
  0.0 378.1 jit_solution(13250639728476014348)
XLA Ops:
  7.3 4.5 %constant_dynamic-slice_fusion.11 = (bf16[1,128,1,768]{3,2,1,0:T(2,128)(2,1)S(1)}, bf16[1,128,1,768]{3,2,1,0:T(2,128)(2,1)}, bf16[1,128,1,768]{3,2,1,0:T(2,128)(...) fusion(bf16[1,512,2,768]{3,2,1,0:T(2,128)(2,1)} %param.11, s32[]{:T(128)S(6)} %select_n.262, ...), kind=kLoop, calls=%fused_computation.122 | loop fusion | bytes 1966104 | tf_op jit(solution)/shard_map/jit(dynamic_index_in_dim)/dynamic_slice | solution.py:506
  12.6 3.1 collective-permute-start
  16.3 2.8 collective-permute-start.1
  20.8 1.8 copy_bitcast_fusion
  30.1 1.9 slice.154
  36.3 4.2 %collective-permute-done.2.refs_0_.refs_2_.ka.va = bf16[576,512]{1,0:T(8,128)(2,1)} collective-permute-done((bf16[576,512]{1,0:T(8,128)(2,1)}, bf16[576,512]{1,0:T(8,128)(2,1)}, u32[]{:S(2)}, u32[]{:S(2)}) %collective-permute-start.2) | collective-permute-done | bytes 589856 | tf_op jit(solution)/shard_map/ppermute | solution.py:496
  40.5 5.2 %key_tables.5.refs_4_ = f32[3,2048,64]{2,1,0:T(8,128)S(1)} custom-call(bf16[64,64]{1,0:T(8,128)(2,1)S(1)} %bitcast.153, bf16[576,512]{1,0:T(8,128)(2,1)} %bitcast.14.refs_0_.refs_2_.ka.va, bf16[576,512]{1,0:T(8,128)(2,1)} %collective-permute-done.3.refs_1_.refs_3_.refs_0_.refs_2_.ka.va, bf16[576,512]{1,0:T(8,128)(2,1)} %bitcast.14.refs_0_.refs_2_.ka.va, ...), custom_call_target="tpu_custom_call" | custom-call | flops 32999999488 | bytes 1048576 | tf_op jit(solution)/shard_map/key_tables/pallas_call | solution.py:192
  48.2 2.2 collective-permute-start.9
  58.4 5.6 %key_tables.6.refs_4_ = f32[3,2048,64]{2,1,0:T(8,128)S(1)} custom-call(bf16[64,64]{1,0:T(8,128)(2,1)S(1)} %bitcast.154, bf16[576,512]{1,0:T(8,128)(2,1)} %collective-permute-done.2.refs_0_.refs_2_.ka.va, bf16[576,512]{1,0:T(8,128)(2,1)S(1)} %collective-permute-done.10.refs_1_.refs_3_.refs_0_.ka.va, ...), custom_call_target="tpu_custom_call" | custom-call | flops 32999999488 | bytes 1048576 | tf_op jit(solution)/shard_map/key_tables/pallas_call | solution.py:192
  65.7 5.7 %key_tables.7.refs_2_ = f32[3,2048,64]{2,1,0:T(8,128)S(1)} custom-call(bf16[64,64]{1,0:T(8,128)(2,1)S(1)} %bitcast.155, bf16[384,512]{1,0:T(8,128)(2,1)S(1)} %bitcast.149, bf16[384,512]{1,0:T(8,128)(2,1)S(1)} %collective-permute-done.9.refs_1_.refs_3_.kb.vb, bf16[384,512]{1,0:T(8,128)(2,1)S(1)} %bitcast.150, ...), custom_call_target="tpu_custom_call" | custom-call | flops 32999999488 | bytes 1048576 | tf_op jit(solution)/shard_map/key_tables/pallas_call | solution.py:192
  76.0 1.7 pad_maximum_fusion.10.x_in
  77.7 4.2 %key_tables.8.refs_2_ = f32[3,2048,64]{2,1,0:T(8,128)S(1)} custom-call(bf16[64,64]{1,0:T(8,128)(2,1)S(1)} %bitcast.156, bf16[384,512]{1,0:T(8,128)(2,1)S(1)} %collective-permute-done.12.refs_0_.refs_1_.kb.vb, bf16[384,512]{1,0:T(8,128)(2,1)S(1)} %collective-permute-done.12.refs_0_.refs_1_.kb.vb, f32[3,2048,64]{2,1,0:T(8,128)} %copy-done.2), custom_call_target="tpu_custom_call" | custom-call | flops 1100000000 | bytes 1048576 | tf_op jit(solution)/shard_map/key_tables/pallas_call | solution.py:192
  82.0 2.6 key_tables.9.tables
  84.7 3.3 query_estimates.4
  88.0 2.8 collective-permute-done.19.refs_16_.refs_12_
  94.0 4.1 %query_estimates.5 = bf16[192,1024]{1,0:T(8,128)(2,1)S(1)} custom-call(bf16[64,64]{1,0:T(8,128)(2,1)S(1)} %bitcast.159, bf16[3,2048,64]{2,1,0:T(8,128)(2,1)S(1)} %key_tables.9.tables, bf16[576,512]{1,0:T(8,128)(2,1)} %collective-permute-done.2.refs_0_.refs_2_.ka.va, bf16[192,512]{1,0:T(8,128)(2,1)S(1)} %collective-permute-done.7.refs_1_), custom_call_target="tpu_custom_call" | custom-call | flops 1100000000 | bytes 1048576 | tf_op jit(solution)/shard_map/query_estimates/pallas_call | solution.py:205
  99.8 4.2 %query_estimates.6 = bf16[192,1024]{1,0:T(8,128)(2,1)S(1)} custom-call(bf16[64,64]{1,0:T(8,128)(2,1)S(1)} %bitcast.160, bf16[3,2048,64]{2,1,0:T(8,128)(2,1)S(1)} %key_tables.9.tables, bf16[576,512]{1,0:T(8,128)(2,1)} %collective-permute-done.3.refs_1_.refs_3_.refs_0_.refs_2_.ka.va, bf16[192,512]{1,0:T(8,128)(2,1)S(1)} %collective-permute-done.14.refs_1_.refs_3_), custom_call_target="tpu_custom_call" | custom-call | flops 1100000000 | bytes 1048576 | tf_op jit(solution)/shard_map/query_estimates/pallas_call | solution.py:205
  105.7 4.7 %query_estimates.7 = f32[192,1024]{1,0:T(8,128)S(1)} custom-call(bf16[64,64]{1,0:T(8,128)(2,1)S(1)} %bitcast.162, bf16[3,2048,64]{2,1,0:T(8,128)(2,1)S(1)} %key_tables.9.tables, bf16[576,512]{1,0:T(8,128)(2,1)} %bitcast.14.refs_0_.refs_2_.ka.va, bf16[192,512]{1,0:T(8,128)(2,1)S(1)} %convolution_convert_fusion.1.refs_1_), custom_call_target="tpu_custom_call" | custom-call | flops 1100000000 | bytes 1048576 | tf_op jit(solution)/shard_map/query_estimates/pallas_call | solution.py:205
  110.4 5.9 %collective-permute-done.30.refs_18_.refs_14_ = bf16[480,768]{1,0:T(8,128)(2,1)} collective-permute-done((bf16[480,768]{1,0:T(8,128)(2,1)}, bf16[480,768]{1,0:T(8,128)(2,1)}, u32[]{:S(2)}, u32[]{:S(2)}) %collective-permute-start.30) | collective-permute-done | bytes 737312 | tf_op jit(solution)/shard_map/ppermute | solution.py:503
  126.6 12.2 %dense.1 = (bf16[256,768]{1,0:T(8,128)(2,1)}, f32[256,768]{1,0:T(8,128)}, f32[256,768]{1,0:T(8,128)}, f32[8,256,384]{2,1,0:T(8,128)}, bf16[8,256,384]{2,1,0:T(8,...) custom-call(s32[2]{0:T(128)} %pad_add_fusion.core, ...), custom_call_target="tpu_custom_call" | custom-call | flops 15399999488 | bytes 1048576 | tf_op jit(solution)/shard_map/dense/pallas_call | solution.py:399
  138.9 12.2 %dense_back.1 = (f32[256,768]{1,0:T(8,128)}, bf16[6,256,384]{2,1,0:T(8,128)(2,1)}, bf16[6,256,384]{2,1,0:T(8,128)(2,1)}, bf16[192,256]{1,0:T(8,128)(2,1)}, bf16[...) custom-call(s32[2]{0:T(128)} %pad_add_fusion.core, ...), custom_call_target="tpu_custom_call" | custom-call | flops 8800000000 | bytes 1048576 | tf_op jit(solution)/shard_map/dense_back/pallas_call | solution.py:399
  151.2 2.1 collective-permute-start.32
  155.3 1.9 collective-permute-start.36
  158.5 3.0 collective-permute-start.38
  162.4 2.6 collective-permute-start.40
  167.8 8.5 %weight_grads.1 = bf16[4,896,768]{2,1,0:T(8,128)(2,1)} custom-call(s32[2]{0:T(128)} %pad_add_fusion.core, f32[8,768]{1,0:T(8,128)} %get-tuple-element.165.small_a, f32[8,768]{1,0:T(8,128)} %get-tuple-element.166.small_b, bf16[8,256,384]{2,1,0:T(8,128)(2,1)} %get-tuple-element.167.refs_0_, bf16[8,256,384]{2,1,0:T(8,128)(2,1)} %copy-done.47, ...), custom_call_target="tpu_custom_call" | custom-call | flops 7699999744 | bytes 1048576 | tf_op jit(solution)/shard_map/weight_grads/pallas_call | solution.py:399
  179.3 20.3 %query_backward.3 = (f32[3,2048,64]{2,1,0:T(8,128)}, f32[192,1024]{1,0:T(8,128)S(1)}, bf16[192,1024]{1,0:T(8,128)(2,1)S(1)}) custom-call(bf16[64,64]{1,0:T(8,128)(2,1)S(1)} %bitcast.163, bf16[64,128]{1,0:T(8,128)(2,1)S(1)} %pad_maximum_fusion.21.planes_t, bf16[80,2048]{1,0:T(8,128)(2,1)S(1)} %copy-done.15, bf16[3,2048,64]{2,1,0:T(8,128)(2,1)S(1)} %key_tables.9.tables, ...), custom_call_target="tpu_custom_call" | custom-call | flops 54999998464 | bytes 1048576 | tf_op jit(solution)/shard_map/query_backward/pallas_call | solution.py:229
  200.1 11.7 %query_backward.4 = (f32[3,2048,64]{2,1,0:T(8,128)}, f32[192,1024]{1,0:T(8,128)S(1)}) custom-call(bf16[64,64]{1,0:T(8,128)(2,1)S(1)} %bitcast.164, bf16[64,128]{1,0:T(8,128)(2,1)S(1)} %pad_maximum_fusion.21.planes_t, bf16[80,2048]{1,0:T(8,128)(2,1)S(1)} %copy-done.15, bf16[3,2048,64]{2,1,0:T(8,128)(2,1)S(1)} %key_tables.9.tables, ...), custom_call_target="tpu_custom_call" | custom-call | flops 27499999232 | bytes 1048576 | tf_op jit(solution)/shard_map/query_backward/pallas_call | solution.py:229
  214.6 11.2 %query_backward.5 = (bf16[3,2048,64]{2,1,0:T(8,128)(2,1)S(1)}, bf16[192,1024]{1,0:T(8,128)(2,1)S(1)}) custom-call(bf16[64,64]{1,0:T(8,128)(2,1)S(1)} %bitcast.165, bf16[64,128]{1,0:T(8,128)(2,1)S(1)} %pad_maximum_fusion.21.planes_t, bf16[80,2048]{1,0:T(8,128)(2,1)S(1)} %copy-done.15, bf16[3,2048,64]{2,1,0:T(8,128)(2,1)S(1)} %key_tables.9.tables, ...), custom_call_target="tpu_custom_call" | custom-call | flops 27499999232 | bytes 1048576 | tf_op jit(solution)/shard_map/query_backward/pallas_call | solution.py:229
  227.2 8.7 %key_backward.4 = bf16[2,192,1024]{2,1,0:T(8,128)(2,1)S(1)} custom-call(bf16[64,64]{1,0:T(8,128)(2,1)S(1)} %bitcast.166, bf16[64,128]{1,0:T(8,128)(2,1)S(1)} %pad_maximum_fusion.21.planes_t, bf16[80,2048]{1,0:T(8,128)(2,1)S(1)} %copy-done.16, bf16[576,512]{1,0:T(8,128)(2,1)S(1)} %copy-done.10, bf16[384,512]{1,0:T(8,128)(2,1)S(1)} %copy-done.6, ...), custom_call_target="tpu_custom_call" | custom-call | flops 27499999232 | bytes 1048576 | tf_op jit(solution)/shard_map/key_backward/pallas_call | solution.py:243
  236.9 9.7 %key_backward.5 = bf16[2,192,1024]{2,1,0:T(8,128)(2,1)S(1)} custom-call(bf16[64,64]{1,0:T(8,128)(2,1)S(1)} %bitcast.167, bf16[64,128]{1,0:T(8,128)(2,1)S(1)} %pad_maximum_fusion.21.planes_t, bf16[80,2048]{1,0:T(8,128)(2,1)S(1)} %copy-done.16, bf16[576,512]{1,0:T(8,128)(2,1)} %collective-permute-done.2.refs_0_.refs_2_.ka.va, bf16[384,512]{1,0:T(8,128)(2,1)S(1)} %copy-done.4, ...), custom_call_target="tpu_custom_call" | custom-call | flops 27499999232 | bytes 1048576 | tf_op jit(solution)/shard_map/key_backward/pallas_call | solution.py:243
  253.1 9.7 %key_backward.6 = bf16[2,192,1024]{2,1,0:T(8,128)(2,1)S(1)} custom-call(bf16[64,64]{1,0:T(8,128)(2,1)S(1)} %bitcast.168, bf16[64,128]{1,0:T(8,128)(2,1)S(1)} %pad_maximum_fusion.21.planes_t, bf16[80,2048]{1,0:T(8,128)(2,1)S(1)} %copy-done.17, bf16[576,512]{1,0:T(8,128)(2,1)} %collective-permute-done.3.refs_1_.refs_3_.refs_0_.refs_2_.ka.va, ...), custom_call_target="tpu_custom_call" | custom-call | flops 27499999232 | bytes 1048576 | tf_op jit(solution)/shard_map/key_backward/pallas_call | solution.py:243
  262.8 1.9 collective-permute-start.53
  264.7 4.7 %collective-permute-done.51.refs_6_ = bf16[3,96,768]{2,1,0:T(8,128)(2,1)} collective-permute-done((bf16[3,96,768]{2,1,0:T(8,128)(2,1)}, bf16[3,96,768]{2,1,0:T(8,128)(2,1)}, u32[]{:S(2)}, u32[]{:S(2)}) %collective-permute-start.51) | collective-permute-done | bytes 442400 | tf_op jit(solution)/shard_map/ppermute | solution.py:503
  269.5 7.1 %collective-permute-start.60 = (bf16[3,96,768]{2,1,0:T(8,128)(2,1)}, bf16[3,96,768]{2,1,0:T(8,128)(2,1)S(1)}, u32[]{:S(2)}, u32[]{:S(2)}) collective-permute-start(bf16[3,96,768]{2,1,0:T(8,128)(2,1)} %collective-permute-done.52.refs_7_), channel_id=1, source_target_pairs={{0,1},{1,0},{2,3},{3,2},{4,5},{5,4},{6,7},{7,6},{8,9},{9,8},{10,11... | collective-permute-start | bytes 1327112 | tf_op jit(solution)/shard_map/ppermute | solution.py:493
  277.1 10.1 %key_backward.7 = f32[2,192,1024]{2,1,0:T(8,128)S(1)} custom-call(bf16[64,64]{1,0:T(8,128)(2,1)S(1)} %bitcast.169, bf16[64,128]{1,0:T(8,128)(2,1)S(1)} %pad_maximum_fusion.21.planes_t, bf16[80,2048]{1,0:T(8,128)(2,1)S(1)} %copy-done.17, bf16[576,512]{1,0:T(8,128)(2,1)} %bitcast.14.refs_0_.refs_2_.ka.va, bf16[384,512]{1,0:T(8,128)(2,1)S(1)} %bitcast.151, ...), custom_call_target="tpu_custom_call" | custom-call | flops 27499999232 | bytes 1048576 | tf_op jit(solution)/shard_map/key_backward/pallas_call | solution.py:243
  287.3 5.3 %collective-permute-done.54 = bf16[192,1024]{1,0:T(8,128)(2,1)S(1)} collective-permute-done((bf16[192,1024]{1,0:T(8,128)(2,1)S(1)}, bf16[192,1024]{1,0:T(8,128)(2,1)S(1)}, u32[]{:S(2)}, u32[]{:S(2)}) %collective-permute-start.54) | collective-permute-done | bytes 393248 | tf_op jit(solution)/shard_map/ppermute | solution.py:496
  301.0 3.1 collective-permute-done.57.refs_3_
  304.1 7.0 %collective-permute-done.56.refs_2_ = bf16[3,192,256]{2,1,0:T(8,128)(2,1)S(1)} collective-permute-done((bf16[3,192,256]{2,1,0:T(8,128)(2,1)S(1)}, bf16[3,192,256]{2,1,0:T(8,128)(2,1)S(1)}, u32[]{:S(2)}, u32[]{:S(2)}) %collective-permute-start.56) | collective-permute-done | bytes 294944 | tf_op jit(solution)/shard_map/ppermute | solution.py:503
  311.9 5.2 %input_grad.1 = bf16[256,768]{1,0:T(8,128)(2,1)} custom-call(s32[2]{0:T(128)} %pad_add_fusion.core, f32[256,768]{1,0:T(8,128)} %get-tuple-element.190.grad_first, bf16[3,192,256]{2,1,0:T(8,128)(2,1)} %pad_maximum_fusion.13.refs_0_, bf16[3,192,256]{2,1,0:T(8,128)(2,1)} %copy-done.62, bf16[3,192,256]{2,1,0:T(8,128)(2,1)} %copy-done.61, ...), custom_call_target="tpu_custom_call" | custom-call | flops 3300000000 | bytes 1048576 | tf_op jit(solution)/shard_map/input_grad/pallas_call | solution.py:399
  319.8 11.2 %collective-permute-done.61 = bf16[128,768]{1,0:T(8,128)(2,1)S(1)} collective-permute-done((bf16[128,768]{1,0:T(8,128)(2,1)S(1)}, bf16[128,768]{1,0:T(8,128)(2,1)S(1)}, u32[]{:S(2)}, u32[]{:S(2)}) %collective-permute-start.61) | collective-permute-done | bytes 196640 | tf_op jit(solution)/shard_map/ppermute | solution.py:500
  337.1 2.8 copy.55
  339.8 3.5 collective-permute-done.67
  343.5 8.0 %collective-permute-done.66 = bf16[2,128,768]{2,1,0:T(8,128)(2,1)S(1)} collective-permute-done((bf16[2,128,768]{2,1,0:T(8,128)(2,1)S(1)}, bf16[2,128,768]{2,1,0:T(8,128)(2,1)S(1)}, u32[]{:S(2)}, u32[]{:S(2)}) %collective-permute-start.66) | collective-permute-done | bytes 393248 | tf_op jit(solution)/shard_map/ppermute | solution.py:503
  352.0 2.2 collective-permute-start.69
  354.6 4.1 %copy.56 = f32[1,512,2,768]{3,2,1,0:T(2,128)} copy(f32[1,512,2,768]{3,1,2,0:T(8,128)S(1)} %maximum_convert_fusion) | data formatting | bytes 6291456
  363.0 2.0 copy.57
  366.3 3.0 maximum_convert_fusion.1
  (350 shorter events, 96.8 us)
Async XLA Ops:
  7.2 244.4 %reduce-scatter.4.cloned.1.call-start = ((), (), s32[]{:S(2)}) async-start(), calls=%async_computation.2 | async-start | bytes 6881280
  12.6 12.5 %collective-permute-start = (bf16[128,768]{1,0:T(8,128)(2,1)}, bf16[128,768]{1,0:T(8,128)(2,1)}, u32[]{:S(2)}, u32[]{:S(2)}) collective-permute-start(bf16[128,768]{1,0:T(8,128)(2,1)} %bitcast.145), channel_id=1, source_target_pairs={{0,16},{8,24},{16,0},{24,8},{1,17},{9,25},{17,1},{25,9},{2,18},{10... | collective-permute-start | bytes 589832 | tf_op jit(solution)/shard_map/ppermute | solution.py:500
  16.3 19.8 %collective-permute-start.1 = (bf16[8,8,64]{2,0,1:T(8,128)(2,1)}, bf16[8,8,64]{2,0,1:T(8,128)(2,1)S(1)}, u32[]{:S(2)}, u32[]{:S(2)}) collective-permute-start(bf16[8,8,64]{2,0,1:T(8,128)(2,1)} %fusion.17), channel_id=1, source_target_pairs={{0,0},{8,1},{16,8},{24,9},{1,16},{9,17},{17,24},{25,25},{2,2},{10,... | collective-permute-start | bytes 24584 | tf_op jit(solution)/shard_map/ppermute | solution.py:524
  26.6 13.9 %collective-permute-start.2 = (bf16[576,512]{1,0:T(8,128)(2,1)}, bf16[576,512]{1,0:T(8,128)(2,1)}, u32[]{:S(2)}, u32[]{:S(2)}) collective-permute-start(bf16[576,512]{1,0:T(8,128)(2,1)} %bitcast.14.refs_0_.refs_2_.ka.va), channel_id=1, source_target_pairs={{0,8},{8,0},{16,24},{24,16},{1,9},{9,1},{17,25},{25,17},{2,10},{10... | collective-permute-start | bytes 1769480 | tf_op jit(solution)/shard_map/ppermute | solution.py:496
  27.8 12.7 %collective-permute-start.3 = (bf16[576,512]{1,0:T(8,128)(2,1)}, bf16[576,512]{1,0:T(8,128)(2,1)}, u32[]{:S(2)}, u32[]{:S(2)}) collective-permute-start(bf16[576,512]{1,0:T(8,128)(2,1)} %bitcast.14.refs_0_.refs_2_.ka.va), channel_id=1, source_target_pairs={{0,1},{1,0},{2,3},{3,2},{4,5},{5,4},{6,7},{7,6},{8,9},{9,8},{10,11... | collective-permute-start | bytes 1769480 | tf_op jit(solution)/shard_map/ppermute | solution.py:493
  33.7 12.1 %collective-permute-start.4 = (bf16[1,128,768]{2,1,0:T(8,128)(2,1)}, bf16[1,128,768]{2,1,0:T(8,128)(2,1)S(1)}, u32[]{:S(2)}, u32[]{:S(2)}) collective-permute-start(bf16[1,128,768]{2,1,0:T(8,128)(2,1)} %bitcast.20), channel_id=1, source_target_pairs={{0,2},{2,0},{4,6},{6,4},{1,3},{3,1},{5,7},{7,5},{8,10},{10,8},{12,... | collective-permute-start | bytes 589832 | tf_op jit(solution)/shard_map/ppermute | solution.py:503
  34.9 10.9 %collective-permute-start.5 = (bf16[1,128,768]{2,1,0:T(8,128)(2,1)}, bf16[1,128,768]{2,1,0:T(8,128)(2,1)S(1)}, u32[]{:S(2)}, u32[]{:S(2)}) collective-permute-start(bf16[1,128,768]{2,1,0:T(8,128)(2,1)} %bitcast.20), channel_id=1, source_target_pairs={{0,4},{2,6},{4,0},{6,2},{1,5},{3,7},{5,1},{7,3},{8,12},{10,14},{12... | collective-permute-start | bytes 589832 | tf_op jit(solution)/shard_map/ppermute | solution.py:503
  48.2 17.5 %collective-permute-start.9 = (bf16[384,512]{1,0:T(8,128)(2,1)S(1)}, bf16[384,512]{1,0:T(8,128)(2,1)S(1)}, u32[]{:S(2)}, u32[]{:S(2)}) collective-permute-start(bf16[384,512]{1,0:T(8,128)(2,1)S(1)} %bitcast.147), channel_id=1, source_target_pairs={{0,1},{1,0},{2,3},{3,2},{4,5},{5,4},{6,7},{7,6},{8,9},{9,8},{10,11... | collective-permute-start | bytes 1179656 | tf_op jit(solution)/shard_map/ppermute | solution.py:493
  50.4 23.1 %collective-permute-start.12 = (bf16[384,512]{1,0:T(8,128)(2,1)S(1)}, bf16[384,512]{1,0:T(8,128)(2,1)S(1)}, u32[]{:S(2)}, u32[]{:S(2)}) collective-permute-start(bf16[384,512]{1,0:T(8,128)(2,1)S(1)} %bitcast.148), channel_id=1, source_target_pairs={{0,8},{8,0},{16,24},{24,16},{1,9},{9,1},{17,25},{25,17},{2,10},{10... | collective-permute-start | bytes 1179656 | tf_op jit(solution)/shard_map/ppermute | solution.py:496
  52.5 20.5 %collective-permute-start.11 = (bf16[768,384]{1,0:T(8,128)(2,1)S(1)}, bf16[768,384]{1,0:T(8,128)(2,1)S(1)}, u32[]{:S(2)}, u32[]{:S(2)}) collective-permute-start(bf16[768,384]{1,0:T(8,128)(2,1)S(1)} %get-tuple-element.122.refs_4_.refs_0_), channel_id=1, source_target_pairs={{0,4},{2,6},{4,0},{6,2},{1,5},{3,7},{5,1},{7,3},{8,12},{10,14},{12... | collective-permute-start | bytes 1769480 | tf_op jit(solution)/shard_map/ppermute | solution.py:503
  53.7 19.3 %collective-permute-start.8 = (bf16[768,384]{1,0:T(8,128)(2,1)S(1)}, bf16[768,384]{1,0:T(8,128)(2,1)}, u32[]{:S(2)}, u32[]{:S(2)}) collective-permute-start(bf16[768,384]{1,0:T(8,128)(2,1)S(1)} %get-tuple-element.122.refs_4_.refs_0_), channel_id=1, source_target_pairs={{0,2},{2,0},{4,6},{6,4},{1,3},{3,1},{5,7},{7,5},{8,10},{10,8},{12,... | collective-permute-start | bytes 1769480 | tf_op jit(solution)/shard_map/ppermute | solution.py:503
  57.9 16.6 %collective-permute-start.7 = (bf16[192,512]{1,0:T(8,128)(2,1)S(1)}, bf16[192,512]{1,0:T(8,128)(2,1)S(1)}, u32[]{:S(2)}, u32[]{:S(2)}) collective-permute-start(bf16[192,512]{1,0:T(8,128)(2,1)S(1)} %convolution_convert_fusion.1.refs_1_), channel_id=1, source_target_pairs={{0,8},{8,0},{16,24},{24,16},{1,9},{9,1},{17,25},{25,17},{2,10},{10... | collective-permute-start | bytes 589832 | tf_op jit(solution)/shard_map/ppermute | solution.py:496
  73.0 17.8 %collective-permute-start.19 = (bf16[480,768]{1,0:T(8,128)(2,1)S(1)}, bf16[480,768]{1,0:T(8,128)(2,1)}, u32[]{:S(2)}, u32[]{:S(2)}) collective-permute-start(bf16[480,768]{1,0:T(8,128)(2,1)S(1)} %copy-done.36), channel_id=1, source_target_pairs={{0,4},{2,6},{4,0},{6,2},{1,5},{3,7},{5,1},{7,3},{8,12},{10,14},{12... | collective-permute-start | bytes 2211848 | tf_op jit(solution)/shard_map/ppermute | solution.py:503
  73.3 18.8 %collective-permute-start.18 = (bf16[480,768]{1,0:T(8,128)(2,1)S(1)}, bf16[480,768]{1,0:T(8,128)(2,1)S(1)}, u32[]{:S(2)}, u32[]{:S(2)}) collective-permute-start(bf16[480,768]{1,0:T(8,128)(2,1)S(1)} %copy-done.36), channel_id=1, source_target_pairs={{0,2},{2,0},{4,6},{6,4},{1,3},{3,1},{5,7},{7,5},{8,10},{10,8},{12,... | collective-permute-start | bytes 2211848 | tf_op jit(solution)/shard_map/ppermute | solution.py:503
  92.8 24.7 %collective-permute-start.28 = (bf16[768,384]{1,0:T(8,128)(2,1)}, bf16[768,384]{1,0:T(8,128)(2,1)}, u32[]{:S(2)}, u32[]{:S(2)}) collective-permute-start(bf16[768,384]{1,0:T(8,128)(2,1)} %collective-permute-done.8.refs_6_.refs_2_), channel_id=1, source_target_pairs={{0,4},{2,6},{4,0},{6,2},{1,5},{3,7},{5,1},{7,3},{8,12},{10,14},{12... | collective-permute-start | bytes 1769480 | tf_op jit(solution)/shard_map/ppermute | solution.py:503
  98.2 18.2 %collective-permute-start.30 = (bf16[480,768]{1,0:T(8,128)(2,1)}, bf16[480,768]{1,0:T(8,128)(2,1)}, u32[]{:S(2)}, u32[]{:S(2)}) collective-permute-start(bf16[480,768]{1,0:T(8,128)(2,1)} %collective-permute-done.19.refs_16_.refs_12_), channel_id=1, source_target_pairs={{0,2},{2,0},{4,6},{6,4},{1,3},{3,1},{5,7},{7,5},{8,10},{10,8},{12,... | collective-permute-start | bytes 2211848 | tf_op jit(solution)/shard_map/ppermute | solution.py:503
  98.6 11.8 %collective-permute-start.24 = (bf16[192,1024]{1,0:T(8,128)(2,1)S(1)}, bf16[192,1024]{1,0:T(8,128)(2,1)}, u32[]{:S(2)}, u32[]{:S(2)}) collective-permute-start(bf16[192,1024]{1,0:T(8,128)(2,1)S(1)} %add_convert_fusion.5), channel_id=1, source_target_pairs={{0,8},{8,0},{16,24},{24,16},{1,9},{9,1},{17,25},{25,17},{2,10},{10... | collective-permute-start | bytes 1179656 | tf_op jit(solution)/shard_map/ppermute | solution.py:496
  104.0 13.4 %collective-permute-start.23 = (bf16[192,1024]{1,0:T(8,128)(2,1)S(1)}, bf16[192,1024]{1,0:T(8,128)(2,1)}, u32[]{:S(2)}, u32[]{:S(2)}) collective-permute-start(bf16[192,1024]{1,0:T(8,128)(2,1)S(1)} %query_estimates.6), channel_id=1, source_target_pairs={{0,1},{1,0},{2,3},{3,2},{4,5},{5,4},{6,7},{7,6},{8,9},{9,8},{10,11... | collective-permute-start | bytes 1179656 | tf_op jit(solution)/shard_map/ppermute | solution.py:493
  155.3 10.9 %collective-permute-start.36 = (bf16[6,256,384]{2,1,0:T(8,128)(2,1)}, bf16[6,256,384]{2,1,0:T(8,128)(2,1)S(1)}, u32[]{:S(2)}, u32[]{:S(2)}) collective-permute-start(bf16[6,256,384]{2,1,0:T(8,128)(2,1)} %get-tuple-element.170), channel_id=1, source_target_pairs={{0,1},{1,0},{2,3},{3,2},{4,5},{5,4},{6,7},{7,6},{8,9},{9,8},{10,11... | collective-permute-start | bytes 3538952 | tf_op jit(solution)/shard_map/ppermute | solution.py:493
  158.5 17.9 %collective-permute-start.38 = (bf16[128,768]{1,0:T(8,128)(2,1)}, bf16[128,768]{1,0:T(8,128)(2,1)}, u32[]{:S(2)}, u32[]{:S(2)}) collective-permute-start(bf16[128,768]{1,0:T(8,128)(2,1)} %get-tuple-element.298), channel_id=1, source_target_pairs={{0,16},{8,24},{16,0},{24,8},{1,17},{9,25},{17,1},{25,9},{2,18},{10... | collective-permute-start | bytes 589832 | tf_op jit(solution)/shard_map/ppermute | solution.py:500
  162.4 13.9 %collective-permute-start.40 = (bf16[192,1024]{1,0:T(8,128)(2,1)S(1)}, bf16[192,1024]{1,0:T(8,128)(2,1)S(1)}, u32[]{:S(2)}, u32[]{:S(2)}) collective-permute-start(bf16[192,1024]{1,0:T(8,128)(2,1)S(1)} %slice_dynamic-update-slice_fusion.refs_4_), channel_id=1, source_target_pairs={{0,1},{1,0},{2,3},{3,2},{4,5},{5,4},{6,7},{7,6},{8,9},{9,8},{10,11... | collective-permute-start | bytes 1179656 | tf_op jit(solution)/shard_map/ppermute | solution.py:493
  165.0 34.6 %collective-permute-start.39 = (bf16[192,1024]{1,0:T(8,128)(2,1)S(1)}, bf16[192,1024]{1,0:T(8,128)(2,1)S(1)}, u32[]{:S(2)}, u32[]{:S(2)}) collective-permute-start(bf16[192,1024]{1,0:T(8,128)(2,1)S(1)} %slice_dynamic-update-slice_fusion.refs_4_), channel_id=1, source_target_pairs={{0,8},{8,0},{16,24},{24,16},{1,9},{9,1},{17,25},{25,17},{2,10},{10... | collective-permute-start | bytes 1179656 | tf_op jit(solution)/shard_map/ppermute | solution.py:496
  176.3 154.7 %all-reduce.3.cloned.1.call-start = ((), (), s32[]{:S(2)}) async-start(), calls=%async_computation.1 | async-start | bytes 2752512 | tf_op jit(solution)/shard_map/psum | solution.py:699
  199.6 14.9 %collective-permute-start.42 = (bf16[192,1024]{1,0:T(8,128)(2,1)S(1)}, bf16[192,1024]{1,0:T(8,128)(2,1)S(1)}, u32[]{:S(2)}, u32[]{:S(2)}) collective-permute-start(bf16[192,1024]{1,0:T(8,128)(2,1)S(1)} %collective-permute-done.39.refs_2_), channel_id=1, source_target_pairs={{0,1},{1,0},{2,3},{3,2},{4,5},{5,4},{6,7},{7,6},{8,9},{9,8},{10,11... | collective-permute-start | bytes 1179656 | tf_op jit(solution)/shard_map/ppermute | solution.py:493
  200.0 14.5 %collective-permute-start.41 = (bf16[192,1024]{1,0:T(8,128)(2,1)S(1)}, bf16[192,1024]{1,0:T(8,128)(2,1)S(1)}, u32[]{:S(2)}, u32[]{:S(2)}) collective-permute-start(bf16[192,1024]{1,0:T(8,128)(2,1)S(1)} %get-tuple-element.180), channel_id=1, source_target_pairs={{0,1},{1,0},{2,3},{3,2},{4,5},{5,4},{6,7},{7,6},{8,9},{9,8},{10,11... | collective-permute-start | bytes 1179656 | tf_op jit(solution)/shard_map/ppermute | solution.py:493
  211.8 34.8 %collective-permute-start.48 = (bf16[2,128,768]{2,1,0:T(8,128)(2,1)S(1)}, bf16[2,128,768]{2,1,0:T(8,128)(2,1)S(1)}, u32[]{:S(2)}, u32[]{:S(2)}) collective-permute-start(bf16[2,128,768]{2,1,0:T(8,128)(2,1)S(1)} %pad_maximum_fusion.11), channel_id=1, source_target_pairs={{0,4},{2,6},{4,0},{6,2},{1,5},{3,7},{5,1},{7,3},{8,12},{10,14},{12... | collective-permute-start | bytes 1179656 | tf_op jit(solution)/shard_map/ppermute | solution.py:503
  211.9 36.0 %collective-permute-start.47 = (bf16[2,128,768]{2,1,0:T(8,128)(2,1)S(1)}, bf16[2,128,768]{2,1,0:T(8,128)(2,1)S(1)}, u32[]{:S(2)}, u32[]{:S(2)}) collective-permute-start(bf16[2,128,768]{2,1,0:T(8,128)(2,1)S(1)} %pad_maximum_fusion.11), channel_id=1, source_target_pairs={{0,2},{2,0},{4,6},{6,4},{1,3},{3,1},{5,7},{7,5},{8,10},{10,8},{12,... | collective-permute-start | bytes 1179656 | tf_op jit(solution)/shard_map/ppermute | solution.py:503
  213.3 34.6 %collective-permute-start.49 = (bf16[2,128,768]{2,1,0:T(8,128)(2,1)S(1)}, bf16[2,128,768]{2,1,0:T(8,128)(2,1)S(1)}, u32[]{:S(2)}, u32[]{:S(2)}) collective-permute-start(bf16[2,128,768]{2,1,0:T(8,128)(2,1)S(1)} %pad_maximum_fusion.11), channel_id=1, source_target_pairs={{0,6},{2,4},{4,2},{6,0},{1,7},{3,5},{5,3},{7,1},{8,14},{10,12},{12... | collective-permute-start | bytes 1179656 | tf_op jit(solution)/shard_map/ppermute | solution.py:503
  235.9 13.4 %collective-permute-start.45 = (bf16[2,192,1024]{2,1,0:T(8,128)(2,1)S(1)}, bf16[2,192,1024]{2,1,0:T(8,128)(2,1)S(1)}, u32[]{:S(2)}, u32[]{:S(2)}) collective-permute-start(bf16[2,192,1024]{2,1,0:T(8,128)(2,1)S(1)} %key_backward.4), channel_id=1, source_target_pairs={{0,1},{1,0},{2,3},{3,2},{4,5},{5,4},{6,7},{7,6},{8,9},{9,8},{10,11... | collective-permute-start | bytes 2359304 | tf_op jit(solution)/shard_map/ppermute | solution.py:493
  236.1 15.3 %collective-permute-start.44 = (bf16[192,1024]{1,0:T(8,128)(2,1)S(1)}, bf16[192,1024]{1,0:T(8,128)(2,1)S(1)}, u32[]{:S(2)}, u32[]{:S(2)}) collective-permute-start(bf16[192,1024]{1,0:T(8,128)(2,1)S(1)} %add_convert_fusion.3), channel_id=1, source_target_pairs={{0,8},{8,0},{16,24},{24,16},{1,9},{9,1},{17,25},{25,17},{2,10},{10... | collective-permute-start | bytes 1179656 | tf_op jit(solution)/shard_map/ppermute | solution.py:496
  246.6 18.1 %collective-permute-start.52 = (bf16[3,96,768]{2,1,0:T(8,128)(2,1)}, bf16[3,96,768]{2,1,0:T(8,128)(2,1)}, u32[]{:S(2)}, u32[]{:S(2)}) collective-permute-start(bf16[3,96,768]{2,1,0:T(8,128)(2,1)} %get-tuple-element.199.refs_4_), channel_id=1, source_target_pairs={{0,6},{2,4},{4,2},{6,0},{1,7},{3,5},{5,3},{7,1},{8,14},{10,12},{12... | collective-permute-start | bytes 1327112 | tf_op jit(solution)/shard_map/ppermute | solution.py:503
  247.9 21.6 %collective-permute-start.51 = (bf16[3,96,768]{2,1,0:T(8,128)(2,1)}, bf16[3,96,768]{2,1,0:T(8,128)(2,1)}, u32[]{:S(2)}, u32[]{:S(2)}) collective-permute-start(bf16[3,96,768]{2,1,0:T(8,128)(2,1)} %get-tuple-element.199.refs_4_), channel_id=1, source_target_pairs={{0,4},{2,6},{4,0},{6,2},{1,5},{3,7},{5,1},{7,3},{8,12},{10,14},{12... | collective-permute-start | bytes 1327112 | tf_op jit(solution)/shard_map/ppermute | solution.py:503
  247.9 21.6 %collective-permute-start.50 = (bf16[3,96,768]{2,1,0:T(8,128)(2,1)}, bf16[3,96,768]{2,1,0:T(8,128)(2,1)}, u32[]{:S(2)}, u32[]{:S(2)}) collective-permute-start(bf16[3,96,768]{2,1,0:T(8,128)(2,1)} %get-tuple-element.199.refs_4_), channel_id=1, source_target_pairs={{0,2},{2,0},{4,6},{6,4},{1,3},{3,1},{5,7},{7,5},{8,10},{10,8},{12,... | collective-permute-start | bytes 1327112 | tf_op jit(solution)/shard_map/ppermute | solution.py:503
  250.6 18.9 %collective-permute-start.46 = (bf16[192,1024]{1,0:T(8,128)(2,1)}, bf16[192,1024]{1,0:T(8,128)(2,1)}, u32[]{:S(2)}, u32[]{:S(2)}) collective-permute-start(bf16[192,1024]{1,0:T(8,128)(2,1)} %get-tuple-element.291), channel_id=1, source_target_pairs={{0,8},{8,0},{16,24},{24,16},{1,9},{9,1},{17,25},{25,17},{2,10},{10... | collective-permute-start | bytes 1179656 | tf_op jit(solution)/shard_map/ppermute | solution.py:496
  262.8 29.7 %collective-permute-start.53 = (bf16[2,192,1024]{2,1,0:T(8,128)(2,1)S(1)}, bf16[2,192,1024]{2,1,0:T(8,128)(2,1)S(1)}, u32[]{:S(2)}, u32[]{:S(2)}) collective-permute-start(bf16[2,192,1024]{2,1,0:T(8,128)(2,1)S(1)} %key_backward.6), channel_id=1, source_target_pairs={{0,1},{1,0},{2,3},{3,2},{4,5},{5,4},{6,7},{7,6},{8,9},{9,8},{10,11... | collective-permute-start | bytes 2359304 | tf_op jit(solution)/shard_map/ppermute | solution.py:493
  269.5 23.1 %collective-permute-start.60 = (bf16[3,96,768]{2,1,0:T(8,128)(2,1)}, bf16[3,96,768]{2,1,0:T(8,128)(2,1)S(1)}, u32[]{:S(2)}, u32[]{:S(2)}) collective-permute-start(bf16[3,96,768]{2,1,0:T(8,128)(2,1)} %collective-permute-done.52.refs_7_), channel_id=1, source_target_pairs={{0,1},{1,0},{2,3},{3,2},{4,5},{5,4},{6,7},{7,6},{8,9},{9,8},{10,11... | collective-permute-start | bytes 1327112 | tf_op jit(solution)/shard_map/ppermute | solution.py:493
  276.6 16.0 %collective-permute-start.59 = (bf16[3,96,768]{2,1,0:T(8,128)(2,1)}, bf16[3,96,768]{2,1,0:T(8,128)(2,1)S(1)}, u32[]{:S(2)}, u32[]{:S(2)}) collective-permute-start(bf16[3,96,768]{2,1,0:T(8,128)(2,1)} %collective-permute-done.51.refs_6_), channel_id=1, source_target_pairs={{0,1},{1,0},{2,3},{3,2},{4,5},{5,4},{6,7},{7,6},{8,9},{9,8},{10,11... | collective-permute-start | bytes 1327112 | tf_op jit(solution)/shard_map/ppermute | solution.py:493
  276.6 16.0 %collective-permute-start.58 = (bf16[3,96,768]{2,1,0:T(8,128)(2,1)}, bf16[3,96,768]{2,1,0:T(8,128)(2,1)S(1)}, u32[]{:S(2)}, u32[]{:S(2)}) collective-permute-start(bf16[3,96,768]{2,1,0:T(8,128)(2,1)} %collective-permute-done.50.refs_5_), channel_id=1, source_target_pairs={{0,1},{1,0},{2,3},{3,2},{4,5},{5,4},{6,7},{7,6},{8,9},{9,8},{10,11... | collective-permute-start | bytes 1327112 | tf_op jit(solution)/shard_map/ppermute | solution.py:493
  277.1 15.4 %collective-permute-start.54 = (bf16[192,1024]{1,0:T(8,128)(2,1)S(1)}, bf16[192,1024]{1,0:T(8,128)(2,1)S(1)}, u32[]{:S(2)}, u32[]{:S(2)}) collective-permute-start(bf16[192,1024]{1,0:T(8,128)(2,1)S(1)} %copy-done.43), channel_id=1, source_target_pairs={{0,8},{8,0},{16,24},{24,16},{1,9},{9,1},{17,25},{25,17},{2,10},{10... | collective-permute-start | bytes 1179656 | tf_op jit(solution)/shard_map/ppermute | solution.py:496
  296.0 15.1 %collective-permute-start.56 = (bf16[3,192,256]{2,1,0:T(8,128)(2,1)S(1)}, bf16[3,192,256]{2,1,0:T(8,128)(2,1)S(1)}, u32[]{:S(2)}, u32[]{:S(2)}) collective-permute-start(bf16[3,192,256]{2,1,0:T(8,128)(2,1)S(1)} %pad_maximum_fusion.15), channel_id=1, source_target_pairs={{0,4},{2,6},{4,0},{6,2},{1,5},{3,7},{5,1},{7,3},{8,12},{10,14},{12... | collective-permute-start | bytes 884744 | tf_op jit(solution)/shard_map/ppermute | solution.py:503
  296.3 14.8 %collective-permute-start.55 = (bf16[3,192,256]{2,1,0:T(8,128)(2,1)S(1)}, bf16[3,192,256]{2,1,0:T(8,128)(2,1)S(1)}, u32[]{:S(2)}, u32[]{:S(2)}) collective-permute-start(bf16[3,192,256]{2,1,0:T(8,128)(2,1)S(1)} %pad_maximum_fusion.14), channel_id=1, source_target_pairs={{0,2},{2,0},{4,6},{6,4},{1,3},{3,1},{5,7},{7,5},{8,10},{10,8},{12,... | collective-permute-start | bytes 884744 | tf_op jit(solution)/shard_map/ppermute | solution.py:503
  298.9 19.5 %collective-permute-start.62 = (bf16[288,768]{1,0:T(8,128)(2,1)S(1)}, bf16[288,768]{1,0:T(8,128)(2,1)S(1)}, u32[]{:S(2)}, u32[]{:S(2)}) collective-permute-start(bf16[288,768]{1,0:T(8,128)(2,1)S(1)} %constant_dynamic-slice_fusion.1), channel_id=1, source_target_pairs={{0,1},{1,0},{2,3},{3,2},{4,5},{5,4},{6,7},{7,6},{8,9},{9,8},{10,11... | collective-permute-start | bytes 1327112 | tf_op jit(solution)/shard_map/ppermute | solution.py:493
  318.2 12.8 %collective-permute-start.61 = (bf16[128,768]{1,0:T(8,128)(2,1)S(1)}, bf16[128,768]{1,0:T(8,128)(2,1)S(1)}, u32[]{:S(2)}, u32[]{:S(2)}) collective-permute-start(bf16[128,768]{1,0:T(8,128)(2,1)S(1)} %get-tuple-element.296), channel_id=1, source_target_pairs={{0,16},{8,24},{16,0},{24,8},{1,17},{9,25},{17,1},{25,9},{2,18},{10... | collective-permute-start | bytes 589832 | tf_op jit(solution)/shard_map/ppermute | solution.py:500
  318.6 13.0 %collective-permute-start.63 = (bf16[144,768]{1,0:T(8,128)(2,1)S(1)}, bf16[144,768]{1,0:T(8,128)(2,1)S(1)}, u32[]{:S(2)}, u32[]{:S(2)}) collective-permute-start(bf16[144,768]{1,0:T(8,128)(2,1)S(1)} %constant_dynamic-slice_fusion), channel_id=1, source_target_pairs={{0,8},{8,0},{16,24},{24,16},{1,9},{9,1},{17,25},{25,17},{2,10},{10... | collective-permute-start | bytes 663560 | tf_op jit(solution)/shard_map/ppermute | solution.py:496
  331.0 29.3 %collective-permute-start.70 = (bf16[896,768]{1,0:T(8,128)(2,1)}, bf16[896,768]{1,0:T(8,128)(2,1)S(1)}, u32[]{:S(2)}, u32[]{:S(2)}) collective-permute-start(bf16[896,768]{1,0:T(8,128)(2,1)} %all-reduce.3.cloned.1.call-done), channel_id=1, source_target_pairs={{0,1},{1,0},{2,3},{3,2},{4,5},{5,4},{6,7},{7,6},{8,9},{9,8},{10,11... | collective-permute-start | bytes 4128776 | tf_op jit(solution)/shard_map/ppermute | solution.py:493
  331.6 11.7 %collective-permute-start.67 = (bf16[144,768]{1,0:T(8,128)(2,1)S(1)}, bf16[144,768]{1,0:T(8,128)(2,1)S(1)}, u32[]{:S(2)}, u32[]{:S(2)}) collective-permute-start(bf16[144,768]{1,0:T(8,128)(2,1)S(1)} %fusion.12), channel_id=1, source_target_pairs={{0,16},{8,24},{16,0},{24,8},{1,17},{9,25},{17,1},{25,9},{2,18},{10... | collective-permute-start | bytes 663560 | tf_op jit(solution)/shard_map/ppermute | solution.py:500
  332.6 10.9 %collective-permute-start.64 = (bf16[2,128,768]{2,1,0:T(8,128)(2,1)S(1)}, bf16[2,128,768]{2,1,0:T(8,128)(2,1)S(1)}, u32[]{:S(2)}, u32[]{:S(2)}) collective-permute-start(bf16[2,128,768]{2,1,0:T(8,128)(2,1)S(1)} %pad_maximum_fusion.12), channel_id=1, source_target_pairs={{0,2},{2,0},{4,6},{6,4},{1,3},{3,1},{5,7},{7,5},{8,10},{10,8},{12,... | collective-permute-start | bytes 1179656 | tf_op jit(solution)/shard_map/ppermute | solution.py:503
  334.9 16.6 %collective-permute-start.66 = (bf16[2,128,768]{2,1,0:T(8,128)(2,1)S(1)}, bf16[2,128,768]{2,1,0:T(8,128)(2,1)S(1)}, u32[]{:S(2)}, u32[]{:S(2)}) collective-permute-start(bf16[2,128,768]{2,1,0:T(8,128)(2,1)S(1)} %pad_maximum_fusion.12), channel_id=1, source_target_pairs={{0,6},{2,4},{4,2},{6,0},{1,7},{3,5},{5,3},{7,1},{8,14},{10,12},{12... | collective-permute-start | bytes 1179656 | tf_op jit(solution)/shard_map/ppermute | solution.py:503
  (93 other events, 665.1 us)
Sparse Core Ops, SparseCore 0:
  176.4 71.4 reduce-scatter.3
  251.7 70.0 all-reduce.2

commit v9 on v8

--- a/solution.py
+++ b/solution.py
@@ -192,7 +192,7 @@
     return call(
         partial(key_kernel, chunk=2, blocks=len(blocks)),
         heads,
-        30 if len(blocks) > 1 else 1,
+        30 if len(blocks) > 1 and start is not None else 1,
         "key_tables",
         specs,
         table_spec(),
@@ -511,7 +511,8 @@
     ]
     near_tokens = jnp.concatenate(here)
     my_quarter = lax.dynamic_slice_in_dim(own, d * quarter, quarter, 0)
-    arrived = [over_group(seq_rows(my_quarter, g + k), k) for k in range(1, groups)]
+    sent = [seq_rows(my_quarter, g + k) for k in range(1, groups)]
+    arrived = [over_group(x, k + 1) for k, x in enumerate(sent)]
 
     signed = (2 * planes - 1).astype(bf16)
     if planes.shape[0] == SETS and groups == 2:
@@ -535,6 +536,12 @@
         return jnp.concatenate([rows_down, lax.dynamic_slice_in_dim(w_out, at * out_cut, out_cut, 0)])
 
     down, downs = down_half(s), [down_half(1 - s)]
+    up_weight = after(up_weight, *sent)
+    up, up_other = [
+        lax.dynamic_slice_in_dim(up_weight, at * (hidden_own // 2), hidden_own // 2, 1) for at in (s, 1 - s)
+    ]
+    ups = [up, up_other]
+    up_x, up_y = over_head(up, 1), over_head(up, 2)
 
     head_n = head_width // HEAD_DIM
 
@@ -547,18 +554,13 @@
     near_z, near_o = over_place(near), over_seq(near)
     far_quarter = jnp.stack(arrived)
     moved = [over_head(far_quarter, j) for j in range(1, head_count)]
-    ready = after(signed, near_z)
-    tables = key_tables(ready, head_n, [near, near_o], None, f32)
+    tables = key_tables(after(signed, up_x, up_y), head_n, [near, near_o], None, f32)
     moved = [after(x, tables) for x in moved]
 
     near_z = after(near_z, tables)
     near_zo = over_seq(near_z)
 
-    up_weight, mask_pos = after(up_weight, tables), after(mask_pos, tables)
-    up, up_other = [
-        lax.dynamic_slice_in_dim(up_weight, at * (hidden_own // 2), hidden_own // 2, 1) for at in (s, 1 - s)
-    ]
-    ups = [up_other]
+    mask_pos = after(mask_pos, tables)
     slot = jnp.arange(groups, dtype=jnp.int32)[:, None]
     place_of = ((g - slot) % groups) * places + r
     position = s * half_len + place_of * piece + d * quarter + jnp.arange(quarter, dtype=jnp.int32)[None]
@@ -566,7 +568,7 @@
     cot = lax.dynamic_index_in_dim(cot_rows, g, 0, keepdims=False)
     pick = (position.reshape(rows)[:, None] == mask_row[None]).astype(bf16)
     grad_out = jnp.dot(pick, cot, preferred_element_type=f32)
-    ready = after(signed, grad_out, up, down, *ups, *downs)
+    ready = after(signed, grad_out, down, *ups, *downs)
     tables = key_tables(ready, head_n, [near_z, near_zo], tables, f32)
 
     far_tokens = jnp.stack([far_quarter, *moved]).reshape(-1, width)
@@ -578,9 +580,10 @@
     q_o, q_z = over_seq(q), over_place(q)
     n_near = near.shape[1]
 
-    ups, downs = [up] + ups, [down] + downs
-    up = after(up, kv)
-    up_x, up_y = over_head(up, 1), over_head(up, 2)
+    downs = [down] + downs
+    down = after(down, kv)
+    down_x, down_y, up_d = over_head(down, 1), over_head(down, 2), over_head(after(up_x, kv), 2)
+    up_xo, up_yo = over_seq(after(up_x, kv)), over_seq(after(up_y, kv))
     qkv_cut = head_width // 2
     w_qkv_t = w_qkv.transpose(0, 2, 1)
     qkv_near = [lax.dynamic_slice_in_dim(w_qkv_t, s * qkv_cut, qkv_cut, 1)]
@@ -589,27 +592,22 @@
 
     kv_z = after(kv_z, tables)
     kv_zo = over_seq(kv_z)
-    up_x, up_y = after(up_x, tables), after(up_y, tables)
-    down = after(down, up_x, up_y)
-    down_x, down_y, up_d = over_head(down, 1), over_head(down, 2), over_head(up_x, 2)
-    up_xo, up_yo = over_seq(up_x), over_seq(up_y)
-    ready = after(signed, down, tokens, dense_in, qkv_near[0], qkv_far[0])
+    up_xo, up_yo = after(up_xo, tables), after(up_yo, tables)
+    ready = after(signed, up_xo, up_yo, tokens, dense_in, qkv_near[0], qkv_far[0])
     tables = key_tables(ready, head_n, [kv_z], tables, f32)
 
     q_z = after(q_z, tables)
     q_zo = over_seq(q_z)
     kv_zo = after(kv_zo, tables)
-    tables = key_tables(after(signed, q_z), head_n, [kv_zo], tables, bf16)
-
-    q_zo = after(q_zo, tables)
-    up_xo, up_yo = after(up_xo, tables), after(up_yo, tables)
-    q_zo = after(q_zo, up_xo, up_yo)
-    e_zo = query_estimates(signed, head_n, near_zo, q_zo, tables, bf16)
-    down_x, down_y = after(down_x, e_zo), after(down_y, e_zo)
+    down_x, down_y = after(down_x, tables), after(down_y, tables)
     down_d = over_head(down_y, 1)
     down_xo, down_yo = over_seq(down_x), over_seq(down_y)
+    tables = key_tables(after(signed, q_z, down_x, down_y), head_n, [kv_zo], tables, bf16)
+
+    q_zo = after(q_zo, tables)
+    e_zo = query_estimates(signed, head_n, near_zo, q_zo, tables, bf16)
     e_zo_moved = over_seq(e_zo)
-    e_z = query_estimates(signed, head_n, near_z, after(q_z, e_zo, down_x, down_y), tables, bf16)
+    e_z = query_estimates(signed, head_n, near_z, after(q_z, e_zo), tables, bf16)
     e_far = add(e_z, after(e_zo_moved, e_z)).astype(bf16)
     down_xo, down_yo = after(down_xo, e_z), after(down_yo, e_z)
     ready = after(q_o, e_far, down_xo, down_yo)

time: 382 us -> 377 us (0.987)
  starting transfers between devices: 71.9 us -> 65.9 us
    ppermute x29, starting transfers between devices: 30.1 us -> 20.9 us  [over_seq(): return lax.ppermute(x, 'seq', [(0, 1), (1, 0)])]
  transfers between devices with their start and end apart: 73 -> 73, of which waited for: 13 -> 11; matrix products, arithmetic and copies ran while one was open for 11% -> 12% of each run, Pallas kernels for 36% -> 36%
where the time goes in v9:
time: 377 us; the launch traced here: 373 us
  Pallas kernels  159 us (42%)
  starting transfers between devices  65.9 us (17%)
  waiting for transfers between devices  57.8 us (15%)
  local copies, waits for them, and re-layouts  42.7 us (11%)
  other arithmetic  27.8 us (7%)
  between operations  15.6 us (4%)
  matrix products  4.13 us (1%)
    pallas_call x3, Pallas kernels, query_backward(): call(partial(query_back_kernel, chunk=4, blocks=blocks, last=last), heads...  43.4 us
    pallas_call x4, Pallas kernels, key_backward(): call(partial(key_back_kernel, chunk=4), heads, 25, 'key_backward', [whole...  38.3 us
    pallas_call x4, Pallas kernels, single(): pl.pallas_call(kernel, in_specs=[pl.BlockSpec(memory_space=pltpu.SMEM)] +...  38.1 us
    ppermute x27, waiting for transfers between devices, over_head(): return lax.ppermute(x, 'head', [(h, h ^ j) for h in range(head_count)])  31.8 us
    unnamed x149, local copies, waits for them, and re-layouts  25.9 us
    ppermute x27, starting transfers between devices, over_head(): return lax.ppermute(x, 'head', [(h, h ^ j) for h in range(head_count)])  25.9 us
    pallas_call x5, Pallas kernels, key_tables(): call(partial(key_kernel, chunk=2, blocks=len(blocks)), heads, 30 if len(b...  23.1 us
    ppermute x29, starting transfers between devices, over_seq(): return lax.ppermute(x, 'seq', [(0, 1), (1, 0)])  20.9 us
  transfers between devices with their start and end apart: 73, of which 11 were waited for; matrix products, arithmetic and copies ran while one was open for 12% of the time, Pallas kernels for 36%

profile of v9, /device:TPU:1, one launch (start us, length us, event | category | flops | bytes accessed | tf_op | source)
XLA Modules:
  0.0 373.1 jit_solution(12877941171267807037)
XLA Ops:
  7.3 4.5 %constant_dynamic-slice_fusion.10 = (bf16[1,128,1,768]{3,2,1,0:T(2,128)(2,1)S(1)}, bf16[1,128,1,768]{3,2,1,0:T(2,128)(2,1)}, bf16[1,128,1,768]{3,2,1,0:T(2,128)(...) fusion(bf16[1,512,2,768]{3,2,1,0:T(2,128)(2,1)} %param.11, s32[]{:T(128)S(6)} %select_n.263, ...), kind=kLoop, calls=%fused_computation.121 | loop fusion | bytes 1966104 | tf_op jit(solution)/shard_map/jit(dynamic_index_in_dim)/dynamic_slice | solution.py:506
  12.6 3.1 collective-permute-start
  15.7 2.4 constant_dynamic-slice_fusion.4
  21.2 3.6 collective-permute-start.1
  36.3 1.9 slice.154
  39.9 5.2 %key_tables.5.refs_4_ = f32[3,2048,64]{2,1,0:T(8,128)S(1)} custom-call(bf16[64,64]{1,0:T(8,128)(2,1)S(1)} %bitcast.153, bf16[576,512]{1,0:T(8,128)(2,1)} %bitcast.14.refs_0_.refs_2_.ka.va, bf16[576,512]{1,0:T(8,128)(2,1)} %collective-permute-done.4.refs_1_.refs_3_.refs_0_.refs_2_.ka.va, bf16[576,512]{1,0:T(8,128)(2,1)} %bitcast.14.refs_0_.refs_2_.ka.va, ...), custom_call_target="tpu_custom_call" | custom-call | flops 1100000000 | bytes 1048576 | tf_op jit(solution)/shard_map/key_tables/pallas_call | solution.py:192
  45.2 2.1 pad_maximum_fusion.6
  48.2 2.2 collective-permute-start.10
  50.4 2.3 collective-permute-start.14
  57.2 5.6 %key_tables.6.refs_4_ = f32[3,2048,64]{2,1,0:T(8,128)S(1)} custom-call(bf16[64,64]{1,0:T(8,128)(2,1)S(1)} %bitcast.154, bf16[576,512]{1,0:T(8,128)(2,1)} %collective-permute-done.11.refs_0_.refs_2_.ka.va, bf16[576,512]{1,0:T(8,128)(2,1)S(1)} %collective-permute-done.12.refs_1_.refs_3_.refs_0_.ka.va, ...), custom_call_target="tpu_custom_call" | custom-call | flops 32999999488 | bytes 1048576 | tf_op jit(solution)/shard_map/key_tables/pallas_call | solution.py:192
  64.9 5.5 %key_tables.7.refs_2_ = f32[3,2048,64]{2,1,0:T(8,128)S(1)} custom-call(bf16[64,64]{1,0:T(8,128)(2,1)S(1)} %bitcast.155, bf16[384,512]{1,0:T(8,128)(2,1)S(1)} %bitcast.149, bf16[384,512]{1,0:T(8,128)(2,1)S(1)} %collective-permute-done.10.refs_1_.refs_3_.kb.vb, bf16[384,512]{1,0:T(8,128)(2,1)S(1)} %bitcast.150, ...), custom_call_target="tpu_custom_call" | custom-call | flops 32999999488 | bytes 1048576 | tf_op jit(solution)/shard_map/key_tables/pallas_call | solution.py:192
  73.5 1.8 pad_maximum_fusion.10.x_in
  76.2 4.2 %key_tables.8.refs_2_ = f32[3,2048,64]{2,1,0:T(8,128)S(1)} custom-call(bf16[64,64]{1,0:T(8,128)(2,1)S(1)} %bitcast.156, bf16[384,512]{1,0:T(8,128)(2,1)S(1)} %collective-permute-done.14.refs_0_.refs_1_.kb.vb, bf16[384,512]{1,0:T(8,128)(2,1)S(1)} %collective-permute-done.14.refs_0_.refs_1_.kb.vb, f32[3,2048,64]{2,1,0:T(8,128)} %copy-done.2), custom_call_target="tpu_custom_call" | custom-call | flops 1100000000 | bytes 1048576 | tf_op jit(solution)/shard_map/key_tables/pallas_call | solution.py:192
  81.4 2.6 key_tables.9.tables
  84.0 3.3 query_estimates.4
  88.2 4.2 %query_estimates.5 = bf16[192,1024]{1,0:T(8,128)(2,1)S(1)} custom-call(bf16[64,64]{1,0:T(8,128)(2,1)S(1)} %bitcast.159, bf16[3,2048,64]{2,1,0:T(8,128)(2,1)S(1)} %key_tables.9.tables, bf16[576,512]{1,0:T(8,128)(2,1)} %collective-permute-done.11.refs_0_.refs_2_.ka.va, bf16[192,512]{1,0:T(8,128)(2,1)S(1)} %collective-permute-done.8.refs_1_), custom_call_target="tpu_custom_call" | custom-call | flops 1100000000 | bytes 1048576 | tf_op jit(solution)/shard_map/query_estimates/pallas_call | solution.py:205
  95.5 4.2 %query_estimates.6 = bf16[192,1024]{1,0:T(8,128)(2,1)S(1)} custom-call(bf16[64,64]{1,0:T(8,128)(2,1)S(1)} %bitcast.160, bf16[3,2048,64]{2,1,0:T(8,128)(2,1)S(1)} %key_tables.9.tables, bf16[576,512]{1,0:T(8,128)(2,1)} %collective-permute-done.4.refs_1_.refs_3_.refs_0_.refs_2_.ka.va, bf16[192,512]{1,0:T(8,128)(2,1)S(1)} %collective-permute-done.18.refs_1_.refs_3_), custom_call_target="tpu_custom_call" | custom-call | flops 1100000000 | bytes 1048576 | tf_op jit(solution)/shard_map/query_estimates/pallas_call | solution.py:205
  101.3 4.7 %query_estimates.7 = f32[192,1024]{1,0:T(8,128)S(1)} custom-call(bf16[64,64]{1,0:T(8,128)(2,1)S(1)} %bitcast.162, bf16[3,2048,64]{2,1,0:T(8,128)(2,1)S(1)} %key_tables.9.tables, bf16[576,512]{1,0:T(8,128)(2,1)} %bitcast.14.refs_0_.refs_2_.ka.va, bf16[192,512]{1,0:T(8,128)(2,1)S(1)} %convolution_convert_fusion.1.refs_1_), custom_call_target="tpu_custom_call" | custom-call | flops 1100000000 | bytes 1048576 | tf_op jit(solution)/shard_map/query_estimates/pallas_call | solution.py:205
  106.0 4.4 %collective-permute-done.30.refs_18_.refs_14_ = bf16[480,768]{1,0:T(8,128)(2,1)} collective-permute-done((bf16[480,768]{1,0:T(8,128)(2,1)}, bf16[480,768]{1,0:T(8,128)(2,1)}, u32[]{:S(2)}, u32[]{:S(2)}) %collective-permute-start.30) | collective-permute-done | bytes 737312 | tf_op jit(solution)/shard_map/ppermute | solution.py:503
  113.0 2.7 collective-permute-start.27
  118.5 2.0 collective-permute-done.26.refs_2_.refs_6_
  122.2 12.2 %dense.1 = (bf16[256,768]{1,0:T(8,128)(2,1)}, f32[256,768]{1,0:T(8,128)}, f32[256,768]{1,0:T(8,128)}, f32[8,256,384]{2,1,0:T(8,128)}, bf16[8,256,384]{2,1,0:T(8,...) custom-call(s32[2]{0:T(128)} %pad_add_fusion.core, ...), custom_call_target="tpu_custom_call" | custom-call | flops 15399999488 | bytes 1048576 | tf_op jit(solution)/shard_map/dense/pallas_call | solution.py:399
  134.5 12.2 %dense_back.1 = (f32[256,768]{1,0:T(8,128)}, bf16[6,256,384]{2,1,0:T(8,128)(2,1)}, bf16[6,256,384]{2,1,0:T(8,128)(2,1)}, bf16[192,256]{1,0:T(8,128)(2,1)}, bf16[...) custom-call(s32[2]{0:T(128)} %pad_add_fusion.core, ...), custom_call_target="tpu_custom_call" | custom-call | flops 8800000000 | bytes 1048576 | tf_op jit(solution)/shard_map/dense_back/pallas_call | solution.py:399
  146.8 1.9 collective-permute-start.32
  155.3 2.1 collective-permute-start.40
  160.3 8.5 %weight_grads.1 = bf16[4,896,768]{2,1,0:T(8,128)(2,1)} custom-call(s32[2]{0:T(128)} %pad_add_fusion.core, f32[8,768]{1,0:T(8,128)} %get-tuple-element.161.small_a, f32[8,768]{1,0:T(8,128)} %get-tuple-element.162.small_b, bf16[8,256,384]{2,1,0:T(8,128)(2,1)} %get-tuple-element.163.refs_0_, bf16[8,256,384]{2,1,0:T(8,128)(2,1)} %copy-done.47, ...), custom_call_target="tpu_custom_call" | custom-call | flops 7699999744 | bytes 1048576 | tf_op jit(solution)/shard_map/weight_grads/pallas_call | solution.py:399
  171.8 20.2 %query_backward.3 = (f32[3,2048,64]{2,1,0:T(8,128)}, f32[192,1024]{1,0:T(8,128)S(1)}, bf16[192,1024]{1,0:T(8,128)(2,1)S(1)}) custom-call(bf16[64,64]{1,0:T(8,128)(2,1)S(1)} %bitcast.163, bf16[64,128]{1,0:T(8,128)(2,1)S(1)} %pad_maximum_fusion.21.planes_t, bf16[80,2048]{1,0:T(8,128)(2,1)S(1)} %copy-done.16, bf16[3,2048,64]{2,1,0:T(8,128)(2,1)S(1)} %key_tables.9.tables, ...), custom_call_target="tpu_custom_call" | custom-call | flops 54999998464 | bytes 1048576 | tf_op jit(solution)/shard_map/query_backward/pallas_call | solution.py:229
  192.7 11.9 %query_backward.4 = (f32[3,2048,64]{2,1,0:T(8,128)}, f32[192,1024]{1,0:T(8,128)S(1)}) custom-call(bf16[64,64]{1,0:T(8,128)(2,1)S(1)} %bitcast.164, bf16[64,128]{1,0:T(8,128)(2,1)S(1)} %pad_maximum_fusion.21.planes_t, bf16[80,2048]{1,0:T(8,128)(2,1)S(1)} %copy-done.16, bf16[3,2048,64]{2,1,0:T(8,128)(2,1)S(1)} %key_tables.9.tables, ...), custom_call_target="tpu_custom_call" | custom-call | flops 27499999232 | bytes 1048576 | tf_op jit(solution)/shard_map/query_backward/pallas_call | solution.py:229
  207.4 11.3 %query_backward.5 = (bf16[3,2048,64]{2,1,0:T(8,128)(2,1)S(1)}, bf16[192,1024]{1,0:T(8,128)(2,1)S(1)}) custom-call(bf16[64,64]{1,0:T(8,128)(2,1)S(1)} %bitcast.165, bf16[64,128]{1,0:T(8,128)(2,1)S(1)} %pad_maximum_fusion.21.planes_t, bf16[80,2048]{1,0:T(8,128)(2,1)S(1)} %copy-done.16, bf16[3,2048,64]{2,1,0:T(8,128)(2,1)S(1)} %key_tables.9.tables, ...), custom_call_target="tpu_custom_call" | custom-call | flops 27499999232 | bytes 1048576 | tf_op jit(solution)/shard_map/query_backward/pallas_call | solution.py:229
  220.0 8.7 %key_backward.4 = bf16[2,192,1024]{2,1,0:T(8,128)(2,1)S(1)} custom-call(bf16[64,64]{1,0:T(8,128)(2,1)S(1)} %bitcast.166, bf16[64,128]{1,0:T(8,128)(2,1)S(1)} %pad_maximum_fusion.21.planes_t, bf16[80,2048]{1,0:T(8,128)(2,1)S(1)} %copy-done.17, bf16[576,512]{1,0:T(8,128)(2,1)S(1)} %copy-done.11, bf16[384,512]{1,0:T(8,128)(2,1)S(1)} %copy-done.7, ...), custom_call_target="tpu_custom_call" | custom-call | flops 27499999232 | bytes 1048576 | tf_op jit(solution)/shard_map/key_backward/pallas_call | solution.py:243
  229.8 9.7 %key_backward.5 = bf16[2,192,1024]{2,1,0:T(8,128)(2,1)S(1)} custom-call(bf16[64,64]{1,0:T(8,128)(2,1)S(1)} %bitcast.167, bf16[64,128]{1,0:T(8,128)(2,1)S(1)} %pad_maximum_fusion.21.planes_t, bf16[80,2048]{1,0:T(8,128)(2,1)S(1)} %copy-done.17, bf16[576,512]{1,0:T(8,128)(2,1)} %collective-permute-done.11.refs_0_.refs_2_.ka.va, bf16[384,512]{1,0:T(8,128)(2,1)S(1)} %copy-done.5, ...), custom_call_target="tpu_custom_call" | custom-call | flops 27499999232 | bytes 1048576 | tf_op jit(solution)/shard_map/key_backward/pallas_call | solution.py:243
  246.0 9.7 %key_backward.6 = bf16[2,192,1024]{2,1,0:T(8,128)(2,1)S(1)} custom-call(bf16[64,64]{1,0:T(8,128)(2,1)S(1)} %bitcast.168, bf16[64,128]{1,0:T(8,128)(2,1)S(1)} %pad_maximum_fusion.21.planes_t, bf16[80,2048]{1,0:T(8,128)(2,1)S(1)} %copy-done.18, bf16[576,512]{1,0:T(8,128)(2,1)} %collective-permute-done.4.refs_1_.refs_3_.refs_0_.refs_2_.ka.va, ...), custom_call_target="tpu_custom_call" | custom-call | flops 27499999232 | bytes 1048576 | tf_op jit(solution)/shard_map/key_backward/pallas_call | solution.py:243
  255.8 1.8 collective-permute-start.53
  257.6 4.8 %collective-permute-done.51.refs_6_ = bf16[3,96,768]{2,1,0:T(8,128)(2,1)} collective-permute-done((bf16[3,96,768]{2,1,0:T(8,128)(2,1)}, bf16[3,96,768]{2,1,0:T(8,128)(2,1)}, u32[]{:S(2)}, u32[]{:S(2)}) %collective-permute-start.51) | collective-permute-done | bytes 442400 | tf_op jit(solution)/shard_map/ppermute | solution.py:503
  264.4 10.1 %key_backward.7 = f32[2,192,1024]{2,1,0:T(8,128)S(1)} custom-call(bf16[64,64]{1,0:T(8,128)(2,1)S(1)} %bitcast.169, bf16[64,128]{1,0:T(8,128)(2,1)S(1)} %pad_maximum_fusion.21.planes_t, bf16[80,2048]{1,0:T(8,128)(2,1)S(1)} %copy-done.18, bf16[576,512]{1,0:T(8,128)(2,1)} %bitcast.14.refs_0_.refs_2_.ka.va, bf16[384,512]{1,0:T(8,128)(2,1)S(1)} %bitcast.151, ...), custom_call_target="tpu_custom_call" | custom-call | flops 27499999232 | bytes 1048576 | tf_op jit(solution)/shard_map/key_backward/pallas_call | solution.py:243
  274.5 10.9 %collective-permute-done.54 = bf16[192,1024]{1,0:T(8,128)(2,1)S(1)} collective-permute-done((bf16[192,1024]{1,0:T(8,128)(2,1)S(1)}, bf16[192,1024]{1,0:T(8,128)(2,1)S(1)}, u32[]{:S(2)}, u32[]{:S(2)}) %collective-permute-start.54) | collective-permute-done | bytes 393248 | tf_op jit(solution)/shard_map/ppermute | solution.py:496
  293.9 3.0 collective-permute-done.57.refs_3_
  296.9 7.1 %collective-permute-done.56.refs_2_ = bf16[3,192,256]{2,1,0:T(8,128)(2,1)S(1)} collective-permute-done((bf16[3,192,256]{2,1,0:T(8,128)(2,1)S(1)}, bf16[3,192,256]{2,1,0:T(8,128)(2,1)S(1)}, u32[]{:S(2)}, u32[]{:S(2)}) %collective-permute-start.56) | collective-permute-done | bytes 294944 | tf_op jit(solution)/shard_map/ppermute | solution.py:503
  304.8 5.2 %input_grad.1 = bf16[256,768]{1,0:T(8,128)(2,1)} custom-call(s32[2]{0:T(128)} %pad_add_fusion.core, f32[256,768]{1,0:T(8,128)} %get-tuple-element.186.grad_first, bf16[3,192,256]{2,1,0:T(8,128)(2,1)} %pad_maximum_fusion.13.refs_0_, bf16[3,192,256]{2,1,0:T(8,128)(2,1)} %copy-done.61, bf16[3,192,256]{2,1,0:T(8,128)(2,1)} %copy-done.60, ...), custom_call_target="tpu_custom_call" | custom-call | flops 3300000000 | bytes 1048576 | tf_op jit(solution)/shard_map/input_grad/pallas_call | solution.py:399
  311.0 2.4 collective-permute-start.61
  314.5 11.5 %collective-permute-done.61 = bf16[128,768]{1,0:T(8,128)(2,1)S(1)} collective-permute-done((bf16[128,768]{1,0:T(8,128)(2,1)S(1)}, bf16[128,768]{1,0:T(8,128)(2,1)S(1)}, u32[]{:S(2)}, u32[]{:S(2)}) %collective-permute-start.61) | collective-permute-done | bytes 196640 | tf_op jit(solution)/shard_map/ppermute | solution.py:500
  332.3 2.8 copy.55
  335.0 3.4 collective-permute-done.67
  338.6 8.1 %collective-permute-done.66 = bf16[2,128,768]{2,1,0:T(8,128)(2,1)S(1)} collective-permute-done((bf16[2,128,768]{2,1,0:T(8,128)(2,1)S(1)}, bf16[2,128,768]{2,1,0:T(8,128)(2,1)S(1)}, u32[]{:S(2)}, u32[]{:S(2)}) %collective-permute-start.66) | collective-permute-done | bytes 393248 | tf_op jit(solution)/shard_map/ppermute | solution.py:503
  347.2 2.0 collective-permute-start.69
  349.6 4.1 %copy.56 = f32[1,512,2,768]{3,2,1,0:T(2,128)} copy(f32[1,512,2,768]{3,1,2,0:T(8,128)S(1)} %maximum_convert_fusion) | data formatting | bytes 6291456
  358.0 2.0 copy.57
  361.2 3.0 maximum_convert_fusion.1
  (350 shorter events, 94.5 us)
Async XLA Ops:
  7.2 237.3 %reduce-scatter.4.cloned.1.call-start = ((), (), s32[]{:S(2)}) async-start(), calls=%async_computation.2 | async-start | bytes 6881280
  12.6 15.9 %collective-permute-start = (bf16[128,768]{1,0:T(8,128)(2,1)}, bf16[128,768]{1,0:T(8,128)(2,1)}, u32[]{:S(2)}, u32[]{:S(2)}) collective-permute-start(bf16[128,768]{1,0:T(8,128)(2,1)} %bitcast.145), channel_id=1, source_target_pairs={{0,16},{8,24},{16,0},{24,8},{1,17},{9,25},{17,1},{25,9},{2,18},{10... | collective-permute-start | bytes 589832 | tf_op jit(solution)/shard_map/ppermute | solution.py:500
  18.1 14.5 %collective-permute-start.2 = (bf16[768,384]{1,0:T(8,128)(2,1)}, bf16[768,384]{1,0:T(8,128)(2,1)}, u32[]{:S(2)}, u32[]{:S(2)}) collective-permute-start(bf16[768,384]{1,0:T(8,128)(2,1)} %get-tuple-element.282.refs_4_.refs_0_), channel_id=1, source_target_pairs={{0,2},{2,0},{4,6},{6,4},{1,3},{3,1},{5,7},{7,5},{8,10},{10,8},{12,... | collective-permute-start | bytes 1769480 | tf_op jit(solution)/shard_map/ppermute | solution.py:503
  19.4 14.2 %collective-permute-start.3 = (bf16[768,384]{1,0:T(8,128)(2,1)}, bf16[768,384]{1,0:T(8,128)(2,1)}, u32[]{:S(2)}, u32[]{:S(2)}) collective-permute-start(bf16[768,384]{1,0:T(8,128)(2,1)} %get-tuple-element.282.refs_4_.refs_0_), channel_id=1, source_target_pairs={{0,4},{2,6},{4,0},{6,2},{1,5},{3,7},{5,1},{7,3},{8,12},{10,14},{12... | collective-permute-start | bytes 1769480 | tf_op jit(solution)/shard_map/ppermute | solution.py:503
  21.2 11.2 %collective-permute-start.1 = (bf16[8,8,64]{2,0,1:T(8,128)(2,1)}, bf16[8,8,64]{2,0,1:T(8,128)(2,1)S(1)}, u32[]{:S(2)}, u32[]{:S(2)}) collective-permute-start(bf16[8,8,64]{2,0,1:T(8,128)(2,1)} %fusion.17), channel_id=1, source_target_pairs={{0,0},{8,1},{16,8},{24,9},{1,16},{9,17},{17,24},{25,25},{2,2},{10,... | collective-permute-start | bytes 24584 | tf_op jit(solution)/shard_map/ppermute | solution.py:525
  31.0 23.4 %collective-permute-start.11 = (bf16[576,512]{1,0:T(8,128)(2,1)}, bf16[576,512]{1,0:T(8,128)(2,1)}, u32[]{:S(2)}, u32[]{:S(2)}) collective-permute-start(bf16[576,512]{1,0:T(8,128)(2,1)} %bitcast.14.refs_0_.refs_2_.ka.va), channel_id=1, source_target_pairs={{0,8},{8,0},{16,24},{24,16},{1,9},{9,1},{17,25},{25,17},{2,10},{10... | collective-permute-start | bytes 1769480 | tf_op jit(solution)/shard_map/ppermute | solution.py:496
  32.4 12.7 %collective-permute-start.5 = (bf16[1,128,768]{2,1,0:T(8,128)(2,1)}, bf16[1,128,768]{2,1,0:T(8,128)(2,1)S(1)}, u32[]{:S(2)}, u32[]{:S(2)}) collective-permute-start(bf16[1,128,768]{2,1,0:T(8,128)(2,1)} %bitcast.20), channel_id=1, source_target_pairs={{0,2},{2,0},{4,6},{6,4},{1,3},{3,1},{5,7},{7,5},{8,10},{10,8},{12,... | collective-permute-start | bytes 589832 | tf_op jit(solution)/shard_map/ppermute | solution.py:503
  32.7 12.5 %collective-permute-start.6 = (bf16[1,128,768]{2,1,0:T(8,128)(2,1)}, bf16[1,128,768]{2,1,0:T(8,128)(2,1)}, u32[]{:S(2)}, u32[]{:S(2)}) collective-permute-start(bf16[1,128,768]{2,1,0:T(8,128)(2,1)} %bitcast.20), channel_id=1, source_target_pairs={{0,4},{2,6},{4,0},{6,2},{1,5},{3,7},{5,1},{7,3},{8,12},{10,14},{12... | collective-permute-start | bytes 589832 | tf_op jit(solution)/shard_map/ppermute | solution.py:503
  33.6 11.6 %collective-permute-start.7 = (bf16[1,128,768]{2,1,0:T(8,128)(2,1)}, bf16[1,128,768]{2,1,0:T(8,128)(2,1)}, u32[]{:S(2)}, u32[]{:S(2)}) collective-permute-start(bf16[1,128,768]{2,1,0:T(8,128)(2,1)} %bitcast.20), channel_id=1, source_target_pairs={{0,6},{2,4},{4,2},{6,0},{1,7},{3,5},{5,3},{7,1},{8,14},{10,12},{12... | collective-permute-start | bytes 589832 | tf_op jit(solution)/shard_map/ppermute | solution.py:503
  48.2 16.3 %collective-permute-start.10 = (bf16[384,512]{1,0:T(8,128)(2,1)S(1)}, bf16[384,512]{1,0:T(8,128)(2,1)S(1)}, u32[]{:S(2)}, u32[]{:S(2)}) collective-permute-start(bf16[384,512]{1,0:T(8,128)(2,1)S(1)} %bitcast.147), channel_id=1, source_target_pairs={{0,1},{1,0},{2,3},{3,2},{4,5},{5,4},{6,7},{7,6},{8,9},{9,8},{10,11... | collective-permute-start | bytes 1179656 | tf_op jit(solution)/shard_map/ppermute | solution.py:493
  50.4 21.7 %collective-permute-start.14 = (bf16[384,512]{1,0:T(8,128)(2,1)S(1)}, bf16[384,512]{1,0:T(8,128)(2,1)S(1)}, u32[]{:S(2)}, u32[]{:S(2)}) collective-permute-start(bf16[384,512]{1,0:T(8,128)(2,1)S(1)} %bitcast.148), channel_id=1, source_target_pairs={{0,8},{8,0},{16,24},{24,16},{1,9},{9,1},{17,25},{25,17},{2,10},{10... | collective-permute-start | bytes 1179656 | tf_op jit(solution)/shard_map/ppermute | solution.py:496
  52.7 28.1 %collective-permute-start.16 = (bf16[480,768]{1,0:T(8,128)(2,1)S(1)}, bf16[480,768]{1,0:T(8,128)(2,1)}, u32[]{:S(2)}, u32[]{:S(2)}) collective-permute-start(bf16[480,768]{1,0:T(8,128)(2,1)S(1)} %copy-done.36), channel_id=1, source_target_pairs={{0,4},{2,6},{4,0},{6,2},{1,5},{3,7},{5,1},{7,3},{8,12},{10,14},{12... | collective-permute-start | bytes 2211848 | tf_op jit(solution)/shard_map/ppermute | solution.py:503
  54.4 26.4 %collective-permute-start.15 = (bf16[480,768]{1,0:T(8,128)(2,1)S(1)}, bf16[480,768]{1,0:T(8,128)(2,1)S(1)}, u32[]{:S(2)}, u32[]{:S(2)}) collective-permute-start(bf16[480,768]{1,0:T(8,128)(2,1)S(1)} %copy-done.36), channel_id=1, source_target_pairs={{0,2},{2,0},{4,6},{6,4},{1,3},{3,1},{5,7},{7,5},{8,10},{10,8},{12,... | collective-permute-start | bytes 2211848 | tf_op jit(solution)/shard_map/ppermute | solution.py:503
  57.0 16.4 %collective-permute-start.13 = (bf16[768,384]{1,0:T(8,128)(2,1)}, bf16[768,384]{1,0:T(8,128)(2,1)S(1)}, u32[]{:S(2)}, u32[]{:S(2)}) collective-permute-start(bf16[768,384]{1,0:T(8,128)(2,1)} %collective-permute-done.3.refs_8_.refs_4_), channel_id=1, source_target_pairs={{0,1},{1,0},{2,3},{3,2},{4,5},{5,4},{6,7},{7,6},{8,9},{9,8},{10,11... | collective-permute-start | bytes 1769480 | tf_op jit(solution)/shard_map/ppermute | solution.py:493
  80.8 13.2 %collective-permute-start.22 = (bf16[480,768]{1,0:T(8,128)(2,1)}, bf16[480,768]{1,0:T(8,128)(2,1)S(1)}, u32[]{:S(2)}, u32[]{:S(2)}) collective-permute-start(bf16[480,768]{1,0:T(8,128)(2,1)} %collective-permute-done.16.refs_16_.refs_12_), channel_id=1, source_target_pairs={{0,1},{1,0},{2,3},{3,2},{4,5},{5,4},{6,7},{7,6},{8,9},{9,8},{10,11... | collective-permute-start | bytes 2211848 | tf_op jit(solution)/shard_map/ppermute | solution.py:493
  81.0 14.5 %collective-permute-start.21 = (bf16[480,768]{1,0:T(8,128)(2,1)S(1)}, bf16[480,768]{1,0:T(8,128)(2,1)S(1)}, u32[]{:S(2)}, u32[]{:S(2)}) collective-permute-start(bf16[480,768]{1,0:T(8,128)(2,1)S(1)} %collective-permute-done.15.refs_14_.refs_10_), channel_id=1, source_target_pairs={{0,1},{1,0},{2,3},{3,2},{4,5},{5,4},{6,7},{7,6},{8,9},{9,8},{10,11... | collective-permute-start | bytes 2211848 | tf_op jit(solution)/shard_map/ppermute | solution.py:493
  87.9 23.7 %collective-permute-start.28 = (bf16[768,384]{1,0:T(8,128)(2,1)}, bf16[768,384]{1,0:T(8,128)(2,1)}, u32[]{:S(2)}, u32[]{:S(2)}) collective-permute-start(bf16[768,384]{1,0:T(8,128)(2,1)} %collective-permute-done.2.refs_6_.refs_2_), channel_id=1, source_target_pairs={{0,4},{2,6},{4,0},{6,2},{1,5},{3,7},{5,1},{7,3},{8,12},{10,14},{12... | collective-permute-start | bytes 1769480 | tf_op jit(solution)/shard_map/ppermute | solution.py:503
  92.3 18.0 %collective-permute-start.30 = (bf16[480,768]{1,0:T(8,128)(2,1)}, bf16[480,768]{1,0:T(8,128)(2,1)}, u32[]{:S(2)}, u32[]{:S(2)}) collective-permute-start(bf16[480,768]{1,0:T(8,128)(2,1)} %collective-permute-done.16.refs_16_.refs_12_), channel_id=1, source_target_pairs={{0,2},{2,0},{4,6},{6,4},{1,3},{3,1},{5,7},{7,5},{8,10},{10,8},{12,... | collective-permute-start | bytes 2211848 | tf_op jit(solution)/shard_map/ppermute | solution.py:503
  94.0 11.9 %collective-permute-start.24 = (bf16[192,1024]{1,0:T(8,128)(2,1)S(1)}, bf16[192,1024]{1,0:T(8,128)(2,1)}, u32[]{:S(2)}, u32[]{:S(2)}) collective-permute-start(bf16[192,1024]{1,0:T(8,128)(2,1)S(1)} %add_convert_fusion.5), channel_id=1, source_target_pairs={{0,8},{8,0},{16,24},{24,16},{1,9},{9,1},{17,25},{25,17},{2,10},{10... | collective-permute-start | bytes 1179656 | tf_op jit(solution)/shard_map/ppermute | solution.py:496
  99.8 11.8 %collective-permute-start.23 = (bf16[192,1024]{1,0:T(8,128)(2,1)S(1)}, bf16[192,1024]{1,0:T(8,128)(2,1)}, u32[]{:S(2)}, u32[]{:S(2)}) collective-permute-start(bf16[192,1024]{1,0:T(8,128)(2,1)S(1)} %query_estimates.6), channel_id=1, source_target_pairs={{0,1},{1,0},{2,3},{3,2},{4,5},{5,4},{6,7},{7,6},{8,9},{9,8},{10,11... | collective-permute-start | bytes 1179656 | tf_op jit(solution)/shard_map/ppermute | solution.py:493
  153.6 15.3 %collective-permute-start.38 = (bf16[128,768]{1,0:T(8,128)(2,1)}, bf16[128,768]{1,0:T(8,128)(2,1)}, u32[]{:S(2)}, u32[]{:S(2)}) collective-permute-start(bf16[128,768]{1,0:T(8,128)(2,1)} %get-tuple-element.294), channel_id=1, source_target_pairs={{0,16},{8,24},{16,0},{24,8},{1,17},{9,25},{17,1},{25,9},{2,18},{10... | collective-permute-start | bytes 589832 | tf_op jit(solution)/shard_map/ppermute | solution.py:500
  155.3 13.5 %collective-permute-start.40 = (bf16[192,1024]{1,0:T(8,128)(2,1)S(1)}, bf16[192,1024]{1,0:T(8,128)(2,1)S(1)}, u32[]{:S(2)}, u32[]{:S(2)}) collective-permute-start(bf16[192,1024]{1,0:T(8,128)(2,1)S(1)} %slice_dynamic-update-slice_fusion.refs_4_), channel_id=1, source_target_pairs={{0,1},{1,0},{2,3},{3,2},{4,5},{5,4},{6,7},{7,6},{8,9},{9,8},{10,11... | collective-permute-start | bytes 1179656 | tf_op jit(solution)/shard_map/ppermute | solution.py:493
  157.4 34.7 %collective-permute-start.39 = (bf16[192,1024]{1,0:T(8,128)(2,1)S(1)}, bf16[192,1024]{1,0:T(8,128)(2,1)S(1)}, u32[]{:S(2)}, u32[]{:S(2)}) collective-permute-start(bf16[192,1024]{1,0:T(8,128)(2,1)S(1)} %slice_dynamic-update-slice_fusion.refs_4_), channel_id=1, source_target_pairs={{0,8},{8,0},{16,24},{24,16},{1,9},{9,1},{17,25},{25,17},{2,10},{10... | collective-permute-start | bytes 1179656 | tf_op jit(solution)/shard_map/ppermute | solution.py:496
  168.8 157.3 %all-reduce.3.cloned.1.call-start = ((), (), s32[]{:S(2)}) async-start(), calls=%async_computation.1 | async-start | bytes 2752512 | tf_op jit(solution)/shard_map/psum | solution.py:697
  192.1 15.2 %collective-permute-start.42 = (bf16[192,1024]{1,0:T(8,128)(2,1)S(1)}, bf16[192,1024]{1,0:T(8,128)(2,1)S(1)}, u32[]{:S(2)}, u32[]{:S(2)}) collective-permute-start(bf16[192,1024]{1,0:T(8,128)(2,1)S(1)} %collective-permute-done.39.refs_2_), channel_id=1, source_target_pairs={{0,1},{1,0},{2,3},{3,2},{4,5},{5,4},{6,7},{7,6},{8,9},{9,8},{10,11... | collective-permute-start | bytes 1179656 | tf_op jit(solution)/shard_map/ppermute | solution.py:493
  192.7 14.6 %collective-permute-start.41 = (bf16[192,1024]{1,0:T(8,128)(2,1)S(1)}, bf16[192,1024]{1,0:T(8,128)(2,1)S(1)}, u32[]{:S(2)}, u32[]{:S(2)}) collective-permute-start(bf16[192,1024]{1,0:T(8,128)(2,1)S(1)} %get-tuple-element.176), channel_id=1, source_target_pairs={{0,1},{1,0},{2,3},{3,2},{4,5},{5,4},{6,7},{7,6},{8,9},{9,8},{10,11... | collective-permute-start | bytes 1179656 | tf_op jit(solution)/shard_map/ppermute | solution.py:493
  204.6 34.8 %collective-permute-start.48 = (bf16[2,128,768]{2,1,0:T(8,128)(2,1)S(1)}, bf16[2,128,768]{2,1,0:T(8,128)(2,1)S(1)}, u32[]{:S(2)}, u32[]{:S(2)}) collective-permute-start(bf16[2,128,768]{2,1,0:T(8,128)(2,1)S(1)} %pad_maximum_fusion.11), channel_id=1, source_target_pairs={{0,4},{2,6},{4,0},{6,2},{1,5},{3,7},{5,1},{7,3},{8,12},{10,14},{12... | collective-permute-start | bytes 1179656 | tf_op jit(solution)/shard_map/ppermute | solution.py:503
  205.9 35.2 %collective-permute-start.47 = (bf16[2,128,768]{2,1,0:T(8,128)(2,1)S(1)}, bf16[2,128,768]{2,1,0:T(8,128)(2,1)S(1)}, u32[]{:S(2)}, u32[]{:S(2)}) collective-permute-start(bf16[2,128,768]{2,1,0:T(8,128)(2,1)S(1)} %pad_maximum_fusion.11), channel_id=1, source_target_pairs={{0,2},{2,0},{4,6},{6,4},{1,3},{3,1},{5,7},{7,5},{8,10},{10,8},{12,... | collective-permute-start | bytes 1179656 | tf_op jit(solution)/shard_map/ppermute | solution.py:503
  206.4 35.8 %collective-permute-start.49 = (bf16[2,128,768]{2,1,0:T(8,128)(2,1)S(1)}, bf16[2,128,768]{2,1,0:T(8,128)(2,1)S(1)}, u32[]{:S(2)}, u32[]{:S(2)}) collective-permute-start(bf16[2,128,768]{2,1,0:T(8,128)(2,1)S(1)} %pad_maximum_fusion.11), channel_id=1, source_target_pairs={{0,6},{2,4},{4,2},{6,0},{1,7},{3,5},{5,3},{7,1},{8,14},{10,12},{12... | collective-permute-start | bytes 1179656 | tf_op jit(solution)/shard_map/ppermute | solution.py:503
  228.8 13.5 %collective-permute-start.45 = (bf16[2,192,1024]{2,1,0:T(8,128)(2,1)S(1)}, bf16[2,192,1024]{2,1,0:T(8,128)(2,1)S(1)}, u32[]{:S(2)}, u32[]{:S(2)}) collective-permute-start(bf16[2,192,1024]{2,1,0:T(8,128)(2,1)S(1)} %key_backward.4), channel_id=1, source_target_pairs={{0,1},{1,0},{2,3},{3,2},{4,5},{5,4},{6,7},{7,6},{8,9},{9,8},{10,11... | collective-permute-start | bytes 2359304 | tf_op jit(solution)/shard_map/ppermute | solution.py:493
  229.0 15.4 %collective-permute-start.44 = (bf16[192,1024]{1,0:T(8,128)(2,1)S(1)}, bf16[192,1024]{1,0:T(8,128)(2,1)S(1)}, u32[]{:S(2)}, u32[]{:S(2)}) collective-permute-start(bf16[192,1024]{1,0:T(8,128)(2,1)S(1)} %add_convert_fusion.3), channel_id=1, source_target_pairs={{0,8},{8,0},{16,24},{24,16},{1,9},{9,1},{17,25},{25,17},{2,10},{10... | collective-permute-start | bytes 1179656 | tf_op jit(solution)/shard_map/ppermute | solution.py:496
  239.5 18.1 %collective-permute-start.52 = (bf16[3,96,768]{2,1,0:T(8,128)(2,1)}, bf16[3,96,768]{2,1,0:T(8,128)(2,1)}, u32[]{:S(2)}, u32[]{:S(2)}) collective-permute-start(bf16[3,96,768]{2,1,0:T(8,128)(2,1)} %get-tuple-element.195.refs_4_), channel_id=1, source_target_pairs={{0,6},{2,4},{4,2},{6,0},{1,7},{3,5},{5,3},{7,1},{8,14},{10,12},{12... | collective-permute-start | bytes 1327112 | tf_op jit(solution)/shard_map/ppermute | solution.py:503
  241.1 21.2 %collective-permute-start.51 = (bf16[3,96,768]{2,1,0:T(8,128)(2,1)}, bf16[3,96,768]{2,1,0:T(8,128)(2,1)}, u32[]{:S(2)}, u32[]{:S(2)}) collective-permute-start(bf16[3,96,768]{2,1,0:T(8,128)(2,1)} %get-tuple-element.195.refs_4_), channel_id=1, source_target_pairs={{0,4},{2,6},{4,0},{6,2},{1,5},{3,7},{5,1},{7,3},{8,12},{10,14},{12... | collective-permute-start | bytes 1327112 | tf_op jit(solution)/shard_map/ppermute | solution.py:503
  242.2 20.1 %collective-permute-start.50 = (bf16[3,96,768]{2,1,0:T(8,128)(2,1)}, bf16[3,96,768]{2,1,0:T(8,128)(2,1)}, u32[]{:S(2)}, u32[]{:S(2)}) collective-permute-start(bf16[3,96,768]{2,1,0:T(8,128)(2,1)} %get-tuple-element.195.refs_4_), channel_id=1, source_target_pairs={{0,2},{2,0},{4,6},{6,4},{1,3},{3,1},{5,7},{7,5},{8,10},{10,8},{12,... | collective-permute-start | bytes 1327112 | tf_op jit(solution)/shard_map/ppermute | solution.py:503
  243.5 18.8 %collective-permute-start.46 = (bf16[192,1024]{1,0:T(8,128)(2,1)}, bf16[192,1024]{1,0:T(8,128)(2,1)}, u32[]{:S(2)}, u32[]{:S(2)}) collective-permute-start(bf16[192,1024]{1,0:T(8,128)(2,1)} %get-tuple-element.287), channel_id=1, source_target_pairs={{0,8},{8,0},{16,24},{24,16},{1,9},{9,1},{17,25},{25,17},{2,10},{10... | collective-permute-start | bytes 1179656 | tf_op jit(solution)/shard_map/ppermute | solution.py:496
  255.8 29.7 %collective-permute-start.53 = (bf16[2,192,1024]{2,1,0:T(8,128)(2,1)S(1)}, bf16[2,192,1024]{2,1,0:T(8,128)(2,1)S(1)}, u32[]{:S(2)}, u32[]{:S(2)}) collective-permute-start(bf16[2,192,1024]{2,1,0:T(8,128)(2,1)S(1)} %key_backward.6), channel_id=1, source_target_pairs={{0,1},{1,0},{2,3},{3,2},{4,5},{5,4},{6,7},{7,6},{8,9},{9,8},{10,11... | collective-permute-start | bytes 2359304 | tf_op jit(solution)/shard_map/ppermute | solution.py:493
  262.4 23.0 %collective-permute-start.60 = (bf16[3,96,768]{2,1,0:T(8,128)(2,1)}, bf16[3,96,768]{2,1,0:T(8,128)(2,1)S(1)}, u32[]{:S(2)}, u32[]{:S(2)}) collective-permute-start(bf16[3,96,768]{2,1,0:T(8,128)(2,1)} %collective-permute-done.52.refs_7_), channel_id=1, source_target_pairs={{0,1},{1,0},{2,3},{3,2},{4,5},{5,4},{6,7},{7,6},{8,9},{9,8},{10,11... | collective-permute-start | bytes 1327112 | tf_op jit(solution)/shard_map/ppermute | solution.py:493
  263.6 21.8 %collective-permute-start.59 = (bf16[3,96,768]{2,1,0:T(8,128)(2,1)}, bf16[3,96,768]{2,1,0:T(8,128)(2,1)S(1)}, u32[]{:S(2)}, u32[]{:S(2)}) collective-permute-start(bf16[3,96,768]{2,1,0:T(8,128)(2,1)} %collective-permute-done.51.refs_6_), channel_id=1, source_target_pairs={{0,1},{1,0},{2,3},{3,2},{4,5},{5,4},{6,7},{7,6},{8,9},{9,8},{10,11... | collective-permute-start | bytes 1327112 | tf_op jit(solution)/shard_map/ppermute | solution.py:493
  263.6 21.9 %collective-permute-start.58 = (bf16[3,96,768]{2,1,0:T(8,128)(2,1)}, bf16[3,96,768]{2,1,0:T(8,128)(2,1)S(1)}, u32[]{:S(2)}, u32[]{:S(2)}) collective-permute-start(bf16[3,96,768]{2,1,0:T(8,128)(2,1)} %collective-permute-done.50.refs_5_), channel_id=1, source_target_pairs={{0,1},{1,0},{2,3},{3,2},{4,5},{5,4},{6,7},{7,6},{8,9},{9,8},{10,11... | collective-permute-start | bytes 1327112 | tf_op jit(solution)/shard_map/ppermute | solution.py:493
  264.1 21.3 %collective-permute-start.54 = (bf16[192,1024]{1,0:T(8,128)(2,1)S(1)}, bf16[192,1024]{1,0:T(8,128)(2,1)S(1)}, u32[]{:S(2)}, u32[]{:S(2)}) collective-permute-start(bf16[192,1024]{1,0:T(8,128)(2,1)S(1)} %copy-done.42), channel_id=1, source_target_pairs={{0,8},{8,0},{16,24},{24,16},{1,9},{9,1},{17,25},{25,17},{2,10},{10... | collective-permute-start | bytes 1179656 | tf_op jit(solution)/shard_map/ppermute | solution.py:496
  289.3 14.7 %collective-permute-start.56 = (bf16[3,192,256]{2,1,0:T(8,128)(2,1)S(1)}, bf16[3,192,256]{2,1,0:T(8,128)(2,1)S(1)}, u32[]{:S(2)}, u32[]{:S(2)}) collective-permute-start(bf16[3,192,256]{2,1,0:T(8,128)(2,1)S(1)} %pad_maximum_fusion.15), channel_id=1, source_target_pairs={{0,4},{2,6},{4,0},{6,2},{1,5},{3,7},{5,1},{7,3},{8,12},{10,14},{12... | collective-permute-start | bytes 884744 | tf_op jit(solution)/shard_map/ppermute | solution.py:503
  290.6 13.4 %collective-permute-start.55 = (bf16[3,192,256]{2,1,0:T(8,128)(2,1)S(1)}, bf16[3,192,256]{2,1,0:T(8,128)(2,1)S(1)}, u32[]{:S(2)}, u32[]{:S(2)}) collective-permute-start(bf16[3,192,256]{2,1,0:T(8,128)(2,1)S(1)} %pad_maximum_fusion.14), channel_id=1, source_target_pairs={{0,2},{2,0},{4,6},{6,4},{1,3},{3,1},{5,7},{7,5},{8,10},{10,8},{12,... | collective-permute-start | bytes 884744 | tf_op jit(solution)/shard_map/ppermute | solution.py:503
  291.8 21.6 %collective-permute-start.62 = (bf16[288,768]{1,0:T(8,128)(2,1)S(1)}, bf16[288,768]{1,0:T(8,128)(2,1)S(1)}, u32[]{:S(2)}, u32[]{:S(2)}) collective-permute-start(bf16[288,768]{1,0:T(8,128)(2,1)S(1)} %constant_dynamic-slice_fusion.1), channel_id=1, source_target_pairs={{0,1},{1,0},{2,3},{3,2},{4,5},{5,4},{6,7},{7,6},{8,9},{9,8},{10,11... | collective-permute-start | bytes 1327112 | tf_op jit(solution)/shard_map/ppermute | solution.py:493
  311.0 15.0 %collective-permute-start.61 = (bf16[128,768]{1,0:T(8,128)(2,1)S(1)}, bf16[128,768]{1,0:T(8,128)(2,1)S(1)}, u32[]{:S(2)}, u32[]{:S(2)}) collective-permute-start(bf16[128,768]{1,0:T(8,128)(2,1)S(1)} %get-tuple-element.292), channel_id=1, source_target_pairs={{0,16},{8,24},{16,0},{24,8},{1,17},{9,25},{17,1},{25,9},{2,18},{10... | collective-permute-start | bytes 589832 | tf_op jit(solution)/shard_map/ppermute | solution.py:500
  313.6 13.1 %collective-permute-start.63 = (bf16[144,768]{1,0:T(8,128)(2,1)S(1)}, bf16[144,768]{1,0:T(8,128)(2,1)S(1)}, u32[]{:S(2)}, u32[]{:S(2)}) collective-permute-start(bf16[144,768]{1,0:T(8,128)(2,1)S(1)} %constant_dynamic-slice_fusion), channel_id=1, source_target_pairs={{0,8},{8,0},{16,24},{24,16},{1,9},{9,1},{17,25},{25,17},{2,10},{10... | collective-permute-start | bytes 663560 | tf_op jit(solution)/shard_map/ppermute | solution.py:496
  326.1 29.2 %collective-permute-start.70 = (bf16[896,768]{1,0:T(8,128)(2,1)}, bf16[896,768]{1,0:T(8,128)(2,1)S(1)}, u32[]{:S(2)}, u32[]{:S(2)}) collective-permute-start(bf16[896,768]{1,0:T(8,128)(2,1)} %all-reduce.3.cloned.1.call-done), channel_id=1, source_target_pairs={{0,1},{1,0},{2,3},{3,2},{4,5},{5,4},{6,7},{7,6},{8,9},{9,8},{10,11... | collective-permute-start | bytes 4128776 | tf_op jit(solution)/shard_map/ppermute | solution.py:493
  326.7 11.7 %collective-permute-start.67 = (bf16[144,768]{1,0:T(8,128)(2,1)S(1)}, bf16[144,768]{1,0:T(8,128)(2,1)S(1)}, u32[]{:S(2)}, u32[]{:S(2)}) collective-permute-start(bf16[144,768]{1,0:T(8,128)(2,1)S(1)} %fusion.12), channel_id=1, source_target_pairs={{0,16},{8,24},{16,0},{24,8},{1,17},{9,25},{17,1},{25,9},{2,18},{10... | collective-permute-start | bytes 663560 | tf_op jit(solution)/shard_map/ppermute | solution.py:500
  330.1 16.6 %collective-permute-start.66 = (bf16[2,128,768]{2,1,0:T(8,128)(2,1)S(1)}, bf16[2,128,768]{2,1,0:T(8,128)(2,1)S(1)}, u32[]{:S(2)}, u32[]{:S(2)}) collective-permute-start(bf16[2,128,768]{2,1,0:T(8,128)(2,1)S(1)} %pad_maximum_fusion.12), channel_id=1, source_target_pairs={{0,6},{2,4},{4,2},{6,0},{1,7},{3,5},{5,3},{7,1},{8,14},{10,12},{12... | collective-permute-start | bytes 1179656 | tf_op jit(solution)/shard_map/ppermute | solution.py:503
  (93 other events, 653.9 us)
Sparse Core Ops, SparseCore 0:
  168.9 72.8 reduce-scatter.3
  244.6 76.9 all-reduce.2

commit v10 on v9

--- a/solution.py
+++ b/solution.py
@@ -238,12 +238,12 @@
     )(*args)
 
 
-def key_backward(planes, planes_t, bits, heads, near, far, grad_tables, kind):
+def key_backward(planes, planes_t, bits, heads, near, far, grad_tables, kind, micros=25):
     width = near.shape[1] + far.shape[1]
     return call(
         partial(key_back_kernel, chunk=4),
         heads,
-        25,
+        micros,
         "key_backward",
         [whole(64, 64), whole(64, 128), whole(80, ROWS)]
         + [head_rows(x, heads, w) for w in (1, 2) for x in (near, far)]
@@ -285,14 +285,15 @@
 
 
 def dense_kernel(core, x_in, grad_out, gain, bias, *refs):
-    attn, ups, downs = refs[0:4], refs[4:12], refs[12:20]
-    layer_out, first_out, grad_second_out, slope, keep, give, heads_give, small = refs[20:28]
+    attn, weights = refs[0:4], refs[4:6]
+    layer_out, first_out, grad_second_out, slope, keep, give, heads_give, small = refs[6:14]
+    owner = [core[1] ^ (b // 2) for b in range(8)]
     for j in range(4):
         heads_give[j] = core_rows(core, attn[j], 1)
     part = slope.shape[2]
     blocks = range(8)
     heads = jnp.concatenate([core_rows(core, attn[b // 2], b % 2) for b in blocks], axis=0)
-    out_w = jnp.concatenate([downs[b][part:, :] for b in blocks], axis=0)
+    out_w = jnp.concatenate([weights[b % 2][owner[b], 2 * part :, :] for b in blocks], axis=0)
     attn_out = dot(heads, out_w, TN)
     resid = x_in[...].astype(f32)
     first = resid + attn_out
@@ -305,12 +306,12 @@
     share_rows(keep, give, 4, normed)
     second = normed.astype(f32)
     for b in blocks:
-        pre = dot(normed, ups[b][...], NN)
+        pre = dot(normed, weights[b % 2][owner[b], 0:part, :], NT)
         below = 0.5 * (1.0 + lax.erf(pre * 0.7071067811865476))
         rows = (pre * below).astype(bf16)
         (keep, give)[b % 2][b // 2] = rows
         slope[b] = below + pre * (0.3989422804014327 * jnp.exp(-0.5 * pre * pre))
-        second = second + dot(rows, downs[b][0:part, :], NN)
+        second = second + dot(rows, weights[b % 2][owner[b], part : 2 * part, :], NN)
     unit_2, inv_2 = norm(second)
     layer_out[...] = (unit_2 * gain[1:2, :] + bias[1:2, :]).astype(layer_out.dtype)
     grad = grad_out[...]
@@ -323,17 +324,19 @@
 
 
 def dense_back_kernel(core, first, grad_second, slope, gain, *refs):
-    ups, downs = refs[0:8], refs[8:16]
-    grad_first_out, keep, give = refs[16:19]
-    estimates, small = refs[19:23], refs[23]
+    weights = refs[0:2]
+    grad_first_out, keep, give = refs[2:5]
+    estimates, small = refs[5:9], refs[9]
+    owner = [core[1] ^ (b // 2) for b in range(8)]
     part = slope.shape[2]
     blocks = range(8)
     grad_normed = grad_second[...]
     grad_ffn = grad_normed.astype(bf16)
     for b in blocks:
-        rows = (dot(grad_ffn, downs[b][0:part, :], NT) * slope[b]).astype(bf16)
+        rows = dot(grad_ffn, weights[b % 2][owner[b], part : 2 * part, :], NT)
+        rows = (rows * slope[b]).astype(bf16)
         (keep, give)[b % 2][b // 2] = rows
-        grad_normed = grad_normed + dot(rows, ups[b][...], NT)
+        grad_normed = grad_normed + dot(rows, weights[b % 2][owner[b], 0:part, :], NN)
     unit, inv = norm(first[...])
     small[0:1, :] = column_sum(grad_normed * unit)
     small[1:2, :] = column_sum(grad_normed)
@@ -346,7 +349,7 @@
         half = estimates[0].shape[0] // 2
         at = core[0] if b % 2 == 0 else 1 - core[0]
         estimates[b // 2][pl.ds(pl.multiple_of(at * half, 16), half), :] = dot(
-            downs[b][part:, :], grad_attn, NT
+            weights[b % 2][owner[b], 2 * part :, :], grad_attn, NT
         ).astype(bf16)
 
 
@@ -378,15 +381,15 @@
 
 
 def input_grad_kernel(core, grad_first, *refs):
-    blocks, near, far, out = refs[0:4], refs[4:8], refs[8:12], refs[12]
-    half = near[0].shape[1]
+    blocks, near, far, out = refs[0:4], refs[4], refs[5], refs[6]
+    half = near.shape[2]
     total = grad_first[...]
     for which, halves in enumerate((near, far)):
         at = core[0] if which == 0 else 1 - core[0]
         at = pl.ds(pl.multiple_of(at * half, 16), half)
         for j in range(4):
             rows = jnp.concatenate([blocks[j][c, at, :] for c in range(3)], axis=0)
-            weights = jnp.concatenate([halves[j][c] for c in range(3)], axis=0)
+            weights = jnp.concatenate([halves[core[1] ^ j, c] for c in range(3)], axis=0)
             total = total + dot(rows, weights, TN)
     out[...] = total.astype(out.dtype)
 
@@ -410,9 +413,9 @@
     )(core, *args)
 
 
-def dense(core, x_in, grad_out, gain, bias, attn, ups, downs):
+def dense(core, x_in, grad_out, gain, bias, attn, weights):
     rows, width = x_in.shape
-    part = ups[0].shape[1]
+    part = (weights[0].shape[1] - attn[0].shape[0] // 2) // 2
     out_shape = [
         shape((rows, width), bf16),
         shape((rows, width), f32),
@@ -423,13 +426,13 @@
         shape((4, attn[0].shape[0] // 2, rows), bf16),
         shape((8, width), f32),
     ]
-    args = [x_in, grad_out, gain, bias, *attn, *ups, *downs]
+    args = [x_in, grad_out, gain, bias, *attn, *weights]
     return single(dense_kernel, core, args, out_shape, 14, "dense")
 
 
-def dense_back(core, first, grad_second, slope, gain, attn, ups, downs):
+def dense_back(core, first, grad_second, slope, gain, attn, weights):
     rows, width = first.shape
-    part = ups[0].shape[1]
+    part = (weights[0].shape[1] - attn[0].shape[0] // 2) // 2
     out_shape = [
         shape((rows, width), f32),
         shape((6, rows, part), bf16),
@@ -437,7 +440,7 @@
         *[shape(attn[0].shape, bf16)] * 4,
         shape((8, width), f32),
     ]
-    args = [first, grad_second, slope, gain, *ups, *downs]
+    args = [first, grad_second, slope, gain, *weights]
     return single(dense_back_kernel, core, args, out_shape, 8, "dense_back")
 
 
@@ -450,7 +453,7 @@
 
 def input_grad(core, grad_first, blocks, near, far):
     out_shape = [shape(grad_first.shape, bf16)]
-    args = [grad_first, *blocks, *near, *far]
+    args = [grad_first, *blocks, near, far]
     return single(input_grad_kernel, core, args, out_shape, 3, "input_grad")[0]
 
 
@@ -530,18 +533,16 @@
     signed_t = jnp.concatenate([signed.T, signed.T], axis=1)
     bits = bit_rows()
 
-    def down_half(at):
-        cut, out_cut = hidden_own // 2, head_width // 2
-        rows_down = lax.dynamic_slice_in_dim(down_weight, at * cut, cut, 0)
-        return jnp.concatenate([rows_down, lax.dynamic_slice_in_dim(w_out, at * out_cut, out_cut, 0)])
-
-    down, downs = down_half(s), [down_half(1 - s)]
-    up_weight = after(up_weight, *sent)
-    up, up_other = [
-        lax.dynamic_slice_in_dim(up_weight, at * (hidden_own // 2), hidden_own // 2, 1) for at in (s, 1 - s)
-    ]
-    ups = [up, up_other]
-    up_x, up_y = over_head(up, 1), over_head(up, 2)
+    cut, out_cut = hidden_own // 2, head_width // 2
+    weights = jnp.concatenate(
+        [
+            lax.dynamic_slice_in_dim(after(up_weight, *sent), s * cut, cut, 1).T,
+            lax.dynamic_slice_in_dim(down_weight, s * cut, cut, 0),
+            lax.dynamic_slice_in_dim(w_out, s * out_cut, out_cut, 0),
+        ]
+    )
+    weights = lax.all_gather(weights, "head", axis=0)
+    w_qkv_t = lax.dynamic_slice_in_dim(w_qkv.transpose(0, 2, 1), s * out_cut, out_cut, 1)
 
     head_n = head_width // HEAD_DIM
 
@@ -554,7 +555,7 @@
     near_z, near_o = over_place(near), over_seq(near)
     far_quarter = jnp.stack(arrived)
     moved = [over_head(far_quarter, j) for j in range(1, head_count)]
-    tables = key_tables(after(signed, up_x, up_y), head_n, [near, near_o], None, f32)
+    tables = key_tables(signed, head_n, [near, near_o], None, f32)
     moved = [after(x, tables) for x in moved]
 
     near_z = after(near_z, tables)
@@ -568,7 +569,7 @@
     cot = lax.dynamic_index_in_dim(cot_rows, g, 0, keepdims=False)
     pick = (position.reshape(rows)[:, None] == mask_row[None]).astype(bf16)
     grad_out = jnp.dot(pick, cot, preferred_element_type=f32)
-    ready = after(signed, grad_out, down, *ups, *downs)
+    ready = after(signed, grad_out)
     tables = key_tables(ready, head_n, [near_z, near_zo], tables, f32)
 
     far_tokens = jnp.stack([far_quarter, *moved]).reshape(-1, width)
@@ -580,45 +581,32 @@
     q_o, q_z = over_seq(q), over_place(q)
     n_near = near.shape[1]
 
-    downs = [down] + downs
-    down = after(down, kv)
-    down_x, down_y, up_d = over_head(down, 1), over_head(down, 2), over_head(after(up_x, kv), 2)
-    up_xo, up_yo = over_seq(after(up_x, kv)), over_seq(after(up_y, kv))
-    qkv_cut = head_width // 2
-    w_qkv_t = w_qkv.transpose(0, 2, 1)
-    qkv_near = [lax.dynamic_slice_in_dim(w_qkv_t, s * qkv_cut, qkv_cut, 1)]
-    qkv_far = [lax.dynamic_slice_in_dim(w_qkv_t, (1 - s) * qkv_cut, qkv_cut, 1)]
     tables = key_tables(after(signed, q), head_n, [kv, kv_o], tables, f32)
 
     kv_z = after(kv_z, tables)
     kv_zo = over_seq(kv_z)
-    up_xo, up_yo = after(up_xo, tables), after(up_yo, tables)
-    ready = after(signed, up_xo, up_yo, tokens, dense_in, qkv_near[0], qkv_far[0])
+    ready = after(signed, tokens, dense_in)
     tables = key_tables(ready, head_n, [kv_z], tables, f32)
 
     q_z = after(q_z, tables)
     q_zo = over_seq(q_z)
     kv_zo = after(kv_zo, tables)
-    down_x, down_y = after(down_x, tables), after(down_y, tables)
-    down_d = over_head(down_y, 1)
-    down_xo, down_yo = over_seq(down_x), over_seq(down_y)
-    tables = key_tables(after(signed, q_z, down_x, down_y), head_n, [kv_zo], tables, bf16)
+    tables = key_tables(after(signed, q_z), head_n, [kv_zo], tables, bf16)
 
     q_zo = after(q_zo, tables)
     e_zo = query_estimates(signed, head_n, near_zo, q_zo, tables, bf16)
     e_zo_moved = over_seq(e_zo)
     e_z = query_estimates(signed, head_n, near_z, after(q_z, e_zo), tables, bf16)
     e_far = add(e_z, after(e_zo_moved, e_z)).astype(bf16)
-    down_xo, down_yo = after(down_xo, e_z), after(down_yo, e_z)
-    ready = after(q_o, e_far, down_xo, down_yo)
+    ready = after(q_o, e_far)
     e_o = query_estimates(signed, head_n, near_o, ready, tables, bf16)
     e_far = over_place(e_far)
     e_o_moved = over_seq(e_o)
     e = query_estimates(signed, head_n, near, after(q, e_o), tables, f32)
     e_far = after(e_far, e)
-    up_d, down_d = after(up_d, e_far), after(down_d, e_far)
-    ups += [up_x, up_xo, up_y, up_yo, up_d, over_seq(up_d)]
-    downs += [down_x, down_xo, down_y, down_yo, down_d, over_seq(down_d)]
+    weights = after(weights, e_o)
+    weights = [weights, over_seq(weights)]
+    w_qkv_t = lax.all_gather(after(w_qkv_t, weights[0]), "head", axis=0)
     attn = add(e, after(e_o_moved, e), e_far).astype(bf16)
 
     def to_dense(block):
@@ -638,11 +626,11 @@
 
     core = jnp.stack([s, d]).astype(jnp.int32)
     layer_rows, first, grad_second, slope, keep, give, heads_give, small_a = dense(
-        core, dense_in, grad_out, norm_gain, norm_bias, attn_parts, ups, downs
+        core, dense_in, grad_out, norm_gain, norm_bias, attn_parts, weights
     )
     taken, heads_far = over_seq(give), over_seq(heads_give)
     grad_first, keep_back, give_back, *est_parts, small_b = dense_back(
-        core, first, grad_second, slope, norm_gain, attn_parts, ups, downs
+        core, first, grad_second, slope, norm_gain, attn_parts, weights
     )
     taken_back = over_seq(give_back)
     est_moved = [over_head(est_parts[j], j) for j in range(1, head_count)]
@@ -652,7 +640,7 @@
     )
     layer_moved = away(layer_rows)
     weight_parts = weight_grads(
-        core, after(small_a, grad), small_b, [keep, taken, keep_back, taken_back], attn_parts, heads_far
+        core, after(small_a, grad, w_qkv_t), small_b, [keep, taken, keep_back, taken_back], attn_parts, heads_far
     )
 
     weight_sum = lax.psum_scatter(weight_parts, "head", scatter_dimension=0, tiled=True)[0]
@@ -678,6 +666,8 @@
     )
 
     dq_zo = over_seq(dq_zo)
+    w_qkv_t = after(w_qkv_t, grad_tables)
+    w_qkv_far = over_seq(w_qkv_t)
     dkv_zo = key_backward(signed, signed_t, bits, head_n, near_zo, kv_zo, grad_tables, bf16)
 
     dkv_zo_moved = over_seq(dkv_zo)
@@ -692,29 +682,21 @@
     layer_moved = [after(x, dkv_z) for x in layer_moved]
     dkv_o = key_backward(
         signed, signed_t, bits, head_n, near_o, after(kv_o, dkv_far, grad_q, weight_sum, *layer_moved),
-        grad_tables, bf16,
+        grad_tables, bf16, 2,
     )
     weight_sum = lax.psum(weight_sum, "hash")
-    dk_far, dv_far = over_place(dkv_far[0]), over_place(after(dkv_far[1], dkv_o))
-    qkv_half = after(qkv_near[0], dkv_z)
-    qkv_moved = [over_head(qkv_half, j) for j in range(1, head_count)]
-
+    dkv_far = over_place(dkv_far)
     dkv_o_moved = over_seq(dkv_o)
-    dk_far = after(dk_far, dkv_o)
-    qkv_near += [after(x, dkv_o) for x in qkv_moved]
     dkv = key_backward(
-        signed, signed_t, bits, head_n, near, after(kv, dk_far, *qkv_near[1:]), grad_tables, f32
-    )
-    qkv_far += [over_seq(x) for x in qkv_near[1:]]
+        signed, signed_t, bits, head_n, near, kv, grad_tables, f32, 2
+    )
 
     dkv_o_moved = after(dkv_o_moved, dkv)
-    qkv_far[1:] = [after(x, dkv) for x in qkv_far[1:]]
-    grad_k = add(dkv[0], dkv_o_moved[0], dk_far)
-    grad_v = add(dkv[1], dkv_o_moved[1], after(dv_far, dkv))
-    grad_qkv = jnp.stack([grad_q, grad_k.astype(bf16), grad_v.astype(bf16)])
+    grad_kv = add(dkv, dkv_o_moved, after(dkv_far, dkv)).astype(bf16)
+    grad_qkv = jnp.concatenate([grad_q[None], grad_kv])
     qkv_parts = to_dense(grad_qkv)
 
-    grad_in = input_grad(core, grad_first, qkv_parts, qkv_near, qkv_far)
+    grad_in = input_grad(core, grad_first, qkv_parts, w_qkv_t, after(w_qkv_far, dkv))
 
     def in_halves(index, mine, other):
         first = jnp.where(index == 0, mine, other)
@@ -759,7 +741,6 @@
     grad_w_qkv = w_grad.transpose(0, 2, 1).astype(f32)
     weight_sum = after(weight_sum, grad_in)
     weight_far = over_seq(weight_sum)
-    cut = hidden_own // 2
     ends = [0, cut, 2 * cut, 2 * cut + head_width // 2]
     grad_w_up, grad_w_down, grad_w_out = [
         in_halves(s, weight_sum[a:b], weight_far[a:b]) for a, b in zip(ends, ends[1:])

time: 377 us -> 378 us (level)
  starting transfers between devices: 65.9 us -> 53 us
  waiting for transfers between devices: 57.8 us -> 69.4 us
    psum x1, waiting for transfers between devices: 0.02 us -> 24.1 us  [shards(): weight_sum = lax.psum(weight_sum, 'hash')]
    ppermute x27 -> x18, starting transfers between devices: 25.9 us -> 16.3 us  [over_head(): return lax.ppermute(x, 'head', [(h, h ^ j) for h in range(head_count)])]
    ppermute x27 -> x18, waiting for transfers between devices: 31.8 us -> 23.1 us  [over_head(): return lax.ppermute(x, 'head', [(h, h ^ j) for h in range(head_count)])]
    ppermute x10 -> x9, waiting for transfers between devices: 10.9 us -> 3.11 us  [over_place(): return lax.ppermute(x, 'hash', [(h, h ^ 1) for h in range(hash_count)])]
    all_gather x0 -> x2, waiting for transfers between devices: none -> 4.94 us  [the longest x1 4.94 us: shards(): weights = lax.all_gather(weights, 'head', axis=0)]
    ppermute x29 -> x22, starting transfers between devices: 20.9 us -> 17.8 us  [over_seq(): return lax.ppermute(x, 'seq', [(0, 1), (1, 0)])]
    unnamed x149 -> x117, local copies, waits for them, and re-layouts: 25.9 us -> 23.3 us
    ppermute x10 -> x9, starting transfers between devices: 8.85 us -> 7 us  [over_place(): return lax.ppermute(x, 'hash', [(h, h ^ 1) for h in range(hash_count)])]
  transfers between devices with their start and end apart: 73 -> 58, of which waited for: 11 -> 14; matrix products, arithmetic and copies ran while one was open for 12% -> 13% of each run, Pallas kernels for 36% -> 43%
where the time goes in v10:
time: 378 us; the launch traced here: 373 us
  Pallas kernels  159 us (42%)
  waiting for transfers between devices  69.4 us (18%)
  starting transfers between devices  53 us (14%)
  local copies, waits for them, and re-layouts  43 us (11%)
  other arithmetic  28.4 us (8%)
  between operations  15.5 us (4%)
  matrix products  4.15 us (1%)
    pallas_call x3, Pallas kernels, query_backward(): call(partial(query_back_kernel, chunk=4, blocks=blocks, last=last), heads...  43.4 us
    pallas_call x4, Pallas kernels, single(): pl.pallas_call(kernel, in_specs=[pl.BlockSpec(memory_space=pltpu.SMEM)] +...  38.8 us
    pallas_call x4, Pallas kernels, key_backward(): call(partial(key_back_kernel, chunk=4), heads, micros, 'key_backward', [w...  38.1 us
    psum x1, waiting for transfers between devices, shards(): weight_sum = lax.psum(weight_sum, 'hash')  24.1 us
    pallas_call x5, Pallas kernels, key_tables(): call(partial(key_kernel, chunk=2, blocks=len(blocks)), heads, 30 if len(b...  23.5 us
    unnamed x117, local copies, waits for them, and re-layouts  23.3 us
    ppermute x18, waiting for transfers between devices, over_head(): return lax.ppermute(x, 'head', [(h, h ^ j) for h in range(head_count)])  23.1 us
    ppermute x22, starting transfers between devices, over_seq(): return lax.ppermute(x, 'seq', [(0, 1), (1, 0)])  17.8 us
  transfers between devices with their start and end apart: 58, of which 14 were waited for; matrix products, arithmetic and copies ran while one was open for 13% of the time, Pallas kernels for 43%

profile of v10, /device:TPU:1, one launch (start us, length us, event | category | flops | bytes accessed | tf_op | source)
XLA Modules:
  0.0 372.8 jit_solution(6473508281048259536)
XLA Ops:
  7.3 4.5 %constant_dynamic-slice_fusion.7 = (bf16[1,128,1,768]{3,2,1,0:T(2,128)(2,1)S(1)}, bf16[1,128,1,768]{3,2,1,0:T(2,128)(2,1)}, bf16[1,128,1,768]{3,2,1,0:T(2,128)(2...) fusion(bf16[1,512,2,768]{3,2,1,0:T(2,128)(2,1)} %param.11, s32[]{:T(128)S(6)} %select_n.254, ...), kind=kLoop, calls=%fused_computation.130 | loop fusion | bytes 1966104 | tf_op jit(solution)/shard_map/jit(dynamic_index_in_dim)/dynamic_slice | solution.py:509
  12.6 3.1 collective-permute-start
  16.3 2.5 collective-permute-start.1
  20.5 2.4 copy.56
  22.9 1.8 copy_bitcast_fusion
  24.7 1.9 dynamic-slice_bitcast_fusion
  37.1 1.9 slice.136
  39.0 1.7 slice.135
  40.7 5.3 %key_tables.5.refs_4_ = f32[3,2048,64]{2,1,0:T(8,128)S(1)} custom-call(bf16[64,64]{1,0:T(8,128)(2,1)S(1)} %bitcast.131, bf16[576,512]{1,0:T(8,128)(2,1)} %bitcast.14.refs_0_.refs_2_.ka.va, bf16[576,512]{1,0:T(8,128)(2,1)} %collective-permute-done.2.refs_1_.refs_3_.refs_0_.refs_2_.ka.va, bf16[576,512]{1,0:T(8,128)(2,1)} %bitcast.14.refs_0_.refs_2_.ka.va, ...), custom_call_target="tpu_custom_call" | custom-call | flops 1100000000 | bytes 1048576 | tf_op jit(solution)/shard_map/key_tables/pallas_call | solution.py:192
  46.0 2.1 pad_maximum_fusion.7
  49.1 1.9 collective-permute-start.8
  53.4 5.8 %key_tables.6.refs_4_ = f32[3,2048,64]{2,1,0:T(8,128)S(1)} custom-call(bf16[64,64]{1,0:T(8,128)(2,1)S(1)} %bitcast.132, bf16[576,512]{1,0:T(8,128)(2,1)} %collective-permute-done.9.refs_0_.refs_2_.ka.va, bf16[576,512]{1,0:T(8,128)(2,1)S(1)} %collective-permute-done.10.refs_1_.refs_3_.refs_0_.ka.va, ...), custom_call_target="tpu_custom_call" | custom-call | flops 32999999488 | bytes 1048576 | tf_op jit(solution)/shard_map/key_tables/pallas_call | solution.py:192
  60.9 5.6 %key_tables.7.refs_2_ = f32[3,2048,64]{2,1,0:T(8,128)S(1)} custom-call(bf16[64,64]{1,0:T(8,128)(2,1)S(1)} %bitcast.133, bf16[384,512]{1,0:T(8,128)(2,1)S(1)} %bitcast.127, bf16[384,512]{1,0:T(8,128)(2,1)S(1)} %collective-permute-done.8.refs_1_.refs_3_.kb.vb, bf16[384,512]{1,0:T(8,128)(2,1)S(1)} %bitcast.128, ...), custom_call_target="tpu_custom_call" | custom-call | flops 32999999488 | bytes 1048576 | tf_op jit(solution)/shard_map/key_tables/pallas_call | solution.py:192
  71.5 4.2 %key_tables.8.refs_2_ = f32[3,2048,64]{2,1,0:T(8,128)S(1)} custom-call(bf16[64,64]{1,0:T(8,128)(2,1)S(1)} %bitcast.134, bf16[384,512]{1,0:T(8,128)(2,1)S(1)} %collective-permute-done.7.refs_0_.refs_1_.kb.vb, bf16[384,512]{1,0:T(8,128)(2,1)S(1)} %collective-permute-done.7.refs_0_.refs_1_.kb.vb, f32[3,2048,64]{2,1,0:T(8,128)} %copy-done.2), custom_call_target="tpu_custom_call" | custom-call | flops 1100000000 | bytes 1048576 | tf_op jit(solution)/shard_map/key_tables/pallas_call | solution.py:192
  76.4 2.6 key_tables.9.tables
  79.0 3.3 query_estimates.4
  82.9 4.1 %query_estimates.5 = bf16[192,1024]{1,0:T(8,128)(2,1)S(1)} custom-call(bf16[64,64]{1,0:T(8,128)(2,1)S(1)} %bitcast.137, bf16[3,2048,64]{2,1,0:T(8,128)(2,1)S(1)} %key_tables.9.tables, bf16[576,512]{1,0:T(8,128)(2,1)} %collective-permute-done.9.refs_0_.refs_2_.ka.va, bf16[192,512]{1,0:T(8,128)(2,1)S(1)} %collective-permute-done.6.refs_1_), custom_call_target="tpu_custom_call" | custom-call | flops 1100000000 | bytes 1048576 | tf_op jit(solution)/shard_map/query_estimates/pallas_call | solution.py:205
  87.2 4.2 %query_estimates.6 = bf16[192,1024]{1,0:T(8,128)(2,1)S(1)} custom-call(bf16[64,64]{1,0:T(8,128)(2,1)S(1)} %bitcast.138, bf16[3,2048,64]{2,1,0:T(8,128)(2,1)S(1)} %key_tables.9.tables, bf16[576,512]{1,0:T(8,128)(2,1)} %collective-permute-done.2.refs_1_.refs_3_.refs_0_.refs_2_.ka.va, bf16[192,512]{1,0:T(8,128)(2,1)S(1)} %collective-permute-done.12.refs_1_.refs_3_), custom_call_target="tpu_custom_call" | custom-call | flops 1100000000 | bytes 1048576 | tf_op jit(solution)/shard_map/query_estimates/pallas_call | solution.py:205
  91.4 4.9 %all-gather.5.cloned.1.call-done = bf16[3456,768]{1,0:T(8,128)(2,1)} async-done(((bf16[864,768]{1,0:T(8,128)(2,1)}), bf16[3456,768]{1,0:T(8,128)(2,1)}) %all-gather.5.cloned.1.call-update) | async-done | bytes 5308432 | tf_op jit(solution)/shard_map/all_gather | solution.py:544
  98.8 1.8 dynamic-slice_bitcast_fusion.1
  100.8 4.2 %query_estimates.7 = f32[192,1024]{1,0:T(8,128)S(1)} custom-call(bf16[64,64]{1,0:T(8,128)(2,1)S(1)} %bitcast.140, bf16[3,2048,64]{2,1,0:T(8,128)(2,1)S(1)} %key_tables.9.tables, bf16[576,512]{1,0:T(8,128)(2,1)} %bitcast.14.refs_0_.refs_2_.ka.va, bf16[192,512]{1,0:T(8,128)(2,1)S(1)} %convolution_convert_fusion.1.refs_1_), custom_call_target="tpu_custom_call" | custom-call | flops 1100000000 | bytes 1048576 | tf_op jit(solution)/shard_map/query_estimates/pallas_call | solution.py:205
  105.0 2.3 collective-permute-done.16
  116.4 12.7 %dense.1 = (bf16[256,768]{1,0:T(8,128)(2,1)}, f32[256,768]{1,0:T(8,128)}, f32[256,768]{1,0:T(8,128)}, f32[8,256,384]{2,1,0:T(8,128)}, bf16[8,256,384]{2,1,0:T(8,...) custom-call(s32[2]{0:T(128)} %pad_add_fusion.core, ...), custom_call_target="tpu_custom_call" | custom-call | flops 15399999488 | bytes 1048576 | tf_op jit(solution)/shard_map/dense/pallas_call | solution.py:402
  129.1 12.6 %dense_back.1 = (f32[256,768]{1,0:T(8,128)}, bf16[6,256,384]{2,1,0:T(8,128)(2,1)}, bf16[6,256,384]{2,1,0:T(8,128)(2,1)}, bf16[192,256]{1,0:T(8,128)(2,1)}, bf16[...) custom-call(s32[2]{0:T(128)} %pad_add_fusion.core, ...), custom_call_target="tpu_custom_call" | custom-call | flops 8800000000 | bytes 1048576 | tf_op jit(solution)/shard_map/dense_back/pallas_call | solution.py:402
  144.4 2.8 collective-permute-start.25
  148.7 2.9 collective-permute-start.26
  151.6 2.1 collective-permute-start.27
  157.3 8.2 %weight_grads.1 = bf16[4,896,768]{2,1,0:T(8,128)(2,1)} custom-call(s32[2]{0:T(128)} %pad_add_fusion.core, f32[8,768]{1,0:T(8,128)} %get-tuple-element.133.small_a, f32[8,768]{1,0:T(8,128)} %get-tuple-element.134.small_b, bf16[8,256,384]{2,1,0:T(8,128)(2,1)} %get-tuple-element.135.refs_0_, bf16[8,256,384]{2,1,0:T(8,128)(2,1)} %collective-permute-done.24.refs_1_, ...), custom_call_target="tpu_custom_call" | custom-call | flops 7699999744 | bytes 1048576 | tf_op jit(solution)/shard_map/weight_grads/pallas_call | solution.py:402
  167.9 20.3 %query_backward.3 = (f32[3,2048,64]{2,1,0:T(8,128)}, f32[192,1024]{1,0:T(8,128)S(1)}, bf16[192,1024]{1,0:T(8,128)(2,1)S(1)}) custom-call(bf16[64,64]{1,0:T(8,128)(2,1)S(1)} %bitcast.141, bf16[64,128]{1,0:T(8,128)(2,1)S(1)} %pad_maximum_fusion.20.planes_t, bf16[80,2048]{1,0:T(8,128)(2,1)S(1)} %copy-done.16, bf16[3,2048,64]{2,1,0:T(8,128)(2,1)S(1)} %key_tables.9.tables, ...), custom_call_target="tpu_custom_call" | custom-call | flops 54999998464 | bytes 1048576 | tf_op jit(solution)/shard_map/query_backward/pallas_call | solution.py:229
  188.7 11.8 %query_backward.4 = (f32[3,2048,64]{2,1,0:T(8,128)}, f32[192,1024]{1,0:T(8,128)S(1)}) custom-call(bf16[64,64]{1,0:T(8,128)(2,1)S(1)} %bitcast.142, bf16[64,128]{1,0:T(8,128)(2,1)S(1)} %pad_maximum_fusion.20.planes_t, bf16[80,2048]{1,0:T(8,128)(2,1)S(1)} %copy-done.16, bf16[3,2048,64]{2,1,0:T(8,128)(2,1)S(1)} %key_tables.9.tables, ...), custom_call_target="tpu_custom_call" | custom-call | flops 27499999232 | bytes 1048576 | tf_op jit(solution)/shard_map/query_backward/pallas_call | solution.py:229
  203.3 11.2 %query_backward.5 = (bf16[3,2048,64]{2,1,0:T(8,128)(2,1)S(1)}, bf16[192,1024]{1,0:T(8,128)(2,1)S(1)}) custom-call(bf16[64,64]{1,0:T(8,128)(2,1)S(1)} %bitcast.143, bf16[64,128]{1,0:T(8,128)(2,1)S(1)} %pad_maximum_fusion.20.planes_t, bf16[80,2048]{1,0:T(8,128)(2,1)S(1)} %copy-done.17, bf16[3,2048,64]{2,1,0:T(8,128)(2,1)S(1)} %key_tables.9.tables, ...), custom_call_target="tpu_custom_call" | custom-call | flops 27499999232 | bytes 1048576 | tf_op jit(solution)/shard_map/query_backward/pallas_call | solution.py:229
  216.0 8.7 %key_backward.4 = bf16[2,192,1024]{2,1,0:T(8,128)(2,1)S(1)} custom-call(bf16[64,64]{1,0:T(8,128)(2,1)S(1)} %bitcast.144, bf16[64,128]{1,0:T(8,128)(2,1)S(1)} %pad_maximum_fusion.20.planes_t, bf16[80,2048]{1,0:T(8,128)(2,1)S(1)} %copy-done.17, bf16[576,512]{1,0:T(8,128)(2,1)S(1)} %copy-done.11, bf16[384,512]{1,0:T(8,128)(2,1)S(1)} %copy-done.7, ...), custom_call_target="tpu_custom_call" | custom-call | flops 27499999232 | bytes 1048576 | tf_op jit(solution)/shard_map/key_backward/pallas_call | solution.py:243
  226.2 9.7 %key_backward.5 = bf16[2,192,1024]{2,1,0:T(8,128)(2,1)S(1)} custom-call(bf16[64,64]{1,0:T(8,128)(2,1)S(1)} %bitcast.145, bf16[64,128]{1,0:T(8,128)(2,1)S(1)} %pad_maximum_fusion.20.planes_t, bf16[80,2048]{1,0:T(8,128)(2,1)S(1)} %copy-done.17, bf16[576,512]{1,0:T(8,128)(2,1)} %collective-permute-done.9.refs_0_.refs_2_.ka.va, bf16[384,512]{1,0:T(8,128)(2,1)S(1)} %copy-done.5, ...), custom_call_target="tpu_custom_call" | custom-call | flops 27499999232 | bytes 1048576 | tf_op jit(solution)/shard_map/key_backward/pallas_call | solution.py:243
  240.8 9.7 %key_backward.7 = bf16[2,192,1024]{2,1,0:T(8,128)(2,1)S(1)} custom-call(bf16[64,64]{1,0:T(8,128)(2,1)S(1)} %bitcast.146, bf16[64,128]{1,0:T(8,128)(2,1)S(1)} %pad_maximum_fusion.20.planes_t, bf16[80,2048]{1,0:T(8,128)(2,1)S(1)} %copy-done.17, bf16[576,512]{1,0:T(8,128)(2,1)} %collective-permute-done.2.refs_1_.refs_3_.refs_0_.refs_2_.ka.va, ...), custom_call_target="tpu_custom_call" | custom-call | flops 2200000000 | bytes 1048576 | tf_op jit(solution)/shard_map/key_backward/pallas_call | solution.py:243
  252.7 10.0 %key_backward.6 = f32[2,192,1024]{2,1,0:T(8,128)S(1)} custom-call(bf16[64,64]{1,0:T(8,128)(2,1)S(1)} %bitcast.147, bf16[64,128]{1,0:T(8,128)(2,1)S(1)} %pad_maximum_fusion.20.planes_t, bf16[80,2048]{1,0:T(8,128)(2,1)S(1)} %copy-done.17, bf16[576,512]{1,0:T(8,128)(2,1)} %bitcast.14.refs_0_.refs_2_.ka.va, bf16[384,512]{1,0:T(8,128)(2,1)S(1)} %bitcast.129, ...), custom_call_target="tpu_custom_call" | custom-call | flops 2200000000 | bytes 1048576 | tf_op jit(solution)/shard_map/key_backward/pallas_call | solution.py:243
  262.7 1.8 add_convert_fusion
  270.7 4.0 %collective-permute-done.42.refs_3_ = bf16[3,192,256]{2,1,0:T(8,128)(2,1)S(1)} collective-permute-done((bf16[3,192,256]{2,1,0:T(8,128)(2,1)S(1)}, bf16[3,192,256]{2,1,0:T(8,128)(2,1)S(1)}, u32[]{:S(2)}, u32[]{:S(2)}) %collective-permute-start.42) | collective-permute-done | bytes 294944 | tf_op jit(solution)/shard_map/ppermute | solution.py:506
  274.6 6.6 %collective-permute-done.41.refs_2_ = bf16[3,192,256]{2,1,0:T(8,128)(2,1)S(1)} collective-permute-done((bf16[3,192,256]{2,1,0:T(8,128)(2,1)S(1)}, bf16[3,192,256]{2,1,0:T(8,128)(2,1)S(1)}, u32[]{:S(2)}, u32[]{:S(2)}) %collective-permute-start.41) | collective-permute-done | bytes 294944 | tf_op jit(solution)/shard_map/ppermute | solution.py:506
  282.1 5.3 %input_grad.1 = bf16[256,768]{1,0:T(8,128)(2,1)} custom-call(s32[2]{0:T(128)} %pad_add_fusion.core, f32[256,768]{1,0:T(8,128)} %get-tuple-element.158.grad_first, bf16[3,192,256]{2,1,0:T(8,128)(2,1)} %pad_maximum_fusion.12.refs_0_, bf16[3,192,256]{2,1,0:T(8,128)(2,1)} %copy-done.47, bf16[3,192,256]{2,1,0:T(8,128)(2,1)} %copy-done.46, ...), custom_call_target="tpu_custom_call" | custom-call | flops 3300000000 | bytes 1048576 | tf_op jit(solution)/shard_map/input_grad/pallas_call | solution.py:402
  291.2 9.0 %collective-permute-done.44 = bf16[128,768]{1,0:T(8,128)(2,1)S(1)} collective-permute-done((bf16[128,768]{1,0:T(8,128)(2,1)S(1)}, bf16[128,768]{1,0:T(8,128)(2,1)S(1)}, u32[]{:S(2)}, u32[]{:S(2)}) %collective-permute-start.44) | collective-permute-done | bytes 196640 | tf_op jit(solution)/shard_map/ppermute | solution.py:503
  300.3 24.1 %all-reduce.3.cloned.1.call-done = bf16[896,768]{1,0:T(8,128)(2,1)} async-done(((bf16[896,768]{1,0:T(8,128)(2,1)}), bf16[896,768]{1,0:T(8,128)(2,1)}) %all-reduce.3.cloned.1.call-update) | async-done | bytes 1376272 | tf_op jit(solution)/shard_map/psum | solution.py:687
  325.3 1.9 collective-permute-start.50
  330.7 2.8 copy.58
  333.5 4.6 %collective-permute-done.50 = bf16[144,768]{1,0:T(8,128)(2,1)S(1)} collective-permute-done((bf16[144,768]{1,0:T(8,128)(2,1)S(1)}, bf16[144,768]{1,0:T(8,128)(2,1)S(1)}, u32[]{:S(2)}, u32[]{:S(2)}) %collective-permute-start.50) | collective-permute-done | bytes 221216 | tf_op jit(solution)/shard_map/ppermute | solution.py:503
  338.5 8.5 %collective-permute-done.49 = bf16[2,128,768]{2,1,0:T(8,128)(2,1)S(1)} collective-permute-done((bf16[2,128,768]{2,1,0:T(8,128)(2,1)S(1)}, bf16[2,128,768]{2,1,0:T(8,128)(2,1)S(1)}, u32[]{:S(2)}, u32[]{:S(2)}) %collective-permute-start.49) | collective-permute-done | bytes 393248 | tf_op jit(solution)/shard_map/ppermute | solution.py:506
  349.3 4.1 %copy.59 = f32[1,512,2,768]{3,2,1,0:T(2,128)} copy(f32[1,512,2,768]{3,1,2,0:T(8,128)S(1)} %maximum_convert_fusion) | data formatting | bytes 6291456
  357.7 2.0 copy.60
  360.9 3.0 maximum_convert_fusion.1
  (290 shorter events, 85.0 us)
Async XLA Ops:
  7.2 89.1 %all-gather.5.cloned.1.call-start = ((), (), s32[]{:S(2)}) async-start(), calls=%async_computation.2 | async-start | bytes 6635520 | tf_op jit(solution)/shard_map/all_gather | solution.py:544
  12.6 16.4 %collective-permute-start = (bf16[128,768]{1,0:T(8,128)(2,1)}, bf16[128,768]{1,0:T(8,128)(2,1)}, u32[]{:S(2)}, u32[]{:S(2)}) collective-permute-start(bf16[128,768]{1,0:T(8,128)(2,1)} %bitcast.123), channel_id=1, source_target_pairs={{0,16},{8,24},{16,0},{24,8},{1,17},{9,25},{17,1},{25,9},{2,18},{10... | collective-permute-start | bytes 589832 | tf_op jit(solution)/shard_map/ppermute | solution.py:503
  16.3 19.9 %collective-permute-start.1 = (bf16[8,8,64]{2,0,1:T(8,128)(2,1)}, bf16[8,8,64]{2,0,1:T(8,128)(2,1)S(1)}, u32[]{:S(2)}, u32[]{:S(2)}) collective-permute-start(bf16[8,8,64]{2,0,1:T(8,128)(2,1)} %fusion.17), channel_id=1, source_target_pairs={{0,0},{8,1},{16,8},{24,9},{1,16},{9,17},{17,24},{25,25},{2,2},{10,... | collective-permute-start | bytes 24584 | tf_op jit(solution)/shard_map/ppermute | solution.py:528
  30.5 10.2 %collective-permute-start.2 = (bf16[576,512]{1,0:T(8,128)(2,1)}, bf16[576,512]{1,0:T(8,128)(2,1)}, u32[]{:S(2)}, u32[]{:S(2)}) collective-permute-start(bf16[576,512]{1,0:T(8,128)(2,1)} %bitcast.14.refs_0_.refs_2_.ka.va), channel_id=1, source_target_pairs={{0,1},{1,0},{2,3},{3,2},{4,5},{5,4},{6,7},{7,6},{8,9},{9,8},{10,11... | collective-permute-start | bytes 1769480 | tf_op jit(solution)/shard_map/ppermute | solution.py:496
  32.2 123.9 %all-gather.7.cloned.1.call-start = ((), (), s32[]{:S(2)}) async-start(), calls=%async_computation.3 | async-start | bytes 2211840 | tf_op jit(solution)/shard_map/all_gather | solution.py:609
  32.4 18.5 %collective-permute-start.9 = (bf16[576,512]{1,0:T(8,128)(2,1)}, bf16[576,512]{1,0:T(8,128)(2,1)}, u32[]{:S(2)}, u32[]{:S(2)}) collective-permute-start(bf16[576,512]{1,0:T(8,128)(2,1)} %bitcast.14.refs_0_.refs_2_.ka.va), channel_id=1, source_target_pairs={{0,8},{8,0},{16,24},{24,16},{1,9},{9,1},{17,25},{25,17},{2,10},{10... | collective-permute-start | bytes 1769480 | tf_op jit(solution)/shard_map/ppermute | solution.py:499
  33.8 12.2 %collective-permute-start.3 = (bf16[1,128,768]{2,1,0:T(8,128)(2,1)}, bf16[1,128,768]{2,1,0:T(8,128)(2,1)S(1)}, u32[]{:S(2)}, u32[]{:S(2)}) collective-permute-start(bf16[1,128,768]{2,1,0:T(8,128)(2,1)} %bitcast.20), channel_id=1, source_target_pairs={{0,2},{2,0},{4,6},{6,4},{1,3},{3,1},{5,7},{7,5},{8,10},{10,8},{12,... | collective-permute-start | bytes 589832 | tf_op jit(solution)/shard_map/ppermute | solution.py:506
  35.0 11.0 %collective-permute-start.4 = (bf16[1,128,768]{2,1,0:T(8,128)(2,1)}, bf16[1,128,768]{2,1,0:T(8,128)(2,1)}, u32[]{:S(2)}, u32[]{:S(2)}) collective-permute-start(bf16[1,128,768]{2,1,0:T(8,128)(2,1)} %bitcast.20), channel_id=1, source_target_pairs={{0,4},{2,6},{4,0},{6,2},{1,5},{3,7},{5,1},{7,3},{8,12},{10,14},{12... | collective-permute-start | bytes 589832 | tf_op jit(solution)/shard_map/ppermute | solution.py:506
  36.2 9.8 %collective-permute-start.5 = (bf16[1,128,768]{2,1,0:T(8,128)(2,1)}, bf16[1,128,768]{2,1,0:T(8,128)(2,1)}, u32[]{:S(2)}, u32[]{:S(2)}) collective-permute-start(bf16[1,128,768]{2,1,0:T(8,128)(2,1)} %bitcast.20), channel_id=1, source_target_pairs={{0,6},{2,4},{4,2},{6,0},{1,7},{3,5},{5,3},{7,1},{8,14},{10,12},{12... | collective-permute-start | bytes 589832 | tf_op jit(solution)/shard_map/ppermute | solution.py:506
  49.1 11.8 %collective-permute-start.8 = (bf16[384,512]{1,0:T(8,128)(2,1)S(1)}, bf16[384,512]{1,0:T(8,128)(2,1)S(1)}, u32[]{:S(2)}, u32[]{:S(2)}) collective-permute-start(bf16[384,512]{1,0:T(8,128)(2,1)S(1)} %bitcast.125), channel_id=1, source_target_pairs={{0,1},{1,0},{2,3},{3,2},{4,5},{5,4},{6,7},{7,6},{8,9},{9,8},{10,11... | collective-permute-start | bytes 1179656 | tf_op jit(solution)/shard_map/ppermute | solution.py:496
  51.0 17.2 %collective-permute-start.7 = (bf16[384,512]{1,0:T(8,128)(2,1)S(1)}, bf16[384,512]{1,0:T(8,128)(2,1)S(1)}, u32[]{:S(2)}, u32[]{:S(2)}) collective-permute-start(bf16[384,512]{1,0:T(8,128)(2,1)S(1)} %bitcast.126), channel_id=1, source_target_pairs={{0,8},{8,0},{16,24},{24,16},{1,9},{9,1},{17,25},{25,17},{2,10},{10... | collective-permute-start | bytes 1179656 | tf_op jit(solution)/shard_map/ppermute | solution.py:499
  68.2 8.2 %collective-permute-start.11 = (bf16[384,512]{1,0:T(8,128)(2,1)S(1)}, bf16[384,512]{1,0:T(8,128)(2,1)S(1)}, u32[]{:S(2)}, u32[]{:S(2)}) collective-permute-start(bf16[384,512]{1,0:T(8,128)(2,1)S(1)} %collective-permute-done.7.refs_0_.refs_1_.kb.vb), channel_id=1, source_target_pairs={{0,1},{1,0},{2,3},{3,2},{4,5},{5,4},{6,7},{7,6},{8,9},{9,8},{10,11... | collective-permute-start | bytes 1179656 | tf_op jit(solution)/shard_map/ppermute | solution.py:496
  96.3 19.9 %collective-permute-start.20 = (bf16[4,864,768]{2,1,0:T(8,128)(2,1)}, bf16[4,864,768]{2,1,0:T(8,128)(2,1)}, u32[]{:S(2)}, u32[]{:S(2)}) collective-permute-start(bf16[4,864,768]{2,1,0:T(8,128)(2,1)} %bitcast.176), channel_id=1, source_target_pairs={{0,1},{1,0},{2,3},{3,2},{4,5},{5,4},{6,7},{7,6},{8,9},{9,8},{10,11... | collective-permute-start | bytes 15925256 | tf_op jit(solution)/shard_map/ppermute | solution.py:496
  97.0 8.0 %collective-permute-start.15 = (bf16[192,1024]{1,0:T(8,128)(2,1)S(1)}, bf16[192,1024]{1,0:T(8,128)(2,1)S(1)}, u32[]{:S(2)}, u32[]{:S(2)}) collective-permute-start(bf16[192,1024]{1,0:T(8,128)(2,1)S(1)} %query_estimates.6), channel_id=1, source_target_pairs={{0,1},{1,0},{2,3},{3,2},{4,5},{5,4},{6,7},{7,6},{8,9},{9,8},{10,11... | collective-permute-start | bytes 1179656 | tf_op jit(solution)/shard_map/ppermute | solution.py:496
  97.0 10.3 %collective-permute-start.16 = (bf16[192,1024]{1,0:T(8,128)(2,1)S(1)}, bf16[192,1024]{1,0:T(8,128)(2,1)}, u32[]{:S(2)}, u32[]{:S(2)}) collective-permute-start(bf16[192,1024]{1,0:T(8,128)(2,1)S(1)} %add_convert_fusion.6), channel_id=1, source_target_pairs={{0,8},{8,0},{16,24},{24,16},{1,9},{9,1},{17,25},{25,17},{2,10},{10... | collective-permute-start | bytes 1179656 | tf_op jit(solution)/shard_map/ppermute | solution.py:499
  115.8 123.6 %reduce-scatter.4.cloned.1.call-start = ((), (), s32[]{:S(2)}) async-start(), calls=%async_computation.4 | async-start | bytes 6881280
  142.0 9.6 %collective-permute-start.22 = (bf16[192,256]{1,0:T(8,128)(2,1)}, bf16[192,256]{1,0:T(8,128)(2,1)S(1)}, u32[]{:S(2)}, u32[]{:S(2)}) collective-permute-start(bf16[192,256]{1,0:T(8,128)(2,1)} %get-tuple-element.127), channel_id=1, source_target_pairs={{0,4},{2,6},{4,0},{6,2},{1,5},{3,7},{5,1},{7,3},{8,12},{10,14},{12... | collective-permute-start | bytes 294920 | tf_op jit(solution)/shard_map/ppermute | solution.py:506
  143.2 10.5 %collective-permute-start.23 = (bf16[192,256]{1,0:T(8,128)(2,1)}, bf16[192,256]{1,0:T(8,128)(2,1)S(1)}, u32[]{:S(2)}, u32[]{:S(2)}) collective-permute-start(bf16[192,256]{1,0:T(8,128)(2,1)} %get-tuple-element.128), channel_id=1, source_target_pairs={{0,6},{2,4},{4,2},{6,0},{1,7},{3,5},{5,3},{7,1},{8,14},{10,12},{12... | collective-permute-start | bytes 294920 | tf_op jit(solution)/shard_map/ppermute | solution.py:506
  144.4 12.9 %collective-permute-start.25 = (bf16[6,256,384]{2,1,0:T(8,128)(2,1)}, bf16[6,256,384]{2,1,0:T(8,128)(2,1)}, u32[]{:S(2)}, u32[]{:S(2)}) collective-permute-start(bf16[6,256,384]{2,1,0:T(8,128)(2,1)} %get-tuple-element.138), channel_id=1, source_target_pairs={{0,1},{1,0},{2,3},{3,2},{4,5},{5,4},{6,7},{7,6},{8,9},{9,8},{10,11... | collective-permute-start | bytes 3538952 | tf_op jit(solution)/shard_map/ppermute | solution.py:496
  147.1 10.2 %collective-permute-start.24 = (bf16[8,256,384]{2,1,0:T(8,128)(2,1)}, bf16[8,256,384]{2,1,0:T(8,128)(2,1)}, u32[]{:S(2)}, u32[]{:S(2)}) collective-permute-start(bf16[8,256,384]{2,1,0:T(8,128)(2,1)} %get-tuple-element.136), channel_id=1, source_target_pairs={{0,1},{1,0},{2,3},{3,2},{4,5},{5,4},{6,7},{7,6},{8,9},{9,8},{10,11... | collective-permute-start | bytes 4718600 | tf_op jit(solution)/shard_map/ppermute | solution.py:496
  148.7 7.4 %collective-permute-start.26 = (bf16[4,96,256]{2,1,0:T(8,128)(2,1)}, bf16[4,96,256]{2,1,0:T(8,128)(2,1)}, u32[]{:S(2)}, u32[]{:S(2)}) collective-permute-start(bf16[4,96,256]{2,1,0:T(8,128)(2,1)} %get-tuple-element.139), channel_id=1, source_target_pairs={{0,1},{1,0},{2,3},{3,2},{4,5},{5,4},{6,7},{7,6},{8,9},{9,8},{10,11... | collective-permute-start | bytes 589832 | tf_op jit(solution)/shard_map/ppermute | solution.py:496
  151.6 14.2 %collective-permute-start.27 = (bf16[128,768]{1,0:T(8,128)(2,1)}, bf16[128,768]{1,0:T(8,128)(2,1)}, u32[]{:S(2)}, u32[]{:S(2)}) collective-permute-start(bf16[128,768]{1,0:T(8,128)(2,1)} %get-tuple-element.248), channel_id=1, source_target_pairs={{0,16},{8,24},{16,0},{24,8},{1,17},{9,25},{17,1},{25,9},{2,18},{10... | collective-permute-start | bytes 589832 | tf_op jit(solution)/shard_map/ppermute | solution.py:503
  154.7 11.1 %collective-permute-start.29 = (bf16[192,1024]{1,0:T(8,128)(2,1)S(1)}, bf16[192,1024]{1,0:T(8,128)(2,1)S(1)}, u32[]{:S(2)}, u32[]{:S(2)}) collective-permute-start(bf16[192,1024]{1,0:T(8,128)(2,1)S(1)} %slice_dynamic-update-slice_fusion.refs_4_), channel_id=1, source_target_pairs={{0,1},{1,0},{2,3},{3,2},{4,5},{5,4},{6,7},{7,6},{8,9},{9,8},{10,11... | collective-permute-start | bytes 1179656 | tf_op jit(solution)/shard_map/ppermute | solution.py:496
  156.1 32.1 %collective-permute-start.28 = (bf16[192,1024]{1,0:T(8,128)(2,1)S(1)}, bf16[192,1024]{1,0:T(8,128)(2,1)S(1)}, u32[]{:S(2)}, u32[]{:S(2)}) collective-permute-start(bf16[192,1024]{1,0:T(8,128)(2,1)S(1)} %slice_dynamic-update-slice_fusion.refs_4_), channel_id=1, source_target_pairs={{0,8},{8,0},{16,24},{24,16},{1,9},{9,1},{17,25},{25,17},{2,10},{10... | collective-permute-start | bytes 1179656 | tf_op jit(solution)/shard_map/ppermute | solution.py:499
  165.7 158.6 %all-reduce.3.cloned.1.call-start = ((), (), s32[]{:S(2)}) async-start(), calls=%async_computation.1 | async-start | bytes 2752512 | tf_op jit(solution)/shard_map/psum | solution.py:687
  188.1 15.0 %collective-permute-start.31 = (bf16[192,1024]{1,0:T(8,128)(2,1)S(1)}, bf16[192,1024]{1,0:T(8,128)(2,1)S(1)}, u32[]{:S(2)}, u32[]{:S(2)}) collective-permute-start(bf16[192,1024]{1,0:T(8,128)(2,1)S(1)} %collective-permute-done.28.refs_2_), channel_id=1, source_target_pairs={{0,1},{1,0},{2,3},{3,2},{4,5},{5,4},{6,7},{7,6},{8,9},{9,8},{10,11... | collective-permute-start | bytes 1179656 | tf_op jit(solution)/shard_map/ppermute | solution.py:496
  188.5 14.7 %collective-permute-start.30 = (bf16[192,1024]{1,0:T(8,128)(2,1)S(1)}, bf16[192,1024]{1,0:T(8,128)(2,1)S(1)}, u32[]{:S(2)}, u32[]{:S(2)}) collective-permute-start(bf16[192,1024]{1,0:T(8,128)(2,1)S(1)} %get-tuple-element.148), channel_id=1, source_target_pairs={{0,1},{1,0},{2,3},{3,2},{4,5},{5,4},{6,7},{7,6},{8,9},{9,8},{10,11... | collective-permute-start | bytes 1179656 | tf_op jit(solution)/shard_map/ppermute | solution.py:496
  200.5 24.8 %collective-permute-start.36 = (bf16[2,128,768]{2,1,0:T(8,128)(2,1)S(1)}, bf16[2,128,768]{2,1,0:T(8,128)(2,1)S(1)}, u32[]{:S(2)}, u32[]{:S(2)}) collective-permute-start(bf16[2,128,768]{2,1,0:T(8,128)(2,1)S(1)} %pad_maximum_fusion.10), channel_id=1, source_target_pairs={{0,4},{2,6},{4,0},{6,2},{1,5},{3,7},{5,1},{7,3},{8,12},{10,14},{12... | collective-permute-start | bytes 1179656 | tf_op jit(solution)/shard_map/ppermute | solution.py:506
  201.4 34.5 %collective-permute-start.35 = (bf16[2,128,768]{2,1,0:T(8,128)(2,1)S(1)}, bf16[2,128,768]{2,1,0:T(8,128)(2,1)S(1)}, u32[]{:S(2)}, u32[]{:S(2)}) collective-permute-start(bf16[2,128,768]{2,1,0:T(8,128)(2,1)S(1)} %pad_maximum_fusion.10), channel_id=1, source_target_pairs={{0,2},{2,0},{4,6},{6,4},{1,3},{3,1},{5,7},{7,5},{8,10},{10,8},{12,... | collective-permute-start | bytes 1179656 | tf_op jit(solution)/shard_map/ppermute | solution.py:506
  202.0 34.0 %collective-permute-start.37 = (bf16[2,128,768]{2,1,0:T(8,128)(2,1)S(1)}, bf16[2,128,768]{2,1,0:T(8,128)(2,1)S(1)}, u32[]{:S(2)}, u32[]{:S(2)}) collective-permute-start(bf16[2,128,768]{2,1,0:T(8,128)(2,1)S(1)} %pad_maximum_fusion.10), channel_id=1, source_target_pairs={{0,6},{2,4},{4,2},{6,0},{1,7},{3,5},{5,3},{7,1},{8,14},{10,12},{12... | collective-permute-start | bytes 1179656 | tf_op jit(solution)/shard_map/ppermute | solution.py:506
  214.5 48.1 %collective-permute-start.43 = (bf16[4,3,96,768]{3,2,1,0:T(8,128)(2,1)}, bf16[4,3,96,768]{3,2,1,0:T(8,128)(2,1)}, u32[]{:S(2)}, u32[]{:S(2)}) collective-permute-start(bf16[4,3,96,768]{3,2,1,0:T(8,128)(2,1)} %bitcast.35.refs_4_), channel_id=1, source_target_pairs={{0,1},{1,0},{2,3},{3,2},{4,5},{5,4},{6,7},{7,6},{8,9},{9,8},{10,11... | collective-permute-start | bytes 5308424 | tf_op jit(solution)/shard_map/ppermute | solution.py:496
  215.9 8.8 %collective-permute-start.32 = (bf16[192,1024]{1,0:T(8,128)(2,1)S(1)}, bf16[192,1024]{1,0:T(8,128)(2,1)S(1)}, u32[]{:S(2)}, u32[]{:S(2)}) collective-permute-start(bf16[192,1024]{1,0:T(8,128)(2,1)S(1)} %get-tuple-element.153), channel_id=1, source_target_pairs={{0,1},{1,0},{2,3},{3,2},{4,5},{5,4},{6,7},{7,6},{8,9},{9,8},{10,11... | collective-permute-start | bytes 1179656 | tf_op jit(solution)/shard_map/ppermute | solution.py:496
  224.8 12.0 %collective-permute-start.34 = (bf16[2,192,1024]{2,1,0:T(8,128)(2,1)S(1)}, bf16[2,192,1024]{2,1,0:T(8,128)(2,1)S(1)}, u32[]{:S(2)}, u32[]{:S(2)}) collective-permute-start(bf16[2,192,1024]{2,1,0:T(8,128)(2,1)S(1)} %key_backward.4), channel_id=1, source_target_pairs={{0,1},{1,0},{2,3},{3,2},{4,5},{5,4},{6,7},{7,6},{8,9},{9,8},{10,11... | collective-permute-start | bytes 2359304 | tf_op jit(solution)/shard_map/ppermute | solution.py:496
  226.1 10.7 %collective-permute-start.33 = (bf16[192,1024]{1,0:T(8,128)(2,1)S(1)}, bf16[192,1024]{1,0:T(8,128)(2,1)S(1)}, u32[]{:S(2)}, u32[]{:S(2)}) collective-permute-start(bf16[192,1024]{1,0:T(8,128)(2,1)S(1)} %add_convert_fusion.4), channel_id=1, source_target_pairs={{0,8},{8,0},{16,24},{24,16},{1,9},{9,1},{17,25},{25,17},{2,10},{10... | collective-permute-start | bytes 1179656 | tf_op jit(solution)/shard_map/ppermute | solution.py:499
  238.0 24.7 %collective-permute-start.39 = (bf16[2,192,1024]{2,1,0:T(8,128)(2,1)}, bf16[2,192,1024]{2,1,0:T(8,128)(2,1)}, u32[]{:S(2)}, u32[]{:S(2)}) collective-permute-start(bf16[2,192,1024]{2,1,0:T(8,128)(2,1)} %add_convert_fusion.1), channel_id=1, source_target_pairs={{0,8},{8,0},{16,24},{24,16},{1,9},{9,1},{17,25},{25,17},{2,10},{10... | collective-permute-start | bytes 2359304 | tf_op jit(solution)/shard_map/ppermute | solution.py:499
  250.5 12.2 %collective-permute-start.38 = (bf16[2,192,1024]{2,1,0:T(8,128)(2,1)S(1)}, bf16[2,192,1024]{2,1,0:T(8,128)(2,1)}, u32[]{:S(2)}, u32[]{:S(2)}) collective-permute-start(bf16[2,192,1024]{2,1,0:T(8,128)(2,1)S(1)} %key_backward.7), channel_id=1, source_target_pairs={{0,1},{1,0},{2,3},{3,2},{4,5},{5,4},{6,7},{7,6},{8,9},{9,8},{10,11... | collective-permute-start | bytes 2359304 | tf_op jit(solution)/shard_map/ppermute | solution.py:496
  264.9 9.7 %collective-permute-start.42 = (bf16[3,192,256]{2,1,0:T(8,128)(2,1)S(1)}, bf16[3,192,256]{2,1,0:T(8,128)(2,1)S(1)}, u32[]{:S(2)}, u32[]{:S(2)}) collective-permute-start(bf16[3,192,256]{2,1,0:T(8,128)(2,1)S(1)} %pad_maximum_fusion.15), channel_id=1, source_target_pairs={{0,6},{2,4},{4,2},{6,0},{1,7},{3,5},{5,3},{7,1},{8,14},{10,12},{12... | collective-permute-start | bytes 884744 | tf_op jit(solution)/shard_map/ppermute | solution.py:506
  266.2 15.1 %collective-permute-start.41 = (bf16[3,192,256]{2,1,0:T(8,128)(2,1)S(1)}, bf16[3,192,256]{2,1,0:T(8,128)(2,1)S(1)}, u32[]{:S(2)}, u32[]{:S(2)}) collective-permute-start(bf16[3,192,256]{2,1,0:T(8,128)(2,1)S(1)} %pad_maximum_fusion.14), channel_id=1, source_target_pairs={{0,4},{2,6},{4,0},{6,2},{1,5},{3,7},{5,1},{7,3},{8,12},{10,14},{12... | collective-permute-start | bytes 884744 | tf_op jit(solution)/shard_map/ppermute | solution.py:506
  267.4 13.9 %collective-permute-start.40 = (bf16[3,192,256]{2,1,0:T(8,128)(2,1)S(1)}, bf16[3,192,256]{2,1,0:T(8,128)(2,1)S(1)}, u32[]{:S(2)}, u32[]{:S(2)}) collective-permute-start(bf16[3,192,256]{2,1,0:T(8,128)(2,1)S(1)} %pad_maximum_fusion.13), channel_id=1, source_target_pairs={{0,2},{2,0},{4,6},{6,4},{1,3},{3,1},{5,7},{7,5},{8,10},{10,8},{12,... | collective-permute-start | bytes 884744 | tf_op jit(solution)/shard_map/ppermute | solution.py:506
  269.0 20.9 %collective-permute-start.45 = (bf16[288,768]{1,0:T(8,128)(2,1)S(1)}, bf16[288,768]{1,0:T(8,128)(2,1)S(1)}, u32[]{:S(2)}, u32[]{:S(2)}) collective-permute-start(bf16[288,768]{1,0:T(8,128)(2,1)S(1)} %constant_dynamic-slice_fusion.1), channel_id=1, source_target_pairs={{0,1},{1,0},{2,3},{3,2},{4,5},{5,4},{6,7},{7,6},{8,9},{9,8},{10,11... | collective-permute-start | bytes 1327112 | tf_op jit(solution)/shard_map/ppermute | solution.py:496
  288.4 11.8 %collective-permute-start.44 = (bf16[128,768]{1,0:T(8,128)(2,1)S(1)}, bf16[128,768]{1,0:T(8,128)(2,1)S(1)}, u32[]{:S(2)}, u32[]{:S(2)}) collective-permute-start(bf16[128,768]{1,0:T(8,128)(2,1)S(1)} %get-tuple-element.246), channel_id=1, source_target_pairs={{0,16},{8,24},{16,0},{24,8},{1,17},{9,25},{17,1},{25,9},{2,18},{10... | collective-permute-start | bytes 589832 | tf_op jit(solution)/shard_map/ppermute | solution.py:503
  290.0 35.2 %collective-permute-start.46 = (bf16[144,768]{1,0:T(8,128)(2,1)S(1)}, bf16[144,768]{1,0:T(8,128)(2,1)S(1)}, u32[]{:S(2)}, u32[]{:S(2)}) collective-permute-start(bf16[144,768]{1,0:T(8,128)(2,1)S(1)} %constant_dynamic-slice_fusion), channel_id=1, source_target_pairs={{0,8},{8,0},{16,24},{24,16},{1,9},{9,1},{17,25},{25,17},{2,10},{10... | collective-permute-start | bytes 663560 | tf_op jit(solution)/shard_map/ppermute | solution.py:499
  324.4 30.6 %collective-permute-start.53 = (bf16[896,768]{1,0:T(8,128)(2,1)}, bf16[896,768]{1,0:T(8,128)(2,1)S(1)}, u32[]{:S(2)}, u32[]{:S(2)}) collective-permute-start(bf16[896,768]{1,0:T(8,128)(2,1)} %all-reduce.3.cloned.1.call-done), channel_id=1, source_target_pairs={{0,1},{1,0},{2,3},{3,2},{4,5},{5,4},{6,7},{7,6},{8,9},{9,8},{10,11... | collective-permute-start | bytes 4128776 | tf_op jit(solution)/shard_map/ppermute | solution.py:496
  325.3 12.8 %collective-permute-start.50 = (bf16[144,768]{1,0:T(8,128)(2,1)S(1)}, bf16[144,768]{1,0:T(8,128)(2,1)S(1)}, u32[]{:S(2)}, u32[]{:S(2)}) collective-permute-start(bf16[144,768]{1,0:T(8,128)(2,1)S(1)} %fusion.6), channel_id=1, source_target_pairs={{0,16},{8,24},{16,0},{24,8},{1,17},{9,25},{17,1},{25,9},{2,18},{10... | collective-permute-start | bytes 663560 | tf_op jit(solution)/shard_map/ppermute | solution.py:503
  327.2 11.0 %collective-permute-start.47 = (bf16[2,128,768]{2,1,0:T(8,128)(2,1)S(1)}, bf16[2,128,768]{2,1,0:T(8,128)(2,1)S(1)}, u32[]{:S(2)}, u32[]{:S(2)}) collective-permute-start(bf16[2,128,768]{2,1,0:T(8,128)(2,1)S(1)} %pad_maximum_fusion.11), channel_id=1, source_target_pairs={{0,2},{2,0},{4,6},{6,4},{1,3},{3,1},{5,7},{7,5},{8,10},{10,8},{12,... | collective-permute-start | bytes 1179656 | tf_op jit(solution)/shard_map/ppermute | solution.py:506
  328.4 10.1 %collective-permute-start.48 = (bf16[2,128,768]{2,1,0:T(8,128)(2,1)S(1)}, bf16[2,128,768]{2,1,0:T(8,128)(2,1)S(1)}, u32[]{:S(2)}, u32[]{:S(2)}) collective-permute-start(bf16[2,128,768]{2,1,0:T(8,128)(2,1)S(1)} %pad_maximum_fusion.11), channel_id=1, source_target_pairs={{0,4},{2,6},{4,0},{6,2},{1,5},{3,7},{5,1},{7,3},{8,12},{10,14},{12... | collective-permute-start | bytes 1179656 | tf_op jit(solution)/shard_map/ppermute | solution.py:506
  329.6 17.4 %collective-permute-start.49 = (bf16[2,128,768]{2,1,0:T(8,128)(2,1)S(1)}, bf16[2,128,768]{2,1,0:T(8,128)(2,1)S(1)}, u32[]{:S(2)}, u32[]{:S(2)}) collective-permute-start(bf16[2,128,768]{2,1,0:T(8,128)(2,1)S(1)} %pad_maximum_fusion.11), channel_id=1, source_target_pairs={{0,6},{2,4},{4,2},{6,0},{1,7},{3,5},{5,3},{7,1},{8,14},{10,12},{12... | collective-permute-start | bytes 1179656 | tf_op jit(solution)/shard_map/ppermute | solution.py:506
  338.2 9.3 %collective-permute-start.51 = (bf16[144,768]{1,0:T(8,128)(2,1)S(1)}, bf16[144,768]{1,0:T(8,128)(2,1)S(1)}, u32[]{:S(2)}, u32[]{:S(2)}) collective-permute-start(bf16[144,768]{1,0:T(8,128)(2,1)S(1)} %add_convert_fusion.7), channel_id=1, source_target_pairs={{0,8},{8,0},{16,24},{24,16},{1,9},{9,1},{17,25},{25,17},{2,10},{10... | collective-permute-start | bytes 663560 | tf_op jit(solution)/shard_map/ppermute | solution.py:499
  (62 other events, 515.2 us)
Sparse Core Ops, SparseCore 0:
  32.3 64.0 all-gather.4
  115.9 37.5 all-gather.6
  165.9 71.4 reduce-scatter.3
  262.8 61.4 all-reduce.2

commit v11 on v10

--- a/solution.py
+++ b/solution.py
@@ -451,10 +451,30 @@
     return single(weight_grad_kernel, core, args, out_shape, 7, "weight_grads")[0]
 
 
+def weight_results_kernel(core, near, far, up, down, out):
+    part, rows = up.shape[1] // 2, out.shape[0] // 2
+    for which, ref in enumerate((near, far)):
+        at = core[0] if which == 0 else 1 - core[0]
+        at_part = pl.ds(pl.multiple_of(at * part, 128), part)
+        up[:, at_part] = ref[0:part, :].astype(f32).T
+        down[at_part, :] = ref[part : 2 * part, :].astype(f32)
+        at_rows = pl.ds(pl.multiple_of(at * rows, 16), rows)
+        out[at_rows, :] = ref[2 * part : 2 * part + rows, :].astype(f32)
+
+
+def weight_results(core, near, far, head_width):
+    width = near.shape[1]
+    part = (near.shape[0] - 32 - head_width // 2) // 2
+    out_shape = [
+        shape((width, 2 * part), f32), shape((2 * part, width), f32), shape((head_width, width), f32)
+    ]
+    return single(weight_results_kernel, core, [near, far], out_shape, 3, "weight_results")
+
+
 def input_grad(core, grad_first, blocks, near, far):
     out_shape = [shape(grad_first.shape, bf16)]
     args = [grad_first, *blocks, near, far]
-    return single(input_grad_kernel, core, args, out_shape, 3, "input_grad")[0]
+    return single(input_grad_kernel, core, args, out_shape, 40, "input_grad")[0]
 
 
 def after(x, *others):
@@ -682,13 +702,13 @@
     layer_moved = [after(x, dkv_z) for x in layer_moved]
     dkv_o = key_backward(
         signed, signed_t, bits, head_n, near_o, after(kv_o, dkv_far, grad_q, weight_sum, *layer_moved),
-        grad_tables, bf16, 2,
+        grad_tables, bf16, 25,
     )
     weight_sum = lax.psum(weight_sum, "hash")
     dkv_far = over_place(dkv_far)
     dkv_o_moved = over_seq(dkv_o)
     dkv = key_backward(
-        signed, signed_t, bits, head_n, near, kv, grad_tables, f32, 2
+        signed, signed_t, bits, head_n, near, kv, grad_tables, f32, 25
     )
 
     dkv_o_moved = after(dkv_o_moved, dkv)
@@ -739,15 +759,10 @@
     w_grad = in_halves(r, w_keep, over_place(w_keep))
     w_grad = in_halves(s, w_grad, over_seq(w_grad)).reshape(3, head_width, width)
     grad_w_qkv = w_grad.transpose(0, 2, 1).astype(f32)
-    weight_sum = after(weight_sum, grad_in)
+    weight_sum = after(weight_sum, *grad_moved)
     weight_far = over_seq(weight_sum)
-    ends = [0, cut, 2 * cut, 2 * cut + head_width // 2]
-    grad_w_up, grad_w_down, grad_w_out = [
-        in_halves(s, weight_sum[a:b], weight_far[a:b]) for a, b in zip(ends, ends[1:])
-    ]
-    grad_w_up = grad_w_up.T.astype(f32)
-    grad_w_down, grad_w_out = grad_w_down.astype(f32), grad_w_out.astype(f32)
-    at = slice(ends[3], ends[3] + 16)
+    grad_w_up, grad_w_down, grad_w_out = weight_results(core, weight_sum, weight_far, head_width)
+    at = slice(2 * cut + out_cut, 2 * cut + out_cut + 16)
     small = add(weight_sum[at], weight_far[at])
 
     count = piece * seqs * width * hash_count * 2

time: 378 us -> 363 us (0.960)
  waiting for transfers between devices: 69.4 us -> 58.3 us
  local copies, waits for them, and re-layouts: 43 us -> 37.8 us
  Pallas kernels: 159 us -> 164 us
    psum x1, waiting for transfers between devices: 24.1 us -> 6.02 us  [shards(): weight_sum = lax.psum(weight_sum, 'hash')]
    ppermute x4, waiting for transfers between devices: 13.6 us -> 29 us  [over_group(): return lax.ppermute(x, 'hash', moves)]
    ppermute x18, waiting for transfers between devices: 23.1 us -> 14.1 us  [over_head(): return lax.ppermute(x, 'head', [(h, h ^ j) for h in range(head_count)])]
    pallas_call x4 -> x5, Pallas kernels: 38.8 us -> 43.5 us  [single(): pl.pallas_call(kernel, in_specs=[pl.BlockSpec(memory_space=pltpu.SMEM)] +...]
    unnamed x117 -> x118, local copies, waits for them, and re-layouts: 23.3 us -> 19.1 us
    convert_element_type x3 -> x0, other arithmetic: 3.99 us -> none  [the longest x2 3.82 us: shards(): grad_w_down, grad_w_out = (grad_w_down.astype(f32), grad_w_out.astype(f32))]
  transfers between devices with their start and end apart: 58 -> 58, of which waited for: 14 -> 12; matrix products, arithmetic and copies ran while one was open for 13% -> 14% of each run, Pallas kernels for 43% -> 45%
where the time goes in v11:
time: 363 us; the launch traced here: 358 us
  Pallas kernels  164 us (45%)
  waiting for transfers between devices  58.3 us (16%)
  starting transfers between devices  53.3 us (15%)
  local copies, waits for them, and re-layouts  37.8 us (10%)
  other arithmetic  24.9 us (7%)
  between operations  15.4 us (4%)
  matrix products  4.15 us (1%)
    pallas_call x5, Pallas kernels, single(): pl.pallas_call(kernel, in_specs=[pl.BlockSpec(memory_space=pltpu.SMEM)] +...  43.5 us
    pallas_call x3, Pallas kernels, query_backward(): call(partial(query_back_kernel, chunk=4, blocks=blocks, last=last), heads...  43.2 us
    pallas_call x4, Pallas kernels, key_backward(): call(partial(key_back_kernel, chunk=4), heads, micros, 'key_backward', [w...  38.2 us
    ppermute x4, waiting for transfers between devices, over_group(): return lax.ppermute(x, 'hash', moves)  29 us
    pallas_call x5, Pallas kernels, key_tables(): call(partial(key_kernel, chunk=2, blocks=len(blocks)), heads, 30 if len(b...  23.5 us
    unnamed x118, local copies, waits for them, and re-layouts  19.1 us
    ppermute x22, starting transfers between devices, over_seq(): return lax.ppermute(x, 'seq', [(0, 1), (1, 0)])  16.9 us
    ppermute x18, starting transfers between devices, over_head(): return lax.ppermute(x, 'head', [(h, h ^ j) for h in range(head_count)])  16.6 us
  transfers between devices with their start and end apart: 58, of which 12 were waited for; matrix products, arithmetic and copies ran while one was open for 14% of the time, Pallas kernels for 45%

profile of v11, /device:TPU:1, one launch (start us, length us, event | category | flops | bytes accessed | tf_op | source)
XLA Modules:
  0.0 358.0 jit_solution(17606683767663198029)
XLA Ops:
  7.3 4.5 %constant_dynamic-slice_fusion.7 = (bf16[1,128,1,768]{3,2,1,0:T(2,128)(2,1)S(1)}, bf16[1,128,1,768]{3,2,1,0:T(2,128)(2,1)}, bf16[1,128,1,768]{3,2,1,0:T(2,128)(2...) fusion(bf16[1,512,2,768]{3,2,1,0:T(2,128)(2,1)} %param.11, s32[]{:T(128)S(6)} %select_n.222, ...), kind=kLoop, calls=%fused_computation.121 | loop fusion | bytes 1966104 | tf_op jit(solution)/shard_map/jit(dynamic_index_in_dim)/dynamic_slice | solution.py:529
  12.6 3.1 collective-permute-start
  16.3 2.5 collective-permute-start.1
  20.5 2.4 copy.54
  22.9 1.8 copy_bitcast_fusion
  24.7 1.9 dynamic-slice_bitcast_fusion
  37.1 1.9 slice.118
  39.0 1.7 slice.117
  40.7 5.3 %key_tables.5.refs_4_ = f32[3,2048,64]{2,1,0:T(8,128)S(1)} custom-call(bf16[64,64]{1,0:T(8,128)(2,1)S(1)} %bitcast.129, bf16[576,512]{1,0:T(8,128)(2,1)} %bitcast.14.refs_0_.refs_2_.ka.va, bf16[576,512]{1,0:T(8,128)(2,1)} %collective-permute-done.2.refs_1_.refs_3_.refs_0_.refs_2_.ka.va, bf16[576,512]{1,0:T(8,128)(2,1)} %bitcast.14.refs_0_.refs_2_.ka.va, ...), custom_call_target="tpu_custom_call" | custom-call | flops 1100000000 | bytes 1048576 | tf_op jit(solution)/shard_map/key_tables/pallas_call | solution.py:192
  46.0 2.1 pad_maximum_fusion.7
  49.1 1.9 collective-permute-start.8
  53.4 5.8 %key_tables.6.refs_4_ = f32[3,2048,64]{2,1,0:T(8,128)S(1)} custom-call(bf16[64,64]{1,0:T(8,128)(2,1)S(1)} %bitcast.130, bf16[576,512]{1,0:T(8,128)(2,1)} %collective-permute-done.9.refs_0_.refs_2_.ka.va, bf16[576,512]{1,0:T(8,128)(2,1)S(1)} %collective-permute-done.10.refs_1_.refs_3_.refs_0_.ka.va, ...), custom_call_target="tpu_custom_call" | custom-call | flops 32999999488 | bytes 1048576 | tf_op jit(solution)/shard_map/key_tables/pallas_call | solution.py:192
  60.9 5.6 %key_tables.7.refs_2_ = f32[3,2048,64]{2,1,0:T(8,128)S(1)} custom-call(bf16[64,64]{1,0:T(8,128)(2,1)S(1)} %bitcast.131, bf16[384,512]{1,0:T(8,128)(2,1)S(1)} %bitcast.125, bf16[384,512]{1,0:T(8,128)(2,1)S(1)} %collective-permute-done.8.refs_1_.refs_3_.kb.vb, bf16[384,512]{1,0:T(8,128)(2,1)S(1)} %bitcast.126, ...), custom_call_target="tpu_custom_call" | custom-call | flops 32999999488 | bytes 1048576 | tf_op jit(solution)/shard_map/key_tables/pallas_call | solution.py:192
  69.8 1.7 pad_maximum_fusion.9.x_in
  71.5 4.2 %key_tables.8.refs_2_ = f32[3,2048,64]{2,1,0:T(8,128)S(1)} custom-call(bf16[64,64]{1,0:T(8,128)(2,1)S(1)} %bitcast.132, bf16[384,512]{1,0:T(8,128)(2,1)S(1)} %collective-permute-done.7.refs_0_.refs_1_.kb.vb, bf16[384,512]{1,0:T(8,128)(2,1)S(1)} %collective-permute-done.7.refs_0_.refs_1_.kb.vb, f32[3,2048,64]{2,1,0:T(8,128)} %copy-done.2), custom_call_target="tpu_custom_call" | custom-call | flops 1100000000 | bytes 1048576 | tf_op jit(solution)/shard_map/key_tables/pallas_call | solution.py:192
  76.4 2.6 key_tables.9.tables
  79.0 3.3 query_estimates.4
  82.9 4.1 %query_estimates.5 = bf16[192,1024]{1,0:T(8,128)(2,1)S(1)} custom-call(bf16[64,64]{1,0:T(8,128)(2,1)S(1)} %bitcast.135, bf16[3,2048,64]{2,1,0:T(8,128)(2,1)S(1)} %key_tables.9.tables, bf16[576,512]{1,0:T(8,128)(2,1)} %collective-permute-done.9.refs_0_.refs_2_.ka.va, bf16[192,512]{1,0:T(8,128)(2,1)S(1)} %collective-permute-done.6.refs_1_), custom_call_target="tpu_custom_call" | custom-call | flops 1100000000 | bytes 1048576 | tf_op jit(solution)/shard_map/query_estimates/pallas_call | solution.py:205
  87.9 4.2 %query_estimates.6 = bf16[192,1024]{1,0:T(8,128)(2,1)S(1)} custom-call(bf16[64,64]{1,0:T(8,128)(2,1)S(1)} %bitcast.136, bf16[3,2048,64]{2,1,0:T(8,128)(2,1)S(1)} %key_tables.9.tables, bf16[576,512]{1,0:T(8,128)(2,1)} %collective-permute-done.2.refs_1_.refs_3_.refs_0_.refs_2_.ka.va, bf16[192,512]{1,0:T(8,128)(2,1)S(1)} %collective-permute-done.12.refs_1_.refs_3_), custom_call_target="tpu_custom_call" | custom-call | flops 1100000000 | bytes 1048576 | tf_op jit(solution)/shard_map/query_estimates/pallas_call | solution.py:205
  92.9 3.5 all-gather.5.cloned.1.call-done
  99.9 4.2 %query_estimates.7 = f32[192,1024]{1,0:T(8,128)S(1)} custom-call(bf16[64,64]{1,0:T(8,128)(2,1)S(1)} %bitcast.138, bf16[3,2048,64]{2,1,0:T(8,128)(2,1)S(1)} %key_tables.9.tables, bf16[576,512]{1,0:T(8,128)(2,1)} %bitcast.14.refs_0_.refs_2_.ka.va, bf16[192,512]{1,0:T(8,128)(2,1)S(1)} %convolution_convert_fusion.1.refs_1_), custom_call_target="tpu_custom_call" | custom-call | flops 1100000000 | bytes 1048576 | tf_op jit(solution)/shard_map/query_estimates/pallas_call | solution.py:205
  104.1 3.4 collective-permute-done.16
  116.7 12.7 %dense.1 = (bf16[256,768]{1,0:T(8,128)(2,1)}, f32[256,768]{1,0:T(8,128)}, f32[256,768]{1,0:T(8,128)}, f32[8,256,384]{2,1,0:T(8,128)}, bf16[8,256,384]{2,1,0:T(8,...) custom-call(s32[2]{0:T(128)} %pad_add_fusion.core, ...), custom_call_target="tpu_custom_call" | custom-call | flops 15399999488 | bytes 1048576 | tf_op jit(solution)/shard_map/dense/pallas_call | solution.py:402
  129.5 12.6 %dense_back.1 = (f32[256,768]{1,0:T(8,128)}, bf16[6,256,384]{2,1,0:T(8,128)(2,1)}, bf16[6,256,384]{2,1,0:T(8,128)(2,1)}, bf16[192,256]{1,0:T(8,128)(2,1)}, bf16[...) custom-call(s32[2]{0:T(128)} %pad_add_fusion.core, ...), custom_call_target="tpu_custom_call" | custom-call | flops 8800000000 | bytes 1048576 | tf_op jit(solution)/shard_map/dense_back/pallas_call | solution.py:402
  144.7 2.8 collective-permute-start.25
  149.0 2.9 collective-permute-start.26
  151.9 2.1 collective-permute-start.27
  157.6 8.2 %weight_grads.1 = bf16[4,896,768]{2,1,0:T(8,128)(2,1)} custom-call(s32[2]{0:T(128)} %pad_add_fusion.core, f32[8,768]{1,0:T(8,128)} %get-tuple-element.136.small_a, f32[8,768]{1,0:T(8,128)} %get-tuple-element.137.small_b, bf16[8,256,384]{2,1,0:T(8,128)(2,1)} %get-tuple-element.138.refs_0_, bf16[8,256,384]{2,1,0:T(8,128)(2,1)} %collective-permute-done.24.refs_1_, ...), custom_call_target="tpu_custom_call" | custom-call | flops 7699999744 | bytes 1048576 | tf_op jit(solution)/shard_map/weight_grads/pallas_call | solution.py:402
  169.1 20.2 %query_backward.3 = (f32[3,2048,64]{2,1,0:T(8,128)}, f32[192,1024]{1,0:T(8,128)S(1)}, bf16[192,1024]{1,0:T(8,128)(2,1)S(1)}) custom-call(bf16[64,64]{1,0:T(8,128)(2,1)S(1)} %bitcast.139, bf16[64,128]{1,0:T(8,128)(2,1)S(1)} %pad_maximum_fusion.20.planes_t, bf16[80,2048]{1,0:T(8,128)(2,1)S(1)} %copy-done.16, bf16[3,2048,64]{2,1,0:T(8,128)(2,1)S(1)} %key_tables.9.tables, ...), custom_call_target="tpu_custom_call" | custom-call | flops 54999998464 | bytes 1048576 | tf_op jit(solution)/shard_map/query_backward/pallas_call | solution.py:229
  189.9 11.7 %query_backward.4 = (f32[3,2048,64]{2,1,0:T(8,128)}, f32[192,1024]{1,0:T(8,128)S(1)}) custom-call(bf16[64,64]{1,0:T(8,128)(2,1)S(1)} %bitcast.140, bf16[64,128]{1,0:T(8,128)(2,1)S(1)} %pad_maximum_fusion.20.planes_t, bf16[80,2048]{1,0:T(8,128)(2,1)S(1)} %copy-done.16, bf16[3,2048,64]{2,1,0:T(8,128)(2,1)S(1)} %key_tables.9.tables, ...), custom_call_target="tpu_custom_call" | custom-call | flops 27499999232 | bytes 1048576 | tf_op jit(solution)/shard_map/query_backward/pallas_call | solution.py:229
  204.4 11.2 %query_backward.5 = (bf16[3,2048,64]{2,1,0:T(8,128)(2,1)S(1)}, bf16[192,1024]{1,0:T(8,128)(2,1)S(1)}) custom-call(bf16[64,64]{1,0:T(8,128)(2,1)S(1)} %bitcast.141, bf16[64,128]{1,0:T(8,128)(2,1)S(1)} %pad_maximum_fusion.20.planes_t, bf16[80,2048]{1,0:T(8,128)(2,1)S(1)} %copy-done.16, bf16[3,2048,64]{2,1,0:T(8,128)(2,1)S(1)} %key_tables.9.tables, ...), custom_call_target="tpu_custom_call" | custom-call | flops 27499999232 | bytes 1048576 | tf_op jit(solution)/shard_map/query_backward/pallas_call | solution.py:229
  216.9 8.8 %key_backward.4 = bf16[2,192,1024]{2,1,0:T(8,128)(2,1)S(1)} custom-call(bf16[64,64]{1,0:T(8,128)(2,1)S(1)} %bitcast.142, bf16[64,128]{1,0:T(8,128)(2,1)S(1)} %pad_maximum_fusion.20.planes_t, bf16[80,2048]{1,0:T(8,128)(2,1)S(1)} %copy-done.17, bf16[576,512]{1,0:T(8,128)(2,1)S(1)} %copy-done.11, bf16[384,512]{1,0:T(8,128)(2,1)S(1)} %copy-done.7, ...), custom_call_target="tpu_custom_call" | custom-call | flops 27499999232 | bytes 1048576 | tf_op jit(solution)/shard_map/key_backward/pallas_call | solution.py:243
  226.7 9.7 %key_backward.5 = bf16[2,192,1024]{2,1,0:T(8,128)(2,1)S(1)} custom-call(bf16[64,64]{1,0:T(8,128)(2,1)S(1)} %bitcast.143, bf16[64,128]{1,0:T(8,128)(2,1)S(1)} %pad_maximum_fusion.20.planes_t, bf16[80,2048]{1,0:T(8,128)(2,1)S(1)} %copy-done.17, bf16[576,512]{1,0:T(8,128)(2,1)} %collective-permute-done.9.refs_0_.refs_2_.ka.va, bf16[384,512]{1,0:T(8,128)(2,1)S(1)} %copy-done.5, ...), custom_call_target="tpu_custom_call" | custom-call | flops 27499999232 | bytes 1048576 | tf_op jit(solution)/shard_map/key_backward/pallas_call | solution.py:243
  240.1 9.8 %key_backward.7 = bf16[2,192,1024]{2,1,0:T(8,128)(2,1)S(1)} custom-call(bf16[64,64]{1,0:T(8,128)(2,1)S(1)} %bitcast.144, bf16[64,128]{1,0:T(8,128)(2,1)S(1)} %pad_maximum_fusion.20.planes_t, bf16[80,2048]{1,0:T(8,128)(2,1)S(1)} %copy-done.18, bf16[576,512]{1,0:T(8,128)(2,1)} %collective-permute-done.2.refs_1_.refs_3_.refs_0_.refs_2_.ka.va, ...), custom_call_target="tpu_custom_call" | custom-call | flops 27499999232 | bytes 1048576 | tf_op jit(solution)/shard_map/key_backward/pallas_call | solution.py:243
  250.3 10.0 %key_backward.6 = f32[2,192,1024]{2,1,0:T(8,128)S(1)} custom-call(bf16[64,64]{1,0:T(8,128)(2,1)S(1)} %bitcast.145, bf16[64,128]{1,0:T(8,128)(2,1)S(1)} %pad_maximum_fusion.20.planes_t, bf16[80,2048]{1,0:T(8,128)(2,1)S(1)} %copy-done.18, bf16[576,512]{1,0:T(8,128)(2,1)} %bitcast.14.refs_0_.refs_2_.ka.va, bf16[384,512]{1,0:T(8,128)(2,1)S(1)} %bitcast.127, ...), custom_call_target="tpu_custom_call" | custom-call | flops 27499999232 | bytes 1048576 | tf_op jit(solution)/shard_map/key_backward/pallas_call | solution.py:243
  260.3 1.8 add_convert_fusion
  268.4 3.6 %collective-permute-done.42.refs_3_ = bf16[3,192,256]{2,1,0:T(8,128)(2,1)S(1)} collective-permute-done((bf16[3,192,256]{2,1,0:T(8,128)(2,1)S(1)}, bf16[3,192,256]{2,1,0:T(8,128)(2,1)S(1)}, u32[]{:S(2)}, u32[]{:S(2)}) %collective-permute-start.42) | collective-permute-done | bytes 294944 | tf_op jit(solution)/shard_map/ppermute | solution.py:526
  272.0 6.8 %collective-permute-done.41.refs_2_ = bf16[3,192,256]{2,1,0:T(8,128)(2,1)S(1)} collective-permute-done((bf16[3,192,256]{2,1,0:T(8,128)(2,1)S(1)}, bf16[3,192,256]{2,1,0:T(8,128)(2,1)S(1)}, u32[]{:S(2)}, u32[]{:S(2)}) %collective-permute-start.41) | collective-permute-done | bytes 294944 | tf_op jit(solution)/shard_map/ppermute | solution.py:526
  279.6 5.3 %input_grad.1 = bf16[256,768]{1,0:T(8,128)(2,1)} custom-call(s32[2]{0:T(128)} %pad_add_fusion.core, f32[256,768]{1,0:T(8,128)} %get-tuple-element.161.grad_first, bf16[3,192,256]{2,1,0:T(8,128)(2,1)} %pad_maximum_fusion.12.refs_0_, bf16[3,192,256]{2,1,0:T(8,128)(2,1)} %copy-done.48, bf16[3,192,256]{2,1,0:T(8,128)(2,1)} %copy-done.47, ...), custom_call_target="tpu_custom_call" | custom-call | flops 44000002048 | bytes 1048576 | tf_op jit(solution)/shard_map/input_grad/pallas_call | solution.py:402
  286.0 1.8 collective-permute-start.44
  289.0 8.7 %collective-permute-done.44 = bf16[128,768]{1,0:T(8,128)(2,1)S(1)} collective-permute-done((bf16[128,768]{1,0:T(8,128)(2,1)S(1)}, bf16[128,768]{1,0:T(8,128)(2,1)S(1)}, u32[]{:S(2)}, u32[]{:S(2)}) %collective-permute-start.44) | collective-permute-done | bytes 196640 | tf_op jit(solution)/shard_map/ppermute | solution.py:523
  300.8 1.7 collective-permute-start.50
  303.3 2.8 copy.56
  306.1 20.3 %collective-permute-done.50 = bf16[144,768]{1,0:T(8,128)(2,1)S(1)} collective-permute-done((bf16[144,768]{1,0:T(8,128)(2,1)S(1)}, bf16[144,768]{1,0:T(8,128)(2,1)S(1)}, u32[]{:S(2)}, u32[]{:S(2)}) %collective-permute-start.50) | collective-permute-done | bytes 221216 | tf_op jit(solution)/shard_map/ppermute | solution.py:523
  326.6 6.0 %all-reduce.3.cloned.1.call-done.near = bf16[896,768]{1,0:T(8,128)(2,1)} async-done(((bf16[896,768]{1,0:T(8,128)(2,1)}), bf16[896,768]{1,0:T(8,128)(2,1)}) %all-reduce.3.cloned.1.call-update) | async-done | bytes 1376272 | tf_op jit(solution)/shard_map/psum | solution.py:707
  335.0 1.7 collective-permute-done.51
  337.9 4.1 %copy.57 = f32[1,512,2,768]{3,2,1,0:T(2,128)} copy(f32[1,512,2,768]{3,1,2,0:T(8,128)S(1)} %maximum_convert_fusion) | data formatting | bytes 6291456
  346.2 4.7 %weight_results.1 = (f32[768,768]{1,0:T(8,128)}, f32[768,768]{1,0:T(8,128)}, f32[192,768]{1,0:T(8,128)}) custom-call(s32[2]{0:T(128)} %pad_add_fusion.core, bf16[896,768]{1,0:T(8,128)(2,1)} %all-reduce.3.cloned.1.call-done.near, bf16[896,768]{1,0:T(8,128)(2,1)} %copy-done.45), custom_call_target="tpu_custom_call" | custom-call | flops 3300000000 | bytes 1048576 | tf_op jit(solution)/shard_map/weight_results/pallas_call | solution.py:402
  (287 shorter events, 79.0 us)
Async XLA Ops:
  7.2 89.1 %all-gather.5.cloned.1.call-start = ((), (), s32[]{:S(2)}) async-start(), calls=%async_computation.2 | async-start | bytes 6635520 | tf_op jit(solution)/shard_map/all_gather | solution.py:564
  12.6 16.4 %collective-permute-start = (bf16[128,768]{1,0:T(8,128)(2,1)}, bf16[128,768]{1,0:T(8,128)(2,1)}, u32[]{:S(2)}, u32[]{:S(2)}) collective-permute-start(bf16[128,768]{1,0:T(8,128)(2,1)} %bitcast.121), channel_id=1, source_target_pairs={{0,16},{8,24},{16,0},{24,8},{1,17},{9,25},{17,1},{25,9},{2,18},{10... | collective-permute-start | bytes 589832 | tf_op jit(solution)/shard_map/ppermute | solution.py:523
  16.3 19.9 %collective-permute-start.1 = (bf16[8,8,64]{2,0,1:T(8,128)(2,1)}, bf16[8,8,64]{2,0,1:T(8,128)(2,1)S(1)}, u32[]{:S(2)}, u32[]{:S(2)}) collective-permute-start(bf16[8,8,64]{2,0,1:T(8,128)(2,1)} %fusion.17), channel_id=1, source_target_pairs={{0,0},{8,1},{16,8},{24,9},{1,16},{9,17},{17,24},{25,25},{2,2},{10,... | collective-permute-start | bytes 24584 | tf_op jit(solution)/shard_map/ppermute | solution.py:548
  30.5 10.2 %collective-permute-start.2 = (bf16[576,512]{1,0:T(8,128)(2,1)}, bf16[576,512]{1,0:T(8,128)(2,1)}, u32[]{:S(2)}, u32[]{:S(2)}) collective-permute-start(bf16[576,512]{1,0:T(8,128)(2,1)} %bitcast.14.refs_0_.refs_2_.ka.va), channel_id=1, source_target_pairs={{0,1},{1,0},{2,3},{3,2},{4,5},{5,4},{6,7},{7,6},{8,9},{9,8},{10,11... | collective-permute-start | bytes 1769480 | tf_op jit(solution)/shard_map/ppermute | solution.py:516
  32.2 124.2 %all-gather.7.cloned.1.call-start = ((), (), s32[]{:S(2)}) async-start(), calls=%async_computation.3 | async-start | bytes 2211840 | tf_op jit(solution)/shard_map/all_gather | solution.py:629
  32.4 18.5 %collective-permute-start.9 = (bf16[576,512]{1,0:T(8,128)(2,1)}, bf16[576,512]{1,0:T(8,128)(2,1)}, u32[]{:S(2)}, u32[]{:S(2)}) collective-permute-start(bf16[576,512]{1,0:T(8,128)(2,1)} %bitcast.14.refs_0_.refs_2_.ka.va), channel_id=1, source_target_pairs={{0,8},{8,0},{16,24},{24,16},{1,9},{9,1},{17,25},{25,17},{2,10},{10... | collective-permute-start | bytes 1769480 | tf_op jit(solution)/shard_map/ppermute | solution.py:519
  33.8 12.2 %collective-permute-start.3 = (bf16[1,128,768]{2,1,0:T(8,128)(2,1)}, bf16[1,128,768]{2,1,0:T(8,128)(2,1)S(1)}, u32[]{:S(2)}, u32[]{:S(2)}) collective-permute-start(bf16[1,128,768]{2,1,0:T(8,128)(2,1)} %bitcast.20), channel_id=1, source_target_pairs={{0,2},{2,0},{4,6},{6,4},{1,3},{3,1},{5,7},{7,5},{8,10},{10,8},{12,... | collective-permute-start | bytes 589832 | tf_op jit(solution)/shard_map/ppermute | solution.py:526
  35.0 11.0 %collective-permute-start.4 = (bf16[1,128,768]{2,1,0:T(8,128)(2,1)}, bf16[1,128,768]{2,1,0:T(8,128)(2,1)}, u32[]{:S(2)}, u32[]{:S(2)}) collective-permute-start(bf16[1,128,768]{2,1,0:T(8,128)(2,1)} %bitcast.20), channel_id=1, source_target_pairs={{0,4},{2,6},{4,0},{6,2},{1,5},{3,7},{5,1},{7,3},{8,12},{10,14},{12... | collective-permute-start | bytes 589832 | tf_op jit(solution)/shard_map/ppermute | solution.py:526
  36.2 9.8 %collective-permute-start.5 = (bf16[1,128,768]{2,1,0:T(8,128)(2,1)}, bf16[1,128,768]{2,1,0:T(8,128)(2,1)}, u32[]{:S(2)}, u32[]{:S(2)}) collective-permute-start(bf16[1,128,768]{2,1,0:T(8,128)(2,1)} %bitcast.20), channel_id=1, source_target_pairs={{0,6},{2,4},{4,2},{6,0},{1,7},{3,5},{5,3},{7,1},{8,14},{10,12},{12... | collective-permute-start | bytes 589832 | tf_op jit(solution)/shard_map/ppermute | solution.py:526
  49.1 11.8 %collective-permute-start.8 = (bf16[384,512]{1,0:T(8,128)(2,1)S(1)}, bf16[384,512]{1,0:T(8,128)(2,1)S(1)}, u32[]{:S(2)}, u32[]{:S(2)}) collective-permute-start(bf16[384,512]{1,0:T(8,128)(2,1)S(1)} %bitcast.123), channel_id=1, source_target_pairs={{0,1},{1,0},{2,3},{3,2},{4,5},{5,4},{6,7},{7,6},{8,9},{9,8},{10,11... | collective-permute-start | bytes 1179656 | tf_op jit(solution)/shard_map/ppermute | solution.py:516
  51.0 17.2 %collective-permute-start.7 = (bf16[384,512]{1,0:T(8,128)(2,1)S(1)}, bf16[384,512]{1,0:T(8,128)(2,1)S(1)}, u32[]{:S(2)}, u32[]{:S(2)}) collective-permute-start(bf16[384,512]{1,0:T(8,128)(2,1)S(1)} %bitcast.124), channel_id=1, source_target_pairs={{0,8},{8,0},{16,24},{24,16},{1,9},{9,1},{17,25},{25,17},{2,10},{10... | collective-permute-start | bytes 1179656 | tf_op jit(solution)/shard_map/ppermute | solution.py:519
  68.2 8.2 %collective-permute-start.11 = (bf16[384,512]{1,0:T(8,128)(2,1)S(1)}, bf16[384,512]{1,0:T(8,128)(2,1)S(1)}, u32[]{:S(2)}, u32[]{:S(2)}) collective-permute-start(bf16[384,512]{1,0:T(8,128)(2,1)S(1)} %collective-permute-done.7.refs_0_.refs_1_.kb.vb), channel_id=1, source_target_pairs={{0,1},{1,0},{2,3},{3,2},{4,5},{5,4},{6,7},{7,6},{8,9},{9,8},{10,11... | collective-permute-start | bytes 1179656 | tf_op jit(solution)/shard_map/ppermute | solution.py:516
  68.5 7.2 %collective-permute-start.6 = (bf16[192,512]{1,0:T(8,128)(2,1)S(1)}, bf16[192,512]{1,0:T(8,128)(2,1)S(1)}, u32[]{:S(2)}, u32[]{:S(2)}) collective-permute-start(bf16[192,512]{1,0:T(8,128)(2,1)S(1)} %convolution_convert_fusion.1.refs_1_), channel_id=1, source_target_pairs={{0,8},{8,0},{16,24},{24,16},{1,9},{9,1},{17,25},{25,17},{2,10},{10... | collective-permute-start | bytes 589832 | tf_op jit(solution)/shard_map/ppermute | solution.py:519
  96.3 20.3 %collective-permute-start.20 = (bf16[4,864,768]{2,1,0:T(8,128)(2,1)}, bf16[4,864,768]{2,1,0:T(8,128)(2,1)}, u32[]{:S(2)}, u32[]{:S(2)}) collective-permute-start(bf16[4,864,768]{2,1,0:T(8,128)(2,1)} %bitcast.172), channel_id=1, source_target_pairs={{0,1},{1,0},{2,3},{3,2},{4,5},{5,4},{6,7},{7,6},{8,9},{9,8},{10,11... | collective-permute-start | bytes 15925256 | tf_op jit(solution)/shard_map/ppermute | solution.py:516
  97.0 10.5 %collective-permute-start.16 = (bf16[192,1024]{1,0:T(8,128)(2,1)}, bf16[192,1024]{1,0:T(8,128)(2,1)}, u32[]{:S(2)}, u32[]{:S(2)}) collective-permute-start(bf16[192,1024]{1,0:T(8,128)(2,1)} %add_convert_fusion.6), channel_id=1, source_target_pairs={{0,8},{8,0},{16,24},{24,16},{1,9},{9,1},{17,25},{25,17},{2,10},{10... | collective-permute-start | bytes 1179656 | tf_op jit(solution)/shard_map/ppermute | solution.py:519
  116.1 123.9 %reduce-scatter.4.cloned.1.call-start = ((), (), s32[]{:S(2)}) async-start(), calls=%async_computation.4 | async-start | bytes 6881280
  142.3 9.6 %collective-permute-start.22 = (bf16[192,256]{1,0:T(8,128)(2,1)}, bf16[192,256]{1,0:T(8,128)(2,1)S(1)}, u32[]{:S(2)}, u32[]{:S(2)}) collective-permute-start(bf16[192,256]{1,0:T(8,128)(2,1)} %get-tuple-element.130), channel_id=1, source_target_pairs={{0,4},{2,6},{4,0},{6,2},{1,5},{3,7},{5,1},{7,3},{8,12},{10,14},{12... | collective-permute-start | bytes 294920 | tf_op jit(solution)/shard_map/ppermute | solution.py:526
  143.5 10.5 %collective-permute-start.23 = (bf16[192,256]{1,0:T(8,128)(2,1)}, bf16[192,256]{1,0:T(8,128)(2,1)S(1)}, u32[]{:S(2)}, u32[]{:S(2)}) collective-permute-start(bf16[192,256]{1,0:T(8,128)(2,1)} %get-tuple-element.131), channel_id=1, source_target_pairs={{0,6},{2,4},{4,2},{6,0},{1,7},{3,5},{5,3},{7,1},{8,14},{10,12},{12... | collective-permute-start | bytes 294920 | tf_op jit(solution)/shard_map/ppermute | solution.py:526
  144.7 12.9 %collective-permute-start.25 = (bf16[6,256,384]{2,1,0:T(8,128)(2,1)}, bf16[6,256,384]{2,1,0:T(8,128)(2,1)}, u32[]{:S(2)}, u32[]{:S(2)}) collective-permute-start(bf16[6,256,384]{2,1,0:T(8,128)(2,1)} %get-tuple-element.141), channel_id=1, source_target_pairs={{0,1},{1,0},{2,3},{3,2},{4,5},{5,4},{6,7},{7,6},{8,9},{9,8},{10,11... | collective-permute-start | bytes 3538952 | tf_op jit(solution)/shard_map/ppermute | solution.py:516
  147.4 10.2 %collective-permute-start.24 = (bf16[8,256,384]{2,1,0:T(8,128)(2,1)}, bf16[8,256,384]{2,1,0:T(8,128)(2,1)}, u32[]{:S(2)}, u32[]{:S(2)}) collective-permute-start(bf16[8,256,384]{2,1,0:T(8,128)(2,1)} %get-tuple-element.139), channel_id=1, source_target_pairs={{0,1},{1,0},{2,3},{3,2},{4,5},{5,4},{6,7},{7,6},{8,9},{9,8},{10,11... | collective-permute-start | bytes 4718600 | tf_op jit(solution)/shard_map/ppermute | solution.py:516
  149.0 7.4 %collective-permute-start.26 = (bf16[4,96,256]{2,1,0:T(8,128)(2,1)}, bf16[4,96,256]{2,1,0:T(8,128)(2,1)}, u32[]{:S(2)}, u32[]{:S(2)}) collective-permute-start(bf16[4,96,256]{2,1,0:T(8,128)(2,1)} %get-tuple-element.142), channel_id=1, source_target_pairs={{0,1},{1,0},{2,3},{3,2},{4,5},{5,4},{6,7},{7,6},{8,9},{9,8},{10,11... | collective-permute-start | bytes 589832 | tf_op jit(solution)/shard_map/ppermute | solution.py:516
  151.9 14.2 %collective-permute-start.27 = (bf16[128,768]{1,0:T(8,128)(2,1)}, bf16[128,768]{1,0:T(8,128)(2,1)}, u32[]{:S(2)}, u32[]{:S(2)}) collective-permute-start(bf16[128,768]{1,0:T(8,128)(2,1)} %get-tuple-element.239), channel_id=1, source_target_pairs={{0,16},{8,24},{16,0},{24,8},{1,17},{9,25},{17,1},{25,9},{2,18},{10... | collective-permute-start | bytes 589832 | tf_op jit(solution)/shard_map/ppermute | solution.py:523
  155.0 11.1 %collective-permute-start.29 = (bf16[192,1024]{1,0:T(8,128)(2,1)S(1)}, bf16[192,1024]{1,0:T(8,128)(2,1)S(1)}, u32[]{:S(2)}, u32[]{:S(2)}) collective-permute-start(bf16[192,1024]{1,0:T(8,128)(2,1)S(1)} %slice_dynamic-update-slice_fusion.refs_4_), channel_id=1, source_target_pairs={{0,1},{1,0},{2,3},{3,2},{4,5},{5,4},{6,7},{7,6},{8,9},{9,8},{10,11... | collective-permute-start | bytes 1179656 | tf_op jit(solution)/shard_map/ppermute | solution.py:516
  156.4 33.0 %collective-permute-start.28 = (bf16[192,1024]{1,0:T(8,128)(2,1)S(1)}, bf16[192,1024]{1,0:T(8,128)(2,1)S(1)}, u32[]{:S(2)}, u32[]{:S(2)}) collective-permute-start(bf16[192,1024]{1,0:T(8,128)(2,1)S(1)} %slice_dynamic-update-slice_fusion.refs_4_), channel_id=1, source_target_pairs={{0,8},{8,0},{16,24},{24,16},{1,9},{9,1},{17,25},{25,17},{2,10},{10... | collective-permute-start | bytes 1179656 | tf_op jit(solution)/shard_map/ppermute | solution.py:519
  166.1 166.5 %all-reduce.3.cloned.1.call-start = ((), (), s32[]{:S(2)}) async-start(), calls=%async_computation.1 | async-start | bytes 2752512 | tf_op jit(solution)/shard_map/psum | solution.py:707
  189.4 14.9 %collective-permute-start.31 = (bf16[192,1024]{1,0:T(8,128)(2,1)S(1)}, bf16[192,1024]{1,0:T(8,128)(2,1)S(1)}, u32[]{:S(2)}, u32[]{:S(2)}) collective-permute-start(bf16[192,1024]{1,0:T(8,128)(2,1)S(1)} %collective-permute-done.28.refs_2_), channel_id=1, source_target_pairs={{0,1},{1,0},{2,3},{3,2},{4,5},{5,4},{6,7},{7,6},{8,9},{9,8},{10,11... | collective-permute-start | bytes 1179656 | tf_op jit(solution)/shard_map/ppermute | solution.py:516
  189.7 14.5 %collective-permute-start.30 = (bf16[192,1024]{1,0:T(8,128)(2,1)S(1)}, bf16[192,1024]{1,0:T(8,128)(2,1)S(1)}, u32[]{:S(2)}, u32[]{:S(2)}) collective-permute-start(bf16[192,1024]{1,0:T(8,128)(2,1)S(1)} %get-tuple-element.151), channel_id=1, source_target_pairs={{0,1},{1,0},{2,3},{3,2},{4,5},{5,4},{6,7},{7,6},{8,9},{9,8},{10,11... | collective-permute-start | bytes 1179656 | tf_op jit(solution)/shard_map/ppermute | solution.py:516
  201.6 34.8 %collective-permute-start.36 = (bf16[2,128,768]{2,1,0:T(8,128)(2,1)S(1)}, bf16[2,128,768]{2,1,0:T(8,128)(2,1)S(1)}, u32[]{:S(2)}, u32[]{:S(2)}) collective-permute-start(bf16[2,128,768]{2,1,0:T(8,128)(2,1)S(1)} %pad_maximum_fusion.10), channel_id=1, source_target_pairs={{0,4},{2,6},{4,0},{6,2},{1,5},{3,7},{5,1},{7,3},{8,12},{10,14},{12... | collective-permute-start | bytes 1179656 | tf_op jit(solution)/shard_map/ppermute | solution.py:526
  202.5 34.5 %collective-permute-start.35 = (bf16[2,128,768]{2,1,0:T(8,128)(2,1)S(1)}, bf16[2,128,768]{2,1,0:T(8,128)(2,1)S(1)}, u32[]{:S(2)}, u32[]{:S(2)}) collective-permute-start(bf16[2,128,768]{2,1,0:T(8,128)(2,1)S(1)} %pad_maximum_fusion.10), channel_id=1, source_target_pairs={{0,2},{2,0},{4,6},{6,4},{1,3},{3,1},{5,7},{7,5},{8,10},{10,8},{12,... | collective-permute-start | bytes 1179656 | tf_op jit(solution)/shard_map/ppermute | solution.py:526
  203.0 33.9 %collective-permute-start.37 = (bf16[2,128,768]{2,1,0:T(8,128)(2,1)S(1)}, bf16[2,128,768]{2,1,0:T(8,128)(2,1)S(1)}, u32[]{:S(2)}, u32[]{:S(2)}) collective-permute-start(bf16[2,128,768]{2,1,0:T(8,128)(2,1)S(1)} %pad_maximum_fusion.10), channel_id=1, source_target_pairs={{0,6},{2,4},{4,2},{6,0},{1,7},{3,5},{5,3},{7,1},{8,14},{10,12},{12... | collective-permute-start | bytes 1179656 | tf_op jit(solution)/shard_map/ppermute | solution.py:526
  215.6 10.2 %collective-permute-start.32 = (bf16[192,1024]{1,0:T(8,128)(2,1)S(1)}, bf16[192,1024]{1,0:T(8,128)(2,1)S(1)}, u32[]{:S(2)}, u32[]{:S(2)}) collective-permute-start(bf16[192,1024]{1,0:T(8,128)(2,1)S(1)} %get-tuple-element.156), channel_id=1, source_target_pairs={{0,1},{1,0},{2,3},{3,2},{4,5},{5,4},{6,7},{7,6},{8,9},{9,8},{10,11... | collective-permute-start | bytes 1179656 | tf_op jit(solution)/shard_map/ppermute | solution.py:516
  225.7 11.3 %collective-permute-start.34 = (bf16[2,192,1024]{2,1,0:T(8,128)(2,1)S(1)}, bf16[2,192,1024]{2,1,0:T(8,128)(2,1)S(1)}, u32[]{:S(2)}, u32[]{:S(2)}) collective-permute-start(bf16[2,192,1024]{2,1,0:T(8,128)(2,1)S(1)} %key_backward.4), channel_id=1, source_target_pairs={{0,1},{1,0},{2,3},{3,2},{4,5},{5,4},{6,7},{7,6},{8,9},{9,8},{10,11... | collective-permute-start | bytes 2359304 | tf_op jit(solution)/shard_map/ppermute | solution.py:516
  225.9 11.1 %collective-permute-start.33 = (bf16[192,1024]{1,0:T(8,128)(2,1)S(1)}, bf16[192,1024]{1,0:T(8,128)(2,1)S(1)}, u32[]{:S(2)}, u32[]{:S(2)}) collective-permute-start(bf16[192,1024]{1,0:T(8,128)(2,1)S(1)} %add_convert_fusion.4), channel_id=1, source_target_pairs={{0,8},{8,0},{16,24},{24,16},{1,9},{9,1},{17,25},{25,17},{2,10},{10... | collective-permute-start | bytes 1179656 | tf_op jit(solution)/shard_map/ppermute | solution.py:519
  236.4 23.9 %collective-permute-start.43 = (bf16[4,3,96,768]{3,2,1,0:T(8,128)(2,1)}, bf16[4,3,96,768]{3,2,1,0:T(8,128)(2,1)}, u32[]{:S(2)}, u32[]{:S(2)}) collective-permute-start(bf16[4,3,96,768]{3,2,1,0:T(8,128)(2,1)} %bitcast.35.refs_4_), channel_id=1, source_target_pairs={{0,1},{1,0},{2,3},{3,2},{4,5},{5,4},{6,7},{7,6},{8,9},{9,8},{10,11... | collective-permute-start | bytes 5308424 | tf_op jit(solution)/shard_map/ppermute | solution.py:516
  238.2 22.1 %collective-permute-start.39 = (bf16[2,192,1024]{2,1,0:T(8,128)(2,1)}, bf16[2,192,1024]{2,1,0:T(8,128)(2,1)}, u32[]{:S(2)}, u32[]{:S(2)}) collective-permute-start(bf16[2,192,1024]{2,1,0:T(8,128)(2,1)} %add_convert_fusion.1), channel_id=1, source_target_pairs={{0,8},{8,0},{16,24},{24,16},{1,9},{9,1},{17,25},{25,17},{2,10},{10... | collective-permute-start | bytes 2359304 | tf_op jit(solution)/shard_map/ppermute | solution.py:519
  249.9 10.4 %collective-permute-start.38 = (bf16[2,192,1024]{2,1,0:T(8,128)(2,1)S(1)}, bf16[2,192,1024]{2,1,0:T(8,128)(2,1)}, u32[]{:S(2)}, u32[]{:S(2)}) collective-permute-start(bf16[2,192,1024]{2,1,0:T(8,128)(2,1)S(1)} %key_backward.7), channel_id=1, source_target_pairs={{0,1},{1,0},{2,3},{3,2},{4,5},{5,4},{6,7},{7,6},{8,9},{9,8},{10,11... | collective-permute-start | bytes 2359304 | tf_op jit(solution)/shard_map/ppermute | solution.py:516
  262.5 9.5 %collective-permute-start.42 = (bf16[3,192,256]{2,1,0:T(8,128)(2,1)S(1)}, bf16[3,192,256]{2,1,0:T(8,128)(2,1)S(1)}, u32[]{:S(2)}, u32[]{:S(2)}) collective-permute-start(bf16[3,192,256]{2,1,0:T(8,128)(2,1)S(1)} %pad_maximum_fusion.15), channel_id=1, source_target_pairs={{0,6},{2,4},{4,2},{6,0},{1,7},{3,5},{5,3},{7,1},{8,14},{10,12},{12... | collective-permute-start | bytes 884744 | tf_op jit(solution)/shard_map/ppermute | solution.py:526
  263.8 15.0 %collective-permute-start.41 = (bf16[3,192,256]{2,1,0:T(8,128)(2,1)S(1)}, bf16[3,192,256]{2,1,0:T(8,128)(2,1)S(1)}, u32[]{:S(2)}, u32[]{:S(2)}) collective-permute-start(bf16[3,192,256]{2,1,0:T(8,128)(2,1)S(1)} %pad_maximum_fusion.14), channel_id=1, source_target_pairs={{0,4},{2,6},{4,0},{6,2},{1,5},{3,7},{5,1},{7,3},{8,12},{10,14},{12... | collective-permute-start | bytes 884744 | tf_op jit(solution)/shard_map/ppermute | solution.py:526
  265.0 13.8 %collective-permute-start.40 = (bf16[3,192,256]{2,1,0:T(8,128)(2,1)S(1)}, bf16[3,192,256]{2,1,0:T(8,128)(2,1)S(1)}, u32[]{:S(2)}, u32[]{:S(2)}) collective-permute-start(bf16[3,192,256]{2,1,0:T(8,128)(2,1)S(1)} %pad_maximum_fusion.13), channel_id=1, source_target_pairs={{0,2},{2,0},{4,6},{6,4},{1,3},{3,1},{5,7},{7,5},{8,10},{10,8},{12,... | collective-permute-start | bytes 884744 | tf_op jit(solution)/shard_map/ppermute | solution.py:526
  266.6 21.2 %collective-permute-start.45 = (bf16[288,768]{1,0:T(8,128)(2,1)S(1)}, bf16[288,768]{1,0:T(8,128)(2,1)S(1)}, u32[]{:S(2)}, u32[]{:S(2)}) collective-permute-start(bf16[288,768]{1,0:T(8,128)(2,1)S(1)} %constant_dynamic-slice_fusion.1), channel_id=1, source_target_pairs={{0,1},{1,0},{2,3},{3,2},{4,5},{5,4},{6,7},{7,6},{8,9},{9,8},{10,11... | collective-permute-start | bytes 1327112 | tf_op jit(solution)/shard_map/ppermute | solution.py:516
  286.0 11.7 %collective-permute-start.44 = (bf16[128,768]{1,0:T(8,128)(2,1)S(1)}, bf16[128,768]{1,0:T(8,128)(2,1)S(1)}, u32[]{:S(2)}, u32[]{:S(2)}) collective-permute-start(bf16[128,768]{1,0:T(8,128)(2,1)S(1)} %get-tuple-element.237), channel_id=1, source_target_pairs={{0,16},{8,24},{16,0},{24,8},{1,17},{9,25},{17,1},{25,9},{2,18},{10... | collective-permute-start | bytes 589832 | tf_op jit(solution)/shard_map/ppermute | solution.py:523
  287.9 9.8 %collective-permute-start.46 = (bf16[144,768]{1,0:T(8,128)(2,1)S(1)}, bf16[144,768]{1,0:T(8,128)(2,1)S(1)}, u32[]{:S(2)}, u32[]{:S(2)}) collective-permute-start(bf16[144,768]{1,0:T(8,128)(2,1)S(1)} %constant_dynamic-slice_fusion), channel_id=1, source_target_pairs={{0,8},{8,0},{16,24},{24,16},{1,9},{9,1},{17,25},{25,17},{2,10},{10... | collective-permute-start | bytes 663560 | tf_op jit(solution)/shard_map/ppermute | solution.py:519
  297.8 34.8 %collective-permute-start.47 = (bf16[2,128,768]{2,1,0:T(8,128)(2,1)S(1)}, bf16[2,128,768]{2,1,0:T(8,128)(2,1)S(1)}, u32[]{:S(2)}, u32[]{:S(2)}) collective-permute-start(bf16[2,128,768]{2,1,0:T(8,128)(2,1)S(1)} %pad_maximum_fusion.11), channel_id=1, source_target_pairs={{0,2},{2,0},{4,6},{6,4},{1,3},{3,1},{5,7},{7,5},{8,10},{10,8},{12,... | collective-permute-start | bytes 1179656 | tf_op jit(solution)/shard_map/ppermute | solution.py:526
  299.2 33.4 %collective-permute-start.48 = (bf16[2,128,768]{2,1,0:T(8,128)(2,1)S(1)}, bf16[2,128,768]{2,1,0:T(8,128)(2,1)}, u32[]{:S(2)}, u32[]{:S(2)}) collective-permute-start(bf16[2,128,768]{2,1,0:T(8,128)(2,1)S(1)} %pad_maximum_fusion.11), channel_id=1, source_target_pairs={{0,4},{2,6},{4,0},{6,2},{1,5},{3,7},{5,1},{7,3},{8,12},{10,14},{12... | collective-permute-start | bytes 1179656 | tf_op jit(solution)/shard_map/ppermute | solution.py:526
  300.8 31.8 %collective-permute-start.49 = (bf16[2,128,768]{2,1,0:T(8,128)(2,1)S(1)}, bf16[2,128,768]{2,1,0:T(8,128)(2,1)}, u32[]{:S(2)}, u32[]{:S(2)}) collective-permute-start(bf16[2,128,768]{2,1,0:T(8,128)(2,1)S(1)} %pad_maximum_fusion.11), channel_id=1, source_target_pairs={{0,6},{2,4},{4,2},{6,0},{1,7},{3,5},{5,3},{7,1},{8,14},{10,12},{12... | collective-permute-start | bytes 1179656 | tf_op jit(solution)/shard_map/ppermute | solution.py:526
  300.8 25.6 %collective-permute-start.50 = (bf16[144,768]{1,0:T(8,128)(2,1)S(1)}, bf16[144,768]{1,0:T(8,128)(2,1)S(1)}, u32[]{:S(2)}, u32[]{:S(2)}) collective-permute-start(bf16[144,768]{1,0:T(8,128)(2,1)S(1)} %fusion.6), channel_id=1, source_target_pairs={{0,16},{8,24},{16,0},{24,8},{1,17},{9,25},{17,1},{25,9},{2,18},{10... | collective-permute-start | bytes 663560 | tf_op jit(solution)/shard_map/ppermute | solution.py:523
  326.5 10.2 %collective-permute-start.51 = (bf16[144,768]{1,0:T(8,128)(2,1)S(1)}, bf16[144,768]{1,0:T(8,128)(2,1)S(1)}, u32[]{:S(2)}, u32[]{:S(2)}) collective-permute-start(bf16[144,768]{1,0:T(8,128)(2,1)S(1)} %add_convert_fusion.7), channel_id=1, source_target_pairs={{0,8},{8,0},{16,24},{24,16},{1,9},{9,1},{17,25},{25,17},{2,10},{10... | collective-permute-start | bytes 663560 | tf_op jit(solution)/shard_map/ppermute | solution.py:519
  332.6 11.0 %collective-permute-start.53 = (bf16[896,768]{1,0:T(8,128)(2,1)}, bf16[896,768]{1,0:T(8,128)(2,1)S(1)}, u32[]{:S(2)}, u32[]{:S(2)}) collective-permute-start(bf16[896,768]{1,0:T(8,128)(2,1)} %all-reduce.3.cloned.1.call-done.near), channel_id=1, source_target_pairs={{0,1},{1,0},{2,3},{3,2},{4,5},{5,4},{6,7},{7,6},{8,9},{9,8},{10,11... | collective-permute-start | bytes 4128776 | tf_op jit(solution)/shard_map/ppermute | solution.py:516
  (63 other events, 422.4 us)
Sparse Core Ops, SparseCore 0:
  32.3 64.0 all-gather.4
  116.2 37.5 all-gather.6
  166.2 72.1 reduce-scatter.3
  260.4 72.1 all-reduce.2

commit v12 on v11

--- a/solution.py
+++ b/solution.py
@@ -512,6 +512,15 @@
     hash_id, d, s = lax.axis_index("hash"), lax.axis_index("head"), lax.axis_index("seq")
     g, r = hash_id // places, hash_id % places
 
+    def in_halves(index, mine, other):
+        first = jnp.where(index == 0, mine, other)
+        second = jnp.where(index == 0, other, mine)
+        return jnp.concatenate([first, second], axis=0)
+
+    def split(x, index):
+        half = x.shape[0] // 2
+        return [lax.dynamic_slice_in_dim(x, at * half, half, 0) for at in (index, 1 - index)]
+
     def over_seq(x):
         return lax.ppermute(x, "seq", [(0, 1), (1, 0)])
 
@@ -704,28 +713,27 @@
         signed, signed_t, bits, head_n, near_o, after(kv_o, dkv_far, grad_q, weight_sum, *layer_moved),
         grad_tables, bf16, 25,
     )
-    weight_sum = lax.psum(weight_sum, "hash")
+    half = weight_sum.shape[0] // 2
+    low_keep, low_send = split(weight_sum[:half], r)
+    low_far = over_place(low_send)
+    high_sum = lax.psum(weight_sum[half:], "hash")
     dkv_far = over_place(dkv_far)
     dkv_o_moved = over_seq(dkv_o)
+    low_keep = add(low_keep, after(low_far, dkv_o))
+    low_send = low_keep.astype(bf16)
+    low_far = [over_group(low_send, k) for k in range(1, groups)]
     dkv = key_backward(
-        signed, signed_t, bits, head_n, near, kv, grad_tables, f32, 25
+        signed, signed_t, bits, head_n, near, after(kv, low_send), grad_tables, f32, 25
     )
 
     dkv_o_moved = after(dkv_o_moved, dkv)
     grad_kv = add(dkv, dkv_o_moved, after(dkv_far, dkv)).astype(bf16)
     grad_qkv = jnp.concatenate([grad_q[None], grad_kv])
     qkv_parts = to_dense(grad_qkv)
+    low_keep = add(low_keep, *[after(x, qkv_parts[1]) for x in low_far]).astype(bf16)
+    low_far = over_place(low_keep)
 
     grad_in = input_grad(core, grad_first, qkv_parts, w_qkv_t, after(w_qkv_far, dkv))
-
-    def in_halves(index, mine, other):
-        first = jnp.where(index == 0, mine, other)
-        second = jnp.where(index == 0, other, mine)
-        return jnp.concatenate([first, second], axis=0)
-
-    def split(x, index):
-        half = x.shape[0] // 2
-        return [lax.dynamic_slice_in_dim(x, at * half, half, 0) for at in (index, 1 - index)]
 
     w_grad = dot(grad_qkv.reshape(3 * head_width, n_tokens), tokens, NN).astype(bf16)
     w_keep, w_send = split(w_grad, s)
@@ -759,7 +767,8 @@
     w_grad = in_halves(r, w_keep, over_place(w_keep))
     w_grad = in_halves(s, w_grad, over_seq(w_grad)).reshape(3, head_width, width)
     grad_w_qkv = w_grad.transpose(0, 2, 1).astype(f32)
-    weight_sum = after(weight_sum, *grad_moved)
+    low_keep = in_halves(r, low_keep, after(low_far, *grad_moved))
+    weight_sum = jnp.concatenate([low_keep, after(high_sum, *grad_moved)])
     weight_far = over_seq(weight_sum)
     grad_w_up, grad_w_down, grad_w_out = weight_results(core, weight_sum, weight_far, head_width)
     at = slice(2 * cut + out_cut, 2 * cut + out_cut + 16)

time: 363 us -> 376 us (1.036)
  starting transfers between devices: 53.3 us -> 69.6 us
  waiting for transfers between devices: 58.3 us -> 45.7 us
  local copies, waits for them, and re-layouts: 37.8 us -> 45 us
    ppermute x4 -> x5, waiting for transfers between devices: 29 us -> 2.62 us  [over_group(): return lax.ppermute(x, 'hash', moves)]
    ppermute x9 -> x11, waiting for transfers between devices: 5.11 us -> 25.6 us  [over_place(): return lax.ppermute(x, 'hash', [(h, h ^ 1) for h in range(hash_count)])]
    ppermute x9 -> x11, starting transfers between devices: 7.73 us -> 16.6 us  [over_place(): return lax.ppermute(x, 'hash', [(h, h ^ 1) for h in range(hash_count)])]
    psum x1, waiting for transfers between devices: 6.02 us -> 0.01 us  [shards(): high_sum = lax.psum(weight_sum[half:], 'hash')]
    ppermute x22, starting transfers between devices: 16.9 us -> 22.2 us  [over_seq(): return lax.ppermute(x, 'seq', [(0, 1), (1, 0)])]
    unnamed x118 -> x126, local copies, waits for them, and re-layouts: 19.1 us -> 22.8 us
    ppermute x4 -> x5, starting transfers between devices: 8.76 us -> 11.2 us  [over_group(): return lax.ppermute(x, 'hash', moves)]
  transfers between devices with their start and end apart: 58 -> 61, of which waited for: 12 -> 11; matrix products, arithmetic and copies ran while one was open for 14% -> 15% of each run, Pallas kernels for 45% -> 43%
where the time goes in v12:
time: 376 us; the launch traced here: 370 us
  Pallas kernels  164 us (44%)
  starting transfers between devices  69.6 us (19%)
  waiting for transfers between devices  45.7 us (12%)
  local copies, waits for them, and re-layouts  45 us (12%)
  other arithmetic  25.9 us (7%)
  between operations  15.5 us (4%)
  matrix products  4.15 us (1%)
    pallas_call x5, Pallas kernels, single(): pl.pallas_call(kernel, in_specs=[pl.BlockSpec(memory_space=pltpu.SMEM)] +...  43.4 us
    pallas_call x3, Pallas kernels, query_backward(): call(partial(query_back_kernel, chunk=4, blocks=blocks, last=last), heads...  43.2 us
    pallas_call x4, Pallas kernels, key_backward(): call(partial(key_back_kernel, chunk=4), heads, micros, 'key_backward', [w...  38 us
    ppermute x11, waiting for transfers between devices, over_place(): return lax.ppermute(x, 'hash', [(h, h ^ 1) for h in range(hash_count)])  25.6 us
    pallas_call x5, Pallas kernels, key_tables(): call(partial(key_kernel, chunk=2, blocks=len(blocks)), heads, 30 if len(b...  23.5 us
    unnamed x126, local copies, waits for them, and re-layouts  22.8 us
    ppermute x22, starting transfers between devices, over_seq(): return lax.ppermute(x, 'seq', [(0, 1), (1, 0)])  22.2 us
    ppermute x11, starting transfers between devices, over_place(): return lax.ppermute(x, 'hash', [(h, h ^ 1) for h in range(hash_count)])  16.6 us
  transfers between devices with their start and end apart: 61, of which 11 were waited for; matrix products, arithmetic and copies ran while one was open for 15% of the time, Pallas kernels for 43%

profile of v12, /device:TPU:1, one launch (start us, length us, event | category | flops | bytes accessed | tf_op | source)
XLA Modules:
  0.0 369.7 jit_solution(4088172890828649257)
XLA Ops:
  7.3 4.5 %constant_dynamic-slice_fusion.8 = (bf16[1,128,1,768]{3,2,1,0:T(2,128)(2,1)S(1)}, bf16[1,128,1,768]{3,2,1,0:T(2,128)(2,1)}, bf16[1,128,1,768]{3,2,1,0:T(2,128)(2...) fusion(bf16[1,512,2,768]{3,2,1,0:T(2,128)(2,1)} %param.11, s32[]{:T(128)S(6)} %select_n.240, ...), kind=kLoop, calls=%fused_computation.128 | loop fusion | bytes 1966104 | tf_op jit(solution)/shard_map/jit(dynamic_index_in_dim)/dynamic_slice | solution.py:538
  12.6 3.1 collective-permute-start
  16.3 2.5 collective-permute-start.1
  20.5 2.4 copy.54
  24.7 1.9 dynamic-slice_bitcast_fusion
  37.1 1.9 slice.124
  40.7 5.3 %key_tables.5.refs_4_ = f32[3,2048,64]{2,1,0:T(8,128)S(1)} custom-call(bf16[64,64]{1,0:T(8,128)(2,1)S(1)} %bitcast.129, bf16[576,512]{1,0:T(8,128)(2,1)} %bitcast.14.refs_0_.refs_2_.ka.va, bf16[576,512]{1,0:T(8,128)(2,1)} %collective-permute-done.2.refs_1_.refs_3_.refs_0_.refs_2_.ka.va, bf16[576,512]{1,0:T(8,128)(2,1)} %bitcast.14.refs_0_.refs_2_.ka.va, ...), custom_call_target="tpu_custom_call" | custom-call | flops 1100000000 | bytes 1048576 | tf_op jit(solution)/shard_map/key_tables/pallas_call | solution.py:192
  46.1 2.1 pad_maximum_fusion.8
  53.4 5.8 %key_tables.6.refs_4_ = f32[3,2048,64]{2,1,0:T(8,128)S(1)} custom-call(bf16[64,64]{1,0:T(8,128)(2,1)S(1)} %bitcast.130, bf16[576,512]{1,0:T(8,128)(2,1)} %collective-permute-done.9.refs_0_.refs_2_.ka.va, bf16[576,512]{1,0:T(8,128)(2,1)S(1)} %collective-permute-done.10.refs_1_.refs_3_.refs_0_.ka.va, ...), custom_call_target="tpu_custom_call" | custom-call | flops 32999999488 | bytes 1048576 | tf_op jit(solution)/shard_map/key_tables/pallas_call | solution.py:192
  60.9 5.6 %key_tables.7.refs_2_ = f32[3,2048,64]{2,1,0:T(8,128)S(1)} custom-call(bf16[64,64]{1,0:T(8,128)(2,1)S(1)} %bitcast.131, bf16[384,512]{1,0:T(8,128)(2,1)S(1)} %bitcast.125, bf16[384,512]{1,0:T(8,128)(2,1)S(1)} %collective-permute-done.8.refs_1_.refs_3_.kb.vb, bf16[384,512]{1,0:T(8,128)(2,1)S(1)} %bitcast.126, ...), custom_call_target="tpu_custom_call" | custom-call | flops 32999999488 | bytes 1048576 | tf_op jit(solution)/shard_map/key_tables/pallas_call | solution.py:192
  71.5 4.2 %key_tables.8.refs_2_ = f32[3,2048,64]{2,1,0:T(8,128)S(1)} custom-call(bf16[64,64]{1,0:T(8,128)(2,1)S(1)} %bitcast.132, bf16[384,512]{1,0:T(8,128)(2,1)S(1)} %collective-permute-done.7.refs_0_.refs_1_.kb.vb, bf16[384,512]{1,0:T(8,128)(2,1)S(1)} %collective-permute-done.7.refs_0_.refs_1_.kb.vb, f32[3,2048,64]{2,1,0:T(8,128)} %copy-done.2), custom_call_target="tpu_custom_call" | custom-call | flops 1100000000 | bytes 1048576 | tf_op jit(solution)/shard_map/key_tables/pallas_call | solution.py:192
  76.4 2.6 key_tables.9.tables
  79.0 3.3 query_estimates.4
  82.9 4.1 %query_estimates.5 = bf16[192,1024]{1,0:T(8,128)(2,1)S(1)} custom-call(bf16[64,64]{1,0:T(8,128)(2,1)S(1)} %bitcast.135, bf16[3,2048,64]{2,1,0:T(8,128)(2,1)S(1)} %key_tables.9.tables, bf16[576,512]{1,0:T(8,128)(2,1)} %collective-permute-done.9.refs_0_.refs_2_.ka.va, bf16[192,512]{1,0:T(8,128)(2,1)S(1)} %collective-permute-done.6.refs_1_), custom_call_target="tpu_custom_call" | custom-call | flops 1100000000 | bytes 1048576 | tf_op jit(solution)/shard_map/query_estimates/pallas_call | solution.py:205
  87.2 4.2 %query_estimates.6 = bf16[192,1024]{1,0:T(8,128)(2,1)S(1)} custom-call(bf16[64,64]{1,0:T(8,128)(2,1)S(1)} %bitcast.136, bf16[3,2048,64]{2,1,0:T(8,128)(2,1)S(1)} %key_tables.9.tables, bf16[576,512]{1,0:T(8,128)(2,1)} %collective-permute-done.2.refs_1_.refs_3_.refs_0_.refs_2_.ka.va, bf16[192,512]{1,0:T(8,128)(2,1)S(1)} %collective-permute-done.12.refs_1_.refs_3_), custom_call_target="tpu_custom_call" | custom-call | flops 1100000000 | bytes 1048576 | tf_op jit(solution)/shard_map/query_estimates/pallas_call | solution.py:205
  92.0 4.3 %all-gather.5.cloned.1.call-done = bf16[3456,768]{1,0:T(8,128)(2,1)} async-done(((bf16[864,768]{1,0:T(8,128)(2,1)}), bf16[3456,768]{1,0:T(8,128)(2,1)}) %all-gather.5.cloned.1.call-update) | async-done | bytes 5308432 | tf_op jit(solution)/shard_map/all_gather | solution.py:573
  100.9 4.2 %query_estimates.7 = f32[192,1024]{1,0:T(8,128)S(1)} custom-call(bf16[64,64]{1,0:T(8,128)(2,1)S(1)} %bitcast.138, bf16[3,2048,64]{2,1,0:T(8,128)(2,1)S(1)} %key_tables.9.tables, bf16[576,512]{1,0:T(8,128)(2,1)} %bitcast.14.refs_0_.refs_2_.ka.va, bf16[192,512]{1,0:T(8,128)(2,1)S(1)} %convolution_convert_fusion.1.refs_1_), custom_call_target="tpu_custom_call" | custom-call | flops 1100000000 | bytes 1048576 | tf_op jit(solution)/shard_map/query_estimates/pallas_call | solution.py:205
  105.1 2.2 collective-permute-done.16
  116.4 12.7 %dense.1 = (bf16[256,768]{1,0:T(8,128)(2,1)}, f32[256,768]{1,0:T(8,128)}, f32[256,768]{1,0:T(8,128)}, f32[8,256,384]{2,1,0:T(8,128)}, bf16[8,256,384]{2,1,0:T(8,...) custom-call(s32[2]{0:T(128)} %pad_add_fusion.core, ...), custom_call_target="tpu_custom_call" | custom-call | flops 15399999488 | bytes 1048576 | tf_op jit(solution)/shard_map/dense/pallas_call | solution.py:402
  129.1 12.6 %dense_back.1 = (f32[256,768]{1,0:T(8,128)}, bf16[6,256,384]{2,1,0:T(8,128)(2,1)}, bf16[6,256,384]{2,1,0:T(8,128)(2,1)}, bf16[192,256]{1,0:T(8,128)(2,1)}, bf16[...) custom-call(s32[2]{0:T(128)} %pad_add_fusion.core, ...), custom_call_target="tpu_custom_call" | custom-call | flops 8800000000 | bytes 1048576 | tf_op jit(solution)/shard_map/dense_back/pallas_call | solution.py:402
  144.4 2.8 collective-permute-start.25
  148.7 2.8 collective-permute-start.26
  151.6 2.1 collective-permute-start.27
  157.3 8.2 %weight_grads.1 = bf16[4,896,768]{2,1,0:T(8,128)(2,1)} custom-call(s32[2]{0:T(128)} %pad_add_fusion.core, f32[8,768]{1,0:T(8,128)} %get-tuple-element.140.small_a, f32[8,768]{1,0:T(8,128)} %get-tuple-element.141.small_b, bf16[8,256,384]{2,1,0:T(8,128)(2,1)} %get-tuple-element.142.refs_0_, bf16[8,256,384]{2,1,0:T(8,128)(2,1)} %collective-permute-done.24.refs_1_, ...), custom_call_target="tpu_custom_call" | custom-call | flops 7699999744 | bytes 1048576 | tf_op jit(solution)/shard_map/weight_grads/pallas_call | solution.py:402
  168.8 20.2 %query_backward.3 = (f32[3,2048,64]{2,1,0:T(8,128)}, f32[192,1024]{1,0:T(8,128)S(1)}, bf16[192,1024]{1,0:T(8,128)(2,1)S(1)}) custom-call(bf16[64,64]{1,0:T(8,128)(2,1)S(1)} %bitcast.139, bf16[64,128]{1,0:T(8,128)(2,1)S(1)} %pad_maximum_fusion.21.planes_t, bf16[80,2048]{1,0:T(8,128)(2,1)S(1)} %copy-done.16, bf16[3,2048,64]{2,1,0:T(8,128)(2,1)S(1)} %key_tables.9.tables, ...), custom_call_target="tpu_custom_call" | custom-call | flops 54999998464 | bytes 1048576 | tf_op jit(solution)/shard_map/query_backward/pallas_call | solution.py:229
  189.5 11.7 %query_backward.4 = (f32[3,2048,64]{2,1,0:T(8,128)}, f32[192,1024]{1,0:T(8,128)S(1)}) custom-call(bf16[64,64]{1,0:T(8,128)(2,1)S(1)} %bitcast.140, bf16[64,128]{1,0:T(8,128)(2,1)S(1)} %pad_maximum_fusion.21.planes_t, bf16[80,2048]{1,0:T(8,128)(2,1)S(1)} %copy-done.16, bf16[3,2048,64]{2,1,0:T(8,128)(2,1)S(1)} %key_tables.9.tables, ...), custom_call_target="tpu_custom_call" | custom-call | flops 27499999232 | bytes 1048576 | tf_op jit(solution)/shard_map/query_backward/pallas_call | solution.py:229
  204.1 11.2 %query_backward.5 = (bf16[3,2048,64]{2,1,0:T(8,128)(2,1)S(1)}, bf16[192,1024]{1,0:T(8,128)(2,1)S(1)}) custom-call(bf16[64,64]{1,0:T(8,128)(2,1)S(1)} %bitcast.141, bf16[64,128]{1,0:T(8,128)(2,1)S(1)} %pad_maximum_fusion.21.planes_t, bf16[80,2048]{1,0:T(8,128)(2,1)S(1)} %copy-done.16, bf16[3,2048,64]{2,1,0:T(8,128)(2,1)S(1)} %key_tables.9.tables, ...), custom_call_target="tpu_custom_call" | custom-call | flops 27499999232 | bytes 1048576 | tf_op jit(solution)/shard_map/query_backward/pallas_call | solution.py:229
  216.6 8.8 %key_backward.4 = bf16[2,192,1024]{2,1,0:T(8,128)(2,1)S(1)} custom-call(bf16[64,64]{1,0:T(8,128)(2,1)S(1)} %bitcast.142, bf16[64,128]{1,0:T(8,128)(2,1)S(1)} %pad_maximum_fusion.21.planes_t, bf16[80,2048]{1,0:T(8,128)(2,1)S(1)} %copy-done.17, bf16[576,512]{1,0:T(8,128)(2,1)S(1)} %copy-done.11, bf16[384,512]{1,0:T(8,128)(2,1)S(1)} %copy-done.7, ...), custom_call_target="tpu_custom_call" | custom-call | flops 27499999232 | bytes 1048576 | tf_op jit(solution)/shard_map/key_backward/pallas_call | solution.py:243
  226.4 9.7 %key_backward.5 = bf16[2,192,1024]{2,1,0:T(8,128)(2,1)S(1)} custom-call(bf16[64,64]{1,0:T(8,128)(2,1)S(1)} %bitcast.143, bf16[64,128]{1,0:T(8,128)(2,1)S(1)} %pad_maximum_fusion.21.planes_t, bf16[80,2048]{1,0:T(8,128)(2,1)S(1)} %copy-done.17, bf16[576,512]{1,0:T(8,128)(2,1)} %collective-permute-done.9.refs_0_.refs_2_.ka.va, bf16[384,512]{1,0:T(8,128)(2,1)S(1)} %copy-done.5, ...), custom_call_target="tpu_custom_call" | custom-call | flops 27499999232 | bytes 1048576 | tf_op jit(solution)/shard_map/key_backward/pallas_call | solution.py:243
  239.0 2.4 fusion.26
  242.7 9.6 %key_backward.6 = bf16[2,192,1024]{2,1,0:T(8,128)(2,1)S(1)} custom-call(bf16[64,64]{1,0:T(8,128)(2,1)S(1)} %bitcast.144, bf16[64,128]{1,0:T(8,128)(2,1)S(1)} %pad_maximum_fusion.21.planes_t, bf16[80,2048]{1,0:T(8,128)(2,1)S(1)} %copy-done.17, bf16[576,512]{1,0:T(8,128)(2,1)} %collective-permute-done.2.refs_1_.refs_3_.refs_0_.refs_2_.ka.va, ...), custom_call_target="tpu_custom_call" | custom-call | flops 27499999232 | bytes 1048576 | tf_op jit(solution)/shard_map/key_backward/pallas_call | solution.py:243
  253.6 17.2 %collective-permute-done.34 = bf16[224,768]{1,0:T(8,128)(2,1)S(1)} collective-permute-done((bf16[224,768]{1,0:T(8,128)(2,1)S(1)}, bf16[224,768]{1,0:T(8,128)(2,1)S(1)}, u32[]{:S(2)}, u32[]{:S(2)}) %collective-permute-start.34) | collective-permute-done | bytes 344096 | tf_op jit(solution)/shard_map/ppermute | solution.py:528
  271.9 3.3 collective-permute-start.54
  276.6 10.0 %key_backward.7 = f32[2,192,1024]{2,1,0:T(8,128)S(1)} custom-call(bf16[64,64]{1,0:T(8,128)(2,1)S(1)} %bitcast.145, bf16[64,128]{1,0:T(8,128)(2,1)S(1)} %pad_maximum_fusion.21.planes_t, bf16[80,2048]{1,0:T(8,128)(2,1)S(1)} %copy-done.17, bf16[576,512]{1,0:T(8,128)(2,1)} %bitcast.14.refs_0_.refs_2_.ka.va, bf16[384,512]{1,0:T(8,128)(2,1)S(1)} %bitcast.127, ...), custom_call_target="tpu_custom_call" | custom-call | flops 27499999232 | bytes 1048576 | tf_op jit(solution)/shard_map/key_backward/pallas_call | solution.py:243
  288.8 1.9 collective-permute-start.42
  292.8 4.1 %collective-permute-start.46 = (bf16[288,768]{1,0:T(8,128)(2,1)S(1)}, bf16[288,768]{1,0:T(8,128)(2,1)S(1)}, u32[]{:S(2)}, u32[]{:S(2)}) collective-permute-start(bf16[288,768]{1,0:T(8,128)(2,1)S(1)} %constant_dynamic-slice_fusion.1), channel_id=1, source_target_pairs={{0,1},{1,0},{2,3},{3,2},{4,5},{5,4},{6,7},{7,6},{8,9},{9,8},{10,11... | collective-permute-start | bytes 1327112 | tf_op jit(solution)/shard_map/ppermute | solution.py:525
  297.6 6.4 %collective-permute-done.42.refs_2_ = bf16[3,192,256]{2,1,0:T(8,128)(2,1)S(1)} collective-permute-done((bf16[3,192,256]{2,1,0:T(8,128)(2,1)S(1)}, bf16[3,192,256]{2,1,0:T(8,128)(2,1)S(1)}, u32[]{:S(2)}, u32[]{:S(2)}) %collective-permute-start.42) | collective-permute-done | bytes 294944 | tf_op jit(solution)/shard_map/ppermute | solution.py:535
  304.9 5.2 %input_grad.1 = bf16[256,768]{1,0:T(8,128)(2,1)} custom-call(s32[2]{0:T(128)} %pad_add_fusion.core, f32[256,768]{1,0:T(8,128)} %get-tuple-element.165.grad_first, bf16[3,192,256]{2,1,0:T(8,128)(2,1)} %pad_maximum_fusion.13.refs_0_, bf16[3,192,256]{2,1,0:T(8,128)(2,1)} %copy-done.52, bf16[3,192,256]{2,1,0:T(8,128)(2,1)} %copy-done.51, ...), custom_call_target="tpu_custom_call" | custom-call | flops 44000002048 | bytes 1048576 | tf_op jit(solution)/shard_map/input_grad/pallas_call | solution.py:402
  311.5 3.2 collective-permute-start.47
  314.9 2.6 collective-permute-done.45
  317.6 6.1 %collective-permute-done.47 = bf16[144,768]{1,0:T(8,128)(2,1)S(1)} collective-permute-done((bf16[144,768]{1,0:T(8,128)(2,1)S(1)}, bf16[144,768]{1,0:T(8,128)(2,1)S(1)}, u32[]{:S(2)}, u32[]{:S(2)}) %collective-permute-start.47) | collective-permute-done | bytes 221216 | tf_op jit(solution)/shard_map/ppermute | solution.py:528
  326.5 2.6 collective-permute-start.51
  329.9 2.8 copy.56
  332.8 6.3 %collective-permute-start.52 = (bf16[144,768]{1,0:T(8,128)(2,1)S(1)}, bf16[144,768]{1,0:T(8,128)(2,1)}, u32[]{:S(2)}, u32[]{:S(2)}) collective-permute-start(bf16[144,768]{1,0:T(8,128)(2,1)S(1)} %add_convert_fusion.8), channel_id=1, source_target_pairs={{0,8},{8,0},{16,24},{24,16},{1,9},{9,1},{17,25},{25,17},{2,10},{10... | collective-permute-start | bytes 663560 | tf_op jit(solution)/shard_map/ppermute | solution.py:528
  340.5 2.5 collective-permute-done.50
  344.3 2.3 collective-permute-start.56
  350.2 4.1 %copy.57 = f32[1,512,2,768]{3,2,1,0:T(2,128)} copy(f32[1,512,2,768]{3,1,2,0:T(8,128)S(1)} %maximum_convert_fusion) | data formatting | bytes 6291456
  357.9 4.7 %weight_results.1 = (f32[768,768]{1,0:T(8,128)}, f32[768,768]{1,0:T(8,128)}, f32[192,768]{1,0:T(8,128)}) custom-call(s32[2]{0:T(128)} %pad_add_fusion.core, bf16[896,768]{1,0:T(8,128)(2,1)} %copy-done.33, bf16[896,768]{1,0:T(8,128)(2,1)} %copy-done.49), custom_call_target="tpu_custom_call" | custom-call | flops 3300000000 | bytes 1048576 | tf_op jit(solution)/shard_map/weight_results/pallas_call | solution.py:402
  (307 shorter events, 89.9 us)
Async XLA Ops:
  7.2 89.1 %all-gather.5.cloned.1.call-start = ((), (), s32[]{:S(2)}) async-start(), calls=%async_computation.2 | async-start | bytes 6635520 | tf_op jit(solution)/shard_map/all_gather | solution.py:573
  12.6 16.4 %collective-permute-start = (bf16[128,768]{1,0:T(8,128)(2,1)}, bf16[128,768]{1,0:T(8,128)(2,1)}, u32[]{:S(2)}, u32[]{:S(2)}) collective-permute-start(bf16[128,768]{1,0:T(8,128)(2,1)} %bitcast.121), channel_id=1, source_target_pairs={{0,16},{8,24},{16,0},{24,8},{1,17},{9,25},{17,1},{25,9},{2,18},{10... | collective-permute-start | bytes 589832 | tf_op jit(solution)/shard_map/ppermute | solution.py:532
  16.3 19.9 %collective-permute-start.1 = (bf16[8,8,64]{2,0,1:T(8,128)(2,1)}, bf16[8,8,64]{2,0,1:T(8,128)(2,1)S(1)}, u32[]{:S(2)}, u32[]{:S(2)}) collective-permute-start(bf16[8,8,64]{2,0,1:T(8,128)(2,1)} %fusion.18), channel_id=1, source_target_pairs={{0,0},{8,1},{16,8},{24,9},{1,16},{9,17},{17,24},{25,25},{2,2},{10,... | collective-permute-start | bytes 24584 | tf_op jit(solution)/shard_map/ppermute | solution.py:557
  30.5 10.2 %collective-permute-start.2 = (bf16[576,512]{1,0:T(8,128)(2,1)}, bf16[576,512]{1,0:T(8,128)(2,1)}, u32[]{:S(2)}, u32[]{:S(2)}) collective-permute-start(bf16[576,512]{1,0:T(8,128)(2,1)} %bitcast.14.refs_0_.refs_2_.ka.va), channel_id=1, source_target_pairs={{0,1},{1,0},{2,3},{3,2},{4,5},{5,4},{6,7},{7,6},{8,9},{9,8},{10,11... | collective-permute-start | bytes 1769480 | tf_op jit(solution)/shard_map/ppermute | solution.py:525
  32.1 123.9 %all-gather.7.cloned.1.call-start = ((), (), s32[]{:S(2)}) async-start(), calls=%async_computation.3 | async-start | bytes 2211840 | tf_op jit(solution)/shard_map/all_gather | solution.py:638
  32.4 18.6 %collective-permute-start.9 = (bf16[576,512]{1,0:T(8,128)(2,1)}, bf16[576,512]{1,0:T(8,128)(2,1)}, u32[]{:S(2)}, u32[]{:S(2)}) collective-permute-start(bf16[576,512]{1,0:T(8,128)(2,1)} %bitcast.14.refs_0_.refs_2_.ka.va), channel_id=1, source_target_pairs={{0,8},{8,0},{16,24},{24,16},{1,9},{9,1},{17,25},{25,17},{2,10},{10... | collective-permute-start | bytes 1769480 | tf_op jit(solution)/shard_map/ppermute | solution.py:528
  33.8 12.2 %collective-permute-start.3 = (bf16[1,128,768]{2,1,0:T(8,128)(2,1)}, bf16[1,128,768]{2,1,0:T(8,128)(2,1)S(1)}, u32[]{:S(2)}, u32[]{:S(2)}) collective-permute-start(bf16[1,128,768]{2,1,0:T(8,128)(2,1)} %bitcast.20), channel_id=1, source_target_pairs={{0,2},{2,0},{4,6},{6,4},{1,3},{3,1},{5,7},{7,5},{8,10},{10,8},{12,... | collective-permute-start | bytes 589832 | tf_op jit(solution)/shard_map/ppermute | solution.py:535
  35.0 11.0 %collective-permute-start.4 = (bf16[1,128,768]{2,1,0:T(8,128)(2,1)}, bf16[1,128,768]{2,1,0:T(8,128)(2,1)}, u32[]{:S(2)}, u32[]{:S(2)}) collective-permute-start(bf16[1,128,768]{2,1,0:T(8,128)(2,1)} %bitcast.20), channel_id=1, source_target_pairs={{0,4},{2,6},{4,0},{6,2},{1,5},{3,7},{5,1},{7,3},{8,12},{10,14},{12... | collective-permute-start | bytes 589832 | tf_op jit(solution)/shard_map/ppermute | solution.py:535
  36.2 9.8 %collective-permute-start.5 = (bf16[1,128,768]{2,1,0:T(8,128)(2,1)}, bf16[1,128,768]{2,1,0:T(8,128)(2,1)}, u32[]{:S(2)}, u32[]{:S(2)}) collective-permute-start(bf16[1,128,768]{2,1,0:T(8,128)(2,1)} %bitcast.20), channel_id=1, source_target_pairs={{0,6},{2,4},{4,2},{6,0},{1,7},{3,5},{5,3},{7,1},{8,14},{10,12},{12... | collective-permute-start | bytes 589832 | tf_op jit(solution)/shard_map/ppermute | solution.py:535
  49.1 11.8 %collective-permute-start.8 = (bf16[384,512]{1,0:T(8,128)(2,1)S(1)}, bf16[384,512]{1,0:T(8,128)(2,1)S(1)}, u32[]{:S(2)}, u32[]{:S(2)}) collective-permute-start(bf16[384,512]{1,0:T(8,128)(2,1)S(1)} %bitcast.123), channel_id=1, source_target_pairs={{0,1},{1,0},{2,3},{3,2},{4,5},{5,4},{6,7},{7,6},{8,9},{9,8},{10,11... | collective-permute-start | bytes 1179656 | tf_op jit(solution)/shard_map/ppermute | solution.py:525
  51.0 17.2 %collective-permute-start.7 = (bf16[384,512]{1,0:T(8,128)(2,1)S(1)}, bf16[384,512]{1,0:T(8,128)(2,1)S(1)}, u32[]{:S(2)}, u32[]{:S(2)}) collective-permute-start(bf16[384,512]{1,0:T(8,128)(2,1)S(1)} %bitcast.124), channel_id=1, source_target_pairs={{0,8},{8,0},{16,24},{24,16},{1,9},{9,1},{17,25},{25,17},{2,10},{10... | collective-permute-start | bytes 1179656 | tf_op jit(solution)/shard_map/ppermute | solution.py:528
  68.2 8.2 %collective-permute-start.11 = (bf16[384,512]{1,0:T(8,128)(2,1)S(1)}, bf16[384,512]{1,0:T(8,128)(2,1)S(1)}, u32[]{:S(2)}, u32[]{:S(2)}) collective-permute-start(bf16[384,512]{1,0:T(8,128)(2,1)S(1)} %collective-permute-done.7.refs_0_.refs_1_.kb.vb), channel_id=1, source_target_pairs={{0,1},{1,0},{2,3},{3,2},{4,5},{5,4},{6,7},{7,6},{8,9},{9,8},{10,11... | collective-permute-start | bytes 1179656 | tf_op jit(solution)/shard_map/ppermute | solution.py:525
  96.3 19.9 %collective-permute-start.20 = (bf16[4,864,768]{2,1,0:T(8,128)(2,1)}, bf16[4,864,768]{2,1,0:T(8,128)(2,1)}, u32[]{:S(2)}, u32[]{:S(2)}) collective-permute-start(bf16[4,864,768]{2,1,0:T(8,128)(2,1)} %bitcast.173), channel_id=1, source_target_pairs={{0,1},{1,0},{2,3},{3,2},{4,5},{5,4},{6,7},{7,6},{8,9},{9,8},{10,11... | collective-permute-start | bytes 15925256 | tf_op jit(solution)/shard_map/ppermute | solution.py:525
  97.0 8.0 %collective-permute-start.15 = (bf16[192,1024]{1,0:T(8,128)(2,1)S(1)}, bf16[192,1024]{1,0:T(8,128)(2,1)S(1)}, u32[]{:S(2)}, u32[]{:S(2)}) collective-permute-start(bf16[192,1024]{1,0:T(8,128)(2,1)S(1)} %query_estimates.6), channel_id=1, source_target_pairs={{0,1},{1,0},{2,3},{3,2},{4,5},{5,4},{6,7},{7,6},{8,9},{9,8},{10,11... | collective-permute-start | bytes 1179656 | tf_op jit(solution)/shard_map/ppermute | solution.py:525
  97.0 10.3 %collective-permute-start.16 = (bf16[192,1024]{1,0:T(8,128)(2,1)S(1)}, bf16[192,1024]{1,0:T(8,128)(2,1)}, u32[]{:S(2)}, u32[]{:S(2)}) collective-permute-start(bf16[192,1024]{1,0:T(8,128)(2,1)S(1)} %add_convert_fusion.6), channel_id=1, source_target_pairs={{0,8},{8,0},{16,24},{24,16},{1,9},{9,1},{17,25},{25,17},{2,10},{10... | collective-permute-start | bytes 1179656 | tf_op jit(solution)/shard_map/ppermute | solution.py:528
  115.8 123.2 %reduce-scatter.4.cloned.1.call-start = ((), (), s32[]{:S(2)}) async-start(), calls=%async_computation.4 | async-start | bytes 6881280
  142.0 9.6 %collective-permute-start.22 = (bf16[192,256]{1,0:T(8,128)(2,1)}, bf16[192,256]{1,0:T(8,128)(2,1)S(1)}, u32[]{:S(2)}, u32[]{:S(2)}) collective-permute-start(bf16[192,256]{1,0:T(8,128)(2,1)} %get-tuple-element.134), channel_id=1, source_target_pairs={{0,4},{2,6},{4,0},{6,2},{1,5},{3,7},{5,1},{7,3},{8,12},{10,14},{12... | collective-permute-start | bytes 294920 | tf_op jit(solution)/shard_map/ppermute | solution.py:535
  143.2 10.5 %collective-permute-start.23 = (bf16[192,256]{1,0:T(8,128)(2,1)}, bf16[192,256]{1,0:T(8,128)(2,1)S(1)}, u32[]{:S(2)}, u32[]{:S(2)}) collective-permute-start(bf16[192,256]{1,0:T(8,128)(2,1)} %get-tuple-element.135), channel_id=1, source_target_pairs={{0,6},{2,4},{4,2},{6,0},{1,7},{3,5},{5,3},{7,1},{8,14},{10,12},{12... | collective-permute-start | bytes 294920 | tf_op jit(solution)/shard_map/ppermute | solution.py:535
  144.4 13.0 %collective-permute-start.25 = (bf16[6,256,384]{2,1,0:T(8,128)(2,1)}, bf16[6,256,384]{2,1,0:T(8,128)(2,1)}, u32[]{:S(2)}, u32[]{:S(2)}) collective-permute-start(bf16[6,256,384]{2,1,0:T(8,128)(2,1)} %get-tuple-element.145), channel_id=1, source_target_pairs={{0,1},{1,0},{2,3},{3,2},{4,5},{5,4},{6,7},{7,6},{8,9},{9,8},{10,11... | collective-permute-start | bytes 3538952 | tf_op jit(solution)/shard_map/ppermute | solution.py:525
  147.1 10.2 %collective-permute-start.24 = (bf16[8,256,384]{2,1,0:T(8,128)(2,1)}, bf16[8,256,384]{2,1,0:T(8,128)(2,1)}, u32[]{:S(2)}, u32[]{:S(2)}) collective-permute-start(bf16[8,256,384]{2,1,0:T(8,128)(2,1)} %get-tuple-element.143), channel_id=1, source_target_pairs={{0,1},{1,0},{2,3},{3,2},{4,5},{5,4},{6,7},{7,6},{8,9},{9,8},{10,11... | collective-permute-start | bytes 4718600 | tf_op jit(solution)/shard_map/ppermute | solution.py:525
  151.6 14.2 %collective-permute-start.27 = (bf16[128,768]{1,0:T(8,128)(2,1)}, bf16[128,768]{1,0:T(8,128)(2,1)}, u32[]{:S(2)}, u32[]{:S(2)}) collective-permute-start(bf16[128,768]{1,0:T(8,128)(2,1)} %get-tuple-element.251), channel_id=1, source_target_pairs={{0,16},{8,24},{16,0},{24,8},{1,17},{9,25},{17,1},{25,9},{2,18},{10... | collective-permute-start | bytes 589832 | tf_op jit(solution)/shard_map/ppermute | solution.py:532
  154.6 11.1 %collective-permute-start.29 = (bf16[192,1024]{1,0:T(8,128)(2,1)S(1)}, bf16[192,1024]{1,0:T(8,128)(2,1)S(1)}, u32[]{:S(2)}, u32[]{:S(2)}) collective-permute-start(bf16[192,1024]{1,0:T(8,128)(2,1)S(1)} %slice_dynamic-update-slice_fusion.refs_4_), channel_id=1, source_target_pairs={{0,1},{1,0},{2,3},{3,2},{4,5},{5,4},{6,7},{7,6},{8,9},{9,8},{10,11... | collective-permute-start | bytes 1179656 | tf_op jit(solution)/shard_map/ppermute | solution.py:525
  156.1 33.0 %collective-permute-start.28 = (bf16[192,1024]{1,0:T(8,128)(2,1)S(1)}, bf16[192,1024]{1,0:T(8,128)(2,1)S(1)}, u32[]{:S(2)}, u32[]{:S(2)}) collective-permute-start(bf16[192,1024]{1,0:T(8,128)(2,1)S(1)} %slice_dynamic-update-slice_fusion.refs_4_), channel_id=1, source_target_pairs={{0,8},{8,0},{16,24},{24,16},{1,9},{9,1},{17,25},{25,17},{2,10},{10... | collective-permute-start | bytes 1179656 | tf_op jit(solution)/shard_map/ppermute | solution.py:528
  165.7 177.3 %all-reduce.3.cloned.1.call-start = ((), (), s32[]{:S(2)}) async-start(), calls=%async_computation.1 | async-start | bytes 1376256 | tf_op jit(solution)/shard_map/psum | solution.py:719
  189.0 14.9 %collective-permute-start.31 = (bf16[192,1024]{1,0:T(8,128)(2,1)S(1)}, bf16[192,1024]{1,0:T(8,128)(2,1)S(1)}, u32[]{:S(2)}, u32[]{:S(2)}) collective-permute-start(bf16[192,1024]{1,0:T(8,128)(2,1)S(1)} %collective-permute-done.28.refs_2_), channel_id=1, source_target_pairs={{0,1},{1,0},{2,3},{3,2},{4,5},{5,4},{6,7},{7,6},{8,9},{9,8},{10,11... | collective-permute-start | bytes 1179656 | tf_op jit(solution)/shard_map/ppermute | solution.py:525
  189.4 14.6 %collective-permute-start.30 = (bf16[192,1024]{1,0:T(8,128)(2,1)S(1)}, bf16[192,1024]{1,0:T(8,128)(2,1)S(1)}, u32[]{:S(2)}, u32[]{:S(2)}) collective-permute-start(bf16[192,1024]{1,0:T(8,128)(2,1)S(1)} %get-tuple-element.155), channel_id=1, source_target_pairs={{0,1},{1,0},{2,3},{3,2},{4,5},{5,4},{6,7},{7,6},{8,9},{9,8},{10,11... | collective-permute-start | bytes 1179656 | tf_op jit(solution)/shard_map/ppermute | solution.py:525
  201.3 34.8 %collective-permute-start.37 = (bf16[2,128,768]{2,1,0:T(8,128)(2,1)S(1)}, bf16[2,128,768]{2,1,0:T(8,128)(2,1)S(1)}, u32[]{:S(2)}, u32[]{:S(2)}) collective-permute-start(bf16[2,128,768]{2,1,0:T(8,128)(2,1)S(1)} %pad_maximum_fusion.11), channel_id=1, source_target_pairs={{0,4},{2,6},{4,0},{6,2},{1,5},{3,7},{5,1},{7,3},{8,12},{10,14},{12... | collective-permute-start | bytes 1179656 | tf_op jit(solution)/shard_map/ppermute | solution.py:535
  202.2 34.5 %collective-permute-start.36 = (bf16[2,128,768]{2,1,0:T(8,128)(2,1)S(1)}, bf16[2,128,768]{2,1,0:T(8,128)(2,1)S(1)}, u32[]{:S(2)}, u32[]{:S(2)}) collective-permute-start(bf16[2,128,768]{2,1,0:T(8,128)(2,1)S(1)} %pad_maximum_fusion.11), channel_id=1, source_target_pairs={{0,2},{2,0},{4,6},{6,4},{1,3},{3,1},{5,7},{7,5},{8,10},{10,8},{12,... | collective-permute-start | bytes 1179656 | tf_op jit(solution)/shard_map/ppermute | solution.py:535
  202.7 33.9 %collective-permute-start.38 = (bf16[2,128,768]{2,1,0:T(8,128)(2,1)S(1)}, bf16[2,128,768]{2,1,0:T(8,128)(2,1)S(1)}, u32[]{:S(2)}, u32[]{:S(2)}) collective-permute-start(bf16[2,128,768]{2,1,0:T(8,128)(2,1)S(1)} %pad_maximum_fusion.11), channel_id=1, source_target_pairs={{0,6},{2,4},{4,2},{6,0},{1,7},{3,5},{5,3},{7,1},{8,14},{10,12},{12... | collective-permute-start | bytes 1179656 | tf_op jit(solution)/shard_map/ppermute | solution.py:535
  215.3 10.2 %collective-permute-start.32 = (bf16[192,1024]{1,0:T(8,128)(2,1)S(1)}, bf16[192,1024]{1,0:T(8,128)(2,1)S(1)}, u32[]{:S(2)}, u32[]{:S(2)}) collective-permute-start(bf16[192,1024]{1,0:T(8,128)(2,1)S(1)} %get-tuple-element.160), channel_id=1, source_target_pairs={{0,1},{1,0},{2,3},{3,2},{4,5},{5,4},{6,7},{7,6},{8,9},{9,8},{10,11... | collective-permute-start | bytes 1179656 | tf_op jit(solution)/shard_map/ppermute | solution.py:525
  225.4 11.2 %collective-permute-start.35 = (bf16[2,192,1024]{2,1,0:T(8,128)(2,1)S(1)}, bf16[2,192,1024]{2,1,0:T(8,128)(2,1)S(1)}, u32[]{:S(2)}, u32[]{:S(2)}) collective-permute-start(bf16[2,192,1024]{2,1,0:T(8,128)(2,1)S(1)} %key_backward.4), channel_id=1, source_target_pairs={{0,1},{1,0},{2,3},{3,2},{4,5},{5,4},{6,7},{7,6},{8,9},{9,8},{10,11... | collective-permute-start | bytes 2359304 | tf_op jit(solution)/shard_map/ppermute | solution.py:525
  225.6 11.0 %collective-permute-start.33 = (bf16[192,1024]{1,0:T(8,128)(2,1)S(1)}, bf16[192,1024]{1,0:T(8,128)(2,1)S(1)}, u32[]{:S(2)}, u32[]{:S(2)}) collective-permute-start(bf16[192,1024]{1,0:T(8,128)(2,1)S(1)} %add_convert_fusion.4), channel_id=1, source_target_pairs={{0,8},{8,0},{16,24},{24,16},{1,9},{9,1},{17,25},{25,17},{2,10},{10... | collective-permute-start | bytes 1179656 | tf_op jit(solution)/shard_map/ppermute | solution.py:528
  236.1 50.5 %collective-permute-start.44 = (bf16[4,3,96,768]{3,2,1,0:T(8,128)(2,1)}, bf16[4,3,96,768]{3,2,1,0:T(8,128)(2,1)}, u32[]{:S(2)}, u32[]{:S(2)}) collective-permute-start(bf16[4,3,96,768]{3,2,1,0:T(8,128)(2,1)} %bitcast.35.refs_4_), channel_id=1, source_target_pairs={{0,1},{1,0},{2,3},{3,2},{4,5},{5,4},{6,7},{7,6},{8,9},{9,8},{10,11... | collective-permute-start | bytes 5308424 | tf_op jit(solution)/shard_map/ppermute | solution.py:525
  237.8 48.7 %collective-permute-start.40 = (bf16[2,192,1024]{2,1,0:T(8,128)(2,1)}, bf16[2,192,1024]{2,1,0:T(8,128)(2,1)}, u32[]{:S(2)}, u32[]{:S(2)}) collective-permute-start(bf16[2,192,1024]{2,1,0:T(8,128)(2,1)} %add_convert_fusion.1), channel_id=1, source_target_pairs={{0,8},{8,0},{16,24},{24,16},{1,9},{9,1},{17,25},{25,17},{2,10},{10... | collective-permute-start | bytes 2359304 | tf_op jit(solution)/shard_map/ppermute | solution.py:528
  242.3 28.6 %collective-permute-start.34 = (bf16[224,768]{1,0:T(8,128)(2,1)S(1)}, bf16[224,768]{1,0:T(8,128)(2,1)S(1)}, u32[]{:S(2)}, u32[]{:S(2)}) collective-permute-start(bf16[224,768]{1,0:T(8,128)(2,1)S(1)} %constant_dynamic-slice_fusion.2), channel_id=1, source_target_pairs={{0,8},{8,0},{16,24},{24,16},{1,9},{9,1},{17,25},{25,17},{2,10},{10... | collective-permute-start | bytes 1032200 | tf_op jit(solution)/shard_map/ppermute | solution.py:528
  252.4 34.2 %collective-permute-start.39 = (bf16[2,192,1024]{2,1,0:T(8,128)(2,1)S(1)}, bf16[2,192,1024]{2,1,0:T(8,128)(2,1)}, u32[]{:S(2)}, u32[]{:S(2)}) collective-permute-start(bf16[2,192,1024]{2,1,0:T(8,128)(2,1)S(1)} %key_backward.6), channel_id=1, source_target_pairs={{0,1},{1,0},{2,3},{3,2},{4,5},{5,4},{6,7},{7,6},{8,9},{9,8},{10,11... | collective-permute-start | bytes 2359304 | tf_op jit(solution)/shard_map/ppermute | solution.py:525
  271.9 38.2 %collective-permute-start.54 = (bf16[224,768]{1,0:T(8,128)(2,1)S(1)}, bf16[224,768]{1,0:T(8,128)(2,1)S(1)}, u32[]{:S(2)}, u32[]{:S(2)}) collective-permute-start(bf16[224,768]{1,0:T(8,128)(2,1)S(1)} %fusion.4), channel_id=1, source_target_pairs={{0,16},{8,24},{16,0},{24,8},{1,17},{9,25},{17,1},{25,9},{2,18},{10... | collective-permute-start | bytes 1032200 | tf_op jit(solution)/shard_map/ppermute | solution.py:532
  288.7 8.9 %collective-permute-start.43 = (bf16[3,192,256]{2,1,0:T(8,128)(2,1)S(1)}, bf16[3,192,256]{2,1,0:T(8,128)(2,1)S(1)}, u32[]{:S(2)}, u32[]{:S(2)}) collective-permute-start(bf16[3,192,256]{2,1,0:T(8,128)(2,1)S(1)} %pad_maximum_fusion.16), channel_id=1, source_target_pairs={{0,6},{2,4},{4,2},{6,0},{1,7},{3,5},{5,3},{7,1},{8,14},{10,12},{12... | collective-permute-start | bytes 884744 | tf_op jit(solution)/shard_map/ppermute | solution.py:535
  288.8 15.2 %collective-permute-start.42 = (bf16[3,192,256]{2,1,0:T(8,128)(2,1)S(1)}, bf16[3,192,256]{2,1,0:T(8,128)(2,1)S(1)}, u32[]{:S(2)}, u32[]{:S(2)}) collective-permute-start(bf16[3,192,256]{2,1,0:T(8,128)(2,1)S(1)} %pad_maximum_fusion.15), channel_id=1, source_target_pairs={{0,4},{2,6},{4,0},{6,2},{1,5},{3,7},{5,1},{7,3},{8,12},{10,14},{12... | collective-permute-start | bytes 884744 | tf_op jit(solution)/shard_map/ppermute | solution.py:535
  290.8 13.2 %collective-permute-start.41 = (bf16[3,192,256]{2,1,0:T(8,128)(2,1)S(1)}, bf16[3,192,256]{2,1,0:T(8,128)(2,1)S(1)}, u32[]{:S(2)}, u32[]{:S(2)}) collective-permute-start(bf16[3,192,256]{2,1,0:T(8,128)(2,1)S(1)} %pad_maximum_fusion.14), channel_id=1, source_target_pairs={{0,2},{2,0},{4,6},{6,4},{1,3},{3,1},{5,7},{7,5},{8,10},{10,8},{12,... | collective-permute-start | bytes 884744 | tf_op jit(solution)/shard_map/ppermute | solution.py:535
  292.8 18.5 %collective-permute-start.46 = (bf16[288,768]{1,0:T(8,128)(2,1)S(1)}, bf16[288,768]{1,0:T(8,128)(2,1)S(1)}, u32[]{:S(2)}, u32[]{:S(2)}) collective-permute-start(bf16[288,768]{1,0:T(8,128)(2,1)S(1)} %constant_dynamic-slice_fusion.1), channel_id=1, source_target_pairs={{0,1},{1,0},{2,3},{3,2},{4,5},{5,4},{6,7},{7,6},{8,9},{9,8},{10,11... | collective-permute-start | bytes 1327112 | tf_op jit(solution)/shard_map/ppermute | solution.py:525
  311.5 12.2 %collective-permute-start.47 = (bf16[144,768]{1,0:T(8,128)(2,1)S(1)}, bf16[144,768]{1,0:T(8,128)(2,1)S(1)}, u32[]{:S(2)}, u32[]{:S(2)}) collective-permute-start(bf16[144,768]{1,0:T(8,128)(2,1)S(1)} %constant_dynamic-slice_fusion), channel_id=1, source_target_pairs={{0,8},{8,0},{16,24},{24,16},{1,9},{9,1},{17,25},{25,17},{2,10},{10... | collective-permute-start | bytes 663560 | tf_op jit(solution)/shard_map/ppermute | solution.py:528
  314.8 24.2 %collective-permute-start.55 = (bf16[224,768]{1,0:T(8,128)(2,1)S(1)}, bf16[224,768]{1,0:T(8,128)(2,1)S(1)}, u32[]{:S(2)}, u32[]{:S(2)}) collective-permute-start(bf16[224,768]{1,0:T(8,128)(2,1)S(1)} %add_convert_fusion.7), channel_id=1, source_target_pairs={{0,8},{8,0},{16,24},{24,16},{1,9},{9,1},{17,25},{25,17},{2,10},{10... | collective-permute-start | bytes 1032200 | tf_op jit(solution)/shard_map/ppermute | solution.py:528
  323.8 15.3 %collective-permute-start.48 = (bf16[2,128,768]{2,1,0:T(8,128)(2,1)S(1)}, bf16[2,128,768]{2,1,0:T(8,128)(2,1)S(1)}, u32[]{:S(2)}, u32[]{:S(2)}) collective-permute-start(bf16[2,128,768]{2,1,0:T(8,128)(2,1)S(1)} %pad_maximum_fusion.12), channel_id=1, source_target_pairs={{0,2},{2,0},{4,6},{6,4},{1,3},{3,1},{5,7},{7,5},{8,10},{10,8},{12,... | collective-permute-start | bytes 1179656 | tf_op jit(solution)/shard_map/ppermute | solution.py:535
  324.5 14.6 %collective-permute-start.49 = (bf16[2,128,768]{2,1,0:T(8,128)(2,1)S(1)}, bf16[2,128,768]{2,1,0:T(8,128)(2,1)S(1)}, u32[]{:S(2)}, u32[]{:S(2)}) collective-permute-start(bf16[2,128,768]{2,1,0:T(8,128)(2,1)S(1)} %pad_maximum_fusion.12), channel_id=1, source_target_pairs={{0,4},{2,6},{4,0},{6,2},{1,5},{3,7},{5,1},{7,3},{8,12},{10,14},{12... | collective-permute-start | bytes 1179656 | tf_op jit(solution)/shard_map/ppermute | solution.py:535
  324.7 18.3 %collective-permute-start.50 = (bf16[2,128,768]{2,1,0:T(8,128)(2,1)S(1)}, bf16[2,128,768]{2,1,0:T(8,128)(2,1)}, u32[]{:S(2)}, u32[]{:S(2)}) collective-permute-start(bf16[2,128,768]{2,1,0:T(8,128)(2,1)S(1)} %pad_maximum_fusion.12), channel_id=1, source_target_pairs={{0,6},{2,4},{4,2},{6,0},{1,7},{3,5},{5,3},{7,1},{8,14},{10,12},{12... | collective-permute-start | bytes 1179656 | tf_op jit(solution)/shard_map/ppermute | solution.py:535
  332.8 15.2 %collective-permute-start.52 = (bf16[144,768]{1,0:T(8,128)(2,1)S(1)}, bf16[144,768]{1,0:T(8,128)(2,1)}, u32[]{:S(2)}, u32[]{:S(2)}) collective-permute-start(bf16[144,768]{1,0:T(8,128)(2,1)S(1)} %add_convert_fusion.8), channel_id=1, source_target_pairs={{0,8},{8,0},{16,24},{24,16},{1,9},{9,1},{17,25},{25,17},{2,10},{10... | collective-permute-start | bytes 663560 | tf_op jit(solution)/shard_map/ppermute | solution.py:528
  344.3 11.6 %collective-permute-start.56 = (bf16[896,768]{1,0:T(8,128)(2,1)S(1)}, bf16[896,768]{1,0:T(8,128)(2,1)S(1)}, u32[]{:S(2)}, u32[]{:S(2)}) collective-permute-start(bf16[896,768]{1,0:T(8,128)(2,1)S(1)} %pad_maximum_fusion.4.near), channel_id=1, source_target_pairs={{0,1},{1,0},{2,3},{3,2},{4,5},{5,4},{6,7},{7,6},{8,9},{9,8},{10,11... | collective-permute-start | bytes 4128776 | tf_op jit(solution)/shard_map/ppermute | solution.py:525
  (70 other events, 446.7 us)
Sparse Core Ops, SparseCore 0:
  32.3 64.0 all-gather.4
  115.9 37.5 all-gather.6
  165.9 72.1 reduce-scatter.3
  253.7 48.7 all-reduce.2

commit v13 on v12

--- a/solution.py
+++ b/solution.py
@@ -713,25 +713,23 @@
         signed, signed_t, bits, head_n, near_o, after(kv_o, dkv_far, grad_q, weight_sum, *layer_moved),
         grad_tables, bf16, 25,
     )
-    half = weight_sum.shape[0] // 2
-    low_keep, low_send = split(weight_sum[:half], r)
+    low = weight_sum.shape[0] // 4
+    low_keep, low_send = split(weight_sum[:low], r)
     low_far = over_place(low_send)
-    high_sum = lax.psum(weight_sum[half:], "hash")
+    high_sum = lax.psum(weight_sum[low:], "hash")
     dkv_far = over_place(dkv_far)
     dkv_o_moved = over_seq(dkv_o)
-    low_keep = add(low_keep, after(low_far, dkv_o))
-    low_send = low_keep.astype(bf16)
-    low_far = [over_group(low_send, k) for k in range(1, groups)]
     dkv = key_backward(
-        signed, signed_t, bits, head_n, near, after(kv, low_send), grad_tables, f32, 25
+        signed, signed_t, bits, head_n, near, kv, grad_tables, f32, 25
     )
 
     dkv_o_moved = after(dkv_o_moved, dkv)
     grad_kv = add(dkv, dkv_o_moved, after(dkv_far, dkv)).astype(bf16)
     grad_qkv = jnp.concatenate([grad_q[None], grad_kv])
     qkv_parts = to_dense(grad_qkv)
-    low_keep = add(low_keep, *[after(x, qkv_parts[1]) for x in low_far]).astype(bf16)
-    low_far = over_place(low_keep)
+    low_keep = add(low_keep, after(low_far, qkv_parts[1]))
+    low_send = low_keep.astype(bf16)
+    low_far = [over_group(low_send, k) for k in range(1, groups)]
 
     grad_in = input_grad(core, grad_first, qkv_parts, w_qkv_t, after(w_qkv_far, dkv))
 
@@ -743,6 +741,8 @@
     w_send = w_keep.astype(bf16)
     grad_moved = after(jnp.stack(grad_moved), w_send)
     w_keep = add(w_keep, *[over_group(w_send, k) for k in range(1, groups)]).astype(bf16)
+    low_keep = add(low_keep, *[after(x, grad_moved) for x in low_far]).astype(bf16)
+    low_far = over_place(low_keep)
     grad_moved = [grad_moved] + [over_head(grad_moved, j) for j in range(1, head_count)]
 
     def home(blocks):
@@ -767,7 +767,7 @@
     w_grad = in_halves(r, w_keep, over_place(w_keep))
     w_grad = in_halves(s, w_grad, over_seq(w_grad)).reshape(3, head_width, width)
     grad_w_qkv = w_grad.transpose(0, 2, 1).astype(f32)
-    low_keep = in_halves(r, low_keep, after(low_far, *grad_moved))
+    low_keep = in_halves(r, low_keep, low_far)
     weight_sum = jnp.concatenate([low_keep, after(high_sum, *grad_moved)])
     weight_far = over_seq(weight_sum)
     grad_w_up, grad_w_down, grad_w_out = weight_results(core, weight_sum, weight_far, head_width)

time: 376 us -> 372 us (0.989)
  waiting for transfers between devices: 45.7 us -> 63.5 us
  starting transfers between devices: 69.6 us -> 53.1 us
  local copies, waits for them, and re-layouts: 45 us -> 39.9 us
    ppermute x5, waiting for transfers between devices: 2.62 us -> 33 us  [over_group(): return lax.ppermute(x, 'hash', moves)]
    ppermute x11, waiting for transfers between devices: 25.6 us -> 11.6 us  [over_place(): return lax.ppermute(x, 'hash', [(h, h ^ 1) for h in range(hash_count)])]
    ppermute x11, starting transfers between devices: 16.6 us -> 8.48 us  [over_place(): return lax.ppermute(x, 'hash', [(h, h ^ 1) for h in range(hash_count)])]
    ppermute x22, starting transfers between devices: 22.2 us -> 17.4 us  [over_seq(): return lax.ppermute(x, 'seq', [(0, 1), (1, 0)])]
    unnamed x126 -> x120, local copies, waits for them, and re-layouts: 22.8 us -> 19.1 us
  transfers between devices with their start and end apart: 61 -> 61, of which waited for: 11 -> 12; matrix products, arithmetic and copies ran while one was open for 15% -> 15% of each run, Pallas kernels for 43% -> 43%
where the time goes in v13:
time: 372 us; the launch traced here: 367 us
  Pallas kernels  164 us (44%)
  waiting for transfers between devices  63.5 us (17%)
  starting transfers between devices  53.1 us (14%)
  local copies, waits for them, and re-layouts  39.9 us (11%)
  other arithmetic  26.4 us (7%)
  between operations  15.6 us (4%)
  matrix products  4.14 us (1%)
    pallas_call x5, Pallas kernels, single(): pl.pallas_call(kernel, in_specs=[pl.BlockSpec(memory_space=pltpu.SMEM)] +...  43.5 us
    pallas_call x3, Pallas kernels, query_backward(): call(partial(query_back_kernel, chunk=4, blocks=blocks, last=last), heads...  43.2 us
    pallas_call x4, Pallas kernels, key_backward(): call(partial(key_back_kernel, chunk=4), heads, micros, 'key_backward', [w...  38.2 us
    ppermute x5, waiting for transfers between devices, over_group(): return lax.ppermute(x, 'hash', moves)  33 us
    pallas_call x5, Pallas kernels, key_tables(): call(partial(key_kernel, chunk=2, blocks=len(blocks)), heads, 30 if len(b...  23.4 us
    unnamed x120, local copies, waits for them, and re-layouts  19.1 us
    ppermute x22, starting transfers between devices, over_seq(): return lax.ppermute(x, 'seq', [(0, 1), (1, 0)])  17.4 us
    ppermute x18, starting transfers between devices, over_head(): return lax.ppermute(x, 'head', [(h, h ^ j) for h in range(head_count)])  16.4 us
  transfers between devices with their start and end apart: 61, of which 12 were waited for; matrix products, arithmetic and copies ran while one was open for 15% of the time, Pallas kernels for 43%

profile of v13, /device:TPU:1, one launch (start us, length us, event | category | flops | bytes accessed | tf_op | source)
XLA Modules:
  0.0 366.7 jit_solution(6871552592178216270)
XLA Ops:
  7.3 4.5 %constant_dynamic-slice_fusion.8 = (bf16[1,128,1,768]{3,2,1,0:T(2,128)(2,1)S(1)}, bf16[1,128,1,768]{3,2,1,0:T(2,128)(2,1)}, bf16[1,128,1,768]{3,2,1,0:T(2,128)(2...) fusion(bf16[1,512,2,768]{3,2,1,0:T(2,128)(2,1)} %param.11, s32[]{:T(128)S(6)} %select_n.240, ...), kind=kLoop, calls=%fused_computation.128 | loop fusion | bytes 1966104 | tf_op jit(solution)/shard_map/jit(dynamic_index_in_dim)/dynamic_slice | solution.py:538
  12.6 3.1 collective-permute-start
  16.3 2.5 collective-permute-start.1
  20.5 2.4 copy.54
  22.9 1.8 copy_bitcast_fusion
  24.7 1.9 dynamic-slice_bitcast_fusion
  37.1 1.9 slice.124
  39.0 1.7 slice.123
  40.7 5.3 %key_tables.5.refs_4_ = f32[3,2048,64]{2,1,0:T(8,128)S(1)} custom-call(bf16[64,64]{1,0:T(8,128)(2,1)S(1)} %bitcast.129, bf16[576,512]{1,0:T(8,128)(2,1)} %bitcast.14.refs_0_.refs_2_.ka.va, bf16[576,512]{1,0:T(8,128)(2,1)} %collective-permute-done.2.refs_1_.refs_3_.refs_0_.refs_2_.ka.va, bf16[576,512]{1,0:T(8,128)(2,1)} %bitcast.14.refs_0_.refs_2_.ka.va, ...), custom_call_target="tpu_custom_call" | custom-call | flops 1100000000 | bytes 1048576 | tf_op jit(solution)/shard_map/key_tables/pallas_call | solution.py:192
  46.0 2.1 pad_maximum_fusion.8
  49.1 1.9 collective-permute-start.8
  53.4 5.8 %key_tables.6.refs_4_ = f32[3,2048,64]{2,1,0:T(8,128)S(1)} custom-call(bf16[64,64]{1,0:T(8,128)(2,1)S(1)} %bitcast.130, bf16[576,512]{1,0:T(8,128)(2,1)} %collective-permute-done.9.refs_0_.refs_2_.ka.va, bf16[576,512]{1,0:T(8,128)(2,1)S(1)} %collective-permute-done.10.refs_1_.refs_3_.refs_0_.ka.va, ...), custom_call_target="tpu_custom_call" | custom-call | flops 32999999488 | bytes 1048576 | tf_op jit(solution)/shard_map/key_tables/pallas_call | solution.py:192
  60.9 5.6 %key_tables.7.refs_2_ = f32[3,2048,64]{2,1,0:T(8,128)S(1)} custom-call(bf16[64,64]{1,0:T(8,128)(2,1)S(1)} %bitcast.131, bf16[384,512]{1,0:T(8,128)(2,1)S(1)} %bitcast.125, bf16[384,512]{1,0:T(8,128)(2,1)S(1)} %collective-permute-done.8.refs_1_.refs_3_.kb.vb, bf16[384,512]{1,0:T(8,128)(2,1)S(1)} %bitcast.126, ...), custom_call_target="tpu_custom_call" | custom-call | flops 32999999488 | bytes 1048576 | tf_op jit(solution)/shard_map/key_tables/pallas_call | solution.py:192
  69.8 1.7 pad_maximum_fusion.10.x_in
  71.5 4.2 %key_tables.8.refs_2_ = f32[3,2048,64]{2,1,0:T(8,128)S(1)} custom-call(bf16[64,64]{1,0:T(8,128)(2,1)S(1)} %bitcast.132, bf16[384,512]{1,0:T(8,128)(2,1)S(1)} %collective-permute-done.7.refs_0_.refs_1_.kb.vb, bf16[384,512]{1,0:T(8,128)(2,1)S(1)} %collective-permute-done.7.refs_0_.refs_1_.kb.vb, f32[3,2048,64]{2,1,0:T(8,128)} %copy-done.2), custom_call_target="tpu_custom_call" | custom-call | flops 1100000000 | bytes 1048576 | tf_op jit(solution)/shard_map/key_tables/pallas_call | solution.py:192
  76.4 2.6 key_tables.9.tables
  79.0 3.3 query_estimates.4
  82.9 4.1 %query_estimates.5 = bf16[192,1024]{1,0:T(8,128)(2,1)S(1)} custom-call(bf16[64,64]{1,0:T(8,128)(2,1)S(1)} %bitcast.135, bf16[3,2048,64]{2,1,0:T(8,128)(2,1)S(1)} %key_tables.9.tables, bf16[576,512]{1,0:T(8,128)(2,1)} %collective-permute-done.9.refs_0_.refs_2_.ka.va, bf16[192,512]{1,0:T(8,128)(2,1)S(1)} %collective-permute-done.6.refs_1_), custom_call_target="tpu_custom_call" | custom-call | flops 1100000000 | bytes 1048576 | tf_op jit(solution)/shard_map/query_estimates/pallas_call | solution.py:205
  87.2 4.2 %query_estimates.6 = bf16[192,1024]{1,0:T(8,128)(2,1)S(1)} custom-call(bf16[64,64]{1,0:T(8,128)(2,1)S(1)} %bitcast.136, bf16[3,2048,64]{2,1,0:T(8,128)(2,1)S(1)} %key_tables.9.tables, bf16[576,512]{1,0:T(8,128)(2,1)} %collective-permute-done.2.refs_1_.refs_3_.refs_0_.refs_2_.ka.va, bf16[192,512]{1,0:T(8,128)(2,1)S(1)} %collective-permute-done.12.refs_1_.refs_3_), custom_call_target="tpu_custom_call" | custom-call | flops 1100000000 | bytes 1048576 | tf_op jit(solution)/shard_map/query_estimates/pallas_call | solution.py:205
  92.1 4.3 %all-gather.5.cloned.1.call-done = bf16[3456,768]{1,0:T(8,128)(2,1)} async-done(((bf16[864,768]{1,0:T(8,128)(2,1)}), bf16[3456,768]{1,0:T(8,128)(2,1)}) %all-gather.5.cloned.1.call-update) | async-done | bytes 5308432 | tf_op jit(solution)/shard_map/all_gather | solution.py:573
  98.9 1.8 dynamic-slice_bitcast_fusion.1
  100.9 4.2 %query_estimates.7 = f32[192,1024]{1,0:T(8,128)S(1)} custom-call(bf16[64,64]{1,0:T(8,128)(2,1)S(1)} %bitcast.138, bf16[3,2048,64]{2,1,0:T(8,128)(2,1)S(1)} %key_tables.9.tables, bf16[576,512]{1,0:T(8,128)(2,1)} %bitcast.14.refs_0_.refs_2_.ka.va, bf16[192,512]{1,0:T(8,128)(2,1)S(1)} %convolution_convert_fusion.1.refs_1_), custom_call_target="tpu_custom_call" | custom-call | flops 1100000000 | bytes 1048576 | tf_op jit(solution)/shard_map/query_estimates/pallas_call | solution.py:205
  105.1 2.2 collective-permute-done.16
  116.4 12.7 %dense.1 = (bf16[256,768]{1,0:T(8,128)(2,1)}, f32[256,768]{1,0:T(8,128)}, f32[256,768]{1,0:T(8,128)}, f32[8,256,384]{2,1,0:T(8,128)}, bf16[8,256,384]{2,1,0:T(8,...) custom-call(s32[2]{0:T(128)} %pad_add_fusion.core, ...), custom_call_target="tpu_custom_call" | custom-call | flops 15399999488 | bytes 1048576 | tf_op jit(solution)/shard_map/dense/pallas_call | solution.py:402
  129.2 12.5 %dense_back.1 = (f32[256,768]{1,0:T(8,128)}, bf16[6,256,384]{2,1,0:T(8,128)(2,1)}, bf16[6,256,384]{2,1,0:T(8,128)(2,1)}, bf16[192,256]{1,0:T(8,128)(2,1)}, bf16[...) custom-call(s32[2]{0:T(128)} %pad_add_fusion.core, ...), custom_call_target="tpu_custom_call" | custom-call | flops 8800000000 | bytes 1048576 | tf_op jit(solution)/shard_map/dense_back/pallas_call | solution.py:402
  144.4 2.8 collective-permute-start.25
  148.7 2.8 collective-permute-start.26
  151.6 2.1 collective-permute-start.27
  157.3 8.2 %weight_grads.1 = bf16[4,896,768]{2,1,0:T(8,128)(2,1)} custom-call(s32[2]{0:T(128)} %pad_add_fusion.core, f32[8,768]{1,0:T(8,128)} %get-tuple-element.138.small_a, f32[8,768]{1,0:T(8,128)} %get-tuple-element.139.small_b, bf16[8,256,384]{2,1,0:T(8,128)(2,1)} %get-tuple-element.140.refs_0_, bf16[8,256,384]{2,1,0:T(8,128)(2,1)} %collective-permute-done.24.refs_1_, ...), custom_call_target="tpu_custom_call" | custom-call | flops 7699999744 | bytes 1048576 | tf_op jit(solution)/shard_map/weight_grads/pallas_call | solution.py:402
  168.8 20.2 %query_backward.3 = (f32[3,2048,64]{2,1,0:T(8,128)}, f32[192,1024]{1,0:T(8,128)S(1)}, bf16[192,1024]{1,0:T(8,128)(2,1)S(1)}) custom-call(bf16[64,64]{1,0:T(8,128)(2,1)S(1)} %bitcast.139, bf16[64,128]{1,0:T(8,128)(2,1)S(1)} %pad_maximum_fusion.21.planes_t, bf16[80,2048]{1,0:T(8,128)(2,1)S(1)} %copy-done.16, bf16[3,2048,64]{2,1,0:T(8,128)(2,1)S(1)} %key_tables.9.tables, ...), custom_call_target="tpu_custom_call" | custom-call | flops 54999998464 | bytes 1048576 | tf_op jit(solution)/shard_map/query_backward/pallas_call | solution.py:229
  189.6 11.8 %query_backward.4 = (f32[3,2048,64]{2,1,0:T(8,128)}, f32[192,1024]{1,0:T(8,128)S(1)}) custom-call(bf16[64,64]{1,0:T(8,128)(2,1)S(1)} %bitcast.140, bf16[64,128]{1,0:T(8,128)(2,1)S(1)} %pad_maximum_fusion.21.planes_t, bf16[80,2048]{1,0:T(8,128)(2,1)S(1)} %copy-done.16, bf16[3,2048,64]{2,1,0:T(8,128)(2,1)S(1)} %key_tables.9.tables, ...), custom_call_target="tpu_custom_call" | custom-call | flops 27499999232 | bytes 1048576 | tf_op jit(solution)/shard_map/query_backward/pallas_call | solution.py:229
  204.1 11.2 %query_backward.5 = (bf16[3,2048,64]{2,1,0:T(8,128)(2,1)S(1)}, bf16[192,1024]{1,0:T(8,128)(2,1)S(1)}) custom-call(bf16[64,64]{1,0:T(8,128)(2,1)S(1)} %bitcast.141, bf16[64,128]{1,0:T(8,128)(2,1)S(1)} %pad_maximum_fusion.21.planes_t, bf16[80,2048]{1,0:T(8,128)(2,1)S(1)} %copy-done.16, bf16[3,2048,64]{2,1,0:T(8,128)(2,1)S(1)} %key_tables.9.tables, ...), custom_call_target="tpu_custom_call" | custom-call | flops 27499999232 | bytes 1048576 | tf_op jit(solution)/shard_map/query_backward/pallas_call | solution.py:229
  216.7 8.8 %key_backward.4 = bf16[2,192,1024]{2,1,0:T(8,128)(2,1)S(1)} custom-call(bf16[64,64]{1,0:T(8,128)(2,1)S(1)} %bitcast.142, bf16[64,128]{1,0:T(8,128)(2,1)S(1)} %pad_maximum_fusion.21.planes_t, bf16[80,2048]{1,0:T(8,128)(2,1)S(1)} %copy-done.17, bf16[576,512]{1,0:T(8,128)(2,1)S(1)} %copy-done.11, bf16[384,512]{1,0:T(8,128)(2,1)S(1)} %copy-done.7, ...), custom_call_target="tpu_custom_call" | custom-call | flops 27499999232 | bytes 1048576 | tf_op jit(solution)/shard_map/key_backward/pallas_call | solution.py:243
  226.4 9.7 %key_backward.5 = bf16[2,192,1024]{2,1,0:T(8,128)(2,1)S(1)} custom-call(bf16[64,64]{1,0:T(8,128)(2,1)S(1)} %bitcast.143, bf16[64,128]{1,0:T(8,128)(2,1)S(1)} %pad_maximum_fusion.21.planes_t, bf16[80,2048]{1,0:T(8,128)(2,1)S(1)} %copy-done.17, bf16[576,512]{1,0:T(8,128)(2,1)} %collective-permute-done.9.refs_0_.refs_2_.ka.va, bf16[384,512]{1,0:T(8,128)(2,1)S(1)} %copy-done.5, ...), custom_call_target="tpu_custom_call" | custom-call | flops 27499999232 | bytes 1048576 | tf_op jit(solution)/shard_map/key_backward/pallas_call | solution.py:243
  239.9 9.8 %key_backward.7 = bf16[2,192,1024]{2,1,0:T(8,128)(2,1)S(1)} custom-call(bf16[64,64]{1,0:T(8,128)(2,1)S(1)} %bitcast.144, bf16[64,128]{1,0:T(8,128)(2,1)S(1)} %pad_maximum_fusion.21.planes_t, bf16[80,2048]{1,0:T(8,128)(2,1)S(1)} %copy-done.18, bf16[576,512]{1,0:T(8,128)(2,1)} %collective-permute-done.2.refs_1_.refs_3_.refs_0_.refs_2_.ka.va, ...), custom_call_target="tpu_custom_call" | custom-call | flops 27499999232 | bytes 1048576 | tf_op jit(solution)/shard_map/key_backward/pallas_call | solution.py:243
  250.1 10.0 %key_backward.6 = f32[2,192,1024]{2,1,0:T(8,128)S(1)} custom-call(bf16[64,64]{1,0:T(8,128)(2,1)S(1)} %bitcast.145, bf16[64,128]{1,0:T(8,128)(2,1)S(1)} %pad_maximum_fusion.21.planes_t, bf16[80,2048]{1,0:T(8,128)(2,1)S(1)} %copy-done.18, bf16[576,512]{1,0:T(8,128)(2,1)} %bitcast.14.refs_0_.refs_2_.ka.va, bf16[384,512]{1,0:T(8,128)(2,1)S(1)} %bitcast.127, ...), custom_call_target="tpu_custom_call" | custom-call | flops 27499999232 | bytes 1048576 | tf_op jit(solution)/shard_map/key_backward/pallas_call | solution.py:243
  262.2 1.8 add_convert_fusion
  270.4 3.3 collective-permute-done.42.refs_3_
  273.7 7.0 %collective-permute-done.41.refs_2_ = bf16[3,192,256]{2,1,0:T(8,128)(2,1)S(1)} collective-permute-done((bf16[3,192,256]{2,1,0:T(8,128)(2,1)S(1)}, bf16[3,192,256]{2,1,0:T(8,128)(2,1)S(1)}, u32[]{:S(2)}, u32[]{:S(2)}) %collective-permute-start.41) | collective-permute-done | bytes 294944 | tf_op jit(solution)/shard_map/ppermute | solution.py:535
  281.5 5.3 %input_grad.1 = bf16[256,768]{1,0:T(8,128)(2,1)} custom-call(s32[2]{0:T(128)} %pad_add_fusion.core, f32[256,768]{1,0:T(8,128)} %get-tuple-element.163.grad_first, bf16[3,192,256]{2,1,0:T(8,128)(2,1)} %pad_maximum_fusion.13.refs_0_, bf16[3,192,256]{2,1,0:T(8,128)(2,1)} %copy-done.49, bf16[3,192,256]{2,1,0:T(8,128)(2,1)} %copy-done.48, ...), custom_call_target="tpu_custom_call" | custom-call | flops 44000002048 | bytes 1048576 | tf_op jit(solution)/shard_map/input_grad/pallas_call | solution.py:402
  287.8 1.8 collective-permute-start.44
  291.2 14.5 %collective-permute-done.44 = bf16[128,768]{1,0:T(8,128)(2,1)S(1)} collective-permute-done((bf16[128,768]{1,0:T(8,128)(2,1)S(1)}, bf16[128,768]{1,0:T(8,128)(2,1)S(1)}, u32[]{:S(2)}, u32[]{:S(2)}) %collective-permute-start.44) | collective-permute-done | bytes 196640 | tf_op jit(solution)/shard_map/ppermute | solution.py:532
  308.4 18.6 %collective-permute-done.54 = bf16[112,768]{1,0:T(8,128)(2,1)S(1)} collective-permute-done((bf16[112,768]{1,0:T(8,128)(2,1)S(1)}, bf16[112,768]{1,0:T(8,128)(2,1)S(1)}, u32[]{:S(2)}, u32[]{:S(2)}) %collective-permute-start.54) | collective-permute-done | bytes 172064 | tf_op jit(solution)/shard_map/ppermute | solution.py:532
  328.1 2.8 copy.56
  330.8 6.2 %collective-permute-done.55 = bf16[112,768]{1,0:T(8,128)(2,1)S(1)} collective-permute-done((bf16[112,768]{1,0:T(8,128)(2,1)S(1)}, bf16[112,768]{1,0:T(8,128)(2,1)S(1)}, u32[]{:S(2)}, u32[]{:S(2)}) %collective-permute-start.55) | collective-permute-done | bytes 172064 | tf_op jit(solution)/shard_map/ppermute | solution.py:528
  340.7 3.1 collective-permute-done.51
  346.6 4.1 %copy.57 = f32[1,512,2,768]{3,2,1,0:T(2,128)} copy(f32[1,512,2,768]{3,1,2,0:T(8,128)S(1)} %maximum_convert_fusion) | data formatting | bytes 6291456
  355.0 4.7 %weight_results.1 = (f32[768,768]{1,0:T(8,128)}, f32[768,768]{1,0:T(8,128)}, f32[192,768]{1,0:T(8,128)}) custom-call(s32[2]{0:T(128)} %pad_add_fusion.core, bf16[896,768]{1,0:T(8,128)(2,1)} %copy-done.33, bf16[896,768]{1,0:T(8,128)(2,1)} %copy-done.46), custom_call_target="tpu_custom_call" | custom-call | flops 3300000000 | bytes 1048576 | tf_op jit(solution)/shard_map/weight_results/pallas_call | solution.py:402
  (302 shorter events, 82.4 us)
Async XLA Ops:
  7.2 89.1 %all-gather.5.cloned.1.call-start = ((), (), s32[]{:S(2)}) async-start(), calls=%async_computation.2 | async-start | bytes 6635520 | tf_op jit(solution)/shard_map/all_gather | solution.py:573
  12.6 16.4 %collective-permute-start = (bf16[128,768]{1,0:T(8,128)(2,1)}, bf16[128,768]{1,0:T(8,128)(2,1)}, u32[]{:S(2)}, u32[]{:S(2)}) collective-permute-start(bf16[128,768]{1,0:T(8,128)(2,1)} %bitcast.121), channel_id=1, source_target_pairs={{0,16},{8,24},{16,0},{24,8},{1,17},{9,25},{17,1},{25,9},{2,18},{10... | collective-permute-start | bytes 589832 | tf_op jit(solution)/shard_map/ppermute | solution.py:532
  16.3 19.9 %collective-permute-start.1 = (bf16[8,8,64]{2,0,1:T(8,128)(2,1)}, bf16[8,8,64]{2,0,1:T(8,128)(2,1)S(1)}, u32[]{:S(2)}, u32[]{:S(2)}) collective-permute-start(bf16[8,8,64]{2,0,1:T(8,128)(2,1)} %fusion.18), channel_id=1, source_target_pairs={{0,0},{8,1},{16,8},{24,9},{1,16},{9,17},{17,24},{25,25},{2,2},{10,... | collective-permute-start | bytes 24584 | tf_op jit(solution)/shard_map/ppermute | solution.py:557
  30.5 10.2 %collective-permute-start.2 = (bf16[576,512]{1,0:T(8,128)(2,1)}, bf16[576,512]{1,0:T(8,128)(2,1)}, u32[]{:S(2)}, u32[]{:S(2)}) collective-permute-start(bf16[576,512]{1,0:T(8,128)(2,1)} %bitcast.14.refs_0_.refs_2_.ka.va), channel_id=1, source_target_pairs={{0,1},{1,0},{2,3},{3,2},{4,5},{5,4},{6,7},{7,6},{8,9},{9,8},{10,11... | collective-permute-start | bytes 1769480 | tf_op jit(solution)/shard_map/ppermute | solution.py:525
  32.1 123.9 %all-gather.7.cloned.1.call-start = ((), (), s32[]{:S(2)}) async-start(), calls=%async_computation.3 | async-start | bytes 2211840 | tf_op jit(solution)/shard_map/all_gather | solution.py:638
  32.4 18.5 %collective-permute-start.9 = (bf16[576,512]{1,0:T(8,128)(2,1)}, bf16[576,512]{1,0:T(8,128)(2,1)}, u32[]{:S(2)}, u32[]{:S(2)}) collective-permute-start(bf16[576,512]{1,0:T(8,128)(2,1)} %bitcast.14.refs_0_.refs_2_.ka.va), channel_id=1, source_target_pairs={{0,8},{8,0},{16,24},{24,16},{1,9},{9,1},{17,25},{25,17},{2,10},{10... | collective-permute-start | bytes 1769480 | tf_op jit(solution)/shard_map/ppermute | solution.py:528
  33.8 12.2 %collective-permute-start.3 = (bf16[1,128,768]{2,1,0:T(8,128)(2,1)}, bf16[1,128,768]{2,1,0:T(8,128)(2,1)S(1)}, u32[]{:S(2)}, u32[]{:S(2)}) collective-permute-start(bf16[1,128,768]{2,1,0:T(8,128)(2,1)} %bitcast.20), channel_id=1, source_target_pairs={{0,2},{2,0},{4,6},{6,4},{1,3},{3,1},{5,7},{7,5},{8,10},{10,8},{12,... | collective-permute-start | bytes 589832 | tf_op jit(solution)/shard_map/ppermute | solution.py:535
  35.0 11.0 %collective-permute-start.4 = (bf16[1,128,768]{2,1,0:T(8,128)(2,1)}, bf16[1,128,768]{2,1,0:T(8,128)(2,1)}, u32[]{:S(2)}, u32[]{:S(2)}) collective-permute-start(bf16[1,128,768]{2,1,0:T(8,128)(2,1)} %bitcast.20), channel_id=1, source_target_pairs={{0,4},{2,6},{4,0},{6,2},{1,5},{3,7},{5,1},{7,3},{8,12},{10,14},{12... | collective-permute-start | bytes 589832 | tf_op jit(solution)/shard_map/ppermute | solution.py:535
  36.2 9.8 %collective-permute-start.5 = (bf16[1,128,768]{2,1,0:T(8,128)(2,1)}, bf16[1,128,768]{2,1,0:T(8,128)(2,1)}, u32[]{:S(2)}, u32[]{:S(2)}) collective-permute-start(bf16[1,128,768]{2,1,0:T(8,128)(2,1)} %bitcast.20), channel_id=1, source_target_pairs={{0,6},{2,4},{4,2},{6,0},{1,7},{3,5},{5,3},{7,1},{8,14},{10,12},{12... | collective-permute-start | bytes 589832 | tf_op jit(solution)/shard_map/ppermute | solution.py:535
  49.1 11.8 %collective-permute-start.8 = (bf16[384,512]{1,0:T(8,128)(2,1)S(1)}, bf16[384,512]{1,0:T(8,128)(2,1)S(1)}, u32[]{:S(2)}, u32[]{:S(2)}) collective-permute-start(bf16[384,512]{1,0:T(8,128)(2,1)S(1)} %bitcast.123), channel_id=1, source_target_pairs={{0,1},{1,0},{2,3},{3,2},{4,5},{5,4},{6,7},{7,6},{8,9},{9,8},{10,11... | collective-permute-start | bytes 1179656 | tf_op jit(solution)/shard_map/ppermute | solution.py:525
  51.0 17.2 %collective-permute-start.7 = (bf16[384,512]{1,0:T(8,128)(2,1)S(1)}, bf16[384,512]{1,0:T(8,128)(2,1)S(1)}, u32[]{:S(2)}, u32[]{:S(2)}) collective-permute-start(bf16[384,512]{1,0:T(8,128)(2,1)S(1)} %bitcast.124), channel_id=1, source_target_pairs={{0,8},{8,0},{16,24},{24,16},{1,9},{9,1},{17,25},{25,17},{2,10},{10... | collective-permute-start | bytes 1179656 | tf_op jit(solution)/shard_map/ppermute | solution.py:528
  68.2 8.2 %collective-permute-start.11 = (bf16[384,512]{1,0:T(8,128)(2,1)S(1)}, bf16[384,512]{1,0:T(8,128)(2,1)S(1)}, u32[]{:S(2)}, u32[]{:S(2)}) collective-permute-start(bf16[384,512]{1,0:T(8,128)(2,1)S(1)} %collective-permute-done.7.refs_0_.refs_1_.kb.vb), channel_id=1, source_target_pairs={{0,1},{1,0},{2,3},{3,2},{4,5},{5,4},{6,7},{7,6},{8,9},{9,8},{10,11... | collective-permute-start | bytes 1179656 | tf_op jit(solution)/shard_map/ppermute | solution.py:525
  96.3 19.9 %collective-permute-start.20 = (bf16[4,864,768]{2,1,0:T(8,128)(2,1)}, bf16[4,864,768]{2,1,0:T(8,128)(2,1)}, u32[]{:S(2)}, u32[]{:S(2)}) collective-permute-start(bf16[4,864,768]{2,1,0:T(8,128)(2,1)} %bitcast.173), channel_id=1, source_target_pairs={{0,1},{1,0},{2,3},{3,2},{4,5},{5,4},{6,7},{7,6},{8,9},{9,8},{10,11... | collective-permute-start | bytes 15925256 | tf_op jit(solution)/shard_map/ppermute | solution.py:525
  97.0 10.3 %collective-permute-start.16 = (bf16[192,1024]{1,0:T(8,128)(2,1)S(1)}, bf16[192,1024]{1,0:T(8,128)(2,1)}, u32[]{:S(2)}, u32[]{:S(2)}) collective-permute-start(bf16[192,1024]{1,0:T(8,128)(2,1)S(1)} %add_convert_fusion.6), channel_id=1, source_target_pairs={{0,8},{8,0},{16,24},{24,16},{1,9},{9,1},{17,25},{25,17},{2,10},{10... | collective-permute-start | bytes 1179656 | tf_op jit(solution)/shard_map/ppermute | solution.py:528
  115.8 124.0 %reduce-scatter.4.cloned.1.call-start = ((), (), s32[]{:S(2)}) async-start(), calls=%async_computation.4 | async-start | bytes 6881280
  142.0 9.6 %collective-permute-start.22 = (bf16[192,256]{1,0:T(8,128)(2,1)}, bf16[192,256]{1,0:T(8,128)(2,1)S(1)}, u32[]{:S(2)}, u32[]{:S(2)}) collective-permute-start(bf16[192,256]{1,0:T(8,128)(2,1)} %get-tuple-element.132), channel_id=1, source_target_pairs={{0,4},{2,6},{4,0},{6,2},{1,5},{3,7},{5,1},{7,3},{8,12},{10,14},{12... | collective-permute-start | bytes 294920 | tf_op jit(solution)/shard_map/ppermute | solution.py:535
  143.2 10.5 %collective-permute-start.23 = (bf16[192,256]{1,0:T(8,128)(2,1)}, bf16[192,256]{1,0:T(8,128)(2,1)S(1)}, u32[]{:S(2)}, u32[]{:S(2)}) collective-permute-start(bf16[192,256]{1,0:T(8,128)(2,1)} %get-tuple-element.133), channel_id=1, source_target_pairs={{0,6},{2,4},{4,2},{6,0},{1,7},{3,5},{5,3},{7,1},{8,14},{10,12},{12... | collective-permute-start | bytes 294920 | tf_op jit(solution)/shard_map/ppermute | solution.py:535
  144.4 12.9 %collective-permute-start.25 = (bf16[6,256,384]{2,1,0:T(8,128)(2,1)}, bf16[6,256,384]{2,1,0:T(8,128)(2,1)}, u32[]{:S(2)}, u32[]{:S(2)}) collective-permute-start(bf16[6,256,384]{2,1,0:T(8,128)(2,1)} %get-tuple-element.143), channel_id=1, source_target_pairs={{0,1},{1,0},{2,3},{3,2},{4,5},{5,4},{6,7},{7,6},{8,9},{9,8},{10,11... | collective-permute-start | bytes 3538952 | tf_op jit(solution)/shard_map/ppermute | solution.py:525
  147.1 10.2 %collective-permute-start.24 = (bf16[8,256,384]{2,1,0:T(8,128)(2,1)}, bf16[8,256,384]{2,1,0:T(8,128)(2,1)}, u32[]{:S(2)}, u32[]{:S(2)}) collective-permute-start(bf16[8,256,384]{2,1,0:T(8,128)(2,1)} %get-tuple-element.141), channel_id=1, source_target_pairs={{0,1},{1,0},{2,3},{3,2},{4,5},{5,4},{6,7},{7,6},{8,9},{9,8},{10,11... | collective-permute-start | bytes 4718600 | tf_op jit(solution)/shard_map/ppermute | solution.py:525
  151.6 14.2 %collective-permute-start.27 = (bf16[128,768]{1,0:T(8,128)(2,1)}, bf16[128,768]{1,0:T(8,128)(2,1)}, u32[]{:S(2)}, u32[]{:S(2)}) collective-permute-start(bf16[128,768]{1,0:T(8,128)(2,1)} %get-tuple-element.243), channel_id=1, source_target_pairs={{0,16},{8,24},{16,0},{24,8},{1,17},{9,25},{17,1},{25,9},{2,18},{10... | collective-permute-start | bytes 589832 | tf_op jit(solution)/shard_map/ppermute | solution.py:532
  154.7 11.2 %collective-permute-start.29 = (bf16[192,1024]{1,0:T(8,128)(2,1)S(1)}, bf16[192,1024]{1,0:T(8,128)(2,1)S(1)}, u32[]{:S(2)}, u32[]{:S(2)}) collective-permute-start(bf16[192,1024]{1,0:T(8,128)(2,1)S(1)} %slice_dynamic-update-slice_fusion.refs_4_), channel_id=1, source_target_pairs={{0,1},{1,0},{2,3},{3,2},{4,5},{5,4},{6,7},{7,6},{8,9},{9,8},{10,11... | collective-permute-start | bytes 1179656 | tf_op jit(solution)/shard_map/ppermute | solution.py:525
  156.1 33.0 %collective-permute-start.28 = (bf16[192,1024]{1,0:T(8,128)(2,1)S(1)}, bf16[192,1024]{1,0:T(8,128)(2,1)S(1)}, u32[]{:S(2)}, u32[]{:S(2)}) collective-permute-start(bf16[192,1024]{1,0:T(8,128)(2,1)S(1)} %slice_dynamic-update-slice_fusion.refs_4_), channel_id=1, source_target_pairs={{0,8},{8,0},{16,24},{24,16},{1,9},{9,1},{17,25},{25,17},{2,10},{10... | collective-permute-start | bytes 1179656 | tf_op jit(solution)/shard_map/ppermute | solution.py:528
  165.8 171.5 %all-reduce.3.cloned.1.call-start = ((), (), s32[]{:S(2)}) async-start(), calls=%async_computation.1 | async-start | bytes 2064384 | tf_op jit(solution)/shard_map/psum | solution.py:719
  189.1 14.9 %collective-permute-start.31 = (bf16[192,1024]{1,0:T(8,128)(2,1)S(1)}, bf16[192,1024]{1,0:T(8,128)(2,1)S(1)}, u32[]{:S(2)}, u32[]{:S(2)}) collective-permute-start(bf16[192,1024]{1,0:T(8,128)(2,1)S(1)} %collective-permute-done.28.refs_2_), channel_id=1, source_target_pairs={{0,1},{1,0},{2,3},{3,2},{4,5},{5,4},{6,7},{7,6},{8,9},{9,8},{10,11... | collective-permute-start | bytes 1179656 | tf_op jit(solution)/shard_map/ppermute | solution.py:525
  189.4 14.6 %collective-permute-start.30 = (bf16[192,1024]{1,0:T(8,128)(2,1)S(1)}, bf16[192,1024]{1,0:T(8,128)(2,1)S(1)}, u32[]{:S(2)}, u32[]{:S(2)}) collective-permute-start(bf16[192,1024]{1,0:T(8,128)(2,1)S(1)} %get-tuple-element.153), channel_id=1, source_target_pairs={{0,1},{1,0},{2,3},{3,2},{4,5},{5,4},{6,7},{7,6},{8,9},{9,8},{10,11... | collective-permute-start | bytes 1179656 | tf_op jit(solution)/shard_map/ppermute | solution.py:525
  201.3 34.8 %collective-permute-start.36 = (bf16[2,128,768]{2,1,0:T(8,128)(2,1)S(1)}, bf16[2,128,768]{2,1,0:T(8,128)(2,1)S(1)}, u32[]{:S(2)}, u32[]{:S(2)}) collective-permute-start(bf16[2,128,768]{2,1,0:T(8,128)(2,1)S(1)} %pad_maximum_fusion.11), channel_id=1, source_target_pairs={{0,4},{2,6},{4,0},{6,2},{1,5},{3,7},{5,1},{7,3},{8,12},{10,14},{12... | collective-permute-start | bytes 1179656 | tf_op jit(solution)/shard_map/ppermute | solution.py:535
  202.2 34.5 %collective-permute-start.35 = (bf16[2,128,768]{2,1,0:T(8,128)(2,1)S(1)}, bf16[2,128,768]{2,1,0:T(8,128)(2,1)S(1)}, u32[]{:S(2)}, u32[]{:S(2)}) collective-permute-start(bf16[2,128,768]{2,1,0:T(8,128)(2,1)S(1)} %pad_maximum_fusion.11), channel_id=1, source_target_pairs={{0,2},{2,0},{4,6},{6,4},{1,3},{3,1},{5,7},{7,5},{8,10},{10,8},{12,... | collective-permute-start | bytes 1179656 | tf_op jit(solution)/shard_map/ppermute | solution.py:535
  202.8 33.9 %collective-permute-start.37 = (bf16[2,128,768]{2,1,0:T(8,128)(2,1)S(1)}, bf16[2,128,768]{2,1,0:T(8,128)(2,1)S(1)}, u32[]{:S(2)}, u32[]{:S(2)}) collective-permute-start(bf16[2,128,768]{2,1,0:T(8,128)(2,1)S(1)} %pad_maximum_fusion.11), channel_id=1, source_target_pairs={{0,6},{2,4},{4,2},{6,0},{1,7},{3,5},{5,3},{7,1},{8,14},{10,12},{12... | collective-permute-start | bytes 1179656 | tf_op jit(solution)/shard_map/ppermute | solution.py:535
  215.4 10.2 %collective-permute-start.32 = (bf16[192,1024]{1,0:T(8,128)(2,1)S(1)}, bf16[192,1024]{1,0:T(8,128)(2,1)S(1)}, u32[]{:S(2)}, u32[]{:S(2)}) collective-permute-start(bf16[192,1024]{1,0:T(8,128)(2,1)S(1)} %get-tuple-element.158), channel_id=1, source_target_pairs={{0,1},{1,0},{2,3},{3,2},{4,5},{5,4},{6,7},{7,6},{8,9},{9,8},{10,11... | collective-permute-start | bytes 1179656 | tf_op jit(solution)/shard_map/ppermute | solution.py:525
  225.5 11.3 %collective-permute-start.34 = (bf16[2,192,1024]{2,1,0:T(8,128)(2,1)S(1)}, bf16[2,192,1024]{2,1,0:T(8,128)(2,1)S(1)}, u32[]{:S(2)}, u32[]{:S(2)}) collective-permute-start(bf16[2,192,1024]{2,1,0:T(8,128)(2,1)S(1)} %key_backward.4), channel_id=1, source_target_pairs={{0,1},{1,0},{2,3},{3,2},{4,5},{5,4},{6,7},{7,6},{8,9},{9,8},{10,11... | collective-permute-start | bytes 2359304 | tf_op jit(solution)/shard_map/ppermute | solution.py:525
  225.7 11.1 %collective-permute-start.33 = (bf16[192,1024]{1,0:T(8,128)(2,1)S(1)}, bf16[192,1024]{1,0:T(8,128)(2,1)S(1)}, u32[]{:S(2)}, u32[]{:S(2)}) collective-permute-start(bf16[192,1024]{1,0:T(8,128)(2,1)S(1)} %add_convert_fusion.4), channel_id=1, source_target_pairs={{0,8},{8,0},{16,24},{24,16},{1,9},{9,1},{17,25},{25,17},{2,10},{10... | collective-permute-start | bytes 1179656 | tf_op jit(solution)/shard_map/ppermute | solution.py:528
  236.2 23.9 %collective-permute-start.43 = (bf16[4,3,96,768]{3,2,1,0:T(8,128)(2,1)}, bf16[4,3,96,768]{3,2,1,0:T(8,128)(2,1)}, u32[]{:S(2)}, u32[]{:S(2)}) collective-permute-start(bf16[4,3,96,768]{3,2,1,0:T(8,128)(2,1)} %bitcast.35.refs_4_), channel_id=1, source_target_pairs={{0,1},{1,0},{2,3},{3,2},{4,5},{5,4},{6,7},{7,6},{8,9},{9,8},{10,11... | collective-permute-start | bytes 5308424 | tf_op jit(solution)/shard_map/ppermute | solution.py:525
  237.9 22.1 %collective-permute-start.39 = (bf16[2,192,1024]{2,1,0:T(8,128)(2,1)}, bf16[2,192,1024]{2,1,0:T(8,128)(2,1)}, u32[]{:S(2)}, u32[]{:S(2)}) collective-permute-start(bf16[2,192,1024]{2,1,0:T(8,128)(2,1)} %add_convert_fusion.1), channel_id=1, source_target_pairs={{0,8},{8,0},{16,24},{24,16},{1,9},{9,1},{17,25},{25,17},{2,10},{10... | collective-permute-start | bytes 2359304 | tf_op jit(solution)/shard_map/ppermute | solution.py:528
  249.7 12.5 %collective-permute-start.38 = (bf16[2,192,1024]{2,1,0:T(8,128)(2,1)S(1)}, bf16[2,192,1024]{2,1,0:T(8,128)(2,1)}, u32[]{:S(2)}, u32[]{:S(2)}) collective-permute-start(bf16[2,192,1024]{2,1,0:T(8,128)(2,1)S(1)} %key_backward.7), channel_id=1, source_target_pairs={{0,1},{1,0},{2,3},{3,2},{4,5},{5,4},{6,7},{7,6},{8,9},{9,8},{10,11... | collective-permute-start | bytes 2359304 | tf_op jit(solution)/shard_map/ppermute | solution.py:525
  261.2 25.6 %collective-permute-start.53 = (bf16[112,768]{1,0:T(8,128)(2,1)S(1)}, bf16[112,768]{1,0:T(8,128)(2,1)S(1)}, u32[]{:S(2)}, u32[]{:S(2)}) collective-permute-start(bf16[112,768]{1,0:T(8,128)(2,1)S(1)} %constant_dynamic-slice_fusion), channel_id=1, source_target_pairs={{0,8},{8,0},{16,24},{24,16},{1,9},{9,1},{17,25},{25,17},{2,10},{10... | collective-permute-start | bytes 516104 | tf_op jit(solution)/shard_map/ppermute | solution.py:528
  264.4 9.3 %collective-permute-start.42 = (bf16[3,192,256]{2,1,0:T(8,128)(2,1)S(1)}, bf16[3,192,256]{2,1,0:T(8,128)(2,1)S(1)}, u32[]{:S(2)}, u32[]{:S(2)}) collective-permute-start(bf16[3,192,256]{2,1,0:T(8,128)(2,1)S(1)} %pad_maximum_fusion.16), channel_id=1, source_target_pairs={{0,6},{2,4},{4,2},{6,0},{1,7},{3,5},{5,3},{7,1},{8,14},{10,12},{12... | collective-permute-start | bytes 884744 | tf_op jit(solution)/shard_map/ppermute | solution.py:535
  265.7 15.0 %collective-permute-start.41 = (bf16[3,192,256]{2,1,0:T(8,128)(2,1)S(1)}, bf16[3,192,256]{2,1,0:T(8,128)(2,1)S(1)}, u32[]{:S(2)}, u32[]{:S(2)}) collective-permute-start(bf16[3,192,256]{2,1,0:T(8,128)(2,1)S(1)} %pad_maximum_fusion.15), channel_id=1, source_target_pairs={{0,4},{2,6},{4,0},{6,2},{1,5},{3,7},{5,1},{7,3},{8,12},{10,14},{12... | collective-permute-start | bytes 884744 | tf_op jit(solution)/shard_map/ppermute | solution.py:535
  266.8 13.9 %collective-permute-start.40 = (bf16[3,192,256]{2,1,0:T(8,128)(2,1)S(1)}, bf16[3,192,256]{2,1,0:T(8,128)(2,1)S(1)}, u32[]{:S(2)}, u32[]{:S(2)}) collective-permute-start(bf16[3,192,256]{2,1,0:T(8,128)(2,1)S(1)} %pad_maximum_fusion.14), channel_id=1, source_target_pairs={{0,2},{2,0},{4,6},{6,4},{1,3},{3,1},{5,7},{7,5},{8,10},{10,8},{12,... | collective-permute-start | bytes 884744 | tf_op jit(solution)/shard_map/ppermute | solution.py:535
  268.4 21.2 %collective-permute-start.45 = (bf16[288,768]{1,0:T(8,128)(2,1)S(1)}, bf16[288,768]{1,0:T(8,128)(2,1)S(1)}, u32[]{:S(2)}, u32[]{:S(2)}) collective-permute-start(bf16[288,768]{1,0:T(8,128)(2,1)S(1)} %constant_dynamic-slice_fusion.2), channel_id=1, source_target_pairs={{0,1},{1,0},{2,3},{3,2},{4,5},{5,4},{6,7},{7,6},{8,9},{9,8},{10,11... | collective-permute-start | bytes 1327112 | tf_op jit(solution)/shard_map/ppermute | solution.py:525
  287.8 17.8 %collective-permute-start.44 = (bf16[128,768]{1,0:T(8,128)(2,1)S(1)}, bf16[128,768]{1,0:T(8,128)(2,1)S(1)}, u32[]{:S(2)}, u32[]{:S(2)}) collective-permute-start(bf16[128,768]{1,0:T(8,128)(2,1)S(1)} %get-tuple-element.241), channel_id=1, source_target_pairs={{0,16},{8,24},{16,0},{24,8},{1,17},{9,25},{17,1},{25,9},{2,18},{10... | collective-permute-start | bytes 589832 | tf_op jit(solution)/shard_map/ppermute | solution.py:532
  289.8 15.9 %collective-permute-start.46 = (bf16[144,768]{1,0:T(8,128)(2,1)S(1)}, bf16[144,768]{1,0:T(8,128)(2,1)S(1)}, u32[]{:S(2)}, u32[]{:S(2)}) collective-permute-start(bf16[144,768]{1,0:T(8,128)(2,1)S(1)} %constant_dynamic-slice_fusion.1), channel_id=1, source_target_pairs={{0,8},{8,0},{16,24},{24,16},{1,9},{9,1},{17,25},{25,17},{2,10},{10... | collective-permute-start | bytes 663560 | tf_op jit(solution)/shard_map/ppermute | solution.py:528
  290.6 36.5 %collective-permute-start.54 = (bf16[112,768]{1,0:T(8,128)(2,1)S(1)}, bf16[112,768]{1,0:T(8,128)(2,1)S(1)}, u32[]{:S(2)}, u32[]{:S(2)}) collective-permute-start(bf16[112,768]{1,0:T(8,128)(2,1)S(1)} %fusion.7), channel_id=1, source_target_pairs={{0,16},{8,24},{16,0},{24,8},{1,17},{9,25},{17,1},{25,9},{2,18},{10... | collective-permute-start | bytes 516104 | tf_op jit(solution)/shard_map/ppermute | solution.py:532
  305.7 31.6 %collective-permute-start.47 = (bf16[2,128,768]{2,1,0:T(8,128)(2,1)S(1)}, bf16[2,128,768]{2,1,0:T(8,128)(2,1)S(1)}, u32[]{:S(2)}, u32[]{:S(2)}) collective-permute-start(bf16[2,128,768]{2,1,0:T(8,128)(2,1)S(1)} %pad_maximum_fusion.12), channel_id=1, source_target_pairs={{0,2},{2,0},{4,6},{6,4},{1,3},{3,1},{5,7},{7,5},{8,10},{10,8},{12,... | collective-permute-start | bytes 1179656 | tf_op jit(solution)/shard_map/ppermute | solution.py:535
  306.8 30.5 %collective-permute-start.48 = (bf16[2,128,768]{2,1,0:T(8,128)(2,1)S(1)}, bf16[2,128,768]{2,1,0:T(8,128)(2,1)}, u32[]{:S(2)}, u32[]{:S(2)}) collective-permute-start(bf16[2,128,768]{2,1,0:T(8,128)(2,1)S(1)} %pad_maximum_fusion.12), channel_id=1, source_target_pairs={{0,4},{2,6},{4,0},{6,2},{1,5},{3,7},{5,1},{7,3},{8,12},{10,14},{12... | collective-permute-start | bytes 1179656 | tf_op jit(solution)/shard_map/ppermute | solution.py:535
  307.2 30.1 %collective-permute-start.49 = (bf16[2,128,768]{2,1,0:T(8,128)(2,1)S(1)}, bf16[2,128,768]{2,1,0:T(8,128)(2,1)}, u32[]{:S(2)}, u32[]{:S(2)}) collective-permute-start(bf16[2,128,768]{2,1,0:T(8,128)(2,1)S(1)} %pad_maximum_fusion.12), channel_id=1, source_target_pairs={{0,6},{2,4},{4,2},{6,0},{1,7},{3,5},{5,3},{7,1},{8,14},{10,12},{12... | collective-permute-start | bytes 1179656 | tf_op jit(solution)/shard_map/ppermute | solution.py:535
  308.4 28.6 %collective-permute-start.50 = (bf16[144,768]{1,0:T(8,128)(2,1)S(1)}, bf16[144,768]{1,0:T(8,128)(2,1)S(1)}, u32[]{:S(2)}, u32[]{:S(2)}) collective-permute-start(bf16[144,768]{1,0:T(8,128)(2,1)S(1)} %fusion.6), channel_id=1, source_target_pairs={{0,16},{8,24},{16,0},{24,8},{1,17},{9,25},{17,1},{25,9},{2,18},{10... | collective-permute-start | bytes 663560 | tf_op jit(solution)/shard_map/ppermute | solution.py:532
  327.1 9.9 %collective-permute-start.55 = (bf16[112,768]{1,0:T(8,128)(2,1)S(1)}, bf16[112,768]{1,0:T(8,128)(2,1)S(1)}, u32[]{:S(2)}, u32[]{:S(2)}) collective-permute-start(bf16[112,768]{1,0:T(8,128)(2,1)S(1)} %add_convert_fusion.8), channel_id=1, source_target_pairs={{0,8},{8,0},{16,24},{24,16},{1,9},{9,1},{17,25},{25,17},{2,10},{10... | collective-permute-start | bytes 516104 | tf_op jit(solution)/shard_map/ppermute | solution.py:528
  338.6 13.7 %collective-permute-start.56 = (bf16[896,768]{1,0:T(8,128)(2,1)S(1)}, bf16[896,768]{1,0:T(8,128)(2,1)S(1)}, u32[]{:S(2)}, u32[]{:S(2)}) collective-permute-start(bf16[896,768]{1,0:T(8,128)(2,1)S(1)} %pad_maximum_fusion.4.near), channel_id=1, source_target_pairs={{0,1},{1,0},{2,3},{3,2},{4,5},{5,4},{6,7},{7,6},{8,9},{9,8},{10,11... | collective-permute-start | bytes 4128776 | tf_op jit(solution)/shard_map/ppermute | solution.py:525
  (67 other events, 530.0 us)
Sparse Core Ops, SparseCore 0:
  32.3 64.0 all-gather.4
  115.9 37.5 all-gather.6
  165.9 72.1 reduce-scatter.3
  262.3 67.8 all-reduce.2

commit v14 on v11

--- a/solution.py
+++ b/solution.py
@@ -704,7 +704,7 @@
         signed, signed_t, bits, head_n, near_o, after(kv_o, dkv_far, grad_q, weight_sum, *layer_moved),
         grad_tables, bf16, 25,
     )
-    weight_sum = lax.psum(weight_sum, "hash")
+    weight_sum = lax.psum_scatter(weight_sum, "hash", scatter_dimension=0, tiled=True)
     dkv_far = over_place(dkv_far)
     dkv_o_moved = over_seq(dkv_o)
     dkv = key_backward(
@@ -716,7 +716,7 @@
     grad_qkv = jnp.concatenate([grad_q[None], grad_kv])
     qkv_parts = to_dense(grad_qkv)
 
-    grad_in = input_grad(core, grad_first, qkv_parts, w_qkv_t, after(w_qkv_far, dkv))
+    grad_in = input_grad(core, after(grad_first, weight_sum), qkv_parts, w_qkv_t, after(w_qkv_far, dkv))
 
     def in_halves(index, mine, other):
         first = jnp.where(index == 0, mine, other)
@@ -759,6 +759,8 @@
     w_grad = in_halves(r, w_keep, over_place(w_keep))
     w_grad = in_halves(s, w_grad, over_seq(w_grad)).reshape(3, head_width, width)
     grad_w_qkv = w_grad.transpose(0, 2, 1).astype(f32)
+    weight_sum = after(weight_sum, grad_in)
+    weight_sum = lax.all_gather(weight_sum, "hash", axis=0, tiled=True)
     weight_sum = after(weight_sum, *grad_moved)
     weight_far = over_seq(weight_sum)
     grad_w_up, grad_w_down, grad_w_out = weight_results(core, weight_sum, weight_far, head_width)

time: 363 us -> 398 us (1.096)
  waiting for transfers between devices: 58.3 us -> 85.9 us
  starting transfers between devices: 53.3 us -> 60.1 us
    ppermute x9, waiting for transfers between devices: 5.11 us -> 28.3 us  [over_place(): return lax.ppermute(x, 'hash', [(h, h ^ 1) for h in range(hash_count)])]
    ppermute x18, waiting for transfers between devices: 14.1 us -> 30.9 us  [over_head(): return lax.ppermute(x, 'head', [(h, h ^ j) for h in range(head_count)])]
    ppermute x22, starting transfers between devices: 16.9 us -> 28 us  [over_seq(): return lax.ppermute(x, 'seq', [(0, 1), (1, 0)])]
    ppermute x4, waiting for transfers between devices: 29 us -> 20.5 us  [over_group(): return lax.ppermute(x, 'hash', moves)]
    psum x1 -> x0, waiting for transfers between devices: 6.02 us -> none  [shards(): weight_sum = lax.psum(weight_sum, 'hash')]
    unnamed x118 -> x114, local copies, waits for them, and re-layouts: 19.1 us -> 21.8 us
  transfers between devices with their start and end apart: 58 -> 59, of which waited for: 12 -> 17; matrix products, arithmetic and copies ran while one was open for 14% -> 12% of each run, Pallas kernels for 45% -> 41%
where the time goes in v14:
time: 398 us; the launch traced here: 393 us
  Pallas kernels  164 us (41%)
  waiting for transfers between devices  85.9 us (22%)
  starting transfers between devices  60.1 us (15%)
  local copies, waits for them, and re-layouts  40.5 us (10%)
  other arithmetic  22.8 us (6%)
  between operations  15.4 us (4%)
  matrix products  4.14 us (1%)
    pallas_call x5, Pallas kernels, single(): pl.pallas_call(kernel, in_specs=[pl.BlockSpec(memory_space=pltpu.SMEM)] +...  43.4 us
    pallas_call x3, Pallas kernels, query_backward(): call(partial(query_back_kernel, chunk=4, blocks=blocks, last=last), heads...  43.2 us
    pallas_call x4, Pallas kernels, key_backward(): call(partial(key_back_kernel, chunk=4), heads, micros, 'key_backward', [w...  38 us
    ppermute x18, waiting for transfers between devices, over_head(): return lax.ppermute(x, 'head', [(h, h ^ j) for h in range(head_count)])  30.9 us
    ppermute x9, waiting for transfers between devices, over_place(): return lax.ppermute(x, 'hash', [(h, h ^ 1) for h in range(hash_count)])  28.3 us
    ppermute x22, starting transfers between devices, over_seq(): return lax.ppermute(x, 'seq', [(0, 1), (1, 0)])  28 us
    pallas_call x5, Pallas kernels, key_tables(): call(partial(key_kernel, chunk=2, blocks=len(blocks)), heads, 30 if len(b...  23.5 us
    unnamed x114, local copies, waits for them, and re-layouts  21.8 us
  transfers between devices with their start and end apart: 59, of which 17 were waited for; matrix products, arithmetic and copies ran while one was open for 12% of the time, Pallas kernels for 41%

profile of v14, /device:TPU:1, one launch (start us, length us, event | category | flops | bytes accessed | tf_op | source)
XLA Modules:
  0.0 392.8 jit_solution(9974611274595597171)
XLA Ops:
  7.3 4.5 %constant_dynamic-slice_fusion.7 = (bf16[1,128,1,768]{3,2,1,0:T(2,128)(2,1)S(1)}, bf16[1,128,1,768]{3,2,1,0:T(2,128)(2,1)}, bf16[1,128,1,768]{3,2,1,0:T(2,128)(2...) fusion(bf16[1,512,2,768]{3,2,1,0:T(2,128)(2,1)} %param.11, s32[]{:T(128)S(6)} %select_n.222, ...), kind=kLoop, calls=%fused_computation.121 | loop fusion | bytes 1966104 | tf_op jit(solution)/shard_map/jit(dynamic_index_in_dim)/dynamic_slice | solution.py:529
  12.6 3.1 collective-permute-start
  16.3 2.5 collective-permute-start.1
  20.5 2.4 copy.54
  24.7 1.9 dynamic-slice_bitcast_fusion
  37.1 1.9 slice.118
  40.7 5.3 %key_tables.5.refs_4_ = f32[3,2048,64]{2,1,0:T(8,128)S(1)} custom-call(bf16[64,64]{1,0:T(8,128)(2,1)S(1)} %bitcast.129, bf16[576,512]{1,0:T(8,128)(2,1)} %bitcast.14.refs_0_.refs_2_.ka.va, bf16[576,512]{1,0:T(8,128)(2,1)} %collective-permute-done.2.refs_1_.refs_3_.refs_0_.refs_2_.ka.va, bf16[576,512]{1,0:T(8,128)(2,1)} %bitcast.14.refs_0_.refs_2_.ka.va, ...), custom_call_target="tpu_custom_call" | custom-call | flops 1100000000 | bytes 1048576 | tf_op jit(solution)/shard_map/key_tables/pallas_call | solution.py:192
  46.0 2.1 pad_maximum_fusion.7
  49.1 1.9 collective-permute-start.8
  53.4 5.8 %key_tables.6.refs_4_ = f32[3,2048,64]{2,1,0:T(8,128)S(1)} custom-call(bf16[64,64]{1,0:T(8,128)(2,1)S(1)} %bitcast.130, bf16[576,512]{1,0:T(8,128)(2,1)} %collective-permute-done.9.refs_0_.refs_2_.ka.va, bf16[576,512]{1,0:T(8,128)(2,1)S(1)} %collective-permute-done.10.refs_1_.refs_3_.refs_0_.ka.va, ...), custom_call_target="tpu_custom_call" | custom-call | flops 32999999488 | bytes 1048576 | tf_op jit(solution)/shard_map/key_tables/pallas_call | solution.py:192
  60.8 5.6 %key_tables.7.refs_2_ = f32[3,2048,64]{2,1,0:T(8,128)S(1)} custom-call(bf16[64,64]{1,0:T(8,128)(2,1)S(1)} %bitcast.131, bf16[384,512]{1,0:T(8,128)(2,1)S(1)} %bitcast.125, bf16[384,512]{1,0:T(8,128)(2,1)S(1)} %collective-permute-done.8.refs_1_.refs_3_.kb.vb, bf16[384,512]{1,0:T(8,128)(2,1)S(1)} %bitcast.126, ...), custom_call_target="tpu_custom_call" | custom-call | flops 32999999488 | bytes 1048576 | tf_op jit(solution)/shard_map/key_tables/pallas_call | solution.py:192
  71.5 4.2 %key_tables.8.refs_2_ = f32[3,2048,64]{2,1,0:T(8,128)S(1)} custom-call(bf16[64,64]{1,0:T(8,128)(2,1)S(1)} %bitcast.132, bf16[384,512]{1,0:T(8,128)(2,1)S(1)} %collective-permute-done.7.refs_0_.refs_1_.kb.vb, bf16[384,512]{1,0:T(8,128)(2,1)S(1)} %collective-permute-done.7.refs_0_.refs_1_.kb.vb, f32[3,2048,64]{2,1,0:T(8,128)} %copy-done.2), custom_call_target="tpu_custom_call" | custom-call | flops 1100000000 | bytes 1048576 | tf_op jit(solution)/shard_map/key_tables/pallas_call | solution.py:192
  76.3 2.6 key_tables.9.tables
  79.0 3.3 query_estimates.4
  82.9 4.1 %query_estimates.5 = bf16[192,1024]{1,0:T(8,128)(2,1)S(1)} custom-call(bf16[64,64]{1,0:T(8,128)(2,1)S(1)} %bitcast.135, bf16[3,2048,64]{2,1,0:T(8,128)(2,1)S(1)} %key_tables.9.tables, bf16[576,512]{1,0:T(8,128)(2,1)} %collective-permute-done.9.refs_0_.refs_2_.ka.va, bf16[192,512]{1,0:T(8,128)(2,1)S(1)} %collective-permute-done.6.refs_1_), custom_call_target="tpu_custom_call" | custom-call | flops 1100000000 | bytes 1048576 | tf_op jit(solution)/shard_map/query_estimates/pallas_call | solution.py:205
  87.2 4.2 %query_estimates.6 = bf16[192,1024]{1,0:T(8,128)(2,1)S(1)} custom-call(bf16[64,64]{1,0:T(8,128)(2,1)S(1)} %bitcast.136, bf16[3,2048,64]{2,1,0:T(8,128)(2,1)S(1)} %key_tables.9.tables, bf16[576,512]{1,0:T(8,128)(2,1)} %collective-permute-done.2.refs_1_.refs_3_.refs_0_.refs_2_.ka.va, bf16[192,512]{1,0:T(8,128)(2,1)S(1)} %collective-permute-done.12.refs_1_.refs_3_), custom_call_target="tpu_custom_call" | custom-call | flops 1100000000 | bytes 1048576 | tf_op jit(solution)/shard_map/query_estimates/pallas_call | solution.py:205
  92.0 4.3 %all-gather.8.cloned.1.call-done = bf16[3456,768]{1,0:T(8,128)(2,1)} async-done(((bf16[864,768]{1,0:T(8,128)(2,1)}), bf16[3456,768]{1,0:T(8,128)(2,1)}) %all-gather.8.cloned.1.call-update) | async-done | bytes 5308432 | tf_op jit(solution)/shard_map/all_gather | solution.py:564
  98.9 1.8 dynamic-slice_bitcast_fusion.1
  100.9 4.2 %query_estimates.7 = f32[192,1024]{1,0:T(8,128)S(1)} custom-call(bf16[64,64]{1,0:T(8,128)(2,1)S(1)} %bitcast.138, bf16[3,2048,64]{2,1,0:T(8,128)(2,1)S(1)} %key_tables.9.tables, bf16[576,512]{1,0:T(8,128)(2,1)} %bitcast.14.refs_0_.refs_2_.ka.va, bf16[192,512]{1,0:T(8,128)(2,1)S(1)} %convolution_convert_fusion.1.refs_1_), custom_call_target="tpu_custom_call" | custom-call | flops 1100000000 | bytes 1048576 | tf_op jit(solution)/shard_map/query_estimates/pallas_call | solution.py:205
  105.0 2.2 collective-permute-done.16
  116.4 12.7 %dense.1 = (bf16[256,768]{1,0:T(8,128)(2,1)}, f32[256,768]{1,0:T(8,128)}, f32[256,768]{1,0:T(8,128)}, f32[8,256,384]{2,1,0:T(8,128)}, bf16[8,256,384]{2,1,0:T(8,...) custom-call(s32[2]{0:T(128)} %pad_add_fusion.core, ...), custom_call_target="tpu_custom_call" | custom-call | flops 15399999488 | bytes 1048576 | tf_op jit(solution)/shard_map/dense/pallas_call | solution.py:402
  129.1 12.6 %dense_back.1 = (f32[256,768]{1,0:T(8,128)}, bf16[6,256,384]{2,1,0:T(8,128)(2,1)}, bf16[6,256,384]{2,1,0:T(8,128)(2,1)}, bf16[192,256]{1,0:T(8,128)(2,1)}, bf16[...) custom-call(s32[2]{0:T(128)} %pad_add_fusion.core, ...), custom_call_target="tpu_custom_call" | custom-call | flops 8800000000 | bytes 1048576 | tf_op jit(solution)/shard_map/dense_back/pallas_call | solution.py:402
  144.4 2.8 collective-permute-start.25
  148.7 2.9 collective-permute-start.26
  151.6 2.1 collective-permute-start.27
  157.3 8.2 %weight_grads.1 = bf16[4,896,768]{2,1,0:T(8,128)(2,1)} custom-call(s32[2]{0:T(128)} %pad_add_fusion.core, f32[8,768]{1,0:T(8,128)} %get-tuple-element.138.small_a, f32[8,768]{1,0:T(8,128)} %get-tuple-element.139.small_b, bf16[8,256,384]{2,1,0:T(8,128)(2,1)} %get-tuple-element.140.refs_0_, bf16[8,256,384]{2,1,0:T(8,128)(2,1)} %collective-permute-done.24.refs_1_, ...), custom_call_target="tpu_custom_call" | custom-call | flops 7699999744 | bytes 1048576 | tf_op jit(solution)/shard_map/weight_grads/pallas_call | solution.py:402
  168.8 20.2 %query_backward.3 = (f32[3,2048,64]{2,1,0:T(8,128)}, f32[192,1024]{1,0:T(8,128)S(1)}, bf16[192,1024]{1,0:T(8,128)(2,1)S(1)}) custom-call(bf16[64,64]{1,0:T(8,128)(2,1)S(1)} %bitcast.139, bf16[64,128]{1,0:T(8,128)(2,1)S(1)} %pad_maximum_fusion.20.planes_t, bf16[80,2048]{1,0:T(8,128)(2,1)S(1)} %copy-done.16, bf16[3,2048,64]{2,1,0:T(8,128)(2,1)S(1)} %key_tables.9.tables, ...), custom_call_target="tpu_custom_call" | custom-call | flops 54999998464 | bytes 1048576 | tf_op jit(solution)/shard_map/query_backward/pallas_call | solution.py:229
  189.5 11.7 %query_backward.4 = (f32[3,2048,64]{2,1,0:T(8,128)}, f32[192,1024]{1,0:T(8,128)S(1)}) custom-call(bf16[64,64]{1,0:T(8,128)(2,1)S(1)} %bitcast.140, bf16[64,128]{1,0:T(8,128)(2,1)S(1)} %pad_maximum_fusion.20.planes_t, bf16[80,2048]{1,0:T(8,128)(2,1)S(1)} %copy-done.16, bf16[3,2048,64]{2,1,0:T(8,128)(2,1)S(1)} %key_tables.9.tables, ...), custom_call_target="tpu_custom_call" | custom-call | flops 27499999232 | bytes 1048576 | tf_op jit(solution)/shard_map/query_backward/pallas_call | solution.py:229
  204.1 11.2 %query_backward.5 = (bf16[3,2048,64]{2,1,0:T(8,128)(2,1)S(1)}, bf16[192,1024]{1,0:T(8,128)(2,1)S(1)}) custom-call(bf16[64,64]{1,0:T(8,128)(2,1)S(1)} %bitcast.141, bf16[64,128]{1,0:T(8,128)(2,1)S(1)} %pad_maximum_fusion.20.planes_t, bf16[80,2048]{1,0:T(8,128)(2,1)S(1)} %copy-done.16, bf16[3,2048,64]{2,1,0:T(8,128)(2,1)S(1)} %key_tables.9.tables, ...), custom_call_target="tpu_custom_call" | custom-call | flops 27499999232 | bytes 1048576 | tf_op jit(solution)/shard_map/query_backward/pallas_call | solution.py:229
  216.6 8.7 %key_backward.4 = bf16[2,192,1024]{2,1,0:T(8,128)(2,1)S(1)} custom-call(bf16[64,64]{1,0:T(8,128)(2,1)S(1)} %bitcast.142, bf16[64,128]{1,0:T(8,128)(2,1)S(1)} %pad_maximum_fusion.20.planes_t, bf16[80,2048]{1,0:T(8,128)(2,1)S(1)} %copy-done.17, bf16[576,512]{1,0:T(8,128)(2,1)S(1)} %copy-done.11, bf16[384,512]{1,0:T(8,128)(2,1)S(1)} %copy-done.7, ...), custom_call_target="tpu_custom_call" | custom-call | flops 27499999232 | bytes 1048576 | tf_op jit(solution)/shard_map/key_backward/pallas_call | solution.py:243
  226.4 9.7 %key_backward.5 = bf16[2,192,1024]{2,1,0:T(8,128)(2,1)S(1)} custom-call(bf16[64,64]{1,0:T(8,128)(2,1)S(1)} %bitcast.143, bf16[64,128]{1,0:T(8,128)(2,1)S(1)} %pad_maximum_fusion.20.planes_t, bf16[80,2048]{1,0:T(8,128)(2,1)S(1)} %copy-done.17, bf16[576,512]{1,0:T(8,128)(2,1)} %collective-permute-done.9.refs_0_.refs_2_.ka.va, bf16[384,512]{1,0:T(8,128)(2,1)S(1)} %copy-done.5, ...), custom_call_target="tpu_custom_call" | custom-call | flops 27499999232 | bytes 1048576 | tf_op jit(solution)/shard_map/key_backward/pallas_call | solution.py:243
  239.8 9.9 %key_backward.7 = bf16[2,192,1024]{2,1,0:T(8,128)(2,1)S(1)} custom-call(bf16[64,64]{1,0:T(8,128)(2,1)S(1)} %bitcast.144, bf16[64,128]{1,0:T(8,128)(2,1)S(1)} %pad_maximum_fusion.20.planes_t, bf16[80,2048]{1,0:T(8,128)(2,1)S(1)} %copy-done.18, bf16[576,512]{1,0:T(8,128)(2,1)} %collective-permute-done.2.refs_1_.refs_3_.refs_0_.refs_2_.ka.va, ...), custom_call_target="tpu_custom_call" | custom-call | flops 27499999232 | bytes 1048576 | tf_op jit(solution)/shard_map/key_backward/pallas_call | solution.py:243
  250.9 9.7 %key_backward.6 = f32[2,192,1024]{2,1,0:T(8,128)S(1)} custom-call(bf16[64,64]{1,0:T(8,128)(2,1)S(1)} %bitcast.145, bf16[64,128]{1,0:T(8,128)(2,1)S(1)} %pad_maximum_fusion.20.planes_t, bf16[80,2048]{1,0:T(8,128)(2,1)S(1)} %copy-done.18, bf16[576,512]{1,0:T(8,128)(2,1)} %bitcast.14.refs_0_.refs_2_.ka.va, bf16[384,512]{1,0:T(8,128)(2,1)S(1)} %bitcast.127, ...), custom_call_target="tpu_custom_call" | custom-call | flops 27499999232 | bytes 1048576 | tf_op jit(solution)/shard_map/key_backward/pallas_call | solution.py:243
  260.7 8.7 %collective-permute-done.39 = bf16[2,192,1024]{2,1,0:T(8,128)(2,1)} collective-permute-done((bf16[2,192,1024]{2,1,0:T(8,128)(2,1)}, bf16[2,192,1024]{2,1,0:T(8,128)(2,1)}, u32[]{:S(2)}, u32[]{:S(2)}) %collective-permute-start.39) | collective-permute-done | bytes 786464 | tf_op jit(solution)/shard_map/ppermute | solution.py:519
  273.4 8.5 %collective-permute-start.45 = (bf16[288,768]{1,0:T(8,128)(2,1)S(1)}, bf16[288,768]{1,0:T(8,128)(2,1)S(1)}, u32[]{:S(2)}, u32[]{:S(2)}) collective-permute-start(bf16[288,768]{1,0:T(8,128)(2,1)S(1)} %constant_dynamic-slice_fusion.1), channel_id=1, source_target_pairs={{0,1},{1,0},{2,3},{3,2},{4,5},{5,4},{6,7},{7,6},{8,9},{9,8},{10,11... | collective-permute-start | bytes 1327112 | tf_op jit(solution)/shard_map/ppermute | solution.py:516
  283.0 2.6 collective-permute-start.41
  286.7 5.1 %collective-permute-done.42.refs_3_ = bf16[3,192,256]{2,1,0:T(8,128)(2,1)S(1)} collective-permute-done((bf16[3,192,256]{2,1,0:T(8,128)(2,1)S(1)}, bf16[3,192,256]{2,1,0:T(8,128)(2,1)S(1)}, u32[]{:S(2)}, u32[]{:S(2)}) %collective-permute-start.42) | collective-permute-done | bytes 294944 | tf_op jit(solution)/shard_map/ppermute | solution.py:526
  291.8 6.7 %collective-permute-done.41.refs_2_ = bf16[3,192,256]{2,1,0:T(8,128)(2,1)} collective-permute-done((bf16[3,192,256]{2,1,0:T(8,128)(2,1)S(1)}, bf16[3,192,256]{2,1,0:T(8,128)(2,1)}, u32[]{:S(2)}, u32[]{:S(2)}) %collective-permute-start.41) | collective-permute-done | bytes 294944 | tf_op jit(solution)/shard_map/ppermute | solution.py:526
  299.1 5.2 %input_grad.1 = bf16[256,768]{1,0:T(8,128)(2,1)} custom-call(s32[2]{0:T(128)} %pad_add_fusion.core, f32[256,768]{1,0:T(8,128)} %get-tuple-element.165.grad_first, bf16[3,192,256]{2,1,0:T(8,128)(2,1)} %pad_maximum_fusion.12.refs_0_, bf16[3,192,256]{2,1,0:T(8,128)(2,1)} %collective-permute-done.40.refs_1_, ...), custom_call_target="tpu_custom_call" | custom-call | flops 44000002048 | bytes 1048576 | tf_op jit(solution)/shard_map/input_grad/pallas_call | solution.py:402
  304.4 7.1 %collective-permute-done.50 = bf16[144,768]{1,0:T(8,128)(2,1)S(1)} collective-permute-done((bf16[144,768]{1,0:T(8,128)(2,1)S(1)}, bf16[144,768]{1,0:T(8,128)(2,1)S(1)}, u32[]{:S(2)}, u32[]{:S(2)}) %collective-permute-start.50) | collective-permute-done | bytes 221216 | tf_op jit(solution)/shard_map/ppermute | solution.py:523
  311.7 17.4 %collective-permute-done.51 = bf16[144,768]{1,0:T(8,128)(2,1)S(1)} collective-permute-done((bf16[144,768]{1,0:T(8,128)(2,1)S(1)}, bf16[144,768]{1,0:T(8,128)(2,1)S(1)}, u32[]{:S(2)}, u32[]{:S(2)}) %collective-permute-start.51) | collective-permute-done | bytes 221216 | tf_op jit(solution)/shard_map/ppermute | solution.py:519
  329.1 3.6 collective-permute-start.52
  334.4 13.4 %collective-permute-done.44 = bf16[128,768]{1,0:T(8,128)(2,1)S(1)} collective-permute-done((bf16[128,768]{1,0:T(8,128)(2,1)S(1)}, bf16[128,768]{1,0:T(8,128)(2,1)S(1)}, u32[]{:S(2)}, u32[]{:S(2)}) %collective-permute-start.44) | collective-permute-done | bytes 196640 | tf_op jit(solution)/shard_map/ppermute | solution.py:523
  352.1 6.0 %collective-permute-done.47 = bf16[2,128,768]{2,1,0:T(8,128)(2,1)S(1)} collective-permute-done((bf16[2,128,768]{2,1,0:T(8,128)(2,1)S(1)}, bf16[2,128,768]{2,1,0:T(8,128)(2,1)S(1)}, u32[]{:S(2)}, u32[]{:S(2)}) %collective-permute-start.47) | collective-permute-done | bytes 393248 | tf_op jit(solution)/shard_map/ppermute | solution.py:526
  359.2 8.5 %collective-permute-done.49 = bf16[2,128,768]{2,1,0:T(8,128)(2,1)} collective-permute-done((bf16[2,128,768]{2,1,0:T(8,128)(2,1)S(1)}, bf16[2,128,768]{2,1,0:T(8,128)(2,1)}, u32[]{:S(2)}, u32[]{:S(2)}) %collective-permute-start.49) | collective-permute-done | bytes 393248 | tf_op jit(solution)/shard_map/ppermute | solution.py:526
  369.8 2.8 copy.56
  374.3 4.1 %copy.57 = f32[1,512,2,768]{3,2,1,0:T(2,128)} copy(f32[1,512,2,768]{3,1,2,0:T(8,128)S(1)} %maximum_convert_fusion) | data formatting | bytes 6291456
  381.1 4.7 %weight_results.1 = (f32[768,768]{1,0:T(8,128)}, f32[768,768]{1,0:T(8,128)}, f32[192,768]{1,0:T(8,128)}) custom-call(s32[2]{0:T(128)} %pad_add_fusion.core, bf16[896,768]{1,0:T(8,128)(2,1)} %all-gather.6.cloned.1.call-done.near, bf16[896,768]{1,0:T(8,128)(2,1)} %copy-done.45), custom_call_target="tpu_custom_call" | custom-call | flops 3300000000 | bytes 1048576 | tf_op jit(solution)/shard_map/weight_results/pallas_call | solution.py:402
  (286 shorter events, 82.5 us)
Async XLA Ops:
  7.2 89.1 %all-gather.8.cloned.1.call-start = ((), (), s32[]{:S(2)}) async-start(), calls=%async_computation.4 | async-start | bytes 6635520 | tf_op jit(solution)/shard_map/all_gather | solution.py:564
  12.6 16.4 %collective-permute-start = (bf16[128,768]{1,0:T(8,128)(2,1)}, bf16[128,768]{1,0:T(8,128)(2,1)}, u32[]{:S(2)}, u32[]{:S(2)}) collective-permute-start(bf16[128,768]{1,0:T(8,128)(2,1)} %bitcast.121), channel_id=1, source_target_pairs={{0,16},{8,24},{16,0},{24,8},{1,17},{9,25},{17,1},{25,9},{2,18},{10... | collective-permute-start | bytes 589832 | tf_op jit(solution)/shard_map/ppermute | solution.py:523
  16.3 19.9 %collective-permute-start.1 = (bf16[8,8,64]{2,0,1:T(8,128)(2,1)}, bf16[8,8,64]{2,0,1:T(8,128)(2,1)S(1)}, u32[]{:S(2)}, u32[]{:S(2)}) collective-permute-start(bf16[8,8,64]{2,0,1:T(8,128)(2,1)} %fusion.17), channel_id=1, source_target_pairs={{0,0},{8,1},{16,8},{24,9},{1,16},{9,17},{17,24},{25,25},{2,2},{10,... | collective-permute-start | bytes 24584 | tf_op jit(solution)/shard_map/ppermute | solution.py:548
  30.5 10.2 %collective-permute-start.2 = (bf16[576,512]{1,0:T(8,128)(2,1)}, bf16[576,512]{1,0:T(8,128)(2,1)}, u32[]{:S(2)}, u32[]{:S(2)}) collective-permute-start(bf16[576,512]{1,0:T(8,128)(2,1)} %bitcast.14.refs_0_.refs_2_.ka.va), channel_id=1, source_target_pairs={{0,1},{1,0},{2,3},{3,2},{4,5},{5,4},{6,7},{7,6},{8,9},{9,8},{10,11... | collective-permute-start | bytes 1769480 | tf_op jit(solution)/shard_map/ppermute | solution.py:516
  32.1 123.9 %all-gather.10.cloned.1.call-start = ((), (), s32[]{:S(2)}) async-start(), calls=%async_computation.5 | async-start | bytes 2211840 | tf_op jit(solution)/shard_map/all_gather | solution.py:629
  32.4 18.5 %collective-permute-start.9 = (bf16[576,512]{1,0:T(8,128)(2,1)}, bf16[576,512]{1,0:T(8,128)(2,1)}, u32[]{:S(2)}, u32[]{:S(2)}) collective-permute-start(bf16[576,512]{1,0:T(8,128)(2,1)} %bitcast.14.refs_0_.refs_2_.ka.va), channel_id=1, source_target_pairs={{0,8},{8,0},{16,24},{24,16},{1,9},{9,1},{17,25},{25,17},{2,10},{10... | collective-permute-start | bytes 1769480 | tf_op jit(solution)/shard_map/ppermute | solution.py:519
  33.8 12.2 %collective-permute-start.3 = (bf16[1,128,768]{2,1,0:T(8,128)(2,1)}, bf16[1,128,768]{2,1,0:T(8,128)(2,1)S(1)}, u32[]{:S(2)}, u32[]{:S(2)}) collective-permute-start(bf16[1,128,768]{2,1,0:T(8,128)(2,1)} %bitcast.20), channel_id=1, source_target_pairs={{0,2},{2,0},{4,6},{6,4},{1,3},{3,1},{5,7},{7,5},{8,10},{10,8},{12,... | collective-permute-start | bytes 589832 | tf_op jit(solution)/shard_map/ppermute | solution.py:526
  35.0 11.0 %collective-permute-start.4 = (bf16[1,128,768]{2,1,0:T(8,128)(2,1)}, bf16[1,128,768]{2,1,0:T(8,128)(2,1)}, u32[]{:S(2)}, u32[]{:S(2)}) collective-permute-start(bf16[1,128,768]{2,1,0:T(8,128)(2,1)} %bitcast.20), channel_id=1, source_target_pairs={{0,4},{2,6},{4,0},{6,2},{1,5},{3,7},{5,1},{7,3},{8,12},{10,14},{12... | collective-permute-start | bytes 589832 | tf_op jit(solution)/shard_map/ppermute | solution.py:526
  36.2 9.8 %collective-permute-start.5 = (bf16[1,128,768]{2,1,0:T(8,128)(2,1)}, bf16[1,128,768]{2,1,0:T(8,128)(2,1)}, u32[]{:S(2)}, u32[]{:S(2)}) collective-permute-start(bf16[1,128,768]{2,1,0:T(8,128)(2,1)} %bitcast.20), channel_id=1, source_target_pairs={{0,6},{2,4},{4,2},{6,0},{1,7},{3,5},{5,3},{7,1},{8,14},{10,12},{12... | collective-permute-start | bytes 589832 | tf_op jit(solution)/shard_map/ppermute | solution.py:526
  49.1 11.8 %collective-permute-start.8 = (bf16[384,512]{1,0:T(8,128)(2,1)S(1)}, bf16[384,512]{1,0:T(8,128)(2,1)S(1)}, u32[]{:S(2)}, u32[]{:S(2)}) collective-permute-start(bf16[384,512]{1,0:T(8,128)(2,1)S(1)} %bitcast.123), channel_id=1, source_target_pairs={{0,1},{1,0},{2,3},{3,2},{4,5},{5,4},{6,7},{7,6},{8,9},{9,8},{10,11... | collective-permute-start | bytes 1179656 | tf_op jit(solution)/shard_map/ppermute | solution.py:516
  51.0 17.2 %collective-permute-start.7 = (bf16[384,512]{1,0:T(8,128)(2,1)S(1)}, bf16[384,512]{1,0:T(8,128)(2,1)S(1)}, u32[]{:S(2)}, u32[]{:S(2)}) collective-permute-start(bf16[384,512]{1,0:T(8,128)(2,1)S(1)} %bitcast.124), channel_id=1, source_target_pairs={{0,8},{8,0},{16,24},{24,16},{1,9},{9,1},{17,25},{25,17},{2,10},{10... | collective-permute-start | bytes 1179656 | tf_op jit(solution)/shard_map/ppermute | solution.py:519
  68.2 8.2 %collective-permute-start.11 = (bf16[384,512]{1,0:T(8,128)(2,1)S(1)}, bf16[384,512]{1,0:T(8,128)(2,1)S(1)}, u32[]{:S(2)}, u32[]{:S(2)}) collective-permute-start(bf16[384,512]{1,0:T(8,128)(2,1)S(1)} %collective-permute-done.7.refs_0_.refs_1_.kb.vb), channel_id=1, source_target_pairs={{0,1},{1,0},{2,3},{3,2},{4,5},{5,4},{6,7},{7,6},{8,9},{9,8},{10,11... | collective-permute-start | bytes 1179656 | tf_op jit(solution)/shard_map/ppermute | solution.py:516
  96.3 19.9 %collective-permute-start.20 = (bf16[4,864,768]{2,1,0:T(8,128)(2,1)}, bf16[4,864,768]{2,1,0:T(8,128)(2,1)}, u32[]{:S(2)}, u32[]{:S(2)}) collective-permute-start(bf16[4,864,768]{2,1,0:T(8,128)(2,1)} %bitcast.173), channel_id=1, source_target_pairs={{0,1},{1,0},{2,3},{3,2},{4,5},{5,4},{6,7},{7,6},{8,9},{9,8},{10,11... | collective-permute-start | bytes 15925256 | tf_op jit(solution)/shard_map/ppermute | solution.py:516
  97.0 8.0 %collective-permute-start.15 = (bf16[192,1024]{1,0:T(8,128)(2,1)S(1)}, bf16[192,1024]{1,0:T(8,128)(2,1)S(1)}, u32[]{:S(2)}, u32[]{:S(2)}) collective-permute-start(bf16[192,1024]{1,0:T(8,128)(2,1)S(1)} %query_estimates.6), channel_id=1, source_target_pairs={{0,1},{1,0},{2,3},{3,2},{4,5},{5,4},{6,7},{7,6},{8,9},{9,8},{10,11... | collective-permute-start | bytes 1179656 | tf_op jit(solution)/shard_map/ppermute | solution.py:516
  97.0 10.3 %collective-permute-start.16 = (bf16[192,1024]{1,0:T(8,128)(2,1)S(1)}, bf16[192,1024]{1,0:T(8,128)(2,1)}, u32[]{:S(2)}, u32[]{:S(2)}) collective-permute-start(bf16[192,1024]{1,0:T(8,128)(2,1)S(1)} %add_convert_fusion.6), channel_id=1, source_target_pairs={{0,8},{8,0},{16,24},{24,16},{1,9},{9,1},{17,25},{25,17},{2,10},{10... | collective-permute-start | bytes 1179656 | tf_op jit(solution)/shard_map/ppermute | solution.py:519
  115.8 122.4 %reduce-scatter.7.cloned.1.call-start = ((), (), s32[]{:S(2)}) async-start(), calls=%async_computation.6 | async-start | bytes 6881280
  142.0 9.6 %collective-permute-start.22 = (bf16[192,256]{1,0:T(8,128)(2,1)}, bf16[192,256]{1,0:T(8,128)(2,1)S(1)}, u32[]{:S(2)}, u32[]{:S(2)}) collective-permute-start(bf16[192,256]{1,0:T(8,128)(2,1)} %get-tuple-element.132), channel_id=1, source_target_pairs={{0,4},{2,6},{4,0},{6,2},{1,5},{3,7},{5,1},{7,3},{8,12},{10,14},{12... | collective-permute-start | bytes 294920 | tf_op jit(solution)/shard_map/ppermute | solution.py:526
  143.2 10.5 %collective-permute-start.23 = (bf16[192,256]{1,0:T(8,128)(2,1)}, bf16[192,256]{1,0:T(8,128)(2,1)S(1)}, u32[]{:S(2)}, u32[]{:S(2)}) collective-permute-start(bf16[192,256]{1,0:T(8,128)(2,1)} %get-tuple-element.133), channel_id=1, source_target_pairs={{0,6},{2,4},{4,2},{6,0},{1,7},{3,5},{5,3},{7,1},{8,14},{10,12},{12... | collective-permute-start | bytes 294920 | tf_op jit(solution)/shard_map/ppermute | solution.py:526
  144.4 12.9 %collective-permute-start.25 = (bf16[6,256,384]{2,1,0:T(8,128)(2,1)}, bf16[6,256,384]{2,1,0:T(8,128)(2,1)}, u32[]{:S(2)}, u32[]{:S(2)}) collective-permute-start(bf16[6,256,384]{2,1,0:T(8,128)(2,1)} %get-tuple-element.143), channel_id=1, source_target_pairs={{0,1},{1,0},{2,3},{3,2},{4,5},{5,4},{6,7},{7,6},{8,9},{9,8},{10,11... | collective-permute-start | bytes 3538952 | tf_op jit(solution)/shard_map/ppermute | solution.py:516
  147.1 10.2 %collective-permute-start.24 = (bf16[8,256,384]{2,1,0:T(8,128)(2,1)}, bf16[8,256,384]{2,1,0:T(8,128)(2,1)}, u32[]{:S(2)}, u32[]{:S(2)}) collective-permute-start(bf16[8,256,384]{2,1,0:T(8,128)(2,1)} %get-tuple-element.141), channel_id=1, source_target_pairs={{0,1},{1,0},{2,3},{3,2},{4,5},{5,4},{6,7},{7,6},{8,9},{9,8},{10,11... | collective-permute-start | bytes 4718600 | tf_op jit(solution)/shard_map/ppermute | solution.py:516
  151.6 14.2 %collective-permute-start.27 = (bf16[128,768]{1,0:T(8,128)(2,1)}, bf16[128,768]{1,0:T(8,128)(2,1)}, u32[]{:S(2)}, u32[]{:S(2)}) collective-permute-start(bf16[128,768]{1,0:T(8,128)(2,1)} %get-tuple-element.243), channel_id=1, source_target_pairs={{0,16},{8,24},{16,0},{24,8},{1,17},{9,25},{17,1},{25,9},{2,18},{10... | collective-permute-start | bytes 589832 | tf_op jit(solution)/shard_map/ppermute | solution.py:523
  154.6 11.1 %collective-permute-start.29 = (bf16[192,1024]{1,0:T(8,128)(2,1)S(1)}, bf16[192,1024]{1,0:T(8,128)(2,1)S(1)}, u32[]{:S(2)}, u32[]{:S(2)}) collective-permute-start(bf16[192,1024]{1,0:T(8,128)(2,1)S(1)} %slice_dynamic-update-slice_fusion.refs_4_), channel_id=1, source_target_pairs={{0,1},{1,0},{2,3},{3,2},{4,5},{5,4},{6,7},{7,6},{8,9},{9,8},{10,11... | collective-permute-start | bytes 1179656 | tf_op jit(solution)/shard_map/ppermute | solution.py:516
  156.1 33.0 %collective-permute-start.28 = (bf16[192,1024]{1,0:T(8,128)(2,1)S(1)}, bf16[192,1024]{1,0:T(8,128)(2,1)S(1)}, u32[]{:S(2)}, u32[]{:S(2)}) collective-permute-start(bf16[192,1024]{1,0:T(8,128)(2,1)S(1)} %slice_dynamic-update-slice_fusion.refs_4_), channel_id=1, source_target_pairs={{0,8},{8,0},{16,24},{24,16},{1,9},{9,1},{17,25},{25,17},{2,10},{10... | collective-permute-start | bytes 1179656 | tf_op jit(solution)/shard_map/ppermute | solution.py:519
  165.7 133.4 %reduce-scatter.5.cloned.1.call-start = ((), (), s32[]{:S(2)}) async-start(), calls=%async_computation.2 | async-start | bytes 1720320 | tf_op jit(solution)/shard_map/reduce_scatter | solution.py:707
  189.0 14.9 %collective-permute-start.31 = (bf16[192,1024]{1,0:T(8,128)(2,1)S(1)}, bf16[192,1024]{1,0:T(8,128)(2,1)S(1)}, u32[]{:S(2)}, u32[]{:S(2)}) collective-permute-start(bf16[192,1024]{1,0:T(8,128)(2,1)S(1)} %collective-permute-done.28.refs_2_), channel_id=1, source_target_pairs={{0,1},{1,0},{2,3},{3,2},{4,5},{5,4},{6,7},{7,6},{8,9},{9,8},{10,11... | collective-permute-start | bytes 1179656 | tf_op jit(solution)/shard_map/ppermute | solution.py:516
  189.4 14.5 %collective-permute-start.30 = (bf16[192,1024]{1,0:T(8,128)(2,1)S(1)}, bf16[192,1024]{1,0:T(8,128)(2,1)S(1)}, u32[]{:S(2)}, u32[]{:S(2)}) collective-permute-start(bf16[192,1024]{1,0:T(8,128)(2,1)S(1)} %get-tuple-element.153), channel_id=1, source_target_pairs={{0,1},{1,0},{2,3},{3,2},{4,5},{5,4},{6,7},{7,6},{8,9},{9,8},{10,11... | collective-permute-start | bytes 1179656 | tf_op jit(solution)/shard_map/ppermute | solution.py:516
  201.3 34.8 %collective-permute-start.36 = (bf16[2,128,768]{2,1,0:T(8,128)(2,1)S(1)}, bf16[2,128,768]{2,1,0:T(8,128)(2,1)S(1)}, u32[]{:S(2)}, u32[]{:S(2)}) collective-permute-start(bf16[2,128,768]{2,1,0:T(8,128)(2,1)S(1)} %pad_maximum_fusion.10), channel_id=1, source_target_pairs={{0,4},{2,6},{4,0},{6,2},{1,5},{3,7},{5,1},{7,3},{8,12},{10,14},{12... | collective-permute-start | bytes 1179656 | tf_op jit(solution)/shard_map/ppermute | solution.py:526
  202.1 33.9 %collective-permute-start.35 = (bf16[2,128,768]{2,1,0:T(8,128)(2,1)S(1)}, bf16[2,128,768]{2,1,0:T(8,128)(2,1)S(1)}, u32[]{:S(2)}, u32[]{:S(2)}) collective-permute-start(bf16[2,128,768]{2,1,0:T(8,128)(2,1)S(1)} %pad_maximum_fusion.10), channel_id=1, source_target_pairs={{0,2},{2,0},{4,6},{6,4},{1,3},{3,1},{5,7},{7,5},{8,10},{10,8},{12,... | collective-permute-start | bytes 1179656 | tf_op jit(solution)/shard_map/ppermute | solution.py:526
  202.7 33.4 %collective-permute-start.37 = (bf16[2,128,768]{2,1,0:T(8,128)(2,1)S(1)}, bf16[2,128,768]{2,1,0:T(8,128)(2,1)S(1)}, u32[]{:S(2)}, u32[]{:S(2)}) collective-permute-start(bf16[2,128,768]{2,1,0:T(8,128)(2,1)S(1)} %pad_maximum_fusion.10), channel_id=1, source_target_pairs={{0,6},{2,4},{4,2},{6,0},{1,7},{3,5},{5,3},{7,1},{8,14},{10,12},{12... | collective-permute-start | bytes 1179656 | tf_op jit(solution)/shard_map/ppermute | solution.py:526
  215.3 10.2 %collective-permute-start.32 = (bf16[192,1024]{1,0:T(8,128)(2,1)S(1)}, bf16[192,1024]{1,0:T(8,128)(2,1)S(1)}, u32[]{:S(2)}, u32[]{:S(2)}) collective-permute-start(bf16[192,1024]{1,0:T(8,128)(2,1)S(1)} %get-tuple-element.158), channel_id=1, source_target_pairs={{0,1},{1,0},{2,3},{3,2},{4,5},{5,4},{6,7},{7,6},{8,9},{9,8},{10,11... | collective-permute-start | bytes 1179656 | tf_op jit(solution)/shard_map/ppermute | solution.py:516
  225.4 10.7 %collective-permute-start.34 = (bf16[2,192,1024]{2,1,0:T(8,128)(2,1)S(1)}, bf16[2,192,1024]{2,1,0:T(8,128)(2,1)S(1)}, u32[]{:S(2)}, u32[]{:S(2)}) collective-permute-start(bf16[2,192,1024]{2,1,0:T(8,128)(2,1)S(1)} %key_backward.4), channel_id=1, source_target_pairs={{0,1},{1,0},{2,3},{3,2},{4,5},{5,4},{6,7},{7,6},{8,9},{9,8},{10,11... | collective-permute-start | bytes 2359304 | tf_op jit(solution)/shard_map/ppermute | solution.py:516
  225.6 10.5 %collective-permute-start.33 = (bf16[192,1024]{1,0:T(8,128)(2,1)S(1)}, bf16[192,1024]{1,0:T(8,128)(2,1)S(1)}, u32[]{:S(2)}, u32[]{:S(2)}) collective-permute-start(bf16[192,1024]{1,0:T(8,128)(2,1)S(1)} %add_convert_fusion.4), channel_id=1, source_target_pairs={{0,8},{8,0},{16,24},{24,16},{1,9},{9,1},{17,25},{25,17},{2,10},{10... | collective-permute-start | bytes 1179656 | tf_op jit(solution)/shard_map/ppermute | solution.py:519
  237.3 32.1 %collective-permute-start.39 = (bf16[2,192,1024]{2,1,0:T(8,128)(2,1)}, bf16[2,192,1024]{2,1,0:T(8,128)(2,1)}, u32[]{:S(2)}, u32[]{:S(2)}) collective-permute-start(bf16[2,192,1024]{2,1,0:T(8,128)(2,1)} %add_convert_fusion.1), channel_id=1, source_target_pairs={{0,8},{8,0},{16,24},{24,16},{1,9},{9,1},{17,25},{25,17},{2,10},{10... | collective-permute-start | bytes 2359304 | tf_op jit(solution)/shard_map/ppermute | solution.py:519
  238.2 129.5 %all-gather.6.cloned.1.call-start = ((), (), s32[]{:S(2)}) async-start(), calls=%async_computation.3 | async-start | bytes 1720320 | tf_op jit(solution)/shard_map/all_gather | solution.py:763
  249.8 19.6 %collective-permute-start.38 = (bf16[2,192,1024]{2,1,0:T(8,128)(2,1)S(1)}, bf16[2,192,1024]{2,1,0:T(8,128)(2,1)S(1)}, u32[]{:S(2)}, u32[]{:S(2)}) collective-permute-start(bf16[2,192,1024]{2,1,0:T(8,128)(2,1)S(1)} %key_backward.7), channel_id=1, source_target_pairs={{0,1},{1,0},{2,3},{3,2},{4,5},{5,4},{6,7},{7,6},{8,9},{9,8},{10,11... | collective-permute-start | bytes 2359304 | tf_op jit(solution)/shard_map/ppermute | solution.py:516
  260.6 25.3 %collective-permute-start.43 = (bf16[4,3,96,768]{3,2,1,0:T(8,128)(2,1)}, bf16[4,3,96,768]{3,2,1,0:T(8,128)(2,1)}, u32[]{:S(2)}, u32[]{:S(2)}) collective-permute-start(bf16[4,3,96,768]{3,2,1,0:T(8,128)(2,1)} %bitcast.35.refs_4_), channel_id=1, source_target_pairs={{0,1},{1,0},{2,3},{3,2},{4,5},{5,4},{6,7},{7,6},{8,9},{9,8},{10,11... | collective-permute-start | bytes 5308424 | tf_op jit(solution)/shard_map/ppermute | solution.py:516
  273.4 12.2 %collective-permute-start.45 = (bf16[288,768]{1,0:T(8,128)(2,1)S(1)}, bf16[288,768]{1,0:T(8,128)(2,1)S(1)}, u32[]{:S(2)}, u32[]{:S(2)}) collective-permute-start(bf16[288,768]{1,0:T(8,128)(2,1)S(1)} %constant_dynamic-slice_fusion.1), channel_id=1, source_target_pairs={{0,1},{1,0},{2,3},{3,2},{4,5},{5,4},{6,7},{7,6},{8,9},{9,8},{10,11... | collective-permute-start | bytes 1327112 | tf_op jit(solution)/shard_map/ppermute | solution.py:516
  282.2 9.6 %collective-permute-start.42 = (bf16[3,192,256]{2,1,0:T(8,128)(2,1)S(1)}, bf16[3,192,256]{2,1,0:T(8,128)(2,1)S(1)}, u32[]{:S(2)}, u32[]{:S(2)}) collective-permute-start(bf16[3,192,256]{2,1,0:T(8,128)(2,1)S(1)} %pad_maximum_fusion.15), channel_id=1, source_target_pairs={{0,6},{2,4},{4,2},{6,0},{1,7},{3,5},{5,3},{7,1},{8,14},{10,12},{12... | collective-permute-start | bytes 884744 | tf_op jit(solution)/shard_map/ppermute | solution.py:526
  283.0 15.6 %collective-permute-start.41 = (bf16[3,192,256]{2,1,0:T(8,128)(2,1)S(1)}, bf16[3,192,256]{2,1,0:T(8,128)(2,1)}, u32[]{:S(2)}, u32[]{:S(2)}) collective-permute-start(bf16[3,192,256]{2,1,0:T(8,128)(2,1)S(1)} %pad_maximum_fusion.14), channel_id=1, source_target_pairs={{0,4},{2,6},{4,0},{6,2},{1,5},{3,7},{5,1},{7,3},{8,12},{10,14},{12... | collective-permute-start | bytes 884744 | tf_op jit(solution)/shard_map/ppermute | solution.py:526
  285.6 13.4 %collective-permute-start.40 = (bf16[3,192,256]{2,1,0:T(8,128)(2,1)S(1)}, bf16[3,192,256]{2,1,0:T(8,128)(2,1)}, u32[]{:S(2)}, u32[]{:S(2)}) collective-permute-start(bf16[3,192,256]{2,1,0:T(8,128)(2,1)S(1)} %pad_maximum_fusion.13), channel_id=1, source_target_pairs={{0,2},{2,0},{4,6},{6,4},{1,3},{3,1},{5,7},{7,5},{8,10},{10,8},{12,... | collective-permute-start | bytes 884744 | tf_op jit(solution)/shard_map/ppermute | solution.py:526
  285.8 13.1 %collective-permute-start.46 = (bf16[144,768]{1,0:T(8,128)(2,1)S(1)}, bf16[144,768]{1,0:T(8,128)(2,1)S(1)}, u32[]{:S(2)}, u32[]{:S(2)}) collective-permute-start(bf16[144,768]{1,0:T(8,128)(2,1)S(1)} %constant_dynamic-slice_fusion), channel_id=1, source_target_pairs={{0,8},{8,0},{16,24},{24,16},{1,9},{9,1},{17,25},{25,17},{2,10},{10... | collective-permute-start | bytes 663560 | tf_op jit(solution)/shard_map/ppermute | solution.py:519
  299.0 12.5 %collective-permute-start.50 = (bf16[144,768]{1,0:T(8,128)(2,1)S(1)}, bf16[144,768]{1,0:T(8,128)(2,1)S(1)}, u32[]{:S(2)}, u32[]{:S(2)}) collective-permute-start(bf16[144,768]{1,0:T(8,128)(2,1)S(1)} %fusion.6), channel_id=1, source_target_pairs={{0,16},{8,24},{16,0},{24,8},{1,17},{9,25},{17,1},{25,9},{2,18},{10... | collective-permute-start | bytes 663560 | tf_op jit(solution)/shard_map/ppermute | solution.py:523
  311.6 17.4 %collective-permute-start.51 = (bf16[144,768]{1,0:T(8,128)(2,1)S(1)}, bf16[144,768]{1,0:T(8,128)(2,1)S(1)}, u32[]{:S(2)}, u32[]{:S(2)}) collective-permute-start(bf16[144,768]{1,0:T(8,128)(2,1)S(1)} %add_convert_fusion.7), channel_id=1, source_target_pairs={{0,8},{8,0},{16,24},{24,16},{1,9},{9,1},{17,25},{25,17},{2,10},{10... | collective-permute-start | bytes 663560 | tf_op jit(solution)/shard_map/ppermute | solution.py:519
  332.7 15.0 %collective-permute-start.44 = (bf16[128,768]{1,0:T(8,128)(2,1)S(1)}, bf16[128,768]{1,0:T(8,128)(2,1)S(1)}, u32[]{:S(2)}, u32[]{:S(2)}) collective-permute-start(bf16[128,768]{1,0:T(8,128)(2,1)S(1)} %get-tuple-element.241), channel_id=1, source_target_pairs={{0,16},{8,24},{16,0},{24,8},{1,17},{9,25},{17,1},{25,9},{2,18},{10... | collective-permute-start | bytes 589832 | tf_op jit(solution)/shard_map/ppermute | solution.py:523
  347.8 10.2 %collective-permute-start.47 = (bf16[2,128,768]{2,1,0:T(8,128)(2,1)S(1)}, bf16[2,128,768]{2,1,0:T(8,128)(2,1)S(1)}, u32[]{:S(2)}, u32[]{:S(2)}) collective-permute-start(bf16[2,128,768]{2,1,0:T(8,128)(2,1)S(1)} %pad_maximum_fusion.11), channel_id=1, source_target_pairs={{0,2},{2,0},{4,6},{6,4},{1,3},{3,1},{5,7},{7,5},{8,10},{10,8},{12,... | collective-permute-start | bytes 1179656 | tf_op jit(solution)/shard_map/ppermute | solution.py:526
  348.7 9.8 %collective-permute-start.48 = (bf16[2,128,768]{2,1,0:T(8,128)(2,1)S(1)}, bf16[2,128,768]{2,1,0:T(8,128)(2,1)S(1)}, u32[]{:S(2)}, u32[]{:S(2)}) collective-permute-start(bf16[2,128,768]{2,1,0:T(8,128)(2,1)S(1)} %pad_maximum_fusion.11), channel_id=1, source_target_pairs={{0,4},{2,6},{4,0},{6,2},{1,5},{3,7},{5,1},{7,3},{8,12},{10,14},{12... | collective-permute-start | bytes 1179656 | tf_op jit(solution)/shard_map/ppermute | solution.py:526
  349.5 18.3 %collective-permute-start.49 = (bf16[2,128,768]{2,1,0:T(8,128)(2,1)S(1)}, bf16[2,128,768]{2,1,0:T(8,128)(2,1)}, u32[]{:S(2)}, u32[]{:S(2)}) collective-permute-start(bf16[2,128,768]{2,1,0:T(8,128)(2,1)S(1)} %pad_maximum_fusion.11), channel_id=1, source_target_pairs={{0,6},{2,4},{4,2},{6,0},{1,7},{3,5},{5,3},{7,1},{8,14},{10,12},{12... | collective-permute-start | bytes 1179656 | tf_op jit(solution)/shard_map/ppermute | solution.py:526
  367.7 10.7 %collective-permute-start.53 = (bf16[896,768]{1,0:T(8,128)(2,1)}, bf16[896,768]{1,0:T(8,128)(2,1)S(1)}, u32[]{:S(2)}, u32[]{:S(2)}) collective-permute-start(bf16[896,768]{1,0:T(8,128)(2,1)} %all-gather.6.cloned.1.call-done.near), channel_id=1, source_target_pairs={{0,1},{1,0},{2,3},{3,2},{4,5},{5,4},{6,7},{7,6},{8,9},{9,8},{10,11... | collective-permute-start | bytes 4128776 | tf_op jit(solution)/shard_map/ppermute | solution.py:516
  (62 other events, 383.7 us)
Sparse Core Ops, SparseCore 0:
  32.3 63.9 all-gather.7
  115.9 37.5 all-gather.9
  165.8 72.1 reduce-scatter.6
  240.2 40.9 reduce-scatter.4
  304.5 39.3 all-gather.5

commit v15 on v11

--- a/solution.py
+++ b/solution.py
@@ -394,6 +394,38 @@
     out[...] = total.astype(out.dtype)
 
 
+def cut_points(width, near, owners):
+    a, b = near // owners, (width - near) // owners
+    return [(j * a, near + j * b) for j in range(owners)], a, b
+
+
+def join_kernel(*refs, near):
+    out = refs[-1]
+    points, a, b = cut_points(out.shape[1], near, len(refs) - 1)
+    for ref, (p, q) in zip(refs, points):
+        out[:, p : p + a] = ref[:, 0:a]
+        out[:, q : q + b] = ref[:, a:]
+
+
+def cut_kernel(a, b, c, *outs, near):
+    total = (a[...] + b[...].astype(f32) + c[...].astype(f32)).astype(bf16)
+    points, a, b = cut_points(total.shape[1], near, len(outs))
+    for out, (p, q) in zip(outs, points):
+        out[:, 0:a] = total[:, p : p + a]
+        out[:, a:] = total[:, q : q + b]
+
+
+def cut_back_kernel(grad_q, a, b, c, whole_out, *outs, near):
+    total = (a[...] + b[...].astype(f32) + c[...].astype(f32)).astype(bf16)
+    points, wa, wb = cut_points(total.shape[2], near, len(outs))
+    for i in range(3):
+        rows = grad_q[...] if i == 0 else total[i - 1]
+        whole_out[i] = rows
+        for out, (p, q) in zip(outs, points):
+            out[i, :, 0:wa] = rows[:, p : p + wa]
+            out[i, :, wa:] = rows[:, q : q + wb]
+
+
 def vmem(count):
     return [pl.BlockSpec(memory_space=pltpu.VMEM)] * count
 
@@ -411,6 +443,17 @@
         ),
         name=name,
     )(core, *args)
+
+
+def small_call(kernel, args, out_shape, name):
+    return pl.pallas_call(
+        kernel,
+        in_specs=vmem(len(args)),
+        out_specs=vmem(len(out_shape)),
+        out_shape=out_shape,
+        cost_estimate=pl.CostEstimate(flops=1 << 20, bytes_accessed=1 << 20, transcendentals=0),
+        name=name,
+    )(*args)
 
 
 def dense(core, x_in, grad_out, gain, bias, attn, weights):
@@ -627,18 +670,16 @@
     weights = after(weights, e_o)
     weights = [weights, over_seq(weights)]
     w_qkv_t = lax.all_gather(after(w_qkv_t, weights[0]), "head", axis=0)
-    attn = add(e, after(e_o_moved, e), e_far).astype(bf16)
-
-    def to_dense(block):
-        parts = []
-        for j in range(head_count):
-            a, b = j * quarter, n_near + j * (rows - quarter)
-            cut = [block[..., a : a + quarter], block[..., b : b + rows - quarter]]
-            parts.append(jnp.concatenate(cut, axis=-1))
+    pieces = [shape((head_width, rows), bf16)] * head_count
+    parts = small_call(
+        partial(cut_kernel, near=n_near), [e, after(e_o_moved, e), e_far], pieces, "cut_estimates"
+    )
+
+    def to_owners(parts):
         moved = [over_head(parts[j], j) for j in range(1, head_count)]
         return [parts[0], *lax.optimization_barrier(moved)]
 
-    attn_parts = to_dense(attn)
+    attn_parts = to_owners(parts)
 
     def away(dense_rows):
         dense_rows = dense_rows.reshape(groups, quarter, width)
@@ -655,9 +696,9 @@
     taken_back = over_seq(give_back)
     est_moved = [over_head(est_parts[j], j) for j in range(1, head_count)]
     est_parts = [est_parts[0], *lax.optimization_barrier(est_moved)]
-    grad = jnp.concatenate(
-        [x[:, :quarter] for x in est_parts] + [x[:, quarter:] for x in est_parts], axis=1
-    )
+    grad = small_call(
+        partial(join_kernel, near=n_near), est_parts, [shape((head_width, n_tokens), bf16)], "join"
+    )[0]
     layer_moved = away(layer_rows)
     weight_parts = weight_grads(
         core, after(small_a, grad, w_qkv_t), small_b, [keep, taken, keep_back, taken_back], attn_parts, heads_far
@@ -712,9 +753,14 @@
     )
 
     dkv_o_moved = after(dkv_o_moved, dkv)
-    grad_kv = add(dkv, dkv_o_moved, after(dkv_far, dkv)).astype(bf16)
-    grad_qkv = jnp.concatenate([grad_q[None], grad_kv])
-    qkv_parts = to_dense(grad_qkv)
+    out_shape = [shape((3, head_width, n_tokens), bf16)] + [shape((3, head_width, rows), bf16)] * head_count
+    grad_qkv, *parts = small_call(
+        partial(cut_back_kernel, near=n_near),
+        [grad_q, dkv, dkv_o_moved, after(dkv_far, dkv)],
+        out_shape,
+        "cut_gradients",
+    )
+    qkv_parts = to_owners(parts)
 
     grad_in = input_grad(core, grad_first, qkv_parts, w_qkv_t, after(w_qkv_far, dkv))
 

time: 363 us -> 369 us (1.017)
  Pallas kernels: 164 us -> 173 us
  other arithmetic: 24.9 us -> 20.1 us
  starting transfers between devices: 53.3 us -> 48.8 us
  local copies, waits for them, and re-layouts: 37.8 us -> 42.1 us
    pallas_call x0 -> x3, Pallas kernels: none -> 7.77 us  [small_call(): pl.pallas_call(kernel, in_specs=vmem(len(args)), out_specs=vmem(len(out_s...]
    unnamed x118 -> x137, local copies, waits for them, and re-layouts: 19.1 us -> 23.2 us
  transfers between devices with their start and end apart: 58 -> 58, of which waited for: 12 -> 14; matrix products, arithmetic and copies ran while one was open for 14% -> 13% of each run, Pallas kernels for 45% -> 46%
where the time goes in v15:
time: 369 us; the launch traced here: 364 us
  Pallas kernels  173 us (47%)
  waiting for transfers between devices  59 us (16%)
  starting transfers between devices  48.8 us (13%)
  local copies, waits for them, and re-layouts  42.1 us (11%)
  other arithmetic  20.1 us (5%)
  between operations  15.3 us (4%)
  matrix products  5.41 us (1%)
    pallas_call x5, Pallas kernels, single(): pl.pallas_call(kernel, in_specs=[pl.BlockSpec(memory_space=pltpu.SMEM)] +...  43.5 us
    pallas_call x3, Pallas kernels, query_backward(): call(partial(query_back_kernel, chunk=4, blocks=blocks, last=last), heads...  43.4 us
    pallas_call x4, Pallas kernels, key_backward(): call(partial(key_back_kernel, chunk=4), heads, micros, 'key_backward', [w...  38.7 us
    ppermute x4, waiting for transfers between devices, over_group(): return lax.ppermute(x, 'hash', moves)  30.6 us
    pallas_call x5, Pallas kernels, key_tables(): call(partial(key_kernel, chunk=2, blocks=len(blocks)), heads, 30 if len(b...  23.5 us
    unnamed x137, local copies, waits for them, and re-layouts  23.2 us
    ppermute x18, waiting for transfers between devices, over_head(): return lax.ppermute(x, 'head', [(h, h ^ j) for h in range(head_count)])  17.5 us
    pallas_call x4, Pallas kernels, query_estimates(): call(partial(query_kernel, chunk=2), heads, 1, 'query_estimates', [whole(...  16.5 us
  transfers between devices with their start and end apart: 58, of which 14 were waited for; matrix products, arithmetic and copies ran while one was open for 13% of the time, Pallas kernels for 46%

profile of v15, /device:TPU:1, one launch (start us, length us, event | category | flops | bytes accessed | tf_op | source)
XLA Modules:
  0.0 364.1 jit_solution(17293212108318626690)
XLA Ops:
  7.3 4.5 %constant_dynamic-slice_fusion.7 = (bf16[1,128,1,768]{3,2,1,0:T(2,128)(2,1)S(1)}, bf16[1,128,1,768]{3,2,1,0:T(2,128)(2,1)}, bf16[1,128,1,768]{3,2,1,0:T(2,128)(2...) fusion(bf16[1,512,2,768]{3,2,1,0:T(2,128)(2,1)} %param.11, s32[]{:T(128)S(6)} %select_n.222, ...), kind=kLoop, calls=%fused_computation.78 | loop fusion | bytes 1966104 | tf_op jit(solution)/shard_map/jit(dynamic_index_in_dim)/dynamic_slice | solution.py:572
  12.6 3.1 collective-permute-start
  16.3 2.5 collective-permute-start.1
  20.5 2.4 copy.54
  22.9 1.8 copy_bitcast_fusion
  24.7 1.9 dynamic-slice_bitcast_fusion
  37.1 1.9 slice.46
  40.7 5.3 %key_tables.5.refs_4_ = f32[3,2048,64]{2,1,0:T(8,128)S(1)} custom-call(bf16[64,64]{1,0:T(8,128)(2,1)S(1)} %bitcast.128, bf16[576,512]{1,0:T(8,128)(2,1)} %bitcast.14.refs_0_.refs_2_.ka.va, bf16[576,512]{1,0:T(8,128)(2,1)} %collective-permute-done.2.refs_1_.refs_3_.refs_0_.refs_2_.ka.va, bf16[576,512]{1,0:T(8,128)(2,1)} %bitcast.14.refs_0_.refs_2_.ka.va, ...), custom_call_target="tpu_custom_call" | custom-call | flops 1100000000 | bytes 1048576 | tf_op jit(solution)/shard_map/key_tables/pallas_call | solution.py:192
  46.0 2.1 pad_maximum_fusion.6
  49.1 1.9 collective-permute-start.8
  53.4 5.8 %key_tables.6.refs_4_ = f32[3,2048,64]{2,1,0:T(8,128)S(1)} custom-call(bf16[64,64]{1,0:T(8,128)(2,1)S(1)} %bitcast.129, bf16[576,512]{1,0:T(8,128)(2,1)} %collective-permute-done.9.refs_0_.refs_2_.ka.va, bf16[576,512]{1,0:T(8,128)(2,1)S(1)} %collective-permute-done.10.refs_1_.refs_3_.refs_0_.ka.va, ...), custom_call_target="tpu_custom_call" | custom-call | flops 32999999488 | bytes 1048576 | tf_op jit(solution)/shard_map/key_tables/pallas_call | solution.py:192
  60.9 5.6 %key_tables.7.refs_2_ = f32[3,2048,64]{2,1,0:T(8,128)S(1)} custom-call(bf16[64,64]{1,0:T(8,128)(2,1)S(1)} %bitcast.130, bf16[384,512]{1,0:T(8,128)(2,1)S(1)} %bitcast.124, bf16[384,512]{1,0:T(8,128)(2,1)S(1)} %collective-permute-done.8.refs_1_.refs_3_.kb.vb, bf16[384,512]{1,0:T(8,128)(2,1)S(1)} %bitcast.125, ...), custom_call_target="tpu_custom_call" | custom-call | flops 32999999488 | bytes 1048576 | tf_op jit(solution)/shard_map/key_tables/pallas_call | solution.py:192
  71.5 4.2 %key_tables.8.refs_2_ = f32[3,2048,64]{2,1,0:T(8,128)S(1)} custom-call(bf16[64,64]{1,0:T(8,128)(2,1)S(1)} %bitcast.131, bf16[384,512]{1,0:T(8,128)(2,1)S(1)} %collective-permute-done.7.refs_0_.refs_1_.kb.vb, bf16[384,512]{1,0:T(8,128)(2,1)S(1)} %collective-permute-done.7.refs_0_.refs_1_.kb.vb, f32[3,2048,64]{2,1,0:T(8,128)} %copy-done.2), custom_call_target="tpu_custom_call" | custom-call | flops 1100000000 | bytes 1048576 | tf_op jit(solution)/shard_map/key_tables/pallas_call | solution.py:192
  76.4 2.6 key_tables.9.tables
  79.1 3.3 query_estimates.4
  83.0 4.1 %query_estimates.5 = bf16[192,1024]{1,0:T(8,128)(2,1)S(1)} custom-call(bf16[64,64]{1,0:T(8,128)(2,1)S(1)} %bitcast.134, bf16[3,2048,64]{2,1,0:T(8,128)(2,1)S(1)} %key_tables.9.tables, bf16[576,512]{1,0:T(8,128)(2,1)} %collective-permute-done.9.refs_0_.refs_2_.ka.va, bf16[192,512]{1,0:T(8,128)(2,1)S(1)} %collective-permute-done.6.refs_1_), custom_call_target="tpu_custom_call" | custom-call | flops 1100000000 | bytes 1048576 | tf_op jit(solution)/shard_map/query_estimates/pallas_call | solution.py:205
  87.3 4.9 %query_estimates.6 = bf16[192,1024]{1,0:T(8,128)(2,1)} custom-call(bf16[64,64]{1,0:T(8,128)(2,1)S(1)} %bitcast.135, bf16[3,2048,64]{2,1,0:T(8,128)(2,1)S(1)} %key_tables.9.tables, bf16[576,512]{1,0:T(8,128)(2,1)} %collective-permute-done.2.refs_1_.refs_3_.refs_0_.refs_2_.ka.va, bf16[192,512]{1,0:T(8,128)(2,1)S(1)} %collective-permute-done.12.refs_1_.refs_3_), custom_call_target="tpu_custom_call" | custom-call | flops 1100000000 | bytes 1048576 | tf_op jit(solution)/shard_map/query_estimates/pallas_call | solution.py:205
  92.2 4.1 %all-gather.5.cloned.1.call-done = bf16[3456,768]{1,0:T(8,128)(2,1)} async-done(((bf16[864,768]{1,0:T(8,128)(2,1)}), bf16[3456,768]{1,0:T(8,128)(2,1)}) %all-gather.5.cloned.1.call-update) | async-done | bytes 5308432 | tf_op jit(solution)/shard_map/all_gather | solution.py:607
  100.3 4.1 %query_estimates.7.a = f32[192,1024]{1,0:T(8,128)S(1)} custom-call(bf16[64,64]{1,0:T(8,128)(2,1)S(1)} %bitcast.136, bf16[3,2048,64]{2,1,0:T(8,128)(2,1)S(1)} %key_tables.9.tables, bf16[576,512]{1,0:T(8,128)(2,1)} %bitcast.14.refs_0_.refs_2_.ka.va, bf16[192,512]{1,0:T(8,128)(2,1)S(1)} %convolution_convert_fusion.1.refs_1_), custom_call_target="tpu_custom_call" | custom-call | flops 1100000000 | bytes 1048576 | tf_op jit(solution)/shard_map/query_estimates/pallas_call | solution.py:205
  105.3 2.5 collective-permute-done.16.c
  107.8 2.2 cut_estimates.1
  115.2 2.0 collective-permute-done.19.refs_3_.refs_7_
  117.8 12.7 %dense.1 = (bf16[256,768]{1,0:T(8,128)(2,1)}, f32[256,768]{1,0:T(8,128)}, f32[256,768]{1,0:T(8,128)}, f32[8,256,384]{2,1,0:T(8,128)}, bf16[8,256,384]{2,1,0:T(8,...) custom-call(s32[2]{0:T(128)} %pad_add_fusion.core, ...), custom_call_target="tpu_custom_call" | custom-call | flops 15399999488 | bytes 1048576 | tf_op jit(solution)/shard_map/dense/pallas_call | solution.py:434
  130.6 1.9 collective-permute-start.24
  132.4 12.6 %dense_back.1 = (f32[256,768]{1,0:T(8,128)}, bf16[6,256,384]{2,1,0:T(8,128)(2,1)}, bf16[6,256,384]{2,1,0:T(8,128)(2,1)}, bf16[192,256]{1,0:T(8,128)(2,1)}, bf16[...) custom-call(s32[2]{0:T(128)} %pad_add_fusion.core, ...), custom_call_target="tpu_custom_call" | custom-call | flops 8800000000 | bytes 1048576 | tf_op jit(solution)/shard_map/dense_back/pallas_call | solution.py:434
  148.5 3.6 collective-permute-done.21.refs_1_
  153.7 2.2 collective-permute-start.27
  156.6 1.9 join.1.refs_4_
  160.4 8.4 %weight_grads.1 = bf16[4,896,768]{2,1,0:T(8,128)(2,1)} custom-call(s32[2]{0:T(128)} %pad_add_fusion.core, f32[8,768]{1,0:T(8,128)} %get-tuple-element.149.small_a, f32[8,768]{1,0:T(8,128)} %get-tuple-element.150.small_b, bf16[8,256,384]{2,1,0:T(8,128)(2,1)} %get-tuple-element.151.refs_0_, bf16[8,256,384]{2,1,0:T(8,128)(2,1)} %collective-permute-done.24.refs_1_, ...), custom_call_target="tpu_custom_call" | custom-call | flops 7699999744 | bytes 1048576 | tf_op jit(solution)/shard_map/weight_grads/pallas_call | solution.py:434
  173.6 20.4 %query_backward.3 = (f32[3,2048,64]{2,1,0:T(8,128)}, f32[192,1024]{1,0:T(8,128)S(1)}, bf16[192,1024]{1,0:T(8,128)(2,1)S(1)}) custom-call(bf16[64,64]{1,0:T(8,128)(2,1)S(1)} %bitcast.138, bf16[64,128]{1,0:T(8,128)(2,1)S(1)} %copy-done.15, bf16[80,2048]{1,0:T(8,128)(2,1)S(1)} %copy-done.30, bf16[3,2048,64]{2,1,0:T(8,128)(2,1)S(1)} %key_tables.9.tables, ...), custom_call_target="tpu_custom_call" | custom-call | flops 54999998464 | bytes 1048576 | tf_op jit(solution)/shard_map/query_backward/pallas_call | solution.py:229
  194.4 11.9 %query_backward.4 = (f32[3,2048,64]{2,1,0:T(8,128)}, f32[192,1024]{1,0:T(8,128)S(1)}) custom-call(bf16[64,64]{1,0:T(8,128)(2,1)S(1)} %bitcast.139, bf16[64,128]{1,0:T(8,128)(2,1)S(1)} %copy-done.16, bf16[80,2048]{1,0:T(8,128)(2,1)S(1)} %copy-done.30, bf16[3,2048,64]{2,1,0:T(8,128)(2,1)S(1)} %key_tables.9.tables, ...), custom_call_target="tpu_custom_call" | custom-call | flops 27499999232 | bytes 1048576 | tf_op jit(solution)/shard_map/query_backward/pallas_call | solution.py:229
  209.2 11.2 %query_backward.5 = (bf16[3,2048,64]{2,1,0:T(8,128)(2,1)S(1)}, bf16[192,1024]{1,0:T(8,128)(2,1)S(1)}) custom-call(bf16[64,64]{1,0:T(8,128)(2,1)S(1)} %bitcast.140, bf16[64,128]{1,0:T(8,128)(2,1)S(1)} %copy-done.16, bf16[80,2048]{1,0:T(8,128)(2,1)S(1)} %copy-done.31, bf16[3,2048,64]{2,1,0:T(8,128)(2,1)S(1)} %key_tables.9.tables, ...), custom_call_target="tpu_custom_call" | custom-call | flops 27499999232 | bytes 1048576 | tf_op jit(solution)/shard_map/query_backward/pallas_call | solution.py:229
  221.7 8.7 %key_backward.4 = bf16[2,192,1024]{2,1,0:T(8,128)(2,1)S(1)} custom-call(bf16[64,64]{1,0:T(8,128)(2,1)S(1)} %bitcast.141, bf16[64,128]{1,0:T(8,128)(2,1)S(1)} %copy-done.16, bf16[80,2048]{1,0:T(8,128)(2,1)S(1)} %copy-done.31, bf16[576,512]{1,0:T(8,128)(2,1)S(1)} %copy-done.19, bf16[384,512]{1,0:T(8,128)(2,1)S(1)} %copy-done.8, ...), custom_call_target="tpu_custom_call" | custom-call | flops 27499999232 | bytes 1048576 | tf_op jit(solution)/shard_map/key_backward/pallas_call | solution.py:243
  231.4 9.7 %key_backward.5 = bf16[2,192,1024]{2,1,0:T(8,128)(2,1)S(1)} custom-call(bf16[64,64]{1,0:T(8,128)(2,1)S(1)} %bitcast.142, bf16[64,128]{1,0:T(8,128)(2,1)S(1)} %copy-done.16, bf16[80,2048]{1,0:T(8,128)(2,1)S(1)} %copy-done.31, bf16[576,512]{1,0:T(8,128)(2,1)} %collective-permute-done.9.refs_0_.refs_2_.ka.va, bf16[384,512]{1,0:T(8,128)(2,1)S(1)} %copy-done.6, ...), custom_call_target="tpu_custom_call" | custom-call | flops 27499999232 | bytes 1048576 | tf_op jit(solution)/shard_map/key_backward/pallas_call | solution.py:243
  245.8 10.4 %key_backward.7 = bf16[2,192,1024]{2,1,0:T(8,128)(2,1)} custom-call(bf16[64,64]{1,0:T(8,128)(2,1)S(1)} %bitcast.143, bf16[64,128]{1,0:T(8,128)(2,1)S(1)} %copy-done.17, bf16[80,2048]{1,0:T(8,128)(2,1)S(1)} %copy-done.31, bf16[576,512]{1,0:T(8,128)(2,1)} %collective-permute-done.2.refs_1_.refs_3_.refs_0_.refs_2_.ka.va, bf16[384,512]{1,0:T(8,128)(2,1)S(1)} %copy-done.21, ...), custom_call_target="tpu_custom_call" | custom-call | flops 27499999232 | bytes 1048576 | tf_op jit(solution)/shard_map/key_backward/pallas_call | solution.py:243
  256.5 10.0 %key_backward.6.a = f32[2,192,1024]{2,1,0:T(8,128)S(1)} custom-call(bf16[64,64]{1,0:T(8,128)(2,1)S(1)} %bitcast.144, bf16[64,128]{1,0:T(8,128)(2,1)S(1)} %copy-done.17, bf16[80,2048]{1,0:T(8,128)(2,1)S(1)} %copy-done.31, bf16[576,512]{1,0:T(8,128)(2,1)} %bitcast.14.refs_0_.refs_2_.ka.va, bf16[384,512]{1,0:T(8,128)(2,1)S(1)} %bitcast.126, ...), custom_call_target="tpu_custom_call" | custom-call | flops 27499999232 | bytes 1048576 | tf_op jit(solution)/shard_map/key_backward/pallas_call | solution.py:243
  267.6 3.7 %cut_gradients.1 = (bf16[3,192,1024]{2,1,0:T(8,128)(2,1)}, bf16[3,192,256]{2,1,0:T(8,128)(2,1)}, bf16[3,192,256]{2,1,0:T(8,128)(2,1)}, bf16[3,192,256]{2,1,0:T(8,128)(2,1)}, bf16[3,192,256]{2,1,0:T(8,128)(2,1)}) custom-call(bf16[192,1024]{1,0:T(8,128)(2,1)} %add_convert_fusion.2.grad_q, f32[2,192,1024]{2,1,0:T(8,128)} %copy-done.4, ...), custom_call_target="tpu_custom_call" | custom-call | flops 1048576 | bytes 1048576 | tf_op jit(solution)/shard_map/cut_gradients/pallas_call | solution.py:449
  274.0 2.3 convolution_convert_fusion
  277.5 2.6 collective-permute-done.40.refs_1_
  280.1 7.4 %collective-permute-done.41.refs_2_ = bf16[3,192,256]{2,1,0:T(8,128)(2,1)S(1)} collective-permute-done((bf16[3,192,256]{2,1,0:T(8,128)(2,1)}, bf16[3,192,256]{2,1,0:T(8,128)(2,1)S(1)}, u32[]{:S(2)}, u32[]{:S(2)}) %collective-permute-start.41) | collective-permute-done | bytes 294944 | tf_op jit(solution)/shard_map/ppermute | solution.py:569
  288.3 5.2 %input_grad.1 = bf16[256,768]{1,0:T(8,128)(2,1)} custom-call(s32[2]{0:T(128)} %pad_add_fusion.core, f32[256,768]{1,0:T(8,128)} %get-tuple-element.174.grad_first, bf16[3,192,256]{2,1,0:T(8,128)(2,1)} %get-tuple-element.184.refs_0_, bf16[3,192,256]{2,1,0:T(8,128)(2,1)} %copy-done.57, bf16[3,192,256]{2,1,0:T(8,128)(2,1)} %copy-done.58, ...), custom_call_target="tpu_custom_call" | custom-call | flops 44000002048 | bytes 1048576 | tf_op jit(solution)/shard_map/input_grad/pallas_call | solution.py:434
  296.3 10.3 %collective-permute-done.44 = bf16[128,768]{1,0:T(8,128)(2,1)S(1)} collective-permute-done((bf16[128,768]{1,0:T(8,128)(2,1)S(1)}, bf16[128,768]{1,0:T(8,128)(2,1)S(1)}, u32[]{:S(2)}, u32[]{:S(2)}) %collective-permute-start.44) | collective-permute-done | bytes 196640 | tf_op jit(solution)/shard_map/ppermute | solution.py:566
  311.4 2.8 copy.56
  314.2 20.3 %collective-permute-done.50 = bf16[144,768]{1,0:T(8,128)(2,1)S(1)} collective-permute-done((bf16[144,768]{1,0:T(8,128)(2,1)S(1)}, bf16[144,768]{1,0:T(8,128)(2,1)S(1)}, u32[]{:S(2)}, u32[]{:S(2)}) %collective-permute-start.50) | collective-permute-done | bytes 221216 | tf_op jit(solution)/shard_map/ppermute | solution.py:566
  334.6 3.7 %all-reduce.3.cloned.1.call-done.near = bf16[896,768]{1,0:T(8,128)(2,1)} async-done(((bf16[896,768]{1,0:T(8,128)(2,1)}), bf16[896,768]{1,0:T(8,128)(2,1)}) %all-reduce.3.cloned.1.call-update) | async-done | bytes 1376272 | tf_op jit(solution)/shard_map/psum | solution.py:748
  341.1 2.6 collective-permute-start.52
  344.0 4.1 %copy.57 = f32[1,512,2,768]{3,2,1,0:T(2,128)} copy(f32[1,512,2,768]{3,1,2,0:T(8,128)S(1)} %maximum_convert_fusion) | data formatting | bytes 6291456
  352.3 4.7 %weight_results.1 = (f32[768,768]{1,0:T(8,128)}, f32[768,768]{1,0:T(8,128)}, f32[192,768]{1,0:T(8,128)}) custom-call(s32[2]{0:T(128)} %pad_add_fusion.core, bf16[896,768]{1,0:T(8,128)(2,1)} %all-reduce.3.cloned.1.call-done.near, bf16[896,768]{1,0:T(8,128)(2,1)} %copy-done.56), custom_call_target="tpu_custom_call" | custom-call | flops 3300000000 | bytes 1048576 | tf_op jit(solution)/shard_map/weight_results/pallas_call | solution.py:434
  (295 shorter events, 80.8 us)
Async XLA Ops:
  7.2 89.1 %all-gather.5.cloned.1.call-start = ((), (), s32[]{:S(2)}) async-start(), calls=%async_computation.2 | async-start | bytes 6635520 | tf_op jit(solution)/shard_map/all_gather | solution.py:607
  12.6 16.4 %collective-permute-start = (bf16[128,768]{1,0:T(8,128)(2,1)}, bf16[128,768]{1,0:T(8,128)(2,1)}, u32[]{:S(2)}, u32[]{:S(2)}) collective-permute-start(bf16[128,768]{1,0:T(8,128)(2,1)} %bitcast.120), channel_id=1, source_target_pairs={{0,16},{8,24},{16,0},{24,8},{1,17},{9,25},{17,1},{25,9},{2,18},{10... | collective-permute-start | bytes 589832 | tf_op jit(solution)/shard_map/ppermute | solution.py:566
  16.3 19.9 %collective-permute-start.1 = (bf16[8,8,64]{2,0,1:T(8,128)(2,1)}, bf16[8,8,64]{2,0,1:T(8,128)(2,1)S(1)}, u32[]{:S(2)}, u32[]{:S(2)}) collective-permute-start(bf16[8,8,64]{2,0,1:T(8,128)(2,1)} %fusion.9), channel_id=1, source_target_pairs={{0,0},{8,1},{16,8},{24,9},{1,16},{9,17},{17,24},{25,25},{2,2},{10,... | collective-permute-start | bytes 24584 | tf_op jit(solution)/shard_map/ppermute | solution.py:591
  30.5 10.2 %collective-permute-start.2 = (bf16[576,512]{1,0:T(8,128)(2,1)}, bf16[576,512]{1,0:T(8,128)(2,1)}, u32[]{:S(2)}, u32[]{:S(2)}) collective-permute-start(bf16[576,512]{1,0:T(8,128)(2,1)} %bitcast.14.refs_0_.refs_2_.ka.va), channel_id=1, source_target_pairs={{0,1},{1,0},{2,3},{3,2},{4,5},{5,4},{6,7},{7,6},{8,9},{9,8},{10,11... | collective-permute-start | bytes 1769480 | tf_op jit(solution)/shard_map/ppermute | solution.py:559
  32.1 127.0 %all-gather.7.cloned.1.call-start = ((), (), s32[]{:S(2)}) async-start(), calls=%async_computation.3 | async-start | bytes 2211840 | tf_op jit(solution)/shard_map/all_gather | solution.py:672
  32.4 18.5 %collective-permute-start.9 = (bf16[576,512]{1,0:T(8,128)(2,1)}, bf16[576,512]{1,0:T(8,128)(2,1)}, u32[]{:S(2)}, u32[]{:S(2)}) collective-permute-start(bf16[576,512]{1,0:T(8,128)(2,1)} %bitcast.14.refs_0_.refs_2_.ka.va), channel_id=1, source_target_pairs={{0,8},{8,0},{16,24},{24,16},{1,9},{9,1},{17,25},{25,17},{2,10},{10... | collective-permute-start | bytes 1769480 | tf_op jit(solution)/shard_map/ppermute | solution.py:562
  33.8 12.2 %collective-permute-start.3 = (bf16[1,128,768]{2,1,0:T(8,128)(2,1)}, bf16[1,128,768]{2,1,0:T(8,128)(2,1)S(1)}, u32[]{:S(2)}, u32[]{:S(2)}) collective-permute-start(bf16[1,128,768]{2,1,0:T(8,128)(2,1)} %bitcast.20), channel_id=1, source_target_pairs={{0,2},{2,0},{4,6},{6,4},{1,3},{3,1},{5,7},{7,5},{8,10},{10,8},{12,... | collective-permute-start | bytes 589832 | tf_op jit(solution)/shard_map/ppermute | solution.py:569
  35.0 11.0 %collective-permute-start.4 = (bf16[1,128,768]{2,1,0:T(8,128)(2,1)}, bf16[1,128,768]{2,1,0:T(8,128)(2,1)}, u32[]{:S(2)}, u32[]{:S(2)}) collective-permute-start(bf16[1,128,768]{2,1,0:T(8,128)(2,1)} %bitcast.20), channel_id=1, source_target_pairs={{0,4},{2,6},{4,0},{6,2},{1,5},{3,7},{5,1},{7,3},{8,12},{10,14},{12... | collective-permute-start | bytes 589832 | tf_op jit(solution)/shard_map/ppermute | solution.py:569
  36.2 9.8 %collective-permute-start.5 = (bf16[1,128,768]{2,1,0:T(8,128)(2,1)}, bf16[1,128,768]{2,1,0:T(8,128)(2,1)}, u32[]{:S(2)}, u32[]{:S(2)}) collective-permute-start(bf16[1,128,768]{2,1,0:T(8,128)(2,1)} %bitcast.20), channel_id=1, source_target_pairs={{0,6},{2,4},{4,2},{6,0},{1,7},{3,5},{5,3},{7,1},{8,14},{10,12},{12... | collective-permute-start | bytes 589832 | tf_op jit(solution)/shard_map/ppermute | solution.py:569
  49.1 11.8 %collective-permute-start.8 = (bf16[384,512]{1,0:T(8,128)(2,1)S(1)}, bf16[384,512]{1,0:T(8,128)(2,1)S(1)}, u32[]{:S(2)}, u32[]{:S(2)}) collective-permute-start(bf16[384,512]{1,0:T(8,128)(2,1)S(1)} %bitcast.122), channel_id=1, source_target_pairs={{0,1},{1,0},{2,3},{3,2},{4,5},{5,4},{6,7},{7,6},{8,9},{9,8},{10,11... | collective-permute-start | bytes 1179656 | tf_op jit(solution)/shard_map/ppermute | solution.py:559
  51.0 17.2 %collective-permute-start.7 = (bf16[384,512]{1,0:T(8,128)(2,1)S(1)}, bf16[384,512]{1,0:T(8,128)(2,1)S(1)}, u32[]{:S(2)}, u32[]{:S(2)}) collective-permute-start(bf16[384,512]{1,0:T(8,128)(2,1)S(1)} %bitcast.123), channel_id=1, source_target_pairs={{0,8},{8,0},{16,24},{24,16},{1,9},{9,1},{17,25},{25,17},{2,10},{10... | collective-permute-start | bytes 1179656 | tf_op jit(solution)/shard_map/ppermute | solution.py:562
  68.2 8.3 %collective-permute-start.11 = (bf16[384,512]{1,0:T(8,128)(2,1)S(1)}, bf16[384,512]{1,0:T(8,128)(2,1)S(1)}, u32[]{:S(2)}, u32[]{:S(2)}) collective-permute-start(bf16[384,512]{1,0:T(8,128)(2,1)S(1)} %collective-permute-done.7.refs_0_.refs_1_.kb.vb), channel_id=1, source_target_pairs={{0,1},{1,0},{2,3},{3,2},{4,5},{5,4},{6,7},{7,6},{8,9},{9,8},{10,11... | collective-permute-start | bytes 1179656 | tf_op jit(solution)/shard_map/ppermute | solution.py:559
  68.5 7.2 %collective-permute-start.6 = (bf16[192,512]{1,0:T(8,128)(2,1)S(1)}, bf16[192,512]{1,0:T(8,128)(2,1)S(1)}, u32[]{:S(2)}, u32[]{:S(2)}) collective-permute-start(bf16[192,512]{1,0:T(8,128)(2,1)S(1)} %convolution_convert_fusion.1.refs_1_), channel_id=1, source_target_pairs={{0,8},{8,0},{16,24},{24,16},{1,9},{9,1},{17,25},{25,17},{2,10},{10... | collective-permute-start | bytes 589832 | tf_op jit(solution)/shard_map/ppermute | solution.py:562
  96.3 21.4 %collective-permute-start.20 = (bf16[4,864,768]{2,1,0:T(8,128)(2,1)}, bf16[4,864,768]{2,1,0:T(8,128)(2,1)}, u32[]{:S(2)}, u32[]{:S(2)}) collective-permute-start(bf16[4,864,768]{2,1,0:T(8,128)(2,1)} %bitcast.168), channel_id=1, source_target_pairs={{0,1},{1,0},{2,3},{3,2},{4,5},{5,4},{6,7},{7,6},{8,9},{9,8},{10,11... | collective-permute-start | bytes 15925256 | tf_op jit(solution)/shard_map/ppermute | solution.py:559
  97.0 10.9 %collective-permute-start.16 = (bf16[192,1024]{1,0:T(8,128)(2,1)S(1)}, bf16[192,1024]{1,0:T(8,128)(2,1)}, u32[]{:S(2)}, u32[]{:S(2)}) collective-permute-start(bf16[192,1024]{1,0:T(8,128)(2,1)S(1)} %add_convert_fusion.4), channel_id=1, source_target_pairs={{0,8},{8,0},{16,24},{24,16},{1,9},{9,1},{17,25},{25,17},{2,10},{10... | collective-permute-start | bytes 1179656 | tf_op jit(solution)/shard_map/ppermute | solution.py:562
  98.2 9.6 %collective-permute-start.15 = (bf16[192,1024]{1,0:T(8,128)(2,1)}, bf16[192,1024]{1,0:T(8,128)(2,1)}, u32[]{:S(2)}, u32[]{:S(2)}) collective-permute-start(bf16[192,1024]{1,0:T(8,128)(2,1)} %query_estimates.6), channel_id=1, source_target_pairs={{0,1},{1,0},{2,3},{3,2},{4,5},{5,4},{6,7},{7,6},{8,9},{9,8},{10,11... | collective-permute-start | bytes 1179656 | tf_op jit(solution)/shard_map/ppermute | solution.py:559
  117.2 127.6 %reduce-scatter.4.cloned.1.call-start = ((), (), s32[]{:S(2)}) async-start(), calls=%async_computation.4 | async-start | bytes 6881280
  130.6 29.8 %collective-permute-start.24 = (bf16[8,256,384]{2,1,0:T(8,128)(2,1)}, bf16[8,256,384]{2,1,0:T(8,128)(2,1)}, u32[]{:S(2)}, u32[]{:S(2)}) collective-permute-start(bf16[8,256,384]{2,1,0:T(8,128)(2,1)} %get-tuple-element.152), channel_id=1, source_target_pairs={{0,1},{1,0},{2,3},{3,2},{4,5},{5,4},{6,7},{7,6},{8,9},{9,8},{10,11... | collective-permute-start | bytes 4718600 | tf_op jit(solution)/shard_map/ppermute | solution.py:559
  145.0 15.4 %collective-permute-start.25 = (bf16[6,256,384]{2,1,0:T(8,128)(2,1)}, bf16[6,256,384]{2,1,0:T(8,128)(2,1)}, u32[]{:S(2)}, u32[]{:S(2)}) collective-permute-start(bf16[6,256,384]{2,1,0:T(8,128)(2,1)} %get-tuple-element.154), channel_id=1, source_target_pairs={{0,1},{1,0},{2,3},{3,2},{4,5},{5,4},{6,7},{7,6},{8,9},{9,8},{10,11... | collective-permute-start | bytes 3538952 | tf_op jit(solution)/shard_map/ppermute | solution.py:559
  146.6 7.1 %collective-permute-start.22 = (bf16[192,256]{1,0:T(8,128)(2,1)}, bf16[192,256]{1,0:T(8,128)(2,1)S(1)}, u32[]{:S(2)}, u32[]{:S(2)}) collective-permute-start(bf16[192,256]{1,0:T(8,128)(2,1)} %get-tuple-element.143), channel_id=1, source_target_pairs={{0,4},{2,6},{4,0},{6,2},{1,5},{3,7},{5,1},{7,3},{8,12},{10,14},{12... | collective-permute-start | bytes 294920 | tf_op jit(solution)/shard_map/ppermute | solution.py:569
  147.3 8.6 %collective-permute-start.23 = (bf16[192,256]{1,0:T(8,128)(2,1)}, bf16[192,256]{1,0:T(8,128)(2,1)S(1)}, u32[]{:S(2)}, u32[]{:S(2)}) collective-permute-start(bf16[192,256]{1,0:T(8,128)(2,1)} %get-tuple-element.144), channel_id=1, source_target_pairs={{0,6},{2,4},{4,2},{6,0},{1,7},{3,5},{5,3},{7,1},{8,14},{10,12},{12... | collective-permute-start | bytes 294920 | tf_op jit(solution)/shard_map/ppermute | solution.py:569
  152.1 7.1 %collective-permute-start.26 = (bf16[4,96,256]{2,1,0:T(8,128)(2,1)S(1)}, bf16[4,96,256]{2,1,0:T(8,128)(2,1)S(1)}, u32[]{:S(2)}, u32[]{:S(2)}) collective-permute-start(bf16[4,96,256]{2,1,0:T(8,128)(2,1)S(1)} %copy-done.60), channel_id=1, source_target_pairs={{0,1},{1,0},{2,3},{3,2},{4,5},{5,4},{6,7},{7,6},{8,9},{9,8},{10,11... | collective-permute-start | bytes 589832 | tf_op jit(solution)/shard_map/ppermute | solution.py:559
  153.7 15.9 %collective-permute-start.27 = (bf16[128,768]{1,0:T(8,128)(2,1)S(1)}, bf16[128,768]{1,0:T(8,128)(2,1)S(1)}, u32[]{:S(2)}, u32[]{:S(2)}) collective-permute-start(bf16[128,768]{1,0:T(8,128)(2,1)S(1)} %get-tuple-element.249), channel_id=1, source_target_pairs={{0,16},{8,24},{16,0},{24,8},{1,17},{9,25},{17,1},{25,9},{2,18},{10... | collective-permute-start | bytes 589832 | tf_op jit(solution)/shard_map/ppermute | solution.py:566
  158.5 10.4 %collective-permute-start.29 = (bf16[192,1024]{1,0:T(8,128)(2,1)}, bf16[192,1024]{1,0:T(8,128)(2,1)S(1)}, u32[]{:S(2)}, u32[]{:S(2)}) collective-permute-start(bf16[192,1024]{1,0:T(8,128)(2,1)} %join.1.refs_4_), channel_id=1, source_target_pairs={{0,1},{1,0},{2,3},{3,2},{4,5},{5,4},{6,7},{7,6},{8,9},{9,8},{10,11... | collective-permute-start | bytes 1179656 | tf_op jit(solution)/shard_map/ppermute | solution.py:559
  159.2 34.8 %collective-permute-start.28 = (bf16[192,1024]{1,0:T(8,128)(2,1)}, bf16[192,1024]{1,0:T(8,128)(2,1)}, u32[]{:S(2)}, u32[]{:S(2)}) collective-permute-start(bf16[192,1024]{1,0:T(8,128)(2,1)} %join.1.refs_4_), channel_id=1, source_target_pairs={{0,8},{8,0},{16,24},{24,16},{1,9},{9,1},{17,25},{25,17},{2,10},{10... | collective-permute-start | bytes 1179656 | tf_op jit(solution)/shard_map/ppermute | solution.py:562
  168.8 169.6 %all-reduce.3.cloned.1.call-start = ((), (), s32[]{:S(2)}) async-start(), calls=%async_computation.1 | async-start | bytes 2752512 | tf_op jit(solution)/shard_map/psum | solution.py:748
  193.9 15.1 %collective-permute-start.31 = (bf16[192,1024]{1,0:T(8,128)(2,1)}, bf16[192,1024]{1,0:T(8,128)(2,1)S(1)}, u32[]{:S(2)}, u32[]{:S(2)}) collective-permute-start(bf16[192,1024]{1,0:T(8,128)(2,1)} %collective-permute-done.28.refs_2_), channel_id=1, source_target_pairs={{0,1},{1,0},{2,3},{3,2},{4,5},{5,4},{6,7},{7,6},{8,9},{9,8},{10,11... | collective-permute-start | bytes 1179656 | tf_op jit(solution)/shard_map/ppermute | solution.py:559
  194.3 14.8 %collective-permute-start.30 = (bf16[192,1024]{1,0:T(8,128)(2,1)S(1)}, bf16[192,1024]{1,0:T(8,128)(2,1)S(1)}, u32[]{:S(2)}, u32[]{:S(2)}) collective-permute-start(bf16[192,1024]{1,0:T(8,128)(2,1)S(1)} %get-tuple-element.164), channel_id=1, source_target_pairs={{0,1},{1,0},{2,3},{3,2},{4,5},{5,4},{6,7},{7,6},{8,9},{9,8},{10,11... | collective-permute-start | bytes 1179656 | tf_op jit(solution)/shard_map/ppermute | solution.py:559
  206.3 34.8 %collective-permute-start.36 = (bf16[2,128,768]{2,1,0:T(8,128)(2,1)S(1)}, bf16[2,128,768]{2,1,0:T(8,128)(2,1)S(1)}, u32[]{:S(2)}, u32[]{:S(2)}) collective-permute-start(bf16[2,128,768]{2,1,0:T(8,128)(2,1)S(1)} %pad_maximum_fusion.9), channel_id=1, source_target_pairs={{0,4},{2,6},{4,0},{6,2},{1,5},{3,7},{5,1},{7,3},{8,12},{10,14},{12... | collective-permute-start | bytes 1179656 | tf_op jit(solution)/shard_map/ppermute | solution.py:569
  206.7 34.9 %collective-permute-start.35 = (bf16[2,128,768]{2,1,0:T(8,128)(2,1)S(1)}, bf16[2,128,768]{2,1,0:T(8,128)(2,1)S(1)}, u32[]{:S(2)}, u32[]{:S(2)}) collective-permute-start(bf16[2,128,768]{2,1,0:T(8,128)(2,1)S(1)} %pad_maximum_fusion.9), channel_id=1, source_target_pairs={{0,2},{2,0},{4,6},{6,4},{1,3},{3,1},{5,7},{7,5},{8,10},{10,8},{12,... | collective-permute-start | bytes 1179656 | tf_op jit(solution)/shard_map/ppermute | solution.py:569
  207.9 33.7 %collective-permute-start.37 = (bf16[2,128,768]{2,1,0:T(8,128)(2,1)S(1)}, bf16[2,128,768]{2,1,0:T(8,128)(2,1)S(1)}, u32[]{:S(2)}, u32[]{:S(2)}) collective-permute-start(bf16[2,128,768]{2,1,0:T(8,128)(2,1)S(1)} %pad_maximum_fusion.9), channel_id=1, source_target_pairs={{0,6},{2,4},{4,2},{6,0},{1,7},{3,5},{5,3},{7,1},{8,14},{10,12},{12... | collective-permute-start | bytes 1179656 | tf_op jit(solution)/shard_map/ppermute | solution.py:569
  220.4 10.1 %collective-permute-start.32 = (bf16[192,1024]{1,0:T(8,128)(2,1)S(1)}, bf16[192,1024]{1,0:T(8,128)(2,1)S(1)}, u32[]{:S(2)}, u32[]{:S(2)}) collective-permute-start(bf16[192,1024]{1,0:T(8,128)(2,1)S(1)} %get-tuple-element.169), channel_id=1, source_target_pairs={{0,1},{1,0},{2,3},{3,2},{4,5},{5,4},{6,7},{7,6},{8,9},{9,8},{10,11... | collective-permute-start | bytes 1179656 | tf_op jit(solution)/shard_map/ppermute | solution.py:559
  230.4 11.2 %collective-permute-start.34 = (bf16[2,192,1024]{2,1,0:T(8,128)(2,1)S(1)}, bf16[2,192,1024]{2,1,0:T(8,128)(2,1)S(1)}, u32[]{:S(2)}, u32[]{:S(2)}) collective-permute-start(bf16[2,192,1024]{2,1,0:T(8,128)(2,1)S(1)} %key_backward.4), channel_id=1, source_target_pairs={{0,1},{1,0},{2,3},{3,2},{4,5},{5,4},{6,7},{7,6},{8,9},{9,8},{10,11... | collective-permute-start | bytes 2359304 | tf_op jit(solution)/shard_map/ppermute | solution.py:559
  230.6 13.3 %collective-permute-start.33 = (bf16[192,1024]{1,0:T(8,128)(2,1)S(1)}, bf16[192,1024]{1,0:T(8,128)(2,1)S(1)}, u32[]{:S(2)}, u32[]{:S(2)}) collective-permute-start(bf16[192,1024]{1,0:T(8,128)(2,1)S(1)} %add_convert_fusion.3), channel_id=1, source_target_pairs={{0,8},{8,0},{16,24},{24,16},{1,9},{9,1},{17,25},{25,17},{2,10},{10... | collective-permute-start | bytes 1179656 | tf_op jit(solution)/shard_map/ppermute | solution.py:562
  241.2 26.4 %collective-permute-start.43 = (bf16[4,3,96,768]{3,2,1,0:T(8,128)(2,1)}, bf16[4,3,96,768]{3,2,1,0:T(8,128)(2,1)}, u32[]{:S(2)}, u32[]{:S(2)}) collective-permute-start(bf16[4,3,96,768]{3,2,1,0:T(8,128)(2,1)} %bitcast.35.refs_4_), channel_id=1, source_target_pairs={{0,1},{1,0},{2,3},{3,2},{4,5},{5,4},{6,7},{7,6},{8,9},{9,8},{10,11... | collective-permute-start | bytes 5308424 | tf_op jit(solution)/shard_map/ppermute | solution.py:559
  242.8 24.8 %collective-permute-start.39 = (bf16[2,192,1024]{2,1,0:T(8,128)(2,1)}, bf16[2,192,1024]{2,1,0:T(8,128)(2,1)}, u32[]{:S(2)}, u32[]{:S(2)}) collective-permute-start(bf16[2,192,1024]{2,1,0:T(8,128)(2,1)} %add_convert_fusion), channel_id=1, source_target_pairs={{0,8},{8,0},{16,24},{24,16},{1,9},{9,1},{17,25},{25,17},{2,10},{10... | collective-permute-start | bytes 2359304 | tf_op jit(solution)/shard_map/ppermute | solution.py:562
  256.1 11.5 %collective-permute-start.38 = (bf16[2,192,1024]{2,1,0:T(8,128)(2,1)}, bf16[2,192,1024]{2,1,0:T(8,128)(2,1)}, u32[]{:S(2)}, u32[]{:S(2)}) collective-permute-start(bf16[2,192,1024]{2,1,0:T(8,128)(2,1)} %key_backward.7), channel_id=1, source_target_pairs={{0,1},{1,0},{2,3},{3,2},{4,5},{5,4},{6,7},{7,6},{8,9},{9,8},{10,11... | collective-permute-start | bytes 2359304 | tf_op jit(solution)/shard_map/ppermute | solution.py:559
  271.4 8.8 %collective-permute-start.40 = (bf16[3,192,256]{2,1,0:T(8,128)(2,1)}, bf16[3,192,256]{2,1,0:T(8,128)(2,1)S(1)}, u32[]{:S(2)}, u32[]{:S(2)}) collective-permute-start(bf16[3,192,256]{2,1,0:T(8,128)(2,1)} %get-tuple-element.185), channel_id=1, source_target_pairs={{0,2},{2,0},{4,6},{6,4},{1,3},{3,1},{5,7},{7,5},{8,10},{10,8},{12,... | collective-permute-start | bytes 884744 | tf_op jit(solution)/shard_map/ppermute | solution.py:569
  272.7 14.8 %collective-permute-start.41 = (bf16[3,192,256]{2,1,0:T(8,128)(2,1)}, bf16[3,192,256]{2,1,0:T(8,128)(2,1)S(1)}, u32[]{:S(2)}, u32[]{:S(2)}) collective-permute-start(bf16[3,192,256]{2,1,0:T(8,128)(2,1)} %get-tuple-element.186), channel_id=1, source_target_pairs={{0,4},{2,6},{4,0},{6,2},{1,5},{3,7},{5,1},{7,3},{8,12},{10,14},{12... | collective-permute-start | bytes 884744 | tf_op jit(solution)/shard_map/ppermute | solution.py:569
  272.7 14.8 %collective-permute-start.42 = (bf16[3,192,256]{2,1,0:T(8,128)(2,1)}, bf16[3,192,256]{2,1,0:T(8,128)(2,1)S(1)}, u32[]{:S(2)}, u32[]{:S(2)}) collective-permute-start(bf16[3,192,256]{2,1,0:T(8,128)(2,1)} %get-tuple-element.187), channel_id=1, source_target_pairs={{0,6},{2,4},{4,2},{6,0},{1,7},{3,5},{5,3},{7,1},{8,14},{10,12},{12... | collective-permute-start | bytes 884744 | tf_op jit(solution)/shard_map/ppermute | solution.py:569
  276.4 19.2 %collective-permute-start.45 = (bf16[288,768]{1,0:T(8,128)(2,1)S(1)}, bf16[288,768]{1,0:T(8,128)(2,1)S(1)}, u32[]{:S(2)}, u32[]{:S(2)}) collective-permute-start(bf16[288,768]{1,0:T(8,128)(2,1)S(1)} %constant_dynamic-slice_fusion.1), channel_id=1, source_target_pairs={{0,1},{1,0},{2,3},{3,2},{4,5},{5,4},{6,7},{7,6},{8,9},{9,8},{10,11... | collective-permute-start | bytes 1327112 | tf_op jit(solution)/shard_map/ppermute | solution.py:559
  294.6 12.0 %collective-permute-start.44 = (bf16[128,768]{1,0:T(8,128)(2,1)S(1)}, bf16[128,768]{1,0:T(8,128)(2,1)S(1)}, u32[]{:S(2)}, u32[]{:S(2)}) collective-permute-start(bf16[128,768]{1,0:T(8,128)(2,1)S(1)} %get-tuple-element.247), channel_id=1, source_target_pairs={{0,16},{8,24},{16,0},{24,8},{1,17},{9,25},{17,1},{25,9},{2,18},{10... | collective-permute-start | bytes 589832 | tf_op jit(solution)/shard_map/ppermute | solution.py:566
  295.8 10.8 %collective-permute-start.46 = (bf16[144,768]{1,0:T(8,128)(2,1)S(1)}, bf16[144,768]{1,0:T(8,128)(2,1)S(1)}, u32[]{:S(2)}, u32[]{:S(2)}) collective-permute-start(bf16[144,768]{1,0:T(8,128)(2,1)S(1)} %constant_dynamic-slice_fusion), channel_id=1, source_target_pairs={{0,8},{8,0},{16,24},{24,16},{1,9},{9,1},{17,25},{25,17},{2,10},{10... | collective-permute-start | bytes 663560 | tf_op jit(solution)/shard_map/ppermute | solution.py:562
  306.7 31.7 %collective-permute-start.47 = (bf16[2,128,768]{2,1,0:T(8,128)(2,1)S(1)}, bf16[2,128,768]{2,1,0:T(8,128)(2,1)}, u32[]{:S(2)}, u32[]{:S(2)}) collective-permute-start(bf16[2,128,768]{2,1,0:T(8,128)(2,1)S(1)} %pad_maximum_fusion.10), channel_id=1, source_target_pairs={{0,2},{2,0},{4,6},{6,4},{1,3},{3,1},{5,7},{7,5},{8,10},{10,8},{12,... | collective-permute-start | bytes 1179656 | tf_op jit(solution)/shard_map/ppermute | solution.py:569
  306.8 31.6 %collective-permute-start.48 = (bf16[2,128,768]{2,1,0:T(8,128)(2,1)S(1)}, bf16[2,128,768]{2,1,0:T(8,128)(2,1)}, u32[]{:S(2)}, u32[]{:S(2)}) collective-permute-start(bf16[2,128,768]{2,1,0:T(8,128)(2,1)S(1)} %pad_maximum_fusion.10), channel_id=1, source_target_pairs={{0,4},{2,6},{4,0},{6,2},{1,5},{3,7},{5,1},{7,3},{8,12},{10,14},{12... | collective-permute-start | bytes 1179656 | tf_op jit(solution)/shard_map/ppermute | solution.py:569
  307.9 30.5 %collective-permute-start.49 = (bf16[2,128,768]{2,1,0:T(8,128)(2,1)S(1)}, bf16[2,128,768]{2,1,0:T(8,128)(2,1)}, u32[]{:S(2)}, u32[]{:S(2)}) collective-permute-start(bf16[2,128,768]{2,1,0:T(8,128)(2,1)S(1)} %pad_maximum_fusion.10), channel_id=1, source_target_pairs={{0,6},{2,4},{4,2},{6,0},{1,7},{3,5},{5,3},{7,1},{8,14},{10,12},{12... | collective-permute-start | bytes 1179656 | tf_op jit(solution)/shard_map/ppermute | solution.py:569
  309.4 25.0 %collective-permute-start.50 = (bf16[144,768]{1,0:T(8,128)(2,1)S(1)}, bf16[144,768]{1,0:T(8,128)(2,1)S(1)}, u32[]{:S(2)}, u32[]{:S(2)}) collective-permute-start(bf16[144,768]{1,0:T(8,128)(2,1)S(1)} %fusion.6), channel_id=1, source_target_pairs={{0,16},{8,24},{16,0},{24,8},{1,17},{9,25},{17,1},{25,9},{2,18},{10... | collective-permute-start | bytes 663560 | tf_op jit(solution)/shard_map/ppermute | solution.py:566
  338.4 11.3 %collective-permute-start.53 = (bf16[896,768]{1,0:T(8,128)(2,1)}, bf16[896,768]{1,0:T(8,128)(2,1)S(1)}, u32[]{:S(2)}, u32[]{:S(2)}) collective-permute-start(bf16[896,768]{1,0:T(8,128)(2,1)} %all-reduce.3.cloned.1.call-done.near), channel_id=1, source_target_pairs={{0,1},{1,0},{2,3},{3,2},{4,5},{5,4},{6,7},{7,6},{8,9},{9,8},{10,11... | collective-permute-start | bytes 4128776 | tf_op jit(solution)/shard_map/ppermute | solution.py:559
  (76 other events, 501.6 us)
Sparse Core Ops, SparseCore 0:
  32.3 64.0 all-gather.4
  117.3 36.2 all-gather.6
  168.9 73.5 reduce-scatter.3
  267.7 70.6 all-reduce.2

commit v16 on v11

--- a/solution.py
+++ b/solution.py
@@ -207,7 +207,7 @@
         heads,
         1,
         "query_estimates",
-        [whole(64, 64), table_spec(), head_rows(near, heads, 0), per_head(far.shape[1])],
+        [whole(64, 64), table_spec(), head_rows(near, heads, 0), head_rows(far, heads, 0)],
         per_head(width),
         shape((heads * HEAD_DIM, width), kind),
     )(planes, tables, near, far)
@@ -219,7 +219,7 @@
     specs = [whole(64, 64), whole(64, 128), whole(80, ROWS), table_spec()]
     args = [planes, planes_t, bits, tables]
     for near, far in queries:
-        specs += [head_rows(near, heads, 0), per_head(far.shape[1])]
+        specs += [head_rows(near, heads, 0), head_rows(far, heads, 0)]
         args += [near, far]
     specs += [per_head(width)] * blocks
     args += grads
@@ -227,7 +227,7 @@
         specs.append(table_spec())
         args.append(start)
     return call(
-        partial(query_back_kernel, chunk=4, blocks=blocks, last=last),
+        partial(query_back_kernel, chunk=4 * blocks, blocks=blocks, last=last),
         heads,
         25 * blocks,
         "query_backward",
@@ -575,7 +575,8 @@
     near_z, near_o = over_place(near), over_seq(near)
     far_quarter = jnp.stack(arrived)
     moved = [over_head(far_quarter, j) for j in range(1, head_count)]
-    tables = key_tables(signed, head_n, [near, near_o], None, f32)
+    dense_in = jnp.concatenate([here[0], *arrived])
+    tables = key_tables(after(signed, dense_in), head_n, [near, near_o], None, f32)
     moved = [after(x, tables) for x in moved]
 
     near_z = after(near_z, tables)
@@ -593,38 +594,31 @@
     tables = key_tables(ready, head_n, [near_z, near_zo], tables, f32)
 
     far_tokens = jnp.stack([far_quarter, *moved]).reshape(-1, width)
-    kv = project(w_qkv[1:], far_tokens)
-    q = project(after(w_qkv[:1], kv), far_tokens)
+    far = project(w_qkv, far_tokens)
     tokens = jnp.concatenate([near_tokens, far_tokens])
-    dense_in = jnp.concatenate([here[0], *arrived])
-    kv_z, kv_o = over_place(kv), over_seq(kv)
-    q_o, q_z = over_seq(q), over_place(q)
+    far_z, far_o = over_place(far), over_seq(far)
     n_near = near.shape[1]
 
-    tables = key_tables(after(signed, q), head_n, [kv, kv_o], tables, f32)
-
-    kv_z = after(kv_z, tables)
-    kv_zo = over_seq(kv_z)
-    ready = after(signed, tokens, dense_in)
-    tables = key_tables(ready, head_n, [kv_z], tables, f32)
-
-    q_z = after(q_z, tables)
-    q_zo = over_seq(q_z)
-    kv_zo = after(kv_zo, tables)
-    tables = key_tables(after(signed, q_z), head_n, [kv_zo], tables, bf16)
-
-    q_zo = after(q_zo, tables)
-    e_zo = query_estimates(signed, head_n, near_zo, q_zo, tables, bf16)
+    tables = key_tables(signed, head_n, [far, far_o], tables, f32)
+
+    far_z = after(far_z, tables)
+    far_zo = over_seq(far_z)
+    tables = key_tables(after(signed, tokens), head_n, [far_z], tables, f32)
+
+    far_zo = after(far_zo, tables)
+    tables = key_tables(signed, head_n, [far_zo], tables, bf16)
+
+    e_zo = query_estimates(signed, head_n, near_zo, far_zo, tables, bf16)
     e_zo_moved = over_seq(e_zo)
-    e_z = query_estimates(signed, head_n, near_z, after(q_z, e_zo), tables, bf16)
+    e_z = query_estimates(signed, head_n, near_z, after(far_z, e_zo), tables, bf16)
     e_far = add(e_z, after(e_zo_moved, e_z)).astype(bf16)
-    ready = after(q_o, e_far)
+    ready = after(far_o, e_far)
     e_o = query_estimates(signed, head_n, near_o, ready, tables, bf16)
     e_far = over_place(e_far)
     e_o_moved = over_seq(e_o)
-    e = query_estimates(signed, head_n, near, after(q, e_o), tables, f32)
+    e = query_estimates(signed, head_n, near, after(far, e_o), tables, f32)
     e_far = after(e_far, e)
-    weights = after(weights, e_o)
+    weights = after(weights, e_far)
     weights = [weights, over_seq(weights)]
     w_qkv_t = lax.all_gather(after(w_qkv_t, weights[0]), "head", axis=0)
     attn = add(e, after(e_o_moved, e), e_far).astype(bf16)
@@ -668,7 +662,7 @@
     grad_o = after(over_seq(grad), weight_parts)
     layer_moved = jnp.stack([after(x, weight_parts) for x in layer_moved])
     part, dq, dq_o = query_backward(
-        signed, signed_t, bits, head_n, tables, [(near, after(q, layer_moved)), (near_o, q_o)], [grad, grad_o],
+        signed, signed_t, bits, head_n, tables, [(near, after(far, layer_moved)), (near_o, far_o)], [grad, grad_o],
         None, False, [f32, bf16],
     )
 
@@ -676,24 +670,24 @@
     grad_zo = over_seq(grad_z)
     dq_o = over_seq(dq_o)
     part, dq_z = query_backward(
-        signed, signed_t, bits, head_n, tables, [(near_z, q_z)], [grad_z], part, False, [f32]
+        signed, signed_t, bits, head_n, tables, [(near_z, far_z)], [grad_z], part, False, [f32]
     )
 
     dq_own = add(dq, after(dq_o, dq_z))
     grad_zo = after(grad_zo, dq_z)
     grad_tables, dq_zo = query_backward(
-        signed, signed_t, bits, head_n, tables, [(near_zo, after(q_zo, dq_own))], [grad_zo], part, True, [bf16]
+        signed, signed_t, bits, head_n, tables, [(near_zo, after(far_zo, dq_own))], [grad_zo], part, True, [bf16]
     )
 
     dq_zo = over_seq(dq_zo)
     w_qkv_t = after(w_qkv_t, grad_tables)
     w_qkv_far = over_seq(w_qkv_t)
-    dkv_zo = key_backward(signed, signed_t, bits, head_n, near_zo, kv_zo, grad_tables, bf16)
+    dkv_zo = key_backward(signed, signed_t, bits, head_n, near_zo, far_zo, grad_tables, bf16)
 
     dkv_zo_moved = over_seq(dkv_zo)
     dq_far = add(dq_z, after(dq_zo, dkv_zo)).astype(bf16)
     layer_moved = [layer_moved] + [over_head(layer_moved, j) for j in range(1, head_count)]
-    dkv_z = key_backward(signed, signed_t, bits, head_n, near_z, after(kv_z, dq_far), grad_tables, bf16)
+    dkv_z = key_backward(signed, signed_t, bits, head_n, near_z, after(far_z, dq_far), grad_tables, bf16)
     dq_far = over_place(dq_far)
 
     dkv_far = add(dkv_z, after(dkv_zo_moved, dkv_z)).astype(bf16)
@@ -701,14 +695,14 @@
     weight_sum = after(weight_sum, dkv_z)
     layer_moved = [after(x, dkv_z) for x in layer_moved]
     dkv_o = key_backward(
-        signed, signed_t, bits, head_n, near_o, after(kv_o, dkv_far, grad_q, weight_sum, *layer_moved),
+        signed, signed_t, bits, head_n, near_o, after(far_o, dkv_far, grad_q, weight_sum, *layer_moved),
         grad_tables, bf16, 25,
     )
     weight_sum = lax.psum(weight_sum, "hash")
     dkv_far = over_place(dkv_far)
     dkv_o_moved = over_seq(dkv_o)
     dkv = key_backward(
-        signed, signed_t, bits, head_n, near, kv, grad_tables, f32, 25
+        signed, signed_t, bits, head_n, near, far, grad_tables, f32, 25
     )
 
     dkv_o_moved = after(dkv_o_moved, dkv)

time: 363 us -> 358 us (0.986)
  waiting for transfers between devices: 58.3 us -> 64.9 us
  starting transfers between devices: 53.3 us -> 47.9 us
    ppermute x22 -> x20, waiting for transfers between devices: 0.33 us -> 4.31 us  [over_seq(): return lax.ppermute(x, 'seq', [(0, 1), (1, 0)])]
    slice x2 -> x0, local copies, waits for them, and re-layouts: 3.64 us -> none  [the longest x1 1.92 us: shards(): kv = project(w_qkv[1:], far_tokens)]
    ppermute x22 -> x20, starting transfers between devices: 16.9 us -> 13.7 us  [over_seq(): return lax.ppermute(x, 'seq', [(0, 1), (1, 0)])]
    unnamed x118 -> x108, local copies, waits for them, and re-layouts: 19.1 us -> 17.7 us
    ppermute x9 -> x8, starting transfers between devices: 7.73 us -> 6.49 us  [over_place(): return lax.ppermute(x, 'hash', [(h, h ^ 1) for h in range(hash_count)])]
  transfers between devices with their start and end apart: 58 -> 55, of which waited for: 12 -> 14; matrix products, arithmetic and copies ran while one was open for 14% -> 13% of each run, Pallas kernels for 45% -> 45%
where the time goes in v16:
time: 358 us; the launch traced here: 353 us
  Pallas kernels  164 us (46%)
  waiting for transfers between devices  64.9 us (18%)
  starting transfers between devices  47.9 us (13%)
  local copies, waits for them, and re-layouts  34.6 us (10%)
  other arithmetic  22.5 us (6%)
  between operations  15.1 us (4%)
  matrix products  3.89 us (1%)
    pallas_call x5, Pallas kernels, single(): pl.pallas_call(kernel, in_specs=[pl.BlockSpec(memory_space=pltpu.SMEM)] +...  43.8 us
    pallas_call x3, Pallas kernels, query_backward(): call(partial(query_back_kernel, chunk=4 * blocks, blocks=blocks, last=las...  43.3 us
    pallas_call x4, Pallas kernels, key_backward(): call(partial(key_back_kernel, chunk=4), heads, micros, 'key_backward', [w...  38 us
    ppermute x4, waiting for transfers between devices, over_group(): return lax.ppermute(x, 'hash', moves)  29.5 us
    pallas_call x5, Pallas kernels, key_tables(): call(partial(key_kernel, chunk=2, blocks=len(blocks)), heads, 30 if len(b...  23.5 us
    unnamed x108, local copies, waits for them, and re-layouts  17.7 us
    ppermute x18, waiting for transfers between devices, over_head(): return lax.ppermute(x, 'head', [(h, h ^ j) for h in range(head_count)])  16.8 us
    ppermute x18, starting transfers between devices, over_head(): return lax.ppermute(x, 'head', [(h, h ^ j) for h in range(head_count)])  16.5 us
  transfers between devices with their start and end apart: 55, of which 14 were waited for; matrix products, arithmetic and copies ran while one was open for 13% of the time, Pallas kernels for 45%

profile of v16, /device:TPU:1, one launch (start us, length us, event | category | flops | bytes accessed | tf_op | source)
XLA Modules:
  0.0 353.2 jit_solution(4089890907259208167)
XLA Ops:
  7.3 4.5 %constant_dynamic-slice_fusion.7 = (bf16[1,128,1,768]{3,2,1,0:T(2,128)(2,1)S(1)}, bf16[1,128,1,768]{3,2,1,0:T(2,128)(2,1)}, bf16[1,128,1,768]{3,2,1,0:T(2,128)(2...) fusion(bf16[1,512,2,768]{3,2,1,0:T(2,128)(2,1)} %param.11, s32[]{:T(128)S(6)} %select_n.222, ...), kind=kLoop, calls=%fused_computation.119 | loop fusion | bytes 1966104 | tf_op jit(solution)/shard_map/jit(dynamic_index_in_dim)/dynamic_slice | solution.py:529
  12.6 3.1 collective-permute-start
  16.3 2.5 collective-permute-start.1
  20.5 2.4 copy.54
  22.9 2.0 dynamic-slice_bitcast_fusion
  25.8 1.8 copy_bitcast_fusion
  31.3 1.7 collective-permute-start.8
  37.2 1.7 pad_maximum_fusion.9.x_in
  38.9 5.2 %key_tables.5.refs_4_ = f32[3,2048,64]{2,1,0:T(8,128)S(1)} custom-call(bf16[64,64]{1,0:T(8,128)(2,1)S(1)} %bitcast.126, bf16[576,512]{1,0:T(8,128)(2,1)} %bitcast.14.refs_0_.refs_2_.ka.va, bf16[576,512]{1,0:T(8,128)(2,1)} %collective-permute-done.2.refs_1_.refs_3_.refs_0_.refs_2_.ka.va, bf16[576,512]{1,0:T(8,128)(2,1)} %bitcast.14.refs_0_.refs_2_.ka.va, ...), custom_call_target="tpu_custom_call" | custom-call | flops 1100000000 | bytes 1048576 | tf_op jit(solution)/shard_map/key_tables/pallas_call | solution.py:192
  44.1 2.4 collective-permute-done.8.refs_0_.refs_2_.ka.va
  52.6 5.8 %key_tables.6.refs_4_ = f32[3,2048,64]{2,1,0:T(8,128)S(1)} custom-call(bf16[64,64]{1,0:T(8,128)(2,1)S(1)} %bitcast.127, bf16[576,512]{1,0:T(8,128)(2,1)} %collective-permute-done.8.refs_0_.refs_2_.ka.va, bf16[576,512]{1,0:T(8,128)(2,1)S(1)} %collective-permute-done.9.refs_1_.refs_3_.refs_0_.ka.va, ...), custom_call_target="tpu_custom_call" | custom-call | flops 32999999488 | bytes 1048576 | tf_op jit(solution)/shard_map/key_tables/pallas_call | solution.py:192
  58.4 1.7 copy-done.15
  60.1 5.7 %key_tables.7.refs_2_ = f32[3,2048,64]{2,1,0:T(8,128)S(1)} custom-call(bf16[64,64]{1,0:T(8,128)(2,1)S(1)} %bitcast.128, bf16[576,512]{1,0:T(8,128)(2,1)S(1)} %bitcast.120, bf16[576,512]{1,0:T(8,128)(2,1)S(1)} %collective-permute-done.7.refs_1_.refs_3_.kb.vb, bf16[576,512]{1,0:T(8,128)(2,1)S(1)} %bitcast.121, ...), custom_call_target="tpu_custom_call" | custom-call | flops 32999999488 | bytes 1048576 | tf_op jit(solution)/shard_map/key_tables/pallas_call | solution.py:192
  65.8 1.9 copy-done.2
  68.2 4.2 %key_tables.8.refs_2_ = f32[3,2048,64]{2,1,0:T(8,128)S(1)} custom-call(bf16[64,64]{1,0:T(8,128)(2,1)S(1)} %bitcast.129, bf16[576,512]{1,0:T(8,128)(2,1)S(1)} %collective-permute-done.6.refs_0_.refs_1_.kb.vb, bf16[576,512]{1,0:T(8,128)(2,1)S(1)} %collective-permute-done.6.refs_0_.refs_1_.kb.vb, f32[3,2048,64]{2,1,0:T(8,128)} %copy-done.2), custom_call_target="tpu_custom_call" | custom-call | flops 1100000000 | bytes 1048576 | tf_op jit(solution)/shard_map/key_tables/pallas_call | solution.py:192
  72.4 2.6 key_tables.9.tables
  75.1 3.3 query_estimates.4
  78.7 4.1 %query_estimates.5 = bf16[192,1024]{1,0:T(8,128)(2,1)S(1)} custom-call(bf16[64,64]{1,0:T(8,128)(2,1)S(1)} %bitcast.132, bf16[3,2048,64]{2,1,0:T(8,128)(2,1)S(1)} %key_tables.9.tables, bf16[576,512]{1,0:T(8,128)(2,1)} %collective-permute-done.8.refs_0_.refs_2_.ka.va, bf16[576,512]{1,0:T(8,128)(2,1)S(1)} %collective-permute-done.6.refs_0_.refs_1_.kb.vb), custom_call_target="tpu_custom_call" | custom-call | flops 1100000000 | bytes 1048576 | tf_op jit(solution)/shard_map/query_estimates/pallas_call | solution.py:205
  83.8 4.2 %query_estimates.6 = bf16[192,1024]{1,0:T(8,128)(2,1)S(1)} custom-call(bf16[64,64]{1,0:T(8,128)(2,1)S(1)} %bitcast.133, bf16[3,2048,64]{2,1,0:T(8,128)(2,1)S(1)} %key_tables.9.tables, bf16[576,512]{1,0:T(8,128)(2,1)} %collective-permute-done.2.refs_1_.refs_3_.refs_0_.refs_2_.ka.va, bf16[576,512]{1,0:T(8,128)(2,1)S(1)} %collective-permute-done.7.refs_1_.refs_3_.kb.vb), custom_call_target="tpu_custom_call" | custom-call | flops 1100000000 | bytes 1048576 | tf_op jit(solution)/shard_map/query_estimates/pallas_call | solution.py:205
  88.0 4.2 %query_estimates.7 = f32[192,1024]{1,0:T(8,128)S(1)} custom-call(bf16[64,64]{1,0:T(8,128)(2,1)S(1)} %bitcast.134, bf16[3,2048,64]{2,1,0:T(8,128)(2,1)S(1)} %key_tables.9.tables, bf16[576,512]{1,0:T(8,128)(2,1)} %bitcast.14.refs_0_.refs_2_.ka.va, bf16[576,512]{1,0:T(8,128)(2,1)S(1)} %bitcast.122), custom_call_target="tpu_custom_call" | custom-call | flops 1100000000 | bytes 1048576 | tf_op jit(solution)/shard_map/query_estimates/pallas_call | solution.py:205
  93.6 3.5 all-gather.5.cloned.1.call-done
  98.3 1.8 dynamic-slice_bitcast_fusion.1
  100.3 4.3 %collective-permute-done.12 = bf16[192,1024]{1,0:T(8,128)(2,1)S(1)} collective-permute-done((bf16[192,1024]{1,0:T(8,128)(2,1)S(1)}, bf16[192,1024]{1,0:T(8,128)(2,1)S(1)}, u32[]{:S(2)}, u32[]{:S(2)}) %collective-permute-start.12) | collective-permute-done | bytes 393248 | tf_op jit(solution)/shard_map/ppermute | solution.py:516
  109.4 1.7 collective-permute-done.16.refs_3_.refs_7_
  111.1 2.6 collective-permute-done.15.refs_2_.refs_6_
  114.4 12.7 %dense.1 = (bf16[256,768]{1,0:T(8,128)(2,1)}, f32[256,768]{1,0:T(8,128)}, f32[256,768]{1,0:T(8,128)}, f32[8,256,384]{2,1,0:T(8,128)}, bf16[8,256,384]{2,1,0:T(8,...) custom-call(s32[2]{0:T(128)} %pad_add_fusion.core, ...), custom_call_target="tpu_custom_call" | custom-call | flops 15399999488 | bytes 1048576 | tf_op jit(solution)/shard_map/dense/pallas_call | solution.py:402
  127.1 12.6 %dense_back.1 = (f32[256,768]{1,0:T(8,128)}, bf16[6,256,384]{2,1,0:T(8,128)(2,1)}, bf16[6,256,384]{2,1,0:T(8,128)(2,1)}, bf16[192,256]{1,0:T(8,128)(2,1)}, bf16[...) custom-call(s32[2]{0:T(128)} %pad_add_fusion.core, ...), custom_call_target="tpu_custom_call" | custom-call | flops 8800000000 | bytes 1048576 | tf_op jit(solution)/shard_map/dense_back/pallas_call | solution.py:402
  146.6 1.5 collective-permute-start.23
  148.1 2.1 collective-permute-start.24
  154.0 8.6 %weight_grads.1 = bf16[4,896,768]{2,1,0:T(8,128)(2,1)} custom-call(s32[2]{0:T(128)} %pad_add_fusion.core, f32[8,768]{1,0:T(8,128)} %get-tuple-element.128.small_a, f32[8,768]{1,0:T(8,128)} %get-tuple-element.129.small_b, bf16[8,256,384]{2,1,0:T(8,128)(2,1)} %get-tuple-element.130.refs_0_, bf16[8,256,384]{2,1,0:T(8,128)(2,1)} %collective-permute-done.21.refs_1_, ...), custom_call_target="tpu_custom_call" | custom-call | flops 7699999744 | bytes 1048576 | tf_op jit(solution)/shard_map/weight_grads/pallas_call | solution.py:402
  164.1 20.3 %query_backward.3 = (f32[3,2048,64]{2,1,0:T(8,128)}, f32[192,1024]{1,0:T(8,128)S(1)}, bf16[192,1024]{1,0:T(8,128)(2,1)S(1)}) custom-call(bf16[64,64]{1,0:T(8,128)(2,1)S(1)} %bitcast.136, bf16[64,128]{1,0:T(8,128)(2,1)S(1)} %pad_maximum_fusion.20.planes_t, bf16[80,2048]{1,0:T(8,128)(2,1)S(1)} %copy-done.14, bf16[3,2048,64]{2,1,0:T(8,128)(2,1)} %copy-done.6, ...), custom_call_target="tpu_custom_call" | custom-call | flops 54999998464 | bytes 1048576 | tf_op jit(solution)/shard_map/query_backward/pallas_call | solution.py:229
  185.0 11.8 %query_backward.4 = (f32[3,2048,64]{2,1,0:T(8,128)}, f32[192,1024]{1,0:T(8,128)S(1)}) custom-call(bf16[64,64]{1,0:T(8,128)(2,1)S(1)} %bitcast.137, bf16[64,128]{1,0:T(8,128)(2,1)S(1)} %pad_maximum_fusion.20.planes_t, bf16[80,2048]{1,0:T(8,128)(2,1)S(1)} %copy-done.14, bf16[3,2048,64]{2,1,0:T(8,128)(2,1)S(1)} %copy-done.7, ...), custom_call_target="tpu_custom_call" | custom-call | flops 27499999232 | bytes 1048576 | tf_op jit(solution)/shard_map/query_backward/pallas_call | solution.py:229
  197.9 1.5 collective-permute-start.34
  199.5 11.2 %query_backward.5 = (bf16[3,2048,64]{2,1,0:T(8,128)(2,1)S(1)}, bf16[192,1024]{1,0:T(8,128)(2,1)S(1)}) custom-call(bf16[64,64]{1,0:T(8,128)(2,1)S(1)} %bitcast.138, bf16[64,128]{1,0:T(8,128)(2,1)S(1)} %pad_maximum_fusion.20.planes_t, bf16[80,2048]{1,0:T(8,128)(2,1)S(1)} %copy-done.14, bf16[3,2048,64]{2,1,0:T(8,128)(2,1)S(1)} %copy-done.7, ...), custom_call_target="tpu_custom_call" | custom-call | flops 27499999232 | bytes 1048576 | tf_op jit(solution)/shard_map/query_backward/pallas_call | solution.py:229
  212.1 8.8 %key_backward.4 = bf16[2,192,1024]{2,1,0:T(8,128)(2,1)S(1)} custom-call(bf16[64,64]{1,0:T(8,128)(2,1)S(1)} %bitcast.139, bf16[64,128]{1,0:T(8,128)(2,1)S(1)} %pad_maximum_fusion.20.planes_t, bf16[80,2048]{1,0:T(8,128)(2,1)S(1)} %copy-done.14, bf16[576,512]{1,0:T(8,128)(2,1)S(1)} %copy-done.13, ...), custom_call_target="tpu_custom_call" | custom-call | flops 27499999232 | bytes 1048576 | tf_op jit(solution)/shard_map/key_backward/pallas_call | solution.py:243
  221.4 9.7 %key_backward.5 = bf16[2,192,1024]{2,1,0:T(8,128)(2,1)S(1)} custom-call(bf16[64,64]{1,0:T(8,128)(2,1)S(1)} %bitcast.140, bf16[64,128]{1,0:T(8,128)(2,1)S(1)} %pad_maximum_fusion.20.planes_t, bf16[80,2048]{1,0:T(8,128)(2,1)S(1)} %copy-done.14, bf16[576,512]{1,0:T(8,128)(2,1)} %collective-permute-done.8.refs_0_.refs_2_.ka.va, bf16[576,512]{1,0:T(8,128)(2,1)S(1)} %copy-done.5, ...), custom_call_target="tpu_custom_call" | custom-call | flops 27499999232 | bytes 1048576 | tf_op jit(solution)/shard_map/key_backward/pallas_call | solution.py:243
  236.6 9.7 %key_backward.7 = bf16[2,192,1024]{2,1,0:T(8,128)(2,1)S(1)} custom-call(bf16[64,64]{1,0:T(8,128)(2,1)S(1)} %bitcast.141, bf16[64,128]{1,0:T(8,128)(2,1)S(1)} %pad_maximum_fusion.20.planes_t, bf16[80,2048]{1,0:T(8,128)(2,1)S(1)} %copy-done.14, bf16[576,512]{1,0:T(8,128)(2,1)} %collective-permute-done.2.refs_1_.refs_3_.refs_0_.refs_2_.ka.va, ...), custom_call_target="tpu_custom_call" | custom-call | flops 27499999232 | bytes 1048576 | tf_op jit(solution)/shard_map/key_backward/pallas_call | solution.py:243
  246.6 9.9 %key_backward.6 = f32[2,192,1024]{2,1,0:T(8,128)S(1)} custom-call(bf16[64,64]{1,0:T(8,128)(2,1)S(1)} %bitcast.142, bf16[64,128]{1,0:T(8,128)(2,1)S(1)} %pad_maximum_fusion.20.planes_t, bf16[80,2048]{1,0:T(8,128)(2,1)S(1)} %copy-done.14, bf16[576,512]{1,0:T(8,128)(2,1)} %bitcast.14.refs_0_.refs_2_.ka.va, bf16[576,512]{1,0:T(8,128)(2,1)S(1)} %bitcast.124, ...), custom_call_target="tpu_custom_call" | custom-call | flops 27499999232 | bytes 1048576 | tf_op jit(solution)/shard_map/key_backward/pallas_call | solution.py:243
  256.6 1.8 add_convert_fusion
  264.7 3.6 %collective-permute-done.39.refs_3_ = bf16[3,192,256]{2,1,0:T(8,128)(2,1)S(1)} collective-permute-done((bf16[3,192,256]{2,1,0:T(8,128)(2,1)S(1)}, bf16[3,192,256]{2,1,0:T(8,128)(2,1)S(1)}, u32[]{:S(2)}, u32[]{:S(2)}) %collective-permute-start.39) | collective-permute-done | bytes 294944 | tf_op jit(solution)/shard_map/ppermute | solution.py:526
  268.3 6.8 %collective-permute-done.38.refs_2_ = bf16[3,192,256]{2,1,0:T(8,128)(2,1)S(1)} collective-permute-done((bf16[3,192,256]{2,1,0:T(8,128)(2,1)S(1)}, bf16[3,192,256]{2,1,0:T(8,128)(2,1)S(1)}, u32[]{:S(2)}, u32[]{:S(2)}) %collective-permute-start.38) | collective-permute-done | bytes 294944 | tf_op jit(solution)/shard_map/ppermute | solution.py:526
  275.9 5.2 %input_grad.1 = bf16[256,768]{1,0:T(8,128)(2,1)} custom-call(s32[2]{0:T(128)} %pad_add_fusion.core, f32[256,768]{1,0:T(8,128)} %get-tuple-element.153.grad_first, bf16[3,192,256]{2,1,0:T(8,128)(2,1)} %pad_maximum_fusion.12.refs_0_, bf16[3,192,256]{2,1,0:T(8,128)(2,1)} %copy-done.42, bf16[3,192,256]{2,1,0:T(8,128)(2,1)} %copy-done.41, ...), custom_call_target="tpu_custom_call" | custom-call | flops 44000002048 | bytes 1048576 | tf_op jit(solution)/shard_map/input_grad/pallas_call | solution.py:402
  284.6 9.2 %collective-permute-done.41 = bf16[128,768]{1,0:T(8,128)(2,1)S(1)} collective-permute-done((bf16[128,768]{1,0:T(8,128)(2,1)S(1)}, bf16[128,768]{1,0:T(8,128)(2,1)S(1)}, u32[]{:S(2)}, u32[]{:S(2)}) %collective-permute-start.41) | collective-permute-done | bytes 196640 | tf_op jit(solution)/shard_map/ppermute | solution.py:523
  299.1 2.8 copy.56
  301.9 20.3 %collective-permute-done.47 = bf16[144,768]{1,0:T(8,128)(2,1)S(1)} collective-permute-done((bf16[144,768]{1,0:T(8,128)(2,1)S(1)}, bf16[144,768]{1,0:T(8,128)(2,1)S(1)}, u32[]{:S(2)}, u32[]{:S(2)}) %collective-permute-start.47) | collective-permute-done | bytes 221216 | tf_op jit(solution)/shard_map/ppermute | solution.py:523
  322.4 6.2 %all-reduce.3.cloned.1.call-done.near = bf16[896,768]{1,0:T(8,128)(2,1)} async-done(((bf16[896,768]{1,0:T(8,128)(2,1)}), bf16[896,768]{1,0:T(8,128)(2,1)}) %all-reduce.3.cloned.1.call-update) | async-done | bytes 1376272 | tf_op jit(solution)/shard_map/psum | solution.py:701
  333.4 4.1 %copy.57 = f32[1,512,2,768]{3,2,1,0:T(2,128)} copy(f32[1,512,2,768]{3,1,2,0:T(8,128)S(1)} %maximum_convert_fusion) | data formatting | bytes 6291456
  341.7 4.7 %weight_results.1 = (f32[768,768]{1,0:T(8,128)}, f32[768,768]{1,0:T(8,128)}, f32[192,768]{1,0:T(8,128)}) custom-call(s32[2]{0:T(128)} %pad_add_fusion.core, bf16[896,768]{1,0:T(8,128)(2,1)} %all-reduce.3.cloned.1.call-done.near, bf16[896,768]{1,0:T(8,128)(2,1)} %copy-done.39), custom_call_target="tpu_custom_call" | custom-call | flops 3300000000 | bytes 1048576 | tf_op jit(solution)/shard_map/weight_results/pallas_call | solution.py:402
  (268 shorter events, 74.2 us)
Async XLA Ops:
  7.2 89.9 %all-gather.5.cloned.1.call-start = ((), (), s32[]{:S(2)}) async-start(), calls=%async_computation.2 | async-start | bytes 6635520 | tf_op jit(solution)/shard_map/all_gather | solution.py:564
  12.6 17.1 %collective-permute-start = (bf16[128,768]{1,0:T(8,128)(2,1)}, bf16[128,768]{1,0:T(8,128)(2,1)}, u32[]{:S(2)}, u32[]{:S(2)}) collective-permute-start(bf16[128,768]{1,0:T(8,128)(2,1)} %bitcast.116), channel_id=1, source_target_pairs={{0,16},{8,24},{16,0},{24,8},{1,17},{9,25},{17,1},{25,9},{2,18},{10... | collective-permute-start | bytes 589832 | tf_op jit(solution)/shard_map/ppermute | solution.py:523
  16.3 20.6 %collective-permute-start.1 = (bf16[8,8,64]{2,0,1:T(8,128)(2,1)}, bf16[8,8,64]{2,0,1:T(8,128)(2,1)S(1)}, u32[]{:S(2)}, u32[]{:S(2)}) collective-permute-start(bf16[8,8,64]{2,0,1:T(8,128)(2,1)} %fusion.16), channel_id=1, source_target_pairs={{0,0},{8,1},{16,8},{24,9},{1,16},{9,17},{17,24},{25,25},{2,2},{10,... | collective-permute-start | bytes 24584 | tf_op jit(solution)/shard_map/ppermute | solution.py:548
  31.3 7.6 %collective-permute-start.2 = (bf16[576,512]{1,0:T(8,128)(2,1)}, bf16[576,512]{1,0:T(8,128)(2,1)}, u32[]{:S(2)}, u32[]{:S(2)}) collective-permute-start(bf16[576,512]{1,0:T(8,128)(2,1)} %bitcast.14.refs_0_.refs_2_.ka.va), channel_id=1, source_target_pairs={{0,1},{1,0},{2,3},{3,2},{4,5},{5,4},{6,7},{7,6},{8,9},{9,8},{10,11... | collective-permute-start | bytes 1769480 | tf_op jit(solution)/shard_map/ppermute | solution.py:516
  31.3 15.2 %collective-permute-start.8 = (bf16[576,512]{1,0:T(8,128)(2,1)}, bf16[576,512]{1,0:T(8,128)(2,1)}, u32[]{:S(2)}, u32[]{:S(2)}) collective-permute-start(bf16[576,512]{1,0:T(8,128)(2,1)} %bitcast.14.refs_0_.refs_2_.ka.va), channel_id=1, source_target_pairs={{0,8},{8,0},{16,24},{24,16},{1,9},{9,1},{17,25},{25,17},{2,10},{10... | collective-permute-start | bytes 1769480 | tf_op jit(solution)/shard_map/ppermute | solution.py:519
  34.2 118.6 %all-gather.7.cloned.1.call-start = ((), (), s32[]{:S(2)}) async-start(), calls=%async_computation.3 | async-start | bytes 2211840 | tf_op jit(solution)/shard_map/all_gather | solution.py:623
  34.5 13.1 %collective-permute-start.3 = (bf16[1,128,768]{2,1,0:T(8,128)(2,1)}, bf16[1,128,768]{2,1,0:T(8,128)(2,1)S(1)}, u32[]{:S(2)}, u32[]{:S(2)}) collective-permute-start(bf16[1,128,768]{2,1,0:T(8,128)(2,1)} %bitcast.20), channel_id=1, source_target_pairs={{0,2},{2,0},{4,6},{6,4},{1,3},{3,1},{5,7},{7,5},{8,10},{10,8},{12,... | collective-permute-start | bytes 589832 | tf_op jit(solution)/shard_map/ppermute | solution.py:526
  35.7 11.9 %collective-permute-start.4 = (bf16[1,128,768]{2,1,0:T(8,128)(2,1)}, bf16[1,128,768]{2,1,0:T(8,128)(2,1)S(1)}, u32[]{:S(2)}, u32[]{:S(2)}) collective-permute-start(bf16[1,128,768]{2,1,0:T(8,128)(2,1)} %bitcast.20), channel_id=1, source_target_pairs={{0,4},{2,6},{4,0},{6,2},{1,5},{3,7},{5,1},{7,3},{8,12},{10,14},{12... | collective-permute-start | bytes 589832 | tf_op jit(solution)/shard_map/ppermute | solution.py:526
  37.0 10.6 %collective-permute-start.5 = (bf16[1,128,768]{2,1,0:T(8,128)(2,1)}, bf16[1,128,768]{2,1,0:T(8,128)(2,1)S(1)}, u32[]{:S(2)}, u32[]{:S(2)}) collective-permute-start(bf16[1,128,768]{2,1,0:T(8,128)(2,1)} %bitcast.20), channel_id=1, source_target_pairs={{0,6},{2,4},{4,2},{6,0},{1,7},{3,5},{5,3},{7,1},{8,14},{10,12},{12... | collective-permute-start | bytes 589832 | tf_op jit(solution)/shard_map/ppermute | solution.py:526
  49.5 10.5 %collective-permute-start.7 = (bf16[576,512]{1,0:T(8,128)(2,1)S(1)}, bf16[576,512]{1,0:T(8,128)(2,1)S(1)}, u32[]{:S(2)}, u32[]{:S(2)}) collective-permute-start(bf16[576,512]{1,0:T(8,128)(2,1)S(1)} %bitcast.118), channel_id=1, source_target_pairs={{0,1},{1,0},{2,3},{3,2},{4,5},{5,4},{6,7},{7,6},{8,9},{9,8},{10,11... | collective-permute-start | bytes 1769480 | tf_op jit(solution)/shard_map/ppermute | solution.py:516
  50.6 17.1 %collective-permute-start.6 = (bf16[576,512]{1,0:T(8,128)(2,1)S(1)}, bf16[576,512]{1,0:T(8,128)(2,1)S(1)}, u32[]{:S(2)}, u32[]{:S(2)}) collective-permute-start(bf16[576,512]{1,0:T(8,128)(2,1)S(1)} %bitcast.119), channel_id=1, source_target_pairs={{0,8},{8,0},{16,24},{24,16},{1,9},{9,1},{17,25},{25,17},{2,10},{10... | collective-permute-start | bytes 1769480 | tf_op jit(solution)/shard_map/ppermute | solution.py:519
  83.0 10.6 %collective-permute-start.13 = (bf16[192,1024]{1,0:T(8,128)(2,1)S(1)}, bf16[192,1024]{1,0:T(8,128)(2,1)}, u32[]{:S(2)}, u32[]{:S(2)}) collective-permute-start(bf16[192,1024]{1,0:T(8,128)(2,1)S(1)} %add_convert_fusion.6), channel_id=1, source_target_pairs={{0,8},{8,0},{16,24},{24,16},{1,9},{9,1},{17,25},{25,17},{2,10},{10... | collective-permute-start | bytes 1179656 | tf_op jit(solution)/shard_map/ppermute | solution.py:519
  97.1 16.9 %collective-permute-start.17 = (bf16[4,864,768]{2,1,0:T(8,128)(2,1)}, bf16[4,864,768]{2,1,0:T(8,128)(2,1)}, u32[]{:S(2)}, u32[]{:S(2)}) collective-permute-start(bf16[4,864,768]{2,1,0:T(8,128)(2,1)} %bitcast.170), channel_id=1, source_target_pairs={{0,1},{1,0},{2,3},{3,2},{4,5},{5,4},{6,7},{7,6},{8,9},{9,8},{10,11... | collective-permute-start | bytes 15925256 | tf_op jit(solution)/shard_map/ppermute | solution.py:516
  97.7 6.9 %collective-permute-start.12 = (bf16[192,1024]{1,0:T(8,128)(2,1)S(1)}, bf16[192,1024]{1,0:T(8,128)(2,1)S(1)}, u32[]{:S(2)}, u32[]{:S(2)}) collective-permute-start(bf16[192,1024]{1,0:T(8,128)(2,1)S(1)} %query_estimates.6), channel_id=1, source_target_pairs={{0,1},{1,0},{2,3},{3,2},{4,5},{5,4},{6,7},{7,6},{8,9},{9,8},{10,11... | collective-permute-start | bytes 1179656 | tf_op jit(solution)/shard_map/ppermute | solution.py:516
  107.1 6.6 %collective-permute-start.15 = (bf16[192,256]{1,0:T(8,128)(2,1)S(1)}, bf16[192,256]{1,0:T(8,128)(2,1)S(1)}, u32[]{:S(2)}, u32[]{:S(2)}) collective-permute-start(bf16[192,256]{1,0:T(8,128)(2,1)S(1)} %pad_maximum_fusion.18), channel_id=1, source_target_pairs={{0,4},{2,6},{4,0},{6,2},{1,5},{3,7},{5,1},{7,3},{8,12},{10,14},{12... | collective-permute-start | bytes 294920 | tf_op jit(solution)/shard_map/ppermute | solution.py:526
  113.7 121.5 %reduce-scatter.4.cloned.1.call-start = ((), (), s32[]{:S(2)}) async-start(), calls=%async_computation.4 | async-start | bytes 6881280
  139.7 6.9 %collective-permute-start.18 = (bf16[192,256]{1,0:T(8,128)(2,1)}, bf16[192,256]{1,0:T(8,128)(2,1)S(1)}, u32[]{:S(2)}, u32[]{:S(2)}) collective-permute-start(bf16[192,256]{1,0:T(8,128)(2,1)} %get-tuple-element.121), channel_id=1, source_target_pairs={{0,2},{2,0},{4,6},{6,4},{1,3},{3,1},{5,7},{7,5},{8,10},{10,8},{12,... | collective-permute-start | bytes 294920 | tf_op jit(solution)/shard_map/ppermute | solution.py:526
  140.8 7.3 %collective-permute-start.19 = (bf16[192,256]{1,0:T(8,128)(2,1)}, bf16[192,256]{1,0:T(8,128)(2,1)S(1)}, u32[]{:S(2)}, u32[]{:S(2)}) collective-permute-start(bf16[192,256]{1,0:T(8,128)(2,1)} %get-tuple-element.122), channel_id=1, source_target_pairs={{0,4},{2,6},{4,0},{6,2},{1,5},{3,7},{5,1},{7,3},{8,12},{10,14},{12... | collective-permute-start | bytes 294920 | tf_op jit(solution)/shard_map/ppermute | solution.py:526
  141.1 9.9 %collective-permute-start.20 = (bf16[192,256]{1,0:T(8,128)(2,1)}, bf16[192,256]{1,0:T(8,128)(2,1)S(1)}, u32[]{:S(2)}, u32[]{:S(2)}) collective-permute-start(bf16[192,256]{1,0:T(8,128)(2,1)} %get-tuple-element.123), channel_id=1, source_target_pairs={{0,6},{2,4},{4,2},{6,0},{1,7},{3,5},{5,3},{7,1},{8,14},{10,12},{12... | collective-permute-start | bytes 294920 | tf_op jit(solution)/shard_map/ppermute | solution.py:526
  142.3 11.6 %collective-permute-start.22 = (bf16[6,256,384]{2,1,0:T(8,128)(2,1)}, bf16[6,256,384]{2,1,0:T(8,128)(2,1)}, u32[]{:S(2)}, u32[]{:S(2)}) collective-permute-start(bf16[6,256,384]{2,1,0:T(8,128)(2,1)} %get-tuple-element.133), channel_id=1, source_target_pairs={{0,1},{1,0},{2,3},{3,2},{4,5},{5,4},{6,7},{7,6},{8,9},{9,8},{10,11... | collective-permute-start | bytes 3538952 | tf_op jit(solution)/shard_map/ppermute | solution.py:516
  143.6 10.3 %collective-permute-start.21 = (bf16[8,256,384]{2,1,0:T(8,128)(2,1)}, bf16[8,256,384]{2,1,0:T(8,128)(2,1)}, u32[]{:S(2)}, u32[]{:S(2)}) collective-permute-start(bf16[8,256,384]{2,1,0:T(8,128)(2,1)} %get-tuple-element.131), channel_id=1, source_target_pairs={{0,1},{1,0},{2,3},{3,2},{4,5},{5,4},{6,7},{7,6},{8,9},{9,8},{10,11... | collective-permute-start | bytes 4718600 | tf_op jit(solution)/shard_map/ppermute | solution.py:516
  148.1 14.6 %collective-permute-start.24 = (bf16[128,768]{1,0:T(8,128)(2,1)}, bf16[128,768]{1,0:T(8,128)(2,1)}, u32[]{:S(2)}, u32[]{:S(2)}) collective-permute-start(bf16[128,768]{1,0:T(8,128)(2,1)} %get-tuple-element.231), channel_id=1, source_target_pairs={{0,16},{8,24},{16,0},{24,8},{1,17},{9,25},{17,1},{25,9},{2,18},{10... | collective-permute-start | bytes 589832 | tf_op jit(solution)/shard_map/ppermute | solution.py:523
  152.0 10.7 %collective-permute-start.26 = (bf16[192,1024]{1,0:T(8,128)(2,1)S(1)}, bf16[192,1024]{1,0:T(8,128)(2,1)S(1)}, u32[]{:S(2)}, u32[]{:S(2)}) collective-permute-start(bf16[192,1024]{1,0:T(8,128)(2,1)S(1)} %slice_dynamic-update-slice_fusion.refs_4_), channel_id=1, source_target_pairs={{0,1},{1,0},{2,3},{3,2},{4,5},{5,4},{6,7},{7,6},{8,9},{9,8},{10,11... | collective-permute-start | bytes 1179656 | tf_op jit(solution)/shard_map/ppermute | solution.py:516
  152.7 31.7 %collective-permute-start.25 = (bf16[192,1024]{1,0:T(8,128)(2,1)S(1)}, bf16[192,1024]{1,0:T(8,128)(2,1)S(1)}, u32[]{:S(2)}, u32[]{:S(2)}) collective-permute-start(bf16[192,1024]{1,0:T(8,128)(2,1)S(1)} %slice_dynamic-update-slice_fusion.refs_4_), channel_id=1, source_target_pairs={{0,8},{8,0},{16,24},{24,16},{1,9},{9,1},{17,25},{25,17},{2,10},{10... | collective-permute-start | bytes 1179656 | tf_op jit(solution)/shard_map/ppermute | solution.py:519
  162.6 166.0 %all-reduce.3.cloned.1.call-start = ((), (), s32[]{:S(2)}) async-start(), calls=%async_computation.1 | async-start | bytes 2752512 | tf_op jit(solution)/shard_map/psum | solution.py:701
  184.5 15.0 %collective-permute-start.28 = (bf16[192,1024]{1,0:T(8,128)(2,1)S(1)}, bf16[192,1024]{1,0:T(8,128)(2,1)S(1)}, u32[]{:S(2)}, u32[]{:S(2)}) collective-permute-start(bf16[192,1024]{1,0:T(8,128)(2,1)S(1)} %collective-permute-done.25.refs_2_), channel_id=1, source_target_pairs={{0,1},{1,0},{2,3},{3,2},{4,5},{5,4},{6,7},{7,6},{8,9},{9,8},{10,11... | collective-permute-start | bytes 1179656 | tf_op jit(solution)/shard_map/ppermute | solution.py:516
  184.9 14.5 %collective-permute-start.27 = (bf16[192,1024]{1,0:T(8,128)(2,1)S(1)}, bf16[192,1024]{1,0:T(8,128)(2,1)S(1)}, u32[]{:S(2)}, u32[]{:S(2)}) collective-permute-start(bf16[192,1024]{1,0:T(8,128)(2,1)S(1)} %get-tuple-element.143), channel_id=1, source_target_pairs={{0,1},{1,0},{2,3},{3,2},{4,5},{5,4},{6,7},{7,6},{8,9},{9,8},{10,11... | collective-permute-start | bytes 1179656 | tf_op jit(solution)/shard_map/ppermute | solution.py:516
  196.8 34.3 %collective-permute-start.33 = (bf16[2,128,768]{2,1,0:T(8,128)(2,1)S(1)}, bf16[2,128,768]{2,1,0:T(8,128)(2,1)S(1)}, u32[]{:S(2)}, u32[]{:S(2)}) collective-permute-start(bf16[2,128,768]{2,1,0:T(8,128)(2,1)S(1)} %pad_maximum_fusion.10), channel_id=1, source_target_pairs={{0,4},{2,6},{4,0},{6,2},{1,5},{3,7},{5,1},{7,3},{8,12},{10,14},{12... | collective-permute-start | bytes 1179656 | tf_op jit(solution)/shard_map/ppermute | solution.py:526
  197.0 34.9 %collective-permute-start.32 = (bf16[2,128,768]{2,1,0:T(8,128)(2,1)S(1)}, bf16[2,128,768]{2,1,0:T(8,128)(2,1)S(1)}, u32[]{:S(2)}, u32[]{:S(2)}) collective-permute-start(bf16[2,128,768]{2,1,0:T(8,128)(2,1)S(1)} %pad_maximum_fusion.10), channel_id=1, source_target_pairs={{0,2},{2,0},{4,6},{6,4},{1,3},{3,1},{5,7},{7,5},{8,10},{10,8},{12,... | collective-permute-start | bytes 1179656 | tf_op jit(solution)/shard_map/ppermute | solution.py:526
  197.9 34.0 %collective-permute-start.34 = (bf16[2,128,768]{2,1,0:T(8,128)(2,1)S(1)}, bf16[2,128,768]{2,1,0:T(8,128)(2,1)S(1)}, u32[]{:S(2)}, u32[]{:S(2)}) collective-permute-start(bf16[2,128,768]{2,1,0:T(8,128)(2,1)S(1)} %pad_maximum_fusion.10), channel_id=1, source_target_pairs={{0,6},{2,4},{4,2},{6,0},{1,7},{3,5},{5,3},{7,1},{8,14},{10,12},{12... | collective-permute-start | bytes 1179656 | tf_op jit(solution)/shard_map/ppermute | solution.py:526
  210.8 10.2 %collective-permute-start.29 = (bf16[192,1024]{1,0:T(8,128)(2,1)S(1)}, bf16[192,1024]{1,0:T(8,128)(2,1)S(1)}, u32[]{:S(2)}, u32[]{:S(2)}) collective-permute-start(bf16[192,1024]{1,0:T(8,128)(2,1)S(1)} %get-tuple-element.148), channel_id=1, source_target_pairs={{0,1},{1,0},{2,3},{3,2},{4,5},{5,4},{6,7},{7,6},{8,9},{9,8},{10,11... | collective-permute-start | bytes 1179656 | tf_op jit(solution)/shard_map/ppermute | solution.py:516
  220.9 11.0 %collective-permute-start.31 = (bf16[2,192,1024]{2,1,0:T(8,128)(2,1)S(1)}, bf16[2,192,1024]{2,1,0:T(8,128)(2,1)S(1)}, u32[]{:S(2)}, u32[]{:S(2)}) collective-permute-start(bf16[2,192,1024]{2,1,0:T(8,128)(2,1)S(1)} %key_backward.4), channel_id=1, source_target_pairs={{0,1},{1,0},{2,3},{3,2},{4,5},{5,4},{6,7},{7,6},{8,9},{9,8},{10,11... | collective-permute-start | bytes 2359304 | tf_op jit(solution)/shard_map/ppermute | solution.py:516
  221.1 10.8 %collective-permute-start.30 = (bf16[192,1024]{1,0:T(8,128)(2,1)S(1)}, bf16[192,1024]{1,0:T(8,128)(2,1)S(1)}, u32[]{:S(2)}, u32[]{:S(2)}) collective-permute-start(bf16[192,1024]{1,0:T(8,128)(2,1)S(1)} %add_convert_fusion.4), channel_id=1, source_target_pairs={{0,8},{8,0},{16,24},{24,16},{1,9},{9,1},{17,25},{25,17},{2,10},{10... | collective-permute-start | bytes 1179656 | tf_op jit(solution)/shard_map/ppermute | solution.py:519
  231.1 25.5 %collective-permute-start.40 = (bf16[4,3,96,768]{3,2,1,0:T(8,128)(2,1)}, bf16[4,3,96,768]{3,2,1,0:T(8,128)(2,1)}, u32[]{:S(2)}, u32[]{:S(2)}) collective-permute-start(bf16[4,3,96,768]{3,2,1,0:T(8,128)(2,1)} %bitcast.34.refs_4_), channel_id=1, source_target_pairs={{0,1},{1,0},{2,3},{3,2},{4,5},{5,4},{6,7},{7,6},{8,9},{9,8},{10,11... | collective-permute-start | bytes 5308424 | tf_op jit(solution)/shard_map/ppermute | solution.py:516
  233.1 23.5 %collective-permute-start.36 = (bf16[2,192,1024]{2,1,0:T(8,128)(2,1)}, bf16[2,192,1024]{2,1,0:T(8,128)(2,1)}, u32[]{:S(2)}, u32[]{:S(2)}) collective-permute-start(bf16[2,192,1024]{2,1,0:T(8,128)(2,1)} %add_convert_fusion.1), channel_id=1, source_target_pairs={{0,8},{8,0},{16,24},{24,16},{1,9},{9,1},{17,25},{25,17},{2,10},{10... | collective-permute-start | bytes 2359304 | tf_op jit(solution)/shard_map/ppermute | solution.py:519
  246.3 10.4 %collective-permute-start.35 = (bf16[2,192,1024]{2,1,0:T(8,128)(2,1)S(1)}, bf16[2,192,1024]{2,1,0:T(8,128)(2,1)}, u32[]{:S(2)}, u32[]{:S(2)}) collective-permute-start(bf16[2,192,1024]{2,1,0:T(8,128)(2,1)S(1)} %key_backward.7), channel_id=1, source_target_pairs={{0,1},{1,0},{2,3},{3,2},{4,5},{5,4},{6,7},{7,6},{8,9},{9,8},{10,11... | collective-permute-start | bytes 2359304 | tf_op jit(solution)/shard_map/ppermute | solution.py:516
  258.8 9.5 %collective-permute-start.39 = (bf16[3,192,256]{2,1,0:T(8,128)(2,1)S(1)}, bf16[3,192,256]{2,1,0:T(8,128)(2,1)S(1)}, u32[]{:S(2)}, u32[]{:S(2)}) collective-permute-start(bf16[3,192,256]{2,1,0:T(8,128)(2,1)S(1)} %pad_maximum_fusion.15), channel_id=1, source_target_pairs={{0,6},{2,4},{4,2},{6,0},{1,7},{3,5},{5,3},{7,1},{8,14},{10,12},{12... | collective-permute-start | bytes 884744 | tf_op jit(solution)/shard_map/ppermute | solution.py:526
  259.8 15.4 %collective-permute-start.38 = (bf16[3,192,256]{2,1,0:T(8,128)(2,1)S(1)}, bf16[3,192,256]{2,1,0:T(8,128)(2,1)S(1)}, u32[]{:S(2)}, u32[]{:S(2)}) collective-permute-start(bf16[3,192,256]{2,1,0:T(8,128)(2,1)S(1)} %pad_maximum_fusion.14), channel_id=1, source_target_pairs={{0,4},{2,6},{4,0},{6,2},{1,5},{3,7},{5,1},{7,3},{8,12},{10,14},{12... | collective-permute-start | bytes 884744 | tf_op jit(solution)/shard_map/ppermute | solution.py:526
  261.1 14.1 %collective-permute-start.37 = (bf16[3,192,256]{2,1,0:T(8,128)(2,1)S(1)}, bf16[3,192,256]{2,1,0:T(8,128)(2,1)S(1)}, u32[]{:S(2)}, u32[]{:S(2)}) collective-permute-start(bf16[3,192,256]{2,1,0:T(8,128)(2,1)S(1)} %pad_maximum_fusion.13), channel_id=1, source_target_pairs={{0,2},{2,0},{4,6},{6,4},{1,3},{3,1},{5,7},{7,5},{8,10},{10,8},{12,... | collective-permute-start | bytes 884744 | tf_op jit(solution)/shard_map/ppermute | solution.py:526
  262.9 20.9 %collective-permute-start.42 = (bf16[288,768]{1,0:T(8,128)(2,1)S(1)}, bf16[288,768]{1,0:T(8,128)(2,1)S(1)}, u32[]{:S(2)}, u32[]{:S(2)}) collective-permute-start(bf16[288,768]{1,0:T(8,128)(2,1)S(1)} %constant_dynamic-slice_fusion.1), channel_id=1, source_target_pairs={{0,1},{1,0},{2,3},{3,2},{4,5},{5,4},{6,7},{7,6},{8,9},{9,8},{10,11... | collective-permute-start | bytes 1327112 | tf_op jit(solution)/shard_map/ppermute | solution.py:516
  282.3 11.5 %collective-permute-start.41 = (bf16[128,768]{1,0:T(8,128)(2,1)S(1)}, bf16[128,768]{1,0:T(8,128)(2,1)S(1)}, u32[]{:S(2)}, u32[]{:S(2)}) collective-permute-start(bf16[128,768]{1,0:T(8,128)(2,1)S(1)} %get-tuple-element.229), channel_id=1, source_target_pairs={{0,16},{8,24},{16,0},{24,8},{1,17},{9,25},{17,1},{25,9},{2,18},{10... | collective-permute-start | bytes 589832 | tf_op jit(solution)/shard_map/ppermute | solution.py:523
  283.9 9.9 %collective-permute-start.43 = (bf16[144,768]{1,0:T(8,128)(2,1)S(1)}, bf16[144,768]{1,0:T(8,128)(2,1)S(1)}, u32[]{:S(2)}, u32[]{:S(2)}) collective-permute-start(bf16[144,768]{1,0:T(8,128)(2,1)S(1)} %constant_dynamic-slice_fusion), channel_id=1, source_target_pairs={{0,8},{8,0},{16,24},{24,16},{1,9},{9,1},{17,25},{25,17},{2,10},{10... | collective-permute-start | bytes 663560 | tf_op jit(solution)/shard_map/ppermute | solution.py:519
  293.9 34.7 %collective-permute-start.44 = (bf16[2,128,768]{2,1,0:T(8,128)(2,1)S(1)}, bf16[2,128,768]{2,1,0:T(8,128)(2,1)S(1)}, u32[]{:S(2)}, u32[]{:S(2)}) collective-permute-start(bf16[2,128,768]{2,1,0:T(8,128)(2,1)S(1)} %pad_maximum_fusion.11), channel_id=1, source_target_pairs={{0,2},{2,0},{4,6},{6,4},{1,3},{3,1},{5,7},{7,5},{8,10},{10,8},{12,... | collective-permute-start | bytes 1179656 | tf_op jit(solution)/shard_map/ppermute | solution.py:526
  295.3 33.3 %collective-permute-start.45 = (bf16[2,128,768]{2,1,0:T(8,128)(2,1)S(1)}, bf16[2,128,768]{2,1,0:T(8,128)(2,1)}, u32[]{:S(2)}, u32[]{:S(2)}) collective-permute-start(bf16[2,128,768]{2,1,0:T(8,128)(2,1)S(1)} %pad_maximum_fusion.11), channel_id=1, source_target_pairs={{0,4},{2,6},{4,0},{6,2},{1,5},{3,7},{5,1},{7,3},{8,12},{10,14},{12... | collective-permute-start | bytes 1179656 | tf_op jit(solution)/shard_map/ppermute | solution.py:526
  296.8 31.8 %collective-permute-start.46 = (bf16[2,128,768]{2,1,0:T(8,128)(2,1)S(1)}, bf16[2,128,768]{2,1,0:T(8,128)(2,1)}, u32[]{:S(2)}, u32[]{:S(2)}) collective-permute-start(bf16[2,128,768]{2,1,0:T(8,128)(2,1)S(1)} %pad_maximum_fusion.11), channel_id=1, source_target_pairs={{0,6},{2,4},{4,2},{6,0},{1,7},{3,5},{5,3},{7,1},{8,14},{10,12},{12... | collective-permute-start | bytes 1179656 | tf_op jit(solution)/shard_map/ppermute | solution.py:526
  296.8 25.4 %collective-permute-start.47 = (bf16[144,768]{1,0:T(8,128)(2,1)S(1)}, bf16[144,768]{1,0:T(8,128)(2,1)S(1)}, u32[]{:S(2)}, u32[]{:S(2)}) collective-permute-start(bf16[144,768]{1,0:T(8,128)(2,1)S(1)} %fusion.6), channel_id=1, source_target_pairs={{0,16},{8,24},{16,0},{24,8},{1,17},{9,25},{17,1},{25,9},{2,18},{10... | collective-permute-start | bytes 663560 | tf_op jit(solution)/shard_map/ppermute | solution.py:523
  322.3 9.3 %collective-permute-start.48 = (bf16[144,768]{1,0:T(8,128)(2,1)S(1)}, bf16[144,768]{1,0:T(8,128)(2,1)S(1)}, u32[]{:S(2)}, u32[]{:S(2)}) collective-permute-start(bf16[144,768]{1,0:T(8,128)(2,1)S(1)} %add_convert_fusion.7), channel_id=1, source_target_pairs={{0,8},{8,0},{16,24},{24,16},{1,9},{9,1},{17,25},{25,17},{2,10},{10... | collective-permute-start | bytes 663560 | tf_op jit(solution)/shard_map/ppermute | solution.py:519
  328.6 10.5 %collective-permute-start.50 = (bf16[896,768]{1,0:T(8,128)(2,1)}, bf16[896,768]{1,0:T(8,128)(2,1)S(1)}, u32[]{:S(2)}, u32[]{:S(2)}) collective-permute-start(bf16[896,768]{1,0:T(8,128)(2,1)} %all-reduce.3.cloned.1.call-done.near), channel_id=1, source_target_pairs={{0,1},{1,0},{2,3},{3,2},{4,5},{5,4},{6,7},{7,6},{8,9},{9,8},{10,11... | collective-permute-start | bytes 4128776 | tf_op jit(solution)/shard_map/ppermute | solution.py:516
  (55 other events, 457.4 us)
Sparse Core Ops, SparseCore 0:
  34.3 62.7 all-gather.4
  113.8 35.4 all-gather.6
  162.7 70.9 reduce-scatter.3
  256.7 71.7 all-reduce.2

commit v17 on v16

--- a/solution.py
+++ b/solution.py
@@ -603,7 +603,7 @@
 
     far_z = after(far_z, tables)
     far_zo = over_seq(far_z)
-    tables = key_tables(after(signed, tokens), head_n, [far_z], tables, f32)
+    tables = key_tables(after(signed, tokens, w_qkv_t), head_n, [far_z], tables, f32)
 
     far_zo = after(far_zo, tables)
     tables = key_tables(signed, head_n, [far_zo], tables, bf16)
@@ -618,10 +618,11 @@
     e_o_moved = over_seq(e_o)
     e = query_estimates(signed, head_n, near, after(far, e_o), tables, f32)
     e_far = after(e_far, e)
-    weights = after(weights, e_far)
+    e_o_moved = after(e_o_moved, e)
+    weights = after(weights, e_far, e_o_moved)
     weights = [weights, over_seq(weights)]
     w_qkv_t = lax.all_gather(after(w_qkv_t, weights[0]), "head", axis=0)
-    attn = add(e, after(e_o_moved, e), e_far).astype(bf16)
+    attn = add(e, e_o_moved, e_far).astype(bf16)
 
     def to_dense(block):
         parts = []
@@ -660,12 +661,13 @@
     weight_sum = lax.psum_scatter(weight_parts, "head", scatter_dimension=0, tiled=True)[0]
     grad_z = over_place(grad)
     grad_o = after(over_seq(grad), weight_parts)
-    layer_moved = jnp.stack([after(x, weight_parts) for x in layer_moved])
+    layer_moved = [after(x, weight_parts) for x in layer_moved]
     part, dq, dq_o = query_backward(
-        signed, signed_t, bits, head_n, tables, [(near, after(far, layer_moved)), (near_o, far_o)], [grad, grad_o],
+        signed, signed_t, bits, head_n, tables, [(near, after(far, *layer_moved)), (near_o, far_o)], [grad, grad_o],
         None, False, [f32, bf16],
     )
 
+    layer_moved = jnp.stack([after(x, part) for x in layer_moved])
     grad_z = after(grad_z, part)
     grad_zo = over_seq(grad_z)
     dq_o = over_seq(dq_o)

time: 358 us -> 356 us (level)
  waiting for transfers between devices: 64.9 us -> 58.6 us
    ppermute x20, waiting for transfers between devices: 4.31 us -> 0.05 us  [over_seq(): return lax.ppermute(x, 'seq', [(0, 1), (1, 0)])]
    unnamed x108 -> x116, local copies, waits for them, and re-layouts: 17.7 us -> 19.3 us
  transfers between devices with their start and end apart: 55 -> 55, of which waited for: 14 -> 13; matrix products, arithmetic and copies ran while one was open for 13% -> 13% of each run, Pallas kernels for 45% -> 46%
where the time goes in v17:
time: 356 us; the launch traced here: 351 us
  Pallas kernels  165 us (46%)
  waiting for transfers between devices  58.6 us (16%)
  starting transfers between devices  50.5 us (14%)
  local copies, waits for them, and re-layouts  35 us (10%)
  other arithmetic  23.1 us (6%)
  between operations  15.2 us (4%)
  matrix products  3.89 us (1%)
    pallas_call x5, Pallas kernels, single(): pl.pallas_call(kernel, in_specs=[pl.BlockSpec(memory_space=pltpu.SMEM)] +...  43.9 us
    pallas_call x3, Pallas kernels, query_backward(): call(partial(query_back_kernel, chunk=4 * blocks, blocks=blocks, last=las...  43.2 us
    pallas_call x4, Pallas kernels, key_backward(): call(partial(key_back_kernel, chunk=4), heads, micros, 'key_backward', [w...  38.1 us
    ppermute x4, waiting for transfers between devices, over_group(): return lax.ppermute(x, 'hash', moves)  29 us
    pallas_call x5, Pallas kernels, key_tables(): call(partial(key_kernel, chunk=2, blocks=len(blocks)), heads, 30 if len(b...  23.7 us
    unnamed x116, local copies, waits for them, and re-layouts  19.3 us
    ppermute x18, starting transfers between devices, over_head(): return lax.ppermute(x, 'head', [(h, h ^ j) for h in range(head_count)])  17 us
    pallas_call x4, Pallas kernels, query_estimates(): call(partial(query_kernel, chunk=2), heads, 1, 'query_estimates', [whole(...  15.9 us
  transfers between devices with their start and end apart: 55, of which 13 were waited for; matrix products, arithmetic and copies ran while one was open for 13% of the time, Pallas kernels for 46%

profile of v17, /device:TPU:1, one launch (start us, length us, event | category | flops | bytes accessed | tf_op | source)
XLA Modules:
  0.0 350.9 jit_solution(7912064106847405444)
XLA Ops:
  7.3 4.5 %constant_dynamic-slice_fusion.7 = (bf16[1,128,1,768]{3,2,1,0:T(2,128)(2,1)S(1)}, bf16[1,128,1,768]{3,2,1,0:T(2,128)(2,1)}, bf16[1,128,1,768]{3,2,1,0:T(2,128)(2...) fusion(bf16[1,512,2,768]{3,2,1,0:T(2,128)(2,1)} %param.11, s32[]{:T(128)S(6)} %select_n.222, ...), kind=kLoop, calls=%fused_computation.119 | loop fusion | bytes 1966104 | tf_op jit(solution)/shard_map/jit(dynamic_index_in_dim)/dynamic_slice | solution.py:529
  12.6 3.1 collective-permute-start
  16.3 2.5 collective-permute-start.1
  20.5 2.4 copy.54
  22.9 2.0 dynamic-slice_bitcast_fusion
  24.9 1.9 constant_dynamic-slice_fusion.3
  31.2 1.7 collective-permute-start.8
  37.6 1.7 pad_maximum_fusion.9.x_in
  39.4 5.2 %key_tables.5.refs_4_ = f32[3,2048,64]{2,1,0:T(8,128)S(1)} custom-call(bf16[64,64]{1,0:T(8,128)(2,1)S(1)} %bitcast.126, bf16[576,512]{1,0:T(8,128)(2,1)} %bitcast.14.refs_0_.refs_2_.ka.va, bf16[576,512]{1,0:T(8,128)(2,1)} %collective-permute-done.2.refs_1_.refs_3_.refs_0_.refs_2_.ka.va, bf16[576,512]{1,0:T(8,128)(2,1)} %bitcast.14.refs_0_.refs_2_.ka.va, ...), custom_call_target="tpu_custom_call" | custom-call | flops 1100000000 | bytes 1048576 | tf_op jit(solution)/shard_map/key_tables/pallas_call | solution.py:192
  44.6 1.8 collective-permute-done.8.refs_0_.refs_2_.ka.va
  49.5 1.7 collective-permute-start.7
  53.2 5.8 %key_tables.6.refs_4_ = f32[3,2048,64]{2,1,0:T(8,128)S(1)} custom-call(bf16[64,64]{1,0:T(8,128)(2,1)S(1)} %bitcast.127, bf16[576,512]{1,0:T(8,128)(2,1)} %collective-permute-done.8.refs_0_.refs_2_.ka.va, bf16[576,512]{1,0:T(8,128)(2,1)S(1)} %collective-permute-done.9.refs_1_.refs_3_.refs_0_.ka.va, ...), custom_call_target="tpu_custom_call" | custom-call | flops 32999999488 | bytes 1048576 | tf_op jit(solution)/shard_map/key_tables/pallas_call | solution.py:192
  59.0 1.7 copy-done.16
  60.7 5.7 %key_tables.7.refs_2_ = f32[3,2048,64]{2,1,0:T(8,128)S(1)} custom-call(bf16[64,64]{1,0:T(8,128)(2,1)S(1)} %bitcast.128, bf16[576,512]{1,0:T(8,128)(2,1)S(1)} %bitcast.120, bf16[576,512]{1,0:T(8,128)(2,1)S(1)} %collective-permute-done.7.refs_1_.refs_3_.kb.vb, bf16[576,512]{1,0:T(8,128)(2,1)S(1)} %bitcast.121, ...), custom_call_target="tpu_custom_call" | custom-call | flops 32999999488 | bytes 1048576 | tf_op jit(solution)/shard_map/key_tables/pallas_call | solution.py:192
  66.4 1.9 copy-done.2
  69.4 4.4 %key_tables.8.refs_2_ = f32[3,2048,64]{2,1,0:T(8,128)S(1)} custom-call(bf16[64,64]{1,0:T(8,128)(2,1)S(1)} %bitcast.129, bf16[576,512]{1,0:T(8,128)(2,1)} %collective-permute-done.6.refs_0_.refs_1_.kb.vb, bf16[576,512]{1,0:T(8,128)(2,1)} %collective-permute-done.6.refs_0_.refs_1_.kb.vb, f32[3,2048,64]{2,1,0:T(8,128)} %copy-done.2), custom_call_target="tpu_custom_call" | custom-call | flops 1100000000 | bytes 1048576 | tf_op jit(solution)/shard_map/key_tables/pallas_call | solution.py:192
  73.8 2.6 key_tables.9.tables
  76.4 3.3 query_estimates.4
  80.1 4.2 %query_estimates.5 = bf16[192,1024]{1,0:T(8,128)(2,1)S(1)} custom-call(bf16[64,64]{1,0:T(8,128)(2,1)S(1)} %bitcast.132, bf16[3,2048,64]{2,1,0:T(8,128)(2,1)S(1)} %key_tables.9.tables, bf16[576,512]{1,0:T(8,128)(2,1)} %collective-permute-done.8.refs_0_.refs_2_.ka.va, bf16[576,512]{1,0:T(8,128)(2,1)} %collective-permute-done.6.refs_0_.refs_1_.kb.vb), custom_call_target="tpu_custom_call" | custom-call | flops 1100000000 | bytes 1048576 | tf_op jit(solution)/shard_map/query_estimates/pallas_call | solution.py:205
  84.4 4.2 %query_estimates.6 = bf16[192,1024]{1,0:T(8,128)(2,1)S(1)} custom-call(bf16[64,64]{1,0:T(8,128)(2,1)S(1)} %bitcast.133, bf16[3,2048,64]{2,1,0:T(8,128)(2,1)S(1)} %key_tables.9.tables, bf16[576,512]{1,0:T(8,128)(2,1)} %collective-permute-done.2.refs_1_.refs_3_.refs_0_.refs_2_.ka.va, bf16[576,512]{1,0:T(8,128)(2,1)S(1)} %copy-done.9), custom_call_target="tpu_custom_call" | custom-call | flops 1100000000 | bytes 1048576 | tf_op jit(solution)/shard_map/query_estimates/pallas_call | solution.py:205
  90.0 4.1 %query_estimates.7 = f32[192,1024]{1,0:T(8,128)S(1)} custom-call(bf16[64,64]{1,0:T(8,128)(2,1)S(1)} %bitcast.134, bf16[3,2048,64]{2,1,0:T(8,128)(2,1)S(1)} %key_tables.9.tables, bf16[576,512]{1,0:T(8,128)(2,1)} %bitcast.14.refs_0_.refs_2_.ka.va, bf16[576,512]{1,0:T(8,128)(2,1)S(1)} %bitcast.122), custom_call_target="tpu_custom_call" | custom-call | flops 1100000000 | bytes 1048576 | tf_op jit(solution)/shard_map/query_estimates/pallas_call | solution.py:205
  94.9 4.7 %collective-permute-done.13 = bf16[192,1024]{1,0:T(8,128)(2,1)} collective-permute-done((bf16[192,1024]{1,0:T(8,128)(2,1)S(1)}, bf16[192,1024]{1,0:T(8,128)(2,1)}, u32[]{:S(2)}, u32[]{:S(2)}) %collective-permute-start.13) | collective-permute-done | bytes 393248 | tf_op jit(solution)/shard_map/ppermute | solution.py:519
  102.9 2.2 collective-permute-start.16
  108.3 2.4 collective-permute-done.15.refs_2_.refs_6_
  111.7 12.7 %dense.1 = (bf16[256,768]{1,0:T(8,128)(2,1)}, f32[256,768]{1,0:T(8,128)}, f32[256,768]{1,0:T(8,128)}, f32[8,256,384]{2,1,0:T(8,128)}, bf16[8,256,384]{2,1,0:T(8,...) custom-call(s32[2]{0:T(128)} %pad_add_fusion.core, ...), custom_call_target="tpu_custom_call" | custom-call | flops 15399999488 | bytes 1048576 | tf_op jit(solution)/shard_map/dense/pallas_call | solution.py:402
  124.4 12.6 %dense_back.1 = (f32[256,768]{1,0:T(8,128)}, bf16[6,256,384]{2,1,0:T(8,128)(2,1)}, bf16[6,256,384]{2,1,0:T(8,128)(2,1)}, bf16[192,256]{1,0:T(8,128)(2,1)}, bf16[...) custom-call(s32[2]{0:T(128)} %pad_add_fusion.core, ...), custom_call_target="tpu_custom_call" | custom-call | flops 8800000000 | bytes 1048576 | tf_op jit(solution)/shard_map/dense_back/pallas_call | solution.py:402
  139.8 1.6 collective-permute-start.22
  143.7 2.0 collective-permute-start.23
  145.8 2.5 collective-permute-start.24
  151.4 8.7 %weight_grads.1 = bf16[4,896,768]{2,1,0:T(8,128)(2,1)} custom-call(s32[2]{0:T(128)} %pad_add_fusion.core, f32[8,768]{1,0:T(8,128)} %get-tuple-element.130.small_a, f32[8,768]{1,0:T(8,128)} %get-tuple-element.131.small_b, bf16[8,256,384]{2,1,0:T(8,128)(2,1)} %get-tuple-element.132.refs_0_, bf16[8,256,384]{2,1,0:T(8,128)(2,1)} %collective-permute-done.21.refs_1_, ...), custom_call_target="tpu_custom_call" | custom-call | flops 7699999744 | bytes 1048576 | tf_op jit(solution)/shard_map/weight_grads/pallas_call | solution.py:402
  161.2 20.2 %query_backward.3 = (f32[3,2048,64]{2,1,0:T(8,128)}, f32[192,1024]{1,0:T(8,128)S(1)}, bf16[192,1024]{1,0:T(8,128)(2,1)S(1)}) custom-call(bf16[64,64]{1,0:T(8,128)(2,1)S(1)} %bitcast.136, bf16[64,128]{1,0:T(8,128)(2,1)S(1)} %pad_maximum_fusion.20.planes_t, bf16[80,2048]{1,0:T(8,128)(2,1)S(1)} %copy-done.15, bf16[3,2048,64]{2,1,0:T(8,128)(2,1)} %copy-done.4, ...), custom_call_target="tpu_custom_call" | custom-call | flops 54999998464 | bytes 1048576 | tf_op jit(solution)/shard_map/query_backward/pallas_call | solution.py:229
  181.9 11.8 %query_backward.4 = (f32[3,2048,64]{2,1,0:T(8,128)}, f32[192,1024]{1,0:T(8,128)S(1)}) custom-call(bf16[64,64]{1,0:T(8,128)(2,1)S(1)} %bitcast.137, bf16[64,128]{1,0:T(8,128)(2,1)S(1)} %pad_maximum_fusion.20.planes_t, bf16[80,2048]{1,0:T(8,128)(2,1)S(1)} %copy-done.15, bf16[3,2048,64]{2,1,0:T(8,128)(2,1)S(1)} %copy-done.5, ...), custom_call_target="tpu_custom_call" | custom-call | flops 27499999232 | bytes 1048576 | tf_op jit(solution)/shard_map/query_backward/pallas_call | solution.py:229
  197.5 11.2 %query_backward.5 = (bf16[3,2048,64]{2,1,0:T(8,128)(2,1)S(1)}, bf16[192,1024]{1,0:T(8,128)(2,1)S(1)}) custom-call(bf16[64,64]{1,0:T(8,128)(2,1)S(1)} %bitcast.138, bf16[64,128]{1,0:T(8,128)(2,1)S(1)} %pad_maximum_fusion.20.planes_t, bf16[80,2048]{1,0:T(8,128)(2,1)S(1)} %copy-done.15, bf16[3,2048,64]{2,1,0:T(8,128)(2,1)S(1)} %copy-done.5, ...), custom_call_target="tpu_custom_call" | custom-call | flops 27499999232 | bytes 1048576 | tf_op jit(solution)/shard_map/query_backward/pallas_call | solution.py:229
  210.1 8.8 %key_backward.4 = bf16[2,192,1024]{2,1,0:T(8,128)(2,1)S(1)} custom-call(bf16[64,64]{1,0:T(8,128)(2,1)S(1)} %bitcast.139, bf16[64,128]{1,0:T(8,128)(2,1)S(1)} %pad_maximum_fusion.20.planes_t, bf16[80,2048]{1,0:T(8,128)(2,1)S(1)} %copy-done.15, bf16[576,512]{1,0:T(8,128)(2,1)S(1)} %copy-done.14, ...), custom_call_target="tpu_custom_call" | custom-call | flops 27499999232 | bytes 1048576 | tf_op jit(solution)/shard_map/key_backward/pallas_call | solution.py:243
  219.4 9.8 %key_backward.5 = bf16[2,192,1024]{2,1,0:T(8,128)(2,1)S(1)} custom-call(bf16[64,64]{1,0:T(8,128)(2,1)S(1)} %bitcast.140, bf16[64,128]{1,0:T(8,128)(2,1)S(1)} %pad_maximum_fusion.20.planes_t, bf16[80,2048]{1,0:T(8,128)(2,1)S(1)} %copy-done.15, bf16[576,512]{1,0:T(8,128)(2,1)} %collective-permute-done.8.refs_0_.refs_2_.ka.va, ...), custom_call_target="tpu_custom_call" | custom-call | flops 27499999232 | bytes 1048576 | tf_op jit(solution)/shard_map/key_backward/pallas_call | solution.py:243
  234.7 9.7 %key_backward.7 = bf16[2,192,1024]{2,1,0:T(8,128)(2,1)S(1)} custom-call(bf16[64,64]{1,0:T(8,128)(2,1)S(1)} %bitcast.141, bf16[64,128]{1,0:T(8,128)(2,1)S(1)} %pad_maximum_fusion.20.planes_t, bf16[80,2048]{1,0:T(8,128)(2,1)S(1)} %copy-done.15, bf16[576,512]{1,0:T(8,128)(2,1)} %collective-permute-done.2.refs_1_.refs_3_.refs_0_.refs_2_.ka.va, ...), custom_call_target="tpu_custom_call" | custom-call | flops 27499999232 | bytes 1048576 | tf_op jit(solution)/shard_map/key_backward/pallas_call | solution.py:243
  244.7 9.9 %key_backward.6 = f32[2,192,1024]{2,1,0:T(8,128)S(1)} custom-call(bf16[64,64]{1,0:T(8,128)(2,1)S(1)} %bitcast.142, bf16[64,128]{1,0:T(8,128)(2,1)S(1)} %pad_maximum_fusion.20.planes_t, bf16[80,2048]{1,0:T(8,128)(2,1)S(1)} %copy-done.15, bf16[576,512]{1,0:T(8,128)(2,1)} %bitcast.14.refs_0_.refs_2_.ka.va, bf16[576,512]{1,0:T(8,128)(2,1)S(1)} %bitcast.124, ...), custom_call_target="tpu_custom_call" | custom-call | flops 27499999232 | bytes 1048576 | tf_op jit(solution)/shard_map/key_backward/pallas_call | solution.py:243
  254.7 1.8 add_convert_fusion
  262.8 3.6 %collective-permute-done.39.refs_3_ = bf16[3,192,256]{2,1,0:T(8,128)(2,1)S(1)} collective-permute-done((bf16[3,192,256]{2,1,0:T(8,128)(2,1)S(1)}, bf16[3,192,256]{2,1,0:T(8,128)(2,1)S(1)}, u32[]{:S(2)}, u32[]{:S(2)}) %collective-permute-start.39) | collective-permute-done | bytes 294944 | tf_op jit(solution)/shard_map/ppermute | solution.py:526
  266.4 6.8 %collective-permute-done.38.refs_2_ = bf16[3,192,256]{2,1,0:T(8,128)(2,1)S(1)} collective-permute-done((bf16[3,192,256]{2,1,0:T(8,128)(2,1)S(1)}, bf16[3,192,256]{2,1,0:T(8,128)(2,1)S(1)}, u32[]{:S(2)}, u32[]{:S(2)}) %collective-permute-start.38) | collective-permute-done | bytes 294944 | tf_op jit(solution)/shard_map/ppermute | solution.py:526
  274.0 5.2 %input_grad.1 = bf16[256,768]{1,0:T(8,128)(2,1)} custom-call(s32[2]{0:T(128)} %pad_add_fusion.core, f32[256,768]{1,0:T(8,128)} %get-tuple-element.157.grad_first, bf16[3,192,256]{2,1,0:T(8,128)(2,1)} %pad_maximum_fusion.12.refs_0_, bf16[3,192,256]{2,1,0:T(8,128)(2,1)} %copy-done.45, bf16[3,192,256]{2,1,0:T(8,128)(2,1)} %copy-done.44, ...), custom_call_target="tpu_custom_call" | custom-call | flops 44000002048 | bytes 1048576 | tf_op jit(solution)/shard_map/input_grad/pallas_call | solution.py:402
  282.6 9.3 %collective-permute-done.41 = bf16[128,768]{1,0:T(8,128)(2,1)S(1)} collective-permute-done((bf16[128,768]{1,0:T(8,128)(2,1)S(1)}, bf16[128,768]{1,0:T(8,128)(2,1)S(1)}, u32[]{:S(2)}, u32[]{:S(2)}) %collective-permute-start.41) | collective-permute-done | bytes 196640 | tf_op jit(solution)/shard_map/ppermute | solution.py:523
  294.7 1.6 collective-permute-start.47
  297.1 2.8 copy.56
  299.9 19.8 %collective-permute-done.47 = bf16[144,768]{1,0:T(8,128)(2,1)S(1)} collective-permute-done((bf16[144,768]{1,0:T(8,128)(2,1)S(1)}, bf16[144,768]{1,0:T(8,128)(2,1)S(1)}, u32[]{:S(2)}, u32[]{:S(2)}) %collective-permute-start.47) | collective-permute-done | bytes 221216 | tf_op jit(solution)/shard_map/ppermute | solution.py:523
  319.8 6.3 %all-reduce.3.cloned.1.call-done.near = bf16[896,768]{1,0:T(8,128)(2,1)} async-done(((bf16[896,768]{1,0:T(8,128)(2,1)}), bf16[896,768]{1,0:T(8,128)(2,1)}) %all-reduce.3.cloned.1.call-update) | async-done | bytes 1376272 | tf_op jit(solution)/shard_map/psum | solution.py:703
  331.1 4.1 %copy.57 = f32[1,512,2,768]{3,2,1,0:T(2,128)} copy(f32[1,512,2,768]{3,1,2,0:T(8,128)S(1)} %maximum_convert_fusion) | data formatting | bytes 6291456
  339.4 4.7 %weight_results.1 = (f32[768,768]{1,0:T(8,128)}, f32[768,768]{1,0:T(8,128)}, f32[192,768]{1,0:T(8,128)}) custom-call(s32[2]{0:T(128)} %pad_add_fusion.core, bf16[896,768]{1,0:T(8,128)(2,1)} %all-reduce.3.cloned.1.call-done.near, bf16[896,768]{1,0:T(8,128)(2,1)} %copy-done.42), custom_call_target="tpu_custom_call" | custom-call | flops 3300000000 | bytes 1048576 | tf_op jit(solution)/shard_map/weight_results/pallas_call | solution.py:402
  (276 shorter events, 72.7 us)
Async XLA Ops:
  7.2 92.4 %all-gather.5.cloned.1.call-start = ((), (), s32[]{:S(2)}) async-start(), calls=%async_computation.2 | async-start | bytes 6635520 | tf_op jit(solution)/shard_map/all_gather | solution.py:564
  12.6 17.1 %collective-permute-start = (bf16[128,768]{1,0:T(8,128)(2,1)}, bf16[128,768]{1,0:T(8,128)(2,1)}, u32[]{:S(2)}, u32[]{:S(2)}) collective-permute-start(bf16[128,768]{1,0:T(8,128)(2,1)} %bitcast.116), channel_id=1, source_target_pairs={{0,16},{8,24},{16,0},{24,8},{1,17},{9,25},{17,1},{25,9},{2,18},{10... | collective-permute-start | bytes 589832 | tf_op jit(solution)/shard_map/ppermute | solution.py:523
  16.3 21.1 %collective-permute-start.1 = (bf16[8,8,64]{2,0,1:T(8,128)(2,1)}, bf16[8,8,64]{2,0,1:T(8,128)(2,1)S(1)}, u32[]{:S(2)}, u32[]{:S(2)}) collective-permute-start(bf16[8,8,64]{2,0,1:T(8,128)(2,1)} %fusion.16), channel_id=1, source_target_pairs={{0,0},{8,1},{16,8},{24,9},{1,16},{9,17},{17,24},{25,25},{2,2},{10,... | collective-permute-start | bytes 24584 | tf_op jit(solution)/shard_map/ppermute | solution.py:548
  31.2 8.2 %collective-permute-start.2 = (bf16[576,512]{1,0:T(8,128)(2,1)}, bf16[576,512]{1,0:T(8,128)(2,1)}, u32[]{:S(2)}, u32[]{:S(2)}) collective-permute-start(bf16[576,512]{1,0:T(8,128)(2,1)} %bitcast.14.refs_0_.refs_2_.ka.va), channel_id=1, source_target_pairs={{0,1},{1,0},{2,3},{3,2},{4,5},{5,4},{6,7},{7,6},{8,9},{9,8},{10,11... | collective-permute-start | bytes 1769480 | tf_op jit(solution)/shard_map/ppermute | solution.py:516
  31.2 15.2 %collective-permute-start.8 = (bf16[576,512]{1,0:T(8,128)(2,1)}, bf16[576,512]{1,0:T(8,128)(2,1)}, u32[]{:S(2)}, u32[]{:S(2)}) collective-permute-start(bf16[576,512]{1,0:T(8,128)(2,1)} %bitcast.14.refs_0_.refs_2_.ka.va), channel_id=1, source_target_pairs={{0,8},{8,0},{16,24},{24,16},{1,9},{9,1},{17,25},{25,17},{2,10},{10... | collective-permute-start | bytes 1769480 | tf_op jit(solution)/shard_map/ppermute | solution.py:519
  34.1 116.0 %all-gather.7.cloned.1.call-start = ((), (), s32[]{:S(2)}) async-start(), calls=%async_computation.3 | async-start | bytes 2211840 | tf_op jit(solution)/shard_map/all_gather | solution.py:624
  35.0 12.5 %collective-permute-start.3 = (bf16[1,128,768]{2,1,0:T(8,128)(2,1)}, bf16[1,128,768]{2,1,0:T(8,128)(2,1)S(1)}, u32[]{:S(2)}, u32[]{:S(2)}) collective-permute-start(bf16[1,128,768]{2,1,0:T(8,128)(2,1)} %bitcast.20), channel_id=1, source_target_pairs={{0,2},{2,0},{4,6},{6,4},{1,3},{3,1},{5,7},{7,5},{8,10},{10,8},{12,... | collective-permute-start | bytes 589832 | tf_op jit(solution)/shard_map/ppermute | solution.py:526
  36.2 11.3 %collective-permute-start.4 = (bf16[1,128,768]{2,1,0:T(8,128)(2,1)}, bf16[1,128,768]{2,1,0:T(8,128)(2,1)S(1)}, u32[]{:S(2)}, u32[]{:S(2)}) collective-permute-start(bf16[1,128,768]{2,1,0:T(8,128)(2,1)} %bitcast.20), channel_id=1, source_target_pairs={{0,4},{2,6},{4,0},{6,2},{1,5},{3,7},{5,1},{7,3},{8,12},{10,14},{12... | collective-permute-start | bytes 589832 | tf_op jit(solution)/shard_map/ppermute | solution.py:526
  37.4 10.1 %collective-permute-start.5 = (bf16[1,128,768]{2,1,0:T(8,128)(2,1)}, bf16[1,128,768]{2,1,0:T(8,128)(2,1)S(1)}, u32[]{:S(2)}, u32[]{:S(2)}) collective-permute-start(bf16[1,128,768]{2,1,0:T(8,128)(2,1)} %bitcast.20), channel_id=1, source_target_pairs={{0,6},{2,4},{4,2},{6,0},{1,7},{3,5},{5,3},{7,1},{8,14},{10,12},{12... | collective-permute-start | bytes 589832 | tf_op jit(solution)/shard_map/ppermute | solution.py:526
  46.4 6.8 %collective-permute-start.9 = (bf16[576,512]{1,0:T(8,128)(2,1)}, bf16[576,512]{1,0:T(8,128)(2,1)S(1)}, u32[]{:S(2)}, u32[]{:S(2)}) collective-permute-start(bf16[576,512]{1,0:T(8,128)(2,1)} %collective-permute-done.8.refs_0_.refs_2_.ka.va), channel_id=1, source_target_pairs={{0,1},{1,0},{2,3},{3,2},{4,5},{5,4},{6,7},{7,6},{8,9},{9,8},{10,11... | collective-permute-start | bytes 1769480 | tf_op jit(solution)/shard_map/ppermute | solution.py:516
  49.5 11.2 %collective-permute-start.7 = (bf16[576,512]{1,0:T(8,128)(2,1)S(1)}, bf16[576,512]{1,0:T(8,128)(2,1)S(1)}, u32[]{:S(2)}, u32[]{:S(2)}) collective-permute-start(bf16[576,512]{1,0:T(8,128)(2,1)S(1)} %bitcast.118), channel_id=1, source_target_pairs={{0,1},{1,0},{2,3},{3,2},{4,5},{5,4},{6,7},{7,6},{8,9},{9,8},{10,11... | collective-permute-start | bytes 1769480 | tf_op jit(solution)/shard_map/ppermute | solution.py:516
  51.2 17.1 %collective-permute-start.6 = (bf16[576,512]{1,0:T(8,128)(2,1)S(1)}, bf16[576,512]{1,0:T(8,128)(2,1)}, u32[]{:S(2)}, u32[]{:S(2)}) collective-permute-start(bf16[576,512]{1,0:T(8,128)(2,1)S(1)} %bitcast.119), channel_id=1, source_target_pairs={{0,8},{8,0},{16,24},{24,16},{1,9},{9,1},{17,25},{25,17},{2,10},{10... | collective-permute-start | bytes 1769480 | tf_op jit(solution)/shard_map/ppermute | solution.py:519
  89.0 10.6 %collective-permute-start.13 = (bf16[192,1024]{1,0:T(8,128)(2,1)S(1)}, bf16[192,1024]{1,0:T(8,128)(2,1)}, u32[]{:S(2)}, u32[]{:S(2)}) collective-permute-start(bf16[192,1024]{1,0:T(8,128)(2,1)S(1)} %add_convert_fusion.6), channel_id=1, source_target_pairs={{0,8},{8,0},{16,24},{24,16},{1,9},{9,1},{17,25},{25,17},{2,10},{10... | collective-permute-start | bytes 1179656 | tf_op jit(solution)/shard_map/ppermute | solution.py:519
  99.6 11.7 %collective-permute-start.17 = (bf16[4,864,768]{2,1,0:T(8,128)(2,1)}, bf16[4,864,768]{2,1,0:T(8,128)(2,1)}, u32[]{:S(2)}, u32[]{:S(2)}) collective-permute-start(bf16[4,864,768]{2,1,0:T(8,128)(2,1)} %bitcast.170), channel_id=1, source_target_pairs={{0,1},{1,0},{2,3},{3,2},{4,5},{5,4},{6,7},{7,6},{8,9},{9,8},{10,11... | collective-permute-start | bytes 15925256 | tf_op jit(solution)/shard_map/ppermute | solution.py:516
  111.0 122.2 %reduce-scatter.4.cloned.1.call-start = ((), (), s32[]{:S(2)}) async-start(), calls=%async_computation.4 | async-start | bytes 6881280
  137.0 6.8 %collective-permute-start.18 = (bf16[192,256]{1,0:T(8,128)(2,1)}, bf16[192,256]{1,0:T(8,128)(2,1)S(1)}, u32[]{:S(2)}, u32[]{:S(2)}) collective-permute-start(bf16[192,256]{1,0:T(8,128)(2,1)} %get-tuple-element.123), channel_id=1, source_target_pairs={{0,2},{2,0},{4,6},{6,4},{1,3},{3,1},{5,7},{7,5},{8,10},{10,8},{12,... | collective-permute-start | bytes 294920 | tf_op jit(solution)/shard_map/ppermute | solution.py:526
  138.4 7.3 %collective-permute-start.19 = (bf16[192,256]{1,0:T(8,128)(2,1)}, bf16[192,256]{1,0:T(8,128)(2,1)S(1)}, u32[]{:S(2)}, u32[]{:S(2)}) collective-permute-start(bf16[192,256]{1,0:T(8,128)(2,1)} %get-tuple-element.124), channel_id=1, source_target_pairs={{0,4},{2,6},{4,0},{6,2},{1,5},{3,7},{5,1},{7,3},{8,12},{10,14},{12... | collective-permute-start | bytes 294920 | tf_op jit(solution)/shard_map/ppermute | solution.py:526
  138.8 9.6 %collective-permute-start.20 = (bf16[192,256]{1,0:T(8,128)(2,1)}, bf16[192,256]{1,0:T(8,128)(2,1)S(1)}, u32[]{:S(2)}, u32[]{:S(2)}) collective-permute-start(bf16[192,256]{1,0:T(8,128)(2,1)} %get-tuple-element.125), channel_id=1, source_target_pairs={{0,6},{2,4},{4,2},{6,0},{1,7},{3,5},{5,3},{7,1},{8,14},{10,12},{12... | collective-permute-start | bytes 294920 | tf_op jit(solution)/shard_map/ppermute | solution.py:526
  139.8 11.6 %collective-permute-start.22 = (bf16[6,256,384]{2,1,0:T(8,128)(2,1)}, bf16[6,256,384]{2,1,0:T(8,128)(2,1)}, u32[]{:S(2)}, u32[]{:S(2)}) collective-permute-start(bf16[6,256,384]{2,1,0:T(8,128)(2,1)} %get-tuple-element.135), channel_id=1, source_target_pairs={{0,1},{1,0},{2,3},{3,2},{4,5},{5,4},{6,7},{7,6},{8,9},{9,8},{10,11... | collective-permute-start | bytes 3538952 | tf_op jit(solution)/shard_map/ppermute | solution.py:516
  141.3 10.0 %collective-permute-start.21 = (bf16[8,256,384]{2,1,0:T(8,128)(2,1)}, bf16[8,256,384]{2,1,0:T(8,128)(2,1)}, u32[]{:S(2)}, u32[]{:S(2)}) collective-permute-start(bf16[8,256,384]{2,1,0:T(8,128)(2,1)} %get-tuple-element.133), channel_id=1, source_target_pairs={{0,1},{1,0},{2,3},{3,2},{4,5},{5,4},{6,7},{7,6},{8,9},{9,8},{10,11... | collective-permute-start | bytes 4718600 | tf_op jit(solution)/shard_map/ppermute | solution.py:516
  143.7 6.4 %collective-permute-start.23 = (bf16[4,96,256]{2,1,0:T(8,128)(2,1)S(1)}, bf16[4,96,256]{2,1,0:T(8,128)(2,1)S(1)}, u32[]{:S(2)}, u32[]{:S(2)}) collective-permute-start(bf16[4,96,256]{2,1,0:T(8,128)(2,1)S(1)} %copy-done.46), channel_id=1, source_target_pairs={{0,1},{1,0},{2,3},{3,2},{4,5},{5,4},{6,7},{7,6},{8,9},{9,8},{10,11... | collective-permute-start | bytes 589832 | tf_op jit(solution)/shard_map/ppermute | solution.py:516
  145.8 14.4 %collective-permute-start.24 = (bf16[128,768]{1,0:T(8,128)(2,1)}, bf16[128,768]{1,0:T(8,128)(2,1)}, u32[]{:S(2)}, u32[]{:S(2)}) collective-permute-start(bf16[128,768]{1,0:T(8,128)(2,1)} %get-tuple-element.235), channel_id=1, source_target_pairs={{0,16},{8,24},{16,0},{24,8},{1,17},{9,25},{17,1},{25,9},{2,18},{10... | collective-permute-start | bytes 589832 | tf_op jit(solution)/shard_map/ppermute | solution.py:523
  149.4 10.7 %collective-permute-start.25 = (bf16[192,1024]{1,0:T(8,128)(2,1)S(1)}, bf16[192,1024]{1,0:T(8,128)(2,1)S(1)}, u32[]{:S(2)}, u32[]{:S(2)}) collective-permute-start(bf16[192,1024]{1,0:T(8,128)(2,1)S(1)} %slice_dynamic-update-slice_fusion.refs_4_), channel_id=1, source_target_pairs={{0,1},{1,0},{2,3},{3,2},{4,5},{5,4},{6,7},{7,6},{8,9},{9,8},{10,11... | collective-permute-start | bytes 1179656 | tf_op jit(solution)/shard_map/ppermute | solution.py:516
  150.1 31.2 %collective-permute-start.26 = (bf16[192,1024]{1,0:T(8,128)(2,1)S(1)}, bf16[192,1024]{1,0:T(8,128)(2,1)S(1)}, u32[]{:S(2)}, u32[]{:S(2)}) collective-permute-start(bf16[192,1024]{1,0:T(8,128)(2,1)S(1)} %slice_dynamic-update-slice_fusion.refs_4_), channel_id=1, source_target_pairs={{0,8},{8,0},{16,24},{24,16},{1,9},{9,1},{17,25},{25,17},{2,10},{10... | collective-permute-start | bytes 1179656 | tf_op jit(solution)/shard_map/ppermute | solution.py:519
  160.1 166.1 %all-reduce.3.cloned.1.call-start = ((), (), s32[]{:S(2)}) async-start(), calls=%async_computation.1 | async-start | bytes 2752512 | tf_op jit(solution)/shard_map/psum | solution.py:703
  181.4 16.1 %collective-permute-start.28 = (bf16[192,1024]{1,0:T(8,128)(2,1)S(1)}, bf16[192,1024]{1,0:T(8,128)(2,1)S(1)}, u32[]{:S(2)}, u32[]{:S(2)}) collective-permute-start(bf16[192,1024]{1,0:T(8,128)(2,1)S(1)} %collective-permute-done.26.refs_2_), channel_id=1, source_target_pairs={{0,1},{1,0},{2,3},{3,2},{4,5},{5,4},{6,7},{7,6},{8,9},{9,8},{10,11... | collective-permute-start | bytes 1179656 | tf_op jit(solution)/shard_map/ppermute | solution.py:516
  181.8 15.6 %collective-permute-start.27 = (bf16[192,1024]{1,0:T(8,128)(2,1)S(1)}, bf16[192,1024]{1,0:T(8,128)(2,1)S(1)}, u32[]{:S(2)}, u32[]{:S(2)}) collective-permute-start(bf16[192,1024]{1,0:T(8,128)(2,1)S(1)} %get-tuple-element.147), channel_id=1, source_target_pairs={{0,1},{1,0},{2,3},{3,2},{4,5},{5,4},{6,7},{7,6},{8,9},{9,8},{10,11... | collective-permute-start | bytes 1179656 | tf_op jit(solution)/shard_map/ppermute | solution.py:516
  194.7 34.5 %collective-permute-start.33 = (bf16[2,128,768]{2,1,0:T(8,128)(2,1)S(1)}, bf16[2,128,768]{2,1,0:T(8,128)(2,1)S(1)}, u32[]{:S(2)}, u32[]{:S(2)}) collective-permute-start(bf16[2,128,768]{2,1,0:T(8,128)(2,1)S(1)} %pad_maximum_fusion.10), channel_id=1, source_target_pairs={{0,4},{2,6},{4,0},{6,2},{1,5},{3,7},{5,1},{7,3},{8,12},{10,14},{12... | collective-permute-start | bytes 1179656 | tf_op jit(solution)/shard_map/ppermute | solution.py:526
  195.0 35.0 %collective-permute-start.32 = (bf16[2,128,768]{2,1,0:T(8,128)(2,1)S(1)}, bf16[2,128,768]{2,1,0:T(8,128)(2,1)S(1)}, u32[]{:S(2)}, u32[]{:S(2)}) collective-permute-start(bf16[2,128,768]{2,1,0:T(8,128)(2,1)S(1)} %pad_maximum_fusion.10), channel_id=1, source_target_pairs={{0,2},{2,0},{4,6},{6,4},{1,3},{3,1},{5,7},{7,5},{8,10},{10,8},{12,... | collective-permute-start | bytes 1179656 | tf_op jit(solution)/shard_map/ppermute | solution.py:526
  196.3 33.7 %collective-permute-start.34 = (bf16[2,128,768]{2,1,0:T(8,128)(2,1)S(1)}, bf16[2,128,768]{2,1,0:T(8,128)(2,1)S(1)}, u32[]{:S(2)}, u32[]{:S(2)}) collective-permute-start(bf16[2,128,768]{2,1,0:T(8,128)(2,1)S(1)} %pad_maximum_fusion.10), channel_id=1, source_target_pairs={{0,6},{2,4},{4,2},{6,0},{1,7},{3,5},{5,3},{7,1},{8,14},{10,12},{12... | collective-permute-start | bytes 1179656 | tf_op jit(solution)/shard_map/ppermute | solution.py:526
  208.8 10.2 %collective-permute-start.29 = (bf16[192,1024]{1,0:T(8,128)(2,1)S(1)}, bf16[192,1024]{1,0:T(8,128)(2,1)S(1)}, u32[]{:S(2)}, u32[]{:S(2)}) collective-permute-start(bf16[192,1024]{1,0:T(8,128)(2,1)S(1)} %get-tuple-element.152), channel_id=1, source_target_pairs={{0,1},{1,0},{2,3},{3,2},{4,5},{5,4},{6,7},{7,6},{8,9},{9,8},{10,11... | collective-permute-start | bytes 1179656 | tf_op jit(solution)/shard_map/ppermute | solution.py:516
  218.9 11.2 %collective-permute-start.31 = (bf16[2,192,1024]{2,1,0:T(8,128)(2,1)S(1)}, bf16[2,192,1024]{2,1,0:T(8,128)(2,1)S(1)}, u32[]{:S(2)}, u32[]{:S(2)}) collective-permute-start(bf16[2,192,1024]{2,1,0:T(8,128)(2,1)S(1)} %key_backward.4), channel_id=1, source_target_pairs={{0,1},{1,0},{2,3},{3,2},{4,5},{5,4},{6,7},{7,6},{8,9},{9,8},{10,11... | collective-permute-start | bytes 2359304 | tf_op jit(solution)/shard_map/ppermute | solution.py:516
  219.0 11.0 %collective-permute-start.30 = (bf16[192,1024]{1,0:T(8,128)(2,1)S(1)}, bf16[192,1024]{1,0:T(8,128)(2,1)S(1)}, u32[]{:S(2)}, u32[]{:S(2)}) collective-permute-start(bf16[192,1024]{1,0:T(8,128)(2,1)S(1)} %add_convert_fusion.4), channel_id=1, source_target_pairs={{0,8},{8,0},{16,24},{24,16},{1,9},{9,1},{17,25},{25,17},{2,10},{10... | collective-permute-start | bytes 1179656 | tf_op jit(solution)/shard_map/ppermute | solution.py:519
  229.2 25.4 %collective-permute-start.40 = (bf16[4,3,96,768]{3,2,1,0:T(8,128)(2,1)}, bf16[4,3,96,768]{3,2,1,0:T(8,128)(2,1)}, u32[]{:S(2)}, u32[]{:S(2)}) collective-permute-start(bf16[4,3,96,768]{3,2,1,0:T(8,128)(2,1)} %bitcast.34.refs_4_), channel_id=1, source_target_pairs={{0,1},{1,0},{2,3},{3,2},{4,5},{5,4},{6,7},{7,6},{8,9},{9,8},{10,11... | collective-permute-start | bytes 5308424 | tf_op jit(solution)/shard_map/ppermute | solution.py:516
  231.3 23.4 %collective-permute-start.36 = (bf16[2,192,1024]{2,1,0:T(8,128)(2,1)}, bf16[2,192,1024]{2,1,0:T(8,128)(2,1)}, u32[]{:S(2)}, u32[]{:S(2)}) collective-permute-start(bf16[2,192,1024]{2,1,0:T(8,128)(2,1)} %add_convert_fusion.1), channel_id=1, source_target_pairs={{0,8},{8,0},{16,24},{24,16},{1,9},{9,1},{17,25},{25,17},{2,10},{10... | collective-permute-start | bytes 2359304 | tf_op jit(solution)/shard_map/ppermute | solution.py:519
  244.4 10.4 %collective-permute-start.35 = (bf16[2,192,1024]{2,1,0:T(8,128)(2,1)S(1)}, bf16[2,192,1024]{2,1,0:T(8,128)(2,1)}, u32[]{:S(2)}, u32[]{:S(2)}) collective-permute-start(bf16[2,192,1024]{2,1,0:T(8,128)(2,1)S(1)} %key_backward.7), channel_id=1, source_target_pairs={{0,1},{1,0},{2,3},{3,2},{4,5},{5,4},{6,7},{7,6},{8,9},{9,8},{10,11... | collective-permute-start | bytes 2359304 | tf_op jit(solution)/shard_map/ppermute | solution.py:516
  256.9 9.5 %collective-permute-start.39 = (bf16[3,192,256]{2,1,0:T(8,128)(2,1)S(1)}, bf16[3,192,256]{2,1,0:T(8,128)(2,1)S(1)}, u32[]{:S(2)}, u32[]{:S(2)}) collective-permute-start(bf16[3,192,256]{2,1,0:T(8,128)(2,1)S(1)} %pad_maximum_fusion.15), channel_id=1, source_target_pairs={{0,6},{2,4},{4,2},{6,0},{1,7},{3,5},{5,3},{7,1},{8,14},{10,12},{12... | collective-permute-start | bytes 884744 | tf_op jit(solution)/shard_map/ppermute | solution.py:526
  258.3 14.9 %collective-permute-start.38 = (bf16[3,192,256]{2,1,0:T(8,128)(2,1)S(1)}, bf16[3,192,256]{2,1,0:T(8,128)(2,1)S(1)}, u32[]{:S(2)}, u32[]{:S(2)}) collective-permute-start(bf16[3,192,256]{2,1,0:T(8,128)(2,1)S(1)} %pad_maximum_fusion.14), channel_id=1, source_target_pairs={{0,4},{2,6},{4,0},{6,2},{1,5},{3,7},{5,1},{7,3},{8,12},{10,14},{12... | collective-permute-start | bytes 884744 | tf_op jit(solution)/shard_map/ppermute | solution.py:526
  259.3 13.9 %collective-permute-start.37 = (bf16[3,192,256]{2,1,0:T(8,128)(2,1)S(1)}, bf16[3,192,256]{2,1,0:T(8,128)(2,1)S(1)}, u32[]{:S(2)}, u32[]{:S(2)}) collective-permute-start(bf16[3,192,256]{2,1,0:T(8,128)(2,1)S(1)} %pad_maximum_fusion.13), channel_id=1, source_target_pairs={{0,2},{2,0},{4,6},{6,4},{1,3},{3,1},{5,7},{7,5},{8,10},{10,8},{12,... | collective-permute-start | bytes 884744 | tf_op jit(solution)/shard_map/ppermute | solution.py:526
  260.9 20.8 %collective-permute-start.42 = (bf16[288,768]{1,0:T(8,128)(2,1)S(1)}, bf16[288,768]{1,0:T(8,128)(2,1)S(1)}, u32[]{:S(2)}, u32[]{:S(2)}) collective-permute-start(bf16[288,768]{1,0:T(8,128)(2,1)S(1)} %constant_dynamic-slice_fusion.1), channel_id=1, source_target_pairs={{0,1},{1,0},{2,3},{3,2},{4,5},{5,4},{6,7},{7,6},{8,9},{9,8},{10,11... | collective-permute-start | bytes 1327112 | tf_op jit(solution)/shard_map/ppermute | solution.py:516
  280.4 11.5 %collective-permute-start.41 = (bf16[128,768]{1,0:T(8,128)(2,1)S(1)}, bf16[128,768]{1,0:T(8,128)(2,1)S(1)}, u32[]{:S(2)}, u32[]{:S(2)}) collective-permute-start(bf16[128,768]{1,0:T(8,128)(2,1)S(1)} %get-tuple-element.233), channel_id=1, source_target_pairs={{0,16},{8,24},{16,0},{24,8},{1,17},{9,25},{17,1},{25,9},{2,18},{10... | collective-permute-start | bytes 589832 | tf_op jit(solution)/shard_map/ppermute | solution.py:523
  281.9 10.0 %collective-permute-start.43 = (bf16[144,768]{1,0:T(8,128)(2,1)S(1)}, bf16[144,768]{1,0:T(8,128)(2,1)S(1)}, u32[]{:S(2)}, u32[]{:S(2)}) collective-permute-start(bf16[144,768]{1,0:T(8,128)(2,1)S(1)} %constant_dynamic-slice_fusion), channel_id=1, source_target_pairs={{0,8},{8,0},{16,24},{24,16},{1,9},{9,1},{17,25},{25,17},{2,10},{10... | collective-permute-start | bytes 663560 | tf_op jit(solution)/shard_map/ppermute | solution.py:519
  291.9 34.2 %collective-permute-start.44 = (bf16[2,128,768]{2,1,0:T(8,128)(2,1)S(1)}, bf16[2,128,768]{2,1,0:T(8,128)(2,1)S(1)}, u32[]{:S(2)}, u32[]{:S(2)}) collective-permute-start(bf16[2,128,768]{2,1,0:T(8,128)(2,1)S(1)} %pad_maximum_fusion.11), channel_id=1, source_target_pairs={{0,2},{2,0},{4,6},{6,4},{1,3},{3,1},{5,7},{7,5},{8,10},{10,8},{12,... | collective-permute-start | bytes 1179656 | tf_op jit(solution)/shard_map/ppermute | solution.py:526
  293.2 33.0 %collective-permute-start.45 = (bf16[2,128,768]{2,1,0:T(8,128)(2,1)S(1)}, bf16[2,128,768]{2,1,0:T(8,128)(2,1)}, u32[]{:S(2)}, u32[]{:S(2)}) collective-permute-start(bf16[2,128,768]{2,1,0:T(8,128)(2,1)S(1)} %pad_maximum_fusion.11), channel_id=1, source_target_pairs={{0,4},{2,6},{4,0},{6,2},{1,5},{3,7},{5,1},{7,3},{8,12},{10,14},{12... | collective-permute-start | bytes 1179656 | tf_op jit(solution)/shard_map/ppermute | solution.py:526
  294.7 31.5 %collective-permute-start.46 = (bf16[2,128,768]{2,1,0:T(8,128)(2,1)S(1)}, bf16[2,128,768]{2,1,0:T(8,128)(2,1)}, u32[]{:S(2)}, u32[]{:S(2)}) collective-permute-start(bf16[2,128,768]{2,1,0:T(8,128)(2,1)S(1)} %pad_maximum_fusion.11), channel_id=1, source_target_pairs={{0,6},{2,4},{4,2},{6,0},{1,7},{3,5},{5,3},{7,1},{8,14},{10,12},{12... | collective-permute-start | bytes 1179656 | tf_op jit(solution)/shard_map/ppermute | solution.py:526
  294.7 25.0 %collective-permute-start.47 = (bf16[144,768]{1,0:T(8,128)(2,1)S(1)}, bf16[144,768]{1,0:T(8,128)(2,1)S(1)}, u32[]{:S(2)}, u32[]{:S(2)}) collective-permute-start(bf16[144,768]{1,0:T(8,128)(2,1)S(1)} %fusion.6), channel_id=1, source_target_pairs={{0,16},{8,24},{16,0},{24,8},{1,17},{9,25},{17,1},{25,9},{2,18},{10... | collective-permute-start | bytes 663560 | tf_op jit(solution)/shard_map/ppermute | solution.py:523
  319.7 9.7 %collective-permute-start.48 = (bf16[144,768]{1,0:T(8,128)(2,1)S(1)}, bf16[144,768]{1,0:T(8,128)(2,1)S(1)}, u32[]{:S(2)}, u32[]{:S(2)}) collective-permute-start(bf16[144,768]{1,0:T(8,128)(2,1)S(1)} %add_convert_fusion.7), channel_id=1, source_target_pairs={{0,8},{8,0},{16,24},{24,16},{1,9},{9,1},{17,25},{25,17},{2,10},{10... | collective-permute-start | bytes 663560 | tf_op jit(solution)/shard_map/ppermute | solution.py:519
  326.2 10.6 %collective-permute-start.50 = (bf16[896,768]{1,0:T(8,128)(2,1)}, bf16[896,768]{1,0:T(8,128)(2,1)S(1)}, u32[]{:S(2)}, u32[]{:S(2)}) collective-permute-start(bf16[896,768]{1,0:T(8,128)(2,1)} %all-reduce.3.cloned.1.call-done.near), channel_id=1, source_target_pairs={{0,1},{1,0},{2,3},{3,2},{4,5},{5,4},{6,7},{7,6},{8,9},{9,8},{10,11... | collective-permute-start | bytes 4128776 | tf_op jit(solution)/shard_map/ppermute | solution.py:516
  (59 other events, 369.3 us)
Sparse Core Ops, SparseCore 0:
  34.2 63.2 all-gather.4
  111.2 35.5 all-gather.6
  160.2 70.9 reduce-scatter.3
  254.8 71.2 all-reduce.2

commit v18 on v17

--- a/solution.py
+++ b/solution.py
@@ -704,7 +704,7 @@
     dkv_far = over_place(dkv_far)
     dkv_o_moved = over_seq(dkv_o)
     dkv = key_backward(
-        signed, signed_t, bits, head_n, near, far, grad_tables, f32, 25
+        signed, signed_t, bits, head_n, near, after(far, dkv_o), grad_tables, f32, 25
     )
 
     dkv_o_moved = after(dkv_o_moved, dkv)

time: 356 us -> 356 us (level)
    psum x1, waiting for transfers between devices: 6.33 us -> 0.02 us  [shards(): weight_sum = lax.psum(weight_sum, 'hash')]
    ppermute x8, waiting for transfers between devices: 7.49 us -> 13.5 us  [over_place(): return lax.ppermute(x, 'hash', [(h, h ^ 1) for h in range(hash_count)])]
    unnamed x116 -> x102, local copies, waits for them, and re-layouts: 19.3 us -> 20 us
  transfers between devices with their start and end apart: 55 -> 55, of which waited for: 13 -> 12; matrix products, arithmetic and copies ran while one was open for 13% -> 13% of each run, Pallas kernels for 46% -> 46%
where the time goes in v18:
time: 356 us; the launch traced here: 352 us
  Pallas kernels  165 us (46%)
  waiting for transfers between devices  57.2 us (16%)
  starting transfers between devices  51.2 us (14%)
  local copies, waits for them, and re-layouts  35.7 us (10%)
  other arithmetic  23.8 us (7%)
  between operations  15.1 us (4%)
  matrix products  3.89 us (1%)
    pallas_call x5, Pallas kernels, single(): pl.pallas_call(kernel, in_specs=[pl.BlockSpec(memory_space=pltpu.SMEM)] +...  43.8 us
    pallas_call x3, Pallas kernels, query_backward(): call(partial(query_back_kernel, chunk=4 * blocks, blocks=blocks, last=las...  43.2 us
    pallas_call x4, Pallas kernels, key_backward(): call(partial(key_back_kernel, chunk=4), heads, micros, 'key_backward', [w...  38.1 us
    ppermute x4, waiting for transfers between devices, over_group(): return lax.ppermute(x, 'hash', moves)  28.5 us
    pallas_call x5, Pallas kernels, key_tables(): call(partial(key_kernel, chunk=2, blocks=len(blocks)), heads, 30 if len(b...  23.7 us
    unnamed x102, local copies, waits for them, and re-layouts  20 us
    ppermute x20, starting transfers between devices, over_seq(): return lax.ppermute(x, 'seq', [(0, 1), (1, 0)])  17.7 us
    ppermute x18, starting transfers between devices, over_head(): return lax.ppermute(x, 'head', [(h, h ^ j) for h in range(head_count)])  16.6 us
  transfers between devices with their start and end apart: 55, of which 12 were waited for; matrix products, arithmetic and copies ran while one was open for 13% of the time, Pallas kernels for 46%

profile of v18, /device:TPU:1, one launch (start us, length us, event | category | flops | bytes accessed | tf_op | source)
XLA Modules:
  0.0 351.6 jit_solution(1407808996556973662)
XLA Ops:
  7.3 4.5 %constant_dynamic-slice_fusion.7 = (bf16[1,128,1,768]{3,2,1,0:T(2,128)(2,1)S(1)}, bf16[1,128,1,768]{3,2,1,0:T(2,128)(2,1)}, bf16[1,128,1,768]{3,2,1,0:T(2,128)(2...) fusion(bf16[1,512,2,768]{3,2,1,0:T(2,128)(2,1)} %param.11, s32[]{:T(128)S(6)} %select_n.222, ...), kind=kLoop, calls=%fused_computation.119 | loop fusion | bytes 1966104 | tf_op jit(solution)/shard_map/jit(dynamic_index_in_dim)/dynamic_slice | solution.py:529
  12.6 3.1 collective-permute-start
  16.3 2.5 collective-permute-start.1
  20.5 2.4 copy.54
  22.9 2.0 dynamic-slice_bitcast_fusion
  24.9 1.9 constant_dynamic-slice_fusion.3
  31.2 1.7 collective-permute-start.8
  37.1 1.7 pad_maximum_fusion.9.x_in
  38.8 5.2 %key_tables.5.refs_4_ = f32[3,2048,64]{2,1,0:T(8,128)S(1)} custom-call(bf16[64,64]{1,0:T(8,128)(2,1)S(1)} %bitcast.126, bf16[576,512]{1,0:T(8,128)(2,1)} %bitcast.14.refs_0_.refs_2_.ka.va, bf16[576,512]{1,0:T(8,128)(2,1)} %collective-permute-done.2.refs_1_.refs_3_.refs_0_.refs_2_.ka.va, bf16[576,512]{1,0:T(8,128)(2,1)} %bitcast.14.refs_0_.refs_2_.ka.va, ...), custom_call_target="tpu_custom_call" | custom-call | flops 1100000000 | bytes 1048576 | tf_op jit(solution)/shard_map/key_tables/pallas_call | solution.py:192
  44.1 2.3 collective-permute-done.8.refs_0_.refs_2_.ka.va
  52.7 5.8 %key_tables.6.refs_4_ = f32[3,2048,64]{2,1,0:T(8,128)S(1)} custom-call(bf16[64,64]{1,0:T(8,128)(2,1)S(1)} %bitcast.127, bf16[576,512]{1,0:T(8,128)(2,1)} %collective-permute-done.8.refs_0_.refs_2_.ka.va, bf16[576,512]{1,0:T(8,128)(2,1)S(1)} %collective-permute-done.9.refs_1_.refs_3_.refs_0_.ka.va, ...), custom_call_target="tpu_custom_call" | custom-call | flops 32999999488 | bytes 1048576 | tf_op jit(solution)/shard_map/key_tables/pallas_call | solution.py:192
  58.5 1.7 copy-done.15
  60.2 5.7 %key_tables.7.refs_2_ = f32[3,2048,64]{2,1,0:T(8,128)S(1)} custom-call(bf16[64,64]{1,0:T(8,128)(2,1)S(1)} %bitcast.128, bf16[576,512]{1,0:T(8,128)(2,1)S(1)} %bitcast.120, bf16[576,512]{1,0:T(8,128)(2,1)S(1)} %collective-permute-done.7.refs_1_.refs_3_.kb.vb, bf16[576,512]{1,0:T(8,128)(2,1)S(1)} %bitcast.121, ...), custom_call_target="tpu_custom_call" | custom-call | flops 32999999488 | bytes 1048576 | tf_op jit(solution)/shard_map/key_tables/pallas_call | solution.py:192
  65.9 1.9 copy-done.2
  69.1 4.4 %key_tables.8.refs_2_ = f32[3,2048,64]{2,1,0:T(8,128)S(1)} custom-call(bf16[64,64]{1,0:T(8,128)(2,1)S(1)} %bitcast.129, bf16[576,512]{1,0:T(8,128)(2,1)} %collective-permute-done.6.refs_0_.refs_1_.kb.vb, bf16[576,512]{1,0:T(8,128)(2,1)} %collective-permute-done.6.refs_0_.refs_1_.kb.vb, f32[3,2048,64]{2,1,0:T(8,128)} %copy-done.2), custom_call_target="tpu_custom_call" | custom-call | flops 1100000000 | bytes 1048576 | tf_op jit(solution)/shard_map/key_tables/pallas_call | solution.py:192
  73.5 2.6 key_tables.9.tables
  76.1 3.3 query_estimates.4
  79.6 4.2 %query_estimates.5 = bf16[192,1024]{1,0:T(8,128)(2,1)S(1)} custom-call(bf16[64,64]{1,0:T(8,128)(2,1)S(1)} %bitcast.132, bf16[3,2048,64]{2,1,0:T(8,128)(2,1)S(1)} %key_tables.9.tables, bf16[576,512]{1,0:T(8,128)(2,1)} %collective-permute-done.8.refs_0_.refs_2_.ka.va, bf16[576,512]{1,0:T(8,128)(2,1)} %collective-permute-done.6.refs_0_.refs_1_.kb.vb), custom_call_target="tpu_custom_call" | custom-call | flops 1100000000 | bytes 1048576 | tf_op jit(solution)/shard_map/query_estimates/pallas_call | solution.py:205
  84.0 4.2 %query_estimates.6 = bf16[192,1024]{1,0:T(8,128)(2,1)S(1)} custom-call(bf16[64,64]{1,0:T(8,128)(2,1)S(1)} %bitcast.133, bf16[3,2048,64]{2,1,0:T(8,128)(2,1)S(1)} %key_tables.9.tables, bf16[576,512]{1,0:T(8,128)(2,1)} %collective-permute-done.2.refs_1_.refs_3_.refs_0_.refs_2_.ka.va, bf16[576,512]{1,0:T(8,128)(2,1)S(1)} %copy-done.9), custom_call_target="tpu_custom_call" | custom-call | flops 1100000000 | bytes 1048576 | tf_op jit(solution)/shard_map/query_estimates/pallas_call | solution.py:205
  89.4 4.1 %query_estimates.7 = f32[192,1024]{1,0:T(8,128)S(1)} custom-call(bf16[64,64]{1,0:T(8,128)(2,1)S(1)} %bitcast.134, bf16[3,2048,64]{2,1,0:T(8,128)(2,1)S(1)} %key_tables.9.tables, bf16[576,512]{1,0:T(8,128)(2,1)} %bitcast.14.refs_0_.refs_2_.ka.va, bf16[576,512]{1,0:T(8,128)(2,1)S(1)} %bitcast.122), custom_call_target="tpu_custom_call" | custom-call | flops 1100000000 | bytes 1048576 | tf_op jit(solution)/shard_map/query_estimates/pallas_call | solution.py:205
  93.6 5.9 %collective-permute-done.13 = bf16[192,1024]{1,0:T(8,128)(2,1)} collective-permute-done((bf16[192,1024]{1,0:T(8,128)(2,1)S(1)}, bf16[192,1024]{1,0:T(8,128)(2,1)}, u32[]{:S(2)}, u32[]{:S(2)}) %collective-permute-start.13) | collective-permute-done | bytes 393248 | tf_op jit(solution)/shard_map/ppermute | solution.py:519
  102.5 2.4 collective-permute-start.16
  106.1 1.8 collective-permute-done.16.refs_3_.refs_7_
  107.9 2.4 collective-permute-done.15.refs_2_.refs_6_
  110.9 12.7 %dense.1 = (bf16[256,768]{1,0:T(8,128)(2,1)}, f32[256,768]{1,0:T(8,128)}, f32[256,768]{1,0:T(8,128)}, f32[8,256,384]{2,1,0:T(8,128)}, bf16[8,256,384]{2,1,0:T(8,...) custom-call(s32[2]{0:T(128)} %pad_add_fusion.core, ...), custom_call_target="tpu_custom_call" | custom-call | flops 15399999488 | bytes 1048576 | tf_op jit(solution)/shard_map/dense/pallas_call | solution.py:402
  123.6 12.6 %dense_back.1 = (f32[256,768]{1,0:T(8,128)}, bf16[6,256,384]{2,1,0:T(8,128)(2,1)}, bf16[6,256,384]{2,1,0:T(8,128)(2,1)}, bf16[192,256]{1,0:T(8,128)(2,1)}, bf16[...) custom-call(s32[2]{0:T(128)} %pad_add_fusion.core, ...), custom_call_target="tpu_custom_call" | custom-call | flops 8800000000 | bytes 1048576 | tf_op jit(solution)/shard_map/dense_back/pallas_call | solution.py:402
  143.0 2.0 collective-permute-start.23
  145.0 2.7 collective-permute-start.24
  150.8 8.6 %weight_grads.1 = bf16[4,896,768]{2,1,0:T(8,128)(2,1)} custom-call(s32[2]{0:T(128)} %pad_add_fusion.core, f32[8,768]{1,0:T(8,128)} %get-tuple-element.131.small_a, f32[8,768]{1,0:T(8,128)} %get-tuple-element.132.small_b, bf16[8,256,384]{2,1,0:T(8,128)(2,1)} %get-tuple-element.133.refs_0_, bf16[8,256,384]{2,1,0:T(8,128)(2,1)} %collective-permute-done.21.refs_1_, ...), custom_call_target="tpu_custom_call" | custom-call | flops 7699999744 | bytes 1048576 | tf_op jit(solution)/shard_map/weight_grads/pallas_call | solution.py:402
  160.6 20.2 %query_backward.3 = (f32[3,2048,64]{2,1,0:T(8,128)}, f32[192,1024]{1,0:T(8,128)S(1)}, bf16[192,1024]{1,0:T(8,128)(2,1)S(1)}) custom-call(bf16[64,64]{1,0:T(8,128)(2,1)S(1)} %bitcast.136, bf16[64,128]{1,0:T(8,128)(2,1)S(1)} %pad_maximum_fusion.20.planes_t, bf16[80,2048]{1,0:T(8,128)(2,1)S(1)} %copy-done.14, bf16[3,2048,64]{2,1,0:T(8,128)(2,1)} %copy-done.4, ...), custom_call_target="tpu_custom_call" | custom-call | flops 54999998464 | bytes 1048576 | tf_op jit(solution)/shard_map/query_backward/pallas_call | solution.py:229
  181.3 11.8 %query_backward.4 = (f32[3,2048,64]{2,1,0:T(8,128)}, f32[192,1024]{1,0:T(8,128)S(1)}) custom-call(bf16[64,64]{1,0:T(8,128)(2,1)S(1)} %bitcast.137, bf16[64,128]{1,0:T(8,128)(2,1)S(1)} %pad_maximum_fusion.20.planes_t, bf16[80,2048]{1,0:T(8,128)(2,1)S(1)} %copy-done.14, bf16[3,2048,64]{2,1,0:T(8,128)(2,1)S(1)} %copy-done.5, ...), custom_call_target="tpu_custom_call" | custom-call | flops 27499999232 | bytes 1048576 | tf_op jit(solution)/shard_map/query_backward/pallas_call | solution.py:229
  197.0 11.2 %query_backward.5 = (bf16[3,2048,64]{2,1,0:T(8,128)(2,1)S(1)}, bf16[192,1024]{1,0:T(8,128)(2,1)S(1)}) custom-call(bf16[64,64]{1,0:T(8,128)(2,1)S(1)} %bitcast.138, bf16[64,128]{1,0:T(8,128)(2,1)S(1)} %pad_maximum_fusion.20.planes_t, bf16[80,2048]{1,0:T(8,128)(2,1)S(1)} %copy-done.14, bf16[3,2048,64]{2,1,0:T(8,128)(2,1)S(1)} %copy-done.5, ...), custom_call_target="tpu_custom_call" | custom-call | flops 27499999232 | bytes 1048576 | tf_op jit(solution)/shard_map/query_backward/pallas_call | solution.py:229
  209.5 8.8 %key_backward.4 = bf16[2,192,1024]{2,1,0:T(8,128)(2,1)S(1)} custom-call(bf16[64,64]{1,0:T(8,128)(2,1)S(1)} %bitcast.139, bf16[64,128]{1,0:T(8,128)(2,1)S(1)} %pad_maximum_fusion.20.planes_t, bf16[80,2048]{1,0:T(8,128)(2,1)S(1)} %copy-done.14, bf16[576,512]{1,0:T(8,128)(2,1)S(1)} %copy-done.13, ...), custom_call_target="tpu_custom_call" | custom-call | flops 27499999232 | bytes 1048576 | tf_op jit(solution)/shard_map/key_backward/pallas_call | solution.py:243
  218.9 9.8 %key_backward.5 = bf16[2,192,1024]{2,1,0:T(8,128)(2,1)S(1)} custom-call(bf16[64,64]{1,0:T(8,128)(2,1)S(1)} %bitcast.140, bf16[64,128]{1,0:T(8,128)(2,1)S(1)} %pad_maximum_fusion.20.planes_t, bf16[80,2048]{1,0:T(8,128)(2,1)S(1)} %copy-done.14, bf16[576,512]{1,0:T(8,128)(2,1)} %collective-permute-done.8.refs_0_.refs_2_.ka.va, ...), custom_call_target="tpu_custom_call" | custom-call | flops 27499999232 | bytes 1048576 | tf_op jit(solution)/shard_map/key_backward/pallas_call | solution.py:243
  233.4 9.7 %key_backward.6 = bf16[2,192,1024]{2,1,0:T(8,128)(2,1)S(1)} custom-call(bf16[64,64]{1,0:T(8,128)(2,1)S(1)} %bitcast.141, bf16[64,128]{1,0:T(8,128)(2,1)S(1)} %pad_maximum_fusion.20.planes_t, bf16[80,2048]{1,0:T(8,128)(2,1)S(1)} %copy-done.14, bf16[576,512]{1,0:T(8,128)(2,1)} %collective-permute-done.2.refs_1_.refs_3_.refs_0_.refs_2_.ka.va, ...), custom_call_target="tpu_custom_call" | custom-call | flops 27499999232 | bytes 1048576 | tf_op jit(solution)/shard_map/key_backward/pallas_call | solution.py:243
  244.9 9.9 %key_backward.7 = f32[2,192,1024]{2,1,0:T(8,128)S(1)} custom-call(bf16[64,64]{1,0:T(8,128)(2,1)S(1)} %bitcast.142, bf16[64,128]{1,0:T(8,128)(2,1)S(1)} %pad_maximum_fusion.20.planes_t, bf16[80,2048]{1,0:T(8,128)(2,1)S(1)} %copy-done.14, bf16[576,512]{1,0:T(8,128)(2,1)} %bitcast.14.refs_0_.refs_2_.ka.va, bf16[576,512]{1,0:T(8,128)(2,1)S(1)} %bitcast.124, ...), custom_call_target="tpu_custom_call" | custom-call | flops 27499999232 | bytes 1048576 | tf_op jit(solution)/shard_map/key_backward/pallas_call | solution.py:243
  254.8 1.7 add_convert_fusion
  263.4 2.4 collective-permute-done.39.refs_3_
  265.8 7.3 %collective-permute-done.38.refs_2_ = bf16[3,192,256]{2,1,0:T(8,128)(2,1)S(1)} collective-permute-done((bf16[3,192,256]{2,1,0:T(8,128)(2,1)S(1)}, bf16[3,192,256]{2,1,0:T(8,128)(2,1)S(1)}, u32[]{:S(2)}, u32[]{:S(2)}) %collective-permute-start.38) | collective-permute-done | bytes 294944 | tf_op jit(solution)/shard_map/ppermute | solution.py:526
  274.0 5.2 %input_grad.1 = bf16[256,768]{1,0:T(8,128)(2,1)} custom-call(s32[2]{0:T(128)} %pad_add_fusion.core, f32[256,768]{1,0:T(8,128)} %get-tuple-element.158.grad_first, bf16[3,192,256]{2,1,0:T(8,128)(2,1)} %pad_maximum_fusion.12.refs_0_, bf16[3,192,256]{2,1,0:T(8,128)(2,1)} %copy-done.39, bf16[3,192,256]{2,1,0:T(8,128)(2,1)} %copy-done.38, ...), custom_call_target="tpu_custom_call" | custom-call | flops 44000002048 | bytes 1048576 | tf_op jit(solution)/shard_map/input_grad/pallas_call | solution.py:402
  282.7 17.7 %collective-permute-done.41 = bf16[128,768]{1,0:T(8,128)(2,1)S(1)} collective-permute-done((bf16[128,768]{1,0:T(8,128)(2,1)S(1)}, bf16[128,768]{1,0:T(8,128)(2,1)S(1)}, u32[]{:S(2)}, u32[]{:S(2)}) %collective-permute-start.41) | collective-permute-done | bytes 196640 | tf_op jit(solution)/shard_map/ppermute | solution.py:523
  300.4 3.5 %collective-permute-done.43 = bf16[144,768]{1,0:T(8,128)(2,1)S(1)} collective-permute-done((bf16[144,768]{1,0:T(8,128)(2,1)S(1)}, bf16[144,768]{1,0:T(8,128)(2,1)S(1)}, u32[]{:S(2)}, u32[]{:S(2)}) %collective-permute-start.43) | collective-permute-done | bytes 221216 | tf_op jit(solution)/shard_map/ppermute | solution.py:519
  308.6 2.8 copy.56
  311.4 10.8 %collective-permute-done.47 = bf16[144,768]{1,0:T(8,128)(2,1)S(1)} collective-permute-done((bf16[144,768]{1,0:T(8,128)(2,1)S(1)}, bf16[144,768]{1,0:T(8,128)(2,1)S(1)}, u32[]{:S(2)}, u32[]{:S(2)}) %collective-permute-start.47) | collective-permute-done | bytes 221216 | tf_op jit(solution)/shard_map/ppermute | solution.py:523
  322.5 3.0 collective-permute-start.50
  327.1 1.7 collective-permute-done.48
  331.8 4.1 %copy.57 = f32[1,512,2,768]{3,2,1,0:T(2,128)} copy(f32[1,512,2,768]{3,1,2,0:T(8,128)S(1)} %maximum_convert_fusion) | data formatting | bytes 6291456
  340.1 4.7 %weight_results.1 = (f32[768,768]{1,0:T(8,128)}, f32[768,768]{1,0:T(8,128)}, f32[192,768]{1,0:T(8,128)}) custom-call(s32[2]{0:T(128)} %pad_add_fusion.core, bf16[896,768]{1,0:T(8,128)(2,1)} %all-reduce.3.cloned.1.call-done.near, bf16[896,768]{1,0:T(8,128)(2,1)} %copy-done.36), custom_call_target="tpu_custom_call" | custom-call | flops 3300000000 | bytes 1048576 | tf_op jit(solution)/shard_map/weight_results/pallas_call | solution.py:402
  (262 shorter events, 73.9 us)
Async XLA Ops:
  7.2 92.3 %all-gather.5.cloned.1.call-start = ((), (), s32[]{:S(2)}) async-start(), calls=%async_computation.2 | async-start | bytes 6635520 | tf_op jit(solution)/shard_map/all_gather | solution.py:564
  12.6 17.1 %collective-permute-start = (bf16[128,768]{1,0:T(8,128)(2,1)}, bf16[128,768]{1,0:T(8,128)(2,1)}, u32[]{:S(2)}, u32[]{:S(2)}) collective-permute-start(bf16[128,768]{1,0:T(8,128)(2,1)} %bitcast.116), channel_id=1, source_target_pairs={{0,16},{8,24},{16,0},{24,8},{1,17},{9,25},{17,1},{25,9},{2,18},{10... | collective-permute-start | bytes 589832 | tf_op jit(solution)/shard_map/ppermute | solution.py:523
  16.3 20.6 %collective-permute-start.1 = (bf16[8,8,64]{2,0,1:T(8,128)(2,1)}, bf16[8,8,64]{2,0,1:T(8,128)(2,1)S(1)}, u32[]{:S(2)}, u32[]{:S(2)}) collective-permute-start(bf16[8,8,64]{2,0,1:T(8,128)(2,1)} %fusion.16), channel_id=1, source_target_pairs={{0,0},{8,1},{16,8},{24,9},{1,16},{9,17},{17,24},{25,25},{2,2},{10,... | collective-permute-start | bytes 24584 | tf_op jit(solution)/shard_map/ppermute | solution.py:548
  31.2 7.6 %collective-permute-start.2 = (bf16[576,512]{1,0:T(8,128)(2,1)}, bf16[576,512]{1,0:T(8,128)(2,1)}, u32[]{:S(2)}, u32[]{:S(2)}) collective-permute-start(bf16[576,512]{1,0:T(8,128)(2,1)} %bitcast.14.refs_0_.refs_2_.ka.va), channel_id=1, source_target_pairs={{0,1},{1,0},{2,3},{3,2},{4,5},{5,4},{6,7},{7,6},{8,9},{9,8},{10,11... | collective-permute-start | bytes 1769480 | tf_op jit(solution)/shard_map/ppermute | solution.py:516
  31.2 15.2 %collective-permute-start.8 = (bf16[576,512]{1,0:T(8,128)(2,1)}, bf16[576,512]{1,0:T(8,128)(2,1)}, u32[]{:S(2)}, u32[]{:S(2)}) collective-permute-start(bf16[576,512]{1,0:T(8,128)(2,1)} %bitcast.14.refs_0_.refs_2_.ka.va), channel_id=1, source_target_pairs={{0,8},{8,0},{16,24},{24,16},{1,9},{9,1},{17,25},{25,17},{2,10},{10... | collective-permute-start | bytes 1769480 | tf_op jit(solution)/shard_map/ppermute | solution.py:519
  34.1 115.5 %all-gather.7.cloned.1.call-start = ((), (), s32[]{:S(2)}) async-start(), calls=%async_computation.3 | async-start | bytes 2211840 | tf_op jit(solution)/shard_map/all_gather | solution.py:624
  34.4 13.1 %collective-permute-start.3 = (bf16[1,128,768]{2,1,0:T(8,128)(2,1)}, bf16[1,128,768]{2,1,0:T(8,128)(2,1)S(1)}, u32[]{:S(2)}, u32[]{:S(2)}) collective-permute-start(bf16[1,128,768]{2,1,0:T(8,128)(2,1)} %bitcast.20), channel_id=1, source_target_pairs={{0,2},{2,0},{4,6},{6,4},{1,3},{3,1},{5,7},{7,5},{8,10},{10,8},{12,... | collective-permute-start | bytes 589832 | tf_op jit(solution)/shard_map/ppermute | solution.py:526
  35.7 11.9 %collective-permute-start.4 = (bf16[1,128,768]{2,1,0:T(8,128)(2,1)}, bf16[1,128,768]{2,1,0:T(8,128)(2,1)S(1)}, u32[]{:S(2)}, u32[]{:S(2)}) collective-permute-start(bf16[1,128,768]{2,1,0:T(8,128)(2,1)} %bitcast.20), channel_id=1, source_target_pairs={{0,4},{2,6},{4,0},{6,2},{1,5},{3,7},{5,1},{7,3},{8,12},{10,14},{12... | collective-permute-start | bytes 589832 | tf_op jit(solution)/shard_map/ppermute | solution.py:526
  36.9 10.6 %collective-permute-start.5 = (bf16[1,128,768]{2,1,0:T(8,128)(2,1)}, bf16[1,128,768]{2,1,0:T(8,128)(2,1)S(1)}, u32[]{:S(2)}, u32[]{:S(2)}) collective-permute-start(bf16[1,128,768]{2,1,0:T(8,128)(2,1)} %bitcast.20), channel_id=1, source_target_pairs={{0,6},{2,4},{4,2},{6,0},{1,7},{3,5},{5,3},{7,1},{8,14},{10,12},{12... | collective-permute-start | bytes 589832 | tf_op jit(solution)/shard_map/ppermute | solution.py:526
  46.4 6.3 %collective-permute-start.9 = (bf16[576,512]{1,0:T(8,128)(2,1)}, bf16[576,512]{1,0:T(8,128)(2,1)S(1)}, u32[]{:S(2)}, u32[]{:S(2)}) collective-permute-start(bf16[576,512]{1,0:T(8,128)(2,1)} %collective-permute-done.8.refs_0_.refs_2_.ka.va), channel_id=1, source_target_pairs={{0,1},{1,0},{2,3},{3,2},{4,5},{5,4},{6,7},{7,6},{8,9},{9,8},{10,11... | collective-permute-start | bytes 1769480 | tf_op jit(solution)/shard_map/ppermute | solution.py:516
  49.6 10.6 %collective-permute-start.7 = (bf16[576,512]{1,0:T(8,128)(2,1)S(1)}, bf16[576,512]{1,0:T(8,128)(2,1)S(1)}, u32[]{:S(2)}, u32[]{:S(2)}) collective-permute-start(bf16[576,512]{1,0:T(8,128)(2,1)S(1)} %bitcast.118), channel_id=1, source_target_pairs={{0,1},{1,0},{2,3},{3,2},{4,5},{5,4},{6,7},{7,6},{8,9},{9,8},{10,11... | collective-permute-start | bytes 1769480 | tf_op jit(solution)/shard_map/ppermute | solution.py:516
  50.7 17.1 %collective-permute-start.6 = (bf16[576,512]{1,0:T(8,128)(2,1)S(1)}, bf16[576,512]{1,0:T(8,128)(2,1)}, u32[]{:S(2)}, u32[]{:S(2)}) collective-permute-start(bf16[576,512]{1,0:T(8,128)(2,1)S(1)} %bitcast.119), channel_id=1, source_target_pairs={{0,8},{8,0},{16,24},{24,16},{1,9},{9,1},{17,25},{25,17},{2,10},{10... | collective-permute-start | bytes 1769480 | tf_op jit(solution)/shard_map/ppermute | solution.py:519
  88.7 10.8 %collective-permute-start.13 = (bf16[192,1024]{1,0:T(8,128)(2,1)S(1)}, bf16[192,1024]{1,0:T(8,128)(2,1)}, u32[]{:S(2)}, u32[]{:S(2)}) collective-permute-start(bf16[192,1024]{1,0:T(8,128)(2,1)S(1)} %add_convert_fusion.6), channel_id=1, source_target_pairs={{0,8},{8,0},{16,24},{24,16},{1,9},{9,1},{17,25},{25,17},{2,10},{10... | collective-permute-start | bytes 1179656 | tf_op jit(solution)/shard_map/ppermute | solution.py:519
  99.5 11.0 %collective-permute-start.17 = (bf16[4,864,768]{2,1,0:T(8,128)(2,1)}, bf16[4,864,768]{2,1,0:T(8,128)(2,1)}, u32[]{:S(2)}, u32[]{:S(2)}) collective-permute-start(bf16[4,864,768]{2,1,0:T(8,128)(2,1)} %bitcast.169), channel_id=1, source_target_pairs={{0,1},{1,0},{2,3},{3,2},{4,5},{5,4},{6,7},{7,6},{8,9},{9,8},{10,11... | collective-permute-start | bytes 15925256 | tf_op jit(solution)/shard_map/ppermute | solution.py:516
  110.3 121.7 %reduce-scatter.4.cloned.1.call-start = ((), (), s32[]{:S(2)}) async-start(), calls=%async_computation.4 | async-start | bytes 6881280
  136.2 6.8 %collective-permute-start.18 = (bf16[192,256]{1,0:T(8,128)(2,1)}, bf16[192,256]{1,0:T(8,128)(2,1)S(1)}, u32[]{:S(2)}, u32[]{:S(2)}) collective-permute-start(bf16[192,256]{1,0:T(8,128)(2,1)} %get-tuple-element.124), channel_id=1, source_target_pairs={{0,2},{2,0},{4,6},{6,4},{1,3},{3,1},{5,7},{7,5},{8,10},{10,8},{12,... | collective-permute-start | bytes 294920 | tf_op jit(solution)/shard_map/ppermute | solution.py:526
  137.7 7.3 %collective-permute-start.19 = (bf16[192,256]{1,0:T(8,128)(2,1)}, bf16[192,256]{1,0:T(8,128)(2,1)S(1)}, u32[]{:S(2)}, u32[]{:S(2)}) collective-permute-start(bf16[192,256]{1,0:T(8,128)(2,1)} %get-tuple-element.125), channel_id=1, source_target_pairs={{0,4},{2,6},{4,0},{6,2},{1,5},{3,7},{5,1},{7,3},{8,12},{10,14},{12... | collective-permute-start | bytes 294920 | tf_op jit(solution)/shard_map/ppermute | solution.py:526
  137.9 10.0 %collective-permute-start.20 = (bf16[192,256]{1,0:T(8,128)(2,1)}, bf16[192,256]{1,0:T(8,128)(2,1)S(1)}, u32[]{:S(2)}, u32[]{:S(2)}) collective-permute-start(bf16[192,256]{1,0:T(8,128)(2,1)} %get-tuple-element.126), channel_id=1, source_target_pairs={{0,6},{2,4},{4,2},{6,0},{1,7},{3,5},{5,3},{7,1},{8,14},{10,12},{12... | collective-permute-start | bytes 294920 | tf_op jit(solution)/shard_map/ppermute | solution.py:526
  139.0 11.8 %collective-permute-start.22 = (bf16[6,256,384]{2,1,0:T(8,128)(2,1)}, bf16[6,256,384]{2,1,0:T(8,128)(2,1)}, u32[]{:S(2)}, u32[]{:S(2)}) collective-permute-start(bf16[6,256,384]{2,1,0:T(8,128)(2,1)} %get-tuple-element.136), channel_id=1, source_target_pairs={{0,1},{1,0},{2,3},{3,2},{4,5},{5,4},{6,7},{7,6},{8,9},{9,8},{10,11... | collective-permute-start | bytes 3538952 | tf_op jit(solution)/shard_map/ppermute | solution.py:516
  140.5 10.3 %collective-permute-start.21 = (bf16[8,256,384]{2,1,0:T(8,128)(2,1)}, bf16[8,256,384]{2,1,0:T(8,128)(2,1)}, u32[]{:S(2)}, u32[]{:S(2)}) collective-permute-start(bf16[8,256,384]{2,1,0:T(8,128)(2,1)} %get-tuple-element.134), channel_id=1, source_target_pairs={{0,1},{1,0},{2,3},{3,2},{4,5},{5,4},{6,7},{7,6},{8,9},{9,8},{10,11... | collective-permute-start | bytes 4718600 | tf_op jit(solution)/shard_map/ppermute | solution.py:516
  143.0 6.6 %collective-permute-start.23 = (bf16[4,96,256]{2,1,0:T(8,128)(2,1)S(1)}, bf16[4,96,256]{2,1,0:T(8,128)(2,1)S(1)}, u32[]{:S(2)}, u32[]{:S(2)}) collective-permute-start(bf16[4,96,256]{2,1,0:T(8,128)(2,1)S(1)} %copy-done.40), channel_id=1, source_target_pairs={{0,1},{1,0},{2,3},{3,2},{4,5},{5,4},{6,7},{7,6},{8,9},{9,8},{10,11... | collective-permute-start | bytes 589832 | tf_op jit(solution)/shard_map/ppermute | solution.py:516
  145.0 14.6 %collective-permute-start.24 = (bf16[128,768]{1,0:T(8,128)(2,1)}, bf16[128,768]{1,0:T(8,128)(2,1)}, u32[]{:S(2)}, u32[]{:S(2)}) collective-permute-start(bf16[128,768]{1,0:T(8,128)(2,1)} %get-tuple-element.237), channel_id=1, source_target_pairs={{0,16},{8,24},{16,0},{24,8},{1,17},{9,25},{17,1},{25,9},{2,18},{10... | collective-permute-start | bytes 589832 | tf_op jit(solution)/shard_map/ppermute | solution.py:523
  148.8 10.7 %collective-permute-start.25 = (bf16[192,1024]{1,0:T(8,128)(2,1)S(1)}, bf16[192,1024]{1,0:T(8,128)(2,1)S(1)}, u32[]{:S(2)}, u32[]{:S(2)}) collective-permute-start(bf16[192,1024]{1,0:T(8,128)(2,1)S(1)} %slice_dynamic-update-slice_fusion.refs_4_), channel_id=1, source_target_pairs={{0,1},{1,0},{2,3},{3,2},{4,5},{5,4},{6,7},{7,6},{8,9},{9,8},{10,11... | collective-permute-start | bytes 1179656 | tf_op jit(solution)/shard_map/ppermute | solution.py:516
  149.6 31.2 %collective-permute-start.26 = (bf16[192,1024]{1,0:T(8,128)(2,1)S(1)}, bf16[192,1024]{1,0:T(8,128)(2,1)S(1)}, u32[]{:S(2)}, u32[]{:S(2)}) collective-permute-start(bf16[192,1024]{1,0:T(8,128)(2,1)S(1)} %slice_dynamic-update-slice_fusion.refs_4_), channel_id=1, source_target_pairs={{0,8},{8,0},{16,24},{24,16},{1,9},{9,1},{17,25},{25,17},{2,10},{10... | collective-permute-start | bytes 1179656 | tf_op jit(solution)/shard_map/ppermute | solution.py:519
  159.5 162.9 %all-reduce.3.cloned.1.call-start = ((), (), s32[]{:S(2)}) async-start(), calls=%async_computation.1 | async-start | bytes 2752512 | tf_op jit(solution)/shard_map/psum | solution.py:703
  180.8 16.0 %collective-permute-start.28 = (bf16[192,1024]{1,0:T(8,128)(2,1)S(1)}, bf16[192,1024]{1,0:T(8,128)(2,1)S(1)}, u32[]{:S(2)}, u32[]{:S(2)}) collective-permute-start(bf16[192,1024]{1,0:T(8,128)(2,1)S(1)} %collective-permute-done.26.refs_2_), channel_id=1, source_target_pairs={{0,1},{1,0},{2,3},{3,2},{4,5},{5,4},{6,7},{7,6},{8,9},{9,8},{10,11... | collective-permute-start | bytes 1179656 | tf_op jit(solution)/shard_map/ppermute | solution.py:516
  181.2 15.6 %collective-permute-start.27 = (bf16[192,1024]{1,0:T(8,128)(2,1)S(1)}, bf16[192,1024]{1,0:T(8,128)(2,1)S(1)}, u32[]{:S(2)}, u32[]{:S(2)}) collective-permute-start(bf16[192,1024]{1,0:T(8,128)(2,1)S(1)} %get-tuple-element.148), channel_id=1, source_target_pairs={{0,1},{1,0},{2,3},{3,2},{4,5},{5,4},{6,7},{7,6},{8,9},{9,8},{10,11... | collective-permute-start | bytes 1179656 | tf_op jit(solution)/shard_map/ppermute | solution.py:516
  194.1 34.5 %collective-permute-start.33 = (bf16[2,128,768]{2,1,0:T(8,128)(2,1)S(1)}, bf16[2,128,768]{2,1,0:T(8,128)(2,1)S(1)}, u32[]{:S(2)}, u32[]{:S(2)}) collective-permute-start(bf16[2,128,768]{2,1,0:T(8,128)(2,1)S(1)} %pad_maximum_fusion.10), channel_id=1, source_target_pairs={{0,4},{2,6},{4,0},{6,2},{1,5},{3,7},{5,1},{7,3},{8,12},{10,14},{12... | collective-permute-start | bytes 1179656 | tf_op jit(solution)/shard_map/ppermute | solution.py:526
  194.4 35.1 %collective-permute-start.32 = (bf16[2,128,768]{2,1,0:T(8,128)(2,1)S(1)}, bf16[2,128,768]{2,1,0:T(8,128)(2,1)S(1)}, u32[]{:S(2)}, u32[]{:S(2)}) collective-permute-start(bf16[2,128,768]{2,1,0:T(8,128)(2,1)S(1)} %pad_maximum_fusion.10), channel_id=1, source_target_pairs={{0,2},{2,0},{4,6},{6,4},{1,3},{3,1},{5,7},{7,5},{8,10},{10,8},{12,... | collective-permute-start | bytes 1179656 | tf_op jit(solution)/shard_map/ppermute | solution.py:526
  195.9 33.6 %collective-permute-start.34 = (bf16[2,128,768]{2,1,0:T(8,128)(2,1)S(1)}, bf16[2,128,768]{2,1,0:T(8,128)(2,1)S(1)}, u32[]{:S(2)}, u32[]{:S(2)}) collective-permute-start(bf16[2,128,768]{2,1,0:T(8,128)(2,1)S(1)} %pad_maximum_fusion.10), channel_id=1, source_target_pairs={{0,6},{2,4},{4,2},{6,0},{1,7},{3,5},{5,3},{7,1},{8,14},{10,12},{12... | collective-permute-start | bytes 1179656 | tf_op jit(solution)/shard_map/ppermute | solution.py:526
  208.2 10.2 %collective-permute-start.29 = (bf16[192,1024]{1,0:T(8,128)(2,1)S(1)}, bf16[192,1024]{1,0:T(8,128)(2,1)S(1)}, u32[]{:S(2)}, u32[]{:S(2)}) collective-permute-start(bf16[192,1024]{1,0:T(8,128)(2,1)S(1)} %get-tuple-element.153), channel_id=1, source_target_pairs={{0,1},{1,0},{2,3},{3,2},{4,5},{5,4},{6,7},{7,6},{8,9},{9,8},{10,11... | collective-permute-start | bytes 1179656 | tf_op jit(solution)/shard_map/ppermute | solution.py:516
  218.3 11.2 %collective-permute-start.31 = (bf16[2,192,1024]{2,1,0:T(8,128)(2,1)S(1)}, bf16[2,192,1024]{2,1,0:T(8,128)(2,1)S(1)}, u32[]{:S(2)}, u32[]{:S(2)}) collective-permute-start(bf16[2,192,1024]{2,1,0:T(8,128)(2,1)S(1)} %key_backward.4), channel_id=1, source_target_pairs={{0,1},{1,0},{2,3},{3,2},{4,5},{5,4},{6,7},{7,6},{8,9},{9,8},{10,11... | collective-permute-start | bytes 2359304 | tf_op jit(solution)/shard_map/ppermute | solution.py:516
  218.5 11.0 %collective-permute-start.30 = (bf16[192,1024]{1,0:T(8,128)(2,1)S(1)}, bf16[192,1024]{1,0:T(8,128)(2,1)S(1)}, u32[]{:S(2)}, u32[]{:S(2)}) collective-permute-start(bf16[192,1024]{1,0:T(8,128)(2,1)S(1)} %add_convert_fusion.4), channel_id=1, source_target_pairs={{0,8},{8,0},{16,24},{24,16},{1,9},{9,1},{17,25},{25,17},{2,10},{10... | collective-permute-start | bytes 1179656 | tf_op jit(solution)/shard_map/ppermute | solution.py:519
  228.7 26.1 %collective-permute-start.40 = (bf16[4,3,96,768]{3,2,1,0:T(8,128)(2,1)}, bf16[4,3,96,768]{3,2,1,0:T(8,128)(2,1)}, u32[]{:S(2)}, u32[]{:S(2)}) collective-permute-start(bf16[4,3,96,768]{3,2,1,0:T(8,128)(2,1)} %bitcast.34.refs_4_), channel_id=1, source_target_pairs={{0,1},{1,0},{2,3},{3,2},{4,5},{5,4},{6,7},{7,6},{8,9},{9,8},{10,11... | collective-permute-start | bytes 5308424 | tf_op jit(solution)/shard_map/ppermute | solution.py:516
  230.7 24.1 %collective-permute-start.36 = (bf16[2,192,1024]{2,1,0:T(8,128)(2,1)}, bf16[2,192,1024]{2,1,0:T(8,128)(2,1)}, u32[]{:S(2)}, u32[]{:S(2)}) collective-permute-start(bf16[2,192,1024]{2,1,0:T(8,128)(2,1)} %add_convert_fusion.1), channel_id=1, source_target_pairs={{0,8},{8,0},{16,24},{24,16},{1,9},{9,1},{17,25},{25,17},{2,10},{10... | collective-permute-start | bytes 2359304 | tf_op jit(solution)/shard_map/ppermute | solution.py:519
  243.1 11.8 %collective-permute-start.35 = (bf16[2,192,1024]{2,1,0:T(8,128)(2,1)S(1)}, bf16[2,192,1024]{2,1,0:T(8,128)(2,1)}, u32[]{:S(2)}, u32[]{:S(2)}) collective-permute-start(bf16[2,192,1024]{2,1,0:T(8,128)(2,1)S(1)} %key_backward.6), channel_id=1, source_target_pairs={{0,1},{1,0},{2,3},{3,2},{4,5},{5,4},{6,7},{7,6},{8,9},{9,8},{10,11... | collective-permute-start | bytes 2359304 | tf_op jit(solution)/shard_map/ppermute | solution.py:516
  256.9 8.9 %collective-permute-start.39 = (bf16[3,192,256]{2,1,0:T(8,128)(2,1)S(1)}, bf16[3,192,256]{2,1,0:T(8,128)(2,1)S(1)}, u32[]{:S(2)}, u32[]{:S(2)}) collective-permute-start(bf16[3,192,256]{2,1,0:T(8,128)(2,1)S(1)} %pad_maximum_fusion.15), channel_id=1, source_target_pairs={{0,6},{2,4},{4,2},{6,0},{1,7},{3,5},{5,3},{7,1},{8,14},{10,12},{12... | collective-permute-start | bytes 884744 | tf_op jit(solution)/shard_map/ppermute | solution.py:526
  258.5 14.7 %collective-permute-start.38 = (bf16[3,192,256]{2,1,0:T(8,128)(2,1)S(1)}, bf16[3,192,256]{2,1,0:T(8,128)(2,1)S(1)}, u32[]{:S(2)}, u32[]{:S(2)}) collective-permute-start(bf16[3,192,256]{2,1,0:T(8,128)(2,1)S(1)} %pad_maximum_fusion.14), channel_id=1, source_target_pairs={{0,4},{2,6},{4,0},{6,2},{1,5},{3,7},{5,1},{7,3},{8,12},{10,14},{12... | collective-permute-start | bytes 884744 | tf_op jit(solution)/shard_map/ppermute | solution.py:526
  259.1 14.1 %collective-permute-start.37 = (bf16[3,192,256]{2,1,0:T(8,128)(2,1)S(1)}, bf16[3,192,256]{2,1,0:T(8,128)(2,1)S(1)}, u32[]{:S(2)}, u32[]{:S(2)}) collective-permute-start(bf16[3,192,256]{2,1,0:T(8,128)(2,1)S(1)} %pad_maximum_fusion.13), channel_id=1, source_target_pairs={{0,2},{2,0},{4,6},{6,4},{1,3},{3,1},{5,7},{7,5},{8,10},{10,8},{12,... | collective-permute-start | bytes 884744 | tf_op jit(solution)/shard_map/ppermute | solution.py:526
  261.0 20.8 %collective-permute-start.42 = (bf16[288,768]{1,0:T(8,128)(2,1)S(1)}, bf16[288,768]{1,0:T(8,128)(2,1)S(1)}, u32[]{:S(2)}, u32[]{:S(2)}) collective-permute-start(bf16[288,768]{1,0:T(8,128)(2,1)S(1)} %constant_dynamic-slice_fusion.1), channel_id=1, source_target_pairs={{0,1},{1,0},{2,3},{3,2},{4,5},{5,4},{6,7},{7,6},{8,9},{9,8},{10,11... | collective-permute-start | bytes 1327112 | tf_op jit(solution)/shard_map/ppermute | solution.py:516
  280.3 20.1 %collective-permute-start.41 = (bf16[128,768]{1,0:T(8,128)(2,1)S(1)}, bf16[128,768]{1,0:T(8,128)(2,1)S(1)}, u32[]{:S(2)}, u32[]{:S(2)}) collective-permute-start(bf16[128,768]{1,0:T(8,128)(2,1)S(1)} %get-tuple-element.235), channel_id=1, source_target_pairs={{0,16},{8,24},{16,0},{24,8},{1,17},{9,25},{17,1},{25,9},{2,18},{10... | collective-permute-start | bytes 589832 | tf_op jit(solution)/shard_map/ppermute | solution.py:523
  281.9 22.0 %collective-permute-start.43 = (bf16[144,768]{1,0:T(8,128)(2,1)S(1)}, bf16[144,768]{1,0:T(8,128)(2,1)S(1)}, u32[]{:S(2)}, u32[]{:S(2)}) collective-permute-start(bf16[144,768]{1,0:T(8,128)(2,1)S(1)} %constant_dynamic-slice_fusion), channel_id=1, source_target_pairs={{0,8},{8,0},{16,24},{24,16},{1,9},{9,1},{17,25},{25,17},{2,10},{10... | collective-permute-start | bytes 663560 | tf_op jit(solution)/shard_map/ppermute | solution.py:519
  304.0 18.4 %collective-permute-start.44 = (bf16[2,128,768]{2,1,0:T(8,128)(2,1)S(1)}, bf16[2,128,768]{2,1,0:T(8,128)(2,1)}, u32[]{:S(2)}, u32[]{:S(2)}) collective-permute-start(bf16[2,128,768]{2,1,0:T(8,128)(2,1)S(1)} %pad_maximum_fusion.11), channel_id=1, source_target_pairs={{0,2},{2,0},{4,6},{6,4},{1,3},{3,1},{5,7},{7,5},{8,10},{10,8},{12,... | collective-permute-start | bytes 1179656 | tf_op jit(solution)/shard_map/ppermute | solution.py:526
  305.4 17.0 %collective-permute-start.45 = (bf16[2,128,768]{2,1,0:T(8,128)(2,1)S(1)}, bf16[2,128,768]{2,1,0:T(8,128)(2,1)}, u32[]{:S(2)}, u32[]{:S(2)}) collective-permute-start(bf16[2,128,768]{2,1,0:T(8,128)(2,1)S(1)} %pad_maximum_fusion.11), channel_id=1, source_target_pairs={{0,4},{2,6},{4,0},{6,2},{1,5},{3,7},{5,1},{7,3},{8,12},{10,14},{12... | collective-permute-start | bytes 1179656 | tf_op jit(solution)/shard_map/ppermute | solution.py:526
  305.5 16.9 %collective-permute-start.46 = (bf16[2,128,768]{2,1,0:T(8,128)(2,1)S(1)}, bf16[2,128,768]{2,1,0:T(8,128)(2,1)}, u32[]{:S(2)}, u32[]{:S(2)}) collective-permute-start(bf16[2,128,768]{2,1,0:T(8,128)(2,1)S(1)} %pad_maximum_fusion.11), channel_id=1, source_target_pairs={{0,6},{2,4},{4,2},{6,0},{1,7},{3,5},{5,3},{7,1},{8,14},{10,12},{12... | collective-permute-start | bytes 1179656 | tf_op jit(solution)/shard_map/ppermute | solution.py:526
  306.7 15.5 %collective-permute-start.47 = (bf16[144,768]{1,0:T(8,128)(2,1)S(1)}, bf16[144,768]{1,0:T(8,128)(2,1)S(1)}, u32[]{:S(2)}, u32[]{:S(2)}) collective-permute-start(bf16[144,768]{1,0:T(8,128)(2,1)S(1)} %fusion.6), channel_id=1, source_target_pairs={{0,16},{8,24},{16,0},{24,8},{1,17},{9,25},{17,1},{25,9},{2,18},{10... | collective-permute-start | bytes 663560 | tf_op jit(solution)/shard_map/ppermute | solution.py:523
  322.3 6.5 %collective-permute-start.48 = (bf16[144,768]{1,0:T(8,128)(2,1)S(1)}, bf16[144,768]{1,0:T(8,128)(2,1)}, u32[]{:S(2)}, u32[]{:S(2)}) collective-permute-start(bf16[144,768]{1,0:T(8,128)(2,1)S(1)} %add_convert_fusion.7), channel_id=1, source_target_pairs={{0,8},{8,0},{16,24},{24,16},{1,9},{9,1},{17,25},{25,17},{2,10},{10... | collective-permute-start | bytes 663560 | tf_op jit(solution)/shard_map/ppermute | solution.py:519
  322.5 15.0 %collective-permute-start.50 = (bf16[896,768]{1,0:T(8,128)(2,1)}, bf16[896,768]{1,0:T(8,128)(2,1)S(1)}, u32[]{:S(2)}, u32[]{:S(2)}) collective-permute-start(bf16[896,768]{1,0:T(8,128)(2,1)} %all-reduce.3.cloned.1.call-done.near), channel_id=1, source_target_pairs={{0,1},{1,0},{2,3},{3,2},{4,5},{5,4},{6,7},{7,6},{8,9},{9,8},{10,11... | collective-permute-start | bytes 4128776 | tf_op jit(solution)/shard_map/ppermute | solution.py:516
  (52 other events, 320.7 us)
Sparse Core Ops, SparseCore 0:
  34.2 62.7 all-gather.4
  110.4 35.9 all-gather.6
  159.6 70.9 reduce-scatter.3
  243.6 70.6 all-reduce.2

commit v19 on v18

--- a/solution.py
+++ b/solution.py
@@ -286,7 +286,8 @@
 
 def dense_kernel(core, x_in, grad_out, gain, bias, *refs):
     attn, weights = refs[0:4], refs[4:6]
-    layer_out, first_out, grad_second_out, slope, keep, give, heads_give, small = refs[6:14]
+    layer_out, grad_first_out, keep, give, keep_back, give_back, heads_give = refs[6:13]
+    estimates, small, slope = refs[13:17], refs[17], refs[18]
     owner = [core[1] ^ (b // 2) for b in range(8)]
     for j in range(4):
         heads_give[j] = core_rows(core, attn[j], 1)
@@ -297,11 +298,10 @@
     attn_out = dot(heads, out_w, TN)
     resid = x_in[...].astype(f32)
     first = resid + attn_out
-    first_out[...] = first
     small[0:1, :] = column_sum(resid * resid)
     small[1:2, :] = column_sum(attn_out * attn_out)
     small[2:3, :] = column_sum(first * first)
-    unit_1, _ = norm(first)
+    unit_1, inv_1 = norm(first)
     normed = (unit_1 * gain[0:1, :] + bias[0:1, :]).astype(bf16)
     share_rows(keep, give, 4, normed)
     second = normed.astype(f32)
@@ -317,34 +317,22 @@
     grad = grad_out[...]
     small[3:4, :] = column_sum(grad * unit_2)
     small[4:5, :] = column_sum(grad)
-    small[5:8, :] = jnp.zeros_like(small[5:8, :])
     grad_second = norm_back(grad * gain[1:2, :], unit_2, inv_2)
-    grad_second_out[...] = grad_second
-    share_rows(keep, give, 6, grad_second.astype(bf16))
-
-
-def dense_back_kernel(core, first, grad_second, slope, gain, *refs):
-    weights = refs[0:2]
-    grad_first_out, keep, give = refs[2:5]
-    estimates, small = refs[5:9], refs[9]
-    owner = [core[1] ^ (b // 2) for b in range(8)]
-    part = slope.shape[2]
-    blocks = range(8)
-    grad_normed = grad_second[...]
-    grad_ffn = grad_normed.astype(bf16)
+    grad_ffn = grad_second.astype(bf16)
+    share_rows(keep, give, 6, grad_ffn)
+    grad_normed = grad_second
     for b in blocks:
         rows = dot(grad_ffn, weights[b % 2][owner[b], part : 2 * part, :], NT)
         rows = (rows * slope[b]).astype(bf16)
-        (keep, give)[b % 2][b // 2] = rows
+        (keep_back, give_back)[b % 2][b // 2] = rows
         grad_normed = grad_normed + dot(rows, weights[b % 2][owner[b], 0:part, :], NN)
-    unit, inv = norm(first[...])
-    small[0:1, :] = column_sum(grad_normed * unit)
-    small[1:2, :] = column_sum(grad_normed)
-    small[2:8, :] = jnp.zeros_like(small[2:8, :])
-    grad_first = norm_back(grad_normed * gain[0:1, :], unit, inv)
+    small[5:6, :] = column_sum(grad_normed * unit_1)
+    small[6:7, :] = column_sum(grad_normed)
+    small[7:16, :] = jnp.zeros_like(small[7:16, :])
+    grad_first = norm_back(grad_normed * gain[0:1, :], unit_1, inv_1)
     grad_first_out[...] = grad_first
     grad_attn = grad_first.astype(bf16)
-    share_rows(keep, give, 4, grad_attn)
+    share_rows(keep_back, give_back, 4, grad_attn)
     for b in blocks:
         half = estimates[0].shape[0] // 2
         at = core[0] if b % 2 == 0 else 1 - core[0]
@@ -353,11 +341,11 @@
         ).astype(bf16)
 
 
-def weight_grad_kernel(core, small_a, small_b, *refs):
+def weight_grad_kernel(core, small, *refs):
     near, far, near_back, far_back = refs[0:4]
     attn, attn_far, out = refs[4:8], refs[8], refs[9]
     part = near.shape[2]
-    sums = jnp.concatenate([small_a[...], small_b[...]], axis=0).astype(bf16)
+    sums = small[...].astype(bf16)
 
     def wide(ref, at):
         return jnp.concatenate([ref[at], ref[at + 1]], axis=1)
@@ -419,35 +407,21 @@
     out_shape = [
         shape((rows, width), bf16),
         shape((rows, width), f32),
-        shape((rows, width), f32),
-        shape((8, rows, part), f32),
-        shape((8, rows, part), bf16),
-        shape((8, rows, part), bf16),
+        *[shape((8, rows, part), bf16)] * 2,
+        *[shape((6, rows, part), bf16)] * 2,
         shape((4, attn[0].shape[0] // 2, rows), bf16),
-        shape((8, width), f32),
+        *[shape(attn[0].shape, bf16)] * 4,
+        shape((16, width), f32),
     ]
     args = [x_in, grad_out, gain, bias, *attn, *weights]
-    return single(dense_kernel, core, args, out_shape, 14, "dense")
-
-
-def dense_back(core, first, grad_second, slope, gain, attn, weights):
-    rows, width = first.shape
-    part = (weights[0].shape[1] - attn[0].shape[0] // 2) // 2
-    out_shape = [
-        shape((rows, width), f32),
-        shape((6, rows, part), bf16),
-        shape((6, rows, part), bf16),
-        *[shape(attn[0].shape, bf16)] * 4,
-        shape((8, width), f32),
-    ]
-    args = [first, grad_second, slope, gain, *weights]
-    return single(dense_back_kernel, core, args, out_shape, 8, "dense_back")
-
-
-def weight_grads(core, small_a, small_b, shared, attn, attn_far):
-    part, width = shared[0].shape[2], small_a.shape[1]
+    scratch = [pltpu.VMEM((8, rows, part), f32)]
+    return single(dense_kernel, core, args, out_shape, 22, "dense", scratch)
+
+
+def weight_grads(core, small, shared, attn, attn_far):
+    part, width = shared[0].shape[2], small.shape[1]
     out_shape = [shape((4, 2 * part + attn[0].shape[0] // 2 + 32, width), bf16)]
-    args = [small_a, small_b, *shared, *attn, attn_far]
+    args = [small, *shared, *attn, attn_far]
     return single(weight_grad_kernel, core, args, out_shape, 7, "weight_grads")[0]
 
 
@@ -640,14 +614,10 @@
         return [dense_rows[0]] + [over_group(dense_rows[k], groups - k) for k in range(1, groups)]
 
     core = jnp.stack([s, d]).astype(jnp.int32)
-    layer_rows, first, grad_second, slope, keep, give, heads_give, small_a = dense(
+    layer_rows, grad_first, keep, give, keep_back, give_back, heads_give, *est_parts, small = dense(
         core, dense_in, grad_out, norm_gain, norm_bias, attn_parts, weights
     )
-    taken, heads_far = over_seq(give), over_seq(heads_give)
-    grad_first, keep_back, give_back, *est_parts, small_b = dense_back(
-        core, first, grad_second, slope, norm_gain, attn_parts, weights
-    )
-    taken_back = over_seq(give_back)
+    taken, taken_back, heads_far = over_seq(give), over_seq(give_back), over_seq(heads_give)
     est_moved = [over_head(est_parts[j], j) for j in range(1, head_count)]
     est_parts = [est_parts[0], *lax.optimization_barrier(est_moved)]
     grad = jnp.concatenate(
@@ -655,7 +625,7 @@
     )
     layer_moved = away(layer_rows)
     weight_parts = weight_grads(
-        core, after(small_a, grad, w_qkv_t), small_b, [keep, taken, keep_back, taken_back], attn_parts, heads_far
+        core, after(small, grad, w_qkv_t), [keep, taken, keep_back, taken_back], attn_parts, heads_far
     )
 
     weight_sum = lax.psum_scatter(weight_parts, "head", scatter_dimension=0, tiled=True)[0]
@@ -772,8 +742,8 @@
         grad_w_out,
         grad_w_up,
         grad_w_down,
-        jnp.stack([norm_grads[8], norm_grads[3]]),
-        jnp.stack([norm_grads[9], norm_grads[4]]),
+        jnp.stack([norm_grads[5], norm_grads[3]]),
+        jnp.stack([norm_grads[6], norm_grads[4]]),
         stream_rms,
     )
 

time: 356 us -> 355 us (level)
  Pallas kernels: 165 us -> 157 us
  waiting for transfers between devices: 57.2 us -> 63.3 us
    pallas_call x5 -> x4, Pallas kernels: 43.8 us -> 36.4 us  [single(): pl.pallas_call(kernel, in_specs=[pl.BlockSpec(memory_space=pltpu.SMEM)] +...]
    all_gather x1, waiting for transfers between devices: 0.01 us -> 4.17 us  [shards(): w_qkv_t = lax.all_gather(after(w_qkv_t, weights[0]), 'head', axis=0)]
    unnamed x102 -> x98, local copies, waits for them, and re-layouts: 20 us -> 19.5 us
  transfers between devices with their start and end apart: 55 -> 55, of which waited for: 12 -> 12; matrix products, arithmetic and copies ran while one was open for 13% -> 14% of each run, Pallas kernels for 46% -> 44%
where the time goes in v19:
time: 355 us; the launch traced here: 350 us
  Pallas kernels  157 us (44%)
  waiting for transfers between devices  63.3 us (18%)
  starting transfers between devices  50.8 us (14%)
  local copies, waits for them, and re-layouts  36.2 us (10%)
  other arithmetic  23.7 us (7%)
  between operations  15.1 us (4%)
  matrix products  3.91 us (1%)
    pallas_call x3, Pallas kernels, query_backward(): call(partial(query_back_kernel, chunk=4 * blocks, blocks=blocks, last=las...  43.2 us
    pallas_call x4, Pallas kernels, key_backward(): call(partial(key_back_kernel, chunk=4), heads, micros, 'key_backward', [w...  38.2 us
    pallas_call x4, Pallas kernels, single(): pl.pallas_call(kernel, in_specs=[pl.BlockSpec(memory_space=pltpu.SMEM)] +...  36.4 us
    ppermute x4, waiting for transfers between devices, over_group(): return lax.ppermute(x, 'hash', moves)  28.3 us
    pallas_call x5, Pallas kernels, key_tables(): call(partial(key_kernel, chunk=2, blocks=len(blocks)), heads, 30 if len(b...  23.7 us
    unnamed x98, local copies, waits for them, and re-layouts  19.5 us
    ppermute x20, starting transfers between devices, over_seq(): return lax.ppermute(x, 'seq', [(0, 1), (1, 0)])  17.2 us
    ppermute x18, starting transfers between devices, over_head(): return lax.ppermute(x, 'head', [(h, h ^ j) for h in range(head_count)])  16.6 us
  transfers between devices with their start and end apart: 55, of which 12 were waited for; matrix products, arithmetic and copies ran while one was open for 14% of the time, Pallas kernels for 44%

profile of v19, /device:TPU:1, one launch (start us, length us, event | category | flops | bytes accessed | tf_op | source)
XLA Modules:
  0.0 350.3 jit_solution(13437171587620725292)
XLA Ops:
  7.3 4.5 %constant_dynamic-slice_fusion.7 = (bf16[1,128,1,768]{3,2,1,0:T(2,128)(2,1)S(1)}, bf16[1,128,1,768]{3,2,1,0:T(2,128)(2,1)}, bf16[1,128,1,768]{3,2,1,0:T(2,128)(2...) fusion(bf16[1,512,2,768]{3,2,1,0:T(2,128)(2,1)} %param.11, s32[]{:T(128)S(6)} %select_n.222, ...), kind=kLoop, calls=%fused_computation.119 | loop fusion | bytes 1966104 | tf_op jit(solution)/shard_map/jit(dynamic_index_in_dim)/dynamic_slice | solution.py:503
  12.6 3.1 collective-permute-start
  16.3 2.5 collective-permute-start.1
  20.5 2.4 copy.54
  22.9 2.0 dynamic-slice_bitcast_fusion
  24.9 1.9 constant_dynamic-slice_fusion.3
  37.1 1.7 pad_maximum_fusion.9.x_in
  38.8 5.2 %key_tables.5.refs_4_ = f32[3,2048,64]{2,1,0:T(8,128)S(1)} custom-call(bf16[64,64]{1,0:T(8,128)(2,1)S(1)} %bitcast.126, bf16[576,512]{1,0:T(8,128)(2,1)} %bitcast.14.refs_0_.refs_2_.ka.va, bf16[576,512]{1,0:T(8,128)(2,1)} %collective-permute-done.2.refs_1_.refs_3_.refs_0_.refs_2_.ka.va, bf16[576,512]{1,0:T(8,128)(2,1)} %bitcast.14.refs_0_.refs_2_.ka.va, ...), custom_call_target="tpu_custom_call" | custom-call | flops 1100000000 | bytes 1048576 | tf_op jit(solution)/shard_map/key_tables/pallas_call | solution.py:192
  44.1 2.4 collective-permute-done.8.refs_0_.refs_2_.ka.va
  52.7 5.8 %key_tables.6.refs_4_ = f32[3,2048,64]{2,1,0:T(8,128)S(1)} custom-call(bf16[64,64]{1,0:T(8,128)(2,1)S(1)} %bitcast.127, bf16[576,512]{1,0:T(8,128)(2,1)} %collective-permute-done.8.refs_0_.refs_2_.ka.va, bf16[576,512]{1,0:T(8,128)(2,1)S(1)} %collective-permute-done.9.refs_1_.refs_3_.refs_0_.ka.va, ...), custom_call_target="tpu_custom_call" | custom-call | flops 32999999488 | bytes 1048576 | tf_op jit(solution)/shard_map/key_tables/pallas_call | solution.py:192
  60.2 5.7 %key_tables.7.refs_2_ = f32[3,2048,64]{2,1,0:T(8,128)S(1)} custom-call(bf16[64,64]{1,0:T(8,128)(2,1)S(1)} %bitcast.128, bf16[576,512]{1,0:T(8,128)(2,1)S(1)} %bitcast.120, bf16[576,512]{1,0:T(8,128)(2,1)S(1)} %collective-permute-done.7.refs_1_.refs_3_.kb.vb, bf16[576,512]{1,0:T(8,128)(2,1)S(1)} %bitcast.121, ...), custom_call_target="tpu_custom_call" | custom-call | flops 32999999488 | bytes 1048576 | tf_op jit(solution)/shard_map/key_tables/pallas_call | solution.py:192
  65.9 1.9 copy-done.2
  69.1 4.4 %key_tables.8.refs_2_ = f32[3,2048,64]{2,1,0:T(8,128)S(1)} custom-call(bf16[64,64]{1,0:T(8,128)(2,1)S(1)} %bitcast.129, bf16[576,512]{1,0:T(8,128)(2,1)} %collective-permute-done.6.refs_0_.refs_1_.kb.vb, bf16[576,512]{1,0:T(8,128)(2,1)} %collective-permute-done.6.refs_0_.refs_1_.kb.vb, f32[3,2048,64]{2,1,0:T(8,128)} %copy-done.2), custom_call_target="tpu_custom_call" | custom-call | flops 1100000000 | bytes 1048576 | tf_op jit(solution)/shard_map/key_tables/pallas_call | solution.py:192
  73.5 2.6 key_tables.9.tables
  76.1 3.3 query_estimates.4
  79.6 4.2 %query_estimates.5 = bf16[192,1024]{1,0:T(8,128)(2,1)S(1)} custom-call(bf16[64,64]{1,0:T(8,128)(2,1)S(1)} %bitcast.132, bf16[3,2048,64]{2,1,0:T(8,128)(2,1)S(1)} %key_tables.9.tables, bf16[576,512]{1,0:T(8,128)(2,1)} %collective-permute-done.8.refs_0_.refs_2_.ka.va, bf16[576,512]{1,0:T(8,128)(2,1)} %collective-permute-done.6.refs_0_.refs_1_.kb.vb), custom_call_target="tpu_custom_call" | custom-call | flops 1100000000 | bytes 1048576 | tf_op jit(solution)/shard_map/query_estimates/pallas_call | solution.py:205
  84.0 4.2 %query_estimates.6 = bf16[192,1024]{1,0:T(8,128)(2,1)S(1)} custom-call(bf16[64,64]{1,0:T(8,128)(2,1)S(1)} %bitcast.133, bf16[3,2048,64]{2,1,0:T(8,128)(2,1)S(1)} %key_tables.9.tables, bf16[576,512]{1,0:T(8,128)(2,1)} %collective-permute-done.2.refs_1_.refs_3_.refs_0_.refs_2_.ka.va, bf16[576,512]{1,0:T(8,128)(2,1)S(1)} %copy-done.9), custom_call_target="tpu_custom_call" | custom-call | flops 1100000000 | bytes 1048576 | tf_op jit(solution)/shard_map/query_estimates/pallas_call | solution.py:205
  89.4 4.1 %query_estimates.7 = f32[192,1024]{1,0:T(8,128)S(1)} custom-call(bf16[64,64]{1,0:T(8,128)(2,1)S(1)} %bitcast.134, bf16[3,2048,64]{2,1,0:T(8,128)(2,1)S(1)} %key_tables.9.tables, bf16[576,512]{1,0:T(8,128)(2,1)} %bitcast.14.refs_0_.refs_2_.ka.va, bf16[576,512]{1,0:T(8,128)(2,1)S(1)} %bitcast.122), custom_call_target="tpu_custom_call" | custom-call | flops 1100000000 | bytes 1048576 | tf_op jit(solution)/shard_map/query_estimates/pallas_call | solution.py:205
  93.6 5.9 %collective-permute-done.13 = bf16[192,1024]{1,0:T(8,128)(2,1)} collective-permute-done((bf16[192,1024]{1,0:T(8,128)(2,1)S(1)}, bf16[192,1024]{1,0:T(8,128)(2,1)}, u32[]{:S(2)}, u32[]{:S(2)}) %collective-permute-start.13) | collective-permute-done | bytes 393248 | tf_op jit(solution)/shard_map/ppermute | solution.py:493
  102.4 2.4 collective-permute-start.16
  106.0 1.8 collective-permute-done.16.refs_3_.refs_7_
  107.8 2.4 collective-permute-done.15.refs_2_.refs_6_
  110.8 18.3 %dense.1 = (bf16[256,768]{1,0:T(8,128)(2,1)}, f32[256,768]{1,0:T(8,128)}, bf16[8,256,384]{2,1,0:T(8,128)(2,1)}, bf16[8,256,384]{2,1,0:T(8,128)(2,1)}, bf16[6,256...) custom-call(s32[2]{0:T(128)} %pad_add_fusion.core, ...), custom_call_target="tpu_custom_call" | custom-call | flops 24199999488 | bytes 1048576 | tf_op jit(solution)/shard_map/dense/pallas_call | solution.py:390
  138.4 1.9 collective-permute-start.24
  141.3 2.0 collective-permute-start.25
  143.3 4.2 %all-gather.7.cloned.1.call-done = bf16[12,96,768]{2,1,0:T(8,128)(2,1)} async-done(((bf16[3,96,768]{2,1,0:T(8,128)(2,1)}), bf16[12,96,768]{2,1,0:T(8,128)(2,1)}) %all-gather.7.cloned.1.call-update) | async-done | bytes 1769488 | tf_op jit(solution)/shard_map/all_gather | solution.py:598
  148.6 8.2 %weight_grads.1 = bf16[4,896,768]{2,1,0:T(8,128)(2,1)} custom-call(s32[2]{0:T(128)} %pad_add_fusion.core, f32[16,768]{1,0:T(8,128)} %get-tuple-element.124.small, bf16[8,256,384]{2,1,0:T(8,128)(2,1)} %get-tuple-element.125.refs_0_, bf16[8,256,384]{2,1,0:T(8,128)(2,1)} %collective-permute-done.21.refs_1_, bf16[6,256,384]{2,1,0:T(8,128)(2,1)} %get-tuple-element.127.refs_2_, ...), custom_call_target="tpu_custom_call" | custom-call | flops 7699999744 | bytes 1048576 | tf_op jit(solution)/shard_map/weight_grads/pallas_call | solution.py:390
  157.9 20.2 %query_backward.3 = (f32[3,2048,64]{2,1,0:T(8,128)}, f32[192,1024]{1,0:T(8,128)S(1)}, bf16[192,1024]{1,0:T(8,128)(2,1)S(1)}) custom-call(bf16[64,64]{1,0:T(8,128)(2,1)S(1)} %bitcast.136, bf16[64,128]{1,0:T(8,128)(2,1)S(1)} %pad_maximum_fusion.20.planes_t, bf16[80,2048]{1,0:T(8,128)(2,1)S(1)} %copy-done.14, bf16[3,2048,64]{2,1,0:T(8,128)(2,1)} %copy-done.4, ...), custom_call_target="tpu_custom_call" | custom-call | flops 54999998464 | bytes 1048576 | tf_op jit(solution)/shard_map/query_backward/pallas_call | solution.py:229
  179.0 11.8 %query_backward.4 = (f32[3,2048,64]{2,1,0:T(8,128)}, f32[192,1024]{1,0:T(8,128)S(1)}) custom-call(bf16[64,64]{1,0:T(8,128)(2,1)S(1)} %bitcast.137, bf16[64,128]{1,0:T(8,128)(2,1)S(1)} %pad_maximum_fusion.20.planes_t, bf16[80,2048]{1,0:T(8,128)(2,1)S(1)} %copy-done.14, bf16[3,2048,64]{2,1,0:T(8,128)(2,1)S(1)} %copy-done.5, ...), custom_call_target="tpu_custom_call" | custom-call | flops 27499999232 | bytes 1048576 | tf_op jit(solution)/shard_map/query_backward/pallas_call | solution.py:229
  194.6 11.2 %query_backward.5 = (bf16[3,2048,64]{2,1,0:T(8,128)(2,1)S(1)}, bf16[192,1024]{1,0:T(8,128)(2,1)S(1)}) custom-call(bf16[64,64]{1,0:T(8,128)(2,1)S(1)} %bitcast.138, bf16[64,128]{1,0:T(8,128)(2,1)S(1)} %pad_maximum_fusion.20.planes_t, bf16[80,2048]{1,0:T(8,128)(2,1)S(1)} %copy-done.14, bf16[3,2048,64]{2,1,0:T(8,128)(2,1)S(1)} %copy-done.5, ...), custom_call_target="tpu_custom_call" | custom-call | flops 27499999232 | bytes 1048576 | tf_op jit(solution)/shard_map/query_backward/pallas_call | solution.py:229
  207.2 8.8 %key_backward.4 = bf16[2,192,1024]{2,1,0:T(8,128)(2,1)S(1)} custom-call(bf16[64,64]{1,0:T(8,128)(2,1)S(1)} %bitcast.139, bf16[64,128]{1,0:T(8,128)(2,1)S(1)} %pad_maximum_fusion.20.planes_t, bf16[80,2048]{1,0:T(8,128)(2,1)S(1)} %copy-done.14, bf16[576,512]{1,0:T(8,128)(2,1)S(1)} %copy-done.13, ...), custom_call_target="tpu_custom_call" | custom-call | flops 27499999232 | bytes 1048576 | tf_op jit(solution)/shard_map/key_backward/pallas_call | solution.py:243
  216.6 9.8 %key_backward.5 = bf16[2,192,1024]{2,1,0:T(8,128)(2,1)S(1)} custom-call(bf16[64,64]{1,0:T(8,128)(2,1)S(1)} %bitcast.140, bf16[64,128]{1,0:T(8,128)(2,1)S(1)} %pad_maximum_fusion.20.planes_t, bf16[80,2048]{1,0:T(8,128)(2,1)S(1)} %copy-done.14, bf16[576,512]{1,0:T(8,128)(2,1)} %collective-permute-done.8.refs_0_.refs_2_.ka.va, ...), custom_call_target="tpu_custom_call" | custom-call | flops 27499999232 | bytes 1048576 | tf_op jit(solution)/shard_map/key_backward/pallas_call | solution.py:243
  231.1 9.7 %key_backward.6 = bf16[2,192,1024]{2,1,0:T(8,128)(2,1)S(1)} custom-call(bf16[64,64]{1,0:T(8,128)(2,1)S(1)} %bitcast.141, bf16[64,128]{1,0:T(8,128)(2,1)S(1)} %pad_maximum_fusion.20.planes_t, bf16[80,2048]{1,0:T(8,128)(2,1)S(1)} %copy-done.14, bf16[576,512]{1,0:T(8,128)(2,1)} %collective-permute-done.2.refs_1_.refs_3_.refs_0_.refs_2_.ka.va, ...), custom_call_target="tpu_custom_call" | custom-call | flops 27499999232 | bytes 1048576 | tf_op jit(solution)/shard_map/key_backward/pallas_call | solution.py:243
  242.6 9.9 %key_backward.7 = f32[2,192,1024]{2,1,0:T(8,128)S(1)} custom-call(bf16[64,64]{1,0:T(8,128)(2,1)S(1)} %bitcast.142, bf16[64,128]{1,0:T(8,128)(2,1)S(1)} %pad_maximum_fusion.20.planes_t, bf16[80,2048]{1,0:T(8,128)(2,1)S(1)} %copy-done.14, bf16[576,512]{1,0:T(8,128)(2,1)} %bitcast.14.refs_0_.refs_2_.ka.va, bf16[576,512]{1,0:T(8,128)(2,1)S(1)} %bitcast.124, ...), custom_call_target="tpu_custom_call" | custom-call | flops 27499999232 | bytes 1048576 | tf_op jit(solution)/shard_map/key_backward/pallas_call | solution.py:243
  252.6 1.7 add_convert_fusion
  260.6 3.6 %collective-permute-done.39.refs_3_ = bf16[3,192,256]{2,1,0:T(8,128)(2,1)S(1)} collective-permute-done((bf16[3,192,256]{2,1,0:T(8,128)(2,1)S(1)}, bf16[3,192,256]{2,1,0:T(8,128)(2,1)S(1)}, u32[]{:S(2)}, u32[]{:S(2)}) %collective-permute-start.39) | collective-permute-done | bytes 294944 | tf_op jit(solution)/shard_map/ppermute | solution.py:500
  264.2 6.7 %collective-permute-done.38.refs_2_ = bf16[3,192,256]{2,1,0:T(8,128)(2,1)S(1)} collective-permute-done((bf16[3,192,256]{2,1,0:T(8,128)(2,1)S(1)}, bf16[3,192,256]{2,1,0:T(8,128)(2,1)S(1)}, u32[]{:S(2)}, u32[]{:S(2)}) %collective-permute-start.38) | collective-permute-done | bytes 294944 | tf_op jit(solution)/shard_map/ppermute | solution.py:500
  271.7 5.2 %input_grad.1 = bf16[256,768]{1,0:T(8,128)(2,1)} custom-call(s32[2]{0:T(128)} %pad_add_fusion.core, f32[256,768]{1,0:T(8,128)} %get-tuple-element.150.grad_first, bf16[3,192,256]{2,1,0:T(8,128)(2,1)} %pad_maximum_fusion.12.refs_0_, bf16[3,192,256]{2,1,0:T(8,128)(2,1)} %copy-done.38, bf16[3,192,256]{2,1,0:T(8,128)(2,1)} %copy-done.37, ...), custom_call_target="tpu_custom_call" | custom-call | flops 44000002048 | bytes 1048576 | tf_op jit(solution)/shard_map/input_grad/pallas_call | solution.py:390
  278.0 2.0 collective-permute-start.41
  281.1 17.4 %collective-permute-done.41 = bf16[128,768]{1,0:T(8,128)(2,1)S(1)} collective-permute-done((bf16[128,768]{1,0:T(8,128)(2,1)S(1)}, bf16[128,768]{1,0:T(8,128)(2,1)S(1)}, u32[]{:S(2)}, u32[]{:S(2)}) %collective-permute-start.41) | collective-permute-done | bytes 196640 | tf_op jit(solution)/shard_map/ppermute | solution.py:497
  298.5 4.0 %collective-permute-done.43 = bf16[144,768]{1,0:T(8,128)(2,1)S(1)} collective-permute-done((bf16[144,768]{1,0:T(8,128)(2,1)S(1)}, bf16[144,768]{1,0:T(8,128)(2,1)S(1)}, u32[]{:S(2)}, u32[]{:S(2)}) %collective-permute-start.43) | collective-permute-done | bytes 221216 | tf_op jit(solution)/shard_map/ppermute | solution.py:493
  303.4 1.8 collective-permute-start.46
  307.2 2.8 copy.56
  310.0 11.0 %collective-permute-done.47 = bf16[144,768]{1,0:T(8,128)(2,1)S(1)} collective-permute-done((bf16[144,768]{1,0:T(8,128)(2,1)S(1)}, bf16[144,768]{1,0:T(8,128)(2,1)S(1)}, u32[]{:S(2)}, u32[]{:S(2)}) %collective-permute-start.47) | collective-permute-done | bytes 221216 | tf_op jit(solution)/shard_map/ppermute | solution.py:497
  321.2 2.2 collective-permute-start.50
  325.0 2.6 collective-permute-done.48
  330.5 4.1 %copy.57 = f32[1,512,2,768]{3,2,1,0:T(2,128)} copy(f32[1,512,2,768]{3,1,2,0:T(8,128)S(1)} %maximum_convert_fusion) | data formatting | bytes 6291456
  338.8 4.7 %weight_results.1 = (f32[768,768]{1,0:T(8,128)}, f32[768,768]{1,0:T(8,128)}, f32[192,768]{1,0:T(8,128)}) custom-call(s32[2]{0:T(128)} %pad_add_fusion.core, bf16[896,768]{1,0:T(8,128)(2,1)} %all-reduce.3.cloned.1.call-done.near, bf16[896,768]{1,0:T(8,128)(2,1)} %copy-done.35), custom_call_target="tpu_custom_call" | custom-call | flops 3300000000 | bytes 1048576 | tf_op jit(solution)/shard_map/weight_results/pallas_call | solution.py:390
  (257 shorter events, 75.2 us)
Async XLA Ops:
  7.2 92.3 %all-gather.5.cloned.1.call-start = ((), (), s32[]{:S(2)}) async-start(), calls=%async_computation.2 | async-start | bytes 6635520 | tf_op jit(solution)/shard_map/all_gather | solution.py:538
  12.6 17.1 %collective-permute-start = (bf16[128,768]{1,0:T(8,128)(2,1)}, bf16[128,768]{1,0:T(8,128)(2,1)}, u32[]{:S(2)}, u32[]{:S(2)}) collective-permute-start(bf16[128,768]{1,0:T(8,128)(2,1)} %bitcast.116), channel_id=1, source_target_pairs={{0,16},{8,24},{16,0},{24,8},{1,17},{9,25},{17,1},{25,9},{2,18},{10... | collective-permute-start | bytes 589832 | tf_op jit(solution)/shard_map/ppermute | solution.py:497
  16.3 20.6 %collective-permute-start.1 = (bf16[8,8,64]{2,0,1:T(8,128)(2,1)}, bf16[8,8,64]{2,0,1:T(8,128)(2,1)S(1)}, u32[]{:S(2)}, u32[]{:S(2)}) collective-permute-start(bf16[8,8,64]{2,0,1:T(8,128)(2,1)} %fusion.16), channel_id=1, source_target_pairs={{0,0},{8,1},{16,8},{24,9},{1,16},{9,17},{17,24},{25,25},{2,2},{10,... | collective-permute-start | bytes 24584 | tf_op jit(solution)/shard_map/ppermute | solution.py:522
  31.2 7.6 %collective-permute-start.2 = (bf16[576,512]{1,0:T(8,128)(2,1)}, bf16[576,512]{1,0:T(8,128)(2,1)}, u32[]{:S(2)}, u32[]{:S(2)}) collective-permute-start(bf16[576,512]{1,0:T(8,128)(2,1)} %bitcast.14.refs_0_.refs_2_.ka.va), channel_id=1, source_target_pairs={{0,1},{1,0},{2,3},{3,2},{4,5},{5,4},{6,7},{7,6},{8,9},{9,8},{10,11... | collective-permute-start | bytes 1769480 | tf_op jit(solution)/shard_map/ppermute | solution.py:490
  31.2 15.2 %collective-permute-start.8 = (bf16[576,512]{1,0:T(8,128)(2,1)}, bf16[576,512]{1,0:T(8,128)(2,1)}, u32[]{:S(2)}, u32[]{:S(2)}) collective-permute-start(bf16[576,512]{1,0:T(8,128)(2,1)} %bitcast.14.refs_0_.refs_2_.ka.va), channel_id=1, source_target_pairs={{0,8},{8,0},{16,24},{24,16},{1,9},{9,1},{17,25},{25,17},{2,10},{10... | collective-permute-start | bytes 1769480 | tf_op jit(solution)/shard_map/ppermute | solution.py:493
  34.1 113.3 %all-gather.7.cloned.1.call-start = ((), (), s32[]{:S(2)}) async-start(), calls=%async_computation.3 | async-start | bytes 2211840 | tf_op jit(solution)/shard_map/all_gather | solution.py:598
  34.4 13.1 %collective-permute-start.3 = (bf16[1,128,768]{2,1,0:T(8,128)(2,1)}, bf16[1,128,768]{2,1,0:T(8,128)(2,1)S(1)}, u32[]{:S(2)}, u32[]{:S(2)}) collective-permute-start(bf16[1,128,768]{2,1,0:T(8,128)(2,1)} %bitcast.20), channel_id=1, source_target_pairs={{0,2},{2,0},{4,6},{6,4},{1,3},{3,1},{5,7},{7,5},{8,10},{10,8},{12,... | collective-permute-start | bytes 589832 | tf_op jit(solution)/shard_map/ppermute | solution.py:500
  35.7 11.9 %collective-permute-start.4 = (bf16[1,128,768]{2,1,0:T(8,128)(2,1)}, bf16[1,128,768]{2,1,0:T(8,128)(2,1)S(1)}, u32[]{:S(2)}, u32[]{:S(2)}) collective-permute-start(bf16[1,128,768]{2,1,0:T(8,128)(2,1)} %bitcast.20), channel_id=1, source_target_pairs={{0,4},{2,6},{4,0},{6,2},{1,5},{3,7},{5,1},{7,3},{8,12},{10,14},{12... | collective-permute-start | bytes 589832 | tf_op jit(solution)/shard_map/ppermute | solution.py:500
  36.9 10.6 %collective-permute-start.5 = (bf16[1,128,768]{2,1,0:T(8,128)(2,1)}, bf16[1,128,768]{2,1,0:T(8,128)(2,1)S(1)}, u32[]{:S(2)}, u32[]{:S(2)}) collective-permute-start(bf16[1,128,768]{2,1,0:T(8,128)(2,1)} %bitcast.20), channel_id=1, source_target_pairs={{0,6},{2,4},{4,2},{6,0},{1,7},{3,5},{5,3},{7,1},{8,14},{10,12},{12... | collective-permute-start | bytes 589832 | tf_op jit(solution)/shard_map/ppermute | solution.py:500
  46.4 6.3 %collective-permute-start.9 = (bf16[576,512]{1,0:T(8,128)(2,1)}, bf16[576,512]{1,0:T(8,128)(2,1)S(1)}, u32[]{:S(2)}, u32[]{:S(2)}) collective-permute-start(bf16[576,512]{1,0:T(8,128)(2,1)} %collective-permute-done.8.refs_0_.refs_2_.ka.va), channel_id=1, source_target_pairs={{0,1},{1,0},{2,3},{3,2},{4,5},{5,4},{6,7},{7,6},{8,9},{9,8},{10,11... | collective-permute-start | bytes 1769480 | tf_op jit(solution)/shard_map/ppermute | solution.py:490
  49.6 10.6 %collective-permute-start.7 = (bf16[576,512]{1,0:T(8,128)(2,1)S(1)}, bf16[576,512]{1,0:T(8,128)(2,1)S(1)}, u32[]{:S(2)}, u32[]{:S(2)}) collective-permute-start(bf16[576,512]{1,0:T(8,128)(2,1)S(1)} %bitcast.118), channel_id=1, source_target_pairs={{0,1},{1,0},{2,3},{3,2},{4,5},{5,4},{6,7},{7,6},{8,9},{9,8},{10,11... | collective-permute-start | bytes 1769480 | tf_op jit(solution)/shard_map/ppermute | solution.py:490
  50.7 17.1 %collective-permute-start.6 = (bf16[576,512]{1,0:T(8,128)(2,1)S(1)}, bf16[576,512]{1,0:T(8,128)(2,1)}, u32[]{:S(2)}, u32[]{:S(2)}) collective-permute-start(bf16[576,512]{1,0:T(8,128)(2,1)S(1)} %bitcast.119), channel_id=1, source_target_pairs={{0,8},{8,0},{16,24},{24,16},{1,9},{9,1},{17,25},{25,17},{2,10},{10... | collective-permute-start | bytes 1769480 | tf_op jit(solution)/shard_map/ppermute | solution.py:493
  88.7 10.8 %collective-permute-start.13 = (bf16[192,1024]{1,0:T(8,128)(2,1)S(1)}, bf16[192,1024]{1,0:T(8,128)(2,1)}, u32[]{:S(2)}, u32[]{:S(2)}) collective-permute-start(bf16[192,1024]{1,0:T(8,128)(2,1)S(1)} %add_convert_fusion.6), channel_id=1, source_target_pairs={{0,8},{8,0},{16,24},{24,16},{1,9},{9,1},{17,25},{25,17},{2,10},{10... | collective-permute-start | bytes 1179656 | tf_op jit(solution)/shard_map/ppermute | solution.py:493
  99.5 11.0 %collective-permute-start.17 = (bf16[4,864,768]{2,1,0:T(8,128)(2,1)}, bf16[4,864,768]{2,1,0:T(8,128)(2,1)}, u32[]{:S(2)}, u32[]{:S(2)}) collective-permute-start(bf16[4,864,768]{2,1,0:T(8,128)(2,1)} %bitcast.169), channel_id=1, source_target_pairs={{0,1},{1,0},{2,3},{3,2},{4,5},{5,4},{6,7},{7,6},{8,9},{9,8},{10,11... | collective-permute-start | bytes 15925256 | tf_op jit(solution)/shard_map/ppermute | solution.py:490
  110.2 119.5 %reduce-scatter.4.cloned.1.call-start = ((), (), s32[]{:S(2)}) async-start(), calls=%async_computation.4 | async-start | bytes 6881280
  129.1 6.9 %collective-permute-start.18 = (bf16[192,256]{1,0:T(8,128)(2,1)}, bf16[192,256]{1,0:T(8,128)(2,1)S(1)}, u32[]{:S(2)}, u32[]{:S(2)}) collective-permute-start(bf16[192,256]{1,0:T(8,128)(2,1)} %get-tuple-element.117), channel_id=1, source_target_pairs={{0,2},{2,0},{4,6},{6,4},{1,3},{3,1},{5,7},{7,5},{8,10},{10,8},{12,... | collective-permute-start | bytes 294920 | tf_op jit(solution)/shard_map/ppermute | solution.py:500
  130.6 7.9 %collective-permute-start.19 = (bf16[192,256]{1,0:T(8,128)(2,1)}, bf16[192,256]{1,0:T(8,128)(2,1)S(1)}, u32[]{:S(2)}, u32[]{:S(2)}) collective-permute-start(bf16[192,256]{1,0:T(8,128)(2,1)} %get-tuple-element.118), channel_id=1, source_target_pairs={{0,4},{2,6},{4,0},{6,2},{1,5},{3,7},{5,1},{7,3},{8,12},{10,14},{12... | collective-permute-start | bytes 294920 | tf_op jit(solution)/shard_map/ppermute | solution.py:500
  130.8 9.6 %collective-permute-start.20 = (bf16[192,256]{1,0:T(8,128)(2,1)}, bf16[192,256]{1,0:T(8,128)(2,1)S(1)}, u32[]{:S(2)}, u32[]{:S(2)}) collective-permute-start(bf16[192,256]{1,0:T(8,128)(2,1)} %get-tuple-element.119), channel_id=1, source_target_pairs={{0,6},{2,4},{4,2},{6,0},{1,7},{3,5},{5,3},{7,1},{8,14},{10,12},{12... | collective-permute-start | bytes 294920 | tf_op jit(solution)/shard_map/ppermute | solution.py:500
  131.9 16.7 %collective-permute-start.21 = (bf16[8,256,384]{2,1,0:T(8,128)(2,1)}, bf16[8,256,384]{2,1,0:T(8,128)(2,1)}, u32[]{:S(2)}, u32[]{:S(2)}) collective-permute-start(bf16[8,256,384]{2,1,0:T(8,128)(2,1)} %get-tuple-element.126), channel_id=1, source_target_pairs={{0,1},{1,0},{2,3},{3,2},{4,5},{5,4},{6,7},{7,6},{8,9},{9,8},{10,11... | collective-permute-start | bytes 4718600 | tf_op jit(solution)/shard_map/ppermute | solution.py:490
  133.5 15.1 %collective-permute-start.22 = (bf16[6,256,384]{2,1,0:T(8,128)(2,1)}, bf16[6,256,384]{2,1,0:T(8,128)(2,1)}, u32[]{:S(2)}, u32[]{:S(2)}) collective-permute-start(bf16[6,256,384]{2,1,0:T(8,128)(2,1)} %get-tuple-element.128), channel_id=1, source_target_pairs={{0,1},{1,0},{2,3},{3,2},{4,5},{5,4},{6,7},{7,6},{8,9},{9,8},{10,11... | collective-permute-start | bytes 3538952 | tf_op jit(solution)/shard_map/ppermute | solution.py:490
  136.0 11.4 %collective-permute-start.23 = (bf16[4,96,256]{2,1,0:T(8,128)(2,1)}, bf16[4,96,256]{2,1,0:T(8,128)(2,1)S(1)}, u32[]{:S(2)}, u32[]{:S(2)}) collective-permute-start(bf16[4,96,256]{2,1,0:T(8,128)(2,1)} %get-tuple-element.129), channel_id=1, source_target_pairs={{0,1},{1,0},{2,3},{3,2},{4,5},{5,4},{6,7},{7,6},{8,9},{9,8},{10,11... | collective-permute-start | bytes 589832 | tf_op jit(solution)/shard_map/ppermute | solution.py:490
  138.4 18.9 %collective-permute-start.24 = (bf16[128,768]{1,0:T(8,128)(2,1)}, bf16[128,768]{1,0:T(8,128)(2,1)}, u32[]{:S(2)}, u32[]{:S(2)}) collective-permute-start(bf16[128,768]{1,0:T(8,128)(2,1)} %get-tuple-element.229), channel_id=1, source_target_pairs={{0,16},{8,24},{16,0},{24,8},{1,17},{9,25},{17,1},{25,9},{2,18},{10... | collective-permute-start | bytes 589832 | tf_op jit(solution)/shard_map/ppermute | solution.py:497
  141.3 16.0 %collective-permute-start.25 = (bf16[192,1024]{1,0:T(8,128)(2,1)S(1)}, bf16[192,1024]{1,0:T(8,128)(2,1)S(1)}, u32[]{:S(2)}, u32[]{:S(2)}) collective-permute-start(bf16[192,1024]{1,0:T(8,128)(2,1)S(1)} %slice_dynamic-update-slice_fusion.refs_4_), channel_id=1, source_target_pairs={{0,1},{1,0},{2,3},{3,2},{4,5},{5,4},{6,7},{7,6},{8,9},{9,8},{10,11... | collective-permute-start | bytes 1179656 | tf_op jit(solution)/shard_map/ppermute | solution.py:490
  147.5 30.7 %collective-permute-start.26 = (bf16[192,1024]{1,0:T(8,128)(2,1)S(1)}, bf16[192,1024]{1,0:T(8,128)(2,1)S(1)}, u32[]{:S(2)}, u32[]{:S(2)}) collective-permute-start(bf16[192,1024]{1,0:T(8,128)(2,1)S(1)} %slice_dynamic-update-slice_fusion.refs_4_), channel_id=1, source_target_pairs={{0,8},{8,0},{16,24},{24,16},{1,9},{9,1},{17,25},{25,17},{2,10},{10... | collective-permute-start | bytes 1179656 | tf_op jit(solution)/shard_map/ppermute | solution.py:493
  156.8 164.3 %all-reduce.3.cloned.1.call-start = ((), (), s32[]{:S(2)}) async-start(), calls=%async_computation.1 | async-start | bytes 2752512 | tf_op jit(solution)/shard_map/psum | solution.py:673
  178.1 16.4 %collective-permute-start.28 = (bf16[192,1024]{1,0:T(8,128)(2,1)S(1)}, bf16[192,1024]{1,0:T(8,128)(2,1)S(1)}, u32[]{:S(2)}, u32[]{:S(2)}) collective-permute-start(bf16[192,1024]{1,0:T(8,128)(2,1)S(1)} %collective-permute-done.26.refs_2_), channel_id=1, source_target_pairs={{0,1},{1,0},{2,3},{3,2},{4,5},{5,4},{6,7},{7,6},{8,9},{9,8},{10,11... | collective-permute-start | bytes 1179656 | tf_op jit(solution)/shard_map/ppermute | solution.py:490
  178.9 15.6 %collective-permute-start.27 = (bf16[192,1024]{1,0:T(8,128)(2,1)S(1)}, bf16[192,1024]{1,0:T(8,128)(2,1)S(1)}, u32[]{:S(2)}, u32[]{:S(2)}) collective-permute-start(bf16[192,1024]{1,0:T(8,128)(2,1)S(1)} %get-tuple-element.140), channel_id=1, source_target_pairs={{0,1},{1,0},{2,3},{3,2},{4,5},{5,4},{6,7},{7,6},{8,9},{9,8},{10,11... | collective-permute-start | bytes 1179656 | tf_op jit(solution)/shard_map/ppermute | solution.py:490
  191.8 34.7 %collective-permute-start.33 = (bf16[2,128,768]{2,1,0:T(8,128)(2,1)S(1)}, bf16[2,128,768]{2,1,0:T(8,128)(2,1)S(1)}, u32[]{:S(2)}, u32[]{:S(2)}) collective-permute-start(bf16[2,128,768]{2,1,0:T(8,128)(2,1)S(1)} %pad_maximum_fusion.10), channel_id=1, source_target_pairs={{0,4},{2,6},{4,0},{6,2},{1,5},{3,7},{5,1},{7,3},{8,12},{10,14},{12... | collective-permute-start | bytes 1179656 | tf_op jit(solution)/shard_map/ppermute | solution.py:500
  192.2 35.1 %collective-permute-start.32 = (bf16[2,128,768]{2,1,0:T(8,128)(2,1)S(1)}, bf16[2,128,768]{2,1,0:T(8,128)(2,1)S(1)}, u32[]{:S(2)}, u32[]{:S(2)}) collective-permute-start(bf16[2,128,768]{2,1,0:T(8,128)(2,1)S(1)} %pad_maximum_fusion.10), channel_id=1, source_target_pairs={{0,2},{2,0},{4,6},{6,4},{1,3},{3,1},{5,7},{7,5},{8,10},{10,8},{12,... | collective-permute-start | bytes 1179656 | tf_op jit(solution)/shard_map/ppermute | solution.py:500
  193.4 33.9 %collective-permute-start.34 = (bf16[2,128,768]{2,1,0:T(8,128)(2,1)S(1)}, bf16[2,128,768]{2,1,0:T(8,128)(2,1)S(1)}, u32[]{:S(2)}, u32[]{:S(2)}) collective-permute-start(bf16[2,128,768]{2,1,0:T(8,128)(2,1)S(1)} %pad_maximum_fusion.10), channel_id=1, source_target_pairs={{0,6},{2,4},{4,2},{6,0},{1,7},{3,5},{5,3},{7,1},{8,14},{10,12},{12... | collective-permute-start | bytes 1179656 | tf_op jit(solution)/shard_map/ppermute | solution.py:500
  205.9 10.3 %collective-permute-start.29 = (bf16[192,1024]{1,0:T(8,128)(2,1)S(1)}, bf16[192,1024]{1,0:T(8,128)(2,1)S(1)}, u32[]{:S(2)}, u32[]{:S(2)}) collective-permute-start(bf16[192,1024]{1,0:T(8,128)(2,1)S(1)} %get-tuple-element.145), channel_id=1, source_target_pairs={{0,1},{1,0},{2,3},{3,2},{4,5},{5,4},{6,7},{7,6},{8,9},{9,8},{10,11... | collective-permute-start | bytes 1179656 | tf_op jit(solution)/shard_map/ppermute | solution.py:490
  216.0 11.3 %collective-permute-start.31 = (bf16[2,192,1024]{2,1,0:T(8,128)(2,1)S(1)}, bf16[2,192,1024]{2,1,0:T(8,128)(2,1)S(1)}, u32[]{:S(2)}, u32[]{:S(2)}) collective-permute-start(bf16[2,192,1024]{2,1,0:T(8,128)(2,1)S(1)} %key_backward.4), channel_id=1, source_target_pairs={{0,1},{1,0},{2,3},{3,2},{4,5},{5,4},{6,7},{7,6},{8,9},{9,8},{10,11... | collective-permute-start | bytes 2359304 | tf_op jit(solution)/shard_map/ppermute | solution.py:490
  216.2 11.1 %collective-permute-start.30 = (bf16[192,1024]{1,0:T(8,128)(2,1)S(1)}, bf16[192,1024]{1,0:T(8,128)(2,1)S(1)}, u32[]{:S(2)}, u32[]{:S(2)}) collective-permute-start(bf16[192,1024]{1,0:T(8,128)(2,1)S(1)} %add_convert_fusion.4), channel_id=1, source_target_pairs={{0,8},{8,0},{16,24},{24,16},{1,9},{9,1},{17,25},{25,17},{2,10},{10... | collective-permute-start | bytes 1179656 | tf_op jit(solution)/shard_map/ppermute | solution.py:493
  226.4 26.1 %collective-permute-start.40 = (bf16[4,3,96,768]{3,2,1,0:T(8,128)(2,1)}, bf16[4,3,96,768]{3,2,1,0:T(8,128)(2,1)}, u32[]{:S(2)}, u32[]{:S(2)}) collective-permute-start(bf16[4,3,96,768]{3,2,1,0:T(8,128)(2,1)} %bitcast.34.refs_4_), channel_id=1, source_target_pairs={{0,1},{1,0},{2,3},{3,2},{4,5},{5,4},{6,7},{7,6},{8,9},{9,8},{10,11... | collective-permute-start | bytes 5308424 | tf_op jit(solution)/shard_map/ppermute | solution.py:490
  228.5 24.1 %collective-permute-start.36 = (bf16[2,192,1024]{2,1,0:T(8,128)(2,1)}, bf16[2,192,1024]{2,1,0:T(8,128)(2,1)}, u32[]{:S(2)}, u32[]{:S(2)}) collective-permute-start(bf16[2,192,1024]{2,1,0:T(8,128)(2,1)} %add_convert_fusion.1), channel_id=1, source_target_pairs={{0,8},{8,0},{16,24},{24,16},{1,9},{9,1},{17,25},{25,17},{2,10},{10... | collective-permute-start | bytes 2359304 | tf_op jit(solution)/shard_map/ppermute | solution.py:493
  240.8 11.8 %collective-permute-start.35 = (bf16[2,192,1024]{2,1,0:T(8,128)(2,1)S(1)}, bf16[2,192,1024]{2,1,0:T(8,128)(2,1)}, u32[]{:S(2)}, u32[]{:S(2)}) collective-permute-start(bf16[2,192,1024]{2,1,0:T(8,128)(2,1)S(1)} %key_backward.6), channel_id=1, source_target_pairs={{0,1},{1,0},{2,3},{3,2},{4,5},{5,4},{6,7},{7,6},{8,9},{9,8},{10,11... | collective-permute-start | bytes 2359304 | tf_op jit(solution)/shard_map/ppermute | solution.py:490
  254.7 9.5 %collective-permute-start.39 = (bf16[3,192,256]{2,1,0:T(8,128)(2,1)S(1)}, bf16[3,192,256]{2,1,0:T(8,128)(2,1)S(1)}, u32[]{:S(2)}, u32[]{:S(2)}) collective-permute-start(bf16[3,192,256]{2,1,0:T(8,128)(2,1)S(1)} %pad_maximum_fusion.15), channel_id=1, source_target_pairs={{0,6},{2,4},{4,2},{6,0},{1,7},{3,5},{5,3},{7,1},{8,14},{10,12},{12... | collective-permute-start | bytes 884744 | tf_op jit(solution)/shard_map/ppermute | solution.py:500
  256.1 14.8 %collective-permute-start.38 = (bf16[3,192,256]{2,1,0:T(8,128)(2,1)S(1)}, bf16[3,192,256]{2,1,0:T(8,128)(2,1)S(1)}, u32[]{:S(2)}, u32[]{:S(2)}) collective-permute-start(bf16[3,192,256]{2,1,0:T(8,128)(2,1)S(1)} %pad_maximum_fusion.14), channel_id=1, source_target_pairs={{0,4},{2,6},{4,0},{6,2},{1,5},{3,7},{5,1},{7,3},{8,12},{10,14},{12... | collective-permute-start | bytes 884744 | tf_op jit(solution)/shard_map/ppermute | solution.py:500
  256.3 14.6 %collective-permute-start.37 = (bf16[3,192,256]{2,1,0:T(8,128)(2,1)S(1)}, bf16[3,192,256]{2,1,0:T(8,128)(2,1)S(1)}, u32[]{:S(2)}, u32[]{:S(2)}) collective-permute-start(bf16[3,192,256]{2,1,0:T(8,128)(2,1)S(1)} %pad_maximum_fusion.13), channel_id=1, source_target_pairs={{0,2},{2,0},{4,6},{6,4},{1,3},{3,1},{5,7},{7,5},{8,10},{10,8},{12,... | collective-permute-start | bytes 884744 | tf_op jit(solution)/shard_map/ppermute | solution.py:500
  258.8 21.3 %collective-permute-start.42 = (bf16[288,768]{1,0:T(8,128)(2,1)S(1)}, bf16[288,768]{1,0:T(8,128)(2,1)S(1)}, u32[]{:S(2)}, u32[]{:S(2)}) collective-permute-start(bf16[288,768]{1,0:T(8,128)(2,1)S(1)} %constant_dynamic-slice_fusion.1), channel_id=1, source_target_pairs={{0,1},{1,0},{2,3},{3,2},{4,5},{5,4},{6,7},{7,6},{8,9},{9,8},{10,11... | collective-permute-start | bytes 1327112 | tf_op jit(solution)/shard_map/ppermute | solution.py:490
  278.0 20.4 %collective-permute-start.41 = (bf16[128,768]{1,0:T(8,128)(2,1)S(1)}, bf16[128,768]{1,0:T(8,128)(2,1)S(1)}, u32[]{:S(2)}, u32[]{:S(2)}) collective-permute-start(bf16[128,768]{1,0:T(8,128)(2,1)S(1)} %get-tuple-element.227), channel_id=1, source_target_pairs={{0,16},{8,24},{16,0},{24,8},{1,17},{9,25},{17,1},{25,9},{2,18},{10... | collective-permute-start | bytes 589832 | tf_op jit(solution)/shard_map/ppermute | solution.py:497
  280.2 22.3 %collective-permute-start.43 = (bf16[144,768]{1,0:T(8,128)(2,1)S(1)}, bf16[144,768]{1,0:T(8,128)(2,1)S(1)}, u32[]{:S(2)}, u32[]{:S(2)}) collective-permute-start(bf16[144,768]{1,0:T(8,128)(2,1)S(1)} %constant_dynamic-slice_fusion), channel_id=1, source_target_pairs={{0,8},{8,0},{16,24},{24,16},{1,9},{9,1},{17,25},{25,17},{2,10},{10... | collective-permute-start | bytes 663560 | tf_op jit(solution)/shard_map/ppermute | solution.py:493
  302.6 18.6 %collective-permute-start.44 = (bf16[2,128,768]{2,1,0:T(8,128)(2,1)S(1)}, bf16[2,128,768]{2,1,0:T(8,128)(2,1)}, u32[]{:S(2)}, u32[]{:S(2)}) collective-permute-start(bf16[2,128,768]{2,1,0:T(8,128)(2,1)S(1)} %pad_maximum_fusion.11), channel_id=1, source_target_pairs={{0,2},{2,0},{4,6},{6,4},{1,3},{3,1},{5,7},{7,5},{8,10},{10,8},{12,... | collective-permute-start | bytes 1179656 | tf_op jit(solution)/shard_map/ppermute | solution.py:500
  303.3 17.9 %collective-permute-start.45 = (bf16[2,128,768]{2,1,0:T(8,128)(2,1)S(1)}, bf16[2,128,768]{2,1,0:T(8,128)(2,1)}, u32[]{:S(2)}, u32[]{:S(2)}) collective-permute-start(bf16[2,128,768]{2,1,0:T(8,128)(2,1)S(1)} %pad_maximum_fusion.11), channel_id=1, source_target_pairs={{0,4},{2,6},{4,0},{6,2},{1,5},{3,7},{5,1},{7,3},{8,12},{10,14},{12... | collective-permute-start | bytes 1179656 | tf_op jit(solution)/shard_map/ppermute | solution.py:500
  303.4 17.7 %collective-permute-start.46 = (bf16[2,128,768]{2,1,0:T(8,128)(2,1)S(1)}, bf16[2,128,768]{2,1,0:T(8,128)(2,1)}, u32[]{:S(2)}, u32[]{:S(2)}) collective-permute-start(bf16[2,128,768]{2,1,0:T(8,128)(2,1)S(1)} %pad_maximum_fusion.11), channel_id=1, source_target_pairs={{0,6},{2,4},{4,2},{6,0},{1,7},{3,5},{5,3},{7,1},{8,14},{10,12},{12... | collective-permute-start | bytes 1179656 | tf_op jit(solution)/shard_map/ppermute | solution.py:500
  305.3 15.7 %collective-permute-start.47 = (bf16[144,768]{1,0:T(8,128)(2,1)S(1)}, bf16[144,768]{1,0:T(8,128)(2,1)S(1)}, u32[]{:S(2)}, u32[]{:S(2)}) collective-permute-start(bf16[144,768]{1,0:T(8,128)(2,1)S(1)} %fusion.6), channel_id=1, source_target_pairs={{0,16},{8,24},{16,0},{24,8},{1,17},{9,25},{17,1},{25,9},{2,18},{10... | collective-permute-start | bytes 663560 | tf_op jit(solution)/shard_map/ppermute | solution.py:497
  321.0 6.6 %collective-permute-start.48 = (bf16[144,768]{1,0:T(8,128)(2,1)S(1)}, bf16[144,768]{1,0:T(8,128)(2,1)}, u32[]{:S(2)}, u32[]{:S(2)}) collective-permute-start(bf16[144,768]{1,0:T(8,128)(2,1)S(1)} %add_convert_fusion.7), channel_id=1, source_target_pairs={{0,8},{8,0},{16,24},{24,16},{1,9},{9,1},{17,25},{25,17},{2,10},{10... | collective-permute-start | bytes 663560 | tf_op jit(solution)/shard_map/ppermute | solution.py:493
  321.2 15.0 %collective-permute-start.50 = (bf16[896,768]{1,0:T(8,128)(2,1)}, bf16[896,768]{1,0:T(8,128)(2,1)S(1)}, u32[]{:S(2)}, u32[]{:S(2)}) collective-permute-start(bf16[896,768]{1,0:T(8,128)(2,1)} %all-reduce.3.cloned.1.call-done.near), channel_id=1, source_target_pairs={{0,1},{1,0},{2,3},{3,2},{4,5},{5,4},{6,7},{7,6},{8,9},{9,8},{10,11... | collective-permute-start | bytes 4128776 | tf_op jit(solution)/shard_map/ppermute | solution.py:490
  (50 other events, 283.7 us)
Sparse Core Ops, SparseCore 0:
  34.2 62.7 all-gather.4
  110.3 37.0 all-gather.6
  156.9 71.6 reduce-scatter.3
  241.3 75.1 all-reduce.2

commit v20 on v19

--- a/solution.py
+++ b/solution.py
@@ -625,7 +625,7 @@
     )
     layer_moved = away(layer_rows)
     weight_parts = weight_grads(
-        core, after(small, grad, w_qkv_t), [keep, taken, keep_back, taken_back], attn_parts, heads_far
+        core, after(small, grad), [keep, taken, keep_back, taken_back], attn_parts, heads_far
     )
 
     weight_sum = lax.psum_scatter(weight_parts, "head", scatter_dimension=0, tiled=True)[0]
@@ -633,7 +633,7 @@
     grad_o = after(over_seq(grad), weight_parts)
     layer_moved = [after(x, weight_parts) for x in layer_moved]
     part, dq, dq_o = query_backward(
-        signed, signed_t, bits, head_n, tables, [(near, after(far, *layer_moved)), (near_o, far_o)], [grad, grad_o],
+        signed, signed_t, bits, head_n, tables, [(near, after(far, w_qkv_t, *layer_moved)), (near_o, far_o)], [grad, grad_o],
         None, False, [f32, bf16],
     )
 

time: 355 us -> 352 us (level)
  waiting for transfers between devices: 63.3 us -> 58.4 us
    all_gather x1, waiting for transfers between devices: 4.17 us -> 0.02 us  [shards(): w_qkv_t = lax.all_gather(after(w_qkv_t, weights[0]), 'head', axis=0)]
    unnamed x98 -> x102, local copies, waits for them, and re-layouts: 19.5 us -> 20.9 us
where the time goes in v20:
time: 352 us; the launch traced here: 347 us
  Pallas kernels  157 us (45%)
  waiting for transfers between devices  58.4 us (17%)
  starting transfers between devices  50.8 us (14%)
  local copies, waits for them, and re-layouts  37.6 us (11%)
  other arithmetic  23.7 us (7%)
  between operations  15.1 us (4%)
  matrix products  3.9 us (1%)
    pallas_call x3, Pallas kernels, query_backward(): call(partial(query_back_kernel, chunk=4 * blocks, blocks=blocks, last=las...  43.3 us
    pallas_call x4, Pallas kernels, key_backward(): call(partial(key_back_kernel, chunk=4), heads, micros, 'key_backward', [w...  38.1 us
    pallas_call x4, Pallas kernels, single(): pl.pallas_call(kernel, in_specs=[pl.BlockSpec(memory_space=pltpu.SMEM)] +...  36.4 us
    ppermute x4, waiting for transfers between devices, over_group(): return lax.ppermute(x, 'hash', moves)  28.5 us
    pallas_call x5, Pallas kernels, key_tables(): call(partial(key_kernel, chunk=2, blocks=len(blocks)), heads, 30 if len(b...  23.7 us
    unnamed x102, local copies, waits for them, and re-layouts  20.9 us
    ppermute x20, starting transfers between devices, over_seq(): return lax.ppermute(x, 'seq', [(0, 1), (1, 0)])  17.3 us
    ppermute x18, starting transfers between devices, over_head(): return lax.ppermute(x, 'head', [(h, h ^ j) for h in range(head_count)])  16.7 us
  transfers between devices with their start and end apart: 55, of which 12 were waited for; matrix products, arithmetic and copies ran while one was open for 14% of the time, Pallas kernels for 44%

profile of v20, /device:TPU:1, one launch (start us, length us, event | category | flops | bytes accessed | tf_op | source)
XLA Modules:
  0.0 347.0 jit_solution(6120027635719664575)
XLA Ops:
  7.3 4.5 %constant_dynamic-slice_fusion.7 = (bf16[1,128,1,768]{3,2,1,0:T(2,128)(2,1)S(1)}, bf16[1,128,1,768]{3,2,1,0:T(2,128)(2,1)}, bf16[1,128,1,768]{3,2,1,0:T(2,128)(2...) fusion(bf16[1,512,2,768]{3,2,1,0:T(2,128)(2,1)} %param.11, s32[]{:T(128)S(6)} %select_n.222, ...), kind=kLoop, calls=%fused_computation.119 | loop fusion | bytes 1966104 | tf_op jit(solution)/shard_map/jit(dynamic_index_in_dim)/dynamic_slice | solution.py:503
  12.6 3.1 collective-permute-start
  16.3 2.5 collective-permute-start.1
  20.5 2.4 copy.54
  22.9 2.0 dynamic-slice_bitcast_fusion
  24.9 1.9 constant_dynamic-slice_fusion.3
  37.1 1.7 pad_maximum_fusion.9.x_in
  38.8 5.2 %key_tables.5.refs_4_ = f32[3,2048,64]{2,1,0:T(8,128)S(1)} custom-call(bf16[64,64]{1,0:T(8,128)(2,1)S(1)} %bitcast.126, bf16[576,512]{1,0:T(8,128)(2,1)} %bitcast.14.refs_0_.refs_2_.ka.va, bf16[576,512]{1,0:T(8,128)(2,1)} %collective-permute-done.2.refs_1_.refs_3_.refs_0_.refs_2_.ka.va, bf16[576,512]{1,0:T(8,128)(2,1)} %bitcast.14.refs_0_.refs_2_.ka.va, ...), custom_call_target="tpu_custom_call" | custom-call | flops 1100000000 | bytes 1048576 | tf_op jit(solution)/shard_map/key_tables/pallas_call | solution.py:192
  44.1 2.4 collective-permute-done.8.refs_0_.refs_2_.ka.va
  52.7 5.8 %key_tables.6.refs_4_ = f32[3,2048,64]{2,1,0:T(8,128)S(1)} custom-call(bf16[64,64]{1,0:T(8,128)(2,1)S(1)} %bitcast.127, bf16[576,512]{1,0:T(8,128)(2,1)} %collective-permute-done.8.refs_0_.refs_2_.ka.va, bf16[576,512]{1,0:T(8,128)(2,1)S(1)} %collective-permute-done.9.refs_1_.refs_3_.refs_0_.ka.va, ...), custom_call_target="tpu_custom_call" | custom-call | flops 32999999488 | bytes 1048576 | tf_op jit(solution)/shard_map/key_tables/pallas_call | solution.py:192
  60.2 5.7 %key_tables.7.refs_2_ = f32[3,2048,64]{2,1,0:T(8,128)S(1)} custom-call(bf16[64,64]{1,0:T(8,128)(2,1)S(1)} %bitcast.128, bf16[576,512]{1,0:T(8,128)(2,1)S(1)} %bitcast.120, bf16[576,512]{1,0:T(8,128)(2,1)S(1)} %collective-permute-done.7.refs_1_.refs_3_.kb.vb, bf16[576,512]{1,0:T(8,128)(2,1)S(1)} %bitcast.121, ...), custom_call_target="tpu_custom_call" | custom-call | flops 32999999488 | bytes 1048576 | tf_op jit(solution)/shard_map/key_tables/pallas_call | solution.py:192
  65.9 1.9 copy-done.2
  69.1 4.4 %key_tables.8.refs_2_ = f32[3,2048,64]{2,1,0:T(8,128)S(1)} custom-call(bf16[64,64]{1,0:T(8,128)(2,1)S(1)} %bitcast.129, bf16[576,512]{1,0:T(8,128)(2,1)} %collective-permute-done.6.refs_0_.refs_1_.kb.vb, bf16[576,512]{1,0:T(8,128)(2,1)} %collective-permute-done.6.refs_0_.refs_1_.kb.vb, f32[3,2048,64]{2,1,0:T(8,128)} %copy-done.2), custom_call_target="tpu_custom_call" | custom-call | flops 1100000000 | bytes 1048576 | tf_op jit(solution)/shard_map/key_tables/pallas_call | solution.py:192
  73.5 2.6 key_tables.9.tables
  76.1 3.3 query_estimates.4
  79.6 4.2 %query_estimates.5 = bf16[192,1024]{1,0:T(8,128)(2,1)S(1)} custom-call(bf16[64,64]{1,0:T(8,128)(2,1)S(1)} %bitcast.132, bf16[3,2048,64]{2,1,0:T(8,128)(2,1)S(1)} %key_tables.9.tables, bf16[576,512]{1,0:T(8,128)(2,1)} %collective-permute-done.8.refs_0_.refs_2_.ka.va, bf16[576,512]{1,0:T(8,128)(2,1)} %collective-permute-done.6.refs_0_.refs_1_.kb.vb), custom_call_target="tpu_custom_call" | custom-call | flops 1100000000 | bytes 1048576 | tf_op jit(solution)/shard_map/query_estimates/pallas_call | solution.py:205
  84.0 4.2 %query_estimates.6 = bf16[192,1024]{1,0:T(8,128)(2,1)S(1)} custom-call(bf16[64,64]{1,0:T(8,128)(2,1)S(1)} %bitcast.133, bf16[3,2048,64]{2,1,0:T(8,128)(2,1)S(1)} %key_tables.9.tables, bf16[576,512]{1,0:T(8,128)(2,1)} %collective-permute-done.2.refs_1_.refs_3_.refs_0_.refs_2_.ka.va, bf16[576,512]{1,0:T(8,128)(2,1)S(1)} %copy-done.9), custom_call_target="tpu_custom_call" | custom-call | flops 1100000000 | bytes 1048576 | tf_op jit(solution)/shard_map/query_estimates/pallas_call | solution.py:205
  89.4 4.1 %query_estimates.7 = f32[192,1024]{1,0:T(8,128)S(1)} custom-call(bf16[64,64]{1,0:T(8,128)(2,1)S(1)} %bitcast.134, bf16[3,2048,64]{2,1,0:T(8,128)(2,1)S(1)} %key_tables.9.tables, bf16[576,512]{1,0:T(8,128)(2,1)} %bitcast.14.refs_0_.refs_2_.ka.va, bf16[576,512]{1,0:T(8,128)(2,1)S(1)} %bitcast.122), custom_call_target="tpu_custom_call" | custom-call | flops 1100000000 | bytes 1048576 | tf_op jit(solution)/shard_map/query_estimates/pallas_call | solution.py:205
  93.6 5.9 %collective-permute-done.13 = bf16[192,1024]{1,0:T(8,128)(2,1)} collective-permute-done((bf16[192,1024]{1,0:T(8,128)(2,1)S(1)}, bf16[192,1024]{1,0:T(8,128)(2,1)}, u32[]{:S(2)}, u32[]{:S(2)}) %collective-permute-start.13) | collective-permute-done | bytes 393248 | tf_op jit(solution)/shard_map/ppermute | solution.py:493
  102.4 2.4 collective-permute-start.16
  106.0 1.8 collective-permute-done.16.refs_3_.refs_7_
  107.8 2.4 collective-permute-done.15.refs_2_.refs_6_
  110.8 18.3 %dense.1 = (bf16[256,768]{1,0:T(8,128)(2,1)}, f32[256,768]{1,0:T(8,128)}, bf16[8,256,384]{2,1,0:T(8,128)(2,1)}, bf16[8,256,384]{2,1,0:T(8,128)(2,1)}, bf16[6,256...) custom-call(s32[2]{0:T(128)} %pad_add_fusion.core, ...), custom_call_target="tpu_custom_call" | custom-call | flops 24199999488 | bytes 1048576 | tf_op jit(solution)/shard_map/dense/pallas_call | solution.py:390
  134.4 1.7 fusion.24
  138.3 2.0 collective-permute-start.24
  141.3 2.1 collective-permute-start.25
  145.9 8.2 %weight_grads.1 = bf16[4,896,768]{2,1,0:T(8,128)(2,1)} custom-call(s32[2]{0:T(128)} %pad_add_fusion.core, f32[16,768]{1,0:T(8,128)} %get-tuple-element.123.small, bf16[8,256,384]{2,1,0:T(8,128)(2,1)} %get-tuple-element.124.refs_0_, bf16[8,256,384]{2,1,0:T(8,128)(2,1)} %copy-done.36, bf16[6,256,384]{2,1,0:T(8,128)(2,1)} %get-tuple-element.126.refs_2_, ...), custom_call_target="tpu_custom_call" | custom-call | flops 7699999744 | bytes 1048576 | tf_op jit(solution)/shard_map/weight_grads/pallas_call | solution.py:390
  155.2 20.3 %query_backward.3 = (f32[3,2048,64]{2,1,0:T(8,128)}, f32[192,1024]{1,0:T(8,128)S(1)}, bf16[192,1024]{1,0:T(8,128)(2,1)S(1)}) custom-call(bf16[64,64]{1,0:T(8,128)(2,1)S(1)} %bitcast.136, bf16[64,128]{1,0:T(8,128)(2,1)S(1)} %pad_maximum_fusion.20.planes_t, bf16[80,2048]{1,0:T(8,128)(2,1)S(1)} %copy-done.14, bf16[3,2048,64]{2,1,0:T(8,128)(2,1)} %copy-done.4, ...), custom_call_target="tpu_custom_call" | custom-call | flops 54999998464 | bytes 1048576 | tf_op jit(solution)/shard_map/query_backward/pallas_call | solution.py:229
  176.0 11.8 %query_backward.4 = (f32[3,2048,64]{2,1,0:T(8,128)}, f32[192,1024]{1,0:T(8,128)S(1)}) custom-call(bf16[64,64]{1,0:T(8,128)(2,1)S(1)} %bitcast.137, bf16[64,128]{1,0:T(8,128)(2,1)S(1)} %pad_maximum_fusion.20.planes_t, bf16[80,2048]{1,0:T(8,128)(2,1)S(1)} %copy-done.14, bf16[3,2048,64]{2,1,0:T(8,128)(2,1)S(1)} %copy-done.5, ...), custom_call_target="tpu_custom_call" | custom-call | flops 27499999232 | bytes 1048576 | tf_op jit(solution)/shard_map/query_backward/pallas_call | solution.py:229
  191.7 11.2 %query_backward.5 = (bf16[3,2048,64]{2,1,0:T(8,128)(2,1)S(1)}, bf16[192,1024]{1,0:T(8,128)(2,1)S(1)}) custom-call(bf16[64,64]{1,0:T(8,128)(2,1)S(1)} %bitcast.138, bf16[64,128]{1,0:T(8,128)(2,1)S(1)} %pad_maximum_fusion.20.planes_t, bf16[80,2048]{1,0:T(8,128)(2,1)S(1)} %copy-done.14, bf16[3,2048,64]{2,1,0:T(8,128)(2,1)S(1)} %copy-done.5, ...), custom_call_target="tpu_custom_call" | custom-call | flops 27499999232 | bytes 1048576 | tf_op jit(solution)/shard_map/query_backward/pallas_call | solution.py:229
  204.2 8.8 %key_backward.4 = bf16[2,192,1024]{2,1,0:T(8,128)(2,1)S(1)} custom-call(bf16[64,64]{1,0:T(8,128)(2,1)S(1)} %bitcast.139, bf16[64,128]{1,0:T(8,128)(2,1)S(1)} %pad_maximum_fusion.20.planes_t, bf16[80,2048]{1,0:T(8,128)(2,1)S(1)} %copy-done.14, bf16[576,512]{1,0:T(8,128)(2,1)S(1)} %copy-done.13, ...), custom_call_target="tpu_custom_call" | custom-call | flops 27499999232 | bytes 1048576 | tf_op jit(solution)/shard_map/key_backward/pallas_call | solution.py:243
  213.8 9.8 %key_backward.5 = bf16[2,192,1024]{2,1,0:T(8,128)(2,1)S(1)} custom-call(bf16[64,64]{1,0:T(8,128)(2,1)S(1)} %bitcast.140, bf16[64,128]{1,0:T(8,128)(2,1)S(1)} %pad_maximum_fusion.20.planes_t, bf16[80,2048]{1,0:T(8,128)(2,1)S(1)} %copy-done.14, bf16[576,512]{1,0:T(8,128)(2,1)} %collective-permute-done.8.refs_0_.refs_2_.ka.va, ...), custom_call_target="tpu_custom_call" | custom-call | flops 27499999232 | bytes 1048576 | tf_op jit(solution)/shard_map/key_backward/pallas_call | solution.py:243
  228.1 9.7 %key_backward.6 = bf16[2,192,1024]{2,1,0:T(8,128)(2,1)S(1)} custom-call(bf16[64,64]{1,0:T(8,128)(2,1)S(1)} %bitcast.141, bf16[64,128]{1,0:T(8,128)(2,1)S(1)} %pad_maximum_fusion.20.planes_t, bf16[80,2048]{1,0:T(8,128)(2,1)S(1)} %copy-done.14, bf16[576,512]{1,0:T(8,128)(2,1)} %collective-permute-done.2.refs_1_.refs_3_.refs_0_.refs_2_.ka.va, ...), custom_call_target="tpu_custom_call" | custom-call | flops 27499999232 | bytes 1048576 | tf_op jit(solution)/shard_map/key_backward/pallas_call | solution.py:243
  239.5 9.9 %key_backward.7 = f32[2,192,1024]{2,1,0:T(8,128)S(1)} custom-call(bf16[64,64]{1,0:T(8,128)(2,1)S(1)} %bitcast.142, bf16[64,128]{1,0:T(8,128)(2,1)S(1)} %pad_maximum_fusion.20.planes_t, bf16[80,2048]{1,0:T(8,128)(2,1)S(1)} %copy-done.14, bf16[576,512]{1,0:T(8,128)(2,1)} %bitcast.14.refs_0_.refs_2_.ka.va, bf16[576,512]{1,0:T(8,128)(2,1)S(1)} %bitcast.124, ...), custom_call_target="tpu_custom_call" | custom-call | flops 27499999232 | bytes 1048576 | tf_op jit(solution)/shard_map/key_backward/pallas_call | solution.py:243
  249.5 1.7 add_convert_fusion
  251.6 1.8 collective-permute-start.39
  257.5 3.6 %collective-permute-done.39.refs_3_ = bf16[3,192,256]{2,1,0:T(8,128)(2,1)S(1)} collective-permute-done((bf16[3,192,256]{2,1,0:T(8,128)(2,1)S(1)}, bf16[3,192,256]{2,1,0:T(8,128)(2,1)S(1)}, u32[]{:S(2)}, u32[]{:S(2)}) %collective-permute-start.39) | collective-permute-done | bytes 294944 | tf_op jit(solution)/shard_map/ppermute | solution.py:500
  261.2 6.7 %collective-permute-done.38.refs_2_ = bf16[3,192,256]{2,1,0:T(8,128)(2,1)S(1)} collective-permute-done((bf16[3,192,256]{2,1,0:T(8,128)(2,1)S(1)}, bf16[3,192,256]{2,1,0:T(8,128)(2,1)S(1)}, u32[]{:S(2)}, u32[]{:S(2)}) %collective-permute-start.38) | collective-permute-done | bytes 294944 | tf_op jit(solution)/shard_map/ppermute | solution.py:500
  268.7 5.2 %input_grad.1 = bf16[256,768]{1,0:T(8,128)(2,1)} custom-call(s32[2]{0:T(128)} %pad_add_fusion.core, f32[256,768]{1,0:T(8,128)} %get-tuple-element.150.grad_first, bf16[3,192,256]{2,1,0:T(8,128)(2,1)} %pad_maximum_fusion.12.refs_0_, bf16[3,192,256]{2,1,0:T(8,128)(2,1)} %copy-done.40, bf16[3,192,256]{2,1,0:T(8,128)(2,1)} %copy-done.39, ...), custom_call_target="tpu_custom_call" | custom-call | flops 44000002048 | bytes 1048576 | tf_op jit(solution)/shard_map/input_grad/pallas_call | solution.py:390
  274.9 1.9 collective-permute-start.41
  277.9 17.8 %collective-permute-done.41 = bf16[128,768]{1,0:T(8,128)(2,1)S(1)} collective-permute-done((bf16[128,768]{1,0:T(8,128)(2,1)S(1)}, bf16[128,768]{1,0:T(8,128)(2,1)S(1)}, u32[]{:S(2)}, u32[]{:S(2)}) %collective-permute-start.41) | collective-permute-done | bytes 196640 | tf_op jit(solution)/shard_map/ppermute | solution.py:497
  295.8 3.6 %collective-permute-done.43 = bf16[144,768]{1,0:T(8,128)(2,1)S(1)} collective-permute-done((bf16[144,768]{1,0:T(8,128)(2,1)S(1)}, bf16[144,768]{1,0:T(8,128)(2,1)S(1)}, u32[]{:S(2)}, u32[]{:S(2)}) %collective-permute-start.43) | collective-permute-done | bytes 221216 | tf_op jit(solution)/shard_map/ppermute | solution.py:493
  304.1 2.8 copy.56
  306.9 10.7 %collective-permute-done.47 = bf16[144,768]{1,0:T(8,128)(2,1)S(1)} collective-permute-done((bf16[144,768]{1,0:T(8,128)(2,1)S(1)}, bf16[144,768]{1,0:T(8,128)(2,1)S(1)}, u32[]{:S(2)}, u32[]{:S(2)}) %collective-permute-start.47) | collective-permute-done | bytes 221216 | tf_op jit(solution)/shard_map/ppermute | solution.py:497
  317.8 2.7 collective-permute-start.50
  322.1 2.1 collective-permute-done.48
  327.1 4.1 %copy.57 = f32[1,512,2,768]{3,2,1,0:T(2,128)} copy(f32[1,512,2,768]{3,1,2,0:T(8,128)S(1)} %maximum_convert_fusion) | data formatting | bytes 6291456
  335.5 4.7 %weight_results.1 = (f32[768,768]{1,0:T(8,128)}, f32[768,768]{1,0:T(8,128)}, f32[192,768]{1,0:T(8,128)}) custom-call(s32[2]{0:T(128)} %pad_add_fusion.core, bf16[896,768]{1,0:T(8,128)(2,1)} %all-reduce.3.cloned.1.call-done.near, bf16[896,768]{1,0:T(8,128)(2,1)} %copy-done.35), custom_call_target="tpu_custom_call" | custom-call | flops 3300000000 | bytes 1048576 | tf_op jit(solution)/shard_map/weight_results/pallas_call | solution.py:390
  (261 shorter events, 74.3 us)
Async XLA Ops:
  7.2 92.3 %all-gather.5.cloned.1.call-start = ((), (), s32[]{:S(2)}) async-start(), calls=%async_computation.2 | async-start | bytes 6635520 | tf_op jit(solution)/shard_map/all_gather | solution.py:538
  12.6 17.1 %collective-permute-start = (bf16[128,768]{1,0:T(8,128)(2,1)}, bf16[128,768]{1,0:T(8,128)(2,1)}, u32[]{:S(2)}, u32[]{:S(2)}) collective-permute-start(bf16[128,768]{1,0:T(8,128)(2,1)} %bitcast.116), channel_id=1, source_target_pairs={{0,16},{8,24},{16,0},{24,8},{1,17},{9,25},{17,1},{25,9},{2,18},{10... | collective-permute-start | bytes 589832 | tf_op jit(solution)/shard_map/ppermute | solution.py:497
  16.3 20.6 %collective-permute-start.1 = (bf16[8,8,64]{2,0,1:T(8,128)(2,1)}, bf16[8,8,64]{2,0,1:T(8,128)(2,1)S(1)}, u32[]{:S(2)}, u32[]{:S(2)}) collective-permute-start(bf16[8,8,64]{2,0,1:T(8,128)(2,1)} %fusion.16), channel_id=1, source_target_pairs={{0,0},{8,1},{16,8},{24,9},{1,16},{9,17},{17,24},{25,25},{2,2},{10,... | collective-permute-start | bytes 24584 | tf_op jit(solution)/shard_map/ppermute | solution.py:522
  31.2 7.6 %collective-permute-start.2 = (bf16[576,512]{1,0:T(8,128)(2,1)}, bf16[576,512]{1,0:T(8,128)(2,1)}, u32[]{:S(2)}, u32[]{:S(2)}) collective-permute-start(bf16[576,512]{1,0:T(8,128)(2,1)} %bitcast.14.refs_0_.refs_2_.ka.va), channel_id=1, source_target_pairs={{0,1},{1,0},{2,3},{3,2},{4,5},{5,4},{6,7},{7,6},{8,9},{9,8},{10,11... | collective-permute-start | bytes 1769480 | tf_op jit(solution)/shard_map/ppermute | solution.py:490
  31.2 15.2 %collective-permute-start.8 = (bf16[576,512]{1,0:T(8,128)(2,1)}, bf16[576,512]{1,0:T(8,128)(2,1)}, u32[]{:S(2)}, u32[]{:S(2)}) collective-permute-start(bf16[576,512]{1,0:T(8,128)(2,1)} %bitcast.14.refs_0_.refs_2_.ka.va), channel_id=1, source_target_pairs={{0,8},{8,0},{16,24},{24,16},{1,9},{9,1},{17,25},{25,17},{2,10},{10... | collective-permute-start | bytes 1769480 | tf_op jit(solution)/shard_map/ppermute | solution.py:493
  34.1 120.5 %all-gather.7.cloned.1.call-start = ((), (), s32[]{:S(2)}) async-start(), calls=%async_computation.3 | async-start | bytes 2211840 | tf_op jit(solution)/shard_map/all_gather | solution.py:598
  34.4 13.1 %collective-permute-start.3 = (bf16[1,128,768]{2,1,0:T(8,128)(2,1)}, bf16[1,128,768]{2,1,0:T(8,128)(2,1)S(1)}, u32[]{:S(2)}, u32[]{:S(2)}) collective-permute-start(bf16[1,128,768]{2,1,0:T(8,128)(2,1)} %bitcast.20), channel_id=1, source_target_pairs={{0,2},{2,0},{4,6},{6,4},{1,3},{3,1},{5,7},{7,5},{8,10},{10,8},{12,... | collective-permute-start | bytes 589832 | tf_op jit(solution)/shard_map/ppermute | solution.py:500
  35.7 11.9 %collective-permute-start.4 = (bf16[1,128,768]{2,1,0:T(8,128)(2,1)}, bf16[1,128,768]{2,1,0:T(8,128)(2,1)S(1)}, u32[]{:S(2)}, u32[]{:S(2)}) collective-permute-start(bf16[1,128,768]{2,1,0:T(8,128)(2,1)} %bitcast.20), channel_id=1, source_target_pairs={{0,4},{2,6},{4,0},{6,2},{1,5},{3,7},{5,1},{7,3},{8,12},{10,14},{12... | collective-permute-start | bytes 589832 | tf_op jit(solution)/shard_map/ppermute | solution.py:500
  36.9 10.6 %collective-permute-start.5 = (bf16[1,128,768]{2,1,0:T(8,128)(2,1)}, bf16[1,128,768]{2,1,0:T(8,128)(2,1)S(1)}, u32[]{:S(2)}, u32[]{:S(2)}) collective-permute-start(bf16[1,128,768]{2,1,0:T(8,128)(2,1)} %bitcast.20), channel_id=1, source_target_pairs={{0,6},{2,4},{4,2},{6,0},{1,7},{3,5},{5,3},{7,1},{8,14},{10,12},{12... | collective-permute-start | bytes 589832 | tf_op jit(solution)/shard_map/ppermute | solution.py:500
  46.4 6.3 %collective-permute-start.9 = (bf16[576,512]{1,0:T(8,128)(2,1)}, bf16[576,512]{1,0:T(8,128)(2,1)S(1)}, u32[]{:S(2)}, u32[]{:S(2)}) collective-permute-start(bf16[576,512]{1,0:T(8,128)(2,1)} %collective-permute-done.8.refs_0_.refs_2_.ka.va), channel_id=1, source_target_pairs={{0,1},{1,0},{2,3},{3,2},{4,5},{5,4},{6,7},{7,6},{8,9},{9,8},{10,11... | collective-permute-start | bytes 1769480 | tf_op jit(solution)/shard_map/ppermute | solution.py:490
  49.6 10.6 %collective-permute-start.7 = (bf16[576,512]{1,0:T(8,128)(2,1)S(1)}, bf16[576,512]{1,0:T(8,128)(2,1)S(1)}, u32[]{:S(2)}, u32[]{:S(2)}) collective-permute-start(bf16[576,512]{1,0:T(8,128)(2,1)S(1)} %bitcast.118), channel_id=1, source_target_pairs={{0,1},{1,0},{2,3},{3,2},{4,5},{5,4},{6,7},{7,6},{8,9},{9,8},{10,11... | collective-permute-start | bytes 1769480 | tf_op jit(solution)/shard_map/ppermute | solution.py:490
  50.7 17.1 %collective-permute-start.6 = (bf16[576,512]{1,0:T(8,128)(2,1)S(1)}, bf16[576,512]{1,0:T(8,128)(2,1)}, u32[]{:S(2)}, u32[]{:S(2)}) collective-permute-start(bf16[576,512]{1,0:T(8,128)(2,1)S(1)} %bitcast.119), channel_id=1, source_target_pairs={{0,8},{8,0},{16,24},{24,16},{1,9},{9,1},{17,25},{25,17},{2,10},{10... | collective-permute-start | bytes 1769480 | tf_op jit(solution)/shard_map/ppermute | solution.py:493
  88.7 10.8 %collective-permute-start.13 = (bf16[192,1024]{1,0:T(8,128)(2,1)S(1)}, bf16[192,1024]{1,0:T(8,128)(2,1)}, u32[]{:S(2)}, u32[]{:S(2)}) collective-permute-start(bf16[192,1024]{1,0:T(8,128)(2,1)S(1)} %add_convert_fusion.6), channel_id=1, source_target_pairs={{0,8},{8,0},{16,24},{24,16},{1,9},{9,1},{17,25},{25,17},{2,10},{10... | collective-permute-start | bytes 1179656 | tf_op jit(solution)/shard_map/ppermute | solution.py:493
  99.5 11.0 %collective-permute-start.17 = (bf16[4,864,768]{2,1,0:T(8,128)(2,1)}, bf16[4,864,768]{2,1,0:T(8,128)(2,1)}, u32[]{:S(2)}, u32[]{:S(2)}) collective-permute-start(bf16[4,864,768]{2,1,0:T(8,128)(2,1)} %bitcast.169), channel_id=1, source_target_pairs={{0,1},{1,0},{2,3},{3,2},{4,5},{5,4},{6,7},{7,6},{8,9},{9,8},{10,11... | collective-permute-start | bytes 15925256 | tf_op jit(solution)/shard_map/ppermute | solution.py:490
  110.2 116.5 %reduce-scatter.4.cloned.1.call-start = ((), (), s32[]{:S(2)}) async-start(), calls=%async_computation.4 | async-start | bytes 6881280
  129.1 7.0 %collective-permute-start.18 = (bf16[192,256]{1,0:T(8,128)(2,1)}, bf16[192,256]{1,0:T(8,128)(2,1)S(1)}, u32[]{:S(2)}, u32[]{:S(2)}) collective-permute-start(bf16[192,256]{1,0:T(8,128)(2,1)} %get-tuple-element.117), channel_id=1, source_target_pairs={{0,2},{2,0},{4,6},{6,4},{1,3},{3,1},{5,7},{7,5},{8,10},{10,8},{12,... | collective-permute-start | bytes 294920 | tf_op jit(solution)/shard_map/ppermute | solution.py:500
  130.6 7.7 %collective-permute-start.19 = (bf16[192,256]{1,0:T(8,128)(2,1)}, bf16[192,256]{1,0:T(8,128)(2,1)S(1)}, u32[]{:S(2)}, u32[]{:S(2)}) collective-permute-start(bf16[192,256]{1,0:T(8,128)(2,1)} %get-tuple-element.118), channel_id=1, source_target_pairs={{0,4},{2,6},{4,0},{6,2},{1,5},{3,7},{5,1},{7,3},{8,12},{10,14},{12... | collective-permute-start | bytes 294920 | tf_op jit(solution)/shard_map/ppermute | solution.py:500
  130.8 9.5 %collective-permute-start.20 = (bf16[192,256]{1,0:T(8,128)(2,1)}, bf16[192,256]{1,0:T(8,128)(2,1)S(1)}, u32[]{:S(2)}, u32[]{:S(2)}) collective-permute-start(bf16[192,256]{1,0:T(8,128)(2,1)} %get-tuple-element.119), channel_id=1, source_target_pairs={{0,6},{2,4},{4,2},{6,0},{1,7},{3,5},{5,3},{7,1},{8,14},{10,12},{12... | collective-permute-start | bytes 294920 | tf_op jit(solution)/shard_map/ppermute | solution.py:500
  132.7 11.6 %collective-permute-start.21 = (bf16[8,256,384]{2,1,0:T(8,128)(2,1)}, bf16[8,256,384]{2,1,0:T(8,128)(2,1)S(1)}, u32[]{:S(2)}, u32[]{:S(2)}) collective-permute-start(bf16[8,256,384]{2,1,0:T(8,128)(2,1)} %get-tuple-element.125), channel_id=1, source_target_pairs={{0,1},{1,0},{2,3},{3,2},{4,5},{5,4},{6,7},{7,6},{8,9},{9,8},{10,11... | collective-permute-start | bytes 4718600 | tf_op jit(solution)/shard_map/ppermute | solution.py:490
  134.3 10.0 %collective-permute-start.22 = (bf16[6,256,384]{2,1,0:T(8,128)(2,1)}, bf16[6,256,384]{2,1,0:T(8,128)(2,1)S(1)}, u32[]{:S(2)}, u32[]{:S(2)}) collective-permute-start(bf16[6,256,384]{2,1,0:T(8,128)(2,1)} %get-tuple-element.127), channel_id=1, source_target_pairs={{0,1},{1,0},{2,3},{3,2},{4,5},{5,4},{6,7},{7,6},{8,9},{9,8},{10,11... | collective-permute-start | bytes 3538952 | tf_op jit(solution)/shard_map/ppermute | solution.py:490
  136.1 7.2 %collective-permute-start.23 = (bf16[4,96,256]{2,1,0:T(8,128)(2,1)}, bf16[4,96,256]{2,1,0:T(8,128)(2,1)S(1)}, u32[]{:S(2)}, u32[]{:S(2)}) collective-permute-start(bf16[4,96,256]{2,1,0:T(8,128)(2,1)} %get-tuple-element.128), channel_id=1, source_target_pairs={{0,1},{1,0},{2,3},{3,2},{4,5},{5,4},{6,7},{7,6},{8,9},{9,8},{10,11... | collective-permute-start | bytes 589832 | tf_op jit(solution)/shard_map/ppermute | solution.py:490
  138.3 15.8 %collective-permute-start.24 = (bf16[128,768]{1,0:T(8,128)(2,1)}, bf16[128,768]{1,0:T(8,128)(2,1)}, u32[]{:S(2)}, u32[]{:S(2)}) collective-permute-start(bf16[128,768]{1,0:T(8,128)(2,1)} %get-tuple-element.229), channel_id=1, source_target_pairs={{0,16},{8,24},{16,0},{24,8},{1,17},{9,25},{17,1},{25,9},{2,18},{10... | collective-permute-start | bytes 589832 | tf_op jit(solution)/shard_map/ppermute | solution.py:497
  141.3 12.8 %collective-permute-start.25 = (bf16[192,1024]{1,0:T(8,128)(2,1)S(1)}, bf16[192,1024]{1,0:T(8,128)(2,1)S(1)}, u32[]{:S(2)}, u32[]{:S(2)}) collective-permute-start(bf16[192,1024]{1,0:T(8,128)(2,1)S(1)} %slice_dynamic-update-slice_fusion.refs_4_), channel_id=1, source_target_pairs={{0,1},{1,0},{2,3},{3,2},{4,5},{5,4},{6,7},{7,6},{8,9},{9,8},{10,11... | collective-permute-start | bytes 1179656 | tf_op jit(solution)/shard_map/ppermute | solution.py:490
  143.4 32.2 %collective-permute-start.26 = (bf16[192,1024]{1,0:T(8,128)(2,1)S(1)}, bf16[192,1024]{1,0:T(8,128)(2,1)S(1)}, u32[]{:S(2)}, u32[]{:S(2)}) collective-permute-start(bf16[192,1024]{1,0:T(8,128)(2,1)S(1)} %slice_dynamic-update-slice_fusion.refs_4_), channel_id=1, source_target_pairs={{0,8},{8,0},{16,24},{24,16},{1,9},{9,1},{17,25},{25,17},{2,10},{10... | collective-permute-start | bytes 1179656 | tf_op jit(solution)/shard_map/ppermute | solution.py:493
  154.1 163.6 %all-reduce.3.cloned.1.call-start = ((), (), s32[]{:S(2)}) async-start(), calls=%async_computation.1 | async-start | bytes 2752512 | tf_op jit(solution)/shard_map/psum | solution.py:673
  175.5 16.0 %collective-permute-start.28 = (bf16[192,1024]{1,0:T(8,128)(2,1)S(1)}, bf16[192,1024]{1,0:T(8,128)(2,1)S(1)}, u32[]{:S(2)}, u32[]{:S(2)}) collective-permute-start(bf16[192,1024]{1,0:T(8,128)(2,1)S(1)} %collective-permute-done.26.refs_2_), channel_id=1, source_target_pairs={{0,1},{1,0},{2,3},{3,2},{4,5},{5,4},{6,7},{7,6},{8,9},{9,8},{10,11... | collective-permute-start | bytes 1179656 | tf_op jit(solution)/shard_map/ppermute | solution.py:490
  175.9 15.7 %collective-permute-start.27 = (bf16[192,1024]{1,0:T(8,128)(2,1)S(1)}, bf16[192,1024]{1,0:T(8,128)(2,1)S(1)}, u32[]{:S(2)}, u32[]{:S(2)}) collective-permute-start(bf16[192,1024]{1,0:T(8,128)(2,1)S(1)} %get-tuple-element.140), channel_id=1, source_target_pairs={{0,1},{1,0},{2,3},{3,2},{4,5},{5,4},{6,7},{7,6},{8,9},{9,8},{10,11... | collective-permute-start | bytes 1179656 | tf_op jit(solution)/shard_map/ppermute | solution.py:490
  188.8 34.7 %collective-permute-start.33 = (bf16[2,128,768]{2,1,0:T(8,128)(2,1)S(1)}, bf16[2,128,768]{2,1,0:T(8,128)(2,1)S(1)}, u32[]{:S(2)}, u32[]{:S(2)}) collective-permute-start(bf16[2,128,768]{2,1,0:T(8,128)(2,1)S(1)} %pad_maximum_fusion.10), channel_id=1, source_target_pairs={{0,4},{2,6},{4,0},{6,2},{1,5},{3,7},{5,1},{7,3},{8,12},{10,14},{12... | collective-permute-start | bytes 1179656 | tf_op jit(solution)/shard_map/ppermute | solution.py:500
  189.8 34.6 %collective-permute-start.32 = (bf16[2,128,768]{2,1,0:T(8,128)(2,1)S(1)}, bf16[2,128,768]{2,1,0:T(8,128)(2,1)S(1)}, u32[]{:S(2)}, u32[]{:S(2)}) collective-permute-start(bf16[2,128,768]{2,1,0:T(8,128)(2,1)S(1)} %pad_maximum_fusion.10), channel_id=1, source_target_pairs={{0,2},{2,0},{4,6},{6,4},{1,3},{3,1},{5,7},{7,5},{8,10},{10,8},{12,... | collective-permute-start | bytes 1179656 | tf_op jit(solution)/shard_map/ppermute | solution.py:500
  191.0 33.4 %collective-permute-start.34 = (bf16[2,128,768]{2,1,0:T(8,128)(2,1)S(1)}, bf16[2,128,768]{2,1,0:T(8,128)(2,1)S(1)}, u32[]{:S(2)}, u32[]{:S(2)}) collective-permute-start(bf16[2,128,768]{2,1,0:T(8,128)(2,1)S(1)} %pad_maximum_fusion.10), channel_id=1, source_target_pairs={{0,6},{2,4},{4,2},{6,0},{1,7},{3,5},{5,3},{7,1},{8,14},{10,12},{12... | collective-permute-start | bytes 1179656 | tf_op jit(solution)/shard_map/ppermute | solution.py:500
  203.0 10.1 %collective-permute-start.29 = (bf16[192,1024]{1,0:T(8,128)(2,1)S(1)}, bf16[192,1024]{1,0:T(8,128)(2,1)S(1)}, u32[]{:S(2)}, u32[]{:S(2)}) collective-permute-start(bf16[192,1024]{1,0:T(8,128)(2,1)S(1)} %get-tuple-element.145), channel_id=1, source_target_pairs={{0,1},{1,0},{2,3},{3,2},{4,5},{5,4},{6,7},{7,6},{8,9},{9,8},{10,11... | collective-permute-start | bytes 1179656 | tf_op jit(solution)/shard_map/ppermute | solution.py:490
  213.0 11.5 %collective-permute-start.31 = (bf16[2,192,1024]{2,1,0:T(8,128)(2,1)S(1)}, bf16[2,192,1024]{2,1,0:T(8,128)(2,1)S(1)}, u32[]{:S(2)}, u32[]{:S(2)}) collective-permute-start(bf16[2,192,1024]{2,1,0:T(8,128)(2,1)S(1)} %key_backward.4), channel_id=1, source_target_pairs={{0,1},{1,0},{2,3},{3,2},{4,5},{5,4},{6,7},{7,6},{8,9},{9,8},{10,11... | collective-permute-start | bytes 2359304 | tf_op jit(solution)/shard_map/ppermute | solution.py:490
  213.2 11.3 %collective-permute-start.30 = (bf16[192,1024]{1,0:T(8,128)(2,1)S(1)}, bf16[192,1024]{1,0:T(8,128)(2,1)S(1)}, u32[]{:S(2)}, u32[]{:S(2)}) collective-permute-start(bf16[192,1024]{1,0:T(8,128)(2,1)S(1)} %add_convert_fusion.4), channel_id=1, source_target_pairs={{0,8},{8,0},{16,24},{24,16},{1,9},{9,1},{17,25},{25,17},{2,10},{10... | collective-permute-start | bytes 1179656 | tf_op jit(solution)/shard_map/ppermute | solution.py:493
  223.6 25.9 %collective-permute-start.40 = (bf16[4,3,96,768]{3,2,1,0:T(8,128)(2,1)}, bf16[4,3,96,768]{3,2,1,0:T(8,128)(2,1)}, u32[]{:S(2)}, u32[]{:S(2)}) collective-permute-start(bf16[4,3,96,768]{3,2,1,0:T(8,128)(2,1)} %bitcast.35.refs_4_), channel_id=1, source_target_pairs={{0,1},{1,0},{2,3},{3,2},{4,5},{5,4},{6,7},{7,6},{8,9},{9,8},{10,11... | collective-permute-start | bytes 5308424 | tf_op jit(solution)/shard_map/ppermute | solution.py:490
  225.6 23.8 %collective-permute-start.36 = (bf16[2,192,1024]{2,1,0:T(8,128)(2,1)}, bf16[2,192,1024]{2,1,0:T(8,128)(2,1)}, u32[]{:S(2)}, u32[]{:S(2)}) collective-permute-start(bf16[2,192,1024]{2,1,0:T(8,128)(2,1)} %add_convert_fusion.1), channel_id=1, source_target_pairs={{0,8},{8,0},{16,24},{24,16},{1,9},{9,1},{17,25},{25,17},{2,10},{10... | collective-permute-start | bytes 2359304 | tf_op jit(solution)/shard_map/ppermute | solution.py:493
  237.7 11.8 %collective-permute-start.35 = (bf16[2,192,1024]{2,1,0:T(8,128)(2,1)S(1)}, bf16[2,192,1024]{2,1,0:T(8,128)(2,1)}, u32[]{:S(2)}, u32[]{:S(2)}) collective-permute-start(bf16[2,192,1024]{2,1,0:T(8,128)(2,1)S(1)} %key_backward.6), channel_id=1, source_target_pairs={{0,1},{1,0},{2,3},{3,2},{4,5},{5,4},{6,7},{7,6},{8,9},{9,8},{10,11... | collective-permute-start | bytes 2359304 | tf_op jit(solution)/shard_map/ppermute | solution.py:490
  251.6 9.5 %collective-permute-start.39 = (bf16[3,192,256]{2,1,0:T(8,128)(2,1)S(1)}, bf16[3,192,256]{2,1,0:T(8,128)(2,1)S(1)}, u32[]{:S(2)}, u32[]{:S(2)}) collective-permute-start(bf16[3,192,256]{2,1,0:T(8,128)(2,1)S(1)} %pad_maximum_fusion.15), channel_id=1, source_target_pairs={{0,6},{2,4},{4,2},{6,0},{1,7},{3,5},{5,3},{7,1},{8,14},{10,12},{12... | collective-permute-start | bytes 884744 | tf_op jit(solution)/shard_map/ppermute | solution.py:500
  253.5 14.4 %collective-permute-start.38 = (bf16[3,192,256]{2,1,0:T(8,128)(2,1)S(1)}, bf16[3,192,256]{2,1,0:T(8,128)(2,1)S(1)}, u32[]{:S(2)}, u32[]{:S(2)}) collective-permute-start(bf16[3,192,256]{2,1,0:T(8,128)(2,1)S(1)} %pad_maximum_fusion.14), channel_id=1, source_target_pairs={{0,4},{2,6},{4,0},{6,2},{1,5},{3,7},{5,1},{7,3},{8,12},{10,14},{12... | collective-permute-start | bytes 884744 | tf_op jit(solution)/shard_map/ppermute | solution.py:500
  253.6 14.3 %collective-permute-start.37 = (bf16[3,192,256]{2,1,0:T(8,128)(2,1)S(1)}, bf16[3,192,256]{2,1,0:T(8,128)(2,1)S(1)}, u32[]{:S(2)}, u32[]{:S(2)}) collective-permute-start(bf16[3,192,256]{2,1,0:T(8,128)(2,1)S(1)} %pad_maximum_fusion.13), channel_id=1, source_target_pairs={{0,2},{2,0},{4,6},{6,4},{1,3},{3,1},{5,7},{7,5},{8,10},{10,8},{12,... | collective-permute-start | bytes 884744 | tf_op jit(solution)/shard_map/ppermute | solution.py:500
  255.7 21.1 %collective-permute-start.42 = (bf16[288,768]{1,0:T(8,128)(2,1)S(1)}, bf16[288,768]{1,0:T(8,128)(2,1)S(1)}, u32[]{:S(2)}, u32[]{:S(2)}) collective-permute-start(bf16[288,768]{1,0:T(8,128)(2,1)S(1)} %constant_dynamic-slice_fusion.1), channel_id=1, source_target_pairs={{0,1},{1,0},{2,3},{3,2},{4,5},{5,4},{6,7},{7,6},{8,9},{9,8},{10,11... | collective-permute-start | bytes 1327112 | tf_op jit(solution)/shard_map/ppermute | solution.py:490
  274.9 20.8 %collective-permute-start.41 = (bf16[128,768]{1,0:T(8,128)(2,1)S(1)}, bf16[128,768]{1,0:T(8,128)(2,1)S(1)}, u32[]{:S(2)}, u32[]{:S(2)}) collective-permute-start(bf16[128,768]{1,0:T(8,128)(2,1)S(1)} %get-tuple-element.227), channel_id=1, source_target_pairs={{0,16},{8,24},{16,0},{24,8},{1,17},{9,25},{17,1},{25,9},{2,18},{10... | collective-permute-start | bytes 589832 | tf_op jit(solution)/shard_map/ppermute | solution.py:497
  277.0 22.4 %collective-permute-start.43 = (bf16[144,768]{1,0:T(8,128)(2,1)S(1)}, bf16[144,768]{1,0:T(8,128)(2,1)S(1)}, u32[]{:S(2)}, u32[]{:S(2)}) collective-permute-start(bf16[144,768]{1,0:T(8,128)(2,1)S(1)} %constant_dynamic-slice_fusion), channel_id=1, source_target_pairs={{0,8},{8,0},{16,24},{24,16},{1,9},{9,1},{17,25},{25,17},{2,10},{10... | collective-permute-start | bytes 663560 | tf_op jit(solution)/shard_map/ppermute | solution.py:493
  299.5 18.3 %collective-permute-start.44 = (bf16[2,128,768]{2,1,0:T(8,128)(2,1)S(1)}, bf16[2,128,768]{2,1,0:T(8,128)(2,1)}, u32[]{:S(2)}, u32[]{:S(2)}) collective-permute-start(bf16[2,128,768]{2,1,0:T(8,128)(2,1)S(1)} %pad_maximum_fusion.11), channel_id=1, source_target_pairs={{0,2},{2,0},{4,6},{6,4},{1,3},{3,1},{5,7},{7,5},{8,10},{10,8},{12,... | collective-permute-start | bytes 1179656 | tf_op jit(solution)/shard_map/ppermute | solution.py:500
  300.5 17.3 %collective-permute-start.45 = (bf16[2,128,768]{2,1,0:T(8,128)(2,1)S(1)}, bf16[2,128,768]{2,1,0:T(8,128)(2,1)}, u32[]{:S(2)}, u32[]{:S(2)}) collective-permute-start(bf16[2,128,768]{2,1,0:T(8,128)(2,1)S(1)} %pad_maximum_fusion.11), channel_id=1, source_target_pairs={{0,4},{2,6},{4,0},{6,2},{1,5},{3,7},{5,1},{7,3},{8,12},{10,14},{12... | collective-permute-start | bytes 1179656 | tf_op jit(solution)/shard_map/ppermute | solution.py:500
  300.5 17.3 %collective-permute-start.46 = (bf16[2,128,768]{2,1,0:T(8,128)(2,1)S(1)}, bf16[2,128,768]{2,1,0:T(8,128)(2,1)}, u32[]{:S(2)}, u32[]{:S(2)}) collective-permute-start(bf16[2,128,768]{2,1,0:T(8,128)(2,1)S(1)} %pad_maximum_fusion.11), channel_id=1, source_target_pairs={{0,6},{2,4},{4,2},{6,0},{1,7},{3,5},{5,3},{7,1},{8,14},{10,12},{12... | collective-permute-start | bytes 1179656 | tf_op jit(solution)/shard_map/ppermute | solution.py:500
  302.2 15.4 %collective-permute-start.47 = (bf16[144,768]{1,0:T(8,128)(2,1)S(1)}, bf16[144,768]{1,0:T(8,128)(2,1)S(1)}, u32[]{:S(2)}, u32[]{:S(2)}) collective-permute-start(bf16[144,768]{1,0:T(8,128)(2,1)S(1)} %fusion.6), channel_id=1, source_target_pairs={{0,16},{8,24},{16,0},{24,8},{1,17},{9,25},{17,1},{25,9},{2,18},{10... | collective-permute-start | bytes 663560 | tf_op jit(solution)/shard_map/ppermute | solution.py:497
  317.7 6.6 %collective-permute-start.48 = (bf16[144,768]{1,0:T(8,128)(2,1)S(1)}, bf16[144,768]{1,0:T(8,128)(2,1)}, u32[]{:S(2)}, u32[]{:S(2)}) collective-permute-start(bf16[144,768]{1,0:T(8,128)(2,1)S(1)} %add_convert_fusion.7), channel_id=1, source_target_pairs={{0,8},{8,0},{16,24},{24,16},{1,9},{9,1},{17,25},{25,17},{2,10},{10... | collective-permute-start | bytes 663560 | tf_op jit(solution)/shard_map/ppermute | solution.py:493
  317.8 15.0 %collective-permute-start.50 = (bf16[896,768]{1,0:T(8,128)(2,1)}, bf16[896,768]{1,0:T(8,128)(2,1)S(1)}, u32[]{:S(2)}, u32[]{:S(2)}) collective-permute-start(bf16[896,768]{1,0:T(8,128)(2,1)} %all-reduce.3.cloned.1.call-done.near), channel_id=1, source_target_pairs={{0,1},{1,0},{2,3},{3,2},{4,5},{5,4},{6,7},{7,6},{8,9},{9,8},{10,11... | collective-permute-start | bytes 4128776 | tf_op jit(solution)/shard_map/ppermute | solution.py:490
  (52 other events, 285.2 us)
Sparse Core Ops, SparseCore 0:
  34.2 62.7 all-gather.4
  110.3 37.1 all-gather.6
  154.2 71.4 reduce-scatter.3
  238.2 74.7 all-reduce.2

commit v21 on v20

--- a/solution.py
+++ b/solution.py
@@ -88,13 +88,16 @@
 
 
 def query_kernel(planes, tables, *refs, chunk):
-    rows, out = both(*refs[:-1]), refs[-1]
+    blocks = len(refs) // 3
+    rows, outs = both(*refs[: 2 * blocks]), refs[2 * blocks :]
     _, upper, lower = sides(rows, planes[...])
     low, high = half_codes(upper, lower)
     acc = jnp.zeros((HEAD_DIM, rows.shape[1]), f32)
     for c in range(0, 16, chunk):
         acc += dot(tables[0, 128 * c : 128 * (c + chunk), :], code_chunk(low, high, c, chunk), TN)
-    out[...] = (acc * (1.0 / HASHES)).astype(out.dtype)
+    width = outs[0].shape[1]
+    for i, out in enumerate(outs):
+        out[...] = (acc[:, i * width : (i + 1) * width] * (1.0 / HASHES)).astype(out.dtype)
 
 
 def query_back_kernel(planes, planes_t, bits, tables, *refs, chunk, blocks, last):
@@ -200,17 +203,18 @@
     )(*args)
 
 
-def query_estimates(planes, heads, near, far, tables, kind):
-    width = near.shape[1] + far.shape[1]
+def query_estimates(planes, heads, blocks, tables, kinds):
+    width = blocks[0][0].shape[1] + blocks[0][1].shape[1]
+    arrays = [x for pair in blocks for x in pair]
     return call(
         partial(query_kernel, chunk=2),
         heads,
-        1,
+        1 if len(blocks) == 1 else 20,
         "query_estimates",
-        [whole(64, 64), table_spec(), head_rows(near, heads, 0), head_rows(far, heads, 0)],
-        per_head(width),
-        shape((heads * HEAD_DIM, width), kind),
-    )(planes, tables, near, far)
+        [whole(64, 64), table_spec()] + [head_rows(x, heads, 0) for x in arrays],
+        [per_head(width)] * len(blocks),
+        [shape((heads * HEAD_DIM, width), kind) for kind in kinds],
+    )(planes, tables, *arrays)
 
 
 def query_backward(planes, planes_t, bits, heads, tables, queries, grads, start, last, kinds):
@@ -582,16 +586,14 @@
     far_zo = after(far_zo, tables)
     tables = key_tables(signed, head_n, [far_zo], tables, bf16)
 
-    e_zo = query_estimates(signed, head_n, near_zo, far_zo, tables, bf16)
+    e_zo = query_estimates(signed, head_n, [(near_zo, far_zo)], tables, [bf16])[0]
     e_zo_moved = over_seq(e_zo)
-    e_z = query_estimates(signed, head_n, near_z, after(far_z, e_zo), tables, bf16)
+    e_z = query_estimates(signed, head_n, [(near_z, after(far_z, e_zo))], tables, [bf16])[0]
     e_far = add(e_z, after(e_zo_moved, e_z)).astype(bf16)
     ready = after(far_o, e_far)
-    e_o = query_estimates(signed, head_n, near_o, ready, tables, bf16)
-    e_far = over_place(e_far)
-    e_o_moved = over_seq(e_o)
-    e = query_estimates(signed, head_n, near, after(far, e_o), tables, f32)
-    e_far = after(e_far, e)
+    e, e_o = query_estimates(signed, head_n, [(near, far), (near_o, ready)], tables, [f32, bf16])
+    e_far = after(over_place(e_far), e)
+    e_o_moved = over_seq(after(e_o, e_far))
     e_o_moved = after(e_o_moved, e)
     weights = after(weights, e_far, e_o_moved)
     weights = [weights, over_seq(weights)]

time: 352 us -> 349 us (level)
    pallas_call x4 -> x3, Pallas kernels: 15.9 us -> 14.2 us  [query_estimates(): call(partial(query_kernel, chunk=2), heads, 1 if len(blocks) == 1 else 20...]
    unnamed x102 -> x104, local copies, waits for them, and re-layouts: 20.9 us -> 21 us
  transfers between devices with their start and end apart: 55 -> 55, of which waited for: 12 -> 13; matrix products, arithmetic and copies ran while one was open for 14% -> 14% of each run, Pallas kernels for 44% -> 44%
where the time goes in v21:
time: 349 us; the launch traced here: 344 us
  Pallas kernels  156 us (45%)
  waiting for transfers between devices  57.5 us (16%)
  starting transfers between devices  50.6 us (14%)
  local copies, waits for them, and re-layouts  37.7 us (11%)
  other arithmetic  23.7 us (7%)
  between operations  15.1 us (4%)
  matrix products  3.91 us (1%)
    pallas_call x3, Pallas kernels, query_backward(): call(partial(query_back_kernel, chunk=4 * blocks, blocks=blocks, last=las...  43.3 us
    pallas_call x4, Pallas kernels, key_backward(): call(partial(key_back_kernel, chunk=4), heads, micros, 'key_backward', [w...  38.1 us
    pallas_call x4, Pallas kernels, single(): pl.pallas_call(kernel, in_specs=[pl.BlockSpec(memory_space=pltpu.SMEM)] +...  36.4 us
    ppermute x4, waiting for transfers between devices, over_group(): return lax.ppermute(x, 'hash', moves)  30 us
    pallas_call x5, Pallas kernels, key_tables(): call(partial(key_kernel, chunk=2, blocks=len(blocks)), heads, 30 if len(b...  23.7 us
    unnamed x104, local copies, waits for them, and re-layouts  21 us
    ppermute x20, starting transfers between devices, over_seq(): return lax.ppermute(x, 'seq', [(0, 1), (1, 0)])  16.5 us
    ppermute x18, starting transfers between devices, over_head(): return lax.ppermute(x, 'head', [(h, h ^ j) for h in range(head_count)])  16.5 us
  transfers between devices with their start and end apart: 55, of which 13 were waited for; matrix products, arithmetic and copies ran while one was open for 14% of the time, Pallas kernels for 44%

profile of v21, /device:TPU:1, one launch (start us, length us, event | category | flops | bytes accessed | tf_op | source)
XLA Modules:
  0.0 344.3 jit_solution(16754570414246102713)
XLA Ops:
  7.3 4.5 %constant_dynamic-slice_fusion.7 = (bf16[1,128,1,768]{3,2,1,0:T(2,128)(2,1)S(1)}, bf16[1,128,1,768]{3,2,1,0:T(2,128)(2,1)}, bf16[1,128,1,768]{3,2,1,0:T(2,128)(2...) fusion(bf16[1,512,2,768]{3,2,1,0:T(2,128)(2,1)} %param.11, s32[]{:T(128)S(6)} %select_n.222, ...), kind=kLoop, calls=%fused_computation.119 | loop fusion | bytes 1966104 | tf_op jit(solution)/shard_map/jit(dynamic_index_in_dim)/dynamic_slice | solution.py:507
  12.6 3.1 collective-permute-start
  16.3 2.5 collective-permute-start.1
  20.5 2.4 copy.53
  22.9 2.0 dynamic-slice_bitcast_fusion
  24.9 1.9 constant_dynamic-slice_fusion.3
  31.2 1.7 collective-permute-start.8
  37.1 1.7 pad_maximum_fusion.9.x_in
  38.8 5.2 %key_tables.5.refs_4_ = f32[3,2048,64]{2,1,0:T(8,128)S(1)} custom-call(bf16[64,64]{1,0:T(8,128)(2,1)S(1)} %bitcast.126, bf16[576,512]{1,0:T(8,128)(2,1)} %bitcast.14.refs_0_.refs_2_.ka.va, bf16[576,512]{1,0:T(8,128)(2,1)} %collective-permute-done.2.refs_1_.refs_3_.refs_2_.ka.va, bf16[576,512]{1,0:T(8,128)(2,1)} %bitcast.14.refs_0_.refs_2_.ka.va, ...), custom_call_target="tpu_custom_call" | custom-call | flops 1100000000 | bytes 1048576 | tf_op jit(solution)/shard_map/key_tables/pallas_call | solution.py:195
  44.1 2.3 collective-permute-done.8.refs_0_.refs_2_.ka.va
  52.7 5.8 %key_tables.6.refs_4_ = f32[3,2048,64]{2,1,0:T(8,128)S(1)} custom-call(bf16[64,64]{1,0:T(8,128)(2,1)S(1)} %bitcast.127, bf16[576,512]{1,0:T(8,128)(2,1)} %collective-permute-done.8.refs_0_.refs_2_.ka.va, bf16[576,512]{1,0:T(8,128)(2,1)S(1)} %collective-permute-done.9.refs_1_.refs_3_.refs_0_.ka.va, ...), custom_call_target="tpu_custom_call" | custom-call | flops 32999999488 | bytes 1048576 | tf_op jit(solution)/shard_map/key_tables/pallas_call | solution.py:195
  58.5 1.7 copy-done.15
  60.2 5.7 %key_tables.7.refs_2_ = f32[3,2048,64]{2,1,0:T(8,128)S(1)} custom-call(bf16[64,64]{1,0:T(8,128)(2,1)S(1)} %bitcast.128, bf16[576,512]{1,0:T(8,128)(2,1)S(1)} %bitcast.120, bf16[576,512]{1,0:T(8,128)(2,1)S(1)} %collective-permute-done.7.refs_1_.refs_3_.kb.vb, bf16[576,512]{1,0:T(8,128)(2,1)S(1)} %bitcast.121, ...), custom_call_target="tpu_custom_call" | custom-call | flops 32999999488 | bytes 1048576 | tf_op jit(solution)/shard_map/key_tables/pallas_call | solution.py:195
  65.9 1.9 copy-done.2
  69.1 4.4 %key_tables.8.refs_2_ = f32[3,2048,64]{2,1,0:T(8,128)S(1)} custom-call(bf16[64,64]{1,0:T(8,128)(2,1)S(1)} %bitcast.129, bf16[576,512]{1,0:T(8,128)(2,1)} %collective-permute-done.6.refs_0_.refs_1_.kb.vb, bf16[576,512]{1,0:T(8,128)(2,1)} %collective-permute-done.6.refs_0_.refs_1_.kb.vb, f32[3,2048,64]{2,1,0:T(8,128)} %copy-done.2), custom_call_target="tpu_custom_call" | custom-call | flops 1100000000 | bytes 1048576 | tf_op jit(solution)/shard_map/key_tables/pallas_call | solution.py:195
  73.5 2.6 key_tables.9.tables
  76.1 3.3 query_estimates.3
  79.6 4.3 %query_estimates.4 = bf16[192,1024]{1,0:T(8,128)(2,1)S(1)} custom-call(bf16[64,64]{1,0:T(8,128)(2,1)S(1)} %bitcast.132, bf16[3,2048,64]{2,1,0:T(8,128)(2,1)S(1)} %key_tables.9.tables, bf16[576,512]{1,0:T(8,128)(2,1)} %collective-permute-done.8.refs_0_.refs_2_.ka.va, bf16[576,512]{1,0:T(8,128)(2,1)} %collective-permute-done.6.refs_0_.refs_1_.kb.vb), custom_call_target="tpu_custom_call" | custom-call | flops 1100000000 | bytes 1048576 | tf_op jit(solution)/shard_map/query_estimates/pallas_call | solution.py:209
  84.9 6.6 %query_estimates.5 = (f32[192,1024]{1,0:T(8,128)S(1)}, bf16[192,1024]{1,0:T(8,128)(2,1)S(1)}) custom-call(bf16[64,64]{1,0:T(8,128)(2,1)S(1)} %bitcast.133, bf16[3,2048,64]{2,1,0:T(8,128)(2,1)S(1)} %key_tables.9.tables, bf16[576,512]{1,0:T(8,128)(2,1)} %bitcast.14.refs_0_.refs_2_.ka.va, bf16[576,512]{1,0:T(8,128)(2,1)S(1)} %bitcast.122, ...), custom_call_target="tpu_custom_call" | custom-call | flops 22000001024 | bytes 1048576 | tf_op jit(solution)/shard_map/query_estimates/pallas_call | solution.py:209
  91.6 2.9 collective-permute-done.12
  99.7 2.0 collective-permute-start.16
  103.2 1.9 collective-permute-done.16.refs_3_.refs_7_
  105.1 2.4 collective-permute-done.15.refs_2_.refs_6_
  108.2 18.3 %dense.1 = (bf16[256,768]{1,0:T(8,128)(2,1)}, f32[256,768]{1,0:T(8,128)}, bf16[8,256,384]{2,1,0:T(8,128)(2,1)}, bf16[8,256,384]{2,1,0:T(8,128)(2,1)}, bf16[6,256...) custom-call(s32[2]{0:T(128)} %pad_add_fusion.core, ...), custom_call_target="tpu_custom_call" | custom-call | flops 24199999488 | bytes 1048576 | tf_op jit(solution)/shard_map/dense/pallas_call | solution.py:394
  131.5 1.7 fusion.24
  134.6 2.9 collective-permute-start.24
  138.5 1.9 collective-permute-start.25
  143.4 8.2 %weight_grads.1 = bf16[4,896,768]{2,1,0:T(8,128)(2,1)} custom-call(s32[2]{0:T(128)} %pad_add_fusion.core, f32[16,768]{1,0:T(8,128)} %get-tuple-element.127.small, bf16[8,256,384]{2,1,0:T(8,128)(2,1)} %get-tuple-element.128.refs_0_, bf16[8,256,384]{2,1,0:T(8,128)(2,1)} %copy-done.37, bf16[6,256,384]{2,1,0:T(8,128)(2,1)} %get-tuple-element.130.refs_2_, ...), custom_call_target="tpu_custom_call" | custom-call | flops 7699999744 | bytes 1048576 | tf_op jit(solution)/shard_map/weight_grads/pallas_call | solution.py:394
  152.8 20.3 %query_backward.3 = (f32[3,2048,64]{2,1,0:T(8,128)}, f32[192,1024]{1,0:T(8,128)S(1)}, bf16[192,1024]{1,0:T(8,128)(2,1)S(1)}) custom-call(bf16[64,64]{1,0:T(8,128)(2,1)S(1)} %bitcast.135, bf16[64,128]{1,0:T(8,128)(2,1)S(1)} %pad_maximum_fusion.20.planes_t, bf16[80,2048]{1,0:T(8,128)(2,1)S(1)} %copy-done.14, bf16[3,2048,64]{2,1,0:T(8,128)(2,1)} %copy-done.4, ...), custom_call_target="tpu_custom_call" | custom-call | flops 54999998464 | bytes 1048576 | tf_op jit(solution)/shard_map/query_backward/pallas_call | solution.py:233
  173.6 11.8 %query_backward.4 = (f32[3,2048,64]{2,1,0:T(8,128)}, f32[192,1024]{1,0:T(8,128)S(1)}) custom-call(bf16[64,64]{1,0:T(8,128)(2,1)S(1)} %bitcast.136, bf16[64,128]{1,0:T(8,128)(2,1)S(1)} %pad_maximum_fusion.20.planes_t, bf16[80,2048]{1,0:T(8,128)(2,1)S(1)} %copy-done.14, bf16[3,2048,64]{2,1,0:T(8,128)(2,1)S(1)} %copy-done.5, ...), custom_call_target="tpu_custom_call" | custom-call | flops 27499999232 | bytes 1048576 | tf_op jit(solution)/shard_map/query_backward/pallas_call | solution.py:233
  189.3 11.2 %query_backward.5 = (bf16[3,2048,64]{2,1,0:T(8,128)(2,1)S(1)}, bf16[192,1024]{1,0:T(8,128)(2,1)S(1)}) custom-call(bf16[64,64]{1,0:T(8,128)(2,1)S(1)} %bitcast.137, bf16[64,128]{1,0:T(8,128)(2,1)S(1)} %pad_maximum_fusion.20.planes_t, bf16[80,2048]{1,0:T(8,128)(2,1)S(1)} %copy-done.14, bf16[3,2048,64]{2,1,0:T(8,128)(2,1)S(1)} %copy-done.5, ...), custom_call_target="tpu_custom_call" | custom-call | flops 27499999232 | bytes 1048576 | tf_op jit(solution)/shard_map/query_backward/pallas_call | solution.py:233
  201.7 8.8 %key_backward.4 = bf16[2,192,1024]{2,1,0:T(8,128)(2,1)S(1)} custom-call(bf16[64,64]{1,0:T(8,128)(2,1)S(1)} %bitcast.138, bf16[64,128]{1,0:T(8,128)(2,1)S(1)} %pad_maximum_fusion.20.planes_t, bf16[80,2048]{1,0:T(8,128)(2,1)S(1)} %copy-done.14, bf16[576,512]{1,0:T(8,128)(2,1)S(1)} %copy-done.13, ...), custom_call_target="tpu_custom_call" | custom-call | flops 27499999232 | bytes 1048576 | tf_op jit(solution)/shard_map/key_backward/pallas_call | solution.py:247
  210.8 9.8 %key_backward.5 = bf16[2,192,1024]{2,1,0:T(8,128)(2,1)S(1)} custom-call(bf16[64,64]{1,0:T(8,128)(2,1)S(1)} %bitcast.139, bf16[64,128]{1,0:T(8,128)(2,1)S(1)} %pad_maximum_fusion.20.planes_t, bf16[80,2048]{1,0:T(8,128)(2,1)S(1)} %copy-done.14, bf16[576,512]{1,0:T(8,128)(2,1)} %collective-permute-done.8.refs_0_.refs_2_.ka.va, ...), custom_call_target="tpu_custom_call" | custom-call | flops 27499999232 | bytes 1048576 | tf_op jit(solution)/shard_map/key_backward/pallas_call | solution.py:247
  225.6 9.7 %key_backward.6 = bf16[2,192,1024]{2,1,0:T(8,128)(2,1)S(1)} custom-call(bf16[64,64]{1,0:T(8,128)(2,1)S(1)} %bitcast.140, bf16[64,128]{1,0:T(8,128)(2,1)S(1)} %pad_maximum_fusion.20.planes_t, bf16[80,2048]{1,0:T(8,128)(2,1)S(1)} %copy-done.14, bf16[576,512]{1,0:T(8,128)(2,1)} %collective-permute-done.2.refs_1_.refs_3_.refs_2_.ka.va, ...), custom_call_target="tpu_custom_call" | custom-call | flops 27499999232 | bytes 1048576 | tf_op jit(solution)/shard_map/key_backward/pallas_call | solution.py:247
  237.1 9.9 %key_backward.7 = f32[2,192,1024]{2,1,0:T(8,128)S(1)} custom-call(bf16[64,64]{1,0:T(8,128)(2,1)S(1)} %bitcast.141, bf16[64,128]{1,0:T(8,128)(2,1)S(1)} %pad_maximum_fusion.20.planes_t, bf16[80,2048]{1,0:T(8,128)(2,1)S(1)} %copy-done.14, bf16[576,512]{1,0:T(8,128)(2,1)} %bitcast.14.refs_0_.refs_2_.ka.va, bf16[576,512]{1,0:T(8,128)(2,1)S(1)} %bitcast.124, ...), custom_call_target="tpu_custom_call" | custom-call | flops 27499999232 | bytes 1048576 | tf_op jit(solution)/shard_map/key_backward/pallas_call | solution.py:247
  247.0 1.7 add_convert_fusion
  255.1 3.6 %collective-permute-done.39.refs_3_ = bf16[3,192,256]{2,1,0:T(8,128)(2,1)S(1)} collective-permute-done((bf16[3,192,256]{2,1,0:T(8,128)(2,1)S(1)}, bf16[3,192,256]{2,1,0:T(8,128)(2,1)S(1)}, u32[]{:S(2)}, u32[]{:S(2)}) %collective-permute-start.39) | collective-permute-done | bytes 294944 | tf_op jit(solution)/shard_map/ppermute | solution.py:504
  258.7 6.7 %collective-permute-done.38.refs_2_ = bf16[3,192,256]{2,1,0:T(8,128)(2,1)S(1)} collective-permute-done((bf16[3,192,256]{2,1,0:T(8,128)(2,1)S(1)}, bf16[3,192,256]{2,1,0:T(8,128)(2,1)S(1)}, u32[]{:S(2)}, u32[]{:S(2)}) %collective-permute-start.38) | collective-permute-done | bytes 294944 | tf_op jit(solution)/shard_map/ppermute | solution.py:504
  266.2 5.2 %input_grad.1 = bf16[256,768]{1,0:T(8,128)(2,1)} custom-call(s32[2]{0:T(128)} %pad_add_fusion.core, f32[256,768]{1,0:T(8,128)} %get-tuple-element.154.grad_first, bf16[3,192,256]{2,1,0:T(8,128)(2,1)} %pad_maximum_fusion.12.refs_0_, bf16[3,192,256]{2,1,0:T(8,128)(2,1)} %copy-done.41, bf16[3,192,256]{2,1,0:T(8,128)(2,1)} %copy-done.40, ...), custom_call_target="tpu_custom_call" | custom-call | flops 44000002048 | bytes 1048576 | tf_op jit(solution)/shard_map/input_grad/pallas_call | solution.py:394
  274.6 18.5 %collective-permute-done.41 = bf16[128,768]{1,0:T(8,128)(2,1)S(1)} collective-permute-done((bf16[128,768]{1,0:T(8,128)(2,1)S(1)}, bf16[128,768]{1,0:T(8,128)(2,1)S(1)}, u32[]{:S(2)}, u32[]{:S(2)}) %collective-permute-start.41) | collective-permute-done | bytes 196640 | tf_op jit(solution)/shard_map/ppermute | solution.py:501
  293.2 2.7 collective-permute-done.43
  300.7 2.8 copy.55
  303.4 11.5 %collective-permute-done.47 = bf16[144,768]{1,0:T(8,128)(2,1)S(1)} collective-permute-done((bf16[144,768]{1,0:T(8,128)(2,1)S(1)}, bf16[144,768]{1,0:T(8,128)(2,1)S(1)}, u32[]{:S(2)}, u32[]{:S(2)}) %collective-permute-start.47) | collective-permute-done | bytes 221216 | tf_op jit(solution)/shard_map/ppermute | solution.py:501
  315.2 2.3 collective-permute-start.50
  319.1 2.5 collective-permute-done.48
  322.6 1.5 collective-permute-start.49
  324.5 4.1 %copy.56 = f32[1,512,2,768]{3,2,1,0:T(2,128)} copy(f32[1,512,2,768]{3,1,2,0:T(8,128)S(1)} %maximum_convert_fusion) | data formatting | bytes 6291456
  332.8 4.7 %weight_results.1 = (f32[768,768]{1,0:T(8,128)}, f32[768,768]{1,0:T(8,128)}, f32[192,768]{1,0:T(8,128)}) custom-call(s32[2]{0:T(128)} %pad_add_fusion.core, bf16[896,768]{1,0:T(8,128)(2,1)} %all-reduce.3.cloned.1.call-done.near, bf16[896,768]{1,0:T(8,128)(2,1)} %copy-done.36), custom_call_target="tpu_custom_call" | custom-call | flops 3300000000 | bytes 1048576 | tf_op jit(solution)/shard_map/weight_results/pallas_call | solution.py:394
  (262 shorter events, 74.1 us)
Async XLA Ops:
  7.2 89.8 %all-gather.5.cloned.1.call-start = ((), (), s32[]{:S(2)}) async-start(), calls=%async_computation.2 | async-start | bytes 6635520 | tf_op jit(solution)/shard_map/all_gather | solution.py:542
  12.6 17.1 %collective-permute-start = (bf16[128,768]{1,0:T(8,128)(2,1)}, bf16[128,768]{1,0:T(8,128)(2,1)}, u32[]{:S(2)}, u32[]{:S(2)}) collective-permute-start(bf16[128,768]{1,0:T(8,128)(2,1)} %bitcast.116), channel_id=1, source_target_pairs={{0,16},{8,24},{16,0},{24,8},{1,17},{9,25},{17,1},{25,9},{2,18},{10... | collective-permute-start | bytes 589832 | tf_op jit(solution)/shard_map/ppermute | solution.py:501
  16.3 20.6 %collective-permute-start.1 = (bf16[8,8,64]{2,0,1:T(8,128)(2,1)}, bf16[8,8,64]{2,0,1:T(8,128)(2,1)S(1)}, u32[]{:S(2)}, u32[]{:S(2)}) collective-permute-start(bf16[8,8,64]{2,0,1:T(8,128)(2,1)} %fusion.16), channel_id=1, source_target_pairs={{0,0},{8,1},{16,8},{24,9},{1,16},{9,17},{17,24},{25,25},{2,2},{10,... | collective-permute-start | bytes 24584 | tf_op jit(solution)/shard_map/ppermute | solution.py:526
  31.2 7.6 %collective-permute-start.2 = (bf16[576,512]{1,0:T(8,128)(2,1)}, bf16[576,512]{1,0:T(8,128)(2,1)}, u32[]{:S(2)}, u32[]{:S(2)}) collective-permute-start(bf16[576,512]{1,0:T(8,128)(2,1)} %bitcast.14.refs_0_.refs_2_.ka.va), channel_id=1, source_target_pairs={{0,1},{1,0},{2,3},{3,2},{4,5},{5,4},{6,7},{7,6},{8,9},{9,8},{10,11... | collective-permute-start | bytes 1769480 | tf_op jit(solution)/shard_map/ppermute | solution.py:494
  31.2 15.2 %collective-permute-start.8 = (bf16[576,512]{1,0:T(8,128)(2,1)}, bf16[576,512]{1,0:T(8,128)(2,1)}, u32[]{:S(2)}, u32[]{:S(2)}) collective-permute-start(bf16[576,512]{1,0:T(8,128)(2,1)} %bitcast.14.refs_0_.refs_2_.ka.va), channel_id=1, source_target_pairs={{0,8},{8,0},{16,24},{24,16},{1,9},{9,1},{17,25},{25,17},{2,10},{10... | collective-permute-start | bytes 1769480 | tf_op jit(solution)/shard_map/ppermute | solution.py:497
  34.1 118.0 %all-gather.7.cloned.1.call-start = ((), (), s32[]{:S(2)}) async-start(), calls=%async_computation.3 | async-start | bytes 2211840 | tf_op jit(solution)/shard_map/all_gather | solution.py:600
  34.4 13.1 %collective-permute-start.3 = (bf16[1,128,768]{2,1,0:T(8,128)(2,1)}, bf16[1,128,768]{2,1,0:T(8,128)(2,1)S(1)}, u32[]{:S(2)}, u32[]{:S(2)}) collective-permute-start(bf16[1,128,768]{2,1,0:T(8,128)(2,1)} %bitcast.20), channel_id=1, source_target_pairs={{0,2},{2,0},{4,6},{6,4},{1,3},{3,1},{5,7},{7,5},{8,10},{10,8},{12,... | collective-permute-start | bytes 589832 | tf_op jit(solution)/shard_map/ppermute | solution.py:504
  35.7 11.9 %collective-permute-start.4 = (bf16[1,128,768]{2,1,0:T(8,128)(2,1)}, bf16[1,128,768]{2,1,0:T(8,128)(2,1)S(1)}, u32[]{:S(2)}, u32[]{:S(2)}) collective-permute-start(bf16[1,128,768]{2,1,0:T(8,128)(2,1)} %bitcast.20), channel_id=1, source_target_pairs={{0,4},{2,6},{4,0},{6,2},{1,5},{3,7},{5,1},{7,3},{8,12},{10,14},{12... | collective-permute-start | bytes 589832 | tf_op jit(solution)/shard_map/ppermute | solution.py:504
  36.9 10.6 %collective-permute-start.5 = (bf16[1,128,768]{2,1,0:T(8,128)(2,1)}, bf16[1,128,768]{2,1,0:T(8,128)(2,1)S(1)}, u32[]{:S(2)}, u32[]{:S(2)}) collective-permute-start(bf16[1,128,768]{2,1,0:T(8,128)(2,1)} %bitcast.20), channel_id=1, source_target_pairs={{0,6},{2,4},{4,2},{6,0},{1,7},{3,5},{5,3},{7,1},{8,14},{10,12},{12... | collective-permute-start | bytes 589832 | tf_op jit(solution)/shard_map/ppermute | solution.py:504
  46.4 6.3 %collective-permute-start.9 = (bf16[576,512]{1,0:T(8,128)(2,1)}, bf16[576,512]{1,0:T(8,128)(2,1)S(1)}, u32[]{:S(2)}, u32[]{:S(2)}) collective-permute-start(bf16[576,512]{1,0:T(8,128)(2,1)} %collective-permute-done.8.refs_0_.refs_2_.ka.va), channel_id=1, source_target_pairs={{0,1},{1,0},{2,3},{3,2},{4,5},{5,4},{6,7},{7,6},{8,9},{9,8},{10,11... | collective-permute-start | bytes 1769480 | tf_op jit(solution)/shard_map/ppermute | solution.py:494
  49.6 10.6 %collective-permute-start.7 = (bf16[576,512]{1,0:T(8,128)(2,1)S(1)}, bf16[576,512]{1,0:T(8,128)(2,1)S(1)}, u32[]{:S(2)}, u32[]{:S(2)}) collective-permute-start(bf16[576,512]{1,0:T(8,128)(2,1)S(1)} %bitcast.118), channel_id=1, source_target_pairs={{0,1},{1,0},{2,3},{3,2},{4,5},{5,4},{6,7},{7,6},{8,9},{9,8},{10,11... | collective-permute-start | bytes 1769480 | tf_op jit(solution)/shard_map/ppermute | solution.py:494
  50.7 17.1 %collective-permute-start.6 = (bf16[576,512]{1,0:T(8,128)(2,1)S(1)}, bf16[576,512]{1,0:T(8,128)(2,1)}, u32[]{:S(2)}, u32[]{:S(2)}) collective-permute-start(bf16[576,512]{1,0:T(8,128)(2,1)S(1)} %bitcast.119), channel_id=1, source_target_pairs={{0,8},{8,0},{16,24},{24,16},{1,9},{9,1},{17,25},{25,17},{2,10},{10... | collective-permute-start | bytes 1769480 | tf_op jit(solution)/shard_map/ppermute | solution.py:497
  84.0 10.5 %collective-permute-start.12 = (bf16[192,1024]{1,0:T(8,128)(2,1)S(1)}, bf16[192,1024]{1,0:T(8,128)(2,1)S(1)}, u32[]{:S(2)}, u32[]{:S(2)}) collective-permute-start(bf16[192,1024]{1,0:T(8,128)(2,1)S(1)} %add_convert_fusion.6), channel_id=1, source_target_pairs={{0,8},{8,0},{16,24},{24,16},{1,9},{9,1},{17,25},{25,17},{2,10},{10... | collective-permute-start | bytes 1179656 | tf_op jit(solution)/shard_map/ppermute | solution.py:497
  97.0 10.8 %collective-permute-start.17 = (bf16[4,864,768]{2,1,0:T(8,128)(2,1)}, bf16[4,864,768]{2,1,0:T(8,128)(2,1)}, u32[]{:S(2)}, u32[]{:S(2)}) collective-permute-start(bf16[4,864,768]{2,1,0:T(8,128)(2,1)} %bitcast.168), channel_id=1, source_target_pairs={{0,1},{1,0},{2,3},{3,2},{4,5},{5,4},{6,7},{7,6},{8,9},{9,8},{10,11... | collective-permute-start | bytes 15925256 | tf_op jit(solution)/shard_map/ppermute | solution.py:494
  107.5 116.6 %reduce-scatter.4.cloned.1.call-start = ((), (), s32[]{:S(2)}) async-start(), calls=%async_computation.4 | async-start | bytes 6881280
  126.5 6.7 %collective-permute-start.18 = (bf16[192,256]{1,0:T(8,128)(2,1)}, bf16[192,256]{1,0:T(8,128)(2,1)S(1)}, u32[]{:S(2)}, u32[]{:S(2)}) collective-permute-start(bf16[192,256]{1,0:T(8,128)(2,1)} %get-tuple-element.121), channel_id=1, source_target_pairs={{0,2},{2,0},{4,6},{6,4},{1,3},{3,1},{5,7},{7,5},{8,10},{10,8},{12,... | collective-permute-start | bytes 294920 | tf_op jit(solution)/shard_map/ppermute | solution.py:504
  127.7 6.9 %collective-permute-start.19 = (bf16[192,256]{1,0:T(8,128)(2,1)}, bf16[192,256]{1,0:T(8,128)(2,1)S(1)}, u32[]{:S(2)}, u32[]{:S(2)}) collective-permute-start(bf16[192,256]{1,0:T(8,128)(2,1)} %get-tuple-element.122), channel_id=1, source_target_pairs={{0,4},{2,6},{4,0},{6,2},{1,5},{3,7},{5,1},{7,3},{8,12},{10,14},{12... | collective-permute-start | bytes 294920 | tf_op jit(solution)/shard_map/ppermute | solution.py:504
  128.0 9.5 %collective-permute-start.20 = (bf16[192,256]{1,0:T(8,128)(2,1)}, bf16[192,256]{1,0:T(8,128)(2,1)S(1)}, u32[]{:S(2)}, u32[]{:S(2)}) collective-permute-start(bf16[192,256]{1,0:T(8,128)(2,1)} %get-tuple-element.123), channel_id=1, source_target_pairs={{0,6},{2,4},{4,2},{6,0},{1,7},{3,5},{5,3},{7,1},{8,14},{10,12},{12... | collective-permute-start | bytes 294920 | tf_op jit(solution)/shard_map/ppermute | solution.py:504
  130.0 11.9 %collective-permute-start.21 = (bf16[8,256,384]{2,1,0:T(8,128)(2,1)}, bf16[8,256,384]{2,1,0:T(8,128)(2,1)S(1)}, u32[]{:S(2)}, u32[]{:S(2)}) collective-permute-start(bf16[8,256,384]{2,1,0:T(8,128)(2,1)} %get-tuple-element.129), channel_id=1, source_target_pairs={{0,1},{1,0},{2,3},{3,2},{4,5},{5,4},{6,7},{7,6},{8,9},{9,8},{10,11... | collective-permute-start | bytes 4718600 | tf_op jit(solution)/shard_map/ppermute | solution.py:494
  131.4 10.5 %collective-permute-start.22 = (bf16[6,256,384]{2,1,0:T(8,128)(2,1)}, bf16[6,256,384]{2,1,0:T(8,128)(2,1)S(1)}, u32[]{:S(2)}, u32[]{:S(2)}) collective-permute-start(bf16[6,256,384]{2,1,0:T(8,128)(2,1)} %get-tuple-element.131), channel_id=1, source_target_pairs={{0,1},{1,0},{2,3},{3,2},{4,5},{5,4},{6,7},{7,6},{8,9},{9,8},{10,11... | collective-permute-start | bytes 3538952 | tf_op jit(solution)/shard_map/ppermute | solution.py:494
  133.2 7.2 %collective-permute-start.23 = (bf16[4,96,256]{2,1,0:T(8,128)(2,1)}, bf16[4,96,256]{2,1,0:T(8,128)(2,1)S(1)}, u32[]{:S(2)}, u32[]{:S(2)}) collective-permute-start(bf16[4,96,256]{2,1,0:T(8,128)(2,1)} %get-tuple-element.132), channel_id=1, source_target_pairs={{0,1},{1,0},{2,3},{3,2},{4,5},{5,4},{6,7},{7,6},{8,9},{9,8},{10,11... | collective-permute-start | bytes 589832 | tf_op jit(solution)/shard_map/ppermute | solution.py:494
  134.6 17.0 %collective-permute-start.24 = (bf16[128,768]{1,0:T(8,128)(2,1)}, bf16[128,768]{1,0:T(8,128)(2,1)}, u32[]{:S(2)}, u32[]{:S(2)}) collective-permute-start(bf16[128,768]{1,0:T(8,128)(2,1)} %get-tuple-element.233), channel_id=1, source_target_pairs={{0,16},{8,24},{16,0},{24,8},{1,17},{9,25},{17,1},{25,9},{2,18},{10... | collective-permute-start | bytes 589832 | tf_op jit(solution)/shard_map/ppermute | solution.py:501
  138.5 13.1 %collective-permute-start.25 = (bf16[192,1024]{1,0:T(8,128)(2,1)S(1)}, bf16[192,1024]{1,0:T(8,128)(2,1)S(1)}, u32[]{:S(2)}, u32[]{:S(2)}) collective-permute-start(bf16[192,1024]{1,0:T(8,128)(2,1)S(1)} %slice_dynamic-update-slice_fusion.refs_4_), channel_id=1, source_target_pairs={{0,1},{1,0},{2,3},{3,2},{4,5},{5,4},{6,7},{7,6},{8,9},{9,8},{10,11... | collective-permute-start | bytes 1179656 | tf_op jit(solution)/shard_map/ppermute | solution.py:494
  140.4 32.7 %collective-permute-start.26 = (bf16[192,1024]{1,0:T(8,128)(2,1)S(1)}, bf16[192,1024]{1,0:T(8,128)(2,1)S(1)}, u32[]{:S(2)}, u32[]{:S(2)}) collective-permute-start(bf16[192,1024]{1,0:T(8,128)(2,1)S(1)} %slice_dynamic-update-slice_fusion.refs_4_), channel_id=1, source_target_pairs={{0,8},{8,0},{16,24},{24,16},{1,9},{9,1},{17,25},{25,17},{2,10},{10... | collective-permute-start | bytes 1179656 | tf_op jit(solution)/shard_map/ppermute | solution.py:497
  151.7 163.5 %all-reduce.3.cloned.1.call-start = ((), (), s32[]{:S(2)}) async-start(), calls=%async_computation.1 | async-start | bytes 2752512 | tf_op jit(solution)/shard_map/psum | solution.py:675
  173.1 16.1 %collective-permute-start.28 = (bf16[192,1024]{1,0:T(8,128)(2,1)S(1)}, bf16[192,1024]{1,0:T(8,128)(2,1)S(1)}, u32[]{:S(2)}, u32[]{:S(2)}) collective-permute-start(bf16[192,1024]{1,0:T(8,128)(2,1)S(1)} %collective-permute-done.26.refs_2_), channel_id=1, source_target_pairs={{0,1},{1,0},{2,3},{3,2},{4,5},{5,4},{6,7},{7,6},{8,9},{9,8},{10,11... | collective-permute-start | bytes 1179656 | tf_op jit(solution)/shard_map/ppermute | solution.py:494
  173.4 15.7 %collective-permute-start.27 = (bf16[192,1024]{1,0:T(8,128)(2,1)S(1)}, bf16[192,1024]{1,0:T(8,128)(2,1)S(1)}, u32[]{:S(2)}, u32[]{:S(2)}) collective-permute-start(bf16[192,1024]{1,0:T(8,128)(2,1)S(1)} %get-tuple-element.144), channel_id=1, source_target_pairs={{0,1},{1,0},{2,3},{3,2},{4,5},{5,4},{6,7},{7,6},{8,9},{9,8},{10,11... | collective-permute-start | bytes 1179656 | tf_op jit(solution)/shard_map/ppermute | solution.py:494
  186.4 34.2 %collective-permute-start.33 = (bf16[2,128,768]{2,1,0:T(8,128)(2,1)S(1)}, bf16[2,128,768]{2,1,0:T(8,128)(2,1)S(1)}, u32[]{:S(2)}, u32[]{:S(2)}) collective-permute-start(bf16[2,128,768]{2,1,0:T(8,128)(2,1)S(1)} %pad_maximum_fusion.10), channel_id=1, source_target_pairs={{0,4},{2,6},{4,0},{6,2},{1,5},{3,7},{5,1},{7,3},{8,12},{10,14},{12... | collective-permute-start | bytes 1179656 | tf_op jit(solution)/shard_map/ppermute | solution.py:504
  187.7 33.7 %collective-permute-start.32 = (bf16[2,128,768]{2,1,0:T(8,128)(2,1)S(1)}, bf16[2,128,768]{2,1,0:T(8,128)(2,1)S(1)}, u32[]{:S(2)}, u32[]{:S(2)}) collective-permute-start(bf16[2,128,768]{2,1,0:T(8,128)(2,1)S(1)} %pad_maximum_fusion.10), channel_id=1, source_target_pairs={{0,2},{2,0},{4,6},{6,4},{1,3},{3,1},{5,7},{7,5},{8,10},{10,8},{12,... | collective-permute-start | bytes 1179656 | tf_op jit(solution)/shard_map/ppermute | solution.py:504
  187.7 33.7 %collective-permute-start.34 = (bf16[2,128,768]{2,1,0:T(8,128)(2,1)S(1)}, bf16[2,128,768]{2,1,0:T(8,128)(2,1)S(1)}, u32[]{:S(2)}, u32[]{:S(2)}) collective-permute-start(bf16[2,128,768]{2,1,0:T(8,128)(2,1)S(1)} %pad_maximum_fusion.10), channel_id=1, source_target_pairs={{0,6},{2,4},{4,2},{6,0},{1,7},{3,5},{5,3},{7,1},{8,14},{10,12},{12... | collective-permute-start | bytes 1179656 | tf_op jit(solution)/shard_map/ppermute | solution.py:504
  200.5 10.1 %collective-permute-start.29 = (bf16[192,1024]{1,0:T(8,128)(2,1)S(1)}, bf16[192,1024]{1,0:T(8,128)(2,1)S(1)}, u32[]{:S(2)}, u32[]{:S(2)}) collective-permute-start(bf16[192,1024]{1,0:T(8,128)(2,1)S(1)} %get-tuple-element.149), channel_id=1, source_target_pairs={{0,1},{1,0},{2,3},{3,2},{4,5},{5,4},{6,7},{7,6},{8,9},{9,8},{10,11... | collective-permute-start | bytes 1179656 | tf_op jit(solution)/shard_map/ppermute | solution.py:494
  210.5 10.9 %collective-permute-start.31 = (bf16[2,192,1024]{2,1,0:T(8,128)(2,1)S(1)}, bf16[2,192,1024]{2,1,0:T(8,128)(2,1)S(1)}, u32[]{:S(2)}, u32[]{:S(2)}) collective-permute-start(bf16[2,192,1024]{2,1,0:T(8,128)(2,1)S(1)} %key_backward.4), channel_id=1, source_target_pairs={{0,1},{1,0},{2,3},{3,2},{4,5},{5,4},{6,7},{7,6},{8,9},{9,8},{10,11... | collective-permute-start | bytes 2359304 | tf_op jit(solution)/shard_map/ppermute | solution.py:494
  210.7 10.7 %collective-permute-start.30 = (bf16[192,1024]{1,0:T(8,128)(2,1)S(1)}, bf16[192,1024]{1,0:T(8,128)(2,1)S(1)}, u32[]{:S(2)}, u32[]{:S(2)}) collective-permute-start(bf16[192,1024]{1,0:T(8,128)(2,1)S(1)} %add_convert_fusion.4), channel_id=1, source_target_pairs={{0,8},{8,0},{16,24},{24,16},{1,9},{9,1},{17,25},{25,17},{2,10},{10... | collective-permute-start | bytes 1179656 | tf_op jit(solution)/shard_map/ppermute | solution.py:497
  220.6 26.4 %collective-permute-start.40 = (bf16[4,3,96,768]{3,2,1,0:T(8,128)(2,1)}, bf16[4,3,96,768]{3,2,1,0:T(8,128)(2,1)}, u32[]{:S(2)}, u32[]{:S(2)}) collective-permute-start(bf16[4,3,96,768]{3,2,1,0:T(8,128)(2,1)} %bitcast.35.refs_4_), channel_id=1, source_target_pairs={{0,1},{1,0},{2,3},{3,2},{4,5},{5,4},{6,7},{7,6},{8,9},{9,8},{10,11... | collective-permute-start | bytes 5308424 | tf_op jit(solution)/shard_map/ppermute | solution.py:494
  222.6 24.4 %collective-permute-start.36 = (bf16[2,192,1024]{2,1,0:T(8,128)(2,1)}, bf16[2,192,1024]{2,1,0:T(8,128)(2,1)}, u32[]{:S(2)}, u32[]{:S(2)}) collective-permute-start(bf16[2,192,1024]{2,1,0:T(8,128)(2,1)} %add_convert_fusion.1), channel_id=1, source_target_pairs={{0,8},{8,0},{16,24},{24,16},{1,9},{9,1},{17,25},{25,17},{2,10},{10... | collective-permute-start | bytes 2359304 | tf_op jit(solution)/shard_map/ppermute | solution.py:497
  235.3 11.8 %collective-permute-start.35 = (bf16[2,192,1024]{2,1,0:T(8,128)(2,1)S(1)}, bf16[2,192,1024]{2,1,0:T(8,128)(2,1)}, u32[]{:S(2)}, u32[]{:S(2)}) collective-permute-start(bf16[2,192,1024]{2,1,0:T(8,128)(2,1)S(1)} %key_backward.6), channel_id=1, source_target_pairs={{0,1},{1,0},{2,3},{3,2},{4,5},{5,4},{6,7},{7,6},{8,9},{9,8},{10,11... | collective-permute-start | bytes 2359304 | tf_op jit(solution)/shard_map/ppermute | solution.py:494
  249.1 9.5 %collective-permute-start.39 = (bf16[3,192,256]{2,1,0:T(8,128)(2,1)S(1)}, bf16[3,192,256]{2,1,0:T(8,128)(2,1)S(1)}, u32[]{:S(2)}, u32[]{:S(2)}) collective-permute-start(bf16[3,192,256]{2,1,0:T(8,128)(2,1)S(1)} %pad_maximum_fusion.15), channel_id=1, source_target_pairs={{0,6},{2,4},{4,2},{6,0},{1,7},{3,5},{5,3},{7,1},{8,14},{10,12},{12... | collective-permute-start | bytes 884744 | tf_op jit(solution)/shard_map/ppermute | solution.py:504
  250.4 15.0 %collective-permute-start.38 = (bf16[3,192,256]{2,1,0:T(8,128)(2,1)S(1)}, bf16[3,192,256]{2,1,0:T(8,128)(2,1)S(1)}, u32[]{:S(2)}, u32[]{:S(2)}) collective-permute-start(bf16[3,192,256]{2,1,0:T(8,128)(2,1)S(1)} %pad_maximum_fusion.14), channel_id=1, source_target_pairs={{0,4},{2,6},{4,0},{6,2},{1,5},{3,7},{5,1},{7,3},{8,12},{10,14},{12... | collective-permute-start | bytes 884744 | tf_op jit(solution)/shard_map/ppermute | solution.py:504
  250.6 14.8 %collective-permute-start.37 = (bf16[3,192,256]{2,1,0:T(8,128)(2,1)S(1)}, bf16[3,192,256]{2,1,0:T(8,128)(2,1)S(1)}, u32[]{:S(2)}, u32[]{:S(2)}) collective-permute-start(bf16[3,192,256]{2,1,0:T(8,128)(2,1)S(1)} %pad_maximum_fusion.13), channel_id=1, source_target_pairs={{0,2},{2,0},{4,6},{6,4},{1,3},{3,1},{5,7},{7,5},{8,10},{10,8},{12,... | collective-permute-start | bytes 884744 | tf_op jit(solution)/shard_map/ppermute | solution.py:504
  253.2 20.6 %collective-permute-start.42 = (bf16[288,768]{1,0:T(8,128)(2,1)S(1)}, bf16[288,768]{1,0:T(8,128)(2,1)S(1)}, u32[]{:S(2)}, u32[]{:S(2)}) collective-permute-start(bf16[288,768]{1,0:T(8,128)(2,1)S(1)} %constant_dynamic-slice_fusion.1), channel_id=1, source_target_pairs={{0,1},{1,0},{2,3},{3,2},{4,5},{5,4},{6,7},{7,6},{8,9},{9,8},{10,11... | collective-permute-start | bytes 1327112 | tf_op jit(solution)/shard_map/ppermute | solution.py:494
  272.5 20.6 %collective-permute-start.41 = (bf16[128,768]{1,0:T(8,128)(2,1)S(1)}, bf16[128,768]{1,0:T(8,128)(2,1)S(1)}, u32[]{:S(2)}, u32[]{:S(2)}) collective-permute-start(bf16[128,768]{1,0:T(8,128)(2,1)S(1)} %get-tuple-element.231), channel_id=1, source_target_pairs={{0,16},{8,24},{16,0},{24,8},{1,17},{9,25},{17,1},{25,9},{2,18},{10... | collective-permute-start | bytes 589832 | tf_op jit(solution)/shard_map/ppermute | solution.py:501
  273.9 22.0 %collective-permute-start.43 = (bf16[144,768]{1,0:T(8,128)(2,1)S(1)}, bf16[144,768]{1,0:T(8,128)(2,1)S(1)}, u32[]{:S(2)}, u32[]{:S(2)}) collective-permute-start(bf16[144,768]{1,0:T(8,128)(2,1)S(1)} %constant_dynamic-slice_fusion), channel_id=1, source_target_pairs={{0,8},{8,0},{16,24},{24,16},{1,9},{9,1},{17,25},{25,17},{2,10},{10... | collective-permute-start | bytes 663560 | tf_op jit(solution)/shard_map/ppermute | solution.py:497
  296.0 19.2 %collective-permute-start.44 = (bf16[2,128,768]{2,1,0:T(8,128)(2,1)S(1)}, bf16[2,128,768]{2,1,0:T(8,128)(2,1)}, u32[]{:S(2)}, u32[]{:S(2)}) collective-permute-start(bf16[2,128,768]{2,1,0:T(8,128)(2,1)S(1)} %pad_maximum_fusion.11), channel_id=1, source_target_pairs={{0,2},{2,0},{4,6},{6,4},{1,3},{3,1},{5,7},{7,5},{8,10},{10,8},{12,... | collective-permute-start | bytes 1179656 | tf_op jit(solution)/shard_map/ppermute | solution.py:504
  297.4 17.7 %collective-permute-start.45 = (bf16[2,128,768]{2,1,0:T(8,128)(2,1)S(1)}, bf16[2,128,768]{2,1,0:T(8,128)(2,1)}, u32[]{:S(2)}, u32[]{:S(2)}) collective-permute-start(bf16[2,128,768]{2,1,0:T(8,128)(2,1)S(1)} %pad_maximum_fusion.11), channel_id=1, source_target_pairs={{0,4},{2,6},{4,0},{6,2},{1,5},{3,7},{5,1},{7,3},{8,12},{10,14},{12... | collective-permute-start | bytes 1179656 | tf_op jit(solution)/shard_map/ppermute | solution.py:504
  297.4 17.7 %collective-permute-start.46 = (bf16[2,128,768]{2,1,0:T(8,128)(2,1)S(1)}, bf16[2,128,768]{2,1,0:T(8,128)(2,1)}, u32[]{:S(2)}, u32[]{:S(2)}) collective-permute-start(bf16[2,128,768]{2,1,0:T(8,128)(2,1)S(1)} %pad_maximum_fusion.11), channel_id=1, source_target_pairs={{0,6},{2,4},{4,2},{6,0},{1,7},{3,5},{5,3},{7,1},{8,14},{10,12},{12... | collective-permute-start | bytes 1179656 | tf_op jit(solution)/shard_map/ppermute | solution.py:504
  298.7 16.2 %collective-permute-start.47 = (bf16[144,768]{1,0:T(8,128)(2,1)S(1)}, bf16[144,768]{1,0:T(8,128)(2,1)S(1)}, u32[]{:S(2)}, u32[]{:S(2)}) collective-permute-start(bf16[144,768]{1,0:T(8,128)(2,1)S(1)} %fusion.6), channel_id=1, source_target_pairs={{0,16},{8,24},{16,0},{24,8},{1,17},{9,25},{17,1},{25,9},{2,18},{10... | collective-permute-start | bytes 663560 | tf_op jit(solution)/shard_map/ppermute | solution.py:501
  315.0 6.6 %collective-permute-start.48 = (bf16[144,768]{1,0:T(8,128)(2,1)S(1)}, bf16[144,768]{1,0:T(8,128)(2,1)}, u32[]{:S(2)}, u32[]{:S(2)}) collective-permute-start(bf16[144,768]{1,0:T(8,128)(2,1)S(1)} %add_convert_fusion.7), channel_id=1, source_target_pairs={{0,8},{8,0},{16,24},{24,16},{1,9},{9,1},{17,25},{25,17},{2,10},{10... | collective-permute-start | bytes 663560 | tf_op jit(solution)/shard_map/ppermute | solution.py:497
  315.2 15.0 %collective-permute-start.50 = (bf16[896,768]{1,0:T(8,128)(2,1)}, bf16[896,768]{1,0:T(8,128)(2,1)S(1)}, u32[]{:S(2)}, u32[]{:S(2)}) collective-permute-start(bf16[896,768]{1,0:T(8,128)(2,1)} %all-reduce.3.cloned.1.call-done.near), channel_id=1, source_target_pairs={{0,1},{1,0},{2,3},{3,2},{4,5},{5,4},{6,7},{7,6},{8,9},{9,8},{10,11... | collective-permute-start | bytes 4128776 | tf_op jit(solution)/shard_map/ppermute | solution.py:494
  (53 other events, 280.2 us)
Sparse Core Ops, SparseCore 0:
  34.2 62.7 all-gather.4
  107.7 36.8 all-gather.6
  151.8 71.7 reduce-scatter.3
  235.8 74.6 all-reduce.2
